TPU v7x, 128 devices: a whole 4x4x4 slice. The times are simulated.
128 devices in a mesh: seq: 16 (over y, z_hi, core), chan: 8 (over x, z_lo).
Axes of the slice: x: 4, y: 4, z: 4 (z_hi: 2, z_lo: 2; z = z_hi * 2 + z_lo), core: 2. Of those that a mesh axis runs over, the one named last changes fastest.
Arguments:
- activations: bfloat16 [16384, 8192], P('seq', 'chan'), may hold values from -6 to 6
- proj_weight: bfloat16 [8192, 3, 1024], P('chan'), may hold values from -0.0625 to 0.0625
- filter_taps: float32 [16384, 1024], P('seq', 'chan'), may hold values from -0.046875 to 0.046875
Outputs:
- mixed: float32 [16384, 1024], P('seq', 'chan')
All inputs are finite; a program needn't handle non-finite values.
Results may differ from a plain program's by a relative error of at most 0.0003.
Values sent between devices are 32-bit elements; how exact they have to be, the bound alone decides.
No kernel may reach another device: no remote copies, remote signals or barrier semaphores. Data moves between devices by JAX's collectives and lax.ppermute only.
A program may use at most 128 MiB of HBM per device.

v0:
```python
import math

import jax
import jax.numpy as jnp
from jax import lax
from jax.sharding import PartitionSpec as P

exact_dot = lax.Precision.HIGHEST


def phase_table(row_count, col_count, period, exponent_sign, row_start, col_start):
    row_index = (row_start + jnp.arange(row_count, dtype=jnp.int32))[:, None]
    col_index = (col_start + jnp.arange(col_count, dtype=jnp.int32))[None, :]
    phase = row_index * col_index % period
    angle = exponent_sign * 2.0 * math.pi / period * phase.astype(jnp.float32)
    return (jnp.cos(angle), jnp.sin(angle))


def complex_einsum(formula, matrix_real, matrix_imag, signal_real, signal_imag):
    real_part = jnp.einsum(formula, matrix_real, signal_real, precision=exact_dot)
    imag_part = jnp.einsum(formula, matrix_imag, signal_real, precision=exact_dot)
    if signal_imag is not None:
        real_part = real_part - jnp.einsum(formula, matrix_imag, signal_imag, precision=exact_dot)
        imag_part = imag_part + jnp.einsum(formula, matrix_real, signal_imag, precision=exact_dot)
    return (real_part, imag_part)


def rotate(signal_real, signal_imag, turn_real, turn_imag):
    return (
        signal_real * turn_real - signal_imag * turn_imag,
        signal_real * turn_imag + signal_imag * turn_real,
    )


def split_factor(period):
    factor = int(math.isqrt(period))
    while period % factor != 0:
        factor = factor - 1
    return factor


def dft_middle(signal_real, signal_imag, exponent_sign):
    batch_size, period, trailing = signal_real.shape
    outer_size = split_factor(period)
    second = period // outer_size
    shaped_real = signal_real.reshape(batch_size, outer_size, second, trailing)
    shaped_imag = signal_imag.reshape(batch_size, outer_size, second, trailing)
    matrix_real, matrix_imag = phase_table(outer_size, outer_size, outer_size, exponent_sign, 0, 0)
    section_real, section_imag = complex_einsum(
        "km,zmjc->zkjc", matrix_real, matrix_imag, shaped_real, shaped_imag
    )
    turn_real, turn_imag = phase_table(outer_size, second, period, exponent_sign, 0, 0)
    section_real, section_imag = rotate(
        section_real, section_imag, turn_real[None, :, :, None], turn_imag[None, :, :, None]
    )
    matrix_real, matrix_imag = phase_table(second, second, second, exponent_sign, 0, 0)
    final_real, final_imag = complex_einsum(
        "lj,zkjc->zlkc", matrix_real, matrix_imag, section_real, section_imag
    )
    return (
        final_real.reshape(batch_size, period, trailing),
        final_imag.reshape(batch_size, period, trailing),
    )


def split_convolve(product_kv, filter_taps):
    blocks = lax.axis_size("seq")
    tokens, channels = product_kv.shape
    per_block = tokens // blocks
    fft_length = 2 * blocks * tokens
    seq_index = lax.axis_index("seq")
    moved_kv, moved_taps = (
        lax.all_to_all(
            product_kv.reshape(1, tokens, channels), "seq", split_axis=1, concat_axis=0, tiled=True
        ),
        lax.all_to_all(
            filter_taps.reshape(1, tokens, channels), "seq", split_axis=1, concat_axis=0, tiled=True
        ),
    )
    cross_real, cross_imag = phase_table(2 * blocks, blocks, 2 * blocks, -1.0, 0, 0)
    turn_real, turn_imag = phase_table(
        2 * blocks, per_block, fft_length, -1.0, 0, seq_index * per_block
    )

    def forward(signal):
        part_real, part_imag = complex_einsum("kp,prc->krc", cross_real, cross_imag, signal, None)
        return rotate(part_real, part_imag, turn_real[:, :, None], turn_imag[:, :, None])

    kv_real, kv_imag = forward(moved_kv)
    taps_real, taps_imag = forward(moved_taps)
    left_real, left_imag = dft_middle(
        lax.all_to_all(kv_real, "seq", split_axis=0, concat_axis=1, tiled=True),
        lax.all_to_all(kv_imag, "seq", split_axis=0, concat_axis=1, tiled=True),
        -1.0,
    )
    right_real, right_imag = dft_middle(
        lax.all_to_all(taps_real, "seq", split_axis=0, concat_axis=1, tiled=True),
        lax.all_to_all(taps_imag, "seq", split_axis=0, concat_axis=1, tiled=True),
        -1.0,
    )
    prod_real = left_real * right_real - left_imag * right_imag
    prod_imag = left_real * right_imag + left_imag * right_real
    back_real, back_imag = dft_middle(prod_real, prod_imag, 1.0)
    undo_real, undo_imag = phase_table(2, tokens, fft_length, 1.0, 2 * seq_index, 0)
    back_real, back_imag = rotate(
        back_real, back_imag, undo_real[:, :, None], undo_imag[:, :, None]
    )
    spec_real = lax.all_to_all(back_real, "seq", split_axis=1, concat_axis=0, tiled=True)
    spec_imag = lax.all_to_all(back_imag, "seq", split_axis=1, concat_axis=0, tiled=True)
    inverse_real, inverse_imag = phase_table(blocks, 2 * blocks, 2 * blocks, 1.0, 0, 0)
    rows_real = jnp.einsum("pk,krc->prc", inverse_real, spec_real, precision=exact_dot)
    rows_real = (
        rows_real - jnp.einsum("pk,krc->prc", inverse_imag, spec_imag, precision=exact_dot)
    ) / fft_length
    home_rows = lax.all_to_all(rows_real, "seq", split_axis=0, concat_axis=1, tiled=True)
    return home_rows.reshape(tokens, channels)


def on_device(activations, proj_weight, filter_taps):
    partial_value = jnp.einsum(
        "td,djc->tjc", activations, proj_weight, preferred_element_type=jnp.float32
    )
    projected = lax.psum_scatter(partial_value, "chan", scatter_dimension=2, tiled=True)
    product_kv = projected[:, 1, :] * projected[:, 2, :]
    convolved = split_convolve(product_kv, filter_taps)
    return projected[:, 0, :] * convolved


def solution(mesh):
    return jax.shard_map(
        on_device,
        mesh=mesh,
        in_specs=(P("seq", "chan"), P("chan", None, None), P("seq", "chan")),
        out_specs=P("seq", "chan"),
        check_vma=False,
    )
```

profile of v0, /device:TPU:1, one launch (start us, length us, event | category | flops | bytes accessed | tf_op | source)
XLA Modules:
  0.0 505.2 jit_solution(9217673163473574231)
XLA Ops:
  6.5 1.6 copy-done
  8.1 12.2 %fusion = f32[1024,3,1024]{2,0,1:T(8,128)} fusion(bf16[1024,3,1024]{2,0,1:T(8,128)(2,1)} %param.4, bf16[1024,1024]{1,0:T(8,128)(2,1)S(1)} %copy-done), kind=kOutput, calls=%fused_computation | convolution fusion | flops 6442450944 | bytes 20971520 | tf_op jit(solution)/shard_map/td,djc->tjc/dot_general | solution.py:120
  20.4 9.3 %all-to-all-start.3 = ((f32[1,1024,128]{2,0,1:T(1,128)}), f32[1,1024,128]{2,0,1:T(1,128)S(1)}, u32[]{:S(2)}, u32[]{:S(2)}) async-start(f32[1,1024,128]{2,0,1:T(1,128)} %bitcast.22), calls=%async_computation.4 | async-start | bytes 1048576 | tf_op jit(solution)/shard_map/all_to_all | solution.py:76
  29.7 246.7 %reduce-scatter.2.cloned.1.call-done = f32[1024,3,128]{2,0,1:T(8,128)} async-done(((f32[1024,3,1024]{2,0,1:T(8,128)}), f32[1024,3,128]{2,0,1:T(8,128)}) %reduce-scatter.2.cloned.1.call-update) | async-done | bytes 1572880 | tf_op jit(solution)/shard_map/reduce_scatter | solution.py:123
  276.4 2.0 slice_multiply_fusion
  278.4 6.6 %all-to-all-start = ((f32[1,1024,128]{2,0,1:T(1,128)}), f32[1,1024,128]{2,0,1:T(1,128)S(1)}, u32[]{:S(2)}, u32[]{:S(2)}) async-start(f32[1,1024,128]{2,0,1:T(1,128)} %bitcast.5), calls=%async_computation.1 | async-start | bytes 1048576 | tf_op jit(solution)/shard_map/all_to_all | solution.py:73
  285.3 2.2 fusion.52
  287.5 8.7 %all-to-all-done = f32[1,1024,128]{2,0,1:T(1,128)S(1)} async-done(((f32[1,1024,128]{2,0,1:T(1,128)}), f32[1,1024,128]{2,0,1:T(1,128)S(1)}, u32[]{:S(2)}, u32[]{:S(2)}) %all-to-all-start) | async-done | bytes 524320 | tf_op jit(solution)/shard_map/all_to_all | solution.py:73
  298.6 2.9 multiply_add_fusion.3
  301.5 1.6 copy.103
  303.1 5.4 %all-to-all-start.1 = ((f32[32,64,128]{2,1,0:T(8,128)}), f32[32,64,128]{2,1,0:T(8,128)}, u32[]{:S(2)}, u32[]{:S(2)}) async-start(f32[32,64,128]{2,1,0:T(8,128)} %copy.103), calls=%async_computation.2 | async-start | bytes 2097152 | tf_op jit(solution)/shard_map/all_to_all | solution.py:92
  310.1 15.8 %all-to-all-done.1 = f32[32,64,128]{2,1,0:T(8,128)} async-done(((f32[32,64,128]{2,1,0:T(8,128)}), f32[32,64,128]{2,1,0:T(8,128)}, u32[]{:S(2)}, u32[]{:S(2)}) %all-to-all-start.1) | async-done | bytes 1048608 | tf_op jit(solution)/shard_map/all_to_all | solution.py:92
  325.9 4.3 all-to-all-start.4
  330.7 1.6 copy.106
  332.3 15.2 %all-to-all-done.4 = f32[32,64,128]{2,1,0:T(8,128)S(1)} async-done(((f32[32,64,128]{2,1,0:T(8,128)}), f32[32,64,128]{2,1,0:T(8,128)S(1)}, u32[]{:S(2)}, u32[]{:S(2)}) %all-to-all-start.4) | async-done | bytes 1048608 | tf_op jit(solution)/shard_map/all_to_all | solution.py:97
  347.5 4.7 all-to-all-start.2
  352.5 1.6 copy.120
  355.7 1.7 fusion.47
  357.4 2.7 fusion.45
  360.1 9.2 %all-to-all-done.2 = f32[32,64,128]{2,1,0:T(8,128)S(1)} async-done(((f32[32,64,128]{2,1,0:T(8,128)}), f32[32,64,128]{2,1,0:T(8,128)S(1)}, u32[]{:S(2)}, u32[]{:S(2)}) %all-to-all-start.2) | async-done | bytes 1048608 | tf_op jit(solution)/shard_map/all_to_all | solution.py:93
  369.3 4.9 all-to-all-start.5
  374.3 2.7 fusion.35
  377.0 1.7 fusion.33
  378.8 1.7 fusion.9
  380.5 1.7 fusion.8
  382.2 9.5 %all-to-all-done.5 = f32[32,64,128]{2,1,0:T(8,128)} async-done(((f32[32,64,128]{2,1,0:T(8,128)}), f32[32,64,128]{2,1,0:T(8,128)}, u32[]{:S(2)}, u32[]{:S(2)}) %all-to-all-start.5) | async-done | bytes 1048608 | tf_op jit(solution)/shard_map/all_to_all | solution.py:98
  393.2 1.7 fusion.7
  394.9 2.2 multiply_add_fusion.2
  397.1 10.5 %fusion.27 = f32[2,32,128,32]{2,3,1,0:T(8,128)S(1)} fusion(f32[2,32,32,128]{3,1,2,0:T(8,128)S(1)} %get-tuple-element.14), kind=kOutput, calls=%fused_computation.56 | convolution fusion | flops 100677632 | bytes 2097152 | tf_op jit(solution)/shard_map/lj,zkjc->zlkc/dot_general | solution.py:21
  407.6 1.7 fusion.29
  409.3 1.7 fusion.41
  411.0 1.7 fusion.39
  412.7 1.7 convolution_add_fusion.2
  414.4 1.8 convolution_subtract_fusion.2
  416.2 1.8 convolution_subtract_fusion.4
  418.0 2.3 multiply_add_fusion.1
  425.3 1.7 fusion.23
  427.0 1.7 fusion.21
  428.7 1.7 fusion.3
  431.0 2.0 fusion.2
  434.5 1.8 copy.139
  436.3 4.3 all-to-all-start.6
  440.6 1.8 copy.142
  442.4 15.5 %all-to-all-done.6 = f32[2,1024,128]{2,0,1:T(2,128)S(1)} async-done(((f32[2,1024,128]{2,0,1:T(2,128)}), f32[2,1024,128]{2,0,1:T(2,128)S(1)}, u32[]{:S(2)}, u32[]{:S(2)}) %all-to-all-start.6) | async-done | bytes 1048608 | tf_op jit(solution)/shard_map/all_to_all | solution.py:108
  457.9 4.3 all-to-all-start.7
  463.8 15.7 %all-to-all-done.7 = f32[2,1024,128]{2,0,1:T(2,128)S(1)} async-done(((f32[2,1024,128]{2,0,1:T(2,128)}), f32[2,1024,128]{2,0,1:T(2,128)S(1)}, u32[]{:S(2)}, u32[]{:S(2)}) %all-to-all-start.7) | async-done | bytes 1048608 | tf_op jit(solution)/shard_map/all_to_all | solution.py:109
  481.3 14.8 %all_to_all.129 = f32[16,64,128]{2,1,0:T(8,128)S(1)} all-to-all(f32[16,64,128]{2,1,0:T(8,128)S(1)} %copy.145), channel_id=1, replica_groups=mesh['seq'=16,'chan'=8] {'seq'}, dimensions={0} | all-to-all | bytes 1048576 | tf_op jit(solution)/shard_map/all_to_all | solution.py:115
  496.1 1.9 fusion.49
  (51 shorter events, 18.6 us)
Async XLA Ops:
  6.5 1.6 copy-start
  6.5 269.8 %reduce-scatter.2.cloned.1.call-start = ((), (), s32[]{:S(2)}) async-start(), calls=%async_computation.10 | async-start | bytes 14155776 | tf_op jit(solution)/shard_map/reduce_scatter | solution.py:123
  20.4 258.0 %all-to-all-start.3 = ((f32[1,1024,128]{2,0,1:T(1,128)}), f32[1,1024,128]{2,0,1:T(1,128)S(1)}, u32[]{:S(2)}, u32[]{:S(2)}) async-start(f32[1,1024,128]{2,0,1:T(1,128)} %bitcast.22), calls=%async_computation.4 | async-start | bytes 1048576 | tf_op jit(solution)/shard_map/all_to_all | solution.py:76
  278.4 17.8 %all-to-all-start = ((f32[1,1024,128]{2,0,1:T(1,128)}), f32[1,1024,128]{2,0,1:T(1,128)S(1)}, u32[]{:S(2)}, u32[]{:S(2)}) async-start(f32[1,1024,128]{2,0,1:T(1,128)} %bitcast.5), calls=%async_computation.1 | async-start | bytes 1048576 | tf_op jit(solution)/shard_map/all_to_all | solution.py:73
  296.2 2.5 copy-start.3
  301.5 7.0 %copy-start.4 = (f32[32,64,128]{2,0,1:T(8,128)S(1)}, f32[32,64,128]{2,0,1:T(8,128)}, u32[]{:S(2)}) copy-start(f32[32,64,128]{2,0,1:T(8,128)} %get-tuple-element.8) | copy-start | bytes 3145732
  303.1 22.8 %all-to-all-start.1 = ((f32[32,64,128]{2,1,0:T(8,128)}), f32[32,64,128]{2,1,0:T(8,128)}, u32[]{:S(2)}, u32[]{:S(2)}) async-start(f32[32,64,128]{2,1,0:T(8,128)} %copy.103), calls=%async_computation.2 | async-start | bytes 2097152 | tf_op jit(solution)/shard_map/all_to_all | solution.py:92
  325.9 21.6 %all-to-all-start.4 = ((f32[32,64,128]{2,1,0:T(8,128)}), f32[32,64,128]{2,1,0:T(8,128)S(1)}, u32[]{:S(2)}, u32[]{:S(2)}) async-start(f32[32,64,128]{2,1,0:T(8,128)} %copy.117), calls=%async_computation.5 | async-start | bytes 2097152 | tf_op jit(solution)/shard_map/all_to_all | solution.py:97
  347.5 6.6 %copy-start.6 = (f32[32,64,128]{2,1,0:T(8,128)}, f32[32,64,128]{2,1,0:T(8,128)S(1)}, u32[]{:S(2)}) copy-start(f32[32,64,128]{2,1,0:T(8,128)S(1)} %all-to-all-done.4) | copy-start | bytes 3145732
  347.5 21.8 %all-to-all-start.2 = ((f32[32,64,128]{2,1,0:T(8,128)}), f32[32,64,128]{2,1,0:T(8,128)S(1)}, u32[]{:S(2)}, u32[]{:S(2)}) async-start(f32[32,64,128]{2,1,0:T(8,128)} %copy.106), calls=%async_computation.3 | async-start | bytes 2097152 | tf_op jit(solution)/shard_map/all_to_all | solution.py:93
  354.1 1.5 copy-start.7
  369.3 22.3 %all-to-all-start.5 = ((f32[32,64,128]{2,1,0:T(8,128)}), f32[32,64,128]{2,1,0:T(8,128)}, u32[]{:S(2)}, u32[]{:S(2)}) async-start(f32[32,64,128]{2,1,0:T(8,128)} %copy.120), calls=%async_computation.6 | async-start | bytes 2097152 | tf_op jit(solution)/shard_map/all_to_all | solution.py:98
  378.8 1.7 copy-start.2
  391.7 1.5 copy-start.5
  436.3 21.6 %all-to-all-start.6 = ((f32[2,1024,128]{2,0,1:T(2,128)}), f32[2,1024,128]{2,0,1:T(2,128)S(1)}, u32[]{:S(2)}, u32[]{:S(2)}) async-start(f32[2,1024,128]{2,0,1:T(2,128)} %copy.139), calls=%async_computation.7 | async-start | bytes 2097152 | tf_op jit(solution)/shard_map/all_to_all | solution.py:108
  457.9 21.6 %all-to-all-start.7 = ((f32[2,1024,128]{2,0,1:T(2,128)}), f32[2,1024,128]{2,0,1:T(2,128)S(1)}, u32[]{:S(2)}, u32[]{:S(2)}) async-start(f32[2,1024,128]{2,0,1:T(2,128)} %copy.142), calls=%async_computation.8 | async-start | bytes 2097152 | tf_op jit(solution)/shard_map/all_to_all | solution.py:109
  480.4 17.6 %copy-start.1 = (bf16[1024,1024]{1,0:T(8,128)(2,1)S(1)}, bf16[1024,1024]{1,0:T(8,128)(2,1)}, u32[]{:S(2)}) copy-start(bf16[1024,1024]{1,0:T(8,128)(2,1)} %param.3) | copy-start | bytes 6291460
Sparse Core Ops, SparseCore 0:
  20.5 255.8 reduce-scatter.1
where the time goes:
time: 514 us; the launch traced here: 505 us
  waiting for transfers between devices  336 us (65%)
  matrix products  72.3 us (14%)
  starting transfers between devices  43.8 us (9%)
  local copies, waits for them, and re-layouts  18.2 us (4%)
  blocking collectives  14.8 us (3%)
  between operations  14.2 us (3%)
  other arithmetic  5.56 us (1%)
    reduce_scatter x1, waiting for transfers between devices, on_device(): lax.psum_scatter(partial_value, 'chan', scatter_dimension=2, tiled=True)  247 us
    dot_general x8, matrix products, complex_einsum(): jnp.einsum(formula, matrix_imag, signal_real, precision=exact_dot)  23.5 us
    all_to_all x1, waiting for transfers between devices, split_convolve(): lax.all_to_all(kv_real, 'seq', split_axis=0, concat_axis=1, tiled=True)  15.8 us
    all_to_all x1, waiting for transfers between devices, split_convolve(): lax.all_to_all(back_imag, 'seq', split_axis=1, concat_axis=0, tiled=True)  15.7 us
    all_to_all x1, waiting for transfers between devices, split_convolve(): lax.all_to_all(back_real, 'seq', split_axis=1, concat_axis=0, tiled=True)  15.5 us
    all_to_all x1, waiting for transfers between devices, split_convolve(): lax.all_to_all(taps_real, 'seq', split_axis=0, concat_axis=1, tiled=True)  15.2 us
    all_to_all x1, blocking collectives, split_convolve(): lax.all_to_all(rows_real, 'seq', split_axis=0, concat_axis=1, tiled=True)  14.8 us
    dot_general x8, matrix products, complex_einsum(): jnp.einsum(formula, matrix_real, signal_real, precision=exact_dot)  14 us
  transfers between devices with their start and end apart: 9, of which 8 were waited for; matrix products, arithmetic and copies ran while one was open for 5% of the time, Pallas kernels for 0%

commit v1 on v0

v1 whole, which is shorter than its diff:
```python
import functools

import jax
import jax.numpy as jnp
import ml_dtypes
import numpy as np
from jax import lax
from jax.experimental import pallas as pl
from jax.experimental.pallas import tpu as pltpu
from jax.sharding import PartitionSpec as P

BLOCK = 128
X_SIZE = 4
Z_FIRST_ROWS = 448
PARAMS = pltpu.CompilerParams(vmem_limit_bytes=40 * 1024 * 1024)


def shift_x(value, step):
    return lax.ppermute(value, "chan", [(i, (i + 2 * step) % 8) for i in range(8)])


def swap_z(value):
    return lax.ppermute(value, "chan", [(i, i ^ 1) for i in range(8)])


def project(activations, weight, start, width):
    columns = lax.dynamic_slice_in_dim(weight, start, width, axis=2)
    return jnp.einsum("td,djc->jtc", activations, columns, preferred_element_type=jnp.float32)


def as_halves(value):
    return value.reshape(2, -1, value.shape[-1])


def z_first(activations, weight):
    chan = lax.axis_index("chan")
    x_at, z_at = chan // 2, chan % 2

    def part(dx, dz):
        owner = (x_at + dx) % X_SIZE * 2 + (z_at + dz) % 2
        return as_halves(project(activations, weight, owner * BLOCK, BLOCK))

    far = part(2, 0) + swap_z(part(2, 1))
    from_left = shift_x(far[0], 1)
    from_right = shift_x(far[1], -1)
    right, got_right = part(1, 0), swap_z(part(1, 1))
    left, got_left = part(3, 0), swap_z(part(3, 1))
    right = jnp.stack([right[0] + got_right[0] + from_left, right[1] + got_right[1]])
    left = jnp.stack([left[0] + got_left[0], left[1] + got_left[1] + from_right])
    return part(0, 0), swap_z(part(0, 1)), shift_x(right, 1), shift_x(left, -1)


def x_first(activations, weight):
    chan = lax.axis_index("chan")
    x_at, z_at = chan // 2, chan % 2

    def part(dx):
        owner = (x_at + dx) % X_SIZE
        return as_halves(project(activations, weight, owner * 2 * BLOCK, 2 * BLOCK))

    def pick(value, dz):
        return lax.dynamic_slice_in_dim(value, (z_at + dz) % 2 * BLOCK, BLOCK, axis=-1)

    far = part(2)
    from_left = shift_x(far[0], 1)
    from_right = shift_x(far[1], -1)
    right, left, own = part(1), part(3), part(0)

    def second(dz):
        to_right, to_left = pick(right, dz), pick(left, dz)
        to_right = jnp.stack([to_right[0] + pick(from_left, dz), to_right[1]])
        to_left = jnp.stack([to_left[0], to_left[1] + pick(from_right, dz)])
        return shift_x(to_right, 1), shift_x(to_left, -1)

    a, b = second(1)
    other = swap_z(pick(own, 1) + a + b)
    c, d = second(0)
    return pick(own, 0), c, d, other


def split_bf16(table):
    high = table.astype(np.float32).astype(ml_dtypes.bfloat16)
    low = (table - high.astype(np.float64)).astype(ml_dtypes.bfloat16)
    return high, low


@functools.lru_cache(None)
def tables(length):
    rows = length // BLOCK
    period = 2 * length
    odd = np.arange(rows) + 0.5
    first = -2 * np.pi * np.outer(odd, np.arange(rows)) / (2 * rows)
    turn = -2 * np.pi * np.outer(odd, np.arange(BLOCK)) / period
    second = -2 * np.pi * (np.outer(np.arange(BLOCK), np.arange(BLOCK)) % BLOCK) / BLOCK
    c, s = np.cos(second), np.sin(second)
    scale = 1.0 / length
    return (
        split_bf16(np.concatenate([np.cos(first), np.sin(first)], axis=0)),
        (np.cos(turn).astype(np.float32), np.sin(turn).astype(np.float32)),
        split_bf16(np.block([[c, s], [-s, c]])),
        split_bf16(np.block([[c, -s], [s, c]])),
        split_bf16(np.concatenate([np.cos(first).T, np.sin(first).T], axis=1) * scale),
    )


def split_value(value):
    high = value.astype(jnp.bfloat16)
    return high, (value - high.astype(jnp.float32)).astype(jnp.bfloat16)


def dot3(left, right):
    dot = functools.partial(jnp.dot, preferred_element_type=jnp.float32)
    return dot(left[0], right[0]) + (dot(left[0], right[1]) + dot(left[1], right[0]))


def forward(signal_ref, first, turn, second):
    seqs, channels = signal_ref.shape[:2]
    rows = seqs * signal_ref.shape[2]
    signal = jnp.concatenate(
        [signal_ref[:, c].reshape(rows, BLOCK) for c in range(channels)], axis=1
    )
    part = dot3(first, split_value(signal))
    turned = []
    for c in range(channels):
        real = part[:rows, c * BLOCK : (c + 1) * BLOCK]
        imag = part[rows:, c * BLOCK : (c + 1) * BLOCK]
        turned.append(
            jnp.concatenate(
                [real * turn[0] - imag * turn[1], real * turn[1] + imag * turn[0]], axis=1
            )
        )
    return dot3(split_value(jnp.concatenate(turned, axis=0)), second)


def taps_kernel(taps_ref, f_hi, f_lo, t_re, t_im, s_hi, s_lo, out_ref):
    out_ref[...] = forward(
        taps_ref, (f_hi[...], f_lo[...]), (t_re[...], t_im[...]), (s_hi[...], s_lo[...])
    )


def conv_kernel(
    kv_ref, spec_ref, f_hi, f_lo, t_re, t_im, s_hi, s_lo, b_hi, b_lo, i_hi, i_lo, out_ref
):
    seqs, channels, blocks, _ = kv_ref.shape
    rows = seqs * blocks
    turn = (t_re[...], t_im[...])
    spectrum = forward(kv_ref, (f_hi[...], f_lo[...]), turn, (s_hi[...], s_lo[...]))
    real, imag = spectrum[:, :BLOCK], spectrum[:, BLOCK:]
    taps_real, taps_imag = spec_ref[:, :BLOCK], spec_ref[:, BLOCK:]
    product = jnp.concatenate(
        [real * taps_real - imag * taps_imag, real * taps_imag + imag * taps_real], axis=1
    )
    back = dot3(split_value(product), (b_hi[...], b_lo[...]))
    columns = []
    for c in range(channels):
        real = back[c * rows : (c + 1) * rows, :BLOCK]
        imag = back[c * rows : (c + 1) * rows, BLOCK:]
        columns.append(
            jnp.concatenate(
                [real * turn[0] + imag * turn[1], imag * turn[0] - real * turn[1]], axis=0
            )
        )
    result = dot3((i_hi[...], i_lo[...]), split_value(jnp.concatenate(columns, axis=1)))
    for c in range(channels):
        out_ref[:, c] = result[:, c * BLOCK : (c + 1) * BLOCK].reshape(seqs, blocks, BLOCK)


def turn_blocks(value_ref, out_ref):
    for b in range(out_ref.shape[1]):
        out_ref[:, b, :] = value_ref[b * BLOCK : (b + 1) * BLOCK, :].T


def taps_turn_kernel(taps_ref, out_ref):
    turn_blocks(taps_ref, out_ref)


def kv_kernel(z0, z1, z2, z3, x0, x1, x2, x3, out_ref, kv_ref):
    rows = z0.shape[1]
    total = (z0[...] + z1[...]) + (z2[...] + z3[...])
    kv_ref[:rows] = total[0] * total[1]
    total = (x0[...] + x1[...]) + (x2[...] + x3[...])
    kv_ref[rows:] = total[0] * total[1]
    turn_blocks(kv_ref, out_ref)


def gate_kernel(conv_ref, z0, z1, z2, z3, x0, x1, x2, x3, out_ref):
    for b in range(conv_ref.shape[1]):
        out_ref[b * BLOCK : (b + 1) * BLOCK, :] = conv_ref[:, b, :].T
    rows = 2 * z0.shape[1]
    total = (z0[...] + z1[...]) + (z2[...] + z3[...])
    out_ref[:rows] = out_ref[:rows] * total.reshape(rows, BLOCK)
    total = (x0[...] + x1[...]) + (x2[...] + x3[...])
    out_ref[rows:] = out_ref[rows:] * total.reshape(-1, BLOCK)


def call(kernel, out_shape, *operands, scratch=()):
    return pl.pallas_call(
        kernel,
        out_shape=jax.ShapeDtypeStruct(out_shape, jnp.float32),
        scratch_shapes=scratch,
        compiler_params=PARAMS,
    )(*operands)


def exchange(value):
    return lax.all_to_all(value, "seq", split_axis=0, concat_axis=0, tiled=True)


def on_device(activations, proj_weight, filter_taps):
    tokens, channels = filter_taps.shape
    seqs = lax.axis_size("seq")
    length = tokens * seqs
    blocks = tokens // BLOCK
    owned = channels // seqs
    turned_shape = (channels, blocks, BLOCK)
    moved_shape = (seqs, owned, blocks, BLOCK)
    first, turn, second, back, inverse = tables(length)

    low, high = activations[:Z_FIRST_ROWS], activations[Z_FIRST_ROWS:]
    kv_weight, q_weight = proj_weight[:, 1:], proj_weight[:, :1]
    kv_parts = z_first(low, kv_weight) + x_first(high, kv_weight)
    q_parts = z_first(low, q_weight) + x_first(high, q_weight)

    taps = call(taps_turn_kernel, turned_shape, filter_taps)
    taps = exchange(taps.reshape(moved_shape))
    spectrum = call(
        taps_kernel, (owned * length // BLOCK, 2 * BLOCK), taps, *first, *turn, *second
    )

    kv = call(
        kv_kernel, turned_shape, *kv_parts, scratch=[pltpu.VMEM((tokens, channels), jnp.float32)]
    )
    moved = exchange(kv.reshape(moved_shape))
    convolved = call(
        conv_kernel, moved_shape, moved, spectrum, *first, *turn, *second, *back, *inverse
    )
    home = exchange(convolved).reshape(turned_shape)
    return call(gate_kernel, (tokens, channels), home, *q_parts)


def solution(mesh):
    return jax.shard_map(
        on_device,
        mesh=mesh,
        in_specs=(P("seq", "chan"), P("chan", None, None), P("seq", "chan")),
        out_specs=P("seq", "chan"),
        check_vma=False,
    )
```

time: 514 us -> 217 us (0.42); the launches traced: 505 us -> 216 us
  waiting for transfers between devices: 336 us -> 54.2 us
  starting transfers between devices: 43.8 us -> 59 us
  blocking collectives: 14.8 us -> 0 us
  matrix products: 72.3 us -> 58.1 us
  between operations: 14.2 us -> 0.61 us
  other arithmetic: 5.56 us -> 14.3 us
  Pallas kernels: 0 us -> 7.82 us
    reduce_scatter x1 -> x0, waiting for transfers between devices: 247 us -> none  [on_device(): lax.psum_scatter(partial_value, 'chan', scatter_dimension=2, tiled=True)]
    all_to_all x8 -> x3, waiting for transfers between devices: 89.6 us -> 2.75 us  [exchange(): return lax.all_to_all(value, 'seq', split_axis=0, concat_axis=0, tiled=True)]
    ppermute x0 -> x30, waiting for transfers between devices: none -> 51.5 us  [the longest x20 46.1 us: shift_x(): lax.ppermute(value, 'chan', [(i, (i + 2 * step) % 8) for i in range(8)])]
    ppermute x0 -> x30, starting transfers between devices: none -> 33.9 us  [the longest x20 26.5 us: shift_x(): lax.ppermute(value, 'chan', [(i, (i + 2 * step) % 8) for i in range(8)])]
    all_to_all x8 -> x3, starting transfers between devices: 43.8 us -> 25.1 us  [exchange(): return lax.all_to_all(value, 'seq', split_axis=0, concat_axis=0, tiled=True)]
    all_to_all x1 -> x0, blocking collectives: 14.8 us -> none  [split_convolve(): lax.all_to_all(rows_real, 'seq', split_axis=0, concat_axis=1, tiled=True)]
    dot_general x31 -> x24, matrix products: 72.3 us -> 58.1 us  [project(): jnp.einsum('td,djc->jtc', activations, columns, preferred_element_type=jn...]
    slice x0 -> x8, local copies, waits for them, and re-layouts: none -> 12.4 us  [the longest x2 8.05 us: on_device(): kv_weight, q_weight = (proj_weight[:, 1:], proj_weight[:, :1])]
  transfers between devices with their start and end apart: 9 -> 33, of which waited for: 8 -> 11; matrix products, arithmetic and copies ran while one was open for 5% -> 38% of each run, Pallas kernels for 0% -> 3%
where the time goes in v1:
time: 217 us; the launch traced here: 216 us
  starting transfers between devices  59 us (27%)
  matrix products  58.1 us (27%)
  waiting for transfers between devices  54.2 us (25%)
  local copies, waits for them, and re-layouts  21.7 us (10%)
  other arithmetic  14.3 us (7%)
  Pallas kernels  7.82 us (4%)
    dot_general x24, matrix products, project(): jnp.einsum('td,djc->jtc', activations, columns, preferred_element_type=jn...  58.1 us
    ppermute x20, waiting for transfers between devices, shift_x(): lax.ppermute(value, 'chan', [(i, (i + 2 * step) % 8) for i in range(8)])  46.1 us
    ppermute x20, starting transfers between devices, shift_x(): lax.ppermute(value, 'chan', [(i, (i + 2 * step) % 8) for i in range(8)])  26.5 us
    all_to_all x3, starting transfers between devices, exchange(): return lax.all_to_all(value, 'seq', split_axis=0, concat_axis=0, tiled=True)  25.1 us
    slice x2, local copies, waits for them, and re-layouts, on_device(): kv_weight, q_weight = (proj_weight[:, 1:], proj_weight[:, :1])  8.05 us
    pallas_call x5, Pallas kernels, call(): pl.pallas_call(kernel, out_shape=jax.ShapeDtypeStruct(out_shape, jnp.floa...  7.82 us
    ppermute x10, starting transfers between devices, swap_z(): return lax.ppermute(value, 'chan', [(i, i ^ 1) for i in range(8)])  7.34 us
    ppermute x10, waiting for transfers between devices, swap_z(): return lax.ppermute(value, 'chan', [(i, i ^ 1) for i in range(8)])  5.4 us
  transfers between devices with their start and end apart: 33, of which 11 were waited for; matrix products, arithmetic and copies ran while one was open for 38% of the time, Pallas kernels for 3%

profile of v1, /device:TPU:1, one launch (start us, length us, event | category | flops | bytes accessed | tf_op | source)
XLA Modules:
  0.0 215.7 jit_solution(4330641191744836615)
XLA Ops:
  0.0 4.8 %slice.138 = bf16[1024,2,1024]{2,0,1:T(8,128)(2,1)} slice(bf16[1024,3,1024]{2,0,1:T(8,128)(2,1)} %param.14), slice={[0:1024], [1:3], [0:1024]} | slice | bytes 8388608 | tf_op jit(solution)/shard_map/slice | solution.py:220
  4.8 2.2 %convolution_bitcast_fusion.8 = f32[2,448,128]{2,1,0:T(8,128)} fusion(bf16[1024,2,1024]{2,0,1:T(8,128)(2,1)} %slice.138, s32[]{:T(128)S(6)} %select_n.230, bf16[1024,1024]{1,0:T(8,128)(2,1)S(1)} %copy-done.29), kind=kOutput, calls=%fused_computation.9 | convolution fusion | flops 234881024 | bytes 1900548 | tf_op jit(solution)/shard_map/td,djc->jtc/dot_general | solution.py:28
  7.0 2.5 %collective-permute-start = (f32[2,448,128]{2,1,0:T(8,128)}, f32[2,448,128]{2,1,0:T(8,128)S(1)}, u32[]{:S(2)}, u32[]{:S(2)}) collective-permute-start(f32[2,448,128]{2,1,0:T(8,128)} %convolution_bitcast_fusion.8), channel_id=1, source_target_pairs={{0,1},{1,0},{2,3},{3,2},{4,5},{5,4},{6,7},{7,6},{8,9},{9,8},{10,11... | collective-permute-start | bytes 1376264 | tf_op jit(solution)/shard_map/ppermute | solution.py:23
  9.5 2.3 %convolution_bitcast_fusion.6 = f32[2,448,128]{2,1,0:T(8,128)} fusion(bf16[1024,2,1024]{2,0,1:T(8,128)(2,1)} %slice.138, s32[]{:T(128)S(6)} %select_n.233, bf16[1024,1024]{1,0:T(8,128)(2,1)S(1)} %copy-done.29), kind=kOutput, calls=%fused_computation.7 | convolution fusion | flops 234881024 | bytes 1900548 | tf_op jit(solution)/shard_map/td,djc->jtc/dot_general | solution.py:28
  11.8 2.2 %convolution_bitcast_fusion.4 = f32[2,448,128]{2,1,0:T(8,128)} fusion(bf16[1024,2,1024]{2,0,1:T(8,128)(2,1)} %slice.138, s32[]{:T(128)S(6)} %select_n.236, bf16[1024,1024]{1,0:T(8,128)(2,1)S(1)} %copy-done.29), kind=kOutput, calls=%fused_computation.4 | convolution fusion | flops 234881024 | bytes 1900548 | tf_op jit(solution)/shard_map/td,djc->jtc/dot_general | solution.py:28
  16.6 9.0 %all-to-all-start.1 = ((f32[16,8,8,128]{3,2,1,0:T(8,128)}), f32[16,8,8,128]{3,2,1,0:T(8,128)S(1)}, u32[]{:S(2)}, u32[]{:S(2)}) async-start(f32[16,8,8,128]{3,2,1,0:T(8,128)} %bitcast.34), calls=%async_computation.1 | async-start | bytes 1048576 | tf_op jit(solution)/shard_map/all_to_all | solution.py:206
  25.6 3.2 %slice.161 = bf16[1024,1,1024]{2,0,1:T(8,128)(2,1)} slice(bf16[1024,3,1024]{2,0,1:T(8,128)(2,1)} %param.14), slice={[0:1024], [0:1], [0:1024]} | slice | bytes 4194304 | tf_op jit(solution)/shard_map/slice | solution.py:220
  28.9 2.1 fusion.55
  30.9 2.1 fusion.51
  34.5 2.3 %fusion.58 = f32[128,448]{0,1:T(8,128)} fusion(bf16[1024,1,1024]{2,0,1:T(8,128)(2,1)} %slice.161, s32[]{:T(128)S(6)} %select_n.230, bf16[1024,1024]{1,0:T(8,128)(2,1)} %param.13), kind=kOutput, calls=%fused_computation.95 | convolution fusion | flops 117440512 | bytes 1409028 | tf_op jit(solution)/shard_map/td,djc->jtc/dot_general | solution.py:28
  36.8 2.5 %convolution_bitcast_fusion.7 = f32[2,448,128]{2,1,0:T(8,128)} fusion(bf16[1024,2,1024]{2,0,1:T(8,128)(2,1)} %slice.138, s32[]{:T(128)S(6)} %select_n.232, bf16[1024,1024]{1,0:T(8,128)(2,1)} %param.13), kind=kOutput, calls=%fused_computation.8 | convolution fusion | flops 234881024 | bytes 1900548 | tf_op jit(solution)/shard_map/td,djc->jtc/dot_general | solution.py:28
  39.3 2.3 %convolution_bitcast_fusion.11 = f32[1,448,128]{2,1,0:T(8,128)} fusion(bf16[1024,1,1024]{2,0,1:T(8,128)(2,1)} %slice.161, s32[]{:T(128)S(6)} %select_n.232, bf16[1024,1024]{1,0:T(8,128)(2,1)} %param.13), kind=kOutput, calls=%fused_computation.19 | convolution fusion | flops 117440512 | bytes 1409028 | tf_op jit(solution)/shard_map/td,djc->jtc/dot_general | solution.py:28
  41.7 2.5 %convolution_bitcast_fusion.2 = f32[2,448,128]{2,1,0:T(8,128)} fusion(bf16[1024,2,1024]{2,0,1:T(8,128)(2,1)} %slice.138, s32[]{:T(128)S(6)} %select_n.239, bf16[1024,1024]{1,0:T(8,128)(2,1)} %param.13), kind=kOutput, calls=%fused_computation.2 | convolution fusion | flops 234881024 | bytes 1900548 | tf_op jit(solution)/shard_map/td,djc->jtc/dot_general | solution.py:28
  44.2 2.3 %fusion.48 = f32[128,448]{0,1:T(8,128)} fusion(bf16[1024,1,1024]{2,0,1:T(8,128)(2,1)} %slice.161, s32[]{:T(128)S(6)} %select_n.239, bf16[1024,1024]{1,0:T(8,128)(2,1)} %param.13), kind=kOutput, calls=%fused_computation.85 | convolution fusion | flops 117440512 | bytes 1409028 | tf_op jit(solution)/shard_map/td,djc->jtc/dot_general | solution.py:28
  46.5 2.5 %convolution_bitcast_fusion.3 = f32[2,448,128]{2,1,0:T(8,128)} fusion(bf16[1024,2,1024]{2,0,1:T(8,128)(2,1)} %slice.138, s32[]{:T(128)S(6)} %select_n.238, bf16[1024,1024]{1,0:T(8,128)(2,1)} %param.13), kind=kOutput, calls=%fused_computation.3 | convolution fusion | flops 234881024 | bytes 1900548 | tf_op jit(solution)/shard_map/td,djc->jtc/dot_general | solution.py:28
  49.0 2.3 %convolution_bitcast_fusion.10 = f32[1,448,128]{2,1,0:T(8,128)} fusion(bf16[1024,1,1024]{2,0,1:T(8,128)(2,1)} %slice.161, s32[]{:T(128)S(6)} %select_n.238, bf16[1024,1024]{1,0:T(8,128)(2,1)} %param.13), kind=kOutput, calls=%fused_computation.18 | convolution fusion | flops 117440512 | bytes 1409028 | tf_op jit(solution)/shard_map/td,djc->jtc/dot_general | solution.py:28
  51.3 3.5 %fusion.6 = f32[2,256,576]{1,2,0:T(8,128)} fusion(bf16[1024,2,1024]{2,0,1:T(8,128)(2,1)} %slice.138, s32[]{:T(128)S(6)} %select_n.244, bf16[1024,1024]{1,0:T(8,128)(2,1)} %param.13), kind=kOutput, calls=%fused_computation.16 | convolution fusion | flops 603979776 | bytes 3407876 | tf_op jit(solution)/shard_map/td,djc->jtc/dot_general | solution.py:28
  54.8 2.3 %fusion.21 = f32[256,576]{0,1:T(8,128)} fusion(bf16[1024,1,1024]{2,0,1:T(8,128)(2,1)} %slice.161, s32[]{:T(128)S(6)} %select_n.244, bf16[1024,1024]{1,0:T(8,128)(2,1)S(1)} %copy-done.31), kind=kOutput, calls=%fused_computation.45 | convolution fusion | flops 301989888 | bytes 2293764 | tf_op jit(solution)/shard_map/td,djc->jtc/dot_general | solution.py:28
  57.2 3.6 %convolution_bitcast_fusion = f32[2,576,256]{2,1,0:T(8,128)} fusion(bf16[1024,2,1024]{2,0,1:T(8,128)(2,1)} %slice.138, s32[]{:T(128)S(6)} %select_n.243, bf16[1024,1024]{1,0:T(8,128)(2,1)} %param.13), kind=kOutput, calls=%fused_computation | convolution fusion | flops 603979776 | bytes 3407876 | tf_op jit(solution)/shard_map/td,djc->jtc/dot_general | solution.py:28
  60.7 2.3 %convolution_bitcast_fusion.1 = f32[1,576,256]{2,1,0:T(8,128)} fusion(bf16[1024,1,1024]{2,0,1:T(8,128)(2,1)} %slice.161, s32[]{:T(128)S(6)} %select_n.243, bf16[1024,1024]{1,0:T(8,128)(2,1)S(1)} %copy-done.32), kind=kOutput, calls=%fused_computation.1 | convolution fusion | flops 301989888 | bytes 2293764 | tf_op jit(solution)/shard_map/td,djc->jtc/dot_general | solution.py:28
  63.0 3.5 %fusion.3 = f32[2,256,576]{1,2,0:T(8,128)} fusion(bf16[1024,2,1024]{2,0,1:T(8,128)(2,1)} %slice.138, s32[]{:T(128)S(6)} %select_n.242, bf16[1024,1024]{1,0:T(8,128)(2,1)} %param.13), kind=kOutput, calls=%fused_computation.13 | convolution fusion | flops 603979776 | bytes 3407876 | tf_op jit(solution)/shard_map/td,djc->jtc/dot_general | solution.py:28
  66.5 2.4 %fusion.24 = f32[256,576]{0,1:T(8,128)} fusion(bf16[1024,1,1024]{2,0,1:T(8,128)(2,1)} %slice.161, s32[]{:T(128)S(6)} %select_n.242, bf16[1024,1024]{1,0:T(8,128)(2,1)S(1)} %copy-done.33), kind=kOutput, calls=%fused_computation.48 | convolution fusion | flops 301989888 | bytes 2293764 | tf_op jit(solution)/shard_map/td,djc->jtc/dot_general | solution.py:28
  68.9 2.5 %fusion.1 = f32[2,256,576]{1,2,0:T(8,128)S(1)} fusion(bf16[1024,2,1024]{2,0,1:T(8,128)(2,1)} %slice.138, s32[]{:T(128)S(6)} %select_n.240, bf16[1024,1024]{1,0:T(8,128)(2,1)} %param.13), kind=kOutput, calls=%fused_computation.11 | convolution fusion | flops 603979776 | bytes 3407876 | tf_op jit(solution)/shard_map/td,djc->jtc/dot_general | solution.py:28
  71.5 2.8 %fusion.26 = f32[256,576]{0,1:T(8,128)} fusion(bf16[1024,1,1024]{2,0,1:T(8,128)(2,1)} %slice.161, s32[]{:T(128)S(6)} %select_n.240, bf16[1024,1024]{1,0:T(8,128)(2,1)S(1)} %copy-done.34), kind=kOutput, calls=%fused_computation.50 | convolution fusion | flops 301989888 | bytes 2293764 | tf_op jit(solution)/shard_map/td,djc->jtc/dot_general | solution.py:28
  74.3 1.7 convolution_bitcast_fusion.9.z0
  76.1 1.9 dynamic-slice_bitcast_fusion
  81.5 2.3 %fusion.53 = f32[128,448]{0,1:T(8,128)} fusion(bf16[1024,1,1024]{2,0,1:T(8,128)(2,1)} %slice.161, s32[]{:T(128)S(6)} %select_n.235, bf16[1024,1024]{1,0:T(8,128)(2,1)} %param.13), kind=kOutput, calls=%fused_computation.90 | convolution fusion | flops 117440512 | bytes 1409028 | tf_op jit(solution)/shard_map/td,djc->jtc/dot_general | solution.py:28
  89.0 2.5 %collective-permute-start.25 = (f32[288,256]{1,0:T(8,128)S(1)}, f32[288,256]{1,0:T(8,128)S(1)}, u32[]{:S(2)}, u32[]{:S(2)}) collective-permute-start(f32[288,256]{1,0:T(8,128)S(1)} %get-tuple-element.21), channel_id=1, source_target_pairs={{0,6},{1,7},{2,0},{3,1},{4,2},{5,3},{6,4},{7,5},{8,14},{9,15},{10,... | collective-permute-start | bytes 884744 | tf_op jit(solution)/shard_map/ppermute | solution.py:19
  95.2 1.9 collective-permute-done.25
  98.9 2.6 %collective-permute-start.10 = (f32[576,256]{1,0:T(8,128)S(1)}, f32[576,256]{1,0:T(8,128)S(1)}, u32[]{:S(2)}, u32[]{:S(2)}) collective-permute-start(f32[576,256]{1,0:T(8,128)S(1)} %copy-done.24), channel_id=1, source_target_pairs={{0,6},{1,7},{2,0},{3,1},{4,2},{5,3},{6,4},{7,5},{8,14},{9,15},{10,... | collective-permute-start | bytes 1769480 | tf_op jit(solution)/shard_map/ppermute | solution.py:19
  101.5 1.9 fusion
  105.6 7.0 %collective-permute-done.10 = f32[576,256]{1,0:T(8,128)S(1)} collective-permute-done((f32[576,256]{1,0:T(8,128)S(1)}, f32[576,256]{1,0:T(8,128)S(1)}, u32[]{:S(2)}, u32[]{:S(2)}) %collective-permute-start.10) | collective-permute-done | bytes 589856 | tf_op jit(solution)/shard_map/ppermute | solution.py:19
  112.6 3.4 %collective-permute-start.6 = (f32[448,128]{1,0:T(8,128)S(1)}, f32[448,128]{1,0:T(8,128)S(1)}, u32[]{:S(2)}, u32[]{:S(2)}) collective-permute-start(f32[448,128]{1,0:T(8,128)S(1)} %get-tuple-element.27), channel_id=1, source_target_pairs={{0,6},{1,7},{2,0},{3,1},{4,2},{5,3},{6,4},{7,5},{8,14},{9,15},{10,... | collective-permute-start | bytes 688136 | tf_op jit(solution)/shard_map/ppermute | solution.py:19
  117.2 6.8 %collective-permute-done.3 = f32[448,128]{1,0:T(8,128)S(1)} collective-permute-done((f32[448,128]{1,0:T(8,128)S(1)}, f32[448,128]{1,0:T(8,128)S(1)}, u32[]{:S(2)}, u32[]{:S(2)}) %collective-permute-start.3) | collective-permute-done | bytes 229408 | tf_op jit(solution)/shard_map/ppermute | solution.py:19
  125.1 6.4 %collective-permute-done.13 = f32[2,576,128]{2,1,0:T(8,128)S(1)} collective-permute-done((f32[2,576,128]{2,1,0:T(8,128)S(1)}, f32[2,576,128]{2,1,0:T(8,128)S(1)}, u32[]{:S(2)}, u32[]{:S(2)}) %collective-permute-start.13) | collective-permute-done | bytes 589856 | tf_op jit(solution)/shard_map/ppermute | solution.py:19
  131.5 3.0 %collective-permute-start.11 = (f32[2,576,128]{2,1,0:T(8,128)S(1)}, f32[2,576,128]{2,1,0:T(8,128)S(1)}, u32[]{:S(2)}, u32[]{:S(2)}) collective-permute-start(f32[2,576,128]{2,1,0:T(8,128)S(1)} %pad_maximum_fusion.1), channel_id=1, source_target_pairs={{0,6},{1,7},{2,0},{3,1},{4,2},{5,3},{6,4},{7,5},{8,14},{9,15},{10,... | collective-permute-start | bytes 1769480 | tf_op jit(solution)/shard_map/ppermute | solution.py:19
  134.5 3.3 %collective-permute-done.12 = f32[2,576,128]{2,1,0:T(8,128)S(1)} collective-permute-done((f32[2,576,128]{2,1,0:T(8,128)S(1)}, f32[2,576,128]{2,1,0:T(8,128)S(1)}, u32[]{:S(2)}, u32[]{:S(2)}) %collective-permute-start.12) | collective-permute-done | bytes 589856 | tf_op jit(solution)/shard_map/ppermute | solution.py:19
  138.5 2.7 %collective-permute-start.7 = (f32[2,448,128]{2,1,0:T(8,128)S(1)}, f32[2,448,128]{2,1,0:T(8,128)S(1)}, u32[]{:S(2)}, u32[]{:S(2)}) collective-permute-start(f32[2,448,128]{2,1,0:T(8,128)S(1)} %pad_maximum_fusion.5), channel_id=1, source_target_pairs={{0,6},{1,7},{2,0},{3,1},{4,2},{5,3},{6,4},{7,5},{8,14},{9,15},{10,... | collective-permute-start | bytes 1376264 | tf_op jit(solution)/shard_map/ppermute | solution.py:19
  142.8 17.5 %collective-permute-done.4.z2 = f32[2,448,128]{2,1,0:T(8,128)S(1)} collective-permute-done((f32[2,448,128]{2,1,0:T(8,128)S(1)}, f32[2,448,128]{2,1,0:T(8,128)S(1)}, u32[]{:S(2)}, u32[]{:S(2)}) %collective-permute-start.4) | collective-permute-done | bytes 458784 | tf_op jit(solution)/shard_map/ppermute | solution.py:19
  161.5 2.7 %collective-permute-start.21 = (f32[224,128]{1,0:T(8,128)}, f32[224,128]{1,0:T(8,128)}, u32[]{:S(2)}, u32[]{:S(2)}) collective-permute-start(f32[224,128]{1,0:T(8,128)} %get-tuple-element.29), channel_id=1, source_target_pairs={{0,6},{1,7},{2,0},{3,1},{4,2},{5,3},{6,4},{7,5},{8,14},{9,15},{10,... | collective-permute-start | bytes 344072 | tf_op jit(solution)/shard_map/ppermute | solution.py:19
  167.6 11.2 %all-to-all-start = ((f32[16,8,8,128]{3,2,1,0:T(8,128)}), f32[16,8,8,128]{3,2,1,0:T(8,128)S(1)}, u32[]{:S(2)}, u32[]{:S(2)}) async-start(f32[16,8,8,128]{3,2,1,0:T(8,128)} %bitcast.33), calls=%async_computation | async-start | bytes 1048576 | tf_op jit(solution)/shard_map/all_to_all | solution.py:206
  181.4 3.0 %collective-permute-start.26 = (f32[2,288,128]{2,1,0:T(8,128)}, f32[2,288,128]{2,1,0:T(8,128)S(1)}, u32[]{:S(2)}, u32[]{:S(2)}) collective-permute-start(f32[2,288,128]{2,1,0:T(8,128)} %pad_maximum_fusion.7), channel_id=1, source_target_pairs={{0,6},{1,7},{2,0},{3,1},{4,2},{5,3},{6,4},{7,5},{8,14},{9,15},{10,... | collective-permute-start | bytes 884744 | tf_op jit(solution)/shard_map/ppermute | solution.py:19
  187.2 2.7 %all-to-all-done.kv_ref = f32[16,8,8,128]{3,2,1,0:T(8,128)S(1)} async-done(((f32[16,8,8,128]{3,2,1,0:T(8,128)}), f32[16,8,8,128]{3,2,1,0:T(8,128)S(1)}, u32[]{:S(2)}, u32[]{:S(2)}) %all-to-all-start) | async-done | bytes 524320 | tf_op jit(solution)/shard_map/all_to_all | solution.py:206
  192.6 3.2 %shard_map.130 = f32[16,8,8,128]{3,2,1,0:T(8,128)} custom-call(f32[16,8,8,128]{3,2,1,0:T(8,128)S(1)} %all-to-all-done.kv_ref, f32[1024,256]{1,0:T(8,128)S(1)} %shard_map.129.spec_ref, bf16[256,128]{1,0:T(8,128)(2,1)S(1)} %copy-done.3, bf16[256,128]{1,0:T(8,128)(2,1)S(1)} %copy-done.4, f32[128,128]{1,0:T(8,128)S(1)} %copy-done.5, f32[128,128]{1,0:T(8,128)S(1)} %copy-done.6, ...), custom_call_target="tpu_custom_call" | custom-call | tf_op jit(solution)/shard_map/pallas_call | solution.py:197
  195.8 4.9 %all-to-all-start.2 = ((f32[16,8,8,128]{3,2,1,0:T(8,128)}), f32[16,8,8,128]{3,2,1,0:T(8,128)S(1)}, u32[]{:S(2)}, u32[]{:S(2)}) async-start(f32[16,8,8,128]{3,2,1,0:T(8,128)} %shard_map.130), calls=%async_computation.2 | async-start | bytes 1048576 | tf_op jit(solution)/shard_map/all_to_all | solution.py:206
  202.2 2.9 %collective-permute-start.22 = (f32[2,224,128]{2,1,0:T(8,128)S(1)}, f32[2,224,128]{2,1,0:T(8,128)S(1)}, u32[]{:S(2)}, u32[]{:S(2)}) collective-permute-start(f32[2,224,128]{2,1,0:T(8,128)S(1)} %pad_maximum_fusion.11), channel_id=1, source_target_pairs={{0,6},{1,7},{2,0},{3,1},{4,2},{5,3},{6,4},{7,5},{8,14},{9,15},{10,... | collective-permute-start | bytes 688136 | tf_op jit(solution)/shard_map/ppermute | solution.py:19
  206.8 2.8 %collective-permute-done.19.z2 = f32[2,224,128]{2,1,0:T(8,128)S(1)} collective-permute-done((f32[2,224,128]{2,1,0:T(8,128)}, f32[2,224,128]{2,1,0:T(8,128)S(1)}, u32[]{:S(2)}, u32[]{:S(2)}) %collective-permute-start.19) | collective-permute-done | bytes 229408 | tf_op jit(solution)/shard_map/ppermute | solution.py:19
  210.0 4.6 %collective-permute-done.29.x3 = f32[2,288,128]{2,1,0:T(8,128)S(1)} collective-permute-done((f32[2,288,128]{2,1,0:T(8,128)S(1)}, f32[2,288,128]{2,1,0:T(8,128)S(1)}, u32[]{:S(2)}, u32[]{:S(2)}) %collective-permute-start.29) | collective-permute-done | bytes 294944 | tf_op jit(solution)/shard_map/ppermute | solution.py:23
  (172 shorter events, 42.1 us)
Async XLA Ops:
  7.0 131.5 %collective-permute-start = (f32[2,448,128]{2,1,0:T(8,128)}, f32[2,448,128]{2,1,0:T(8,128)S(1)}, u32[]{:S(2)}, u32[]{:S(2)}) collective-permute-start(f32[2,448,128]{2,1,0:T(8,128)} %convolution_bitcast_fusion.8), channel_id=1, source_target_pairs={{0,1},{1,0},{2,3},{3,2},{4,5},{5,4},{6,7},{7,6},{8,9},{9,8},{10,11... | collective-permute-start | bytes 1376264 | tf_op jit(solution)/shard_map/ppermute | solution.py:23
  11.8 91.6 %collective-permute-start.1 = (f32[2,448,128]{2,1,0:T(8,128)}, f32[2,448,128]{2,1,0:T(8,128)}, u32[]{:S(2)}, u32[]{:S(2)}) collective-permute-start(f32[2,448,128]{2,1,0:T(8,128)} %convolution_bitcast_fusion.6), channel_id=1, source_target_pairs={{0,1},{1,0},{2,3},{3,2},{4,5},{5,4},{6,7},{7,6},{8,9},{9,8},{10,11... | collective-permute-start | bytes 1376264 | tf_op jit(solution)/shard_map/ppermute | solution.py:23
  14.0 84.9 %collective-permute-start.2 = (f32[2,448,128]{2,1,0:T(8,128)}, f32[2,448,128]{2,1,0:T(8,128)}, u32[]{:S(2)}, u32[]{:S(2)}) collective-permute-start(f32[2,448,128]{2,1,0:T(8,128)} %convolution_bitcast_fusion.4), channel_id=1, source_target_pairs={{0,1},{1,0},{2,3},{3,2},{4,5},{5,4},{6,7},{7,6},{8,9},{9,8},{10,11... | collective-permute-start | bytes 1376264 | tf_op jit(solution)/shard_map/ppermute | solution.py:23
  16.6 151.0 %all-to-all-start.1 = ((f32[16,8,8,128]{3,2,1,0:T(8,128)}), f32[16,8,8,128]{3,2,1,0:T(8,128)S(1)}, u32[]{:S(2)}, u32[]{:S(2)}) async-start(f32[16,8,8,128]{3,2,1,0:T(8,128)} %bitcast.34), calls=%async_computation.1 | async-start | bytes 1048576 | tf_op jit(solution)/shard_map/all_to_all | solution.py:206
  30.9 58.0 %collective-permute-start.16 = (f32[2,224,128]{2,1,0:T(8,128)}, f32[2,224,128]{2,1,0:T(8,128)}, u32[]{:S(2)}, u32[]{:S(2)}) collective-permute-start(f32[2,224,128]{2,1,0:T(8,128)} %bitcast.50), channel_id=1, source_target_pairs={{0,1},{1,0},{2,3},{3,2},{4,5},{5,4},{6,7},{7,6},{8,9},{9,8},{10,11... | collective-permute-start | bytes 688136 | tf_op jit(solution)/shard_map/ppermute | solution.py:23
  33.0 54.2 %collective-permute-start.17 = (f32[2,224,128]{2,1,0:T(8,128)}, f32[2,224,128]{2,1,0:T(8,128)}, u32[]{:S(2)}, u32[]{:S(2)}) collective-permute-start(f32[2,224,128]{2,1,0:T(8,128)} %bitcast.59), channel_id=1, source_target_pairs={{0,1},{1,0},{2,3},{3,2},{4,5},{5,4},{6,7},{7,6},{8,9},{9,8},{10,11... | collective-permute-start | bytes 688136 | tf_op jit(solution)/shard_map/ppermute | solution.py:23
  83.9 13.3 %copy-start.23 = (f32[576,256]{1,0:T(8,128)S(1)}, f32[576,256]{1,0:T(8,128)}, u32[]{:S(2)}) copy-start(f32[576,256]{1,0:T(8,128)} %get-tuple-element.10) | copy-start | bytes 1769476
  83.9 14.2 %copy-start.21 = (f32[256,576]{0,1:T(8,128)S(1)}, f32[256,576]{0,1:T(8,128)}, u32[]{:S(2)}) copy-start(f32[256,576]{0,1:T(8,128)} %fusion.21) | copy-start | bytes 1769476
  86.1 12.8 %copy-start.24 = (f32[576,256]{1,0:T(8,128)S(1)}, f32[576,256]{1,0:T(8,128)}, u32[]{:S(2)}) copy-start(f32[576,256]{1,0:T(8,128)} %get-tuple-element.9) | copy-start | bytes 1769476
  87.2 6.6 %collective-permute-start.20 = (f32[2,224,128]{2,1,0:T(8,128)S(1)}, f32[2,224,128]{2,1,0:T(8,128)S(1)}, u32[]{:S(2)}, u32[]{:S(2)}) collective-permute-start(f32[2,224,128]{2,1,0:T(8,128)S(1)} %bitcast.276), channel_id=1, source_target_pairs={{0,1},{1,0},{2,3},{3,2},{4,5},{5,4},{6,7},{7,6},{8,9},{9,8},{10,11... | collective-permute-start | bytes 688136 | tf_op jit(solution)/shard_map/ppermute | solution.py:23
  89.0 8.2 %collective-permute-start.25 = (f32[288,256]{1,0:T(8,128)S(1)}, f32[288,256]{1,0:T(8,128)S(1)}, u32[]{:S(2)}, u32[]{:S(2)}) collective-permute-start(f32[288,256]{1,0:T(8,128)S(1)} %get-tuple-element.21), channel_id=1, source_target_pairs={{0,6},{1,7},{2,0},{3,1},{4,2},{5,3},{6,4},{7,5},{8,14},{9,15},{10,... | collective-permute-start | bytes 884744 | tf_op jit(solution)/shard_map/ppermute | solution.py:19
  93.8 10.6 %collective-permute-start.5 = (f32[2,448,128]{2,1,0:T(8,128)S(1)}, f32[2,448,128]{2,1,0:T(8,128)S(1)}, u32[]{:S(2)}, u32[]{:S(2)}) collective-permute-start(f32[2,448,128]{2,1,0:T(8,128)S(1)} %copy-done.40), channel_id=1, source_target_pairs={{0,1},{1,0},{2,3},{3,2},{4,5},{5,4},{6,7},{7,6},{8,9},{9,8},{10,11... | collective-permute-start | bytes 1376264 | tf_op jit(solution)/shard_map/ppermute | solution.py:23
  97.2 19.0 %collective-permute-start.8 = (f32[576,256]{1,0:T(8,128)S(1)}, f32[576,256]{1,0:T(8,128)S(1)}, u32[]{:S(2)}, u32[]{:S(2)}) collective-permute-start(f32[576,256]{1,0:T(8,128)S(1)} %copy-done.23), channel_id=1, source_target_pairs={{0,2},{1,3},{2,4},{3,5},{4,6},{5,7},{6,0},{7,1},{8,10},{9,11},{10,... | collective-permute-start | bytes 1769480 | tf_op jit(solution)/shard_map/ppermute | solution.py:19
  98.9 17.1 %copy-start.12 = (f32[2,576,128]{2,1,0:T(8,128)S(1)}, f32[2,576,128]{2,1,0:T(8,128)}, u32[]{:S(2)}) copy-start(f32[2,576,128]{2,1,0:T(8,128)} %copy-done.11) | copy-start | bytes 1769476
  98.9 17.1 %copy-start.14 = (f32[2,576,128]{2,1,0:T(8,128)S(1)}, f32[2,576,128]{2,1,0:T(8,128)}, u32[]{:S(2)}) copy-start(f32[2,576,128]{2,1,0:T(8,128)} %copy-done.13) | copy-start | bytes 1769476
  98.9 13.7 %collective-permute-start.10 = (f32[576,256]{1,0:T(8,128)S(1)}, f32[576,256]{1,0:T(8,128)S(1)}, u32[]{:S(2)}, u32[]{:S(2)}) collective-permute-start(f32[576,256]{1,0:T(8,128)S(1)} %copy-done.24), channel_id=1, source_target_pairs={{0,6},{1,7},{2,0},{3,1},{4,2},{5,3},{6,4},{7,5},{8,14},{9,15},{10,... | collective-permute-start | bytes 1769480 | tf_op jit(solution)/shard_map/ppermute | solution.py:19
  103.3 12.7 %copy-start.20 = (f32[1,576,128]{2,1,0:T(8,128)S(1)}, f32[1,576,128]{2,1,0:T(8,128)}, u32[]{:S(2)}) copy-start(f32[1,576,128]{2,1,0:T(8,128)} %slice.200) | copy-start | bytes 884740
  103.4 34.5 %collective-permute-start.23 = (f32[288,256]{1,0:T(8,128)S(1)}, f32[288,256]{1,0:T(8,128)S(1)}, u32[]{:S(2)}, u32[]{:S(2)}) collective-permute-start(f32[288,256]{1,0:T(8,128)S(1)} %get-tuple-element.22), channel_id=1, source_target_pairs={{0,2},{1,3},{2,4},{3,5},{4,6},{5,7},{6,0},{7,1},{8,10},{9,11},{10,... | collective-permute-start | bytes 884744 | tf_op jit(solution)/shard_map/ppermute | solution.py:19
  104.5 19.5 %collective-permute-start.3 = (f32[448,128]{1,0:T(8,128)S(1)}, f32[448,128]{1,0:T(8,128)S(1)}, u32[]{:S(2)}, u32[]{:S(2)}) collective-permute-start(f32[448,128]{1,0:T(8,128)S(1)} %get-tuple-element.28), channel_id=1, source_target_pairs={{0,2},{1,3},{2,4},{3,5},{4,6},{5,7},{6,0},{7,1},{8,10},{9,11},{10,... | collective-permute-start | bytes 688136 | tf_op jit(solution)/shard_map/ppermute | solution.py:19
  112.6 12.3 %collective-permute-start.6 = (f32[448,128]{1,0:T(8,128)S(1)}, f32[448,128]{1,0:T(8,128)S(1)}, u32[]{:S(2)}, u32[]{:S(2)}) collective-permute-start(f32[448,128]{1,0:T(8,128)S(1)} %get-tuple-element.27), channel_id=1, source_target_pairs={{0,6},{1,7},{2,0},{3,1},{4,2},{5,3},{6,4},{7,5},{8,14},{9,15},{10,... | collective-permute-start | bytes 688136 | tf_op jit(solution)/shard_map/ppermute | solution.py:19
  116.2 15.4 %collective-permute-start.13 = (f32[2,576,128]{2,1,0:T(8,128)S(1)}, f32[2,576,128]{2,1,0:T(8,128)S(1)}, u32[]{:S(2)}, u32[]{:S(2)}) collective-permute-start(f32[2,576,128]{2,1,0:T(8,128)S(1)} %pad_maximum_fusion.3), channel_id=1, source_target_pairs={{0,6},{1,7},{2,0},{3,1},{4,2},{5,3},{6,4},{7,5},{8,14},{9,15},{10,... | collective-permute-start | bytes 1769480 | tf_op jit(solution)/shard_map/ppermute | solution.py:19
  117.1 20.8 %copy-start.16 = (f32[2,256,576]{1,2,0:T(8,128)S(1)}, f32[2,256,576]{1,2,0:T(8,128)}, u32[]{:S(2)}) copy-start(f32[2,256,576]{1,2,0:T(8,128)} %copy-done.15) | copy-start | bytes 3538948
  123.9 13.9 %collective-permute-start.12 = (f32[2,576,128]{2,1,0:T(8,128)S(1)}, f32[2,576,128]{2,1,0:T(8,128)S(1)}, u32[]{:S(2)}, u32[]{:S(2)}) collective-permute-start(f32[2,576,128]{2,1,0:T(8,128)S(1)} %pad_maximum_fusion.2), channel_id=1, source_target_pairs={{0,2},{1,3},{2,4},{3,5},{4,6},{5,7},{6,0},{7,1},{8,10},{9,11},{10,... | collective-permute-start | bytes 1769480 | tf_op jit(solution)/shard_map/ppermute | solution.py:19
  124.9 36.6 %collective-permute-start.9 = (f32[2,576,128]{2,1,0:T(8,128)S(1)}, f32[2,576,128]{2,1,0:T(8,128)S(1)}, u32[]{:S(2)}, u32[]{:S(2)}) collective-permute-start(f32[2,576,128]{2,1,0:T(8,128)S(1)} %pad_maximum_fusion), channel_id=1, source_target_pairs={{0,2},{1,3},{2,4},{3,5},{4,6},{5,7},{6,0},{7,1},{8,10},{9,11},{10,... | collective-permute-start | bytes 1769480 | tf_op jit(solution)/shard_map/ppermute | solution.py:19
  125.1 16.2 %copy-start.22 = (f32[256,576]{0,1:T(8,128)S(1)}, f32[256,576]{0,1:T(8,128)}, u32[]{:S(2)}) copy-start(f32[256,576]{0,1:T(8,128)} %fusion.24) | copy-start | bytes 1769476
  131.5 32.7 %collective-permute-start.11 = (f32[2,576,128]{2,1,0:T(8,128)S(1)}, f32[2,576,128]{2,1,0:T(8,128)S(1)}, u32[]{:S(2)}, u32[]{:S(2)}) collective-permute-start(f32[2,576,128]{2,1,0:T(8,128)S(1)} %pad_maximum_fusion.1), channel_id=1, source_target_pairs={{0,6},{1,7},{2,0},{3,1},{4,2},{5,3},{6,4},{7,5},{8,14},{9,15},{10,... | collective-permute-start | bytes 1769480 | tf_op jit(solution)/shard_map/ppermute | solution.py:19
  137.8 22.5 %collective-permute-start.4 = (f32[2,448,128]{2,1,0:T(8,128)S(1)}, f32[2,448,128]{2,1,0:T(8,128)S(1)}, u32[]{:S(2)}, u32[]{:S(2)}) collective-permute-start(f32[2,448,128]{2,1,0:T(8,128)S(1)} %pad_maximum_fusion.4), channel_id=1, source_target_pairs={{0,2},{1,3},{2,4},{3,5},{4,6},{5,7},{6,0},{7,1},{8,10},{9,11},{10,... | collective-permute-start | bytes 1376264 | tf_op jit(solution)/shard_map/ppermute | solution.py:19
  138.0 26.3 %collective-permute-start.14 = (f32[2,576,128]{2,1,0:T(8,128)S(1)}, f32[2,576,128]{2,1,0:T(8,128)S(1)}, u32[]{:S(2)}, u32[]{:S(2)}) collective-permute-start(f32[2,576,128]{2,1,0:T(8,128)S(1)} %fusion.20), channel_id=1, source_target_pairs={{0,1},{1,0},{2,3},{3,2},{4,5},{5,4},{6,7},{7,6},{8,9},{9,8},{10,11... | collective-permute-start | bytes 1769480 | tf_op jit(solution)/shard_map/ppermute | solution.py:23
  138.5 22.5 %collective-permute-start.7 = (f32[2,448,128]{2,1,0:T(8,128)S(1)}, f32[2,448,128]{2,1,0:T(8,128)S(1)}, u32[]{:S(2)}, u32[]{:S(2)}) collective-permute-start(f32[2,448,128]{2,1,0:T(8,128)S(1)} %pad_maximum_fusion.5), channel_id=1, source_target_pairs={{0,6},{1,7},{2,0},{3,1},{4,2},{5,3},{6,4},{7,5},{8,14},{9,15},{10,... | collective-permute-start | bytes 1376264 | tf_op jit(solution)/shard_map/ppermute | solution.py:19
  160.3 6.6 %collective-permute-start.18 = (f32[224,128]{1,0:T(8,128)S(1)}, f32[224,128]{1,0:T(8,128)S(1)}, u32[]{:S(2)}, u32[]{:S(2)}) collective-permute-start(f32[224,128]{1,0:T(8,128)S(1)} %get-tuple-element.30), channel_id=1, source_target_pairs={{0,2},{1,3},{2,4},{3,5},{4,6},{5,7},{6,0},{7,1},{8,10},{9,11},{10,... | collective-permute-start | bytes 344072 | tf_op jit(solution)/shard_map/ppermute | solution.py:19
  161.0 41.2 %collective-permute-start.15 = (f32[2,224,128]{2,1,0:T(8,128)}, f32[2,224,128]{2,1,0:T(8,128)S(1)}, u32[]{:S(2)}, u32[]{:S(2)}) collective-permute-start(f32[2,224,128]{2,1,0:T(8,128)} %bitcast.43), channel_id=1, source_target_pairs={{0,1},{1,0},{2,3},{3,2},{4,5},{5,4},{6,7},{7,6},{8,9},{9,8},{10,11... | collective-permute-start | bytes 688136 | tf_op jit(solution)/shard_map/ppermute | solution.py:23
  161.5 19.9 %collective-permute-start.21 = (f32[224,128]{1,0:T(8,128)}, f32[224,128]{1,0:T(8,128)}, u32[]{:S(2)}, u32[]{:S(2)}) collective-permute-start(f32[224,128]{1,0:T(8,128)} %get-tuple-element.29), channel_id=1, source_target_pairs={{0,6},{1,7},{2,0},{3,1},{4,2},{5,3},{6,4},{7,5},{8,14},{9,15},{10,... | collective-permute-start | bytes 344072 | tf_op jit(solution)/shard_map/ppermute | solution.py:19
  164.2 36.5 %collective-permute-start.28 = (f32[2,288,128]{2,1,0:T(8,128)}, f32[2,288,128]{2,1,0:T(8,128)}, u32[]{:S(2)}, u32[]{:S(2)}) collective-permute-start(f32[2,288,128]{2,1,0:T(8,128)} %pad_maximum_fusion.9), channel_id=1, source_target_pairs={{0,6},{1,7},{2,0},{3,1},{4,2},{5,3},{6,4},{7,5},{8,14},{9,15},{10,... | collective-permute-start | bytes 884744 | tf_op jit(solution)/shard_map/ppermute | solution.py:19
  164.3 36.5 %collective-permute-start.27 = (f32[2,288,128]{2,1,0:T(8,128)}, f32[2,288,128]{2,1,0:T(8,128)}, u32[]{:S(2)}, u32[]{:S(2)}) collective-permute-start(f32[2,288,128]{2,1,0:T(8,128)} %pad_maximum_fusion.8), channel_id=1, source_target_pairs={{0,2},{1,3},{2,4},{3,5},{4,6},{5,7},{6,0},{7,1},{8,10},{9,11},{10,... | collective-permute-start | bytes 884744 | tf_op jit(solution)/shard_map/ppermute | solution.py:19
  166.9 19.2 %copy-start = (bf16[256,256]{1,0:T(8,128)(2,1)S(1)}, bf16[256,256]{1,0:T(8,128)(2,1)}, u32[]{:S(2)}) copy-start(bf16[256,256]{1,0:T(8,128)(2,1)} %constant.215.clone.s_hi) | copy-start | bytes 393220
  166.9 19.2 %copy-start.1 = (bf16[256,256]{1,0:T(8,128)(2,1)S(1)}, bf16[256,256]{1,0:T(8,128)(2,1)}, u32[]{:S(2)}) copy-start(bf16[256,256]{1,0:T(8,128)(2,1)} %constant.216.clone.s_lo) | copy-start | bytes 393220
  166.9 19.2 %copy-start.3 = (bf16[256,128]{1,0:T(8,128)(2,1)S(1)}, bf16[256,128]{1,0:T(8,128)(2,1)}, u32[]{:S(2)}) copy-start(bf16[256,128]{1,0:T(8,128)(2,1)} %constant.211.clone.f_hi) | copy-start | bytes 196612
  166.9 19.2 %copy-start.4 = (bf16[256,128]{1,0:T(8,128)(2,1)S(1)}, bf16[256,128]{1,0:T(8,128)(2,1)}, u32[]{:S(2)}) copy-start(bf16[256,128]{1,0:T(8,128)(2,1)} %constant.212.clone.f_lo) | copy-start | bytes 196612
  166.9 19.2 %copy-start.5 = (f32[128,128]{1,0:T(8,128)S(1)}, f32[128,128]{1,0:T(8,128)}, u32[]{:S(2)}) copy-start(f32[128,128]{1,0:T(8,128)} %constant.213.clone.t_re) | copy-start | bytes 196612
  166.9 19.2 %copy-start.6 = (f32[128,128]{1,0:T(8,128)S(1)}, f32[128,128]{1,0:T(8,128)}, u32[]{:S(2)}) copy-start(f32[128,128]{1,0:T(8,128)} %constant.214.clone.t_im) | copy-start | bytes 196612
  167.6 42.4 %collective-permute-start.24 = (f32[2,288,128]{2,1,0:T(8,128)}, f32[2,288,128]{2,1,0:T(8,128)S(1)}, u32[]{:S(2)}, u32[]{:S(2)}) collective-permute-start(f32[2,288,128]{2,1,0:T(8,128)} %pad_maximum_fusion.6), channel_id=1, source_target_pairs={{0,2},{1,3},{2,4},{3,5},{4,6},{5,7},{6,0},{7,1},{8,10},{9,11},{10,... | collective-permute-start | bytes 884744 | tf_op jit(solution)/shard_map/ppermute | solution.py:19
  167.6 22.3 %copy-start.9 = (bf16[128,256]{1,0:T(8,128)(2,1)S(1)}, bf16[128,256]{1,0:T(8,128)(2,1)}, u32[]{:S(2)}) copy-start(bf16[128,256]{1,0:T(8,128)(2,1)} %constant.219.clone.i_hi) | copy-start | bytes 196612
  167.6 22.3 %all-to-all-start = ((f32[16,8,8,128]{3,2,1,0:T(8,128)}), f32[16,8,8,128]{3,2,1,0:T(8,128)S(1)}, u32[]{:S(2)}, u32[]{:S(2)}) async-start(f32[16,8,8,128]{3,2,1,0:T(8,128)} %bitcast.33), calls=%async_computation | async-start | bytes 1048576 | tf_op jit(solution)/shard_map/all_to_all | solution.py:206
  181.4 28.5 %collective-permute-start.26 = (f32[2,288,128]{2,1,0:T(8,128)}, f32[2,288,128]{2,1,0:T(8,128)S(1)}, u32[]{:S(2)}, u32[]{:S(2)}) collective-permute-start(f32[2,288,128]{2,1,0:T(8,128)} %pad_maximum_fusion.7), channel_id=1, source_target_pairs={{0,6},{1,7},{2,0},{3,1},{4,2},{5,3},{6,4},{7,5},{8,14},{9,15},{10,... | collective-permute-start | bytes 884744 | tf_op jit(solution)/shard_map/ppermute | solution.py:19
  195.8 18.7 %all-to-all-start.2 = ((f32[16,8,8,128]{3,2,1,0:T(8,128)}), f32[16,8,8,128]{3,2,1,0:T(8,128)S(1)}, u32[]{:S(2)}, u32[]{:S(2)}) async-start(f32[16,8,8,128]{3,2,1,0:T(8,128)} %shard_map.130), calls=%async_computation.2 | async-start | bytes 1048576 | tf_op jit(solution)/shard_map/all_to_all | solution.py:206
  200.7 9.0 %collective-permute-start.19 = (f32[2,224,128]{2,1,0:T(8,128)}, f32[2,224,128]{2,1,0:T(8,128)S(1)}, u32[]{:S(2)}, u32[]{:S(2)}) collective-permute-start(f32[2,224,128]{2,1,0:T(8,128)} %pad_maximum_fusion.10), channel_id=1, source_target_pairs={{0,2},{1,3},{2,4},{3,5},{4,6},{5,7},{6,0},{7,1},{8,10},{9,11},{10,... | collective-permute-start | bytes 688136 | tf_op jit(solution)/shard_map/ppermute | solution.py:19
  202.1 12.4 %collective-permute-start.29 = (f32[2,288,128]{2,1,0:T(8,128)S(1)}, f32[2,288,128]{2,1,0:T(8,128)S(1)}, u32[]{:S(2)}, u32[]{:S(2)}) collective-permute-start(f32[2,288,128]{2,1,0:T(8,128)S(1)} %get-tuple-element.15), channel_id=1, source_target_pairs={{0,1},{1,0},{2,3},{3,2},{4,5},{5,4},{6,7},{7,6},{8,9},{9,8},{10,11... | collective-permute-start | bytes 884744 | tf_op jit(solution)/shard_map/ppermute | solution.py:23
  202.2 7.7 %collective-permute-start.22 = (f32[2,224,128]{2,1,0:T(8,128)S(1)}, f32[2,224,128]{2,1,0:T(8,128)S(1)}, u32[]{:S(2)}, u32[]{:S(2)}) collective-permute-start(f32[2,224,128]{2,1,0:T(8,128)S(1)} %pad_maximum_fusion.11), channel_id=1, source_target_pairs={{0,6},{1,7},{2,0},{3,1},{4,2},{5,3},{6,4},{7,5},{8,14},{9,15},{10,... | collective-permute-start | bytes 688136 | tf_op jit(solution)/shard_map/ppermute | solution.py:19
  (27 other events, 107.2 us)

commit v2 on v1

--- a/solution.py
+++ b/solution.py
@@ -11,7 +11,7 @@
 
 BLOCK = 128
 X_SIZE = 4
-Z_FIRST_ROWS = 448
+Z_ROWS = 448
 PARAMS = pltpu.CompilerParams(vmem_limit_bytes=40 * 1024 * 1024)
 
 
@@ -23,59 +23,173 @@
     return lax.ppermute(value, "chan", [(i, i ^ 1) for i in range(8)])
 
 
-def project(activations, weight, start, width):
-    columns = lax.dynamic_slice_in_dim(weight, start, width, axis=2)
-    return jnp.einsum("td,djc->jtc", activations, columns, preferred_element_type=jnp.float32)
-
-
-def as_halves(value):
-    return value.reshape(2, -1, value.shape[-1])
-
-
-def z_first(activations, weight):
-    chan = lax.axis_index("chan")
-    x_at, z_at = chan // 2, chan % 2
-
-    def part(dx, dz):
-        owner = (x_at + dx) % X_SIZE * 2 + (z_at + dz) % 2
-        return as_halves(project(activations, weight, owner * BLOCK, BLOCK))
-
-    far = part(2, 0) + swap_z(part(2, 1))
-    from_left = shift_x(far[0], 1)
-    from_right = shift_x(far[1], -1)
-    right, got_right = part(1, 0), swap_z(part(1, 1))
-    left, got_left = part(3, 0), swap_z(part(3, 1))
-    right = jnp.stack([right[0] + got_right[0] + from_left, right[1] + got_right[1]])
-    left = jnp.stack([left[0] + got_left[0], left[1] + got_left[1] + from_right])
-    return part(0, 0), swap_z(part(0, 1)), shift_x(right, 1), shift_x(left, -1)
-
-
-def x_first(activations, weight):
-    chan = lax.axis_index("chan")
-    x_at, z_at = chan // 2, chan % 2
-
-    def part(dx):
-        owner = (x_at + dx) % X_SIZE
-        return as_halves(project(activations, weight, owner * 2 * BLOCK, 2 * BLOCK))
-
-    def pick(value, dz):
-        return lax.dynamic_slice_in_dim(value, (z_at + dz) % 2 * BLOCK, BLOCK, axis=-1)
-
-    far = part(2)
-    from_left = shift_x(far[0], 1)
-    from_right = shift_x(far[1], -1)
-    right, left, own = part(1), part(3), part(0)
-
-    def second(dz):
-        to_right, to_left = pick(right, dz), pick(left, dz)
-        to_right = jnp.stack([to_right[0] + pick(from_left, dz), to_right[1]])
-        to_left = jnp.stack([to_left[0], to_left[1] + pick(from_right, dz)])
-        return shift_x(to_right, 1), shift_x(to_left, -1)
-
-    a, b = second(1)
-    other = swap_z(pick(own, 1) + a + b)
-    c, d = second(0)
-    return pick(own, 0), c, d, other
+def parts_of(rows, weight_ref, z_at):
+    product = jnp.dot(rows, weight_ref[0], preferred_element_type=jnp.float32)
+    low, high = product[:, :BLOCK], product[:, BLOCK:]
+    return jnp.where(z_at == 0, high, low), jnp.where(z_at == 0, low, high)
+
+
+class Halves:
+    def __init__(self, tokens, z_rows, columns):
+        self.columns = columns
+        parts = 2 // len(columns)
+        self.z_rows = z_rows // parts
+        self.x_rows = (tokens - z_rows) // parts
+        self.z_start = [h % parts * self.z_rows for h in range(2)]
+        self.x_start = [z_rows + h % parts * self.x_rows for h in range(2)]
+
+    def x_part(self, act, weights, half, z_at):
+        rows = act[self.x_start[half] : self.x_start[half] + self.x_rows]
+        return parts_of(rows, weights[half % len(weights)], z_at)
+
+    def z_part(self, act, weights, half, z_at):
+        rows = act[self.z_start[half] : self.z_start[half] + self.z_rows]
+        return parts_of(rows, weights[half % len(weights)], z_at)
+
+
+def far_kernel(halves, place, act, weights, outs):
+    send_r, send_l, z_other, z_mine = outs
+    (far,) = weights
+    for half, out in enumerate((send_r, send_l)):
+        out[0], out[1] = halves.x_part(act, far, half, place[4])
+        z_other[half], z_mine[half] = halves.z_part(act, far, half, place[4])
+
+
+def near_kernel(halves, place, act, weights, outs):
+    send_r, send_l, keep_r, keep_l, z_other, z_mine = outs
+    right, left = weights
+    send_r[0], send_r[1] = halves.x_part(act, right, 1, place[4])
+    send_l[0], send_l[1] = halves.x_part(act, left, 0, place[4])
+    z_other[0], z_mine[0] = halves.z_part(act, right, 0, place[4])
+    z_other[1], z_mine[1] = halves.z_part(act, right, 1, place[4])
+    z_other[2], z_mine[2] = halves.z_part(act, left, 0, place[4])
+    keep_r[0], keep_r[1] = halves.x_part(act, right, 0, place[4])
+    keep_l[0], keep_l[1] = halves.x_part(act, left, 1, place[4])
+
+
+def own_kernel(halves, place, act, weights, outs):
+    x_other, x_mine, z_other, z_mine = outs
+    left, own = weights
+    z_other[0], z_mine[0] = halves.z_part(act, left, 1, place[4])
+    for half in range(2):
+        z_other[1 + half], z_mine[1 + half] = halves.z_part(act, own, half, place[4])
+        x_other[half], x_mine[half] = halves.x_part(act, own, half, place[4])
+
+
+def project(kernel, halves, place, activations, weight, owners, outs, after=()):
+    def spec(j, entry):
+        return pl.BlockSpec((1, weight.shape[1], 2 * BLOCK), lambda i, at: (j, 0, at[entry]))
+
+    def whole(shape):
+        return pl.BlockSpec(shape, lambda i, at: (0,) * len(shape))
+
+    blocks = [spec(j, entry) for entry in owners for j in halves.columns]
+    per_owner = len(halves.columns)
+
+    def body(at, act, *refs):
+        weights = [
+            refs[i * per_owner : (i + 1) * per_owner] for i in range(len(owners))
+        ]
+        kernel(halves, at, act, weights, refs[len(blocks) + len(after) :])
+
+    return pl.pallas_call(
+        body,
+        grid_spec=pltpu.PrefetchScalarGridSpec(
+            num_scalar_prefetch=1,
+            grid=(1,),
+            in_specs=[whole(activations.shape)]
+            + blocks
+            + [pl.BlockSpec(memory_space=pl.ANY)] * len(after),
+            out_specs=[whole(shape) for shape in outs],
+        ),
+        out_shape=[jax.ShapeDtypeStruct(shape, jnp.float32) for shape in outs],
+        compiler_params=PARAMS,
+        name=kernel.__name__,
+    )(place, activations, *[weight] * len(blocks), *after)
+
+
+def first_sum_kernel(keep_r, got_r, keep_l, got_l, z_mine, z_got, out_r, out_l):
+    rows = keep_r.shape[1]
+    for half, (keep, got, out) in enumerate(((keep_r, got_r, out_r), (keep_l, got_l, out_l))):
+        out[:rows] = keep[0] + got[0]
+        out[rows : 2 * rows] = keep[1] + got[1]
+        out[2 * rows :] = z_mine[half] + z_got[half]
+
+
+def second_sum_kernel(
+    z_near, z_near_got, z_own, z_own_got, x_own, dep_r, dep_l, near_r, near_l, out_r, out_l, out_x
+):
+    rows, x_rows = z_near.shape[1], x_own.shape[1]
+    out_r[0] = z_near[0] + z_near_got[0] + dep_r[2 * x_rows : 2 * x_rows + rows]
+    out_r[1] = z_near[1] + z_near_got[1]
+    out_l[0] = z_near[2] + z_near_got[2]
+    out_l[1] = z_own[0] + z_own_got[0] + dep_l[2 * x_rows : 2 * x_rows + rows]
+    out_x[0] = x_own[0] + (dep_r[:x_rows] + near_l[0])
+    out_x[1] = x_own[1] + (near_r[0] + dep_l[:x_rows])
+
+
+def reduce_chunks(halves, place, activations, weight, after=(), beside=None):
+    x_rows, z_rows = halves.x_rows, halves.z_rows
+    x_pair, z_pair, z_three = (2, x_rows, BLOCK), (2, z_rows, BLOCK), (3, z_rows, BLOCK)
+    make = functools.partial(
+        project, halves=halves, place=place, activations=activations, weight=weight
+    )
+    far_r, far_l, z_far, z_far_mine = make(
+        far_kernel, owners=[2], outs=[x_pair, x_pair, z_pair, z_pair], after=after
+    )
+    far_r, far_l, z_far = shift_x(far_r, 1), shift_x(far_l, -1), swap_z(z_far)
+    near_r, near_l, keep_r, keep_l, z_near, z_near_mine = make(
+        near_kernel,
+        owners=[1, 3],
+        outs=[x_pair, x_pair, x_pair, x_pair, z_three, z_three],
+        after=(z_far_mine,),
+    )
+    near_r, near_l, z_near = shift_x(near_r, 1), shift_x(near_l, -1), swap_z(z_near)
+    x_own, x_mine, z_own, z_mine = make(
+        own_kernel, owners=[3, 0], outs=[x_pair, x_pair, z_three, z_three], after=(keep_r,)
+    )
+    dep_shape = (2 * x_rows + z_rows, BLOCK)
+    dep_r, dep_l = call(
+        first_sum_kernel,
+        [dep_shape, dep_shape],
+        keep_r,
+        far_r,
+        keep_l,
+        far_l,
+        z_far_mine,
+        z_far,
+        after=(near_r, near_l, z_near, x_own),
+    )
+    moved = (beside(dep_r),) if beside else ()
+    dep_r, dep_l, z_own_got = shift_x(dep_r, 1), shift_x(dep_l, -1), swap_z(z_own)
+    last_r, last_l, x_sum = call(
+        second_sum_kernel,
+        [z_pair, z_pair, x_pair],
+        z_near_mine,
+        z_near,
+        z_mine,
+        z_own_got,
+        x_own,
+        dep_r,
+        dep_l,
+        near_r,
+        near_l,
+        after=moved,
+    )
+    stage_three = last_r
+    last_r, last_l, x_sum = shift_x(last_r, 1), shift_x(last_l, -1), swap_z(x_sum)
+    parts = (z_mine, z_own_got, last_r, last_l, x_mine, dep_r, near_r, dep_l, near_l, x_sum)
+    return parts, moved, stage_three
+
+
+def summed(z_own, z_got, z_r, z_l, x_own, dep_r, near_r, dep_l, near_l, x_got):
+    rows = x_own.shape[1]
+    z_total = [(z_own[1 + h] + z_got[1 + h]) + (z_r[h] + z_l[h]) for h in range(2)]
+    x_total = [
+        x_own[0] + (dep_r[rows : 2 * rows] + near_l[1]) + x_got[0],
+        x_own[1] + (near_r[1] + dep_l[rows : 2 * rows]) + x_got[1],
+    ]
+    return z_total, x_total
 
 
 def split_bf16(table):
@@ -174,32 +288,44 @@
     turn_blocks(taps_ref, out_ref)
 
 
-def kv_kernel(z0, z1, z2, z3, x0, x1, x2, x3, out_ref, kv_ref):
-    rows = z0.shape[1]
-    total = (z0[...] + z1[...]) + (z2[...] + z3[...])
-    kv_ref[:rows] = total[0] * total[1]
-    total = (x0[...] + x1[...]) + (x2[...] + x3[...])
-    kv_ref[rows:] = total[0] * total[1]
+def kv_kernel(*refs):
+    parts, out_ref, kv_ref = refs[:-2], refs[-2], refs[-1]
+    z_total, x_total = summed(*parts)
+    rows = z_total[0].shape[0]
+    kv_ref[:rows] = z_total[0] * z_total[1]
+    kv_ref[rows:] = x_total[0] * x_total[1]
     turn_blocks(kv_ref, out_ref)
 
 
-def gate_kernel(conv_ref, z0, z1, z2, z3, x0, x1, x2, x3, out_ref):
+def gate_kernel(conv_ref, *refs):
+    parts, out_ref = refs[:-1], refs[-1]
     for b in range(conv_ref.shape[1]):
         out_ref[b * BLOCK : (b + 1) * BLOCK, :] = conv_ref[:, b, :].T
-    rows = 2 * z0.shape[1]
-    total = (z0[...] + z1[...]) + (z2[...] + z3[...])
-    out_ref[:rows] = out_ref[:rows] * total.reshape(rows, BLOCK)
-    total = (x0[...] + x1[...]) + (x2[...] + x3[...])
-    out_ref[rows:] = out_ref[rows:] * total.reshape(-1, BLOCK)
-
-
-def call(kernel, out_shape, *operands, scratch=()):
-    return pl.pallas_call(
-        kernel,
-        out_shape=jax.ShapeDtypeStruct(out_shape, jnp.float32),
+    z_total, x_total = summed(*parts)
+    start = 0
+    for query in z_total + x_total:
+        end = start + query.shape[0]
+        out_ref[start:end] = out_ref[start:end] * query
+        start = end
+
+
+def call(kernel, out_shapes, *operands, after=(), scratch=()):
+    single = not isinstance(out_shapes, list)
+    shapes = [out_shapes] if single else out_shapes
+
+    def body(*refs):
+        kernel(*refs[: len(operands)], *refs[len(operands) + len(after) :])
+
+    result = pl.pallas_call(
+        body,
+        in_specs=[pl.BlockSpec(memory_space=pltpu.VMEM)] * len(operands)
+        + [pl.BlockSpec(memory_space=pl.ANY)] * len(after),
+        out_shape=[jax.ShapeDtypeStruct(shape, jnp.float32) for shape in shapes],
         scratch_shapes=scratch,
         compiler_params=PARAMS,
-    )(*operands)
+        name=kernel.__name__,
+    )(*operands, *after)
+    return result[0] if single else result
 
 
 def exchange(value):
@@ -216,19 +342,31 @@
     moved_shape = (seqs, owned, blocks, BLOCK)
     first, turn, second, back, inverse = tables(length)
 
-    low, high = activations[:Z_FIRST_ROWS], activations[Z_FIRST_ROWS:]
-    kv_weight, q_weight = proj_weight[:, 1:], proj_weight[:, :1]
-    kv_parts = z_first(low, kv_weight) + x_first(high, kv_weight)
-    q_parts = z_first(low, q_weight) + x_first(high, q_weight)
-
-    taps = call(taps_turn_kernel, turned_shape, filter_taps)
-    taps = exchange(taps.reshape(moved_shape))
+    chan = lax.axis_index("chan")
+    x_at, z_at = chan // 2, chan % 2
+    place = jnp.stack([(x_at + dx) % X_SIZE for dx in range(X_SIZE)] + [z_at]).astype(jnp.int32)
+    weight = jnp.transpose(proj_weight, (1, 0, 2))
+    def move_taps(ready):
+        turned = call(taps_turn_kernel, turned_shape, filter_taps, after=(ready,))
+        return exchange(turned.reshape(moved_shape))
+
+    kv_parts, (taps,), kv_last = reduce_chunks(
+        Halves(tokens, Z_ROWS, (1, 2)), place, activations, weight, beside=move_taps
+    )
+    q_parts, _, _ = reduce_chunks(
+        Halves(tokens, Z_ROWS, (0,)), place, activations, weight, after=(kv_last,)
+    )
+
     spectrum = call(
         taps_kernel, (owned * length // BLOCK, 2 * BLOCK), taps, *first, *turn, *second
     )
 
     kv = call(
-        kv_kernel, turned_shape, *kv_parts, scratch=[pltpu.VMEM((tokens, channels), jnp.float32)]
+        kv_kernel,
+        turned_shape,
+        *kv_parts,
+        after=(spectrum,),
+        scratch=[pltpu.VMEM((tokens, channels), jnp.float32)],
     )
     moved = exchange(kv.reshape(moved_shape))
     convolved = call(

time: 217 us -> 169 us (0.78)
  matrix products: 58.1 us -> 0 us
  Pallas kernels: 7.82 us -> 30.6 us
  other arithmetic: 14.3 us -> 0 us
  local copies, waits for them, and re-layouts: 21.7 us -> 34.8 us
  waiting for transfers between devices: 54.2 us -> 48.4 us
  starting transfers between devices: 59 us -> 53.2 us
    dot_general x24 -> x0, matrix products: 58.1 us -> none  [project(): jnp.einsum('td,djc->jtc', activations, columns, preferred_element_type=jn...]
    unnamed x84 -> x116, local copies, waits for them, and re-layouts: 4.19 us -> 34.7 us
    ppermute x20 -> x16, waiting for transfers between devices: 46.1 us -> 21.8 us  [shift_x(): lax.ppermute(value, 'chan', [(i, (i + 2 * step) % 8) for i in range(8)])]
    pallas_call x5 -> x15, Pallas kernels: 7.82 us -> 30.6 us  [the longest x9 17.5 us: call(): pl.pallas_call(body, in_specs=[pl.BlockSpec(memory_space=pltpu.VMEM)] * l...]
    slice x8 -> x0, local copies, waits for them, and re-layouts: 12.4 us -> none  [the longest x2 8.05 us: on_device(): kv_weight, q_weight = (proj_weight[:, 1:], proj_weight[:, :1])]
    ppermute x10 -> x8, waiting for transfers between devices: 5.4 us -> 15.1 us  [swap_z(): return lax.ppermute(value, 'chan', [(i, i ^ 1) for i in range(8)])]
    all_to_all x3, waiting for transfers between devices: 2.75 us -> 11.5 us  [exchange(): return lax.all_to_all(value, 'seq', split_axis=0, concat_axis=0, tiled=True)]
    another operation x20 -> x0, other arithmetic: 8.71 us -> none  [the longest x4 3.63 us: z_first(): jnp.stack([right[0] + got_right[0] + from_left, right[1] + got_right[1]])]
  transfers between devices with their start and end apart: 33 -> 27, of which waited for: 11 -> 9; matrix products, arithmetic and copies ran while one was open for 38% -> 0% of each run, Pallas kernels for 3% -> 14%
where the time goes in v2:
time: 169 us; the launch traced here: 167 us
  starting transfers between devices  53.2 us (31%)
  waiting for transfers between devices  48.4 us (29%)
  local copies, waits for them, and re-layouts  34.8 us (21%)
  Pallas kernels  30.6 us (18%)
    unnamed x116, local copies, waits for them, and re-layouts  34.7 us
    all_to_all x3, starting transfers between devices, exchange(): return lax.all_to_all(value, 'seq', split_axis=0, concat_axis=0, tiled=True)  26.5 us
    ppermute x16, waiting for transfers between devices, shift_x(): lax.ppermute(value, 'chan', [(i, (i + 2 * step) % 8) for i in range(8)])  21.8 us
    ppermute x16, starting transfers between devices, shift_x(): lax.ppermute(value, 'chan', [(i, (i + 2 * step) % 8) for i in range(8)])  20.9 us
    pallas_call x9, Pallas kernels, call(): pl.pallas_call(body, in_specs=[pl.BlockSpec(memory_space=pltpu.VMEM)] * l...  17.5 us
    ppermute x8, waiting for transfers between devices, swap_z(): return lax.ppermute(value, 'chan', [(i, i ^ 1) for i in range(8)])  15.1 us
    pallas_call x6, Pallas kernels, project(): pl.pallas_call(body, grid_spec=pltpu.PrefetchScalarGridSpec(num_scalar_pr...  13.1 us
    all_to_all x3, waiting for transfers between devices, exchange(): return lax.all_to_all(value, 'seq', split_axis=0, concat_axis=0, tiled=True)  11.5 us
  transfers between devices with their start and end apart: 27, of which 9 were waited for; matrix products, arithmetic and copies ran while one was open for 0% of the time, Pallas kernels for 14%

profile of v2, /device:TPU:1, one launch (start us, length us, event | category | flops | bytes accessed | tf_op | source)
XLA Modules:
  0.0 167.4 jit_solution(12780433238098504127)
XLA Ops:
  0.1 2.8 %copy-done = bf16[1024,3,1024]{2,0,1:T(8,128)(2,1)S(1)} copy-done((bf16[1024,3,1024]{2,0,1:T(8,128)(2,1)S(1)}, bf16[1024,3,1024]{2,0,1:T(8,128)(2,1)}, u32[]{:S(2)}) %copy-start) | copy-done | bytes 6291480
  2.9 1.6 copy-done.3
  4.5 1.8 %far_kernel.2 = (f32[2,576,128]{2,1,0:T(8,128)S(1)}, f32[2,576,128]{2,1,0:T(8,128)S(1)}, f32[2,448,128]{2,1,0:T(8,128)S(1)}, f32[2,448,128]{2,1,0:T(8,128)S(1)}) custom-call(s32[5]{0:T(128)S(1)} %stack.23.at, bf16[1024,1024]{1,0:T(8,128)(2,1)S(1)} %copy-done.3, bf16[3,1024,1024]{2,1,0:T(8,128)(2,1)S(1)} %bitcast.9, bf16[3,1024,1024]{2,1,0:T(8,128)(2,1)S(1)} %bitcast.10), custom_call_target="tpu_custom_call" | custom-call | tf_op jit(solution)/shard_map/far_kernel/pallas_call | solution.py:95
  6.3 2.5 %collective-permute-start.4 = (f32[2,448,128]{2,1,0:T(8,128)S(1)}, f32[2,448,128]{2,1,0:T(8,128)S(1)}, u32[]{:S(2)}, u32[]{:S(2)}) collective-permute-start(f32[2,448,128]{2,1,0:T(8,128)S(1)} %get-tuple-element.53), channel_id=1, source_target_pairs={{0,1},{1,0},{2,3},{3,2},{4,5},{5,4},{6,7},{7,6},{8,9},{9,8},{10,11... | collective-permute-start | bytes 1376264 | tf_op jit(solution)/shard_map/ppermute | solution.py:23
  8.8 2.7 %near_kernel.2 = (f32[2,576,128]{2,1,0:T(8,128)S(1)}, f32[2,576,128]{2,1,0:T(8,128)S(1)}, f32[2,576,128]{2,1,0:T(8,128)S(1)}, f32[2,576,128]{2,1,0:T(8,128)S(1)}...) custom-call(s32[5]{0:T(128)S(1)} %stack.23.at, bf16[1024,1024]{1,0:T(8,128)(2,1)S(1)} %copy-done.3, ...), custom_call_target="tpu_custom_call" | custom-call | tf_op jit(solution)/shard_map/near_kernel/pallas_call | solution.py:95
  12.4 1.2 collective-permute-start.2
  13.6 1.5 collective-permute-start.3
  15.1 4.0 %collective-permute-done.4.refs_5_ = f32[2,448,128]{2,1,0:T(8,128)S(1)} collective-permute-done((f32[2,448,128]{2,1,0:T(8,128)S(1)}, f32[2,448,128]{2,1,0:T(8,128)S(1)}, u32[]{:S(2)}, u32[]{:S(2)}) %collective-permute-start.4) | collective-permute-done | bytes 458784 | tf_op jit(solution)/shard_map/ppermute | solution.py:23
  19.0 2.4 %collective-permute-start.6 = (f32[2,576,128]{2,1,0:T(8,128)S(1)}, f32[2,576,128]{2,1,0:T(8,128)S(1)}, u32[]{:S(2)}, u32[]{:S(2)}) collective-permute-start(f32[2,576,128]{2,1,0:T(8,128)S(1)} %get-tuple-element.55), channel_id=1, source_target_pairs={{0,6},{1,7},{2,0},{3,1},{4,2},{5,3},{6,4},{7,5},{8,14},{9,15},{10,... | collective-permute-start | bytes 1769480 | tf_op jit(solution)/shard_map/ppermute | solution.py:19
  21.4 2.4 %own_kernel.2 = (f32[2,576,128]{2,1,0:T(8,128)S(1)}, f32[2,576,128]{2,1,0:T(8,128)S(1)}, f32[3,448,128]{2,1,0:T(8,128)}, f32[3,448,128]{2,1,0:T(8,128)S(1)}) custom-call(s32[5]{0:T(128)S(1)} %stack.23.at, bf16[1024,1024]{1,0:T(8,128)(2,1)S(1)} %copy-done.3, bf16[3,1024,1024]{2,1,0:T(8,128)(2,1)S(1)} %bitcast.15, bf16[3,1024,1024]{2,1,0:T(8,128)(2,1)S(1)} %bitcast.16, ...), custom_call_target="tpu_custom_call" | custom-call | tf_op jit(solution)/shard_map/own_kernel/pallas_call | solution.py:95
  23.9 3.6 %collective-permute-done.2.refs_1_ = f32[2,576,128]{2,1,0:T(8,128)S(1)} collective-permute-done((f32[2,576,128]{2,1,0:T(8,128)S(1)}, f32[2,576,128]{2,1,0:T(8,128)S(1)}, u32[]{:S(2)}, u32[]{:S(2)}) %collective-permute-start.2) | collective-permute-done | bytes 589856 | tf_op jit(solution)/shard_map/ppermute | solution.py:19
  27.5 12.6 %collective-permute-done.5.refs_6_.refs_7_ = f32[2,576,128]{2,1,0:T(8,128)S(1)} collective-permute-done((f32[2,576,128]{2,1,0:T(8,128)S(1)}, f32[2,576,128]{2,1,0:T(8,128)S(1)}, u32[]{:S(2)}, u32[]{:S(2)}) %collective-permute-start.5) | collective-permute-done | bytes 589856 | tf_op jit(solution)/shard_map/ppermute | solution.py:19
  40.1 1.4 first_sum_kernel.2
  42.4 2.4 %collective-permute-start.8 = (f32[1600,128]{1,0:T(8,128)}, f32[1600,128]{1,0:T(8,128)}, u32[]{:S(2)}, u32[]{:S(2)}) collective-permute-start(f32[1600,128]{1,0:T(8,128)} %get-tuple-element.57), channel_id=1, source_target_pairs={{0,6},{1,7},{2,0},{3,1},{4,2},{5,3},{6,4},{7,5},{8,14},{9,15},{10,... | collective-permute-start | bytes 2457608 | tf_op jit(solution)/shard_map/ppermute | solution.py:19
  44.7 1.2 collective-permute-start
  47.1 10.5 %all-to-all-start = ((f32[16,8,8,128]{3,2,1,0:T(8,128)}), f32[16,8,8,128]{3,2,1,0:T(8,128)}, u32[]{:S(2)}, u32[]{:S(2)}) async-start(f32[16,8,8,128]{3,2,1,0:T(8,128)} %bitcast.24), calls=%async_computation | async-start | bytes 1048576 | tf_op jit(solution)/shard_map/all_to_all | solution.py:332
  57.6 2.0 %collective-permute-done.refs_3_.refs_1_ = f32[3,448,128]{2,1,0:T(8,128)} collective-permute-done((f32[3,448,128]{2,1,0:T(8,128)}, f32[3,448,128]{2,1,0:T(8,128)}, u32[]{:S(2)}, u32[]{:S(2)}) %collective-permute-start) | collective-permute-done | bytes 688160 | tf_op jit(solution)/shard_map/ppermute | solution.py:23
  59.6 11.3 %all-to-all-done.refs_9_.refs_0_ = f32[16,8,8,128]{3,2,1,0:T(8,128)} async-done(((f32[16,8,8,128]{3,2,1,0:T(8,128)}), f32[16,8,8,128]{3,2,1,0:T(8,128)}, u32[]{:S(2)}, u32[]{:S(2)}) %all-to-all-start) | async-done | bytes 524320 | tf_op jit(solution)/shard_map/all_to_all | solution.py:332
  70.8 1.1 copy-done.10
  71.9 1.1 copy-done.12
  73.0 1.1 copy-done.15
  74.1 1.1 copy-done.31
  75.2 1.8 %second_sum_kernel.2 = (f32[2,448,128]{2,1,0:T(8,128)S(1)}, f32[2,448,128]{2,1,0:T(8,128)S(1)}, f32[2,576,128]{2,1,0:T(8,128)S(1)}) custom-call(f32[3,448,128]{2,1,0:T(8,128)S(1)} %copy-done.31, f32[3,448,128]{2,1,0:T(8,128)S(1)} %copy-done.10, f32[3,448,128]{2,1,0:T(8,128)S(1)} %copy-done.12, f32[3,448,128]{2,1,0:T(8,128)} %collective-permute-done.refs_3_.refs_1_, ...), custom_call_target="tpu_custom_call" | custom-call | tf_op jit(solution)/shard_map/second_sum_kernel/pallas_call | solution.py:319
  77.1 2.7 %collective-permute-start.10 = (f32[2,448,128]{2,1,0:T(8,128)S(1)}, f32[2,448,128]{2,1,0:T(8,128)S(1)}, u32[]{:S(2)}, u32[]{:S(2)}) collective-permute-start(f32[2,448,128]{2,1,0:T(8,128)S(1)} %get-tuple-element.59), channel_id=1, source_target_pairs={{0,6},{1,7},{2,0},{3,1},{4,2},{5,3},{6,4},{7,5},{8,14},{9,15},{10,... | collective-permute-start | bytes 1376264 | tf_op jit(solution)/shard_map/ppermute | solution.py:19
  79.9 2.8 %copy-done.1 = bf16[1024,3,1024]{2,0,1:T(8,128)(2,1)S(1)} copy-done((bf16[1024,3,1024]{2,0,1:T(8,128)(2,1)S(1)}, bf16[1024,3,1024]{2,0,1:T(8,128)(2,1)}, u32[]{:S(2)}) %copy-start.1) | copy-done | bytes 6291480
  82.6 2.0 %far_kernel.3 = (f32[2,288,128]{2,1,0:T(8,128)}, f32[2,288,128]{2,1,0:T(8,128)}, f32[2,224,128]{2,1,0:T(8,128)S(1)}, f32[2,224,128]{2,1,0:T(8,128)S(1)}) custom-call(s32[5]{0:T(128)S(1)} %stack.23.at, bf16[1024,1024]{1,0:T(8,128)(2,1)S(1)} %copy-done.4, bf16[3,1024,1024]{2,1,0:T(8,128)(2,1)S(1)} %bitcast.19, f32[2,448,128]{2,1,0:T(8,128)S(1)} %get-tuple-element.58.refs_1_), custom_call_target="tpu_custom_call" | custom-call | tf_op jit(solution)/shard_map/far_kernel/pallas_call | solution.py:95
  84.6 1.4 collective-permute-start.16
  86.1 2.2 %near_kernel.3 = (f32[2,288,128]{2,1,0:T(8,128)}, f32[2,288,128]{2,1,0:T(8,128)}, f32[2,288,128]{2,1,0:T(8,128)S(1)}, f32[2,288,128]{2,1,0:T(8,128)S(1)}, f32[3,...) custom-call(s32[5]{0:T(128)S(1)} %stack.23.at, bf16[1024,1024]{1,0:T(8,128)(2,1)S(1)} %copy-done.4, ...), custom_call_target="tpu_custom_call" | custom-call | tf_op jit(solution)/shard_map/near_kernel/pallas_call | solution.py:95
  88.5 8.1 %collective-permute-done.16.refs_5_ = f32[2,224,128]{2,1,0:T(8,128)S(1)} collective-permute-done((f32[2,224,128]{2,1,0:T(8,128)S(1)}, f32[2,224,128]{2,1,0:T(8,128)S(1)}, u32[]{:S(2)}, u32[]{:S(2)}) %collective-permute-start.16) | collective-permute-done | bytes 229408 | tf_op jit(solution)/shard_map/ppermute | solution.py:23
  97.3 2.7 %collective-permute-start.15 = (f32[2,288,128]{2,1,0:T(8,128)}, f32[2,288,128]{2,1,0:T(8,128)}, u32[]{:S(2)}, u32[]{:S(2)}) collective-permute-start(f32[2,288,128]{2,1,0:T(8,128)} %get-tuple-element.71), channel_id=1, source_target_pairs={{0,6},{1,7},{2,0},{3,1},{4,2},{5,3},{6,4},{7,5},{8,14},{9,15},{10,... | collective-permute-start | bytes 884744 | tf_op jit(solution)/shard_map/ppermute | solution.py:19
  100.0 2.7 %collective-permute-start.18 = (f32[2,288,128]{2,1,0:T(8,128)}, f32[2,288,128]{2,1,0:T(8,128)}, u32[]{:S(2)}, u32[]{:S(2)}) collective-permute-start(f32[2,288,128]{2,1,0:T(8,128)} %get-tuple-element.74), channel_id=1, source_target_pairs={{0,6},{1,7},{2,0},{3,1},{4,2},{5,3},{6,4},{7,5},{8,14},{9,15},{10,... | collective-permute-start | bytes 884744 | tf_op jit(solution)/shard_map/ppermute | solution.py:19
  102.7 2.1 %taps_kernel.1.refs_10_.refs_1_ = f32[1024,256]{1,0:T(8,128)S(1)} custom-call(f32[16,8,8,128]{3,2,1,0:T(8,128)} %all-to-all-done.refs_9_.refs_0_, bf16[256,128]{1,0:T(8,128)(2,1)S(1)} %copy-done.50, bf16[256,128]{1,0:T(8,128)(2,1)S(1)} %copy-done.48, f32[128,128]{1,0:T(8,128)S(1)} %copy-done.46, f32[128,128]{1,0:T(8,128)S(1)} %copy-done.45, ...), custom_call_target="tpu_custom_call" | custom-call | tf_op jit(solution)/shard_map/taps_kernel/pallas_call | solution.py:319
  104.8 2.1 %kv_kernel.1 = f32[128,8,128]{2,1,0:T(8,128)S(1)} custom-call(f32[3,448,128]{2,1,0:T(8,128)S(1)} %copy-done.13, f32[3,448,128]{2,1,0:T(8,128)} %collective-permute-done.refs_3_.refs_1_, f32[2,448,128]{2,1,0:T(8,128)S(1)} %collective-permute-done.9.refs_2_, f32[2,448,128]{2,1,0:T(8,128)S(1)} %collective-permute-done.10.refs_3_, ...), custom_call_target="tpu_custom_call" | custom-call | tf_op jit(solution)/shard_map/kv_kernel/pallas_call | solution.py:319
  107.8 7.5 %all-to-all-start.1 = ((f32[16,8,8,128]{3,2,1,0:T(8,128)}), f32[16,8,8,128]{3,2,1,0:T(8,128)}, u32[]{:S(2)}, u32[]{:S(2)}) async-start(f32[16,8,8,128]{3,2,1,0:T(8,128)} %bitcast.26), calls=%async_computation.1 | async-start | bytes 1048576 | tf_op jit(solution)/shard_map/all_to_all | solution.py:332
  115.3 2.8 %copy-done.2 = bf16[1024,3,1024]{2,0,1:T(8,128)(2,1)S(1)} copy-done((bf16[1024,3,1024]{2,0,1:T(8,128)(2,1)S(1)}, bf16[1024,3,1024]{2,0,1:T(8,128)(2,1)}, u32[]{:S(2)}) %copy-start.2) | copy-done | bytes 6291480
  119.1 1.9 %own_kernel.3 = (f32[2,288,128]{2,1,0:T(8,128)S(1)}, f32[2,288,128]{2,1,0:T(8,128)S(1)}, f32[3,224,128]{2,1,0:T(8,128)}, f32[3,224,128]{2,1,0:T(8,128)S(1)}) custom-call(s32[5]{0:T(128)S(1)} %stack.23.at, bf16[1024,1024]{1,0:T(8,128)(2,1)S(1)} %copy-done.4, bf16[3,1024,1024]{2,1,0:T(8,128)(2,1)S(1)} %bitcast.22, bf16[3,1024,1024]{2,1,0:T(8,128)(2,1)S(1)} %bitcast.23, ...), custom_call_target="tpu_custom_call" | custom-call | tf_op jit(solution)/shard_map/own_kernel/pallas_call | solution.py:95
  121.1 2.3 %first_sum_kernel.3 = (f32[800,128]{1,0:T(8,128)}, f32[800,128]{1,0:T(8,128)}) custom-call(f32[2,288,128]{2,1,0:T(8,128)S(1)} %copy-done.27, f32[2,288,128]{2,1,0:T(8,128)} %collective-permute-done.14.refs_1_, f32[2,288,128]{2,1,0:T(8,128)S(1)} %copy-done.44, f32[2,288,128]{2,1,0:T(8,128)} %collective-permute-done.15.refs_3_, f32[2,224,128]{2,1,0:T(8,128)S(1)} %copy-done.29, ...), custom_call_target="tpu_custom_call" | custom-call | tf_op jit(solution)/shard_map/first_sum_kernel/pallas_call | solution.py:319
  123.3 2.7 %collective-permute-start.20 = (f32[800,128]{1,0:T(8,128)}, f32[800,128]{1,0:T(8,128)S(1)}, u32[]{:S(2)}, u32[]{:S(2)}) collective-permute-start(f32[800,128]{1,0:T(8,128)} %get-tuple-element.76), channel_id=1, source_target_pairs={{0,6},{1,7},{2,0},{3,1},{4,2},{5,3},{6,4},{7,5},{8,14},{9,15},{10,... | collective-permute-start | bytes 1228808 | tf_op jit(solution)/shard_map/ppermute | solution.py:19
  134.4 4.2 %conv_kernel.1 = f32[16,8,8,128]{3,2,1,0:T(8,128)} custom-call(f32[16,8,8,128]{3,2,1,0:T(8,128)} %all-to-all-done.1.refs_0_, f32[1024,256]{1,0:T(8,128)S(1)} %taps_kernel.1.refs_10_.refs_1_, bf16[256,128]{1,0:T(8,128)(2,1)S(1)} %copy-done.51, bf16[256,128]{1,0:T(8,128)(2,1)S(1)} %copy-done.49, f32[128,128]{1,0:T(8,128)S(1)} %copy-done.47, ...), custom_call_target="tpu_custom_call" | custom-call | tf_op jit(solution)/shard_map/conv_kernel/pallas_call | solution.py:319
  138.6 8.5 %all-to-all-start.2 = ((f32[16,8,8,128]{3,2,1,0:T(8,128)}), f32[16,8,8,128]{3,2,1,0:T(8,128)S(1)}, u32[]{:S(2)}, u32[]{:S(2)}) async-start(f32[16,8,8,128]{3,2,1,0:T(8,128)} %conv_kernel.1), calls=%async_computation.2 | async-start | bytes 1048576 | tf_op jit(solution)/shard_map/all_to_all | solution.py:332
  148.8 1.0 copy-done.22
  150.8 1.0 copy-done.40
  151.7 1.2 second_sum_kernel.3
  153.1 2.7 %collective-permute-start.22 = (f32[2,224,128]{2,1,0:T(8,128)S(1)}, f32[2,224,128]{2,1,0:T(8,128)S(1)}, u32[]{:S(2)}, u32[]{:S(2)}) collective-permute-start(f32[2,224,128]{2,1,0:T(8,128)S(1)} %get-tuple-element.78), channel_id=1, source_target_pairs={{0,6},{1,7},{2,0},{3,1},{4,2},{5,3},{6,4},{7,5},{8,14},{9,15},{10,... | collective-permute-start | bytes 688136 | tf_op jit(solution)/shard_map/ppermute | solution.py:19
  155.7 5.5 %collective-permute-done.21.refs_3_ = f32[2,224,128]{2,1,0:T(8,128)S(1)} collective-permute-done((f32[2,224,128]{2,1,0:T(8,128)S(1)}, f32[2,224,128]{2,1,0:T(8,128)S(1)}, u32[]{:S(2)}, u32[]{:S(2)}) %collective-permute-start.21) | collective-permute-done | bytes 229408 | tf_op jit(solution)/shard_map/ppermute | solution.py:19
  161.2 1.1 collective-permute-done.23.refs_10_
  162.3 1.0 copy-done.20
  165.3 2.1 %gate_kernel.1 = f32[1024,128]{1,0:T(8,128)} custom-call(f32[128,8,128]{2,1,0:T(8,128)S(1)} %bitcast.25, f32[3,224,128]{2,1,0:T(8,128)S(1)} %copy-done.20, f32[3,224,128]{2,1,0:T(8,128)S(1)} %copy-done.23, f32[2,224,128]{2,1,0:T(8,128)S(1)} %collective-permute-done.21.refs_3_, f32[2,224,128]{2,1,0:T(8,128)S(1)} %collective-permute-done.22.refs_4_, ...), custom_call_target="tpu_custom_call" | custom-call | tf_op jit(solution)/shard_map/gate_kernel/pallas_call | solution.py:319
  (138 shorter events, 18.9 us)
Async XLA Ops:
  6.3 12.8 %collective-permute-start.4 = (f32[2,448,128]{2,1,0:T(8,128)S(1)}, f32[2,448,128]{2,1,0:T(8,128)S(1)}, u32[]{:S(2)}, u32[]{:S(2)}) collective-permute-start(f32[2,448,128]{2,1,0:T(8,128)S(1)} %get-tuple-element.53), channel_id=1, source_target_pairs={{0,1},{1,0},{2,3},{3,2},{4,5},{5,4},{6,7},{7,6},{8,9},{9,8},{10,11... | collective-permute-start | bytes 1376264 | tf_op jit(solution)/shard_map/ppermute | solution.py:23
  12.4 27.8 %collective-permute-start.1 = (f32[3,448,128]{2,1,0:T(8,128)S(1)}, f32[3,448,128]{2,1,0:T(8,128)S(1)}, u32[]{:S(2)}, u32[]{:S(2)}) collective-permute-start(f32[3,448,128]{2,1,0:T(8,128)S(1)} %get-tuple-element.48), channel_id=1, source_target_pairs={{0,1},{1,0},{2,3},{3,2},{4,5},{5,4},{6,7},{7,6},{8,9},{9,8},{10,11... | collective-permute-start | bytes 2064392 | tf_op jit(solution)/shard_map/ppermute | solution.py:23
  12.4 15.1 %collective-permute-start.2 = (f32[2,576,128]{2,1,0:T(8,128)S(1)}, f32[2,576,128]{2,1,0:T(8,128)S(1)}, u32[]{:S(2)}, u32[]{:S(2)}) collective-permute-start(f32[2,576,128]{2,1,0:T(8,128)S(1)} %get-tuple-element.50), channel_id=1, source_target_pairs={{0,2},{1,3},{2,4},{3,5},{4,6},{5,7},{6,0},{7,1},{8,10},{9,11},{10,... | collective-permute-start | bytes 1769480 | tf_op jit(solution)/shard_map/ppermute | solution.py:19
  13.6 13.9 %collective-permute-start.3 = (f32[2,576,128]{2,1,0:T(8,128)S(1)}, f32[2,576,128]{2,1,0:T(8,128)S(1)}, u32[]{:S(2)}, u32[]{:S(2)}) collective-permute-start(f32[2,576,128]{2,1,0:T(8,128)S(1)} %get-tuple-element.52), channel_id=1, source_target_pairs={{0,6},{1,7},{2,0},{3,1},{4,2},{5,3},{6,4},{7,5},{8,14},{9,15},{10,... | collective-permute-start | bytes 1769480 | tf_op jit(solution)/shard_map/ppermute | solution.py:19
  15.1 25.1 %collective-permute-start.5 = (f32[2,576,128]{2,1,0:T(8,128)S(1)}, f32[2,576,128]{2,1,0:T(8,128)S(1)}, u32[]{:S(2)}, u32[]{:S(2)}) collective-permute-start(f32[2,576,128]{2,1,0:T(8,128)S(1)} %get-tuple-element.54), channel_id=1, source_target_pairs={{0,2},{1,3},{2,4},{3,5},{4,6},{5,7},{6,0},{7,1},{8,10},{9,11},{10,... | collective-permute-start | bytes 1769480 | tf_op jit(solution)/shard_map/ppermute | solution.py:19
  19.0 21.1 %collective-permute-start.6 = (f32[2,576,128]{2,1,0:T(8,128)S(1)}, f32[2,576,128]{2,1,0:T(8,128)S(1)}, u32[]{:S(2)}, u32[]{:S(2)}) collective-permute-start(f32[2,576,128]{2,1,0:T(8,128)S(1)} %get-tuple-element.55), channel_id=1, source_target_pairs={{0,6},{1,7},{2,0},{3,1},{4,2},{5,3},{6,4},{7,5},{8,14},{9,15},{10,... | collective-permute-start | bytes 1769480 | tf_op jit(solution)/shard_map/ppermute | solution.py:19
  21.4 24.5 %copy-start.34 = (f32[1024,128]{1,0:T(8,128)S(1)}, f32[1024,128]{1,0:T(8,128)}, u32[]{:S(2)}) copy-start(f32[1024,128]{1,0:T(8,128)} %refs_0_.1) | copy-start | bytes 1572868
  23.9 17.7 %copy-start.11 = (f32[3,448,128]{2,1,0:T(8,128)}, f32[3,448,128]{2,1,0:T(8,128)S(1)}, u32[]{:S(2)}) copy-start(f32[3,448,128]{2,1,0:T(8,128)S(1)} %get-tuple-element.45.refs_2_.refs_0_) | copy-start | bytes 2064388
  23.9 18.5 %copy-start.14 = (f32[2,576,128]{2,1,0:T(8,128)}, f32[2,576,128]{2,1,0:T(8,128)S(1)}, u32[]{:S(2)}) copy-start(f32[2,576,128]{2,1,0:T(8,128)S(1)} %get-tuple-element.49.refs_9_.refs_4_) | copy-start | bytes 1769476
  23.9 22.4 %copy-start.32 = (f32[2,576,128]{2,1,0:T(8,128)}, f32[2,576,128]{2,1,0:T(8,128)S(1)}, u32[]{:S(2)}) copy-start(f32[2,576,128]{2,1,0:T(8,128)S(1)} %get-tuple-element.60.refs_4_) | copy-start | bytes 1769476
  40.1 36.9 %copy-start.5 = (f32[2,576,128]{2,1,0:T(8,128)}, f32[2,576,128]{2,1,0:T(8,128)S(1)}, u32[]{:S(2)}) copy-start(f32[2,576,128]{2,1,0:T(8,128)S(1)} %collective-permute-done.5.refs_6_.refs_7_) | copy-start | bytes 1769476
  40.1 36.9 %copy-start.7 = (f32[2,576,128]{2,1,0:T(8,128)}, f32[2,576,128]{2,1,0:T(8,128)S(1)}, u32[]{:S(2)}) copy-start(f32[2,576,128]{2,1,0:T(8,128)S(1)} %collective-permute-done.6.refs_7_.refs_8_) | copy-start | bytes 1769476
  40.1 39.7 %copy-start.4 = (bf16[1024,1024]{1,0:T(8,128)(2,1)S(1)}, bf16[1024,1024]{1,0:T(8,128)(2,1)}, u32[]{:S(2)}) copy-start(bf16[1024,1024]{1,0:T(8,128)(2,1)} %act.11) | copy-start | bytes 6291460
  42.4 28.5 %collective-permute-start.8 = (f32[1600,128]{1,0:T(8,128)}, f32[1600,128]{1,0:T(8,128)}, u32[]{:S(2)}, u32[]{:S(2)}) collective-permute-start(f32[1600,128]{1,0:T(8,128)} %get-tuple-element.57), channel_id=1, source_target_pairs={{0,6},{1,7},{2,0},{3,1},{4,2},{5,3},{6,4},{7,5},{8,14},{9,15},{10,... | collective-permute-start | bytes 2457608 | tf_op jit(solution)/shard_map/ppermute | solution.py:19
  44.7 26.1 %collective-permute-start.7 = (f32[1600,128]{1,0:T(8,128)}, f32[1600,128]{1,0:T(8,128)}, u32[]{:S(2)}, u32[]{:S(2)}) collective-permute-start(f32[1600,128]{1,0:T(8,128)} %get-tuple-element.56.refs_1_), channel_id=1, source_target_pairs={{0,2},{1,3},{2,4},{3,5},{4,6},{5,7},{6,0},{7,1},{8,10},{9,11},{10,... | collective-permute-start | bytes 2457608 | tf_op jit(solution)/shard_map/ppermute | solution.py:19
  44.7 14.8 %collective-permute-start = (f32[3,448,128]{2,1,0:T(8,128)}, f32[3,448,128]{2,1,0:T(8,128)}, u32[]{:S(2)}, u32[]{:S(2)}) collective-permute-start(f32[3,448,128]{2,1,0:T(8,128)} %get-tuple-element.46), channel_id=1, source_target_pairs={{0,1},{1,0},{2,3},{3,2},{4,5},{5,4},{6,7},{7,6},{8,9},{9,8},{10,11... | collective-permute-start | bytes 2064392 | tf_op jit(solution)/shard_map/ppermute | solution.py:23
  47.1 23.8 %all-to-all-start = ((f32[16,8,8,128]{3,2,1,0:T(8,128)}), f32[16,8,8,128]{3,2,1,0:T(8,128)}, u32[]{:S(2)}, u32[]{:S(2)}) async-start(f32[16,8,8,128]{3,2,1,0:T(8,128)} %bitcast.24), calls=%async_computation | async-start | bytes 1048576 | tf_op jit(solution)/shard_map/all_to_all | solution.py:332
  77.0 22.9 %collective-permute-start.11 = (f32[2,576,128]{2,1,0:T(8,128)S(1)}, f32[2,576,128]{2,1,0:T(8,128)S(1)}, u32[]{:S(2)}, u32[]{:S(2)}) collective-permute-start(f32[2,576,128]{2,1,0:T(8,128)S(1)} %get-tuple-element.61), channel_id=1, source_target_pairs={{0,1},{1,0},{2,3},{3,2},{4,5},{5,4},{6,7},{7,6},{8,9},{9,8},{10,11... | collective-permute-start | bytes 1769480 | tf_op jit(solution)/shard_map/ppermute | solution.py:23
  77.1 20.2 %collective-permute-start.10 = (f32[2,448,128]{2,1,0:T(8,128)S(1)}, f32[2,448,128]{2,1,0:T(8,128)S(1)}, u32[]{:S(2)}, u32[]{:S(2)}) collective-permute-start(f32[2,448,128]{2,1,0:T(8,128)S(1)} %get-tuple-element.59), channel_id=1, source_target_pairs={{0,6},{1,7},{2,0},{3,1},{4,2},{5,3},{6,4},{7,5},{8,14},{9,15},{10,... | collective-permute-start | bytes 1376264 | tf_op jit(solution)/shard_map/ppermute | solution.py:19
  79.9 20.1 %collective-permute-start.9 = (f32[2,448,128]{2,1,0:T(8,128)S(1)}, f32[2,448,128]{2,1,0:T(8,128)S(1)}, u32[]{:S(2)}, u32[]{:S(2)}) collective-permute-start(f32[2,448,128]{2,1,0:T(8,128)S(1)} %get-tuple-element.58.refs_1_), channel_id=1, source_target_pairs={{0,2},{1,3},{2,4},{3,5},{4,6},{5,7},{6,0},{7,1},{8,10},{9,11},{10,... | collective-permute-start | bytes 1376264 | tf_op jit(solution)/shard_map/ppermute | solution.py:19
  84.6 12.0 %collective-permute-start.16 = (f32[2,224,128]{2,1,0:T(8,128)S(1)}, f32[2,224,128]{2,1,0:T(8,128)S(1)}, u32[]{:S(2)}, u32[]{:S(2)}) collective-permute-start(f32[2,224,128]{2,1,0:T(8,128)S(1)} %get-tuple-element.72), channel_id=1, source_target_pairs={{0,1},{1,0},{2,3},{3,2},{4,5},{5,4},{6,7},{7,6},{8,9},{9,8},{10,11... | collective-permute-start | bytes 688136 | tf_op jit(solution)/shard_map/ppermute | solution.py:23
  86.0 16.6 %copy-start.35 = (bf16[256,256]{1,0:T(8,128)(2,1)S(1)}, bf16[256,256]{1,0:T(8,128)(2,1)}, u32[]{:S(2)}) copy-start(bf16[256,256]{1,0:T(8,128)(2,1)} %constant.77.clone.refs_6_.refs_7_) | copy-start | bytes 393220
  86.0 16.6 %copy-start.37 = (bf16[256,256]{1,0:T(8,128)(2,1)S(1)}, bf16[256,256]{1,0:T(8,128)(2,1)}, u32[]{:S(2)}) copy-start(bf16[256,256]{1,0:T(8,128)(2,1)} %constant.76.clone.refs_5_.refs_6_) | copy-start | bytes 393220
  86.0 16.6 %copy-start.45 = (f32[128,128]{1,0:T(8,128)S(1)}, f32[128,128]{1,0:T(8,128)}, u32[]{:S(2)}) copy-start(f32[128,128]{1,0:T(8,128)} %constant.75.clone.refs_4_.refs_5_) | copy-start | bytes 196612
  86.0 16.6 %copy-start.46 = (f32[128,128]{1,0:T(8,128)S(1)}, f32[128,128]{1,0:T(8,128)}, u32[]{:S(2)}) copy-start(f32[128,128]{1,0:T(8,128)} %constant.74.clone.refs_3_.refs_4_) | copy-start | bytes 196612
  86.0 16.6 %copy-start.48 = (bf16[256,128]{1,0:T(8,128)(2,1)S(1)}, bf16[256,128]{1,0:T(8,128)(2,1)}, u32[]{:S(2)}) copy-start(bf16[256,128]{1,0:T(8,128)(2,1)} %constant.73.clone.refs_2_.refs_3_) | copy-start | bytes 196612
  86.0 16.6 %copy-start.50 = (bf16[256,128]{1,0:T(8,128)(2,1)S(1)}, bf16[256,128]{1,0:T(8,128)(2,1)}, u32[]{:S(2)}) copy-start(bf16[256,128]{1,0:T(8,128)(2,1)} %constant.72.clone.refs_1_.refs_2_) | copy-start | bytes 196612
  86.1 18.7 %copy-start.6 = (f32[2,576,128]{2,1,0:T(8,128)S(1)}, f32[2,576,128]{2,1,0:T(8,128)}, u32[]{:S(2)}) copy-start(f32[2,576,128]{2,1,0:T(8,128)} %copy-done.5) | copy-start | bytes 1769476
  86.1 18.7 %copy-start.8 = (f32[2,576,128]{2,1,0:T(8,128)S(1)}, f32[2,576,128]{2,1,0:T(8,128)}, u32[]{:S(2)}) copy-start(f32[2,576,128]{2,1,0:T(8,128)} %copy-done.7) | copy-start | bytes 1769476
  86.1 18.7 %copy-start.13 = (f32[3,448,128]{2,1,0:T(8,128)S(1)}, f32[3,448,128]{2,1,0:T(8,128)}, u32[]{:S(2)}) copy-start(f32[3,448,128]{2,1,0:T(8,128)} %copy-done.11) | copy-start | bytes 2064388
  86.1 18.7 %copy-start.33 = (f32[2,576,128]{2,1,0:T(8,128)S(1)}, f32[2,576,128]{2,1,0:T(8,128)}, u32[]{:S(2)}) copy-start(f32[2,576,128]{2,1,0:T(8,128)} %copy-done.32) | copy-start | bytes 1769476
  88.3 18.6 %copy-start.26 = (f32[2,288,128]{2,1,0:T(8,128)}, f32[2,288,128]{2,1,0:T(8,128)S(1)}, u32[]{:S(2)}) copy-start(f32[2,288,128]{2,1,0:T(8,128)S(1)} %get-tuple-element.63.refs_2_.refs_0_) | copy-start | bytes 884740
  88.3 18.6 %copy-start.39 = (f32[3,224,128]{2,1,0:T(8,128)}, f32[3,224,128]{2,1,0:T(8,128)S(1)}, u32[]{:S(2)}) copy-start(f32[3,224,128]{2,1,0:T(8,128)S(1)} %get-tuple-element.66.refs_0_) | copy-start | bytes 1032196
  88.3 18.6 %copy-start.43 = (f32[2,288,128]{2,1,0:T(8,128)}, f32[2,288,128]{2,1,0:T(8,128)S(1)}, u32[]{:S(2)}) copy-start(f32[2,288,128]{2,1,0:T(8,128)S(1)} %get-tuple-element.70.refs_2_) | copy-start | bytes 884740
  88.4 32.7 %collective-permute-start.13 = (f32[3,224,128]{2,1,0:T(8,128)}, f32[3,224,128]{2,1,0:T(8,128)}, u32[]{:S(2)}, u32[]{:S(2)}) collective-permute-start(f32[3,224,128]{2,1,0:T(8,128)} %get-tuple-element.67), channel_id=1, source_target_pairs={{0,1},{1,0},{2,3},{3,2},{4,5},{5,4},{6,7},{7,6},{8,9},{9,8},{10,11... | collective-permute-start | bytes 1032200 | tf_op jit(solution)/shard_map/ppermute | solution.py:23
  97.3 23.7 %collective-permute-start.14 = (f32[2,288,128]{2,1,0:T(8,128)}, f32[2,288,128]{2,1,0:T(8,128)}, u32[]{:S(2)}, u32[]{:S(2)}) collective-permute-start(f32[2,288,128]{2,1,0:T(8,128)} %get-tuple-element.69), channel_id=1, source_target_pairs={{0,2},{1,3},{2,4},{3,5},{4,6},{5,7},{6,0},{7,1},{8,10},{9,11},{10,... | collective-permute-start | bytes 884744 | tf_op jit(solution)/shard_map/ppermute | solution.py:19
  97.3 23.7 %collective-permute-start.15 = (f32[2,288,128]{2,1,0:T(8,128)}, f32[2,288,128]{2,1,0:T(8,128)}, u32[]{:S(2)}, u32[]{:S(2)}) collective-permute-start(f32[2,288,128]{2,1,0:T(8,128)} %get-tuple-element.71), channel_id=1, source_target_pairs={{0,6},{1,7},{2,0},{3,1},{4,2},{5,3},{6,4},{7,5},{8,14},{9,15},{10,... | collective-permute-start | bytes 884744 | tf_op jit(solution)/shard_map/ppermute | solution.py:19
  100.0 21.0 %collective-permute-start.17 = (f32[2,288,128]{2,1,0:T(8,128)}, f32[2,288,128]{2,1,0:T(8,128)S(1)}, u32[]{:S(2)}, u32[]{:S(2)}) collective-permute-start(f32[2,288,128]{2,1,0:T(8,128)} %get-tuple-element.73), channel_id=1, source_target_pairs={{0,2},{1,3},{2,4},{3,5},{4,6},{5,7},{6,0},{7,1},{8,10},{9,11},{10,... | collective-permute-start | bytes 884744 | tf_op jit(solution)/shard_map/ppermute | solution.py:19
  100.0 21.1 %collective-permute-start.18 = (f32[2,288,128]{2,1,0:T(8,128)}, f32[2,288,128]{2,1,0:T(8,128)}, u32[]{:S(2)}, u32[]{:S(2)}) collective-permute-start(f32[2,288,128]{2,1,0:T(8,128)} %get-tuple-element.74), channel_id=1, source_target_pairs={{0,6},{1,7},{2,0},{3,1},{4,2},{5,3},{6,4},{7,5},{8,14},{9,15},{10,... | collective-permute-start | bytes 884744 | tf_op jit(solution)/shard_map/ppermute | solution.py:19
  107.8 18.8 %all-to-all-start.1 = ((f32[16,8,8,128]{3,2,1,0:T(8,128)}), f32[16,8,8,128]{3,2,1,0:T(8,128)}, u32[]{:S(2)}, u32[]{:S(2)}) async-start(f32[16,8,8,128]{3,2,1,0:T(8,128)} %bitcast.26), calls=%async_computation.1 | async-start | bytes 1048576 | tf_op jit(solution)/shard_map/all_to_all | solution.py:332
  121.0 5.0 %copy-start.41 = (f32[2,288,128]{2,1,0:T(8,128)}, f32[2,288,128]{2,1,0:T(8,128)S(1)}, u32[]{:S(2)}) copy-start(f32[2,288,128]{2,1,0:T(8,128)S(1)} %get-tuple-element.79.refs_5_) | copy-start | bytes 884740
  123.3 24.5 %collective-permute-start.19 = (f32[800,128]{1,0:T(8,128)}, f32[800,128]{1,0:T(8,128)S(1)}, u32[]{:S(2)}, u32[]{:S(2)}) collective-permute-start(f32[800,128]{1,0:T(8,128)} %get-tuple-element.75), channel_id=1, source_target_pairs={{0,2},{1,3},{2,4},{3,5},{4,6},{5,7},{6,0},{7,1},{8,10},{9,11},{10,... | collective-permute-start | bytes 1228808 | tf_op jit(solution)/shard_map/ppermute | solution.py:19
  123.3 24.5 %collective-permute-start.20 = (f32[800,128]{1,0:T(8,128)}, f32[800,128]{1,0:T(8,128)S(1)}, u32[]{:S(2)}, u32[]{:S(2)}) collective-permute-start(f32[800,128]{1,0:T(8,128)} %get-tuple-element.76), channel_id=1, source_target_pairs={{0,6},{1,7},{2,0},{3,1},{4,2},{5,3},{6,4},{7,5},{8,14},{9,15},{10,... | collective-permute-start | bytes 1228808 | tf_op jit(solution)/shard_map/ppermute | solution.py:19
  126.0 21.1 %collective-permute-start.12 = (f32[3,224,128]{2,1,0:T(8,128)}, f32[3,224,128]{2,1,0:T(8,128)S(1)}, u32[]{:S(2)}, u32[]{:S(2)}) collective-permute-start(f32[3,224,128]{2,1,0:T(8,128)} %get-tuple-element.65), channel_id=1, source_target_pairs={{0,1},{1,0},{2,3},{3,2},{4,5},{5,4},{6,7},{7,6},{8,9},{9,8},{10,11... | collective-permute-start | bytes 1032200 | tf_op jit(solution)/shard_map/ppermute | solution.py:23
  138.6 23.7 %all-to-all-start.2 = ((f32[16,8,8,128]{3,2,1,0:T(8,128)}), f32[16,8,8,128]{3,2,1,0:T(8,128)S(1)}, u32[]{:S(2)}, u32[]{:S(2)}) async-start(f32[16,8,8,128]{3,2,1,0:T(8,128)} %conv_kernel.1), calls=%async_computation.2 | async-start | bytes 1048576 | tf_op jit(solution)/shard_map/all_to_all | solution.py:332
  152.9 9.4 %collective-permute-start.23 = (f32[2,288,128]{2,1,0:T(8,128)S(1)}, f32[2,288,128]{2,1,0:T(8,128)S(1)}, u32[]{:S(2)}, u32[]{:S(2)}) collective-permute-start(f32[2,288,128]{2,1,0:T(8,128)S(1)} %get-tuple-element.80), channel_id=1, source_target_pairs={{0,1},{1,0},{2,3},{3,2},{4,5},{5,4},{6,7},{7,6},{8,9},{9,8},{10,11... | collective-permute-start | bytes 884744 | tf_op jit(solution)/shard_map/ppermute | solution.py:23
  153.0 8.3 %collective-permute-start.21 = (f32[2,224,128]{2,1,0:T(8,128)S(1)}, f32[2,224,128]{2,1,0:T(8,128)S(1)}, u32[]{:S(2)}, u32[]{:S(2)}) collective-permute-start(f32[2,224,128]{2,1,0:T(8,128)S(1)} %get-tuple-element.77), channel_id=1, source_target_pairs={{0,2},{1,3},{2,4},{3,5},{4,6},{5,7},{6,0},{7,1},{8,10},{9,11},{10,... | collective-permute-start | bytes 688136 | tf_op jit(solution)/shard_map/ppermute | solution.py:19
  153.1 8.2 %collective-permute-start.22 = (f32[2,224,128]{2,1,0:T(8,128)S(1)}, f32[2,224,128]{2,1,0:T(8,128)S(1)}, u32[]{:S(2)}, u32[]{:S(2)}) collective-permute-start(f32[2,224,128]{2,1,0:T(8,128)S(1)} %get-tuple-element.78), channel_id=1, source_target_pairs={{0,6},{1,7},{2,0},{3,1},{4,2},{5,3},{6,4},{7,5},{8,14},{9,15},{10,... | collective-permute-start | bytes 688136 | tf_op jit(solution)/shard_map/ppermute | solution.py:19
  (37 other events, 51.7 us)

commit v3 on v2

v3 whole, which is shorter than its diff:
```python
import functools

import jax
import jax.numpy as jnp
import ml_dtypes
import numpy as np
from jax import lax
from jax.experimental import pallas as pl
from jax.experimental.pallas import tpu as pltpu
from jax.sharding import PartitionSpec as P

BLOCK = 128
X_SIZE = 4


def params(mebibytes):
    return pltpu.CompilerParams(vmem_limit_bytes=mebibytes * 1024 * 1024)


def in_hbm(value):
    return pltpu.with_memory_space_constraint(value, pltpu.HBM)


def shift_x(value, step):
    return lax.ppermute(value, "chan", [(i, (i + 2 * step) % 8) for i in range(8)])


def swap_z(value):
    return lax.ppermute(value, "chan", [(i, i ^ 1) for i in range(8)])


def parts_of(rows, weight_ref, z_at):
    product = jnp.dot(rows, weight_ref[0], preferred_element_type=jnp.float32)
    low, high = product[:, :BLOCK], product[:, BLOCK:]
    return jnp.where(z_at == 0, high, low), jnp.where(z_at == 0, low, high)


class Halves:
    def __init__(self, tokens, columns):
        self.columns = columns
        parts = 2 // len(columns)
        self.rows = tokens // 2 // parts
        self.z_start = [h % parts * self.rows for h in range(2)]
        self.x_start = [tokens // 2 + start for start in self.z_start]

    def x_part(self, act, weights, half, z_at):
        rows = act[self.x_start[half] : self.x_start[half] + self.rows]
        return parts_of(rows, weights[half % len(weights)], z_at)

    def z_part(self, act, weights, half, z_at):
        rows = act[self.z_start[half] : self.z_start[half] + self.rows]
        return parts_of(rows, weights[half % len(weights)], z_at)


def far_near_kernel(halves, place, act, weights, outs):
    send_r, send_l, keep_r, keep_l, z_other, z_mine = outs
    z_at = place[4]
    step = pl.program_id(0)

    @pl.when(step == 0)
    def _():
        send_r[0], send_r[1] = halves.x_part(act, weights, 0, z_at)
        send_l[0], send_l[1] = halves.x_part(act, weights, 1, z_at)
        z_other[3], z_mine[3] = halves.z_part(act, weights, 0, z_at)
        z_other[4], z_mine[4] = halves.z_part(act, weights, 1, z_at)

    @pl.when(step == 1)
    def _():
        send_r[2], send_r[3] = halves.x_part(act, weights, 1, z_at)
        z_other[0], z_mine[0] = halves.z_part(act, weights, 0, z_at)
        z_other[1], z_mine[1] = halves.z_part(act, weights, 1, z_at)
        keep_r[0], keep_r[1] = halves.x_part(act, weights, 0, z_at)

    @pl.when(step == 2)
    def _():
        send_l[2], send_l[3] = halves.x_part(act, weights, 0, z_at)
        z_other[2], z_mine[2] = halves.z_part(act, weights, 0, z_at)
        keep_l[0], keep_l[1] = halves.x_part(act, weights, 1, z_at)


def left_own_kernel(halves, place, act, weights, outs):
    x_other, x_mine, z_other, z_mine = outs
    z_at = place[4]
    step = pl.program_id(0)

    @pl.when(step == 0)
    def _():
        z_other[2], z_mine[2] = halves.z_part(act, weights, 1, z_at)

    @pl.when(step == 1)
    def _():
        for half in range(2):
            z_other[half], z_mine[half] = halves.z_part(act, weights, half, z_at)
            x_other[half], x_mine[half] = halves.x_part(act, weights, half, z_at)


def project(kernel, halves, place, activations, weight, owner, steps, outs, after=()):
    def spec(j):
        return pl.BlockSpec(
            (1, weight.shape[1], 2 * BLOCK), lambda i, at: (j, 0, at[owner + i])
        )

    count = len(halves.columns)

    def body(at, act, *refs):
        kernel(halves, at, act, refs[:count], refs[count + len(after) :])

    return pl.pallas_call(
        body,
        grid_spec=pltpu.PrefetchScalarGridSpec(
            num_scalar_prefetch=1,
            grid=(steps,),
            in_specs=[pl.BlockSpec(activations.shape, lambda i, at: (0, 0))]
            + [spec(j) for j in halves.columns]
            + [pl.BlockSpec(memory_space=pl.ANY)] * len(after),
            out_specs=[pl.BlockSpec(memory_space=pltpu.VMEM)] * len(outs),
        ),
        out_shape=[jax.ShapeDtypeStruct(shape, jnp.float32) for shape in outs],
        compiler_params=params(24),
        name=kernel.__name__,
    )(place, activations, *[weight] * count, *after)


def first_sum_kernel(keep_r, got_r, keep_l, got_l, z_mine, z_got, out_r, out_l):
    for half, (keep, got, out) in enumerate(((keep_r, got_r, out_r), (keep_l, got_l, out_l))):
        out[0] = keep[0] + got[0]
        out[1] = keep[1] + got[1]
        out[2] = z_mine[3 + half] + z_got[3 + half]


def second_sum_kernel(
    z_near, z_near_got, z_own, z_own_got, x_own, dep_r, dep_l, got_r, got_l, out_r, out_l, out_x
):
    out_r[0] = z_near[0] + z_near_got[0] + dep_r[2]
    out_r[1] = z_near[1] + z_near_got[1]
    out_l[0] = z_near[2] + z_near_got[2]
    out_l[1] = z_own[2] + z_own_got[2] + dep_l[2]
    out_x[0] = x_own[0] + (dep_r[0] + got_l[2])
    out_x[1] = x_own[1] + (got_r[2] + dep_l[0])


def reduce_chunks(halves, place, activations, weight, after=(), beside=None):
    def pieces(count):
        return (count, halves.rows, BLOCK)

    send_r, send_l, keep_r, keep_l, z_near, z_near_mine = project(
        far_near_kernel,
        halves,
        place,
        activations,
        weight,
        0,
        3,
        [pieces(4), pieces(4), pieces(2), pieces(2), pieces(5), pieces(5)],
        after=after,
    )
    got_r, got_l, z_near = shift_x(send_r, 1), shift_x(send_l, -1), swap_z(z_near)
    x_own, x_mine, z_own, z_mine = project(
        left_own_kernel,
        halves,
        place,
        activations,
        weight,
        2,
        2,
        [pieces(2), pieces(2), pieces(3), pieces(3)],
        after=(keep_r,),
    )
    dep_r, dep_l = call(
        first_sum_kernel,
        [pieces(3), pieces(3)],
        keep_r,
        got_r,
        keep_l,
        got_l,
        z_near_mine,
        z_near,
        after=(x_own,),
    )
    moved = (beside(dep_r),) if beside else ()
    dep_r, dep_l, z_own = shift_x(dep_r, 1), shift_x(dep_l, -1), swap_z(z_own)
    last_r, last_l, x_sum = call(
        second_sum_kernel,
        [pieces(2), pieces(2), pieces(2)],
        z_near_mine,
        z_near,
        z_mine,
        z_own,
        x_own,
        dep_r,
        dep_l,
        got_r,
        got_l,
        after=moved,
    )
    last = last_r
    last_r, last_l, x_sum = shift_x(last_r, 1), shift_x(last_l, -1), swap_z(x_sum)
    return (z_mine, z_own, last_r, last_l, x_mine, dep_r, got_r, dep_l, got_l, x_sum), moved, last


def summed(z_own, z_got, z_r, z_l, x_own, dep_r, got_r, dep_l, got_l, x_got):
    return [(z_own[h] + z_got[h]) + (z_r[h] + z_l[h]) for h in range(2)], [
        x_own[0] + (dep_r[1] + got_l[3]) + x_got[0],
        x_own[1] + (got_r[3] + dep_l[1]) + x_got[1],
    ]


def split_bf16(table):
    high = table.astype(np.float32).astype(ml_dtypes.bfloat16)
    low = (table - high.astype(np.float64)).astype(ml_dtypes.bfloat16)
    return high, low


@functools.lru_cache(None)
def tables(length):
    rows = length // BLOCK
    period = 2 * length
    odd = np.arange(rows) + 0.5
    first = -2 * np.pi * np.outer(odd, np.arange(rows)) / (2 * rows)
    turn = -2 * np.pi * np.outer(odd, np.arange(BLOCK)) / period
    second = -2 * np.pi * (np.outer(np.arange(BLOCK), np.arange(BLOCK)) % BLOCK) / BLOCK
    c, s = np.cos(second), np.sin(second)
    scale = 1.0 / length
    return (
        split_bf16(np.concatenate([np.cos(first), np.sin(first)], axis=0)),
        (np.cos(turn).astype(np.float32), np.sin(turn).astype(np.float32)),
        split_bf16(np.block([[c, s], [-s, c]])),
        split_bf16(np.block([[c, -s], [s, c]])),
        split_bf16(np.concatenate([np.cos(first).T, np.sin(first).T], axis=1) * scale),
    )


def split_value(value):
    high = value.astype(jnp.bfloat16)
    return high, (value - high.astype(jnp.float32)).astype(jnp.bfloat16)


def dot3(left, right):
    dot = functools.partial(jnp.dot, preferred_element_type=jnp.float32)
    return dot(left[0], right[0]) + (dot(left[0], right[1]) + dot(left[1], right[0]))


def forward(signal_ref, first, turn, second):
    seqs, channels = signal_ref.shape[:2]
    rows = seqs * signal_ref.shape[2]
    signal = jnp.concatenate(
        [signal_ref[:, c].reshape(rows, BLOCK) for c in range(channels)], axis=1
    )
    part = dot3(first, split_value(signal))
    turned = []
    for c in range(channels):
        real = part[:rows, c * BLOCK : (c + 1) * BLOCK]
        imag = part[rows:, c * BLOCK : (c + 1) * BLOCK]
        turned.append(
            jnp.concatenate(
                [real * turn[0] - imag * turn[1], real * turn[1] + imag * turn[0]], axis=1
            )
        )
    return dot3(split_value(jnp.concatenate(turned, axis=0)), second)


def taps_kernel(taps_ref, f_hi, f_lo, t_re, t_im, s_hi, s_lo, out_ref):
    out_ref[...] = forward(
        taps_ref, (f_hi[...], f_lo[...]), (t_re[...], t_im[...]), (s_hi[...], s_lo[...])
    )


def conv_kernel(
    kv_ref, spec_ref, f_hi, f_lo, t_re, t_im, s_hi, s_lo, b_hi, b_lo, i_hi, i_lo, out_ref
):
    seqs, channels, blocks, _ = kv_ref.shape
    rows = seqs * blocks
    turn = (t_re[...], t_im[...])
    spectrum = forward(kv_ref, (f_hi[...], f_lo[...]), turn, (s_hi[...], s_lo[...]))
    real, imag = spectrum[:, :BLOCK], spectrum[:, BLOCK:]
    taps_real, taps_imag = spec_ref[:, :BLOCK], spec_ref[:, BLOCK:]
    product = jnp.concatenate(
        [real * taps_real - imag * taps_imag, real * taps_imag + imag * taps_real], axis=1
    )
    back = dot3(split_value(product), (b_hi[...], b_lo[...]))
    columns = []
    for c in range(channels):
        real = back[c * rows : (c + 1) * rows, :BLOCK]
        imag = back[c * rows : (c + 1) * rows, BLOCK:]
        columns.append(
            jnp.concatenate(
                [real * turn[0] + imag * turn[1], imag * turn[0] - real * turn[1]], axis=0
            )
        )
    result = dot3((i_hi[...], i_lo[...]), split_value(jnp.concatenate(columns, axis=1)))
    for c in range(channels):
        out_ref[:, c] = result[:, c * BLOCK : (c + 1) * BLOCK].reshape(seqs, blocks, BLOCK)


def turn_blocks(value_ref, out_ref):
    for b in range(out_ref.shape[1]):
        out_ref[:, b, :] = value_ref[b * BLOCK : (b + 1) * BLOCK, :].T


def taps_turn_kernel(taps_ref, out_ref):
    turn_blocks(taps_ref, out_ref)


def kv_kernel(*refs):
    parts, out_ref, kv_ref = refs[:-2], refs[-2], refs[-1]
    z_total, x_total = summed(*parts)
    rows = z_total[0].shape[0]
    kv_ref[:rows] = z_total[0] * z_total[1]
    kv_ref[rows:] = x_total[0] * x_total[1]
    turn_blocks(kv_ref, out_ref)


def gate_kernel(conv_ref, *refs):
    parts, out_ref = refs[:-1], refs[-1]
    for b in range(conv_ref.shape[1]):
        out_ref[b * BLOCK : (b + 1) * BLOCK, :] = conv_ref[:, b, :].T
    z_total, x_total = summed(*parts)
    start = 0
    for query in z_total + x_total:
        end = start + query.shape[0]
        out_ref[start:end] = out_ref[start:end] * query
        start = end


def call(kernel, out_shapes, *operands, after=(), scratch=(), tables=()):
    single = not isinstance(out_shapes, list)
    shapes = [out_shapes] if single else out_shapes

    def body(*refs):
        count = len(operands) + len(tables)
        kernel(*refs[:count], *refs[count + len(after) :])

    def whole(shape):
        return pl.BlockSpec(shape, lambda i: (0,) * len(shape))

    result = pl.pallas_call(
        body,
        grid=(1,),
        in_specs=[pl.BlockSpec(memory_space=pltpu.VMEM)] * len(operands)
        + [whole(table.shape) for table in tables]
        + [pl.BlockSpec(memory_space=pl.ANY)] * len(after),
        out_specs=[pl.BlockSpec(memory_space=pltpu.VMEM)] * len(shapes),
        out_shape=[jax.ShapeDtypeStruct(shape, jnp.float32) for shape in shapes],
        scratch_shapes=scratch,
        compiler_params=params(24),
        name=kernel.__name__,
    )(*operands, *[in_hbm(jnp.asarray(table)) for table in tables], *after)
    return result[0] if single else result


def exchange(value):
    return lax.all_to_all(value, "seq", split_axis=0, concat_axis=0, tiled=True)


def on_device(activations, proj_weight, filter_taps):
    tokens, channels = filter_taps.shape
    seqs = lax.axis_size("seq")
    length = tokens * seqs
    blocks = tokens // BLOCK
    owned = channels // seqs
    turned_shape = (channels, blocks, BLOCK)
    moved_shape = (seqs, owned, blocks, BLOCK)
    first, turn, second, back, inverse = tables(length)

    chan = lax.axis_index("chan")
    x_at, z_at = chan // 2, chan % 2
    owners = [(x_at + dx) % X_SIZE for dx in (2, 1, 3, 0)]
    place = jnp.stack(owners + [z_at]).astype(jnp.int32)
    weight = in_hbm(jnp.transpose(proj_weight, (1, 0, 2)))
    activations = in_hbm(activations)

    def move_taps(ready):
        turned = call(taps_turn_kernel, turned_shape, filter_taps, after=(ready,))
        return exchange(turned.reshape(moved_shape))

    kv_parts, (taps,), kv_last = reduce_chunks(
        Halves(tokens, (1, 2)), place, activations, weight, beside=move_taps
    )
    q_parts, _, _ = reduce_chunks(
        Halves(tokens, (0,)), place, activations, weight, after=(kv_last,)
    )

    spectrum = call(
        taps_kernel,
        (owned * length // BLOCK, 2 * BLOCK),
        taps,
        tables=first + turn + second,
    )

    kv = call(
        kv_kernel,
        turned_shape,
        *kv_parts,
        after=(spectrum,),
        scratch=[pltpu.VMEM((tokens, channels), jnp.float32)],
    )
    moved = exchange(kv.reshape(moved_shape))
    convolved = call(
        conv_kernel,
        moved_shape,
        moved,
        spectrum,
        tables=first + turn + second + back + inverse,
    )
    home = exchange(convolved).reshape(turned_shape)
    return call(gate_kernel, (tokens, channels), home, *q_parts)


def solution(mesh):
    return jax.shard_map(
        on_device,
        mesh=mesh,
        in_specs=(P("seq", "chan"), P("chan", None, None), P("seq", "chan")),
        out_specs=P("seq", "chan"),
        check_vma=False,
    )
```

time: 169 us -> 141 us (0.83)
  local copies, waits for them, and re-layouts: 34.8 us -> 10.2 us
  Pallas kernels: 30.6 us -> 40.3 us
  waiting for transfers between devices: 48.4 us -> 40.8 us
  starting transfers between devices: 53.2 us -> 48.1 us
    unnamed x116 -> x50, local copies, waits for them, and re-layouts: 34.7 us -> 10.1 us
    pallas_call x6 -> x4, Pallas kernels: 13.1 us -> 21.3 us  [project(): pl.pallas_call(body, grid_spec=pltpu.PrefetchScalarGridSpec(num_scalar_pr...]
    ppermute x8 -> x6, waiting for transfers between devices: 15.1 us -> 7.01 us  [swap_z(): return lax.ppermute(value, 'chan', [(i, i ^ 1) for i in range(8)])]
    ppermute x16 -> x12, starting transfers between devices: 20.9 us -> 16.9 us  [shift_x(): lax.ppermute(value, 'chan', [(i, (i + 2 * step) % 8) for i in range(8)])]
    ppermute x16 -> x12, waiting for transfers between devices: 21.8 us -> 24.1 us  [shift_x(): lax.ppermute(value, 'chan', [(i, (i + 2 * step) % 8) for i in range(8)])]
    all_to_all x3, waiting for transfers between devices: 11.5 us -> 9.71 us  [exchange(): return lax.all_to_all(value, 'seq', split_axis=0, concat_axis=0, tiled=True)]
    ppermute x8 -> x6, starting transfers between devices: 5.77 us -> 4.91 us  [swap_z(): return lax.ppermute(value, 'chan', [(i, i ^ 1) for i in range(8)])]
  transfers between devices with their start and end apart: 27 -> 21, of which waited for: 9 -> 7; matrix products, arithmetic and copies ran while one was open for 0% -> 0% of each run, Pallas kernels for 14% -> 21%
where the time goes in v3:
time: 141 us; the launch traced here: 140 us
  starting transfers between devices  48.1 us (34%)
  waiting for transfers between devices  40.8 us (29%)
  Pallas kernels  40.3 us (29%)
  local copies, waits for them, and re-layouts  10.2 us (7%)
    all_to_all x3, starting transfers between devices, exchange(): return lax.all_to_all(value, 'seq', split_axis=0, concat_axis=0, tiled=True)  26.3 us
    ppermute x12, waiting for transfers between devices, shift_x(): lax.ppermute(value, 'chan', [(i, (i + 2 * step) % 8) for i in range(8)])  24.1 us
    pallas_call x4, Pallas kernels, project(): pl.pallas_call(body, grid_spec=pltpu.PrefetchScalarGridSpec(num_scalar_pr...  21.3 us
    pallas_call x9, Pallas kernels, call(): pl.pallas_call(body, grid=(1,), in_specs=[pl.BlockSpec(memory_space=pltpu...  19 us
    ppermute x12, starting transfers between devices, shift_x(): lax.ppermute(value, 'chan', [(i, (i + 2 * step) % 8) for i in range(8)])  16.9 us
    unnamed x50, local copies, waits for them, and re-layouts  10.1 us
    all_to_all x3, waiting for transfers between devices, exchange(): return lax.all_to_all(value, 'seq', split_axis=0, concat_axis=0, tiled=True)  9.71 us
    ppermute x6, waiting for transfers between devices, swap_z(): return lax.ppermute(value, 'chan', [(i, i ^ 1) for i in range(8)])  7.01 us
  transfers between devices with their start and end apart: 21, of which 7 were waited for; matrix products, arithmetic and copies ran while one was open for 0% of the time, Pallas kernels for 21%

profile of v3, /device:TPU:1, one launch (start us, length us, event | category | flops | bytes accessed | tf_op | source)
XLA Modules:
  0.0 139.7 jit_solution(10816431228673906485)
XLA Ops:
  0.0 0.1 stack.23.at
  0.1 6.1 %far_near_kernel.2 = (f32[4,512,128]{2,1,0:T(8,128)S(1)}, f32[4,512,128]{2,1,0:T(8,128)S(1)}, f32[2,512,128]{2,1,0:T(8,128)S(1)}, f32[2,512,128]{2,1,0:T(8,128)S...) custom-call(s32[5]{0:T(128)S(1)} %stack.23.at, bf16[1024,1024]{1,0:T(8,128)(2,1)} %act.7, ...), custom_call_target="tpu_custom_call" | custom-call | tf_op jit(solution)/shard_map/far_near_kernel/pallas_call | solution.py:108
  6.2 2.5 %collective-permute-start.1 = (f32[5,512,128]{2,1,0:T(8,128)S(1)}, f32[5,512,128]{2,1,0:T(8,128)S(1)}, u32[]{:S(2)}, u32[]{:S(2)}) collective-permute-start(f32[5,512,128]{2,1,0:T(8,128)S(1)} %get-tuple-element.39), channel_id=1, source_target_pairs={{0,1},{1,0},{2,3},{3,2},{4,5},{5,4},{6,7},{7,6},{8,9},{9,8},{10,11... | collective-permute-start | bytes 3932168 | tf_op jit(solution)/shard_map/ppermute | solution.py:29
  8.8 1.2 collective-permute-start.2
  10.0 1.5 %collective-permute-start.3 = (f32[4,512,128]{2,1,0:T(8,128)S(1)}, f32[4,512,128]{2,1,0:T(8,128)S(1)}, u32[]{:S(2)}, u32[]{:S(2)}) collective-permute-start(f32[4,512,128]{2,1,0:T(8,128)S(1)} %get-tuple-element.43), channel_id=1, source_target_pairs={{0,6},{1,7},{2,0},{3,1},{4,2},{5,3},{6,4},{7,5},{8,14},{9,15},{10,... | collective-permute-start | bytes 3145736 | tf_op jit(solution)/shard_map/ppermute | solution.py:25
  11.5 5.1 %left_own_kernel.2 = (f32[2,512,128]{2,1,0:T(8,128)S(1)}, f32[2,512,128]{2,1,0:T(8,128)S(1)}, f32[3,512,128]{2,1,0:T(8,128)}, f32[3,512,128]{2,1,0:T(8,128)S(1)}) custom-call(s32[5]{0:T(128)S(1)} %stack.23.at, bf16[1024,1024]{1,0:T(8,128)(2,1)} %act.7, bf16[3,1024,1024]{2,1,0:T(8,128)(2,1)} %bitcast.14, bf16[3,1024,1024]{2,1,0:T(8,128)(2,1)} %bitcast.15, ...), custom_call_target="tpu_custom_call" | custom-call | tf_op jit(solution)/shard_map/left_own_kernel/pallas_call | solution.py:108
  16.6 0.9 copy-done.6
  17.5 0.8 copy-done.19
  18.3 0.1 collective-permute-start
  18.4 15.3 %collective-permute-done.2.refs_1_.refs_7_.refs_6_ = f32[4,512,128]{2,1,0:T(8,128)S(1)} collective-permute-done((f32[4,512,128]{2,1,0:T(8,128)S(1)}, f32[4,512,128]{2,1,0:T(8,128)S(1)}, u32[]{:S(2)}, u32[]{:S(2)}) %collective-permute-start.2) | collective-permute-done | bytes 1048608 | tf_op jit(solution)/shard_map/ppermute | solution.py:25
  33.7 3.6 %collective-permute-done.1.refs_5_.refs_1_ = f32[5,512,128]{2,1,0:T(8,128)S(1)} collective-permute-done((f32[5,512,128]{2,1,0:T(8,128)S(1)}, f32[5,512,128]{2,1,0:T(8,128)S(1)}, u32[]{:S(2)}, u32[]{:S(2)}) %collective-permute-start.1) | collective-permute-done | bytes 1310752 | tf_op jit(solution)/shard_map/ppermute | solution.py:29
  37.3 1.4 first_sum_kernel.2
  38.6 0.2 copy-done.2
  38.8 2.4 %collective-permute-start.5 = (f32[3,512,128]{2,1,0:T(8,128)}, f32[3,512,128]{2,1,0:T(8,128)}, u32[]{:S(2)}, u32[]{:S(2)}) collective-permute-start(f32[3,512,128]{2,1,0:T(8,128)} %get-tuple-element.45), channel_id=1, source_target_pairs={{0,6},{1,7},{2,0},{3,1},{4,2},{5,3},{6,4},{7,5},{8,14},{9,15},{10,... | collective-permute-start | bytes 2359304 | tf_op jit(solution)/shard_map/ppermute | solution.py:25
  41.2 0.4 taps_turn_kernel.1
  41.6 0.8 copy-done.12
  42.4 10.4 %all-to-all-start = ((f32[16,8,8,128]{3,2,1,0:T(8,128)}), f32[16,8,8,128]{3,2,1,0:T(8,128)S(1)}, u32[]{:S(2)}, u32[]{:S(2)}) async-start(f32[16,8,8,128]{3,2,1,0:T(8,128)} %bitcast.11), calls=%async_computation | async-start | bytes 1048576 | tf_op jit(solution)/shard_map/all_to_all | solution.py:352
  52.8 1.4 %collective-permute-done.refs_3_.refs_1_ = f32[3,512,128]{2,1,0:T(8,128)} collective-permute-done((f32[3,512,128]{2,1,0:T(8,128)}, f32[3,512,128]{2,1,0:T(8,128)}, u32[]{:S(2)}, u32[]{:S(2)}) %collective-permute-start) | collective-permute-done | bytes 786464 | tf_op jit(solution)/shard_map/ppermute | solution.py:29
  54.2 9.7 %all-to-all-done.refs_9_.refs_0_ = f32[16,8,8,128]{3,2,1,0:T(8,128)S(1)} async-done(((f32[16,8,8,128]{3,2,1,0:T(8,128)}), f32[16,8,8,128]{3,2,1,0:T(8,128)S(1)}, u32[]{:S(2)}, u32[]{:S(2)}) %all-to-all-start) | async-done | bytes 524320 | tf_op jit(solution)/shard_map/all_to_all | solution.py:352
  63.9 1.5 %copy-done.1 = f32[5,512,128]{2,1,0:T(8,128)S(1)} copy-done((f32[5,512,128]{2,1,0:T(8,128)S(1)}, f32[5,512,128]{2,1,0:T(8,128)}, u32[]{:S(2)}) %copy-start.1) | copy-done | bytes 1310744
  65.4 1.3 copy-done.3
  66.8 1.1 copy-done.7
  67.9 1.8 %second_sum_kernel.2 = (f32[2,512,128]{2,1,0:T(8,128)S(1)}, f32[2,512,128]{2,1,0:T(8,128)S(1)}, f32[2,512,128]{2,1,0:T(8,128)S(1)}) custom-call(f32[5,512,128]{2,1,0:T(8,128)S(1)} %copy-done.1, f32[5,512,128]{2,1,0:T(8,128)S(1)} %copy-done.3, f32[3,512,128]{2,1,0:T(8,128)S(1)} %copy-done.7, f32[3,512,128]{2,1,0:T(8,128)} %collective-permute-done.refs_3_.refs_1_, ...), custom_call_target="tpu_custom_call" | custom-call | tf_op jit(solution)/shard_map/second_sum_kernel/pallas_call | solution.py:336
  69.7 3.0 %collective-permute-start.7 = (f32[2,512,128]{2,1,0:T(8,128)S(1)}, f32[2,512,128]{2,1,0:T(8,128)S(1)}, u32[]{:S(2)}, u32[]{:S(2)}) collective-permute-start(f32[2,512,128]{2,1,0:T(8,128)S(1)} %get-tuple-element.47), channel_id=1, source_target_pairs={{0,6},{1,7},{2,0},{3,1},{4,2},{5,3},{6,4},{7,5},{8,14},{9,15},{10,... | collective-permute-start | bytes 1572872 | tf_op jit(solution)/shard_map/ppermute | solution.py:25
  72.7 0.7 collective-permute-start.8
  73.5 5.9 %far_near_kernel.3 = (f32[4,256,128]{2,1,0:T(8,128)}, f32[4,256,128]{2,1,0:T(8,128)}, f32[2,256,128]{2,1,0:T(8,128)S(1)}, f32[2,256,128]{2,1,0:T(8,128)S(1)}, f3...) custom-call(s32[5]{0:T(128)S(1)} %stack.23.at, bf16[1024,1024]{1,0:T(8,128)(2,1)} %act.7, ...), custom_call_target="tpu_custom_call" | custom-call | tf_op jit(solution)/shard_map/far_near_kernel/pallas_call | solution.py:108
  79.4 0.8 collective-permute-start.10
  80.2 2.4 %collective-permute-done.7.refs_3_ = f32[2,512,128]{2,1,0:T(8,128)S(1)} collective-permute-done((f32[2,512,128]{2,1,0:T(8,128)S(1)}, f32[2,512,128]{2,1,0:T(8,128)S(1)}, u32[]{:S(2)}, u32[]{:S(2)}) %collective-permute-start.7) | collective-permute-done | bytes 524320 | tf_op jit(solution)/shard_map/ppermute | solution.py:25
  82.6 3.4 %collective-permute-start.12 = (f32[4,256,128]{2,1,0:T(8,128)}, f32[4,256,128]{2,1,0:T(8,128)}, u32[]{:S(2)}, u32[]{:S(2)}) collective-permute-start(f32[4,256,128]{2,1,0:T(8,128)} %get-tuple-element.58), channel_id=1, source_target_pairs={{0,6},{1,7},{2,0},{3,1},{4,2},{5,3},{6,4},{7,5},{8,14},{9,15},{10,... | collective-permute-start | bytes 1572872 | tf_op jit(solution)/shard_map/ppermute | solution.py:25
  86.0 2.2 %taps_kernel.1.refs_10_.refs_1_ = f32[1024,256]{1,0:T(8,128)S(1)} custom-call(f32[16,8,8,128]{3,2,1,0:T(8,128)S(1)} %copy-done.5, bf16[256,128]{1,0:T(8,128)(2,1)} %constant.72.clone.refs_1_.refs_2_, bf16[256,128]{1,0:T(8,128)(2,1)} %constant.73.clone.refs_2_.refs_3_, f32[128,128]{1,0:T(8,128)} %constant.74.clone.refs_3_.refs_4_, ...), custom_call_target="tpu_custom_call" | custom-call | tf_op jit(solution)/shard_map/taps_kernel/pallas_call | solution.py:336
  88.3 2.0 %kv_kernel.1 = f32[128,8,128]{2,1,0:T(8,128)S(1)} custom-call(f32[3,512,128]{2,1,0:T(8,128)S(1)} %copy-done.8, f32[3,512,128]{2,1,0:T(8,128)} %collective-permute-done.refs_3_.refs_1_, f32[2,512,128]{2,1,0:T(8,128)S(1)} %collective-permute-done.6.refs_2_, f32[2,512,128]{2,1,0:T(8,128)S(1)} %collective-permute-done.7.refs_3_, f32[2,512,128]{2,1,0:T(8,128)S(1)} %copy-done.20, ...), custom_call_target="tpu_custom_call" | custom-call | tf_op jit(solution)/shard_map/kv_kernel/pallas_call | solution.py:336
  90.3 0.8 copy-done.11
  91.1 7.1 %all-to-all-start.1 = ((f32[16,8,8,128]{3,2,1,0:T(8,128)}), f32[16,8,8,128]{3,2,1,0:T(8,128)}, u32[]{:S(2)}, u32[]{:S(2)}) async-start(f32[16,8,8,128]{3,2,1,0:T(8,128)} %bitcast.10), calls=%async_computation.1 | async-start | bytes 1048576 | tf_op jit(solution)/shard_map/all_to_all | solution.py:352
  98.3 0.9 copy-done.16
  99.2 4.1 %left_own_kernel.3 = (f32[2,256,128]{2,1,0:T(8,128)S(1)}, f32[2,256,128]{2,1,0:T(8,128)S(1)}, f32[3,256,128]{2,1,0:T(8,128)}, f32[3,256,128]{2,1,0:T(8,128)S(1)}) custom-call(s32[5]{0:T(128)S(1)} %stack.23.at, bf16[1024,1024]{1,0:T(8,128)(2,1)} %act.7, bf16[3,1024,1024]{2,1,0:T(8,128)(2,1)} %bitcast.17, f32[2,256,128]{2,1,0:T(8,128)S(1)} %copy-done.16), custom_call_target="tpu_custom_call" | custom-call | tf_op jit(solution)/shard_map/left_own_kernel/pallas_call | solution.py:108
  103.3 0.7 copy-done.21
  104.0 0.7 collective-permute-start.9
  104.8 2.3 %first_sum_kernel.3 = (f32[3,256,128]{2,1,0:T(8,128)}, f32[3,256,128]{2,1,0:T(8,128)}) custom-call(f32[2,256,128]{2,1,0:T(8,128)S(1)} %copy-done.17, f32[4,256,128]{2,1,0:T(8,128)} %collective-permute-done.11.refs_1_.refs_7_, f32[2,256,128]{2,1,0:T(8,128)S(1)} %copy-done.24, f32[4,256,128]{2,1,0:T(8,128)} %collective-permute-done.12.refs_3_.refs_8_.refs_9_, ...), custom_call_target="tpu_custom_call" | custom-call | tf_op jit(solution)/shard_map/first_sum_kernel/pallas_call | solution.py:336
  107.2 2.7 %collective-permute-start.14 = (f32[3,256,128]{2,1,0:T(8,128)}, f32[3,256,128]{2,1,0:T(8,128)}, u32[]{:S(2)}, u32[]{:S(2)}) collective-permute-start(f32[3,256,128]{2,1,0:T(8,128)} %get-tuple-element.60), channel_id=1, source_target_pairs={{0,6},{1,7},{2,0},{3,1},{4,2},{5,3},{6,4},{7,5},{8,14},{9,15},{10,... | collective-permute-start | bytes 1179656 | tf_op jit(solution)/shard_map/ppermute | solution.py:25
  109.8 4.6 %conv_kernel.1 = f32[16,8,8,128]{3,2,1,0:T(8,128)} custom-call(f32[16,8,8,128]{3,2,1,0:T(8,128)} %all-to-all-done.1.refs_0_, f32[1024,256]{1,0:T(8,128)S(1)} %taps_kernel.1.refs_10_.refs_1_, bf16[256,128]{1,0:T(8,128)(2,1)} %constant.72.clone.refs_1_.refs_2_, bf16[256,128]{1,0:T(8,128)(2,1)} %constant.73.clone.refs_2_.refs_3_, ...), custom_call_target="tpu_custom_call" | custom-call | tf_op jit(solution)/shard_map/conv_kernel/pallas_call | solution.py:336
  114.4 8.7 %all-to-all-start.2 = ((f32[16,8,8,128]{3,2,1,0:T(8,128)}), f32[16,8,8,128]{3,2,1,0:T(8,128)S(1)}, u32[]{:S(2)}, u32[]{:S(2)}) async-start(f32[16,8,8,128]{3,2,1,0:T(8,128)} %conv_kernel.1), calls=%async_computation.2 | async-start | bytes 1048576 | tf_op jit(solution)/shard_map/all_to_all | solution.py:352
  123.2 0.9 copy-done.14
  124.1 1.8 %second_sum_kernel.3 = (f32[2,256,128]{2,1,0:T(8,128)S(1)}, f32[2,256,128]{2,1,0:T(8,128)S(1)}, f32[2,256,128]{2,1,0:T(8,128)S(1)}) custom-call(f32[5,256,128]{2,1,0:T(8,128)S(1)} %copy-done.10, f32[5,256,128]{2,1,0:T(8,128)} %collective-permute-done.10.refs_5_.refs_1_, f32[3,256,128]{2,1,0:T(8,128)S(1)} %get-tuple-element.51.refs_2_.refs_1_, ...), custom_call_target="tpu_custom_call" | custom-call | tf_op jit(solution)/shard_map/second_sum_kernel/pallas_call | solution.py:336
  125.9 0.1 collective-permute-start.15
  126.0 2.7 %collective-permute-start.16 = (f32[2,256,128]{2,1,0:T(8,128)S(1)}, f32[2,256,128]{2,1,0:T(8,128)S(1)}, u32[]{:S(2)}, u32[]{:S(2)}) collective-permute-start(f32[2,256,128]{2,1,0:T(8,128)S(1)} %get-tuple-element.62), channel_id=1, source_target_pairs={{0,6},{1,7},{2,0},{3,1},{4,2},{5,3},{6,4},{7,5},{8,14},{9,15},{10,... | collective-permute-start | bytes 786440 | tf_op jit(solution)/shard_map/ppermute | solution.py:25
  128.7 6.4 %collective-permute-done.15.refs_3_ = f32[2,256,128]{2,1,0:T(8,128)S(1)} collective-permute-done((f32[2,256,128]{2,1,0:T(8,128)S(1)}, f32[2,256,128]{2,1,0:T(8,128)S(1)}, u32[]{:S(2)}, u32[]{:S(2)}) %collective-permute-start.15) | collective-permute-done | bytes 262176 | tf_op jit(solution)/shard_map/ppermute | solution.py:25
  135.1 2.0 %collective-permute-done.17.refs_10_ = f32[2,256,128]{2,1,0:T(8,128)S(1)} collective-permute-done((f32[2,256,128]{2,1,0:T(8,128)S(1)}, f32[2,256,128]{2,1,0:T(8,128)S(1)}, u32[]{:S(2)}, u32[]{:S(2)}) %collective-permute-start.17) | collective-permute-done | bytes 262176 | tf_op jit(solution)/shard_map/ppermute | solution.py:29
  137.1 2.6 %gate_kernel.1 = f32[1024,128]{1,0:T(8,128)} custom-call(f32[128,8,128]{2,1,0:T(8,128)S(1)} %bitcast.9, f32[3,256,128]{2,1,0:T(8,128)S(1)} %get-tuple-element.51.refs_2_.refs_1_, f32[3,256,128]{2,1,0:T(8,128)} %collective-permute-done.9.refs_3_.refs_2_, f32[2,256,128]{2,1,0:T(8,128)S(1)} %collective-permute-done.15.refs_3_, ...), custom_call_target="tpu_custom_call" | custom-call | tf_op jit(solution)/shard_map/gate_kernel/pallas_call | solution.py:336
  (58 shorter events, 0.1 us)
Async XLA Ops:
  6.2 31.0 %copy-start = (f32[5,512,128]{2,1,0:T(8,128)}, f32[5,512,128]{2,1,0:T(8,128)S(1)}, u32[]{:S(2)}) copy-start(f32[5,512,128]{2,1,0:T(8,128)S(1)} %get-tuple-element.38.refs_4_.refs_0_) | copy-start | bytes 3932164
  6.2 31.0 %collective-permute-start.1 = (f32[5,512,128]{2,1,0:T(8,128)S(1)}, f32[5,512,128]{2,1,0:T(8,128)S(1)}, u32[]{:S(2)}, u32[]{:S(2)}) collective-permute-start(f32[5,512,128]{2,1,0:T(8,128)S(1)} %get-tuple-element.39), channel_id=1, source_target_pairs={{0,1},{1,0},{2,3},{3,2},{4,5},{5,4},{6,7},{7,6},{8,9},{9,8},{10,11... | collective-permute-start | bytes 3932168 | tf_op jit(solution)/shard_map/ppermute | solution.py:29
  8.8 24.9 %collective-permute-start.2 = (f32[4,512,128]{2,1,0:T(8,128)S(1)}, f32[4,512,128]{2,1,0:T(8,128)S(1)}, u32[]{:S(2)}, u32[]{:S(2)}) collective-permute-start(f32[4,512,128]{2,1,0:T(8,128)S(1)} %get-tuple-element.41), channel_id=1, source_target_pairs={{0,2},{1,3},{2,4},{3,5},{4,6},{5,7},{6,0},{7,1},{8,10},{9,11},{10,... | collective-permute-start | bytes 3145736 | tf_op jit(solution)/shard_map/ppermute | solution.py:25
  10.0 23.7 %collective-permute-start.3 = (f32[4,512,128]{2,1,0:T(8,128)S(1)}, f32[4,512,128]{2,1,0:T(8,128)S(1)}, u32[]{:S(2)}, u32[]{:S(2)}) collective-permute-start(f32[4,512,128]{2,1,0:T(8,128)S(1)} %get-tuple-element.43), channel_id=1, source_target_pairs={{0,6},{1,7},{2,0},{3,1},{4,2},{5,3},{6,4},{7,5},{8,14},{9,15},{10,... | collective-permute-start | bytes 3145736 | tf_op jit(solution)/shard_map/ppermute | solution.py:25
  16.6 0.9 copy-start.6
  17.5 0.8 copy-start.19
  18.3 35.9 %collective-permute-start = (f32[3,512,128]{2,1,0:T(8,128)}, f32[3,512,128]{2,1,0:T(8,128)}, u32[]{:S(2)}, u32[]{:S(2)}) collective-permute-start(f32[3,512,128]{2,1,0:T(8,128)} %get-tuple-element.37), channel_id=1, source_target_pairs={{0,1},{1,0},{2,3},{3,2},{4,5},{5,4},{6,7},{7,6},{8,9},{9,8},{10,11... | collective-permute-start | bytes 2359304 | tf_op jit(solution)/shard_map/ppermute | solution.py:29
  37.3 1.6 %copy-start.2 = (f32[5,512,128]{2,1,0:T(8,128)}, f32[5,512,128]{2,1,0:T(8,128)S(1)}, u32[]{:S(2)}) copy-start(f32[5,512,128]{2,1,0:T(8,128)S(1)} %collective-permute-done.1.refs_5_.refs_1_) | copy-start | bytes 3932164
  37.3 4.0 %copy-start.18 = (f32[1024,128]{1,0:T(8,128)S(1)}, f32[1024,128]{1,0:T(8,128)}, u32[]{:S(2)}) copy-start(f32[1024,128]{1,0:T(8,128)} %refs_0_.1) | copy-start | bytes 1572868
  38.8 25.1 %collective-permute-start.5 = (f32[3,512,128]{2,1,0:T(8,128)}, f32[3,512,128]{2,1,0:T(8,128)}, u32[]{:S(2)}, u32[]{:S(2)}) collective-permute-start(f32[3,512,128]{2,1,0:T(8,128)} %get-tuple-element.45), channel_id=1, source_target_pairs={{0,6},{1,7},{2,0},{3,1},{4,2},{5,3},{6,4},{7,5},{8,14},{9,15},{10,... | collective-permute-start | bytes 2359304 | tf_op jit(solution)/shard_map/ppermute | solution.py:25
  41.2 22.7 %collective-permute-start.4 = (f32[3,512,128]{2,1,0:T(8,128)}, f32[3,512,128]{2,1,0:T(8,128)}, u32[]{:S(2)}, u32[]{:S(2)}) collective-permute-start(f32[3,512,128]{2,1,0:T(8,128)} %get-tuple-element.44.refs_1_), channel_id=1, source_target_pairs={{0,2},{1,3},{2,4},{3,5},{4,6},{5,7},{6,0},{7,1},{8,10},{9,11},{10,... | collective-permute-start | bytes 2359304 | tf_op jit(solution)/shard_map/ppermute | solution.py:25
  41.6 0.8 copy-start.12
  42.4 21.5 %all-to-all-start = ((f32[16,8,8,128]{3,2,1,0:T(8,128)}), f32[16,8,8,128]{3,2,1,0:T(8,128)S(1)}, u32[]{:S(2)}, u32[]{:S(2)}) async-start(f32[16,8,8,128]{3,2,1,0:T(8,128)} %bitcast.11), calls=%async_computation | async-start | bytes 1048576 | tf_op jit(solution)/shard_map/all_to_all | solution.py:352
  63.9 5.8 %copy-start.4 = (f32[16,8,8,128]{3,2,1,0:T(8,128)}, f32[16,8,8,128]{3,2,1,0:T(8,128)S(1)}, u32[]{:S(2)}) copy-start(f32[16,8,8,128]{3,2,1,0:T(8,128)S(1)} %all-to-all-done.refs_9_.refs_0_) | copy-start | bytes 1572868
  63.9 1.5 %copy-start.1 = (f32[5,512,128]{2,1,0:T(8,128)S(1)}, f32[5,512,128]{2,1,0:T(8,128)}, u32[]{:S(2)}) copy-start(f32[5,512,128]{2,1,0:T(8,128)} %copy-done) | copy-start | bytes 3932164
  65.4 1.3 copy-start.3
  66.8 1.1 copy-start.7
  69.7 12.9 %collective-permute-start.7 = (f32[2,512,128]{2,1,0:T(8,128)S(1)}, f32[2,512,128]{2,1,0:T(8,128)S(1)}, u32[]{:S(2)}, u32[]{:S(2)}) collective-permute-start(f32[2,512,128]{2,1,0:T(8,128)S(1)} %get-tuple-element.47), channel_id=1, source_target_pairs={{0,6},{1,7},{2,0},{3,1},{4,2},{5,3},{6,4},{7,5},{8,14},{9,15},{10,... | collective-permute-start | bytes 1572872 | tf_op jit(solution)/shard_map/ppermute | solution.py:25
  72.7 15.5 %collective-permute-start.8 = (f32[2,512,128]{2,1,0:T(8,128)S(1)}, f32[2,512,128]{2,1,0:T(8,128)S(1)}, u32[]{:S(2)}, u32[]{:S(2)}) collective-permute-start(f32[2,512,128]{2,1,0:T(8,128)S(1)} %get-tuple-element.49), channel_id=1, source_target_pairs={{0,1},{1,0},{2,3},{3,2},{4,5},{5,4},{6,7},{7,6},{8,9},{9,8},{10,11... | collective-permute-start | bytes 1572872 | tf_op jit(solution)/shard_map/ppermute | solution.py:29
  73.5 12.6 %copy-start.5 = (f32[16,8,8,128]{3,2,1,0:T(8,128)S(1)}, f32[16,8,8,128]{3,2,1,0:T(8,128)}, u32[]{:S(2)}) copy-start(f32[16,8,8,128]{3,2,1,0:T(8,128)} %copy-done.4) | copy-start | bytes 1572868
  73.5 14.8 %collective-permute-start.6 = (f32[2,512,128]{2,1,0:T(8,128)S(1)}, f32[2,512,128]{2,1,0:T(8,128)S(1)}, u32[]{:S(2)}, u32[]{:S(2)}) collective-permute-start(f32[2,512,128]{2,1,0:T(8,128)S(1)} %get-tuple-element.46.refs_1_), channel_id=1, source_target_pairs={{0,2},{1,3},{2,4},{3,5},{4,6},{5,7},{6,0},{7,1},{8,10},{9,11},{10,... | collective-permute-start | bytes 1572872 | tf_op jit(solution)/shard_map/ppermute | solution.py:25
  79.4 8.8 %copy-start.9 = (f32[5,256,128]{2,1,0:T(8,128)}, f32[5,256,128]{2,1,0:T(8,128)S(1)}, u32[]{:S(2)}) copy-start(f32[5,256,128]{2,1,0:T(8,128)S(1)} %get-tuple-element.53.refs_4_.refs_0_) | copy-start | bytes 1966084
  79.4 8.9 %copy-start.15 = (f32[2,256,128]{2,1,0:T(8,128)}, f32[2,256,128]{2,1,0:T(8,128)S(1)}, u32[]{:S(2)}) copy-start(f32[2,256,128]{2,1,0:T(8,128)S(1)} %get-tuple-element.50.refs_1_.refs_0_) | copy-start | bytes 786436
  79.4 10.9 %copy-start.23 = (f32[2,256,128]{2,1,0:T(8,128)}, f32[2,256,128]{2,1,0:T(8,128)S(1)}, u32[]{:S(2)}) copy-start(f32[2,256,128]{2,1,0:T(8,128)S(1)} %get-tuple-element.57.refs_2_) | copy-start | bytes 786436
  79.4 8.9 %copy-start.8 = (f32[3,512,128]{2,1,0:T(8,128)S(1)}, f32[3,512,128]{2,1,0:T(8,128)}, u32[]{:S(2)}) copy-start(f32[3,512,128]{2,1,0:T(8,128)} %copy-done.6) | copy-start | bytes 2359300
  79.4 8.9 %copy-start.20 = (f32[2,512,128]{2,1,0:T(8,128)S(1)}, f32[2,512,128]{2,1,0:T(8,128)}, u32[]{:S(2)}) copy-start(f32[2,512,128]{2,1,0:T(8,128)} %copy-done.19) | copy-start | bytes 1572868
  79.4 25.4 %collective-permute-start.10 = (f32[5,256,128]{2,1,0:T(8,128)}, f32[5,256,128]{2,1,0:T(8,128)}, u32[]{:S(2)}, u32[]{:S(2)}) collective-permute-start(f32[5,256,128]{2,1,0:T(8,128)} %get-tuple-element.54), channel_id=1, source_target_pairs={{0,1},{1,0},{2,3},{3,2},{4,5},{5,4},{6,7},{7,6},{8,9},{9,8},{10,11... | collective-permute-start | bytes 1966088 | tf_op jit(solution)/shard_map/ppermute | solution.py:29
  80.2 24.6 %collective-permute-start.11 = (f32[4,256,128]{2,1,0:T(8,128)}, f32[4,256,128]{2,1,0:T(8,128)}, u32[]{:S(2)}, u32[]{:S(2)}) collective-permute-start(f32[4,256,128]{2,1,0:T(8,128)} %get-tuple-element.56), channel_id=1, source_target_pairs={{0,2},{1,3},{2,4},{3,5},{4,6},{5,7},{6,0},{7,1},{8,10},{9,11},{10,... | collective-permute-start | bytes 1572872 | tf_op jit(solution)/shard_map/ppermute | solution.py:25
  82.6 22.2 %collective-permute-start.12 = (f32[4,256,128]{2,1,0:T(8,128)}, f32[4,256,128]{2,1,0:T(8,128)}, u32[]{:S(2)}, u32[]{:S(2)}) collective-permute-start(f32[4,256,128]{2,1,0:T(8,128)} %get-tuple-element.58), channel_id=1, source_target_pairs={{0,6},{1,7},{2,0},{3,1},{4,2},{5,3},{6,4},{7,5},{8,14},{9,15},{10,... | collective-permute-start | bytes 1572872 | tf_op jit(solution)/shard_map/ppermute | solution.py:25
  90.3 0.8 copy-start.11
  91.1 18.7 %all-to-all-start.1 = ((f32[16,8,8,128]{3,2,1,0:T(8,128)}), f32[16,8,8,128]{3,2,1,0:T(8,128)}, u32[]{:S(2)}, u32[]{:S(2)}) async-start(f32[16,8,8,128]{3,2,1,0:T(8,128)} %bitcast.10), calls=%async_computation.1 | async-start | bytes 1048576 | tf_op jit(solution)/shard_map/all_to_all | solution.py:352
  98.2 0.9 copy-start.16
  99.2 5.6 %copy-start.10 = (f32[5,256,128]{2,1,0:T(8,128)S(1)}, f32[5,256,128]{2,1,0:T(8,128)}, u32[]{:S(2)}) copy-start(f32[5,256,128]{2,1,0:T(8,128)} %copy-done.9) | copy-start | bytes 1966084
  99.2 5.6 %copy-start.17 = (f32[2,256,128]{2,1,0:T(8,128)S(1)}, f32[2,256,128]{2,1,0:T(8,128)}, u32[]{:S(2)}) copy-start(f32[2,256,128]{2,1,0:T(8,128)} %copy-done.15) | copy-start | bytes 786436
  99.2 5.6 %copy-start.24 = (f32[2,256,128]{2,1,0:T(8,128)S(1)}, f32[2,256,128]{2,1,0:T(8,128)}, u32[]{:S(2)}) copy-start(f32[2,256,128]{2,1,0:T(8,128)} %copy-done.23) | copy-start | bytes 786436
  103.3 0.7 copy-start.21
  104.0 3.1 %copy-start.13 = (f32[2,256,128]{2,1,0:T(8,128)}, f32[2,256,128]{2,1,0:T(8,128)S(1)}, u32[]{:S(2)}) copy-start(f32[2,256,128]{2,1,0:T(8,128)S(1)} %get-tuple-element.55.refs_6_.refs_4_) | copy-start | bytes 786436
  104.0 19.1 %collective-permute-start.9 = (f32[3,256,128]{2,1,0:T(8,128)}, f32[3,256,128]{2,1,0:T(8,128)}, u32[]{:S(2)}, u32[]{:S(2)}) collective-permute-start(f32[3,256,128]{2,1,0:T(8,128)} %get-tuple-element.52), channel_id=1, source_target_pairs={{0,1},{1,0},{2,3},{3,2},{4,5},{5,4},{6,7},{7,6},{8,9},{9,8},{10,11... | collective-permute-start | bytes 1179656 | tf_op jit(solution)/shard_map/ppermute | solution.py:29
  107.2 16.0 %collective-permute-start.13 = (f32[3,256,128]{2,1,0:T(8,128)}, f32[3,256,128]{2,1,0:T(8,128)S(1)}, u32[]{:S(2)}, u32[]{:S(2)}) collective-permute-start(f32[3,256,128]{2,1,0:T(8,128)} %get-tuple-element.59), channel_id=1, source_target_pairs={{0,2},{1,3},{2,4},{3,5},{4,6},{5,7},{6,0},{7,1},{8,10},{9,11},{10,... | collective-permute-start | bytes 1179656 | tf_op jit(solution)/shard_map/ppermute | solution.py:25
  107.2 16.0 %collective-permute-start.14 = (f32[3,256,128]{2,1,0:T(8,128)}, f32[3,256,128]{2,1,0:T(8,128)}, u32[]{:S(2)}, u32[]{:S(2)}) collective-permute-start(f32[3,256,128]{2,1,0:T(8,128)} %get-tuple-element.60), channel_id=1, source_target_pairs={{0,6},{1,7},{2,0},{3,1},{4,2},{5,3},{6,4},{7,5},{8,14},{9,15},{10,... | collective-permute-start | bytes 1179656 | tf_op jit(solution)/shard_map/ppermute | solution.py:25
  114.4 22.7 %all-to-all-start.2 = ((f32[16,8,8,128]{3,2,1,0:T(8,128)}), f32[16,8,8,128]{3,2,1,0:T(8,128)S(1)}, u32[]{:S(2)}, u32[]{:S(2)}) async-start(f32[16,8,8,128]{3,2,1,0:T(8,128)} %conv_kernel.1), calls=%async_computation.2 | async-start | bytes 1048576 | tf_op jit(solution)/shard_map/all_to_all | solution.py:352
  123.2 1.0 copy-start.14
  124.1 13.0 %copy-start.22 = (f32[2,256,128]{2,1,0:T(8,128)S(1)}, f32[2,256,128]{2,1,0:T(8,128)}, u32[]{:S(2)}) copy-start(f32[2,256,128]{2,1,0:T(8,128)} %copy-done.21) | copy-start | bytes 786436
  125.9 9.2 %collective-permute-start.15 = (f32[2,256,128]{2,1,0:T(8,128)S(1)}, f32[2,256,128]{2,1,0:T(8,128)S(1)}, u32[]{:S(2)}, u32[]{:S(2)}) collective-permute-start(f32[2,256,128]{2,1,0:T(8,128)S(1)} %get-tuple-element.61), channel_id=1, source_target_pairs={{0,2},{1,3},{2,4},{3,5},{4,6},{5,7},{6,0},{7,1},{8,10},{9,11},{10,... | collective-permute-start | bytes 786440 | tf_op jit(solution)/shard_map/ppermute | solution.py:25
  126.0 9.1 %collective-permute-start.16 = (f32[2,256,128]{2,1,0:T(8,128)S(1)}, f32[2,256,128]{2,1,0:T(8,128)S(1)}, u32[]{:S(2)}, u32[]{:S(2)}) collective-permute-start(f32[2,256,128]{2,1,0:T(8,128)S(1)} %get-tuple-element.62), channel_id=1, source_target_pairs={{0,6},{1,7},{2,0},{3,1},{4,2},{5,3},{6,4},{7,5},{8,14},{9,15},{10,... | collective-permute-start | bytes 786440 | tf_op jit(solution)/shard_map/ppermute | solution.py:25
  128.7 8.4 %collective-permute-start.17 = (f32[2,256,128]{2,1,0:T(8,128)S(1)}, f32[2,256,128]{2,1,0:T(8,128)S(1)}, u32[]{:S(2)}, u32[]{:S(2)}) collective-permute-start(f32[2,256,128]{2,1,0:T(8,128)S(1)} %get-tuple-element.64), channel_id=1, source_target_pairs={{0,1},{1,0},{2,3},{3,2},{4,5},{5,4},{6,7},{7,6},{8,9},{9,8},{10,11... | collective-permute-start | bytes 786440 | tf_op jit(solution)/shard_map/ppermute | solution.py:29

commit v4 on v3

--- a/solution.py
+++ b/solution.py
@@ -43,55 +43,67 @@
         self.z_start = [h % parts * self.rows for h in range(2)]
         self.x_start = [tokens // 2 + start for start in self.z_start]
 
-    def x_part(self, act, weights, half, z_at):
-        rows = act[self.x_start[half] : self.x_start[half] + self.rows]
-        return parts_of(rows, weights[half % len(weights)], z_at)
-
-    def z_part(self, act, weights, half, z_at):
-        rows = act[self.z_start[half] : self.z_start[half] + self.rows]
-        return parts_of(rows, weights[half % len(weights)], z_at)
-
-
-def far_near_kernel(halves, place, act, weights, outs):
-    send_r, send_l, keep_r, keep_l, z_other, z_mine = outs
-    z_at = place[4]
-    step = pl.program_id(0)
-
-    @pl.when(step == 0)
-    def _():
-        send_r[0], send_r[1] = halves.x_part(act, weights, 0, z_at)
-        send_l[0], send_l[1] = halves.x_part(act, weights, 1, z_at)
-        z_other[3], z_mine[3] = halves.z_part(act, weights, 0, z_at)
-        z_other[4], z_mine[4] = halves.z_part(act, weights, 1, z_at)
-
-    @pl.when(step == 1)
-    def _():
-        send_r[2], send_r[3] = halves.x_part(act, weights, 1, z_at)
-        z_other[0], z_mine[0] = halves.z_part(act, weights, 0, z_at)
-        z_other[1], z_mine[1] = halves.z_part(act, weights, 1, z_at)
-        keep_r[0], keep_r[1] = halves.x_part(act, weights, 0, z_at)
-
-    @pl.when(step == 2)
-    def _():
-        send_l[2], send_l[3] = halves.x_part(act, weights, 0, z_at)
-        z_other[2], z_mine[2] = halves.z_part(act, weights, 0, z_at)
-        keep_l[0], keep_l[1] = halves.x_part(act, weights, 1, z_at)
-
-
-def left_own_kernel(halves, place, act, weights, outs):
-    x_other, x_mine, z_other, z_mine = outs
-    z_at = place[4]
-    step = pl.program_id(0)
-
-    @pl.when(step == 0)
-    def _():
-        z_other[2], z_mine[2] = halves.z_part(act, weights, 1, z_at)
-
-    @pl.when(step == 1)
-    def _():
-        for half in range(2):
-            z_other[half], z_mine[half] = halves.z_part(act, weights, half, z_at)
-            x_other[half], x_mine[half] = halves.x_part(act, weights, half, z_at)
+    def fill(self, place, act, weights, wanted):
+        for j in range(len(weights)):
+            mine = [w for w in wanted if len(weights) == 1 or w[0] == j]
+            starts = [(self.z_start if z_first else self.x_start)[h] for h, z_first, _, _ in mine]
+            if not mine:
+                continue
+            low, high = min(starts), max(starts) + self.rows
+            other, own = parts_of(act[low:high], weights[j], place[4])
+            for start, (_, _, put_other, put_mine) in zip(starts, mine):
+                rows = slice(start - low, start - low + self.rows)
+                put_other[0][put_other[1]] = other[rows]
+                if put_mine is not None:
+                    put_mine[0][put_mine[1]] = own[rows]
+
+
+X, Z = False, True
+
+
+def first_kernel(halves, place, act, weights, outs):
+    send_r, send_l, z_other, z_mine = outs
+    steps = (
+        [
+            (0, X, (send_r, 0), (send_r, 1)),
+            (1, X, (send_l, 0), (send_l, 1)),
+            (0, Z, (z_other, 0), (z_mine, 0)),
+            (1, Z, (z_other, 1), (z_mine, 1)),
+        ],
+        [
+            (1, X, (send_r, 2), (send_r, 3)),
+            (0, Z, (z_other, 2), (z_mine, 2)),
+            (1, Z, (z_other, 3), (z_mine, 3)),
+        ],
+        [(0, X, (send_l, 2), (send_l, 3))],
+    )
+    run_steps(halves, place, act, weights, steps)
+
+
+def second_kernel(halves, place, act, weights, outs):
+    keep_r, keep_l, z_other, z_mine, x_other, x_mine = outs
+    steps = (
+        [(0, X, (keep_r, 0), (keep_r, 1))],
+        [
+            (1, X, (keep_l, 0), (keep_l, 1)),
+            (0, Z, (z_other, 0), (z_mine, 0)),
+            (1, Z, (z_other, 1), (z_mine, 1)),
+        ],
+        [
+            (0, X, (x_other, 0), (x_mine, 0)),
+            (1, X, (x_other, 1), (x_mine, 1)),
+            (0, Z, (z_other, 2), (z_mine, 2)),
+            (1, Z, (z_other, 3), (z_mine, 3)),
+        ],
+    )
+    run_steps(halves, place, act, weights, steps)
+
+
+def run_steps(halves, place, act, weights, steps):
+    for i, wanted in enumerate(steps):
+        pl.when(pl.program_id(0) == i)(
+            functools.partial(halves.fill, place, act, weights, wanted)
+        )
 
 
 def project(kernel, halves, place, activations, weight, owner, steps, outs, after=()):
@@ -115,7 +127,9 @@
             + [pl.BlockSpec(memory_space=pl.ANY)] * len(after),
             out_specs=[pl.BlockSpec(memory_space=pltpu.VMEM)] * len(outs),
         ),
-        out_shape=[jax.ShapeDtypeStruct(shape, jnp.float32) for shape in outs],
+        out_shape=[
+            jax.ShapeDtypeStruct((count, halves.rows, BLOCK), jnp.float32) for count in outs
+        ],
         compiler_params=params(24),
         name=kernel.__name__,
     )(place, activations, *[weight] * count, *after)
@@ -125,84 +139,129 @@
     for half, (keep, got, out) in enumerate(((keep_r, got_r, out_r), (keep_l, got_l, out_l))):
         out[0] = keep[0] + got[0]
         out[1] = keep[1] + got[1]
-        out[2] = z_mine[3 + half] + z_got[3 + half]
-
-
-def second_sum_kernel(
-    z_near, z_near_got, z_own, z_own_got, x_own, dep_r, dep_l, got_r, got_l, out_r, out_l, out_x
-):
-    out_r[0] = z_near[0] + z_near_got[0] + dep_r[2]
-    out_r[1] = z_near[1] + z_near_got[1]
-    out_l[0] = z_near[2] + z_near_got[2]
-    out_l[1] = z_own[2] + z_own_got[2] + dep_l[2]
-    out_x[0] = x_own[0] + (dep_r[0] + got_l[2])
-    out_x[1] = x_own[1] + (got_r[2] + dep_l[0])
-
-
-def reduce_chunks(halves, place, activations, weight, after=(), beside=None):
-    def pieces(count):
-        return (count, halves.rows, BLOCK)
-
-    send_r, send_l, keep_r, keep_l, z_near, z_near_mine = project(
-        far_near_kernel,
+        out[2] = z_mine[half] + z_got[half]
+
+
+def beside_two_kernel(z_mine, z_got, x_other, x_mine, got_r, got_l, out_z, out_other, out_mine):
+    for half in range(2):
+        out_z[half] = z_mine[2 + half] + z_got[2 + half]
+    for half, got in enumerate((got_l, got_r)):
+        out_other[half] = x_other[half] + got[2]
+        out_mine[half] = x_mine[half] + got[3]
+
+
+def second_sum_kernel(z_part, z_mine, z_got, x_part, dep_r, dep_l, out_r, out_l, out_x):
+    out_r[0] = z_part[0] + dep_r[2]
+    out_r[1] = z_part[1]
+    out_l[0] = z_mine[0] + z_got[0]
+    out_l[1] = z_mine[1] + z_got[1] + dep_l[2]
+    out_x[0] = x_part[0] + dep_r[0]
+    out_x[1] = x_part[1] + dep_l[0]
+
+
+def beside_three_kernel(z_mine, z_got, x_part, dep_r, dep_l, out_z, out_x):
+    for half, dep in enumerate((dep_r, dep_l)):
+        out_z[half] = z_mine[2 + half] + z_got[2 + half]
+        out_x[half] = x_part[half] + dep[1]
+
+
+def shapes(halves, *counts):
+    return [(count, halves.rows, BLOCK) for count in counts]
+
+
+def project_all(halves, place, activations, weight, after=()):
+    firsts = project(
+        first_kernel, halves, place, activations, weight, 0, 3, [4, 4, 4, 4], after=after
+    )
+    seconds = project(
+        second_kernel,
         halves,
         place,
         activations,
         weight,
-        0,
+        1,
         3,
-        [pieces(4), pieces(4), pieces(2), pieces(2), pieces(5), pieces(5)],
-        after=after,
-    )
-    got_r, got_l, z_near = shift_x(send_r, 1), shift_x(send_l, -1), swap_z(z_near)
-    x_own, x_mine, z_own, z_mine = project(
-        left_own_kernel,
-        halves,
-        place,
-        activations,
-        weight,
-        2,
-        2,
-        [pieces(2), pieces(2), pieces(3), pieces(3)],
-        after=(keep_r,),
-    )
+        [2, 2, 4, 4, 2, 2],
+        after=(firsts[3],),
+    )
+    return firsts, seconds
+
+
+def reduce_chunks(halves, sends, firsts, seconds, beside_one=None, beside_two=None):
+    _, _, _, z_first_mine = firsts
+    keep_r, keep_l, z_other, z_mine, x_other, x_mine = seconds
+    send_r, send_l, z_send = sends
+    got_r, got_l, z_first_got = shift_x(send_r, 1), shift_x(send_l, -1), swap_z(z_send)
+    ready = beside_one(keep_r) if beside_one else ()
     dep_r, dep_l = call(
         first_sum_kernel,
-        [pieces(3), pieces(3)],
+        shapes(halves, 3, 3),
         keep_r,
         got_r,
         keep_l,
         got_l,
-        z_near_mine,
-        z_near,
-        after=(x_own,),
-    )
-    moved = (beside(dep_r),) if beside else ()
-    dep_r, dep_l, z_own = shift_x(dep_r, 1), shift_x(dep_l, -1), swap_z(z_own)
+        z_first_mine,
+        z_first_got,
+        after=(x_other,) + tuple(ready),
+    )
+    z_part, x_part_other, x_part_mine = call(
+        beside_two_kernel,
+        shapes(halves, 2, 2, 2),
+        z_first_mine,
+        z_first_got,
+        x_other,
+        x_mine,
+        got_r,
+        got_l,
+        after=(dep_r,),
+    )
+    ready = beside_two(dep_r) if beside_two else ()
+    dep_r, dep_l, z_got = shift_x(dep_r, 1), shift_x(dep_l, -1), swap_z(z_other)
     last_r, last_l, x_sum = call(
         second_sum_kernel,
-        [pieces(2), pieces(2), pieces(2)],
-        z_near_mine,
-        z_near,
+        shapes(halves, 2, 2, 2),
+        z_part,
         z_mine,
-        z_own,
-        x_own,
+        z_got,
+        x_part_other,
         dep_r,
         dep_l,
-        got_r,
-        got_l,
-        after=moved,
+        after=ready,
     )
     last = last_r
+    z_part, x_part = call(
+        beside_three_kernel,
+        shapes(halves, 2, 2),
+        z_mine,
+        z_got,
+        x_part_mine,
+        dep_r,
+        dep_l,
+        after=(last,),
+    )
     last_r, last_l, x_sum = shift_x(last_r, 1), shift_x(last_l, -1), swap_z(x_sum)
-    return (z_mine, z_own, last_r, last_l, x_mine, dep_r, got_r, dep_l, got_l, x_sum), moved, last
-
-
-def summed(z_own, z_got, z_r, z_l, x_own, dep_r, got_r, dep_l, got_l, x_got):
-    return [(z_own[h] + z_got[h]) + (z_r[h] + z_l[h]) for h in range(2)], [
-        x_own[0] + (dep_r[1] + got_l[3]) + x_got[0],
-        x_own[1] + (got_r[3] + dep_l[1]) + x_got[1],
+    return (z_part, last_r, last_l, x_part, x_sum), last
+
+
+def summed(z_part, z_r, z_l, x_part, x_got):
+    return [z_part[h] + (z_r[h] + z_l[h]) for h in range(2)] + [
+        x_part[h] + x_got[h] for h in range(2)
     ]
+
+
+def release(values, after):
+    def body(*refs):
+        pass
+
+    count = len(values)
+    return pl.pallas_call(
+        body,
+        in_specs=[pl.BlockSpec(memory_space=pl.ANY)] * (count + 1),
+        out_specs=[pl.BlockSpec(memory_space=pl.ANY)] * count,
+        out_shape=[jax.ShapeDtypeStruct(value.shape, value.dtype) for value in values],
+        input_output_aliases={i: i for i in range(count)},
+        name="release",
+    )(*values, after)
 
 
 def split_bf16(table):
@@ -303,23 +362,24 @@
 
 def kv_kernel(*refs):
     parts, out_ref, kv_ref = refs[:-2], refs[-2], refs[-1]
-    z_total, x_total = summed(*parts)
-    rows = z_total[0].shape[0]
-    kv_ref[:rows] = z_total[0] * z_total[1]
-    kv_ref[rows:] = x_total[0] * x_total[1]
+    z_key, z_value, x_key, x_value = summed(*parts)
+    rows = z_key.shape[0]
+    kv_ref[:rows] = z_key * z_value
+    kv_ref[rows:] = x_key * x_value
     turn_blocks(kv_ref, out_ref)
 
 
-def gate_kernel(conv_ref, *refs):
+def query_kernel(*refs):
     parts, out_ref = refs[:-1], refs[-1]
+    for i, query in enumerate(summed(*parts)):
+        rows = query.shape[0]
+        out_ref[i * rows : (i + 1) * rows] = query
+
+
+def gate_kernel(conv_ref, query_ref, out_ref):
     for b in range(conv_ref.shape[1]):
-        out_ref[b * BLOCK : (b + 1) * BLOCK, :] = conv_ref[:, b, :].T
-    z_total, x_total = summed(*parts)
-    start = 0
-    for query in z_total + x_total:
-        end = start + query.shape[0]
-        out_ref[start:end] = out_ref[start:end] * query
-        start = end
+        rows = slice(b * BLOCK, (b + 1) * BLOCK)
+        out_ref[rows] = conv_ref[:, b, :].T * query_ref[rows]
 
 
 def call(kernel, out_shapes, *operands, after=(), scratch=(), tables=()):
@@ -369,32 +429,40 @@
     weight = in_hbm(jnp.transpose(proj_weight, (1, 0, 2)))
     activations = in_hbm(activations)
 
+    kv_halves, q_halves = Halves(tokens, (1, 2)), Halves(tokens, (0,))
+    hold = {}
+
     def move_taps(ready):
         turned = call(taps_turn_kernel, turned_shape, filter_taps, after=(ready,))
-        return exchange(turned.reshape(moved_shape))
-
-    kv_parts, (taps,), kv_last = reduce_chunks(
-        Halves(tokens, (1, 2)), place, activations, weight, beside=move_taps
-    )
-    q_parts, _, _ = reduce_chunks(
-        Halves(tokens, (0,)), place, activations, weight, after=(kv_last,)
-    )
-
-    spectrum = call(
-        taps_kernel,
-        (owned * length // BLOCK, 2 * BLOCK),
-        taps,
-        tables=first + turn + second,
-    )
+        hold["taps"] = exchange(turned.reshape(moved_shape))
+        return (hold["taps"],)
+
+    def prepare(ready):
+        hold["spectrum"] = call(
+            taps_kernel,
+            (owned * length // BLOCK, 2 * BLOCK),
+            hold["taps"],
+            tables=first + turn + second,
+        )
+        hold["query"] = project_all(q_halves, place, activations, weight, after=(ready,))
+        return hold["spectrum"], hold["query"][1][0]
+
+    kv_firsts, kv_seconds = project_all(kv_halves, place, activations, weight)
+    kv_parts, kv_last = reduce_chunks(
+        kv_halves, kv_firsts[:3], kv_firsts, kv_seconds, move_taps, prepare
+    )
+    spectrum, (q_firsts, q_seconds) = hold["spectrum"], hold["query"]
 
     kv = call(
         kv_kernel,
         turned_shape,
         *kv_parts,
-        after=(spectrum,),
         scratch=[pltpu.VMEM((tokens, channels), jnp.float32)],
     )
     moved = exchange(kv.reshape(moved_shape))
+    q_sends = release(q_firsts[:3], kv_last)
+    q_parts, _ = reduce_chunks(q_halves, q_sends, q_firsts, q_seconds)
+    query = call(query_kernel, (tokens, channels), *q_parts)
     convolved = call(
         conv_kernel,
         moved_shape,
@@ -403,7 +471,7 @@
         tables=first + turn + second + back + inverse,
     )
     home = exchange(convolved).reshape(turned_shape)
-    return call(gate_kernel, (tokens, channels), home, *q_parts)
+    return call(gate_kernel, (tokens, channels), home, query)
 
 
 def solution(mesh):

time: 141 us -> 140 us (level)
  local copies, waits for them, and re-layouts: 10.2 us -> 20.4 us
  starting transfers between devices: 48.1 us -> 38.2 us
  waiting for transfers between devices: 40.8 us -> 33.3 us
  Pallas kernels: 40.3 us -> 46 us
    unnamed x50 -> x70, local copies, waits for them, and re-layouts: 10.1 us -> 20.3 us
    ppermute x12, waiting for transfers between devices: 24.1 us -> 14.8 us  [shift_x(): lax.ppermute(value, 'chan', [(i, (i + 2 * step) % 8) for i in range(8)])]
    all_to_all x3, waiting for transfers between devices: 9.71 us -> 16.6 us  [exchange(): return lax.all_to_all(value, 'seq', split_axis=0, concat_axis=0, tiled=True)]
    all_to_all x3, starting transfers between devices: 26.3 us -> 20 us  [exchange(): return lax.all_to_all(value, 'seq', split_axis=0, concat_axis=0, tiled=True)]
    pallas_call x9 -> x14, Pallas kernels: 19 us -> 24.2 us  [call(): pl.pallas_call(body, grid=(1,), in_specs=[pl.BlockSpec(memory_space=pltpu...]
    ppermute x6, waiting for transfers between devices: 7.01 us -> 1.92 us  [swap_z(): return lax.ppermute(value, 'chan', [(i, i ^ 1) for i in range(8)])]
    ppermute x12, starting transfers between devices: 16.9 us -> 14.2 us  [shift_x(): lax.ppermute(value, 'chan', [(i, (i + 2 * step) % 8) for i in range(8)])]
  transfers between devices with their start and end apart: 21 -> 21, of which waited for: 7 -> 5; matrix products, arithmetic and copies ran while one was open for 0% -> 0% of each run, Pallas kernels for 21% -> 25%
where the time goes in v4:
time: 140 us; the launch traced here: 138 us
  Pallas kernels  46 us (33%)
  starting transfers between devices  38.2 us (27%)
  waiting for transfers between devices  33.3 us (24%)
  local copies, waits for them, and re-layouts  20.4 us (15%)
    pallas_call x14, Pallas kernels, call(): pl.pallas_call(body, grid=(1,), in_specs=[pl.BlockSpec(memory_space=pltpu...  24.2 us
    pallas_call x4, Pallas kernels, project(): pl.pallas_call(body, grid_spec=pltpu.PrefetchScalarGridSpec(num_scalar_pr...  21.7 us
    unnamed x70, local copies, waits for them, and re-layouts  20.3 us
    all_to_all x3, starting transfers between devices, exchange(): return lax.all_to_all(value, 'seq', split_axis=0, concat_axis=0, tiled=True)  20 us
    all_to_all x3, waiting for transfers between devices, exchange(): return lax.all_to_all(value, 'seq', split_axis=0, concat_axis=0, tiled=True)  16.6 us
    ppermute x12, waiting for transfers between devices, shift_x(): lax.ppermute(value, 'chan', [(i, (i + 2 * step) % 8) for i in range(8)])  14.8 us
    ppermute x12, starting transfers between devices, shift_x(): lax.ppermute(value, 'chan', [(i, (i + 2 * step) % 8) for i in range(8)])  14.2 us
    ppermute x6, starting transfers between devices, swap_z(): return lax.ppermute(value, 'chan', [(i, i ^ 1) for i in range(8)])  4.06 us
  transfers between devices with their start and end apart: 21, of which 5 were waited for; matrix products, arithmetic and copies ran while one was open for 0% of the time, Pallas kernels for 25%

profile of v4, /device:TPU:1, one launch (start us, length us, event | category | flops | bytes accessed | tf_op | source)
XLA Modules:
  0.0 138.2 jit_solution(11452176154199349685)
XLA Ops:
  0.1 7.1 %first_kernel.2 = (f32[4,512,128]{2,1,0:T(8,128)}, f32[4,512,128]{2,1,0:T(8,128)}, f32[4,512,128]{2,1,0:T(8,128)}, f32[4,512,128]{2,1,0:T(8,128)S(1)}) custom-call(s32[5]{0:T(128)S(1)} %stack.23.at, bf16[1024,1024]{1,0:T(8,128)(2,1)} %act.7, bf16[3,1024,1024]{2,1,0:T(8,128)(2,1)} %bitcast.11, bf16[3,1024,1024]{2,1,0:T(8,128)(2,1)} %bitcast.12), custom_call_target="tpu_custom_call" | custom-call | tf_op jit(solution)/shard_map/first_kernel/pallas_call | solution.py:120
  7.2 2.5 %collective-permute-start.1 = (f32[4,512,128]{2,1,0:T(8,128)}, f32[4,512,128]{2,1,0:T(8,128)S(1)}, u32[]{:S(2)}, u32[]{:S(2)}) collective-permute-start(f32[4,512,128]{2,1,0:T(8,128)} %get-tuple-element.51), channel_id=1, source_target_pairs={{0,1},{1,0},{2,3},{3,2},{4,5},{5,4},{6,7},{7,6},{8,9},{9,8},{10,11... | collective-permute-start | bytes 3145736 | tf_op jit(solution)/shard_map/ppermute | solution.py:29
  9.7 1.2 collective-permute-start.2
  10.9 1.5 %collective-permute-start.3 = (f32[4,512,128]{2,1,0:T(8,128)}, f32[4,512,128]{2,1,0:T(8,128)}, u32[]{:S(2)}, u32[]{:S(2)}) collective-permute-start(f32[4,512,128]{2,1,0:T(8,128)} %get-tuple-element.55), channel_id=1, source_target_pairs={{0,6},{1,7},{2,0},{3,1},{4,2},{5,3},{6,4},{7,5},{8,14},{9,15},{10,... | collective-permute-start | bytes 3145736 | tf_op jit(solution)/shard_map/ppermute | solution.py:25
  12.4 5.5 %second_kernel.2 = (f32[2,512,128]{2,1,0:T(8,128)S(1)}, f32[2,512,128]{2,1,0:T(8,128)S(1)}, f32[4,512,128]{2,1,0:T(8,128)S(1)}, f32[4,512,128]{2,1,0:T(8,128)S(1...) custom-call(s32[5]{0:T(128)S(1)} %stack.23.at, bf16[1024,1024]{1,0:T(8,128)(2,1)} %act.7, ...), custom_call_target="tpu_custom_call" | custom-call | tf_op jit(solution)/shard_map/second_kernel/pallas_call | solution.py:120
  17.8 1.0 copy-done
  19.7 1.0 copy-done.33
  21.4 0.8 copy-done.11
  22.2 9.0 %all-to-all-start = ((f32[16,8,8,128]{3,2,1,0:T(8,128)}), f32[16,8,8,128]{3,2,1,0:T(8,128)S(1)}, u32[]{:S(2)}, u32[]{:S(2)}) async-start(f32[16,8,8,128]{3,2,1,0:T(8,128)} %bitcast.10), calls=%async_computation | async-start | bytes 1048576 | tf_op jit(solution)/shard_map/all_to_all | solution.py:412
  31.3 12.1 %all-to-all-done.refs_7_.refs_0_ = f32[16,8,8,128]{3,2,1,0:T(8,128)S(1)} async-done(((f32[16,8,8,128]{3,2,1,0:T(8,128)}), f32[16,8,8,128]{3,2,1,0:T(8,128)S(1)}, u32[]{:S(2)}, u32[]{:S(2)}) %all-to-all-start) | async-done | bytes 524320 | tf_op jit(solution)/shard_map/all_to_all | solution.py:412
  43.4 1.4 %copy-done.10 = f32[2,512,128]{2,1,0:T(8,128)S(1)} copy-done((f32[2,512,128]{2,1,0:T(8,128)S(1)}, f32[2,512,128]{2,1,0:T(8,128)}, u32[]{:S(2)}) %copy-start.10) | copy-done | bytes 524312
  44.8 1.0 copy-done.25
  45.9 1.7 %first_sum_kernel.2 = (f32[3,512,128]{2,1,0:T(8,128)S(1)}, f32[3,512,128]{2,1,0:T(8,128)S(1)}) custom-call(f32[2,512,128]{2,1,0:T(8,128)S(1)} %copy-done.10, f32[4,512,128]{2,1,0:T(8,128)} %collective-permute-done.2.refs_1_.refs_4_, f32[2,512,128]{2,1,0:T(8,128)S(1)} %copy-done.25, f32[4,512,128]{2,1,0:T(8,128)} %collective-permute-done.3.refs_3_.refs_5_, ...), custom_call_target="tpu_custom_call" | custom-call | tf_op jit(solution)/shard_map/first_sum_kernel/pallas_call | solution.py:396
  47.6 2.6 %collective-permute-start.5 = (f32[3,512,128]{2,1,0:T(8,128)S(1)}, f32[3,512,128]{2,1,0:T(8,128)S(1)}, u32[]{:S(2)}, u32[]{:S(2)}) collective-permute-start(f32[3,512,128]{2,1,0:T(8,128)S(1)} %get-tuple-element.60), channel_id=1, source_target_pairs={{0,6},{1,7},{2,0},{3,1},{4,2},{5,3},{6,4},{7,5},{8,14},{9,15},{10,... | collective-permute-start | bytes 2359304 | tf_op jit(solution)/shard_map/ppermute | solution.py:25
  50.1 2.2 %taps_kernel.1.refs_6_.refs_1_ = f32[1024,256]{1,0:T(8,128)S(1)} custom-call(f32[16,8,8,128]{3,2,1,0:T(8,128)S(1)} %all-to-all-done.refs_7_.refs_0_, bf16[256,128]{1,0:T(8,128)(2,1)} %constant.72.clone.refs_1_.refs_2_, bf16[256,128]{1,0:T(8,128)(2,1)} %constant.73.clone.refs_2_.refs_3_, f32[128,128]{1,0:T(8,128)} %constant.74.clone.refs_3_.refs_4_, ...), custom_call_target="tpu_custom_call" | custom-call | tf_op jit(solution)/shard_map/taps_kernel/pallas_call | solution.py:396
  52.3 4.4 %first_kernel.3 = (f32[4,256,128]{2,1,0:T(8,128)S(1)}, f32[4,256,128]{2,1,0:T(8,128)S(1)}, f32[4,256,128]{2,1,0:T(8,128)S(1)}, f32[4,256,128]{2,1,0:T(8,128)S(1)}) custom-call(s32[5]{0:T(128)S(1)} %stack.23.at, bf16[1024,1024]{1,0:T(8,128)(2,1)} %act.7, bf16[3,1024,1024]{2,1,0:T(8,128)(2,1)} %bitcast.15, f32[3,512,128]{2,1,0:T(8,128)S(1)} %get-tuple-element.58.refs_6_.refs_1_), custom_call_target="tpu_custom_call" | custom-call | tf_op jit(solution)/shard_map/first_kernel/pallas_call | solution.py:120
  57.5 0.8 copy-done.27
  58.4 0.8 copy-done.28
  59.2 4.7 %second_kernel.3 = (f32[2,256,128]{2,1,0:T(8,128)S(1)}, f32[2,256,128]{2,1,0:T(8,128)S(1)}, f32[4,256,128]{2,1,0:T(8,128)S(1)}, f32[4,256,128]{2,1,0:T(8,128)S(1...) custom-call(s32[5]{0:T(128)S(1)} %stack.23.at, bf16[1024,1024]{1,0:T(8,128)(2,1)} %act.7, ...), custom_call_target="tpu_custom_call" | custom-call | tf_op jit(solution)/shard_map/second_kernel/pallas_call | solution.py:120
  63.9 0.8 copy-done.12
  66.8 0.8 copy-done.34
  67.6 1.8 %beside_two_kernel.2 = (f32[2,512,128]{2,1,0:T(8,128)S(1)}, f32[2,512,128]{2,1,0:T(8,128)S(1)}, f32[2,512,128]{2,1,0:T(8,128)S(1)}) custom-call(f32[4,512,128]{2,1,0:T(8,128)S(1)} %get-tuple-element.48.refs_2_.refs_4_.refs_0_, f32[4,512,128]{2,1,0:T(8,128)S(1)} %copy-done.4, f32[2,512,128]{2,1,0:T(8,128)S(1)} %copy-done.8, f32[2,512,128]{2,1,0:T(8,128)S(1)} %copy-done.23, ...), custom_call_target="tpu_custom_call" | custom-call | tf_op jit(solution)/shard_map/beside_two_kernel/pallas_call | solution.py:396
  70.3 2.9 %second_sum_kernel.2 = (f32[2,512,128]{2,1,0:T(8,128)}, f32[2,512,128]{2,1,0:T(8,128)}, f32[2,512,128]{2,1,0:T(8,128)}) custom-call(f32[2,512,128]{2,1,0:T(8,128)S(1)} %get-tuple-element.61.refs_0_, f32[4,512,128]{2,1,0:T(8,128)S(1)} %copy-done.1, f32[4,512,128]{2,1,0:T(8,128)} %collective-permute-done.refs_2_.refs_1_, ...), custom_call_target="tpu_custom_call" | custom-call | tf_op jit(solution)/shard_map/second_sum_kernel/pallas_call | solution.py:396
  73.1 2.7 %collective-permute-start.7 = (f32[2,512,128]{2,1,0:T(8,128)}, f32[2,512,128]{2,1,0:T(8,128)}, u32[]{:S(2)}, u32[]{:S(2)}) collective-permute-start(f32[2,512,128]{2,1,0:T(8,128)} %get-tuple-element.67), channel_id=1, source_target_pairs={{0,6},{1,7},{2,0},{3,1},{4,2},{5,3},{6,4},{7,5},{8,14},{9,15},{10,... | collective-permute-start | bytes 1572872 | tf_op jit(solution)/shard_map/ppermute | solution.py:25
  75.8 1.5 %collective-permute-start.10 = (f32[4,256,128]{2,1,0:T(8,128)}, f32[4,256,128]{2,1,0:T(8,128)}, u32[]{:S(2)}, u32[]{:S(2)}) collective-permute-start(f32[4,256,128]{2,1,0:T(8,128)} %get-tuple-element.75), channel_id=1, source_target_pairs={{0,1},{1,0},{2,3},{3,2},{4,5},{5,4},{6,7},{7,6},{8,9},{9,8},{10,11... | collective-permute-start | bytes 1572872 | tf_op jit(solution)/shard_map/ppermute | solution.py:29
  77.3 9.6 %collective-permute-done.7.refs_2_ = f32[2,512,128]{2,1,0:T(8,128)} collective-permute-done((f32[2,512,128]{2,1,0:T(8,128)}, f32[2,512,128]{2,1,0:T(8,128)}, u32[]{:S(2)}, u32[]{:S(2)}) %collective-permute-start.7) | collective-permute-done | bytes 524320 | tf_op jit(solution)/shard_map/ppermute | solution.py:25
  86.8 3.4 %collective-permute-start.12 = (f32[4,256,128]{2,1,0:T(8,128)}, f32[4,256,128]{2,1,0:T(8,128)}, u32[]{:S(2)}, u32[]{:S(2)}) collective-permute-start(f32[4,256,128]{2,1,0:T(8,128)} %get-tuple-element.79), channel_id=1, source_target_pairs={{0,6},{1,7},{2,0},{3,1},{4,2},{5,3},{6,4},{7,5},{8,14},{9,15},{10,... | collective-permute-start | bytes 1572872 | tf_op jit(solution)/shard_map/ppermute | solution.py:25
  90.3 1.1 copy-done.6
  91.4 1.0 copy-done.21
  92.4 1.3 beside_three_kernel.2
  93.8 2.5 %kv_kernel.1 = f32[128,8,128]{2,1,0:T(8,128)} custom-call(f32[2,512,128]{2,1,0:T(8,128)S(1)} %get-tuple-element.66.refs_0_, f32[2,512,128]{2,1,0:T(8,128)} %collective-permute-done.6.refs_1_, f32[2,512,128]{2,1,0:T(8,128)} %collective-permute-done.7.refs_2_, f32[2,512,128]{2,1,0:T(8,128)S(1)} %get-tuple-element.68.refs_3_, ...), custom_call_target="tpu_custom_call" | custom-call | tf_op jit(solution)/shard_map/kv_kernel/pallas_call | solution.py:396
  96.3 6.3 %all-to-all-start.1 = ((f32[16,8,8,128]{3,2,1,0:T(8,128)}), f32[16,8,8,128]{3,2,1,0:T(8,128)S(1)}, u32[]{:S(2)}, u32[]{:S(2)}) async-start(f32[16,8,8,128]{3,2,1,0:T(8,128)} %bitcast.7), calls=%async_computation.1 | async-start | bytes 1048576 | tf_op jit(solution)/shard_map/all_to_all | solution.py:412
  102.7 0.9 copy-done.15
  103.6 0.9 copy-done.18
  104.6 0.9 copy-done.32
  105.5 2.3 %first_sum_kernel.3 = (f32[3,256,128]{2,1,0:T(8,128)}, f32[3,256,128]{2,1,0:T(8,128)}) custom-call(f32[2,256,128]{2,1,0:T(8,128)S(1)} %copy-done.18, f32[4,256,128]{2,1,0:T(8,128)} %collective-permute-done.11.refs_1_.refs_4_, f32[2,256,128]{2,1,0:T(8,128)S(1)} %copy-done.32, f32[4,256,128]{2,1,0:T(8,128)} %collective-permute-done.12.refs_3_.refs_5_, ...), custom_call_target="tpu_custom_call" | custom-call | tf_op jit(solution)/shard_map/first_sum_kernel/pallas_call | solution.py:396
  107.8 1.1 collective-permute-start.14
  109.3 4.5 %all-to-all-done.1.refs_0_ = f32[16,8,8,128]{3,2,1,0:T(8,128)S(1)} async-done(((f32[16,8,8,128]{3,2,1,0:T(8,128)}), f32[16,8,8,128]{3,2,1,0:T(8,128)S(1)}, u32[]{:S(2)}, u32[]{:S(2)}) %all-to-all-start.1) | async-done | bytes 524320 | tf_op jit(solution)/shard_map/all_to_all | solution.py:412
  113.8 4.4 %conv_kernel.1 = f32[16,8,8,128]{3,2,1,0:T(8,128)} custom-call(f32[16,8,8,128]{3,2,1,0:T(8,128)S(1)} %all-to-all-done.1.refs_0_, f32[1024,256]{1,0:T(8,128)S(1)} %taps_kernel.1.refs_6_.refs_1_, bf16[256,128]{1,0:T(8,128)(2,1)} %constant.72.clone.refs_1_.refs_2_, bf16[256,128]{1,0:T(8,128)(2,1)} %constant.73.clone.refs_2_.refs_3_, ...), custom_call_target="tpu_custom_call" | custom-call | tf_op jit(solution)/shard_map/conv_kernel/pallas_call | solution.py:396
  118.2 4.7 %all-to-all-start.2 = ((f32[16,8,8,128]{3,2,1,0:T(8,128)}), f32[16,8,8,128]{3,2,1,0:T(8,128)S(1)}, u32[]{:S(2)}, u32[]{:S(2)}) async-start(f32[16,8,8,128]{3,2,1,0:T(8,128)} %conv_kernel.1), calls=%async_computation.2 | async-start | bytes 1048576 | tf_op jit(solution)/shard_map/all_to_all | solution.py:412
  122.9 0.9 copy-done.16
  123.8 0.9 copy-done.30
  124.8 1.4 %beside_two_kernel.3 = (f32[2,256,128]{2,1,0:T(8,128)S(1)}, f32[2,256,128]{2,1,0:T(8,128)S(1)}, f32[2,256,128]{2,1,0:T(8,128)S(1)}) custom-call(f32[4,256,128]{2,1,0:T(8,128)S(1)} %get-tuple-element.63.refs_1_.refs_4_.refs_0_, f32[4,256,128]{2,1,0:T(8,128)} %collective-permute-done.10.refs_5_.refs_1_, f32[2,256,128]{2,1,0:T(8,128)S(1)} %copy-done.16, ...), custom_call_target="tpu_custom_call" | custom-call | tf_op jit(solution)/shard_map/beside_two_kernel/pallas_call | solution.py:396
  126.3 1.1 second_sum_kernel.3
  128.9 1.0 beside_three_kernel.3
  129.9 5.2 %collective-permute-done.16.refs_2_ = f32[2,256,128]{2,1,0:T(8,128)S(1)} collective-permute-done((f32[2,256,128]{2,1,0:T(8,128)S(1)}, f32[2,256,128]{2,1,0:T(8,128)S(1)}, u32[]{:S(2)}, u32[]{:S(2)}) %collective-permute-start.16) | collective-permute-done | bytes 262176 | tf_op jit(solution)/shard_map/ppermute | solution.py:25
  135.1 1.9 %collective-permute-done.17.refs_4_ = f32[2,256,128]{2,1,0:T(8,128)S(1)} collective-permute-done((f32[2,256,128]{2,1,0:T(8,128)S(1)}, f32[2,256,128]{2,1,0:T(8,128)S(1)}, u32[]{:S(2)}, u32[]{:S(2)}) %collective-permute-start.17) | collective-permute-done | bytes 262176 | tf_op jit(solution)/shard_map/ppermute | solution.py:29
  137.1 1.1 gate_kernel.1
  (84 shorter events, 7.4 us)
Async XLA Ops:
  7.2 36.2 %collective-permute-start.1 = (f32[4,512,128]{2,1,0:T(8,128)}, f32[4,512,128]{2,1,0:T(8,128)S(1)}, u32[]{:S(2)}, u32[]{:S(2)}) collective-permute-start(f32[4,512,128]{2,1,0:T(8,128)} %get-tuple-element.51), channel_id=1, source_target_pairs={{0,1},{1,0},{2,3},{3,2},{4,5},{5,4},{6,7},{7,6},{8,9},{9,8},{10,11... | collective-permute-start | bytes 3145736 | tf_op jit(solution)/shard_map/ppermute | solution.py:29
  9.7 33.7 %collective-permute-start.2 = (f32[4,512,128]{2,1,0:T(8,128)}, f32[4,512,128]{2,1,0:T(8,128)}, u32[]{:S(2)}, u32[]{:S(2)}) collective-permute-start(f32[4,512,128]{2,1,0:T(8,128)} %get-tuple-element.54), channel_id=1, source_target_pairs={{0,2},{1,3},{2,4},{3,5},{4,6},{5,7},{6,0},{7,1},{8,10},{9,11},{10,... | collective-permute-start | bytes 3145736 | tf_op jit(solution)/shard_map/ppermute | solution.py:25
  10.9 32.5 %collective-permute-start.3 = (f32[4,512,128]{2,1,0:T(8,128)}, f32[4,512,128]{2,1,0:T(8,128)}, u32[]{:S(2)}, u32[]{:S(2)}) collective-permute-start(f32[4,512,128]{2,1,0:T(8,128)} %get-tuple-element.55), channel_id=1, source_target_pairs={{0,6},{1,7},{2,0},{3,1},{4,2},{5,3},{6,4},{7,5},{8,14},{9,15},{10,... | collective-permute-start | bytes 3145736 | tf_op jit(solution)/shard_map/ppermute | solution.py:25
  12.4 8.3 %copy-start.19 = (f32[1024,128]{1,0:T(8,128)S(1)}, f32[1024,128]{1,0:T(8,128)}, u32[]{:S(2)}) copy-start(f32[1024,128]{1,0:T(8,128)} %refs_0_.1) | copy-start | bytes 1572868
  17.8 1.0 copy-start
  19.7 1.0 copy-start.33
  20.7 1.6 %copy-start.9 = (f32[2,512,128]{2,1,0:T(8,128)}, f32[2,512,128]{2,1,0:T(8,128)S(1)}, u32[]{:S(2)}) copy-start(f32[2,512,128]{2,1,0:T(8,128)S(1)} %get-tuple-element.56.refs_1_.refs_0_) | copy-start | bytes 1572868
  20.7 26.9 %copy-start.7 = (f32[2,512,128]{2,1,0:T(8,128)}, f32[2,512,128]{2,1,0:T(8,128)S(1)}, u32[]{:S(2)}) copy-start(f32[2,512,128]{2,1,0:T(8,128)S(1)} %get-tuple-element.52.refs_6_.refs_2_) | copy-start | bytes 1572868
  21.4 0.8 copy-start.11
  22.2 21.1 %all-to-all-start = ((f32[16,8,8,128]{3,2,1,0:T(8,128)}), f32[16,8,8,128]{3,2,1,0:T(8,128)S(1)}, u32[]{:S(2)}, u32[]{:S(2)}) async-start(f32[16,8,8,128]{3,2,1,0:T(8,128)} %bitcast.10), calls=%async_computation | async-start | bytes 1048576 | tf_op jit(solution)/shard_map/all_to_all | solution.py:412
  31.3 39.0 %collective-permute-start = (f32[4,512,128]{2,1,0:T(8,128)}, f32[4,512,128]{2,1,0:T(8,128)}, u32[]{:S(2)}, u32[]{:S(2)}) collective-permute-start(f32[4,512,128]{2,1,0:T(8,128)} %copy-done.33), channel_id=1, source_target_pairs={{0,1},{1,0},{2,3},{3,2},{4,5},{5,4},{6,7},{7,6},{8,9},{9,8},{10,11... | collective-permute-start | bytes 3145736 | tf_op jit(solution)/shard_map/ppermute | solution.py:29
  43.4 6.7 %copy-start.3 = (f32[4,512,128]{2,1,0:T(8,128)}, f32[4,512,128]{2,1,0:T(8,128)S(1)}, u32[]{:S(2)}) copy-start(f32[4,512,128]{2,1,0:T(8,128)S(1)} %collective-permute-done.1.refs_5_.refs_1_) | copy-start | bytes 3145732
  43.4 1.4 %copy-start.10 = (f32[2,512,128]{2,1,0:T(8,128)S(1)}, f32[2,512,128]{2,1,0:T(8,128)}, u32[]{:S(2)}) copy-start(f32[2,512,128]{2,1,0:T(8,128)} %copy-done.9) | copy-start | bytes 1572868
  44.8 1.0 copy-start.25
  47.6 22.6 %collective-permute-start.5 = (f32[3,512,128]{2,1,0:T(8,128)S(1)}, f32[3,512,128]{2,1,0:T(8,128)S(1)}, u32[]{:S(2)}, u32[]{:S(2)}) collective-permute-start(f32[3,512,128]{2,1,0:T(8,128)S(1)} %get-tuple-element.60), channel_id=1, source_target_pairs={{0,6},{1,7},{2,0},{3,1},{4,2},{5,3},{6,4},{7,5},{8,14},{9,15},{10,... | collective-permute-start | bytes 2359304 | tf_op jit(solution)/shard_map/ppermute | solution.py:25
  50.1 20.1 %collective-permute-start.4 = (f32[3,512,128]{2,1,0:T(8,128)S(1)}, f32[3,512,128]{2,1,0:T(8,128)S(1)}, u32[]{:S(2)}, u32[]{:S(2)}) collective-permute-start(f32[3,512,128]{2,1,0:T(8,128)S(1)} %get-tuple-element.58.refs_6_.refs_1_), channel_id=1, source_target_pairs={{0,2},{1,3},{2,4},{3,5},{4,6},{5,7},{6,0},{7,1},{8,10},{9,11},{10,... | collective-permute-start | bytes 2359304 | tf_op jit(solution)/shard_map/ppermute | solution.py:25
  57.5 0.8 copy-start.27
  59.2 8.5 %copy-start.4 = (f32[4,512,128]{2,1,0:T(8,128)S(1)}, f32[4,512,128]{2,1,0:T(8,128)}, u32[]{:S(2)}) copy-start(f32[4,512,128]{2,1,0:T(8,128)} %copy-done.3) | copy-start | bytes 3145732
  59.2 8.5 %copy-start.8 = (f32[2,512,128]{2,1,0:T(8,128)S(1)}, f32[2,512,128]{2,1,0:T(8,128)}, u32[]{:S(2)}) copy-start(f32[2,512,128]{2,1,0:T(8,128)} %copy-done.7) | copy-start | bytes 1572868
  59.2 8.5 %copy-start.23 = (f32[2,512,128]{2,1,0:T(8,128)S(1)}, f32[2,512,128]{2,1,0:T(8,128)}, u32[]{:S(2)}) copy-start(f32[2,512,128]{2,1,0:T(8,128)} %copy-done.22) | copy-start | bytes 1572868
  59.2 11.1 %copy-start.1 = (f32[4,512,128]{2,1,0:T(8,128)S(1)}, f32[4,512,128]{2,1,0:T(8,128)}, u32[]{:S(2)}) copy-start(f32[4,512,128]{2,1,0:T(8,128)} %copy-done) | copy-start | bytes 3145732
  63.9 0.8 copy-start.12
  66.8 0.8 copy-start.34
  67.6 5.5 %copy-start.17 = (f32[2,256,128]{2,1,0:T(8,128)}, f32[2,256,128]{2,1,0:T(8,128)S(1)}, u32[]{:S(2)}) copy-start(f32[2,256,128]{2,1,0:T(8,128)S(1)} %get-tuple-element.64.refs_7_.refs_0_) | copy-start | bytes 786436
  70.2 20.0 %copy-start.2 = (f32[4,512,128]{2,1,0:T(8,128)S(1)}, f32[4,512,128]{2,1,0:T(8,128)}, u32[]{:S(2)}) copy-start(f32[4,512,128]{2,1,0:T(8,128)} %copy-done) | copy-start | bytes 3145732
  70.2 2.9 %copy-start.5 = (f32[3,512,128]{2,1,0:T(8,128)}, f32[3,512,128]{2,1,0:T(8,128)S(1)}, u32[]{:S(2)}) copy-start(f32[3,512,128]{2,1,0:T(8,128)S(1)} %collective-permute-done.4.refs_4_.refs_3_) | copy-start | bytes 2359300
  73.1 13.7 %collective-permute-start.7 = (f32[2,512,128]{2,1,0:T(8,128)}, f32[2,512,128]{2,1,0:T(8,128)}, u32[]{:S(2)}, u32[]{:S(2)}) collective-permute-start(f32[2,512,128]{2,1,0:T(8,128)} %get-tuple-element.67), channel_id=1, source_target_pairs={{0,6},{1,7},{2,0},{3,1},{4,2},{5,3},{6,4},{7,5},{8,14},{9,15},{10,... | collective-permute-start | bytes 1572872 | tf_op jit(solution)/shard_map/ppermute | solution.py:25
  75.8 18.0 %collective-permute-start.8 = (f32[2,512,128]{2,1,0:T(8,128)}, f32[2,512,128]{2,1,0:T(8,128)}, u32[]{:S(2)}, u32[]{:S(2)}) collective-permute-start(f32[2,512,128]{2,1,0:T(8,128)} %get-tuple-element.69), channel_id=1, source_target_pairs={{0,1},{1,0},{2,3},{3,2},{4,5},{5,4},{6,7},{7,6},{8,9},{9,8},{10,11... | collective-permute-start | bytes 1572872 | tf_op jit(solution)/shard_map/ppermute | solution.py:29
  75.8 18.0 %collective-permute-start.6 = (f32[2,512,128]{2,1,0:T(8,128)}, f32[2,512,128]{2,1,0:T(8,128)}, u32[]{:S(2)}, u32[]{:S(2)}) collective-permute-start(f32[2,512,128]{2,1,0:T(8,128)} %get-tuple-element.65.refs_5_.refs_3_), channel_id=1, source_target_pairs={{0,2},{1,3},{2,4},{3,5},{4,6},{5,7},{6,0},{7,1},{8,10},{9,11},{10,... | collective-permute-start | bytes 1572872 | tf_op jit(solution)/shard_map/ppermute | solution.py:25
  75.8 26.8 %collective-permute-start.10 = (f32[4,256,128]{2,1,0:T(8,128)}, f32[4,256,128]{2,1,0:T(8,128)}, u32[]{:S(2)}, u32[]{:S(2)}) collective-permute-start(f32[4,256,128]{2,1,0:T(8,128)} %get-tuple-element.75), channel_id=1, source_target_pairs={{0,1},{1,0},{2,3},{3,2},{4,5},{5,4},{6,7},{7,6},{8,9},{9,8},{10,11... | collective-permute-start | bytes 1572872 | tf_op jit(solution)/shard_map/ppermute | solution.py:29
  77.3 25.4 %collective-permute-start.11 = (f32[4,256,128]{2,1,0:T(8,128)}, f32[4,256,128]{2,1,0:T(8,128)}, u32[]{:S(2)}, u32[]{:S(2)}) collective-permute-start(f32[4,256,128]{2,1,0:T(8,128)} %get-tuple-element.78), channel_id=1, source_target_pairs={{0,2},{1,3},{2,4},{3,5},{4,6},{5,7},{6,0},{7,1},{8,10},{9,11},{10,... | collective-permute-start | bytes 1572872 | tf_op jit(solution)/shard_map/ppermute | solution.py:25
  86.8 15.8 %collective-permute-start.12 = (f32[4,256,128]{2,1,0:T(8,128)}, f32[4,256,128]{2,1,0:T(8,128)}, u32[]{:S(2)}, u32[]{:S(2)}) collective-permute-start(f32[4,256,128]{2,1,0:T(8,128)} %get-tuple-element.79), channel_id=1, source_target_pairs={{0,6},{1,7},{2,0},{3,1},{4,2},{5,3},{6,4},{7,5},{8,14},{9,15},{10,... | collective-permute-start | bytes 1572872 | tf_op jit(solution)/shard_map/ppermute | solution.py:25
  90.3 1.1 copy-start.6
  91.4 1.0 copy-start.21
  96.3 29.9 %copy-start.13 = (f32[4,256,128]{2,1,0:T(8,128)S(1)}, f32[4,256,128]{2,1,0:T(8,128)}, u32[]{:S(2)}) copy-start(f32[4,256,128]{2,1,0:T(8,128)} %copy-done.12) | copy-start | bytes 1572868
  96.3 17.5 %all-to-all-start.1 = ((f32[16,8,8,128]{3,2,1,0:T(8,128)}), f32[16,8,8,128]{3,2,1,0:T(8,128)S(1)}, u32[]{:S(2)}, u32[]{:S(2)}) async-start(f32[16,8,8,128]{3,2,1,0:T(8,128)} %bitcast.7), calls=%async_computation.1 | async-start | bytes 1048576 | tf_op jit(solution)/shard_map/all_to_all | solution.py:412
  102.6 23.6 %collective-permute-start.9 = (f32[4,256,128]{2,1,0:T(8,128)}, f32[4,256,128]{2,1,0:T(8,128)S(1)}, u32[]{:S(2)}, u32[]{:S(2)}) collective-permute-start(f32[4,256,128]{2,1,0:T(8,128)} %copy-done.34), channel_id=1, source_target_pairs={{0,1},{1,0},{2,3},{3,2},{4,5},{5,4},{6,7},{7,6},{8,9},{9,8},{10,11... | collective-permute-start | bytes 1572872 | tf_op jit(solution)/shard_map/ppermute | solution.py:29
  102.7 1.0 copy-start.15
  103.6 0.9 copy-start.18
  104.6 0.9 copy-start.32
  107.8 18.4 %collective-permute-start.14 = (f32[3,256,128]{2,1,0:T(8,128)}, f32[3,256,128]{2,1,0:T(8,128)S(1)}, u32[]{:S(2)}, u32[]{:S(2)}) collective-permute-start(f32[3,256,128]{2,1,0:T(8,128)} %get-tuple-element.83), channel_id=1, source_target_pairs={{0,6},{1,7},{2,0},{3,1},{4,2},{5,3},{6,4},{7,5},{8,14},{9,15},{10,... | collective-permute-start | bytes 1179656 | tf_op jit(solution)/shard_map/ppermute | solution.py:25
  108.9 17.3 %collective-permute-start.13 = (f32[3,256,128]{2,1,0:T(8,128)}, f32[3,256,128]{2,1,0:T(8,128)}, u32[]{:S(2)}, u32[]{:S(2)}) collective-permute-start(f32[3,256,128]{2,1,0:T(8,128)} %get-tuple-element.81.refs_6_), channel_id=1, source_target_pairs={{0,2},{1,3},{2,4},{3,5},{4,6},{5,7},{6,0},{7,1},{8,10},{9,11},{10,... | collective-permute-start | bytes 1179656 | tf_op jit(solution)/shard_map/ppermute | solution.py:25
  118.2 18.9 %all-to-all-start.2 = ((f32[16,8,8,128]{3,2,1,0:T(8,128)}), f32[16,8,8,128]{3,2,1,0:T(8,128)S(1)}, u32[]{:S(2)}, u32[]{:S(2)}) async-start(f32[16,8,8,128]{3,2,1,0:T(8,128)} %conv_kernel.1), calls=%async_computation.2 | async-start | bytes 1048576 | tf_op jit(solution)/shard_map/all_to_all | solution.py:412
  122.9 0.9 copy-start.16
  123.8 0.9 copy-start.30
  127.3 7.8 %collective-permute-start.16 = (f32[2,256,128]{2,1,0:T(8,128)S(1)}, f32[2,256,128]{2,1,0:T(8,128)S(1)}, u32[]{:S(2)}, u32[]{:S(2)}) collective-permute-start(f32[2,256,128]{2,1,0:T(8,128)S(1)} %get-tuple-element.88), channel_id=1, source_target_pairs={{0,6},{1,7},{2,0},{3,1},{4,2},{5,3},{6,4},{7,5},{8,14},{9,15},{10,... | collective-permute-start | bytes 786440 | tf_op jit(solution)/shard_map/ppermute | solution.py:25
  128.0 9.0 %collective-permute-start.17 = (f32[2,256,128]{2,1,0:T(8,128)S(1)}, f32[2,256,128]{2,1,0:T(8,128)S(1)}, u32[]{:S(2)}, u32[]{:S(2)}) collective-permute-start(f32[2,256,128]{2,1,0:T(8,128)S(1)} %get-tuple-element.90), channel_id=1, source_target_pairs={{0,1},{1,0},{2,3},{3,2},{4,5},{5,4},{6,7},{7,6},{8,9},{9,8},{10,11... | collective-permute-start | bytes 786440 | tf_op jit(solution)/shard_map/ppermute | solution.py:29
  128.1 8.9 %collective-permute-start.15 = (f32[2,256,128]{2,1,0:T(8,128)S(1)}, f32[2,256,128]{2,1,0:T(8,128)S(1)}, u32[]{:S(2)}, u32[]{:S(2)}) collective-permute-start(f32[2,256,128]{2,1,0:T(8,128)S(1)} %get-tuple-element.86.refs_5_), channel_id=1, source_target_pairs={{0,2},{1,3},{2,4},{3,5},{4,6},{5,7},{6,0},{7,1},{8,10},{9,11},{10,... | collective-permute-start | bytes 786440 | tf_op jit(solution)/shard_map/ppermute | solution.py:25
  (8 other events, 6.1 us)

commit v5 on v1

--- a/solution.py
+++ b/solution.py
@@ -11,8 +11,15 @@
 
 BLOCK = 128
 X_SIZE = 4
-Z_FIRST_ROWS = 448
-PARAMS = pltpu.CompilerParams(vmem_limit_bytes=40 * 1024 * 1024)
+CHUNK = 256
+
+
+def params(mebibytes):
+    return pltpu.CompilerParams(vmem_limit_bytes=mebibytes * 1024 * 1024)
+
+
+def in_hbm(value):
+    return pltpu.with_memory_space_constraint(value, pltpu.HBM)
 
 
 def shift_x(value, step):
@@ -23,59 +30,316 @@
     return lax.ppermute(value, "chan", [(i, i ^ 1) for i in range(8)])
 
 
-def project(activations, weight, start, width):
-    columns = lax.dynamic_slice_in_dim(weight, start, width, axis=2)
-    return jnp.einsum("td,djc->jtc", activations, columns, preferred_element_type=jnp.float32)
-
-
-def as_halves(value):
-    return value.reshape(2, -1, value.shape[-1])
-
-
-def z_first(activations, weight):
-    chan = lax.axis_index("chan")
-    x_at, z_at = chan // 2, chan % 2
-
-    def part(dx, dz):
-        owner = (x_at + dx) % X_SIZE * 2 + (z_at + dz) % 2
-        return as_halves(project(activations, weight, owner * BLOCK, BLOCK))
-
-    far = part(2, 0) + swap_z(part(2, 1))
-    from_left = shift_x(far[0], 1)
-    from_right = shift_x(far[1], -1)
-    right, got_right = part(1, 0), swap_z(part(1, 1))
-    left, got_left = part(3, 0), swap_z(part(3, 1))
-    right = jnp.stack([right[0] + got_right[0] + from_left, right[1] + got_right[1]])
-    left = jnp.stack([left[0] + got_left[0], left[1] + got_left[1] + from_right])
-    return part(0, 0), swap_z(part(0, 1)), shift_x(right, 1), shift_x(left, -1)
-
-
-def x_first(activations, weight):
-    chan = lax.axis_index("chan")
-    x_at, z_at = chan // 2, chan % 2
-
-    def part(dx):
-        owner = (x_at + dx) % X_SIZE
-        return as_halves(project(activations, weight, owner * 2 * BLOCK, 2 * BLOCK))
-
-    def pick(value, dz):
-        return lax.dynamic_slice_in_dim(value, (z_at + dz) % 2 * BLOCK, BLOCK, axis=-1)
-
-    far = part(2)
-    from_left = shift_x(far[0], 1)
-    from_right = shift_x(far[1], -1)
-    right, left, own = part(1), part(3), part(0)
-
-    def second(dz):
-        to_right, to_left = pick(right, dz), pick(left, dz)
-        to_right = jnp.stack([to_right[0] + pick(from_left, dz), to_right[1]])
-        to_left = jnp.stack([to_left[0], to_left[1] + pick(from_right, dz)])
-        return shift_x(to_right, 1), shift_x(to_left, -1)
-
-    a, b = second(1)
-    other = swap_z(pick(own, 1) + a + b)
-    c, d = second(0)
-    return pick(own, 0), c, d, other
+def parts_of(rows, weight, z_at):
+    product = jnp.dot(rows, weight, preferred_element_type=jnp.float32)
+    low, high = product[:, :BLOCK], product[:, BLOCK:]
+    return jnp.where(z_at == 0, high, low), jnp.where(z_at == 0, low, high)
+
+
+class Halves:
+    def __init__(self, tokens, columns):
+        self.columns = columns
+        parts = 2 // len(columns)
+        self.rows = tokens // 2 // parts
+        self.z_start = [h % parts * self.rows for h in range(2)]
+        self.x_start = [tokens // 2 + start for start in self.z_start]
+
+    def shape(self, count):
+        return (count, self.rows, BLOCK)
+
+    def fill(self, place, act, weight, half, x_outs, z_outs):
+        for begin, outs in ((self.x_start[half], x_outs), (self.z_start[half], z_outs)):
+            for start in range(0, self.rows, CHUNK):
+                rows = act[begin + start : begin + start + CHUNK]
+                for (ref, piece), part in zip(outs, parts_of(rows, weight[0], place[4])):
+                    ref[piece, start : start + CHUNK] = part
+
+
+def first_kernel(halves, place, act, weight, outs):
+    send_r, send_l, z_other, z_mine = outs
+    for half, send in enumerate((send_r, send_l)):
+        pl.when(pl.program_id(0) == half)(
+            functools.partial(
+                halves.fill,
+                place,
+                act,
+                weight,
+                half,
+                ((send, 0), (send, 1)),
+                ((z_other, half), (z_mine, half)),
+            )
+        )
+
+
+def second_kernel(halves, place, act, weight, outs):
+    dep_r, dep_l, z_send, z_late, z_mine, x_other, x_mine = outs
+    x_outs = (
+        ((dep_r, 2), (dep_r, 3)),
+        ((dep_r, 0), (dep_r, 1)),
+        ((dep_l, 0), (dep_l, 1)),
+        ((dep_l, 2), (dep_l, 3)),
+        ((x_other, 0), (x_mine, 0)),
+        ((x_other, 0), (x_mine, 0)),
+    )
+    for i, outs in enumerate(x_outs):
+        z_other = (z_send, i) if i < 5 else (z_late, 0)
+        pl.when(pl.program_id(0) == i)(
+            functools.partial(
+                halves.fill, place, act, weight, i % 2, outs, (z_other, (z_mine, 0))
+            )
+        )
+
+
+def project(kernel, halves, place, activations, weight, owner, steps, outs, after=()):
+    first, last = halves.columns[0], halves.columns[-1]
+
+    def weight_block(i, at):
+        return (first + (last - first) * (i % 2), 0, at[owner + i // 2])
+
+    def body(at, act, weight_ref, *refs):
+        kernel(halves, at, act, weight_ref, refs[len(after) :])
+
+    specs, results = [], []
+    for count, where in outs:
+        if where == "vmem":
+            specs.append(pl.BlockSpec(memory_space=pltpu.VMEM))
+            results.append(jax.ShapeDtypeStruct(halves.shape(count), jnp.float32))
+            continue
+        results.append(pltpu.HBM(halves.shape(count), jnp.float32))
+        if where == "hbm":
+            specs.append(pl.BlockSpec(halves.shape(count), lambda i, at: (0, 0, 0)))
+        else:
+            specs.append(
+                pl.BlockSpec(
+                    halves.shape(1),
+                    lambda i, at, start=where, end=count - 1: (
+                        jnp.clip(i - start, 0, end),
+                        0,
+                        0,
+                    ),
+                )
+            )
+    return pl.pallas_call(
+        body,
+        grid_spec=pltpu.PrefetchScalarGridSpec(
+            num_scalar_prefetch=1,
+            grid=(steps,),
+            in_specs=[
+                pl.BlockSpec(activations.shape, lambda i, at: (0, 0)),
+                pl.BlockSpec((1, weight.shape[1], 2 * BLOCK), weight_block),
+            ]
+            + [pl.BlockSpec(memory_space=pl.ANY)] * len(after),
+            out_specs=specs,
+        ),
+        out_shape=results,
+        compiler_params=params(24),
+        name=kernel.__name__,
+    )(place, activations, weight, *after)
+
+
+def sum_call(kernel, halves, counts, near, far, after=()):
+    tile = min(BLOCK, halves.rows)
+
+    def body(*refs):
+        rows = pl.ds(pl.multiple_of(pl.program_id(0) * tile, tile), tile)
+        ins = [ref.at[:, rows] for ref in refs[: len(near)]]
+        ins += refs[len(near) : len(near) + len(far)]
+        kernel(*ins, *[ref.at[:, rows] for ref in refs[len(near) + len(far) + len(after) :]])
+
+    return pl.pallas_call(
+        body,
+        grid=(halves.rows // tile,),
+        in_specs=[pl.BlockSpec(memory_space=pltpu.VMEM)] * len(near)
+        + [pl.BlockSpec((value.shape[0], tile, BLOCK), lambda i: (0, i, 0)) for value in far]
+        + [pl.BlockSpec(memory_space=pl.ANY)] * len(after),
+        out_specs=[pl.BlockSpec(memory_space=pltpu.VMEM)] * len(counts),
+        out_shape=[jax.ShapeDtypeStruct(halves.shape(count), jnp.float32) for count in counts],
+        compiler_params=params(16),
+        name=kernel.__name__,
+    )(*near, *[in_hbm(value) for value in far], *after)
+
+
+def kv_first_sum_kernel(dep_r, dep_l, got_r, got_l, z_mine, z_got, out_r, out_l):
+    for half, (dep, got, out) in enumerate(((dep_r, got_r, out_r), (dep_l, got_l, out_l))):
+        out[0] = dep[0]
+        out[1] = dep[1]
+        out[2] = dep[2] + got[0]
+        out[3] = dep[3] + got[1]
+        out[4] = z_mine[half] + z_got[half]
+
+
+def kv_second_sum_kernel(dep_r, dep_l, z_got, z_mine, x_other, z_late, out_r, out_l, out_xz):
+    out_r[0] = z_mine[0] + z_got[0] + dep_r[4]
+    out_r[1] = z_mine[1] + z_got[1]
+    out_l[0] = z_mine[2] + z_got[2]
+    out_l[1] = z_mine[3] + z_got[3] + dep_l[4]
+    out_xz[0] = x_other[0] + (dep_r[2] + dep_l[0])
+    out_xz[1] = x_other[1] + (dep_r[0] + dep_l[2])
+    out_xz[2] = z_late[0]
+
+
+def kv_beside_kernel(dep_r, dep_l, z_got, z_mine, x_mine, out_z, out_x):
+    out_z[0] = z_mine[4] + z_got[4]
+    out_z[1] = z_mine[5]
+    out_x[0] = x_mine[0] + (dep_r[3] + dep_l[1])
+    out_x[1] = x_mine[1] + (dep_r[1] + dep_l[3])
+
+
+def release(values, after):
+    def body(*refs):
+        pass
+
+    count = len(values)
+    return pl.pallas_call(
+        body,
+        in_specs=[pl.BlockSpec(memory_space=pl.ANY)] * (count + 1),
+        out_specs=[pl.BlockSpec(memory_space=pl.ANY)] * count,
+        out_shape=[pltpu.HBM(value.shape, value.dtype) for value in values],
+        input_output_aliases={i: i for i in range(count)},
+        name="release",
+    )(*values, after)
+
+
+def query_project_kernel(halves, place, act, weight, outs):
+    send_r, send_l, keep_r, keep_l, z_send, z_late, z_mine, x_other, x_mine = outs
+    x_outs = (
+        ((send_r, 0), (send_r, 1)),
+        ((send_l, 0), (send_l, 1)),
+        ((keep_r, 0), (keep_r, 1)),
+        ((send_r, 2), (send_r, 3)),
+        ((send_l, 2), (send_l, 3)),
+        ((keep_l, 0), (keep_l, 1)),
+        ((x_other, 0), (x_mine, 0)),
+        ((x_other, 0), (x_mine, 0)),
+    )
+    for i, outs in enumerate(x_outs):
+        z_other = z_send if i < 6 else z_late
+        pl.when(pl.program_id(0) == i)(
+            functools.partial(
+                halves.fill, place, act, weight, i % 2, outs, ((z_other, 0), (z_mine, 0))
+            )
+        )
+
+
+def query_first_sum_kernel(got_r, got_l, z_got, keep_r, keep_l, z_mine, out_r, out_l):
+    for half, (keep, got, out) in enumerate(((keep_r, got_r, out_r), (keep_l, got_l, out_l))):
+        out[0] = keep[0] + got[0]
+        out[1] = keep[1] + got[1]
+        out[2] = z_mine[half] + z_got[half]
+
+
+def query_second_sum_kernel(
+    dep_r, dep_l, got_r, got_l, z_got, z_mine, x_other, out_r, out_l, out_x
+):
+    out_r[0] = z_mine[2] + z_got[2] + dep_r[2]
+    out_r[1] = z_mine[3] + z_got[3]
+    out_l[0] = z_mine[4] + z_got[4]
+    out_l[1] = z_mine[5] + z_got[5] + dep_l[2]
+    out_x[0] = x_other[0] + (dep_r[0] + got_l[2])
+    out_x[1] = x_other[1] + (got_r[2] + dep_l[0])
+
+
+def query_beside_kernel(dep_r, dep_l, got_r, got_l, z_got, z_mine, x_mine, out_z, out_x):
+    out_z[0] = z_mine[6] + z_got[0]
+    out_z[1] = z_mine[7] + z_got[1]
+    out_x[0] = x_mine[0] + (dep_r[1] + got_l[3])
+    out_x[1] = x_mine[1] + (got_r[3] + dep_l[1])
+
+
+def reduce_kv(halves, place, activations, weight, beside):
+    send_r, send_l, z_send, z_mine = project(
+        first_kernel, halves, place, activations, weight, 0, 2, [(2, "vmem")] * 4
+    )
+    got_r, got_l, z_got = shift_x(send_r, 1), shift_x(send_l, -1), swap_z(z_send)
+    dep_r, dep_l, z_send, z_late, z_six, x_other, x_mine = project(
+        second_kernel,
+        halves,
+        place,
+        activations,
+        weight,
+        1,
+        6,
+        [(5, "vmem")] * 3 + [(1, 0), (6, 0), (2, 4), (2, 4)],
+        after=(z_mine,),
+    )
+    dep_r, dep_l = sum_call(
+        kv_first_sum_kernel,
+        halves,
+        [5, 5],
+        [dep_r, dep_l, got_r, got_l, z_mine, z_got],
+        [],
+    )
+    ready = beside(dep_r)
+    dep_r, dep_l, z_got = shift_x(dep_r, 1), shift_x(dep_l, -1), swap_z(z_send)
+    last_r, last_l, last_xz = sum_call(
+        kv_second_sum_kernel,
+        halves,
+        [2, 2, 3],
+        [dep_r, dep_l, z_got],
+        [z_six, x_other, z_late],
+        after=ready,
+    )
+    last = last_r
+    z_part, x_part = sum_call(
+        kv_beside_kernel, halves, [2, 2], [dep_r, dep_l, z_got], [z_six, x_mine], after=(last,)
+    )
+    last_r, last_l, last_xz = shift_x(last_r, 1), shift_x(last_l, -1), swap_z(last_xz)
+    return (z_part, last_r, last_l, x_part, last_xz), last
+
+
+def project_query(halves, place, activations, weight, after):
+    return project(
+        query_project_kernel,
+        halves,
+        place,
+        activations,
+        weight,
+        0,
+        8,
+        [(4, "hbm")] * 2 + [(2, "hbm")] * 2 + [(6, 0), (2, 6), (8, 0), (2, 6), (2, 6)],
+        after=after,
+    )
+
+
+def reduce_query(halves, projected, x_after, z_after):
+    send_r, send_l, keep_r, keep_l, z_send, z_late, z_mine, x_other, x_mine = projected
+    send_r, send_l = release((send_r, send_l), x_after)
+    got_r, got_l = shift_x(send_r, 1), shift_x(send_l, -1)
+    (z_send,) = release((z_send,), z_after)
+    z_got = swap_z(z_send)
+    dep_r, dep_l = sum_call(
+        query_first_sum_kernel,
+        halves,
+        [3, 3],
+        [got_r, got_l, z_got],
+        [keep_r, keep_l, z_mine],
+    )
+    (z_late,) = release((z_late,), dep_r)
+    dep_r, dep_l, late_got = shift_x(dep_r, 1), shift_x(dep_l, -1), swap_z(z_late)
+    last_r, last_l, x_sum = sum_call(
+        query_second_sum_kernel,
+        halves,
+        [2, 2, 2],
+        [dep_r, dep_l, got_r, got_l, z_got],
+        [z_mine, x_other],
+    )
+    z_part, x_part = sum_call(
+        query_beside_kernel,
+        halves,
+        [2, 2],
+        [dep_r, dep_l, got_r, got_l, late_got],
+        [z_mine, x_mine],
+        after=(last_r,),
+    )
+    last_r, last_l, x_sum = shift_x(last_r, 1), shift_x(last_l, -1), swap_z(x_sum)
+    return z_part, last_r, last_l, x_part, x_sum
+
+
+def summed(z_part, last_r, last_l, x_part, last_x):
+    z_total = [z_part[h] + (last_r[h] + last_l[h]) for h in range(2)]
+    if last_x.shape[0] == 3:
+        z_total[1] = z_total[1] + last_x[2]
+    return z_total + [x_part[h] + last_x[h] for h in range(2)]
 
 
 def split_bf16(table):
@@ -174,32 +438,50 @@
     turn_blocks(taps_ref, out_ref)
 
 
-def kv_kernel(z0, z1, z2, z3, x0, x1, x2, x3, out_ref, kv_ref):
-    rows = z0.shape[1]
-    total = (z0[...] + z1[...]) + (z2[...] + z3[...])
-    kv_ref[:rows] = total[0] * total[1]
-    total = (x0[...] + x1[...]) + (x2[...] + x3[...])
-    kv_ref[rows:] = total[0] * total[1]
+def kv_kernel(*refs):
+    parts, out_ref, kv_ref = refs[:-2], refs[-2], refs[-1]
+    z_key, z_value, x_key, x_value = summed(*parts)
+    rows = z_key.shape[0]
+    kv_ref[:rows] = z_key * z_value
+    kv_ref[rows:] = x_key * x_value
     turn_blocks(kv_ref, out_ref)
 
 
-def gate_kernel(conv_ref, z0, z1, z2, z3, x0, x1, x2, x3, out_ref):
+def query_kernel(*refs):
+    parts, out_ref = refs[:-1], refs[-1]
+    for i, query in enumerate(summed(*parts)):
+        rows = query.shape[0]
+        out_ref[i * rows : (i + 1) * rows] = query
+
+
+def gate_kernel(conv_ref, query_ref, out_ref):
     for b in range(conv_ref.shape[1]):
-        out_ref[b * BLOCK : (b + 1) * BLOCK, :] = conv_ref[:, b, :].T
-    rows = 2 * z0.shape[1]
-    total = (z0[...] + z1[...]) + (z2[...] + z3[...])
-    out_ref[:rows] = out_ref[:rows] * total.reshape(rows, BLOCK)
-    total = (x0[...] + x1[...]) + (x2[...] + x3[...])
-    out_ref[rows:] = out_ref[rows:] * total.reshape(-1, BLOCK)
-
-
-def call(kernel, out_shape, *operands, scratch=()):
+        rows = slice(b * BLOCK, (b + 1) * BLOCK)
+        out_ref[rows] = conv_ref[:, b, :].T * query_ref[rows]
+
+
+def call(kernel, out_shape, *operands, after=(), scratch=(), tables=(), to_hbm=False):
+    def body(*refs):
+        count = len(operands) + len(tables)
+        kernel(*refs[:count], *refs[count + len(after) :])
+
+    def whole(shape):
+        return pl.BlockSpec(shape, lambda i: (0,) * len(shape))
+
     return pl.pallas_call(
-        kernel,
-        out_shape=jax.ShapeDtypeStruct(out_shape, jnp.float32),
+        body,
+        grid=(1,),
+        in_specs=[pl.BlockSpec(memory_space=pltpu.VMEM)] * len(operands)
+        + [whole(table.shape) for table in tables]
+        + [pl.BlockSpec(memory_space=pl.ANY)] * len(after),
+        out_specs=whole(out_shape) if to_hbm else pl.BlockSpec(memory_space=pltpu.VMEM),
+        out_shape=pltpu.HBM(out_shape, jnp.float32)
+        if to_hbm
+        else jax.ShapeDtypeStruct(out_shape, jnp.float32),
         scratch_shapes=scratch,
-        compiler_params=PARAMS,
-    )(*operands)
+        compiler_params=params(24),
+        name=kernel.__name__,
+    )(*operands, *[in_hbm(jnp.asarray(table)) for table in tables], *after)
 
 
 def exchange(value):
@@ -216,26 +498,48 @@
     moved_shape = (seqs, owned, blocks, BLOCK)
     first, turn, second, back, inverse = tables(length)
 
-    low, high = activations[:Z_FIRST_ROWS], activations[Z_FIRST_ROWS:]
-    kv_weight, q_weight = proj_weight[:, 1:], proj_weight[:, :1]
-    kv_parts = z_first(low, kv_weight) + x_first(high, kv_weight)
-    q_parts = z_first(low, q_weight) + x_first(high, q_weight)
-
-    taps = call(taps_turn_kernel, turned_shape, filter_taps)
-    taps = exchange(taps.reshape(moved_shape))
-    spectrum = call(
-        taps_kernel, (owned * length // BLOCK, 2 * BLOCK), taps, *first, *turn, *second
-    )
-
+    chan = lax.axis_index("chan")
+    x_at, z_at = chan // 2, chan % 2
+    owners = [(x_at + dx) % X_SIZE for dx in (2, 1, 3, 0)]
+    place = jnp.stack(owners + [z_at]).astype(jnp.int32)
+    weight = in_hbm(jnp.transpose(proj_weight, (1, 0, 2)))
+    activations = in_hbm(activations)
+
+    hold = {}
+    kv_halves, q_halves = Halves(tokens, (1, 2)), Halves(tokens, (0,))
+
+    def prepare(ready):
+        taps = call(taps_turn_kernel, turned_shape, filter_taps, after=(ready,), to_hbm=True)
+        hold["spectrum"] = call(
+            taps_kernel,
+            (owned * length // BLOCK, 2 * BLOCK),
+            exchange(taps.reshape(moved_shape)),
+            tables=first + turn + second,
+        )
+        hold["query"] = project_query(q_halves, place, activations, weight, (ready,))
+        return hold["spectrum"], hold["query"][0]
+
+    kv_parts, kv_last = reduce_kv(kv_halves, place, activations, weight, prepare)
     kv = call(
-        kv_kernel, turned_shape, *kv_parts, scratch=[pltpu.VMEM((tokens, channels), jnp.float32)]
-    )
+        kv_kernel,
+        turned_shape,
+        *kv_parts,
+        scratch=[pltpu.VMEM((tokens, channels), jnp.float32)],
+        to_hbm=True,
+    )
+    q_parts = reduce_query(q_halves, hold["query"], kv_last, kv_last)
     moved = exchange(kv.reshape(moved_shape))
     convolved = call(
-        conv_kernel, moved_shape, moved, spectrum, *first, *turn, *second, *back, *inverse
-    )
+        conv_kernel,
+        moved_shape,
+        moved,
+        hold["spectrum"],
+        tables=first + turn + second + back + inverse,
+        to_hbm=True,
+    )
+    query = call(query_kernel, (tokens, channels), *q_parts)
     home = exchange(convolved).reshape(turned_shape)
-    return call(gate_kernel, (tokens, channels), home, *q_parts)
+    return call(gate_kernel, (tokens, channels), home, query)
 
 
 def solution(mesh):

time: 217 us -> 141 us (0.65)
  matrix products: 58.1 us -> 0 us
  Pallas kernels: 7.82 us -> 49.3 us
  local copies, waits for them, and re-layouts: 21.7 us -> 0.09 us
  starting transfers between devices: 59 us -> 41.7 us
  other arithmetic: 14.3 us -> 0 us
  waiting for transfers between devices: 54.2 us -> 48.5 us
    dot_general x24 -> x0, matrix products: 58.1 us -> none  [project(): jnp.einsum('td,djc->jtc', activations, columns, preferred_element_type=jn...]
    pallas_call x5 -> x18, Pallas kernels: 7.82 us -> 49.3 us  [the longest x3 22.6 us: project(): pl.pallas_call(body, grid_spec=pltpu.PrefetchScalarGridSpec(num_scalar_pr...]
    ppermute x20 -> x12, waiting for transfers between devices: 46.1 us -> 10.6 us  [shift_x(): lax.ppermute(value, 'chan', [(i, (i + 2 * step) % 8) for i in range(8)])]
    ppermute x10 -> x6, waiting for transfers between devices: 5.4 us -> 24.4 us  [swap_z(): return lax.ppermute(value, 'chan', [(i, i ^ 1) for i in range(8)])]
    ppermute x20 -> x12, starting transfers between devices: 26.5 us -> 12.8 us  [shift_x(): lax.ppermute(value, 'chan', [(i, (i + 2 * step) % 8) for i in range(8)])]
    slice x8 -> x0, local copies, waits for them, and re-layouts: 12.4 us -> none  [the longest x2 8.05 us: on_device(): kv_weight, q_weight = (proj_weight[:, 1:], proj_weight[:, :1])]
    all_to_all x3, waiting for transfers between devices: 2.75 us -> 13.6 us  [exchange(): return lax.all_to_all(value, 'seq', split_axis=0, concat_axis=0, tiled=True)]
    another operation x20 -> x0, other arithmetic: 8.71 us -> none  [the longest x4 3.63 us: z_first(): jnp.stack([right[0] + got_right[0] + from_left, right[1] + got_right[1]])]
  transfers between devices with their start and end apart: 33 -> 21, of which waited for: 11 -> 7; matrix products, arithmetic and copies ran while one was open for 38% -> 0% of each run, Pallas kernels for 3% -> 28%
where the time goes in v5:
time: 141 us; the launch traced here: 140 us
  Pallas kernels  49.3 us (35%)
  waiting for transfers between devices  48.5 us (34%)
  starting transfers between devices  41.7 us (30%)
    ppermute x6, waiting for transfers between devices, swap_z(): return lax.ppermute(value, 'chan', [(i, i ^ 1) for i in range(8)])  24.4 us
    all_to_all x3, starting transfers between devices, exchange(): return lax.all_to_all(value, 'seq', split_axis=0, concat_axis=0, tiled=True)  24.1 us
    pallas_call x3, Pallas kernels, project(): pl.pallas_call(body, grid_spec=pltpu.PrefetchScalarGridSpec(num_scalar_pr...  22.6 us
    pallas_call x6, Pallas kernels, sum_call(): pl.pallas_call(body, grid=(halves.rows // tile,), in_specs=[pl.BlockSpec(...  15.3 us
    all_to_all x3, waiting for transfers between devices, exchange(): return lax.all_to_all(value, 'seq', split_axis=0, concat_axis=0, tiled=True)  13.6 us
    ppermute x12, starting transfers between devices, shift_x(): lax.ppermute(value, 'chan', [(i, (i + 2 * step) % 8) for i in range(8)])  12.8 us
    pallas_call x6, Pallas kernels, call(): pl.pallas_call(body, grid=(1,), in_specs=[pl.BlockSpec(memory_space=pltpu...  11.4 us
    ppermute x12, waiting for transfers between devices, shift_x(): lax.ppermute(value, 'chan', [(i, (i + 2 * step) % 8) for i in range(8)])  10.6 us
  transfers between devices with their start and end apart: 21, of which 7 were waited for; matrix products, arithmetic and copies ran while one was open for 0% of the time, Pallas kernels for 28%

profile of v5, /device:TPU:1, one launch (start us, length us, event | category | flops | bytes accessed | tf_op | source)
XLA Modules:
  0.0 139.8 jit_solution(15274647982020591764)
XLA Ops:
  0.0 0.1 stack.23.at
  0.1 3.8 %first_kernel.1 = (f32[2,512,128]{2,1,0:T(8,128)S(1)}, f32[2,512,128]{2,1,0:T(8,128)S(1)}, f32[2,512,128]{2,1,0:T(8,128)S(1)}, f32[2,512,128]{2,1,0:T(8,128)S(1)}) custom-call(s32[5]{0:T(128)S(1)} %stack.23.at, bf16[1024,1024]{1,0:T(8,128)(2,1)} %act.5, bf16[3,1024,1024]{2,1,0:T(8,128)(2,1)} %bitcast.10), custom_call_target="tpu_custom_call" | custom-call | tf_op jit(solution)/shard_map/first_kernel/pallas_call | solution.py:122
  3.9 2.1 %collective-permute-start = (f32[2,512,128]{2,1,0:T(8,128)S(1)}, f32[2,512,128]{2,1,0:T(8,128)S(1)}, u32[]{:S(2)}, u32[]{:S(2)}) collective-permute-start(f32[2,512,128]{2,1,0:T(8,128)S(1)} %get-tuple-element.44), channel_id=1, source_target_pairs={{0,2},{1,3},{2,4},{3,5},{4,6},{5,7},{6,0},{7,1},{8,10},{9,11},{10,... | collective-permute-start | bytes 1572872 | tf_op jit(solution)/shard_map/ppermute | solution.py:26
  6.0 1.4 collective-permute-start.1
  7.4 1.8 %collective-permute-start.2 = (f32[2,512,128]{2,1,0:T(8,128)S(1)}, f32[2,512,128]{2,1,0:T(8,128)S(1)}, u32[]{:S(2)}, u32[]{:S(2)}) collective-permute-start(f32[2,512,128]{2,1,0:T(8,128)S(1)} %get-tuple-element.46), channel_id=1, source_target_pairs={{0,1},{1,0},{2,3},{3,2},{4,5},{5,4},{6,7},{7,6},{8,9},{9,8},{10,11... | collective-permute-start | bytes 1572872 | tf_op jit(solution)/shard_map/ppermute | solution.py:30
  9.2 9.1 %second_kernel.1 = (f32[5,512,128]{2,1,0:T(8,128)S(1)}, f32[5,512,128]{2,1,0:T(8,128)S(1)}, f32[5,512,128]{2,1,0:T(8,128)}, f32[1,512,128]{2,1,0:T(8,128)}, f32[...) custom-call(s32[5]{0:T(128)S(1)} %stack.23.at, bf16[1024,1024]{1,0:T(8,128)(2,1)} %act.5, ...), custom_call_target="tpu_custom_call" | custom-call | tf_op jit(solution)/shard_map/second_kernel/pallas_call | solution.py:122
  18.3 0.2 collective-permute-done.refs_2_
  18.5 1.6 %collective-permute-done.2.refs_5_ = f32[2,512,128]{2,1,0:T(8,128)S(1)} collective-permute-done((f32[2,512,128]{2,1,0:T(8,128)S(1)}, f32[2,512,128]{2,1,0:T(8,128)S(1)}, u32[]{:S(2)}, u32[]{:S(2)}) %collective-permute-start.2) | collective-permute-done | bytes 524320 | tf_op jit(solution)/shard_map/ppermute | solution.py:30
  20.1 1.4 %kv_first_sum_kernel.1 = (f32[5,512,128]{2,1,0:T(8,128)S(1)}, f32[5,512,128]{2,1,0:T(8,128)}) custom-call(f32[5,512,128]{2,1,0:T(8,128)S(1)} %get-tuple-element.42.refs_0_, f32[5,512,128]{2,1,0:T(8,128)S(1)} %get-tuple-element.43.refs_1_, f32[2,512,128]{2,1,0:T(8,128)S(1)} %collective-permute-done.refs_2_, ...), custom_call_target="tpu_custom_call" | custom-call | tf_op jit(solution)/shard_map/kv_first_sum_kernel/pallas_call | solution.py:149
  21.5 1.2 collective-permute-start.4
  22.7 0.3 collective-permute-start.3
  23.0 1.1 taps_turn_kernel.1
  24.2 11.0 %all-to-all-start = ((f32[16,8,8,128]{3,2,1,0:T(8,128)}), f32[16,8,8,128]{3,2,1,0:T(8,128)S(1)}, u32[]{:S(2)}, u32[]{:S(2)}) async-start(f32[16,8,8,128]{3,2,1,0:T(8,128)} %bitcast.14), calls=%async_computation | async-start | bytes 1048576 | tf_op jit(solution)/shard_map/all_to_all | solution.py:488
  35.1 9.6 %query_project_kernel.1 = (f32[4,256,128]{2,1,0:T(8,128)}, f32[4,256,128]{2,1,0:T(8,128)}, f32[2,256,128]{2,1,0:T(8,128)}, f32[2,256,128]{2,1,0:T(8,128)}, f32[6...) custom-call(s32[5]{0:T(128)S(1)} %stack.23.at, ...), custom_call_target="tpu_custom_call" | custom-call | tf_op jit(solution)/shard_map/query_project_kernel/pallas_call | solution.py:122
  44.8 13.6 %all-to-all-done.refs_0_ = f32[16,8,8,128]{3,2,1,0:T(8,128)S(1)} async-done(((f32[16,8,8,128]{3,2,1,0:T(8,128)}), f32[16,8,8,128]{3,2,1,0:T(8,128)S(1)}, u32[]{:S(2)}, u32[]{:S(2)}) %all-to-all-start) | async-done | bytes 524320 | tf_op jit(solution)/shard_map/all_to_all | solution.py:488
  58.3 2.2 %taps_kernel.1.refs_6_.refs_1_ = f32[1024,256]{1,0:T(8,128)S(1)} custom-call(f32[16,8,8,128]{3,2,1,0:T(8,128)S(1)} %all-to-all-done.refs_0_, bf16[256,128]{1,0:T(8,128)(2,1)} %constant.72.clone.refs_1_.refs_2_, bf16[256,128]{1,0:T(8,128)(2,1)} %constant.73.clone.refs_2_.refs_3_, f32[128,128]{1,0:T(8,128)} %constant.74.clone.refs_3_.refs_4_, ...), custom_call_target="tpu_custom_call" | custom-call | tf_op jit(solution)/shard_map/taps_kernel/pallas_call | solution.py:471
  60.5 0.0 collective-permute-done.4.refs_1_
  60.5 0.0 collective-permute-done.3.refs_0_
  60.5 4.8 %kv_second_sum_kernel.1 = (f32[2,512,128]{2,1,0:T(8,128)}, f32[2,512,128]{2,1,0:T(8,128)S(1)}, f32[3,512,128]{2,1,0:T(8,128)}) custom-call(f32[5,512,128]{2,1,0:T(8,128)} %collective-permute-done.3.refs_0_, f32[5,512,128]{2,1,0:T(8,128)} %collective-permute-done.4.refs_1_, f32[5,512,128]{2,1,0:T(8,128)} %collective-permute-done.5.refs_2_, ...), custom_call_target="tpu_custom_call" | custom-call | tf_op jit(solution)/shard_map/kv_second_sum_kernel/pallas_call | solution.py:149
  65.3 0.0 collective-permute-start.8
  65.3 1.3 collective-permute-start.7
  66.6 0.2 collective-permute-start.6
  66.8 1.5 %collective-permute-start.11 = (f32[6,256,128]{2,1,0:T(8,128)}, f32[6,256,128]{2,1,0:T(8,128)S(1)}, u32[]{:S(2)}, u32[]{:S(2)}) collective-permute-start(f32[6,256,128]{2,1,0:T(8,128)} %release.4), channel_id=1, source_target_pairs={{0,1},{1,0},{2,3},{3,2},{4,5},{5,4},{6,7},{7,6},{8,9},{9,8},{10,11... | collective-permute-start | bytes 2359304 | tf_op jit(solution)/shard_map/ppermute | solution.py:30
  68.3 0.0 collective-permute-start.9
  68.3 10.3 %collective-permute-done.7.refs_2_ = f32[2,512,128]{2,1,0:T(8,128)S(1)} collective-permute-done((f32[2,512,128]{2,1,0:T(8,128)S(1)}, f32[2,512,128]{2,1,0:T(8,128)S(1)}, u32[]{:S(2)}, u32[]{:S(2)}) %collective-permute-start.7) | collective-permute-done | bytes 524320 | tf_op jit(solution)/shard_map/ppermute | solution.py:26
  78.6 2.4 %collective-permute-start.10 = (f32[4,256,128]{2,1,0:T(8,128)}, f32[4,256,128]{2,1,0:T(8,128)S(1)}, u32[]{:S(2)}, u32[]{:S(2)}) collective-permute-start(f32[4,256,128]{2,1,0:T(8,128)} %get-tuple-element.62), channel_id=1, source_target_pairs={{0,6},{1,7},{2,0},{3,1},{4,2},{5,3},{6,4},{7,5},{8,14},{9,15},{10,... | collective-permute-start | bytes 1572872 | tf_op jit(solution)/shard_map/ppermute | solution.py:26
  81.0 3.6 %kv_beside_kernel.1 = (f32[2,512,128]{2,1,0:T(8,128)S(1)}, f32[2,512,128]{2,1,0:T(8,128)S(1)}) custom-call(f32[5,512,128]{2,1,0:T(8,128)} %collective-permute-done.3.refs_0_, f32[5,512,128]{2,1,0:T(8,128)} %collective-permute-done.4.refs_1_, f32[5,512,128]{2,1,0:T(8,128)} %collective-permute-done.5.refs_2_, f32[6,512,128]{2,1,0:T(8,128)} %get-tuple-element.50.refs_3_, ...), custom_call_target="tpu_custom_call" | custom-call | tf_op jit(solution)/shard_map/kv_beside_kernel/pallas_call | solution.py:149
  84.6 2.5 %kv_kernel.1 = f32[128,8,128]{2,1,0:T(8,128)} custom-call(f32[2,512,128]{2,1,0:T(8,128)S(1)} %get-tuple-element.56.refs_0_, f32[2,512,128]{2,1,0:T(8,128)} %collective-permute-done.6.refs_1_, f32[2,512,128]{2,1,0:T(8,128)S(1)} %collective-permute-done.7.refs_2_, f32[2,512,128]{2,1,0:T(8,128)S(1)} %get-tuple-element.58.refs_3_, ...), custom_call_target="tpu_custom_call" | custom-call | tf_op jit(solution)/shard_map/kv_kernel/pallas_call | solution.py:471
  87.1 6.2 %all-to-all-start.1 = ((f32[16,8,8,128]{3,2,1,0:T(8,128)}), f32[16,8,8,128]{3,2,1,0:T(8,128)S(1)}, u32[]{:S(2)}, u32[]{:S(2)}) async-start(f32[16,8,8,128]{3,2,1,0:T(8,128)} %bitcast.13), calls=%async_computation.1 | async-start | bytes 1048576 | tf_op jit(solution)/shard_map/all_to_all | solution.py:488
  93.3 0.0 collective-permute-done.9.refs_0_.refs_2_
  93.3 0.0 collective-permute-done.10.refs_1_.refs_3_
  93.3 12.0 %collective-permute-done.11.refs_2_.refs_4_ = f32[6,256,128]{2,1,0:T(8,128)S(1)} collective-permute-done((f32[6,256,128]{2,1,0:T(8,128)}, f32[6,256,128]{2,1,0:T(8,128)S(1)}, u32[]{:S(2)}, u32[]{:S(2)}) %collective-permute-start.11) | collective-permute-done | bytes 786464 | tf_op jit(solution)/shard_map/ppermute | solution.py:30
  105.4 2.4 %query_first_sum_kernel.1 = (f32[3,256,128]{2,1,0:T(8,128)}, f32[3,256,128]{2,1,0:T(8,128)}) custom-call(f32[4,256,128]{2,1,0:T(8,128)S(1)} %collective-permute-done.9.refs_0_.refs_2_, f32[4,256,128]{2,1,0:T(8,128)S(1)} %collective-permute-done.10.refs_1_.refs_3_, f32[6,256,128]{2,1,0:T(8,128)S(1)} %collective-permute-done.11.refs_2_.refs_4_, ...), custom_call_target="tpu_custom_call" | custom-call | tf_op jit(solution)/shard_map/query_first_sum_kernel/pallas_call | solution.py:149
  107.8 1.3 collective-permute-start.13
  109.0 0.2 collective-permute-start.12
  109.2 0.0 all-to-all-done.1.refs_0_
  109.2 4.4 %conv_kernel.1 = f32[16,8,8,128]{3,2,1,0:T(8,128)} custom-call(f32[16,8,8,128]{3,2,1,0:T(8,128)S(1)} %all-to-all-done.1.refs_0_, f32[1024,256]{1,0:T(8,128)S(1)} %taps_kernel.1.refs_6_.refs_1_, bf16[256,128]{1,0:T(8,128)(2,1)} %constant.72.clone.refs_1_.refs_2_, bf16[256,128]{1,0:T(8,128)(2,1)} %constant.73.clone.refs_2_.refs_3_, ...), custom_call_target="tpu_custom_call" | custom-call | tf_op jit(solution)/shard_map/conv_kernel/pallas_call | solution.py:471
  113.6 6.9 %all-to-all-start.2 = ((f32[16,8,8,128]{3,2,1,0:T(8,128)}), f32[16,8,8,128]{3,2,1,0:T(8,128)S(1)}, u32[]{:S(2)}, u32[]{:S(2)}) async-start(f32[16,8,8,128]{3,2,1,0:T(8,128)} %conv_kernel.1), calls=%async_computation.2 | async-start | bytes 1048576 | tf_op jit(solution)/shard_map/all_to_all | solution.py:488
  120.6 0.1 collective-permute-start.14
  120.7 0.0 collective-permute-done.13.refs_1_
  120.7 1.6 %query_second_sum_kernel.1 = (f32[2,256,128]{2,1,0:T(8,128)S(1)}, f32[2,256,128]{2,1,0:T(8,128)S(1)}, f32[2,256,128]{2,1,0:T(8,128)S(1)}) custom-call(f32[3,256,128]{2,1,0:T(8,128)} %collective-permute-done.12.refs_0_, f32[3,256,128]{2,1,0:T(8,128)} %collective-permute-done.13.refs_1_, f32[4,256,128]{2,1,0:T(8,128)S(1)} %collective-permute-done.9.refs_0_.refs_2_, ...), custom_call_target="tpu_custom_call" | custom-call | tf_op jit(solution)/shard_map/query_second_sum_kernel/pallas_call | solution.py:149
  122.3 2.6 %collective-permute-start.16 = (f32[2,256,128]{2,1,0:T(8,128)S(1)}, f32[2,256,128]{2,1,0:T(8,128)S(1)}, u32[]{:S(2)}, u32[]{:S(2)}) collective-permute-start(f32[2,256,128]{2,1,0:T(8,128)S(1)} %get-tuple-element.74), channel_id=1, source_target_pairs={{0,6},{1,7},{2,0},{3,1},{4,2},{5,3},{6,4},{7,5},{8,14},{9,15},{10,... | collective-permute-start | bytes 786440 | tf_op jit(solution)/shard_map/ppermute | solution.py:26
  124.9 1.4 %collective-permute-start.17 = (f32[2,256,128]{2,1,0:T(8,128)S(1)}, f32[2,256,128]{2,1,0:T(8,128)S(1)}, u32[]{:S(2)}, u32[]{:S(2)}) collective-permute-start(f32[2,256,128]{2,1,0:T(8,128)S(1)} %get-tuple-element.76), channel_id=1, source_target_pairs={{0,1},{1,0},{2,3},{3,2},{4,5},{5,4},{6,7},{7,6},{8,9},{9,8},{10,11... | collective-permute-start | bytes 786440 | tf_op jit(solution)/shard_map/ppermute | solution.py:30
  126.3 6.7 %collective-permute-done.14.refs_4_ = f32[2,256,128]{2,1,0:T(8,128)S(1)} collective-permute-done((f32[2,256,128]{2,1,0:T(8,128)}, f32[2,256,128]{2,1,0:T(8,128)S(1)}, u32[]{:S(2)}, u32[]{:S(2)}) %collective-permute-start.14) | collective-permute-done | bytes 262176 | tf_op jit(solution)/shard_map/ppermute | solution.py:30
  132.9 1.6 %query_beside_kernel.1 = (f32[2,256,128]{2,1,0:T(8,128)S(1)}, f32[2,256,128]{2,1,0:T(8,128)S(1)}) custom-call(f32[3,256,128]{2,1,0:T(8,128)} %collective-permute-done.12.refs_0_, f32[3,256,128]{2,1,0:T(8,128)} %collective-permute-done.13.refs_1_, f32[4,256,128]{2,1,0:T(8,128)S(1)} %collective-permute-done.9.refs_0_.refs_2_, ...), custom_call_target="tpu_custom_call" | custom-call | tf_op jit(solution)/shard_map/query_beside_kernel/pallas_call | solution.py:149
  134.5 4.0 %collective-permute-done.17.refs_4_ = f32[2,256,128]{2,1,0:T(8,128)S(1)} collective-permute-done((f32[2,256,128]{2,1,0:T(8,128)S(1)}, f32[2,256,128]{2,1,0:T(8,128)S(1)}, u32[]{:S(2)}, u32[]{:S(2)}) %collective-permute-start.17) | collective-permute-done | bytes 262176 | tf_op jit(solution)/shard_map/ppermute | solution.py:30
  138.6 0.1 query_kernel.1.refs_1_
  138.6 1.1 gate_kernel.1
  (17 shorter events, 0.0 us)
Async XLA Ops:
  3.9 14.6 %collective-permute-start = (f32[2,512,128]{2,1,0:T(8,128)S(1)}, f32[2,512,128]{2,1,0:T(8,128)S(1)}, u32[]{:S(2)}, u32[]{:S(2)}) collective-permute-start(f32[2,512,128]{2,1,0:T(8,128)S(1)} %get-tuple-element.44), channel_id=1, source_target_pairs={{0,2},{1,3},{2,4},{3,5},{4,6},{5,7},{6,0},{7,1},{8,10},{9,11},{10,... | collective-permute-start | bytes 1572872 | tf_op jit(solution)/shard_map/ppermute | solution.py:26
  6.0 12.5 %collective-permute-start.1 = (f32[2,512,128]{2,1,0:T(8,128)S(1)}, f32[2,512,128]{2,1,0:T(8,128)S(1)}, u32[]{:S(2)}, u32[]{:S(2)}) collective-permute-start(f32[2,512,128]{2,1,0:T(8,128)S(1)} %get-tuple-element.45), channel_id=1, source_target_pairs={{0,6},{1,7},{2,0},{3,1},{4,2},{5,3},{6,4},{7,5},{8,14},{9,15},{10,... | collective-permute-start | bytes 1572872 | tf_op jit(solution)/shard_map/ppermute | solution.py:26
  7.4 12.7 %collective-permute-start.2 = (f32[2,512,128]{2,1,0:T(8,128)S(1)}, f32[2,512,128]{2,1,0:T(8,128)S(1)}, u32[]{:S(2)}, u32[]{:S(2)}) collective-permute-start(f32[2,512,128]{2,1,0:T(8,128)S(1)} %get-tuple-element.46), channel_id=1, source_target_pairs={{0,1},{1,0},{2,3},{3,2},{4,5},{5,4},{6,7},{7,6},{8,9},{9,8},{10,11... | collective-permute-start | bytes 1572872 | tf_op jit(solution)/shard_map/ppermute | solution.py:30
  18.3 42.2 %collective-permute-start.5 = (f32[5,512,128]{2,1,0:T(8,128)}, f32[5,512,128]{2,1,0:T(8,128)}, u32[]{:S(2)}, u32[]{:S(2)}) collective-permute-start(f32[5,512,128]{2,1,0:T(8,128)} %get-tuple-element.49), channel_id=1, source_target_pairs={{0,1},{1,0},{2,3},{3,2},{4,5},{5,4},{6,7},{7,6},{8,9},{9,8},{10,11... | collective-permute-start | bytes 3932168 | tf_op jit(solution)/shard_map/ppermute | solution.py:30
  20.1 2.9 %copy-start.1 = (f32[1024,128]{1,0:T(8,128)S(1)}, f32[1024,128]{1,0:T(8,128)}, u32[]{:S(2)}) copy-start(f32[1024,128]{1,0:T(8,128)} %refs_0_.1) | copy-start | bytes 1572868
  21.5 39.0 %collective-permute-start.4 = (f32[5,512,128]{2,1,0:T(8,128)}, f32[5,512,128]{2,1,0:T(8,128)}, u32[]{:S(2)}, u32[]{:S(2)}) collective-permute-start(f32[5,512,128]{2,1,0:T(8,128)} %get-tuple-element.48), channel_id=1, source_target_pairs={{0,6},{1,7},{2,0},{3,1},{4,2},{5,3},{6,4},{7,5},{8,14},{9,15},{10,... | collective-permute-start | bytes 3932168 | tf_op jit(solution)/shard_map/ppermute | solution.py:26
  22.7 37.8 %collective-permute-start.3 = (f32[5,512,128]{2,1,0:T(8,128)S(1)}, f32[5,512,128]{2,1,0:T(8,128)}, u32[]{:S(2)}, u32[]{:S(2)}) collective-permute-start(f32[5,512,128]{2,1,0:T(8,128)S(1)} %get-tuple-element.47.refs_1_.refs_0_), channel_id=1, source_target_pairs={{0,2},{1,3},{2,4},{3,5},{4,6},{5,7},{6,0},{7,1},{8,10},{9,11},{10,... | collective-permute-start | bytes 3932168 | tf_op jit(solution)/shard_map/ppermute | solution.py:26
  24.2 34.2 %all-to-all-start = ((f32[16,8,8,128]{3,2,1,0:T(8,128)}), f32[16,8,8,128]{3,2,1,0:T(8,128)S(1)}, u32[]{:S(2)}, u32[]{:S(2)}) async-start(f32[16,8,8,128]{3,2,1,0:T(8,128)} %bitcast.14), calls=%async_computation | async-start | bytes 1048576 | tf_op jit(solution)/shard_map/all_to_all | solution.py:488
  44.8 15.8 %copy-start = (f32[4,256,128]{2,1,0:T(8,128)S(1)}, f32[4,256,128]{2,1,0:T(8,128)}, u32[]{:S(2)}) copy-start(f32[4,256,128]{2,1,0:T(8,128)} %get-tuple-element.54.refs_7_.refs_0_) | copy-start | bytes 1572868
  65.3 19.3 %collective-permute-start.8 = (f32[3,512,128]{2,1,0:T(8,128)}, f32[3,512,128]{2,1,0:T(8,128)}, u32[]{:S(2)}, u32[]{:S(2)}) collective-permute-start(f32[3,512,128]{2,1,0:T(8,128)} %get-tuple-element.59), channel_id=1, source_target_pairs={{0,1},{1,0},{2,3},{3,2},{4,5},{5,4},{6,7},{7,6},{8,9},{9,8},{10,11... | collective-permute-start | bytes 2359304 | tf_op jit(solution)/shard_map/ppermute | solution.py:30
  65.3 13.3 %collective-permute-start.7 = (f32[2,512,128]{2,1,0:T(8,128)S(1)}, f32[2,512,128]{2,1,0:T(8,128)S(1)}, u32[]{:S(2)}, u32[]{:S(2)}) collective-permute-start(f32[2,512,128]{2,1,0:T(8,128)S(1)} %get-tuple-element.57), channel_id=1, source_target_pairs={{0,6},{1,7},{2,0},{3,1},{4,2},{5,3},{6,4},{7,5},{8,14},{9,15},{10,... | collective-permute-start | bytes 1572872 | tf_op jit(solution)/shard_map/ppermute | solution.py:26
  66.6 18.0 %collective-permute-start.6 = (f32[2,512,128]{2,1,0:T(8,128)}, f32[2,512,128]{2,1,0:T(8,128)}, u32[]{:S(2)}, u32[]{:S(2)}) collective-permute-start(f32[2,512,128]{2,1,0:T(8,128)} %get-tuple-element.55.refs_5_.refs_2_.refs_1_), channel_id=1, source_target_pairs={{0,2},{1,3},{2,4},{3,5},{4,6},{5,7},{6,0},{7,1},{8,10},{9,11},{10,... | collective-permute-start | bytes 1572872 | tf_op jit(solution)/shard_map/ppermute | solution.py:26
  66.8 38.6 %collective-permute-start.11 = (f32[6,256,128]{2,1,0:T(8,128)}, f32[6,256,128]{2,1,0:T(8,128)S(1)}, u32[]{:S(2)}, u32[]{:S(2)}) collective-permute-start(f32[6,256,128]{2,1,0:T(8,128)} %release.4), channel_id=1, source_target_pairs={{0,1},{1,0},{2,3},{3,2},{4,5},{5,4},{6,7},{7,6},{8,9},{9,8},{10,11... | collective-permute-start | bytes 2359304 | tf_op jit(solution)/shard_map/ppermute | solution.py:30
  68.3 25.1 %collective-permute-start.9 = (f32[4,256,128]{2,1,0:T(8,128)}, f32[4,256,128]{2,1,0:T(8,128)S(1)}, u32[]{:S(2)}, u32[]{:S(2)}) collective-permute-start(f32[4,256,128]{2,1,0:T(8,128)} %get-tuple-element.61), channel_id=1, source_target_pairs={{0,2},{1,3},{2,4},{3,5},{4,6},{5,7},{6,0},{7,1},{8,10},{9,11},{10,... | collective-permute-start | bytes 1572872 | tf_op jit(solution)/shard_map/ppermute | solution.py:26
  78.6 14.7 %collective-permute-start.10 = (f32[4,256,128]{2,1,0:T(8,128)}, f32[4,256,128]{2,1,0:T(8,128)S(1)}, u32[]{:S(2)}, u32[]{:S(2)}) collective-permute-start(f32[4,256,128]{2,1,0:T(8,128)} %get-tuple-element.62), channel_id=1, source_target_pairs={{0,6},{1,7},{2,0},{3,1},{4,2},{5,3},{6,4},{7,5},{8,14},{9,15},{10,... | collective-permute-start | bytes 1572872 | tf_op jit(solution)/shard_map/ppermute | solution.py:26
  87.1 22.1 %all-to-all-start.1 = ((f32[16,8,8,128]{3,2,1,0:T(8,128)}), f32[16,8,8,128]{3,2,1,0:T(8,128)S(1)}, u32[]{:S(2)}, u32[]{:S(2)}) async-start(f32[16,8,8,128]{3,2,1,0:T(8,128)} %bitcast.13), calls=%async_computation.1 | async-start | bytes 1048576 | tf_op jit(solution)/shard_map/all_to_all | solution.py:488
  107.8 12.9 %collective-permute-start.13 = (f32[3,256,128]{2,1,0:T(8,128)}, f32[3,256,128]{2,1,0:T(8,128)}, u32[]{:S(2)}, u32[]{:S(2)}) collective-permute-start(f32[3,256,128]{2,1,0:T(8,128)} %get-tuple-element.68), channel_id=1, source_target_pairs={{0,6},{1,7},{2,0},{3,1},{4,2},{5,3},{6,4},{7,5},{8,14},{9,15},{10,... | collective-permute-start | bytes 1179656 | tf_op jit(solution)/shard_map/ppermute | solution.py:26
  109.0 11.7 %collective-permute-start.12 = (f32[3,256,128]{2,1,0:T(8,128)}, f32[3,256,128]{2,1,0:T(8,128)}, u32[]{:S(2)}, u32[]{:S(2)}) collective-permute-start(f32[3,256,128]{2,1,0:T(8,128)} %get-tuple-element.67.refs_1_), channel_id=1, source_target_pairs={{0,2},{1,3},{2,4},{3,5},{4,6},{5,7},{6,0},{7,1},{8,10},{9,11},{10,... | collective-permute-start | bytes 1179656 | tf_op jit(solution)/shard_map/ppermute | solution.py:26
  113.6 25.0 %all-to-all-start.2 = ((f32[16,8,8,128]{3,2,1,0:T(8,128)}), f32[16,8,8,128]{3,2,1,0:T(8,128)S(1)}, u32[]{:S(2)}, u32[]{:S(2)}) async-start(f32[16,8,8,128]{3,2,1,0:T(8,128)} %conv_kernel.1), calls=%async_computation.2 | async-start | bytes 1048576 | tf_op jit(solution)/shard_map/all_to_all | solution.py:488
  120.6 12.4 %collective-permute-start.14 = (f32[2,256,128]{2,1,0:T(8,128)}, f32[2,256,128]{2,1,0:T(8,128)S(1)}, u32[]{:S(2)}, u32[]{:S(2)}) collective-permute-start(f32[2,256,128]{2,1,0:T(8,128)} %release.5), channel_id=1, source_target_pairs={{0,1},{1,0},{2,3},{3,2},{4,5},{5,4},{6,7},{7,6},{8,9},{9,8},{10,11... | collective-permute-start | bytes 786440 | tf_op jit(solution)/shard_map/ppermute | solution.py:30
  122.3 12.2 %collective-permute-start.16 = (f32[2,256,128]{2,1,0:T(8,128)S(1)}, f32[2,256,128]{2,1,0:T(8,128)S(1)}, u32[]{:S(2)}, u32[]{:S(2)}) collective-permute-start(f32[2,256,128]{2,1,0:T(8,128)S(1)} %get-tuple-element.74), channel_id=1, source_target_pairs={{0,6},{1,7},{2,0},{3,1},{4,2},{5,3},{6,4},{7,5},{8,14},{9,15},{10,... | collective-permute-start | bytes 786440 | tf_op jit(solution)/shard_map/ppermute | solution.py:26
  124.9 13.7 %collective-permute-start.17 = (f32[2,256,128]{2,1,0:T(8,128)S(1)}, f32[2,256,128]{2,1,0:T(8,128)S(1)}, u32[]{:S(2)}, u32[]{:S(2)}) collective-permute-start(f32[2,256,128]{2,1,0:T(8,128)S(1)} %get-tuple-element.76), channel_id=1, source_target_pairs={{0,1},{1,0},{2,3},{3,2},{4,5},{5,4},{6,7},{7,6},{8,9},{9,8},{10,11... | collective-permute-start | bytes 786440 | tf_op jit(solution)/shard_map/ppermute | solution.py:30
  126.3 12.3 %collective-permute-start.15 = (f32[2,256,128]{2,1,0:T(8,128)S(1)}, f32[2,256,128]{2,1,0:T(8,128)S(1)}, u32[]{:S(2)}, u32[]{:S(2)}) collective-permute-start(f32[2,256,128]{2,1,0:T(8,128)S(1)} %get-tuple-element.72.refs_7_), channel_id=1, source_target_pairs={{0,2},{1,3},{2,4},{3,5},{4,6},{5,7},{6,0},{7,1},{8,10},{9,11},{10,... | collective-permute-start | bytes 786440 | tf_op jit(solution)/shard_map/ppermute | solution.py:26

commit v6 on v5

--- a/solution.py
+++ b/solution.py
@@ -49,10 +49,13 @@
 
     def fill(self, place, act, weight, half, x_outs, z_outs):
         for begin, outs in ((self.x_start[half], x_outs), (self.z_start[half], z_outs)):
+            if outs == (None, None):
+                continue
             for start in range(0, self.rows, CHUNK):
                 rows = act[begin + start : begin + start + CHUNK]
-                for (ref, piece), part in zip(outs, parts_of(rows, weight[0], place[4])):
-                    ref[piece, start : start + CHUNK] = part
+                for out, part in zip(outs, parts_of(rows, weight[0], place[4])):
+                    if out is not None:
+                        out[0][out[1], start : start + CHUNK] = part
 
 
 def first_kernel(halves, place, act, weight, outs):
@@ -72,20 +75,30 @@
 
 
 def second_kernel(halves, place, act, weight, outs):
-    dep_r, dep_l, z_send, z_late, z_mine, x_other, x_mine = outs
+    near_r, near_l, keep_r, keep_l, z_send = outs
     x_outs = (
-        ((dep_r, 2), (dep_r, 3)),
-        ((dep_r, 0), (dep_r, 1)),
-        ((dep_l, 0), (dep_l, 1)),
-        ((dep_l, 2), (dep_l, 3)),
-        ((x_other, 0), (x_mine, 0)),
-        ((x_other, 0), (x_mine, 0)),
+        ((keep_r, 0), (keep_r, 1)),
+        ((near_r, 0), (near_r, 1)),
+        ((near_l, 0), (near_l, 1)),
+        ((keep_l, 0), (keep_l, 1)),
+        (None, None),
     )
     for i, outs in enumerate(x_outs):
-        z_other = (z_send, i) if i < 5 else (z_late, 0)
         pl.when(pl.program_id(0) == i)(
             functools.partial(
-                halves.fill, place, act, weight, i % 2, outs, (z_other, (z_mine, 0))
+                halves.fill, place, act, weight, i % 2, outs, ((z_send, i), None)
+            )
+        )
+
+
+def third_kernel(halves, place, act, weight, outs):
+    z_mine, z_late, x_other, x_mine = outs
+    for i in range(6):
+        x_outs = (None, None) if i < 4 else ((x_other, i - 4), (x_mine, i - 4))
+        z_other = (z_late, 0) if i == 5 else None
+        pl.when(pl.program_id(0) == i)(
+            functools.partial(
+                halves.fill, place, act, weight, i % 2, x_outs, (z_other, (z_mine, i))
             )
         )
 
@@ -159,30 +172,34 @@
     )(*near, *[in_hbm(value) for value in far], *after)
 
 
-def kv_first_sum_kernel(dep_r, dep_l, got_r, got_l, z_mine, z_got, out_r, out_l):
-    for half, (dep, got, out) in enumerate(((dep_r, got_r, out_r), (dep_l, got_l, out_l))):
-        out[0] = dep[0]
-        out[1] = dep[1]
-        out[2] = dep[2] + got[0]
-        out[3] = dep[3] + got[1]
-        out[4] = z_mine[half] + z_got[half]
-
-
-def kv_second_sum_kernel(dep_r, dep_l, z_got, z_mine, x_other, z_late, out_r, out_l, out_xz):
-    out_r[0] = z_mine[0] + z_got[0] + dep_r[4]
+def first_sum_kernel(got_r, got_l, z_got, keep_r, keep_l, z_mine, out_r, out_l):
+    for half, (keep, got, out) in enumerate(((keep_r, got_r, out_r), (keep_l, got_l, out_l))):
+        out[0] = keep[0] + got[0]
+        out[1] = keep[1] + got[1]
+        out[2] = z_mine[half] + z_got[half]
+
+
+def kv_near_kernel(near_r, near_l, x_other, x_mine, out_other, out_mine):
+    for half, near in enumerate((near_l, near_r)):
+        out_other[half] = x_other[half] + near[0]
+        out_mine[half] = x_mine[half] + near[1]
+
+
+def kv_second_sum_kernel(dep_r, dep_l, z_got, z_mine, x_part, z_late, out_r, out_l, out_xz):
+    out_r[0] = z_mine[0] + z_got[0] + dep_r[2]
     out_r[1] = z_mine[1] + z_got[1]
     out_l[0] = z_mine[2] + z_got[2]
-    out_l[1] = z_mine[3] + z_got[3] + dep_l[4]
-    out_xz[0] = x_other[0] + (dep_r[2] + dep_l[0])
-    out_xz[1] = x_other[1] + (dep_r[0] + dep_l[2])
+    out_l[1] = z_mine[3] + z_got[3] + dep_l[2]
+    out_xz[0] = x_part[0] + dep_r[0]
+    out_xz[1] = x_part[1] + dep_l[0]
     out_xz[2] = z_late[0]
 
 
-def kv_beside_kernel(dep_r, dep_l, z_got, z_mine, x_mine, out_z, out_x):
+def kv_beside_kernel(dep_r, dep_l, z_got, z_mine, x_part, out_z, out_x):
     out_z[0] = z_mine[4] + z_got[4]
     out_z[1] = z_mine[5]
-    out_x[0] = x_mine[0] + (dep_r[3] + dep_l[1])
-    out_x[1] = x_mine[1] + (dep_r[1] + dep_l[3])
+    out_x[0] = x_part[0] + dep_r[1]
+    out_x[1] = x_part[1] + dep_l[1]
 
 
 def release(values, after):
@@ -201,7 +218,7 @@
 
 
 def query_project_kernel(halves, place, act, weight, outs):
-    send_r, send_l, keep_r, keep_l, z_send, z_late, z_mine, x_other, x_mine = outs
+    send_r, send_l, keep_r, keep_l, z_send, z_next, z_late, z_mine, x_other, x_mine = outs
     x_outs = (
         ((send_r, 0), (send_r, 1)),
         ((send_l, 0), (send_l, 1)),
@@ -213,7 +230,7 @@
         ((x_other, 0), (x_mine, 0)),
     )
     for i, outs in enumerate(x_outs):
-        z_other = z_send if i < 6 else z_late
+        z_other = (z_send, z_next, z_late)[i // 3]
         pl.when(pl.program_id(0) == i)(
             functools.partial(
                 halves.fill, place, act, weight, i % 2, outs, ((z_other, 0), (z_mine, 0))
@@ -221,20 +238,13 @@
         )
 
 
-def query_first_sum_kernel(got_r, got_l, z_got, keep_r, keep_l, z_mine, out_r, out_l):
-    for half, (keep, got, out) in enumerate(((keep_r, got_r, out_r), (keep_l, got_l, out_l))):
-        out[0] = keep[0] + got[0]
-        out[1] = keep[1] + got[1]
-        out[2] = z_mine[half] + z_got[half]
-
-
 def query_second_sum_kernel(
-    dep_r, dep_l, got_r, got_l, z_got, z_mine, x_other, out_r, out_l, out_x
+    dep_r, dep_l, got_r, got_l, z_got, z_next, z_mine, x_other, out_r, out_l, out_x
 ):
     out_r[0] = z_mine[2] + z_got[2] + dep_r[2]
-    out_r[1] = z_mine[3] + z_got[3]
-    out_l[0] = z_mine[4] + z_got[4]
-    out_l[1] = z_mine[5] + z_got[5] + dep_l[2]
+    out_r[1] = z_mine[3] + z_next[0]
+    out_l[0] = z_mine[4] + z_next[1]
+    out_l[1] = z_mine[5] + z_next[2] + dep_l[2]
     out_x[0] = x_other[0] + (dep_r[0] + got_l[2])
     out_x[1] = x_other[1] + (got_r[2] + dep_l[0])
 
@@ -247,41 +257,52 @@
 
 
 def reduce_kv(halves, place, activations, weight, beside):
-    send_r, send_l, z_send, z_mine = project(
-        first_kernel, halves, place, activations, weight, 0, 2, [(2, "vmem")] * 4
+    make = functools.partial(
+        project, halves=halves, place=place, activations=activations, weight=weight
+    )
+    send_r, send_l, z_send, z_mine = make(
+        first_kernel, owner=0, steps=2, outs=[(2, "vmem")] * 4
     )
     got_r, got_l, z_got = shift_x(send_r, 1), shift_x(send_l, -1), swap_z(z_send)
-    dep_r, dep_l, z_send, z_late, z_six, x_other, x_mine = project(
+    near_r, near_l, keep_r, keep_l, z_send = make(
         second_kernel,
-        halves,
-        place,
-        activations,
-        weight,
-        1,
-        6,
-        [(5, "vmem")] * 3 + [(1, 0), (6, 0), (2, 4), (2, 4)],
+        owner=1,
+        steps=5,
+        outs=[(2, "vmem")] * 4 + [(5, "vmem")],
         after=(z_mine,),
     )
+    near_r, near_l, z_five = shift_x(near_r, 1), shift_x(near_l, -1), swap_z(z_send)
     dep_r, dep_l = sum_call(
-        kv_first_sum_kernel,
-        halves,
-        [5, 5],
-        [dep_r, dep_l, got_r, got_l, z_mine, z_got],
-        [],
-    )
-    ready = beside(dep_r)
-    dep_r, dep_l, z_got = shift_x(dep_r, 1), shift_x(dep_l, -1), swap_z(z_send)
+        first_sum_kernel, halves, [3, 3], [got_r, got_l, z_got, keep_r, keep_l, z_mine], []
+    )
+    z_six, z_late, x_other, x_mine = make(
+        third_kernel,
+        owner=1,
+        steps=6,
+        outs=[(6, "vmem"), (1, "vmem"), (2, "vmem"), (2, "vmem")],
+        after=(dep_r,),
+    )
+    x_part_other, x_part_mine = sum_call(
+        kv_near_kernel, halves, [2, 2], [near_r, near_l, x_other, x_mine], []
+    )
+    ready = beside(dep_r, x_part_mine)
+    dep_r, dep_l = shift_x(dep_r, 1), shift_x(dep_l, -1)
     last_r, last_l, last_xz = sum_call(
         kv_second_sum_kernel,
         halves,
         [2, 2, 3],
-        [dep_r, dep_l, z_got],
-        [z_six, x_other, z_late],
+        [dep_r, dep_l, z_five, z_six, x_part_other, z_late],
+        [],
         after=ready,
     )
     last = last_r
     z_part, x_part = sum_call(
-        kv_beside_kernel, halves, [2, 2], [dep_r, dep_l, z_got], [z_six, x_mine], after=(last,)
+        kv_beside_kernel,
+        halves,
+        [2, 2],
+        [dep_r, dep_l, z_five, z_six, x_part_mine],
+        [],
+        after=(last,),
     )
     last_r, last_l, last_xz = shift_x(last_r, 1), shift_x(last_l, -1), swap_z(last_xz)
     return (z_part, last_r, last_l, x_part, last_xz), last
@@ -296,19 +317,18 @@
         weight,
         0,
         8,
-        [(4, "hbm")] * 2 + [(2, "hbm")] * 2 + [(6, 0), (2, 6), (8, 0), (2, 6), (2, 6)],
+        [(4, "hbm")] * 2 + [(2, "hbm")] * 2 + [(3, 0), (3, 3), (2, 6), (8, 0), (2, 6), (2, 6)],
         after=after,
     )
 
 
-def reduce_query(halves, projected, x_after, z_after):
-    send_r, send_l, keep_r, keep_l, z_send, z_late, z_mine, x_other, x_mine = projected
-    send_r, send_l = release((send_r, send_l), x_after)
-    got_r, got_l = shift_x(send_r, 1), shift_x(send_l, -1)
-    (z_send,) = release((z_send,), z_after)
-    z_got = swap_z(z_send)
+def reduce_query(halves, projected, after):
+    send_r, send_l, keep_r, keep_l, z_send, z_next, z_late, z_mine, x_other, x_mine = projected
+    got_r, got_l, z_got = shift_x(send_r, 1), shift_x(send_l, -1), swap_z(z_send)
+    (z_next,) = release((z_next,), after)
+    z_next = swap_z(z_next)
     dep_r, dep_l = sum_call(
-        query_first_sum_kernel,
+        first_sum_kernel,
         halves,
         [3, 3],
         [got_r, got_l, z_got],
@@ -320,7 +340,7 @@
         query_second_sum_kernel,
         halves,
         [2, 2, 2],
-        [dep_r, dep_l, got_r, got_l, z_got],
+        [dep_r, dep_l, got_r, got_l, z_got, z_next],
         [z_mine, x_other],
     )
     z_part, x_part = sum_call(
@@ -508,32 +528,35 @@
     hold = {}
     kv_halves, q_halves = Halves(tokens, (1, 2)), Halves(tokens, (0,))
 
-    def prepare(ready):
+    def prepare(ready, later):
         taps = call(taps_turn_kernel, turned_shape, filter_taps, after=(ready,), to_hbm=True)
-        hold["spectrum"] = call(
-            taps_kernel,
-            (owned * length // BLOCK, 2 * BLOCK),
-            exchange(taps.reshape(moved_shape)),
-            tables=first + turn + second,
-        )
-        hold["query"] = project_query(q_halves, place, activations, weight, (ready,))
-        return hold["spectrum"], hold["query"][0]
+        hold["taps"] = exchange(taps.reshape(moved_shape))
+        hold["query"] = project_query(q_halves, place, activations, weight, (later,))
+        return hold["taps"], hold["query"][0]
 
     kv_parts, kv_last = reduce_kv(kv_halves, place, activations, weight, prepare)
+    spectrum = call(
+        taps_kernel,
+        (owned * length // BLOCK, 2 * BLOCK),
+        hold["taps"],
+        tables=first + turn + second,
+        after=(kv_last,),
+    )
     kv = call(
         kv_kernel,
         turned_shape,
         *kv_parts,
+        after=(spectrum,),
         scratch=[pltpu.VMEM((tokens, channels), jnp.float32)],
         to_hbm=True,
     )
-    q_parts = reduce_query(q_halves, hold["query"], kv_last, kv_last)
+    q_parts = reduce_query(q_halves, hold["query"], kv_last)
     moved = exchange(kv.reshape(moved_shape))
     convolved = call(
         conv_kernel,
         moved_shape,
         moved,
-        hold["spectrum"],
+        spectrum,
         tables=first + turn + second + back + inverse,
         to_hbm=True,
     )

time: 141 us -> 142 us (level)
  waiting for transfers between devices: 48.5 us -> 26.2 us
  starting transfers between devices: 41.7 us -> 61.4 us
  local copies, waits for them, and re-layouts: 0.09 us -> 3.69 us
    ppermute x6 -> x7, waiting for transfers between devices: 24.4 us -> 12.5 us  [swap_z(): return lax.ppermute(value, 'chan', [(i, i ^ 1) for i in range(8)])]
    all_to_all x3, starting transfers between devices: 24.1 us -> 35.3 us  [exchange(): return lax.all_to_all(value, 'seq', split_axis=0, concat_axis=0, tiled=True)]
    all_to_all x3, waiting for transfers between devices: 13.6 us -> 5.64 us  [exchange(): return lax.all_to_all(value, 'seq', split_axis=0, concat_axis=0, tiled=True)]
    ppermute x12 -> x14, starting transfers between devices: 12.8 us -> 19.7 us  [shift_x(): lax.ppermute(value, 'chan', [(i, (i + 2 * step) % 8) for i in range(8)])]
    pallas_call x3 -> x4, Pallas kernels: 22.6 us -> 28.4 us  [project(): pl.pallas_call(body, grid_spec=pltpu.PrefetchScalarGridSpec(num_scalar_pr...]
    pallas_call x6 -> x7, Pallas kernels: 15.3 us -> 11.3 us  [sum_call(): pl.pallas_call(body, grid=(halves.rows // tile,), in_specs=[pl.BlockSpec(...]
    unnamed x4 -> x18, local copies, waits for them, and re-layouts: 0.01 us -> 3.6 us
    ppermute x12 -> x14, waiting for transfers between devices: 10.6 us -> 7.99 us  [shift_x(): lax.ppermute(value, 'chan', [(i, (i + 2 * step) % 8) for i in range(8)])]
  transfers between devices with their start and end apart: 21 -> 24, of which waited for: 7 -> 7; matrix products, arithmetic and copies ran while one was open for 0% -> 0% of each run, Pallas kernels for 28% -> 31%
where the time goes in v6:
time: 142 us; the launch traced here: 141 us
  starting transfers between devices  61.4 us (43%)
  Pallas kernels  49.8 us (35%)
  waiting for transfers between devices  26.2 us (18%)
  local copies, waits for them, and re-layouts  3.69 us (3%)
    all_to_all x3, starting transfers between devices, exchange(): return lax.all_to_all(value, 'seq', split_axis=0, concat_axis=0, tiled=True)  35.3 us
    pallas_call x4, Pallas kernels, project(): pl.pallas_call(body, grid_spec=pltpu.PrefetchScalarGridSpec(num_scalar_pr...  28.4 us
    ppermute x14, starting transfers between devices, shift_x(): lax.ppermute(value, 'chan', [(i, (i + 2 * step) % 8) for i in range(8)])  19.7 us
    ppermute x7, waiting for transfers between devices, swap_z(): return lax.ppermute(value, 'chan', [(i, i ^ 1) for i in range(8)])  12.5 us
    pallas_call x7, Pallas kernels, sum_call(): pl.pallas_call(body, grid=(halves.rows // tile,), in_specs=[pl.BlockSpec(...  11.3 us
    pallas_call x6, Pallas kernels, call(): pl.pallas_call(body, grid=(1,), in_specs=[pl.BlockSpec(memory_space=pltpu...  10.1 us
    ppermute x14, waiting for transfers between devices, shift_x(): lax.ppermute(value, 'chan', [(i, (i + 2 * step) % 8) for i in range(8)])  7.99 us
    ppermute x7, starting transfers between devices, swap_z(): return lax.ppermute(value, 'chan', [(i, i ^ 1) for i in range(8)])  6.39 us
  transfers between devices with their start and end apart: 24, of which 7 were waited for; matrix products, arithmetic and copies ran while one was open for 0% of the time, Pallas kernels for 31%

profile of v6, /device:TPU:1, one launch (start us, length us, event | category | flops | bytes accessed | tf_op | source)
XLA Modules:
  0.0 141.3 jit_solution(4951269253090336909)
XLA Ops:
  0.0 0.1 stack.23.at
  0.1 3.8 %first_kernel.1 = (f32[2,512,128]{2,1,0:T(8,128)S(1)}, f32[2,512,128]{2,1,0:T(8,128)S(1)}, f32[2,512,128]{2,1,0:T(8,128)S(1)}, f32[2,512,128]{2,1,0:T(8,128)S(1)}) custom-call(s32[5]{0:T(128)S(1)} %stack.23.at, bf16[1024,1024]{1,0:T(8,128)(2,1)} %act.7, bf16[3,1024,1024]{2,1,0:T(8,128)(2,1)} %bitcast.10), custom_call_target="tpu_custom_call" | custom-call | tf_op jit(solution)/shard_map/first_kernel/pallas_call | solution.py:135
  3.9 2.1 %collective-permute-start = (f32[2,512,128]{2,1,0:T(8,128)S(1)}, f32[2,512,128]{2,1,0:T(8,128)S(1)}, u32[]{:S(2)}, u32[]{:S(2)}) collective-permute-start(f32[2,512,128]{2,1,0:T(8,128)S(1)} %get-tuple-element.44), channel_id=1, source_target_pairs={{0,2},{1,3},{2,4},{3,5},{4,6},{5,7},{6,0},{7,1},{8,10},{9,11},{10,... | collective-permute-start | bytes 1572872 | tf_op jit(solution)/shard_map/ppermute | solution.py:26
  6.0 1.4 collective-permute-start.1
  7.4 1.8 %collective-permute-start.2 = (f32[2,512,128]{2,1,0:T(8,128)S(1)}, f32[2,512,128]{2,1,0:T(8,128)S(1)}, u32[]{:S(2)}, u32[]{:S(2)}) collective-permute-start(f32[2,512,128]{2,1,0:T(8,128)S(1)} %get-tuple-element.46), channel_id=1, source_target_pairs={{0,1},{1,0},{2,3},{3,2},{4,5},{5,4},{6,7},{7,6},{8,9},{9,8},{10,11... | collective-permute-start | bytes 1572872 | tf_op jit(solution)/shard_map/ppermute | solution.py:30
  9.2 7.9 %second_kernel.1 = (f32[2,512,128]{2,1,0:T(8,128)}, f32[2,512,128]{2,1,0:T(8,128)}, f32[2,512,128]{2,1,0:T(8,128)S(1)}, f32[2,512,128]{2,1,0:T(8,128)S(1)}, f32[5,512,128]{2,1,0:T(8,128)}) custom-call(s32[5]{0:T(128)S(1)} %stack.23.at, bf16[1024,1024]{1,0:T(8,128)(2,1)} %act.7, bf16[3,1024,1024]{2,1,0:T(8,128)(2,1)} %bitcast.11, ...), custom_call_target="tpu_custom_call" | custom-call | tf_op jit(solution)/shard_map/second_kernel/pallas_call | solution.py:135
  17.0 1.5 %collective-permute-done.refs_0_ = f32[2,512,128]{2,1,0:T(8,128)S(1)} collective-permute-done((f32[2,512,128]{2,1,0:T(8,128)S(1)}, f32[2,512,128]{2,1,0:T(8,128)S(1)}, u32[]{:S(2)}, u32[]{:S(2)}) %collective-permute-start) | collective-permute-done | bytes 524320 | tf_op jit(solution)/shard_map/ppermute | solution.py:26
  18.5 1.6 %collective-permute-done.2.refs_2_ = f32[2,512,128]{2,1,0:T(8,128)S(1)} collective-permute-done((f32[2,512,128]{2,1,0:T(8,128)S(1)}, f32[2,512,128]{2,1,0:T(8,128)S(1)}, u32[]{:S(2)}, u32[]{:S(2)}) %collective-permute-start.2) | collective-permute-done | bytes 524320 | tf_op jit(solution)/shard_map/ppermute | solution.py:30
  20.1 1.4 first_sum_kernel.2
  21.5 2.7 %collective-permute-start.4 = (f32[3,512,128]{2,1,0:T(8,128)}, f32[3,512,128]{2,1,0:T(8,128)}, u32[]{:S(2)}, u32[]{:S(2)}) collective-permute-start(f32[3,512,128]{2,1,0:T(8,128)} %get-tuple-element.51), channel_id=1, source_target_pairs={{0,6},{1,7},{2,0},{3,1},{4,2},{5,3},{6,4},{7,5},{8,14},{9,15},{10,... | collective-permute-start | bytes 2359304 | tf_op jit(solution)/shard_map/ppermute | solution.py:26
  24.2 2.7 %collective-permute-start.7 = (f32[2,512,128]{2,1,0:T(8,128)}, f32[2,512,128]{2,1,0:T(8,128)}, u32[]{:S(2)}, u32[]{:S(2)}) collective-permute-start(f32[2,512,128]{2,1,0:T(8,128)} %get-tuple-element.55), channel_id=1, source_target_pairs={{0,6},{1,7},{2,0},{3,1},{4,2},{5,3},{6,4},{7,5},{8,14},{9,15},{10,... | collective-permute-start | bytes 1572872 | tf_op jit(solution)/shard_map/ppermute | solution.py:26
  26.9 1.1 taps_turn_kernel.1
  28.0 12.4 %all-to-all-start = ((f32[16,8,8,128]{3,2,1,0:T(8,128)}), f32[16,8,8,128]{3,2,1,0:T(8,128)S(1)}, u32[]{:S(2)}, u32[]{:S(2)}) async-start(f32[16,8,8,128]{3,2,1,0:T(8,128)} %bitcast.15), calls=%async_computation | async-start | bytes 1048576 | tf_op jit(solution)/shard_map/all_to_all | solution.py:508
  40.4 6.9 %third_kernel.1 = (f32[6,512,128]{2,1,0:T(8,128)S(1)}, f32[1,512,128]{2,1,0:T(8,128)S(1)}, f32[2,512,128]{2,1,0:T(8,128)S(1)}, f32[2,512,128]{2,1,0:T(8,128)S(1)}) custom-call(s32[5]{0:T(128)S(1)} %stack.23.at, bf16[1024,1024]{1,0:T(8,128)(2,1)} %act.7, bf16[3,1024,1024]{2,1,0:T(8,128)(2,1)} %bitcast.12, f32[3,512,128]{2,1,0:T(8,128)} %get-tuple-element.50.refs_0_.refs_1_), custom_call_target="tpu_custom_call" | custom-call | tf_op jit(solution)/shard_map/third_kernel/pallas_call | solution.py:135
  47.3 2.6 %collective-permute-done.6.refs_0_ = f32[2,512,128]{2,1,0:T(8,128)} collective-permute-done((f32[2,512,128]{2,1,0:T(8,128)}, f32[2,512,128]{2,1,0:T(8,128)}, u32[]{:S(2)}, u32[]{:S(2)}) %collective-permute-start.6) | collective-permute-done | bytes 524320 | tf_op jit(solution)/shard_map/ppermute | solution.py:26
  49.9 1.4 kv_near_kernel.1
  51.3 0.8 copy-done.4
  52.1 9.7 %query_project_kernel.1 = (f32[4,256,128]{2,1,0:T(8,128)}, f32[4,256,128]{2,1,0:T(8,128)}, f32[2,256,128]{2,1,0:T(8,128)}, f32[2,256,128]{2,1,0:T(8,128)}, f32[3...) custom-call(s32[5]{0:T(128)S(1)} %stack.23.at, ...), custom_call_target="tpu_custom_call" | custom-call | tf_op jit(solution)/shard_map/query_project_kernel/pallas_call | solution.py:135
  61.8 0.8 copy-done.1
  62.7 1.0 copy-done.5
  63.7 0.9 copy-done.8
  64.7 1.7 %kv_second_sum_kernel.1 = (f32[2,512,128]{2,1,0:T(8,128)S(1)}, f32[2,512,128]{2,1,0:T(8,128)S(1)}, f32[3,512,128]{2,1,0:T(8,128)S(1)}) custom-call(f32[3,512,128]{2,1,0:T(8,128)} %collective-permute-done.3.refs_0_, f32[3,512,128]{2,1,0:T(8,128)} %collective-permute-done.4.refs_1_, f32[5,512,128]{2,1,0:T(8,128)S(1)} %collective-permute-done.5.refs_2_, ...), custom_call_target="tpu_custom_call" | custom-call | tf_op jit(solution)/shard_map/kv_second_sum_kernel/pallas_call | solution.py:162
  66.4 0.7 collective-permute-start.10
  67.1 2.7 %collective-permute-start.9 = (f32[2,512,128]{2,1,0:T(8,128)S(1)}, f32[2,512,128]{2,1,0:T(8,128)S(1)}, u32[]{:S(2)}, u32[]{:S(2)}) collective-permute-start(f32[2,512,128]{2,1,0:T(8,128)S(1)} %get-tuple-element.64), channel_id=1, source_target_pairs={{0,6},{1,7},{2,0},{3,1},{4,2},{5,3},{6,4},{7,5},{8,14},{9,15},{10,... | collective-permute-start | bytes 1572872 | tf_op jit(solution)/shard_map/ppermute | solution.py:26
  69.8 2.7 %collective-permute-start.12 = (f32[4,256,128]{2,1,0:T(8,128)}, f32[4,256,128]{2,1,0:T(8,128)}, u32[]{:S(2)}, u32[]{:S(2)}) collective-permute-start(f32[4,256,128]{2,1,0:T(8,128)} %get-tuple-element.67), channel_id=1, source_target_pairs={{0,6},{1,7},{2,0},{3,1},{4,2},{5,3},{6,4},{7,5},{8,14},{9,15},{10,... | collective-permute-start | bytes 1572872 | tf_op jit(solution)/shard_map/ppermute | solution.py:26
  72.4 3.9 %collective-permute-done.8.refs_1_ = f32[2,512,128]{2,1,0:T(8,128)S(1)} collective-permute-done((f32[2,512,128]{2,1,0:T(8,128)S(1)}, f32[2,512,128]{2,1,0:T(8,128)S(1)}, u32[]{:S(2)}, u32[]{:S(2)}) %collective-permute-start.8) | collective-permute-done | bytes 524320 | tf_op jit(solution)/shard_map/ppermute | solution.py:26
  76.3 1.6 %collective-permute-start.13 = (f32[3,256,128]{2,1,0:T(8,128)}, f32[3,256,128]{2,1,0:T(8,128)}, u32[]{:S(2)}, u32[]{:S(2)}) collective-permute-start(f32[3,256,128]{2,1,0:T(8,128)} %get-tuple-element.68), channel_id=1, source_target_pairs={{0,1},{1,0},{2,3},{3,2},{4,5},{5,4},{6,7},{7,6},{8,9},{9,8},{10,11... | collective-permute-start | bytes 1179656 | tf_op jit(solution)/shard_map/ppermute | solution.py:30
  77.9 1.5 %kv_beside_kernel.1 = (f32[2,512,128]{2,1,0:T(8,128)S(1)}, f32[2,512,128]{2,1,0:T(8,128)S(1)}) custom-call(f32[3,512,128]{2,1,0:T(8,128)} %collective-permute-done.3.refs_0_, f32[3,512,128]{2,1,0:T(8,128)} %collective-permute-done.4.refs_1_, f32[5,512,128]{2,1,0:T(8,128)S(1)} %collective-permute-done.5.refs_2_, ...), custom_call_target="tpu_custom_call" | custom-call | tf_op jit(solution)/shard_map/kv_beside_kernel/pallas_call | solution.py:162
  79.5 2.2 %taps_kernel.1.refs_5_.refs_1_ = f32[1024,256]{1,0:T(8,128)S(1)} custom-call(f32[16,8,8,128]{3,2,1,0:T(8,128)S(1)} %all-to-all-done.refs_6_.refs_0_, bf16[256,128]{1,0:T(8,128)(2,1)} %constant.72.clone.refs_1_.refs_2_, bf16[256,128]{1,0:T(8,128)(2,1)} %constant.73.clone.refs_2_.refs_3_, f32[128,128]{1,0:T(8,128)} %constant.74.clone.refs_3_.refs_4_, ...), custom_call_target="tpu_custom_call" | custom-call | tf_op jit(solution)/shard_map/taps_kernel/pallas_call | solution.py:491
  81.7 1.2 kv_kernel.1
  82.9 18.2 %all-to-all-start.1 = ((f32[16,8,8,128]{3,2,1,0:T(8,128)}), f32[16,8,8,128]{3,2,1,0:T(8,128)S(1)}, u32[]{:S(2)}, u32[]{:S(2)}) async-start(f32[16,8,8,128]{3,2,1,0:T(8,128)} %bitcast.14), calls=%async_computation.1 | async-start | bytes 1048576 | tf_op jit(solution)/shard_map/all_to_all | solution.py:508
  101.1 1.9 %first_sum_kernel.3 = (f32[3,256,128]{2,1,0:T(8,128)S(1)}, f32[3,256,128]{2,1,0:T(8,128)S(1)}) custom-call(f32[4,256,128]{2,1,0:T(8,128)} %collective-permute-done.11.refs_0_.refs_2_, f32[4,256,128]{2,1,0:T(8,128)} %collective-permute-done.12.refs_1_.refs_3_, f32[3,256,128]{2,1,0:T(8,128)} %collective-permute-done.13.refs_2_.refs_4_, ...), custom_call_target="tpu_custom_call" | custom-call | tf_op jit(solution)/shard_map/first_sum_kernel/pallas_call | solution.py:162
  103.1 0.1 collective-permute-start.14
  103.2 2.7 %collective-permute-start.15 = (f32[3,256,128]{2,1,0:T(8,128)S(1)}, f32[3,256,128]{2,1,0:T(8,128)S(1)}, u32[]{:S(2)}, u32[]{:S(2)}) collective-permute-start(f32[3,256,128]{2,1,0:T(8,128)S(1)} %get-tuple-element.73), channel_id=1, source_target_pairs={{0,6},{1,7},{2,0},{3,1},{4,2},{5,3},{6,4},{7,5},{8,14},{9,15},{10,... | collective-permute-start | bytes 1179656 | tf_op jit(solution)/shard_map/ppermute | solution.py:26
  105.8 0.8 collective-permute-start.17
  106.6 5.6 %all-to-all-done.1.refs_0_ = f32[16,8,8,128]{3,2,1,0:T(8,128)S(1)} async-done(((f32[16,8,8,128]{3,2,1,0:T(8,128)}), f32[16,8,8,128]{3,2,1,0:T(8,128)S(1)}, u32[]{:S(2)}, u32[]{:S(2)}) %all-to-all-start.1) | async-done | bytes 524320 | tf_op jit(solution)/shard_map/all_to_all | solution.py:508
  112.2 4.4 %conv_kernel.1 = f32[16,8,8,128]{3,2,1,0:T(8,128)} custom-call(f32[16,8,8,128]{3,2,1,0:T(8,128)S(1)} %all-to-all-done.1.refs_0_, f32[1024,256]{1,0:T(8,128)S(1)} %taps_kernel.1.refs_5_.refs_1_, bf16[256,128]{1,0:T(8,128)(2,1)} %constant.72.clone.refs_1_.refs_2_, bf16[256,128]{1,0:T(8,128)(2,1)} %constant.73.clone.refs_2_.refs_3_, ...), custom_call_target="tpu_custom_call" | custom-call | tf_op jit(solution)/shard_map/conv_kernel/pallas_call | solution.py:491
  116.7 4.7 %all-to-all-start.2 = ((f32[16,8,8,128]{3,2,1,0:T(8,128)}), f32[16,8,8,128]{3,2,1,0:T(8,128)S(1)}, u32[]{:S(2)}, u32[]{:S(2)}) async-start(f32[16,8,8,128]{3,2,1,0:T(8,128)} %conv_kernel.1), calls=%async_computation.2 | async-start | bytes 1048576 | tf_op jit(solution)/shard_map/all_to_all | solution.py:508
  121.3 0.8 collective-permute-start.16
  122.2 1.8 %query_second_sum_kernel.1 = (f32[2,256,128]{2,1,0:T(8,128)S(1)}, f32[2,256,128]{2,1,0:T(8,128)S(1)}, f32[2,256,128]{2,1,0:T(8,128)S(1)}) custom-call(f32[3,256,128]{2,1,0:T(8,128)S(1)} %collective-permute-done.14.refs_0_, f32[3,256,128]{2,1,0:T(8,128)S(1)} %collective-permute-done.15.refs_1_, f32[4,256,128]{2,1,0:T(8,128)} %collective-permute-done.11.refs_0_.refs_2_, ...), custom_call_target="tpu_custom_call" | custom-call | tf_op jit(solution)/shard_map/query_second_sum_kernel/pallas_call | solution.py:162
  124.0 0.1 collective-permute-start.18
  124.1 2.7 %collective-permute-start.19 = (f32[2,256,128]{2,1,0:T(8,128)S(1)}, f32[2,256,128]{2,1,0:T(8,128)S(1)}, u32[]{:S(2)}, u32[]{:S(2)}) collective-permute-start(f32[2,256,128]{2,1,0:T(8,128)S(1)} %get-tuple-element.80), channel_id=1, source_target_pairs={{0,6},{1,7},{2,0},{3,1},{4,2},{5,3},{6,4},{7,5},{8,14},{9,15},{10,... | collective-permute-start | bytes 786440 | tf_op jit(solution)/shard_map/ppermute | solution.py:26
  126.7 0.7 collective-permute-start.20
  127.5 7.0 %collective-permute-done.16.refs_4_ = f32[2,256,128]{2,1,0:T(8,128)S(1)} collective-permute-done((f32[2,256,128]{2,1,0:T(8,128)}, f32[2,256,128]{2,1,0:T(8,128)S(1)}, u32[]{:S(2)}, u32[]{:S(2)}) %collective-permute-start.16) | collective-permute-done | bytes 262176 | tf_op jit(solution)/shard_map/ppermute | solution.py:30
  134.4 1.6 %query_beside_kernel.1 = (f32[2,256,128]{2,1,0:T(8,128)S(1)}, f32[2,256,128]{2,1,0:T(8,128)S(1)}) custom-call(f32[3,256,128]{2,1,0:T(8,128)S(1)} %collective-permute-done.14.refs_0_, f32[3,256,128]{2,1,0:T(8,128)S(1)} %collective-permute-done.15.refs_1_, f32[4,256,128]{2,1,0:T(8,128)} %collective-permute-done.11.refs_0_.refs_2_, ...), custom_call_target="tpu_custom_call" | custom-call | tf_op jit(solution)/shard_map/query_beside_kernel/pallas_call | solution.py:162
  136.1 4.0 %collective-permute-done.20.refs_4_ = f32[2,256,128]{2,1,0:T(8,128)S(1)} collective-permute-done((f32[2,256,128]{2,1,0:T(8,128)S(1)}, f32[2,256,128]{2,1,0:T(8,128)S(1)}, u32[]{:S(2)}, u32[]{:S(2)}) %collective-permute-start.20) | collective-permute-done | bytes 262176 | tf_op jit(solution)/shard_map/ppermute | solution.py:30
  140.0 0.1 query_kernel.1.refs_1_
  140.1 1.1 gate_kernel.1
  (38 shorter events, 0.1 us)
Async XLA Ops:
  3.9 14.6 %collective-permute-start = (f32[2,512,128]{2,1,0:T(8,128)S(1)}, f32[2,512,128]{2,1,0:T(8,128)S(1)}, u32[]{:S(2)}, u32[]{:S(2)}) collective-permute-start(f32[2,512,128]{2,1,0:T(8,128)S(1)} %get-tuple-element.44), channel_id=1, source_target_pairs={{0,2},{1,3},{2,4},{3,5},{4,6},{5,7},{6,0},{7,1},{8,10},{9,11},{10,... | collective-permute-start | bytes 1572872 | tf_op jit(solution)/shard_map/ppermute | solution.py:26
  6.0 12.5 %collective-permute-start.1 = (f32[2,512,128]{2,1,0:T(8,128)S(1)}, f32[2,512,128]{2,1,0:T(8,128)S(1)}, u32[]{:S(2)}, u32[]{:S(2)}) collective-permute-start(f32[2,512,128]{2,1,0:T(8,128)S(1)} %get-tuple-element.45), channel_id=1, source_target_pairs={{0,6},{1,7},{2,0},{3,1},{4,2},{5,3},{6,4},{7,5},{8,14},{9,15},{10,... | collective-permute-start | bytes 1572872 | tf_op jit(solution)/shard_map/ppermute | solution.py:26
  7.4 12.7 %collective-permute-start.2 = (f32[2,512,128]{2,1,0:T(8,128)S(1)}, f32[2,512,128]{2,1,0:T(8,128)S(1)}, u32[]{:S(2)}, u32[]{:S(2)}) collective-permute-start(f32[2,512,128]{2,1,0:T(8,128)S(1)} %get-tuple-element.46), channel_id=1, source_target_pairs={{0,1},{1,0},{2,3},{3,2},{4,5},{5,4},{6,7},{7,6},{8,9},{9,8},{10,11... | collective-permute-start | bytes 1572872 | tf_op jit(solution)/shard_map/ppermute | solution.py:30
  17.0 45.6 %collective-permute-start.5 = (f32[5,512,128]{2,1,0:T(8,128)}, f32[5,512,128]{2,1,0:T(8,128)S(1)}, u32[]{:S(2)}, u32[]{:S(2)}) collective-permute-start(f32[5,512,128]{2,1,0:T(8,128)} %get-tuple-element.52), channel_id=1, source_target_pairs={{0,1},{1,0},{2,3},{3,2},{4,5},{5,4},{6,7},{7,6},{8,9},{9,8},{10,11... | collective-permute-start | bytes 3932168 | tf_op jit(solution)/shard_map/ppermute | solution.py:30
  20.1 6.7 %copy-start.3 = (f32[1024,128]{1,0:T(8,128)S(1)}, f32[1024,128]{1,0:T(8,128)}, u32[]{:S(2)}) copy-start(f32[1024,128]{1,0:T(8,128)} %refs_0_.1) | copy-start | bytes 1572868
  21.5 41.1 %collective-permute-start.3 = (f32[3,512,128]{2,1,0:T(8,128)}, f32[3,512,128]{2,1,0:T(8,128)}, u32[]{:S(2)}, u32[]{:S(2)}) collective-permute-start(f32[3,512,128]{2,1,0:T(8,128)} %get-tuple-element.50.refs_0_.refs_1_), channel_id=1, source_target_pairs={{0,2},{1,3},{2,4},{3,5},{4,6},{5,7},{6,0},{7,1},{8,10},{9,11},{10,... | collective-permute-start | bytes 2359304 | tf_op jit(solution)/shard_map/ppermute | solution.py:26
  21.5 41.1 %collective-permute-start.4 = (f32[3,512,128]{2,1,0:T(8,128)}, f32[3,512,128]{2,1,0:T(8,128)}, u32[]{:S(2)}, u32[]{:S(2)}) collective-permute-start(f32[3,512,128]{2,1,0:T(8,128)} %get-tuple-element.51), channel_id=1, source_target_pairs={{0,6},{1,7},{2,0},{3,1},{4,2},{5,3},{6,4},{7,5},{8,14},{9,15},{10,... | collective-permute-start | bytes 2359304 | tf_op jit(solution)/shard_map/ppermute | solution.py:26
  24.2 25.7 %collective-permute-start.6 = (f32[2,512,128]{2,1,0:T(8,128)}, f32[2,512,128]{2,1,0:T(8,128)}, u32[]{:S(2)}, u32[]{:S(2)}) collective-permute-start(f32[2,512,128]{2,1,0:T(8,128)} %get-tuple-element.54), channel_id=1, source_target_pairs={{0,2},{1,3},{2,4},{3,5},{4,6},{5,7},{6,0},{7,1},{8,10},{9,11},{10,... | collective-permute-start | bytes 1572872 | tf_op jit(solution)/shard_map/ppermute | solution.py:26
  24.2 25.7 %collective-permute-start.7 = (f32[2,512,128]{2,1,0:T(8,128)}, f32[2,512,128]{2,1,0:T(8,128)}, u32[]{:S(2)}, u32[]{:S(2)}) collective-permute-start(f32[2,512,128]{2,1,0:T(8,128)} %get-tuple-element.55), channel_id=1, source_target_pairs={{0,6},{1,7},{2,0},{3,1},{4,2},{5,3},{6,4},{7,5},{8,14},{9,15},{10,... | collective-permute-start | bytes 1572872 | tf_op jit(solution)/shard_map/ppermute | solution.py:26
  28.0 34.6 %all-to-all-start = ((f32[16,8,8,128]{3,2,1,0:T(8,128)}), f32[16,8,8,128]{3,2,1,0:T(8,128)S(1)}, u32[]{:S(2)}, u32[]{:S(2)}) async-start(f32[16,8,8,128]{3,2,1,0:T(8,128)} %bitcast.15), calls=%async_computation | async-start | bytes 1048576 | tf_op jit(solution)/shard_map/all_to_all | solution.py:508
  47.3 4.8 %copy-start.7 = (f32[1,512,128]{2,1,0:T(8,128)}, f32[1,512,128]{2,1,0:T(8,128)S(1)}, u32[]{:S(2)}) copy-start(f32[1,512,128]{2,1,0:T(8,128)S(1)} %get-tuple-element.60.refs_5_) | copy-start | bytes 786436
  51.3 0.8 copy-start.4
  61.8 0.8 copy-start.1
  62.7 1.0 copy-start.5
  63.7 0.9 copy-start.8
  64.6 13.3 %copy-start.2 = (f32[2,512,128]{2,1,0:T(8,128)S(1)}, f32[2,512,128]{2,1,0:T(8,128)}, u32[]{:S(2)}) copy-start(f32[2,512,128]{2,1,0:T(8,128)} %copy-done.1) | copy-start | bytes 1572868
  66.3 13.1 %copy-start = (f32[2,512,128]{2,1,0:T(8,128)}, f32[2,512,128]{2,1,0:T(8,128)S(1)}, u32[]{:S(2)}) copy-start(f32[2,512,128]{2,1,0:T(8,128)S(1)} %get-tuple-element.62.refs_5_.refs_7_.refs_1_) | copy-start | bytes 1572868
  66.4 15.3 %collective-permute-start.10 = (f32[3,512,128]{2,1,0:T(8,128)S(1)}, f32[3,512,128]{2,1,0:T(8,128)S(1)}, u32[]{:S(2)}, u32[]{:S(2)}) collective-permute-start(f32[3,512,128]{2,1,0:T(8,128)S(1)} %get-tuple-element.66), channel_id=1, source_target_pairs={{0,1},{1,0},{2,3},{3,2},{4,5},{5,4},{6,7},{7,6},{8,9},{9,8},{10,11... | collective-permute-start | bytes 2359304 | tf_op jit(solution)/shard_map/ppermute | solution.py:30
  67.1 9.2 %collective-permute-start.8 = (f32[2,512,128]{2,1,0:T(8,128)S(1)}, f32[2,512,128]{2,1,0:T(8,128)S(1)}, u32[]{:S(2)}, u32[]{:S(2)}) collective-permute-start(f32[2,512,128]{2,1,0:T(8,128)S(1)} %get-tuple-element.62.refs_5_.refs_7_.refs_1_), channel_id=1, source_target_pairs={{0,2},{1,3},{2,4},{3,5},{4,6},{5,7},{6,0},{7,1},{8,10},{9,11},{10,... | collective-permute-start | bytes 1572872 | tf_op jit(solution)/shard_map/ppermute | solution.py:26
  67.1 14.6 %collective-permute-start.9 = (f32[2,512,128]{2,1,0:T(8,128)S(1)}, f32[2,512,128]{2,1,0:T(8,128)S(1)}, u32[]{:S(2)}, u32[]{:S(2)}) collective-permute-start(f32[2,512,128]{2,1,0:T(8,128)S(1)} %get-tuple-element.64), channel_id=1, source_target_pairs={{0,6},{1,7},{2,0},{3,1},{4,2},{5,3},{6,4},{7,5},{8,14},{9,15},{10,... | collective-permute-start | bytes 1572872 | tf_op jit(solution)/shard_map/ppermute | solution.py:26
  69.8 31.3 %collective-permute-start.11 = (f32[4,256,128]{2,1,0:T(8,128)}, f32[4,256,128]{2,1,0:T(8,128)}, u32[]{:S(2)}, u32[]{:S(2)}) collective-permute-start(f32[4,256,128]{2,1,0:T(8,128)} %get-tuple-element.61.refs_7_), channel_id=1, source_target_pairs={{0,2},{1,3},{2,4},{3,5},{4,6},{5,7},{6,0},{7,1},{8,10},{9,11},{10,... | collective-permute-start | bytes 1572872 | tf_op jit(solution)/shard_map/ppermute | solution.py:26
  69.8 31.3 %collective-permute-start.12 = (f32[4,256,128]{2,1,0:T(8,128)}, f32[4,256,128]{2,1,0:T(8,128)}, u32[]{:S(2)}, u32[]{:S(2)}) collective-permute-start(f32[4,256,128]{2,1,0:T(8,128)} %get-tuple-element.67), channel_id=1, source_target_pairs={{0,6},{1,7},{2,0},{3,1},{4,2},{5,3},{6,4},{7,5},{8,14},{9,15},{10,... | collective-permute-start | bytes 1572872 | tf_op jit(solution)/shard_map/ppermute | solution.py:26
  76.3 24.8 %collective-permute-start.13 = (f32[3,256,128]{2,1,0:T(8,128)}, f32[3,256,128]{2,1,0:T(8,128)}, u32[]{:S(2)}, u32[]{:S(2)}) collective-permute-start(f32[3,256,128]{2,1,0:T(8,128)} %get-tuple-element.68), channel_id=1, source_target_pairs={{0,1},{1,0},{2,3},{3,2},{4,5},{5,4},{6,7},{7,6},{8,9},{9,8},{10,11... | collective-permute-start | bytes 1179656 | tf_op jit(solution)/shard_map/ppermute | solution.py:30
  82.9 29.4 %all-to-all-start.1 = ((f32[16,8,8,128]{3,2,1,0:T(8,128)}), f32[16,8,8,128]{3,2,1,0:T(8,128)S(1)}, u32[]{:S(2)}, u32[]{:S(2)}) async-start(f32[16,8,8,128]{3,2,1,0:T(8,128)} %bitcast.14), calls=%async_computation.1 | async-start | bytes 1048576 | tf_op jit(solution)/shard_map/all_to_all | solution.py:508
  103.1 13.6 %copy-start.6 = (f32[3,256,128]{2,1,0:T(8,128)}, f32[3,256,128]{2,1,0:T(8,128)S(1)}, u32[]{:S(2)}) copy-start(f32[3,256,128]{2,1,0:T(8,128)S(1)} %get-tuple-element.72.refs_1_) | copy-start | bytes 1179652
  103.1 19.1 %collective-permute-start.14 = (f32[3,256,128]{2,1,0:T(8,128)S(1)}, f32[3,256,128]{2,1,0:T(8,128)S(1)}, u32[]{:S(2)}, u32[]{:S(2)}) collective-permute-start(f32[3,256,128]{2,1,0:T(8,128)S(1)} %get-tuple-element.72.refs_1_), channel_id=1, source_target_pairs={{0,2},{1,3},{2,4},{3,5},{4,6},{5,7},{6,0},{7,1},{8,10},{9,11},{10,... | collective-permute-start | bytes 1179656 | tf_op jit(solution)/shard_map/ppermute | solution.py:26
  103.2 19.0 %collective-permute-start.15 = (f32[3,256,128]{2,1,0:T(8,128)S(1)}, f32[3,256,128]{2,1,0:T(8,128)S(1)}, u32[]{:S(2)}, u32[]{:S(2)}) collective-permute-start(f32[3,256,128]{2,1,0:T(8,128)S(1)} %get-tuple-element.73), channel_id=1, source_target_pairs={{0,6},{1,7},{2,0},{3,1},{4,2},{5,3},{6,4},{7,5},{8,14},{9,15},{10,... | collective-permute-start | bytes 1179656 | tf_op jit(solution)/shard_map/ppermute | solution.py:26
  105.8 16.3 %collective-permute-start.17 = (f32[3,256,128]{2,1,0:T(8,128)}, f32[3,256,128]{2,1,0:T(8,128)S(1)}, u32[]{:S(2)}, u32[]{:S(2)}) collective-permute-start(f32[3,256,128]{2,1,0:T(8,128)} %release.3), channel_id=1, source_target_pairs={{0,1},{1,0},{2,3},{3,2},{4,5},{5,4},{6,7},{7,6},{8,9},{9,8},{10,11... | collective-permute-start | bytes 1179656 | tf_op jit(solution)/shard_map/ppermute | solution.py:30
  116.7 23.5 %all-to-all-start.2 = ((f32[16,8,8,128]{3,2,1,0:T(8,128)}), f32[16,8,8,128]{3,2,1,0:T(8,128)S(1)}, u32[]{:S(2)}, u32[]{:S(2)}) async-start(f32[16,8,8,128]{3,2,1,0:T(8,128)} %conv_kernel.1), calls=%async_computation.2 | async-start | bytes 1048576 | tf_op jit(solution)/shard_map/all_to_all | solution.py:508
  121.3 13.1 %collective-permute-start.16 = (f32[2,256,128]{2,1,0:T(8,128)}, f32[2,256,128]{2,1,0:T(8,128)S(1)}, u32[]{:S(2)}, u32[]{:S(2)}) collective-permute-start(f32[2,256,128]{2,1,0:T(8,128)} %release.2), channel_id=1, source_target_pairs={{0,1},{1,0},{2,3},{3,2},{4,5},{5,4},{6,7},{7,6},{8,9},{9,8},{10,11... | collective-permute-start | bytes 786440 | tf_op jit(solution)/shard_map/ppermute | solution.py:30
  124.0 12.1 %collective-permute-start.18 = (f32[2,256,128]{2,1,0:T(8,128)S(1)}, f32[2,256,128]{2,1,0:T(8,128)S(1)}, u32[]{:S(2)}, u32[]{:S(2)}) collective-permute-start(f32[2,256,128]{2,1,0:T(8,128)S(1)} %get-tuple-element.78.refs_7_), channel_id=1, source_target_pairs={{0,2},{1,3},{2,4},{3,5},{4,6},{5,7},{6,0},{7,1},{8,10},{9,11},{10,... | collective-permute-start | bytes 786440 | tf_op jit(solution)/shard_map/ppermute | solution.py:26
  124.1 12.0 %collective-permute-start.19 = (f32[2,256,128]{2,1,0:T(8,128)S(1)}, f32[2,256,128]{2,1,0:T(8,128)S(1)}, u32[]{:S(2)}, u32[]{:S(2)}) collective-permute-start(f32[2,256,128]{2,1,0:T(8,128)S(1)} %get-tuple-element.80), channel_id=1, source_target_pairs={{0,6},{1,7},{2,0},{3,1},{4,2},{5,3},{6,4},{7,5},{8,14},{9,15},{10,... | collective-permute-start | bytes 786440 | tf_op jit(solution)/shard_map/ppermute | solution.py:26
  126.7 13.3 %collective-permute-start.20 = (f32[2,256,128]{2,1,0:T(8,128)S(1)}, f32[2,256,128]{2,1,0:T(8,128)S(1)}, u32[]{:S(2)}, u32[]{:S(2)}) collective-permute-start(f32[2,256,128]{2,1,0:T(8,128)S(1)} %get-tuple-element.82), channel_id=1, source_target_pairs={{0,1},{1,0},{2,3},{3,2},{4,5},{5,4},{6,7},{7,6},{8,9},{9,8},{10,11... | collective-permute-start | bytes 786440 | tf_op jit(solution)/shard_map/ppermute | solution.py:30

commit v7 on v6

--- a/solution.py
+++ b/solution.py
@@ -75,12 +75,12 @@
 
 
 def second_kernel(halves, place, act, weight, outs):
-    near_r, near_l, keep_r, keep_l, z_send = outs
+    next_r, next_l, z_send = outs
     x_outs = (
-        ((keep_r, 0), (keep_r, 1)),
-        ((near_r, 0), (near_r, 1)),
-        ((near_l, 0), (near_l, 1)),
-        ((keep_l, 0), (keep_l, 1)),
+        ((next_r, 2), (next_r, 3)),
+        ((next_r, 0), (next_r, 1)),
+        ((next_l, 0), (next_l, 1)),
+        ((next_l, 2), (next_l, 3)),
         (None, None),
     )
     for i, outs in enumerate(x_outs):
@@ -92,13 +92,13 @@
 
 
 def third_kernel(halves, place, act, weight, outs):
-    z_mine, z_late, x_other, x_mine = outs
+    (mine,) = outs
     for i in range(6):
-        x_outs = (None, None) if i < 4 else ((x_other, i - 4), (x_mine, i - 4))
-        z_other = (z_late, 0) if i == 5 else None
+        x_outs = (None, None) if i < 4 else ((mine, i + 3), (mine, i + 5))
+        z_other = (mine, 6) if i == 5 else None
         pl.when(pl.program_id(0) == i)(
             functools.partial(
-                halves.fill, place, act, weight, i % 2, x_outs, (z_other, (z_mine, i))
+                halves.fill, place, act, weight, i % 2, x_outs, (z_other, (mine, i))
             )
         )
 
@@ -167,7 +167,7 @@
         + [pl.BlockSpec(memory_space=pl.ANY)] * len(after),
         out_specs=[pl.BlockSpec(memory_space=pltpu.VMEM)] * len(counts),
         out_shape=[jax.ShapeDtypeStruct(halves.shape(count), jnp.float32) for count in counts],
-        compiler_params=params(16),
+        compiler_params=params(8),
         name=kernel.__name__,
     )(*near, *[in_hbm(value) for value in far], *after)
 
@@ -179,27 +179,30 @@
         out[2] = z_mine[half] + z_got[half]
 
 
-def kv_near_kernel(near_r, near_l, x_other, x_mine, out_other, out_mine):
-    for half, near in enumerate((near_l, near_r)):
-        out_other[half] = x_other[half] + near[0]
-        out_mine[half] = x_mine[half] + near[1]
-
-
-def kv_second_sum_kernel(dep_r, dep_l, z_got, z_mine, x_part, z_late, out_r, out_l, out_xz):
-    out_r[0] = z_mine[0] + z_got[0] + dep_r[2]
-    out_r[1] = z_mine[1] + z_got[1]
-    out_l[0] = z_mine[2] + z_got[2]
-    out_l[1] = z_mine[3] + z_got[3] + dep_l[2]
-    out_xz[0] = x_part[0] + dep_r[0]
-    out_xz[1] = x_part[1] + dep_l[0]
-    out_xz[2] = z_late[0]
-
-
-def kv_beside_kernel(dep_r, dep_l, z_got, z_mine, x_part, out_z, out_x):
-    out_z[0] = z_mine[4] + z_got[4]
-    out_z[1] = z_mine[5]
-    out_x[0] = x_part[0] + dep_r[1]
-    out_x[1] = x_part[1] + dep_l[1]
+def kv_first_sum_kernel(got_r, got_l, z_got, next_r, next_l, z_mine, out_r, out_l):
+    for half, (mine, got, out) in enumerate(((next_r, got_r, out_r), (next_l, got_l, out_l))):
+        out[0] = mine[0]
+        out[1] = mine[1]
+        out[2] = mine[2] + got[0]
+        out[3] = mine[3] + got[1]
+        out[4] = z_mine[half] + z_got[half]
+
+
+def kv_second_sum_kernel(next_r, next_l, z_got, mine, out_r, out_l, out_xz):
+    out_r[0] = mine[0] + z_got[0] + next_r[4]
+    out_r[1] = mine[1] + z_got[1]
+    out_l[0] = mine[2] + z_got[2]
+    out_l[1] = mine[3] + z_got[3] + next_l[4]
+    out_xz[0] = mine[7] + (next_r[2] + next_l[0])
+    out_xz[1] = mine[8] + (next_r[0] + next_l[2])
+    out_xz[2] = mine[6]
+
+
+def kv_beside_kernel(next_r, next_l, z_got, mine, out):
+    out[0] = mine[4] + z_got[4]
+    out[1] = mine[5]
+    out[2] = mine[9] + (next_r[3] + next_l[1])
+    out[3] = mine[10] + (next_r[1] + next_l[3])
 
 
 def release(values, after):
@@ -217,24 +220,36 @@
     )(*values, after)
 
 
-def query_project_kernel(halves, place, act, weight, outs):
-    send_r, send_l, keep_r, keep_l, z_send, z_next, z_late, z_mine, x_other, x_mine = outs
-    x_outs = (
-        ((send_r, 0), (send_r, 1)),
-        ((send_l, 0), (send_l, 1)),
-        ((keep_r, 0), (keep_r, 1)),
-        ((send_r, 2), (send_r, 3)),
-        ((send_l, 2), (send_l, 3)),
-        ((keep_l, 0), (keep_l, 1)),
-        ((x_other, 0), (x_mine, 0)),
-        ((x_other, 0), (x_mine, 0)),
-    )
-    for i, outs in enumerate(x_outs):
-        z_other = (z_send, z_next, z_late)[i // 3]
+def query_project_kernel(place, act, weight, *refs):
+    send_r, send_l, keep_r, keep_l, z_send, z_next, z_late, z_mine, x_other, x_mine, product = refs[
+        -11:
+    ]
+    product[...] = jnp.dot(act[...], weight[0], preferred_element_type=jnp.float32)
+
+    def put(owner, other, mine):
+        start = pl.multiple_of(place[owner] * 2 * BLOCK, 2 * BLOCK)
+        columns = product[:, pl.ds(start, 2 * BLOCK)]
+        low, high = columns[:, :BLOCK], columns[:, BLOCK:]
+        other[0][other[1]] = jnp.where(place[4] == 0, high, low)
+        mine[0][mine[1]] = jnp.where(place[4] == 0, low, high)
+
+    def z_step(half):
+        for owner in range(4):
+            piece = 2 * owner + half
+            put(owner, ((z_send, z_next, z_late)[piece // 3], piece % 3), (z_mine, piece))
+
+    def x_step(half):
+        far, right, left = (
+            ((send_r, 0), (keep_r, 0), (send_l, 2)),
+            ((send_l, 0), (send_r, 2), (keep_l, 0)),
+        )[half]
+        for owner, (ref, piece) in enumerate((far, right, left)):
+            put(owner, (ref, piece), (ref, piece + 1))
+        put(3, (x_other, half), (x_mine, half))
+
+    for i in range(4):
         pl.when(pl.program_id(0) == i)(
-            functools.partial(
-                halves.fill, place, act, weight, i % 2, outs, ((z_other, 0), (z_mine, 0))
-            )
+            functools.partial(z_step if i < 2 else x_step, i % 2)
         )
 
 
@@ -249,11 +264,11 @@
     out_x[1] = x_other[1] + (got_r[2] + dep_l[0])
 
 
-def query_beside_kernel(dep_r, dep_l, got_r, got_l, z_got, z_mine, x_mine, out_z, out_x):
-    out_z[0] = z_mine[6] + z_got[0]
-    out_z[1] = z_mine[7] + z_got[1]
-    out_x[0] = x_mine[0] + (dep_r[1] + got_l[3])
-    out_x[1] = x_mine[1] + (got_r[3] + dep_l[1])
+def query_beside_kernel(dep_r, dep_l, got_r, got_l, z_got, z_mine, x_mine, out):
+    out[0] = z_mine[6] + z_got[0]
+    out[1] = z_mine[7] + z_got[1]
+    out[2] = x_mine[0] + (dep_r[1] + got_l[3])
+    out[3] = x_mine[1] + (got_r[3] + dep_l[1])
 
 
 def reduce_kv(halves, place, activations, weight, beside):
@@ -264,68 +279,68 @@
         first_kernel, owner=0, steps=2, outs=[(2, "vmem")] * 4
     )
     got_r, got_l, z_got = shift_x(send_r, 1), shift_x(send_l, -1), swap_z(z_send)
-    near_r, near_l, keep_r, keep_l, z_send = make(
-        second_kernel,
-        owner=1,
-        steps=5,
-        outs=[(2, "vmem")] * 4 + [(5, "vmem")],
-        after=(z_mine,),
-    )
-    near_r, near_l, z_five = shift_x(near_r, 1), shift_x(near_l, -1), swap_z(z_send)
-    dep_r, dep_l = sum_call(
-        first_sum_kernel, halves, [3, 3], [got_r, got_l, z_got, keep_r, keep_l, z_mine], []
-    )
-    z_six, z_late, x_other, x_mine = make(
+    next_r, next_l, z_send = make(
+        second_kernel, owner=1, steps=5, outs=[(5, "vmem")] * 3, after=(z_mine,)
+    )
+    next_r, next_l = sum_call(
+        kv_first_sum_kernel, halves, [5, 5], [got_r, got_l, z_got, next_r, next_l, z_mine], []
+    )
+    ready = beside(next_r)
+    (mine,) = make(
         third_kernel,
         owner=1,
         steps=6,
-        outs=[(6, "vmem"), (1, "vmem"), (2, "vmem"), (2, "vmem")],
-        after=(dep_r,),
-    )
-    x_part_other, x_part_mine = sum_call(
-        kv_near_kernel, halves, [2, 2], [near_r, near_l, x_other, x_mine], []
-    )
-    ready = beside(dep_r, x_part_mine)
-    dep_r, dep_l = shift_x(dep_r, 1), shift_x(dep_l, -1)
+        outs=[(11, "vmem")],
+        after=(next_r,) + ready[1:],
+    )
+    next_r, next_l, z_five = shift_x(next_r, 1), shift_x(next_l, -1), swap_z(z_send)
     last_r, last_l, last_xz = sum_call(
         kv_second_sum_kernel,
         halves,
         [2, 2, 3],
-        [dep_r, dep_l, z_five, z_six, x_part_other, z_late],
+        [next_r, next_l, z_five, mine],
         [],
         after=ready,
     )
     last = last_r
-    z_part, x_part = sum_call(
+    (part,) = sum_call(
         kv_beside_kernel,
         halves,
-        [2, 2],
-        [dep_r, dep_l, z_five, z_six, x_part_mine],
+        [4],
+        [next_r, next_l, z_five, mine],
         [],
         after=(last,),
     )
     last_r, last_l, last_xz = shift_x(last_r, 1), shift_x(last_l, -1), swap_z(last_xz)
-    return (z_part, last_r, last_l, x_part, last_xz), last
+    return (part, last_r, last_l, last_xz), part
 
 
 def project_query(halves, place, activations, weight, after):
-    return project(
+    features, columns = weight.shape[1:]
+    shapes = [halves.shape(count) for count in (4, 4, 2, 2, 3, 3, 2, 8, 2, 2)]
+    return pl.pallas_call(
         query_project_kernel,
-        halves,
-        place,
-        activations,
-        weight,
-        0,
-        8,
-        [(4, "hbm")] * 2 + [(2, "hbm")] * 2 + [(3, 0), (3, 3), (2, 6), (8, 0), (2, 6), (2, 6)],
-        after=after,
-    )
+        grid_spec=pltpu.PrefetchScalarGridSpec(
+            num_scalar_prefetch=1,
+            grid=(4,),
+            in_specs=[
+                pl.BlockSpec((halves.rows, features), lambda i, at: (i, 0)),
+                pl.BlockSpec((1, features, columns), lambda i, at: (0, 0, 0)),
+                pl.BlockSpec(memory_space=pl.ANY),
+            ],
+            out_specs=[pl.BlockSpec(shape, lambda i, at: (0, 0, 0)) for shape in shapes],
+            scratch_shapes=[pltpu.VMEM((halves.rows, columns), jnp.float32)],
+        ),
+        out_shape=[pltpu.HBM(shape, jnp.float32) for shape in shapes],
+        compiler_params=params(24),
+        name="query_project_kernel",
+    )(place, activations, weight, after)
 
 
 def reduce_query(halves, projected, after):
     send_r, send_l, keep_r, keep_l, z_send, z_next, z_late, z_mine, x_other, x_mine = projected
+    send_r, send_l, z_send, z_next = release((send_r, send_l, z_send, z_next), after)
     got_r, got_l, z_got = shift_x(send_r, 1), shift_x(send_l, -1), swap_z(z_send)
-    (z_next,) = release((z_next,), after)
     z_next = swap_z(z_next)
     dep_r, dep_l = sum_call(
         first_sum_kernel,
@@ -343,23 +358,23 @@
         [dep_r, dep_l, got_r, got_l, z_got, z_next],
         [z_mine, x_other],
     )
-    z_part, x_part = sum_call(
+    (part,) = sum_call(
         query_beside_kernel,
         halves,
-        [2, 2],
+        [4],
         [dep_r, dep_l, got_r, got_l, late_got],
         [z_mine, x_mine],
         after=(last_r,),
     )
     last_r, last_l, x_sum = shift_x(last_r, 1), shift_x(last_l, -1), swap_z(x_sum)
-    return z_part, last_r, last_l, x_part, x_sum
-
-
-def summed(z_part, last_r, last_l, x_part, last_x):
-    z_total = [z_part[h] + (last_r[h] + last_l[h]) for h in range(2)]
+    return part, last_r, last_l, x_sum
+
+
+def summed(part, last_r, last_l, last_x):
+    z_total = [part[h] + (last_r[h] + last_l[h]) for h in range(2)]
     if last_x.shape[0] == 3:
         z_total[1] = z_total[1] + last_x[2]
-    return z_total + [x_part[h] + last_x[h] for h in range(2)]
+    return z_total + [part[2 + h] + last_x[h] for h in range(2)]
 
 
 def split_bf16(table):
@@ -528,19 +543,20 @@
     hold = {}
     kv_halves, q_halves = Halves(tokens, (1, 2)), Halves(tokens, (0,))
 
-    def prepare(ready, later):
+    def prepare(ready):
         taps = call(taps_turn_kernel, turned_shape, filter_taps, after=(ready,), to_hbm=True)
         hold["taps"] = exchange(taps.reshape(moved_shape))
-        hold["query"] = project_query(q_halves, place, activations, weight, (later,))
+        hold["query"] = project_query(q_halves, place, activations, weight, ready)
         return hold["taps"], hold["query"][0]
 
-    kv_parts, kv_last = reduce_kv(kv_halves, place, activations, weight, prepare)
+    kv_parts, kv_part = reduce_kv(kv_halves, place, activations, weight, prepare)
     spectrum = call(
         taps_kernel,
         (owned * length // BLOCK, 2 * BLOCK),
         hold["taps"],
         tables=first + turn + second,
-        after=(kv_last,),
+        after=(kv_part,),
+        to_hbm=True,
     )
     kv = call(
         kv_kernel,
@@ -550,14 +566,13 @@
         scratch=[pltpu.VMEM((tokens, channels), jnp.float32)],
         to_hbm=True,
     )
-    q_parts = reduce_query(q_halves, hold["query"], kv_last)
+    q_parts = reduce_query(q_halves, hold["query"], spectrum)
     moved = exchange(kv.reshape(moved_shape))
     convolved = call(
         conv_kernel,
         moved_shape,
         moved,
-        spectrum,
-        tables=first + turn + second + back + inverse,
+        tables=(spectrum,) + first + turn + second + back + inverse,
         to_hbm=True,
     )
     query = call(query_kernel, (tokens, channels), *q_parts)

time: 142 us -> 132 us (0.930)
  starting transfers between devices: 61.4 us -> 40.5 us
  waiting for transfers between devices: 26.2 us -> 36.8 us
  Pallas kernels: 49.8 us -> 52.4 us
  local copies, waits for them, and re-layouts: 3.69 us -> 1.14 us
    all_to_all x3, starting transfers between devices: 35.3 us -> 23.2 us  [exchange(): return lax.all_to_all(value, 'seq', split_axis=0, concat_axis=0, tiled=True)]
    pallas_call x4 -> x3, Pallas kernels: 28.4 us -> 18.2 us  [project(): pl.pallas_call(body, grid_spec=pltpu.PrefetchScalarGridSpec(num_scalar_pr...]
    ppermute x14 -> x12, starting transfers between devices: 19.7 us -> 11.7 us  [shift_x(): lax.ppermute(value, 'chan', [(i, (i + 2 * step) % 8) for i in range(8)])]
    pallas_call x0 -> x1, Pallas kernels: none -> 7.86 us  [project_query(): pl.pallas_call(query_project_kernel, grid_spec=pltpu.PrefetchScalarGridSp...]
    all_to_all x3, waiting for transfers between devices: 5.64 us -> 12.8 us  [exchange(): return lax.all_to_all(value, 'seq', split_axis=0, concat_axis=0, tiled=True)]
    ppermute x7, waiting for transfers between devices: 12.5 us -> 17.8 us  [swap_z(): return lax.ppermute(value, 'chan', [(i, i ^ 1) for i in range(8)])]
    pallas_call x6, Pallas kernels: 10.1 us -> 13.4 us  [call(): pl.pallas_call(body, grid=(1,), in_specs=[pl.BlockSpec(memory_space=pltpu...]
    unnamed x18 -> x12, local copies, waits for them, and re-layouts: 3.6 us -> 1.06 us
  transfers between devices with their start and end apart: 24 -> 22, of which waited for: 7 -> 9; matrix products, arithmetic and copies ran while one was open for 0% -> 0% of each run, Pallas kernels for 31% -> 33%
where the time goes in v7:
time: 132 us; the launch traced here: 131 us
  Pallas kernels  52.4 us (40%)
  starting transfers between devices  40.5 us (31%)
  waiting for transfers between devices  36.8 us (28%)
    all_to_all x3, starting transfers between devices, exchange(): return lax.all_to_all(value, 'seq', split_axis=0, concat_axis=0, tiled=True)  23.2 us
    pallas_call x3, Pallas kernels, project(): pl.pallas_call(body, grid_spec=pltpu.PrefetchScalarGridSpec(num_scalar_pr...  18.2 us
    ppermute x7, waiting for transfers between devices, swap_z(): return lax.ppermute(value, 'chan', [(i, i ^ 1) for i in range(8)])  17.8 us
    pallas_call x6, Pallas kernels, call(): pl.pallas_call(body, grid=(1,), in_specs=[pl.BlockSpec(memory_space=pltpu...  13.4 us
    pallas_call x6, Pallas kernels, sum_call(): pl.pallas_call(body, grid=(halves.rows // tile,), in_specs=[pl.BlockSpec(...  12.9 us
    all_to_all x3, waiting for transfers between devices, exchange(): return lax.all_to_all(value, 'seq', split_axis=0, concat_axis=0, tiled=True)  12.8 us
    ppermute x12, starting transfers between devices, shift_x(): lax.ppermute(value, 'chan', [(i, (i + 2 * step) % 8) for i in range(8)])  11.7 us
    pallas_call x1, Pallas kernels, project_query(): pl.pallas_call(query_project_kernel, grid_spec=pltpu.PrefetchScalarGridSp...  7.86 us
  transfers between devices with their start and end apart: 22, of which 9 were waited for; matrix products, arithmetic and copies ran while one was open for 0% of the time, Pallas kernels for 33%

profile of v7, /device:TPU:1, one launch (start us, length us, event | category | flops | bytes accessed | tf_op | source)
XLA Modules:
  0.0 131.1 jit_solution(9261259291034387170)
XLA Ops:
  0.0 0.1 stack.23.at.place
  0.1 3.8 %first_kernel.1 = (f32[2,512,128]{2,1,0:T(8,128)S(1)}, f32[2,512,128]{2,1,0:T(8,128)S(1)}, f32[2,512,128]{2,1,0:T(8,128)S(1)}, f32[2,512,128]{2,1,0:T(8,128)S(1)}) custom-call(s32[5]{0:T(128)S(1)} %stack.23.at.place, bf16[1024,1024]{1,0:T(8,128)(2,1)} %act.7, bf16[3,1024,1024]{2,1,0:T(8,128)(2,1)} %bitcast.10), custom_call_target="tpu_custom_call" | custom-call | tf_op jit(solution)/shard_map/first_kernel/pallas_call | solution.py:135
  3.9 2.1 %collective-permute-start = (f32[2,512,128]{2,1,0:T(8,128)S(1)}, f32[2,512,128]{2,1,0:T(8,128)S(1)}, u32[]{:S(2)}, u32[]{:S(2)}) collective-permute-start(f32[2,512,128]{2,1,0:T(8,128)S(1)} %get-tuple-element.36), channel_id=1, source_target_pairs={{0,2},{1,3},{2,4},{3,5},{4,6},{5,7},{6,0},{7,1},{8,10},{9,11},{10,... | collective-permute-start | bytes 1572872 | tf_op jit(solution)/shard_map/ppermute | solution.py:26
  6.0 1.4 %collective-permute-start.1 = (f32[2,512,128]{2,1,0:T(8,128)S(1)}, f32[2,512,128]{2,1,0:T(8,128)S(1)}, u32[]{:S(2)}, u32[]{:S(2)}) collective-permute-start(f32[2,512,128]{2,1,0:T(8,128)S(1)} %get-tuple-element.37), channel_id=1, source_target_pairs={{0,6},{1,7},{2,0},{3,1},{4,2},{5,3},{6,4},{7,5},{8,14},{9,15},{10,... | collective-permute-start | bytes 1572872 | tf_op jit(solution)/shard_map/ppermute | solution.py:26
  7.4 1.8 %collective-permute-start.2 = (f32[2,512,128]{2,1,0:T(8,128)S(1)}, f32[2,512,128]{2,1,0:T(8,128)S(1)}, u32[]{:S(2)}, u32[]{:S(2)}) collective-permute-start(f32[2,512,128]{2,1,0:T(8,128)S(1)} %get-tuple-element.38), channel_id=1, source_target_pairs={{0,1},{1,0},{2,3},{3,2},{4,5},{5,4},{6,7},{7,6},{8,9},{9,8},{10,11... | collective-permute-start | bytes 1572872 | tf_op jit(solution)/shard_map/ppermute | solution.py:30
  9.2 7.5 %second_kernel.1 = (f32[5,512,128]{2,1,0:T(8,128)S(1)}, f32[5,512,128]{2,1,0:T(8,128)S(1)}, f32[5,512,128]{2,1,0:T(8,128)}) custom-call(s32[5]{0:T(128)S(1)} %stack.23.at.place, bf16[1024,1024]{1,0:T(8,128)(2,1)} %act.7, bf16[3,1024,1024]{2,1,0:T(8,128)(2,1)} %bitcast.11, f32[2,512,128]{2,1,0:T(8,128)S(1)} %get-tuple-element.39.refs_0_.refs_5_), custom_call_target="tpu_custom_call" | custom-call | tf_op jit(solution)/shard_map/second_kernel/pallas_call | solution.py:135
  16.6 0.0 collective-permute-start.5
  16.6 1.9 %collective-permute-done.refs_0_ = f32[2,512,128]{2,1,0:T(8,128)S(1)} collective-permute-done((f32[2,512,128]{2,1,0:T(8,128)S(1)}, f32[2,512,128]{2,1,0:T(8,128)S(1)}, u32[]{:S(2)}, u32[]{:S(2)}) %collective-permute-start) | collective-permute-done | bytes 524320 | tf_op jit(solution)/shard_map/ppermute | solution.py:26
  18.5 1.6 %collective-permute-done.2.refs_2_ = f32[2,512,128]{2,1,0:T(8,128)S(1)} collective-permute-done((f32[2,512,128]{2,1,0:T(8,128)S(1)}, f32[2,512,128]{2,1,0:T(8,128)S(1)}, u32[]{:S(2)}, u32[]{:S(2)}) %collective-permute-start.2) | collective-permute-done | bytes 524320 | tf_op jit(solution)/shard_map/ppermute | solution.py:30
  20.1 1.8 %kv_first_sum_kernel.1 = (f32[5,512,128]{2,1,0:T(8,128)}, f32[5,512,128]{2,1,0:T(8,128)}) custom-call(f32[2,512,128]{2,1,0:T(8,128)S(1)} %collective-permute-done.refs_0_, f32[2,512,128]{2,1,0:T(8,128)S(1)} %collective-permute-done.1.refs_1_, f32[2,512,128]{2,1,0:T(8,128)S(1)} %collective-permute-done.2.refs_2_, ...), custom_call_target="tpu_custom_call" | custom-call | tf_op jit(solution)/shard_map/kv_first_sum_kernel/pallas_call | solution.py:162
  21.9 1.2 collective-permute-start.4
  23.1 0.3 collective-permute-start.3
  23.4 1.2 taps_turn_kernel.1
  24.6 11.8 %all-to-all-start = ((f32[16,8,8,128]{3,2,1,0:T(8,128)}), f32[16,8,8,128]{3,2,1,0:T(8,128)}, u32[]{:S(2)}, u32[]{:S(2)}) async-start(f32[16,8,8,128]{3,2,1,0:T(8,128)} %bitcast.15), calls=%async_computation | async-start | bytes 1048576 | tf_op jit(solution)/shard_map/all_to_all | solution.py:523
  36.4 7.9 %query_project_kernel.1 = (f32[4,256,128]{2,1,0:T(8,128)}, f32[4,256,128]{2,1,0:T(8,128)}, f32[2,256,128]{2,1,0:T(8,128)}, f32[2,256,128]{2,1,0:T(8,128)}, f32[3...) custom-call(s32[5]{0:T(128)S(1)} %stack.23.at.place, ...), custom_call_target="tpu_custom_call" | custom-call | tf_op jit(solution)/shard_map/query_project_kernel/pallas_call | solution.py:321
  44.3 1.0 copy-done.3
  45.3 6.9 %third_kernel.1.refs_3_ = f32[11,512,128]{2,1,0:T(8,128)S(1)} custom-call(s32[5]{0:T(128)S(1)} %stack.23.at.place, bf16[1024,1024]{1,0:T(8,128)(2,1)} %act.7, bf16[3,1024,1024]{2,1,0:T(8,128)(2,1)} %bitcast.13, f32[5,512,128]{2,1,0:T(8,128)} %get-tuple-element.42.refs_0_.refs_1_, f32[4,256,128]{2,1,0:T(8,128)S(1)} %copy-done.3), custom_call_target="tpu_custom_call" | custom-call | tf_op jit(solution)/shard_map/third_kernel/pallas_call | solution.py:135
  52.2 6.2 %all-to-all-done.refs_4_.refs_0_ = f32[16,8,8,128]{3,2,1,0:T(8,128)} async-done(((f32[16,8,8,128]{3,2,1,0:T(8,128)}), f32[16,8,8,128]{3,2,1,0:T(8,128)}, u32[]{:S(2)}, u32[]{:S(2)}) %all-to-all-start) | async-done | bytes 524320 | tf_op jit(solution)/shard_map/all_to_all | solution.py:523
  58.5 3.6 %kv_second_sum_kernel.1 = (f32[2,512,128]{2,1,0:T(8,128)}, f32[2,512,128]{2,1,0:T(8,128)}, f32[3,512,128]{2,1,0:T(8,128)}) custom-call(f32[5,512,128]{2,1,0:T(8,128)} %collective-permute-done.3.refs_0_, f32[5,512,128]{2,1,0:T(8,128)} %collective-permute-done.4.refs_1_, f32[5,512,128]{2,1,0:T(8,128)} %collective-permute-done.5.refs_2_, ...), custom_call_target="tpu_custom_call" | custom-call | tf_op jit(solution)/shard_map/kv_second_sum_kernel/pallas_call | solution.py:162
  62.1 1.3 collective-permute-start.7
  63.4 0.2 collective-permute-start.6
  63.6 2.3 %kv_beside_kernel.1.refs_7_.refs_0_ = f32[4,512,128]{2,1,0:T(8,128)S(1)} custom-call(f32[5,512,128]{2,1,0:T(8,128)} %collective-permute-done.3.refs_0_, f32[5,512,128]{2,1,0:T(8,128)} %collective-permute-done.4.refs_1_, f32[5,512,128]{2,1,0:T(8,128)} %collective-permute-done.5.refs_2_, f32[11,512,128]{2,1,0:T(8,128)S(1)} %third_kernel.1.refs_3_, ...), custom_call_target="tpu_custom_call" | custom-call | tf_op jit(solution)/shard_map/kv_beside_kernel/pallas_call | solution.py:162
  65.9 3.6 %taps_kernel.1.refs_4_.refs_1_ = f32[1024,256]{1,0:T(8,128)} custom-call(f32[16,8,8,128]{3,2,1,0:T(8,128)} %all-to-all-done.refs_4_.refs_0_, bf16[256,128]{1,0:T(8,128)(2,1)} %constant.72.clone.refs_1_.refs_2_, bf16[256,128]{1,0:T(8,128)(2,1)} %constant.73.clone.refs_2_.refs_3_, f32[128,128]{1,0:T(8,128)} %constant.74.clone.refs_3_.refs_4_, ...), custom_call_target="tpu_custom_call" | custom-call | tf_op jit(solution)/shard_map/taps_kernel/pallas_call | solution.py:506
  69.6 0.1 collective-permute-start.9
  69.6 2.7 %collective-permute-start.10 = (f32[4,256,128]{2,1,0:T(8,128)}, f32[4,256,128]{2,1,0:T(8,128)S(1)}, u32[]{:S(2)}, u32[]{:S(2)}) collective-permute-start(f32[4,256,128]{2,1,0:T(8,128)} %get-tuple-element.53), channel_id=1, source_target_pairs={{0,6},{1,7},{2,0},{3,1},{4,2},{5,3},{6,4},{7,5},{8,14},{9,15},{10,... | collective-permute-start | bytes 1572872 | tf_op jit(solution)/shard_map/ppermute | solution.py:26
  72.3 3.3 %collective-permute-done.7.refs_2_ = f32[2,512,128]{2,1,0:T(8,128)} collective-permute-done((f32[2,512,128]{2,1,0:T(8,128)}, f32[2,512,128]{2,1,0:T(8,128)}, u32[]{:S(2)}, u32[]{:S(2)}) %collective-permute-start.7) | collective-permute-done | bytes 524320 | tf_op jit(solution)/shard_map/ppermute | solution.py:26
  75.6 1.1 collective-permute-start.11
  76.8 1.0 collective-permute-done.6.refs_1_
  77.8 3.5 %collective-permute-done.8.refs_3_ = f32[3,512,128]{2,1,0:T(8,128)} collective-permute-done((f32[3,512,128]{2,1,0:T(8,128)}, f32[3,512,128]{2,1,0:T(8,128)}, u32[]{:S(2)}, u32[]{:S(2)}) %collective-permute-start.8) | collective-permute-done | bytes 786464 | tf_op jit(solution)/shard_map/ppermute | solution.py:30
  81.2 2.6 %kv_kernel.1 = f32[128,8,128]{2,1,0:T(8,128)} custom-call(f32[4,512,128]{2,1,0:T(8,128)S(1)} %copy-done.2, f32[2,512,128]{2,1,0:T(8,128)} %collective-permute-done.6.refs_1_, f32[2,512,128]{2,1,0:T(8,128)} %collective-permute-done.7.refs_2_, f32[3,512,128]{2,1,0:T(8,128)} %collective-permute-done.8.refs_3_, f32[1024,256]{1,0:T(8,128)S(1)} %copy-done), custom_call_target="tpu_custom_call" | custom-call | tf_op jit(solution)/shard_map/kv_kernel/pallas_call | solution.py:506
  83.9 6.7 %all-to-all-start.1 = ((f32[16,8,8,128]{3,2,1,0:T(8,128)}), f32[16,8,8,128]{3,2,1,0:T(8,128)S(1)}, u32[]{:S(2)}, u32[]{:S(2)}) async-start(f32[16,8,8,128]{3,2,1,0:T(8,128)} %bitcast.14), calls=%async_computation.1 | async-start | bytes 1048576 | tf_op jit(solution)/shard_map/all_to_all | solution.py:523
  90.6 0.7 collective-permute-start.15
  91.3 2.4 %first_sum_kernel.1 = (f32[3,256,128]{2,1,0:T(8,128)}, f32[3,256,128]{2,1,0:T(8,128)}) custom-call(f32[4,256,128]{2,1,0:T(8,128)S(1)} %collective-permute-done.9.refs_0_.refs_2_, f32[4,256,128]{2,1,0:T(8,128)S(1)} %collective-permute-done.10.refs_1_.refs_3_, f32[3,256,128]{2,1,0:T(8,128)S(1)} %collective-permute-done.11.refs_2_.refs_4_, ...), custom_call_target="tpu_custom_call" | custom-call | tf_op jit(solution)/shard_map/first_sum_kernel/pallas_call | solution.py:162
  93.7 0.6 collective-permute-start.13
  94.3 0.9 collective-permute-start.12
  95.2 6.5 %all-to-all-done.1.refs_0_ = f32[16,8,8,128]{3,2,1,0:T(8,128)S(1)} async-done(((f32[16,8,8,128]{3,2,1,0:T(8,128)}), f32[16,8,8,128]{3,2,1,0:T(8,128)S(1)}, u32[]{:S(2)}, u32[]{:S(2)}) %all-to-all-start.1) | async-done | bytes 524320 | tf_op jit(solution)/shard_map/all_to_all | solution.py:523
  101.7 4.7 %conv_kernel.1 = f32[16,8,8,128]{3,2,1,0:T(8,128)} custom-call(f32[16,8,8,128]{3,2,1,0:T(8,128)S(1)} %all-to-all-done.1.refs_0_, f32[1024,256]{1,0:T(8,128)} %taps_kernel.1.refs_4_.refs_1_, bf16[256,128]{1,0:T(8,128)(2,1)} %constant.72.clone.refs_1_.refs_2_, bf16[256,128]{1,0:T(8,128)(2,1)} %constant.73.clone.refs_2_.refs_3_, ...), custom_call_target="tpu_custom_call" | custom-call | tf_op jit(solution)/shard_map/conv_kernel/pallas_call | solution.py:506
  106.5 4.7 %all-to-all-start.2 = ((f32[16,8,8,128]{3,2,1,0:T(8,128)}), f32[16,8,8,128]{3,2,1,0:T(8,128)S(1)}, u32[]{:S(2)}, u32[]{:S(2)}) async-start(f32[16,8,8,128]{3,2,1,0:T(8,128)} %conv_kernel.1), calls=%async_computation.2 | async-start | bytes 1048576 | tf_op jit(solution)/shard_map/all_to_all | solution.py:523
  111.1 0.8 collective-permute-start.14
  112.0 1.5 %query_second_sum_kernel.1 = (f32[2,256,128]{2,1,0:T(8,128)S(1)}, f32[2,256,128]{2,1,0:T(8,128)S(1)}, f32[2,256,128]{2,1,0:T(8,128)S(1)}) custom-call(f32[3,256,128]{2,1,0:T(8,128)S(1)} %collective-permute-done.12.refs_0_, f32[3,256,128]{2,1,0:T(8,128)S(1)} %collective-permute-done.13.refs_1_, f32[4,256,128]{2,1,0:T(8,128)S(1)} %collective-permute-done.9.refs_0_.refs_2_, ...), custom_call_target="tpu_custom_call" | custom-call | tf_op jit(solution)/shard_map/query_second_sum_kernel/pallas_call | solution.py:162
  113.5 0.6 collective-permute-start.17
  114.1 1.2 collective-permute-start.18
  115.3 0.5 collective-permute-start.16
  115.7 8.5 %collective-permute-done.14.refs_4_ = f32[2,256,128]{2,1,0:T(8,128)S(1)} collective-permute-done((f32[2,256,128]{2,1,0:T(8,128)}, f32[2,256,128]{2,1,0:T(8,128)S(1)}, u32[]{:S(2)}, u32[]{:S(2)}) %collective-permute-start.14) | collective-permute-done | bytes 262176 | tf_op jit(solution)/shard_map/ppermute | solution.py:30
  124.2 1.3 %query_beside_kernel.1.refs_0_ = f32[4,256,128]{2,1,0:T(8,128)S(1)} custom-call(f32[3,256,128]{2,1,0:T(8,128)S(1)} %collective-permute-done.12.refs_0_, f32[3,256,128]{2,1,0:T(8,128)S(1)} %collective-permute-done.13.refs_1_, f32[4,256,128]{2,1,0:T(8,128)S(1)} %collective-permute-done.9.refs_0_.refs_2_, ...), custom_call_target="tpu_custom_call" | custom-call | tf_op jit(solution)/shard_map/query_beside_kernel/pallas_call | solution.py:162
  125.5 4.3 %collective-permute-done.18.refs_3_ = f32[2,256,128]{2,1,0:T(8,128)S(1)} collective-permute-done((f32[2,256,128]{2,1,0:T(8,128)S(1)}, f32[2,256,128]{2,1,0:T(8,128)S(1)}, u32[]{:S(2)}, u32[]{:S(2)}) %collective-permute-start.18) | collective-permute-done | bytes 262176 | tf_op jit(solution)/shard_map/ppermute | solution.py:30
  129.8 0.1 query_kernel.1.refs_1_
  129.9 1.1 gate_kernel.1
  (27 shorter events, 0.1 us)
Async XLA Ops:
  3.9 14.6 %collective-permute-start = (f32[2,512,128]{2,1,0:T(8,128)S(1)}, f32[2,512,128]{2,1,0:T(8,128)S(1)}, u32[]{:S(2)}, u32[]{:S(2)}) collective-permute-start(f32[2,512,128]{2,1,0:T(8,128)S(1)} %get-tuple-element.36), channel_id=1, source_target_pairs={{0,2},{1,3},{2,4},{3,5},{4,6},{5,7},{6,0},{7,1},{8,10},{9,11},{10,... | collective-permute-start | bytes 1572872 | tf_op jit(solution)/shard_map/ppermute | solution.py:26
  6.0 12.5 %collective-permute-start.1 = (f32[2,512,128]{2,1,0:T(8,128)S(1)}, f32[2,512,128]{2,1,0:T(8,128)S(1)}, u32[]{:S(2)}, u32[]{:S(2)}) collective-permute-start(f32[2,512,128]{2,1,0:T(8,128)S(1)} %get-tuple-element.37), channel_id=1, source_target_pairs={{0,6},{1,7},{2,0},{3,1},{4,2},{5,3},{6,4},{7,5},{8,14},{9,15},{10,... | collective-permute-start | bytes 1572872 | tf_op jit(solution)/shard_map/ppermute | solution.py:26
  7.4 12.7 %collective-permute-start.2 = (f32[2,512,128]{2,1,0:T(8,128)S(1)}, f32[2,512,128]{2,1,0:T(8,128)S(1)}, u32[]{:S(2)}, u32[]{:S(2)}) collective-permute-start(f32[2,512,128]{2,1,0:T(8,128)S(1)} %get-tuple-element.38), channel_id=1, source_target_pairs={{0,1},{1,0},{2,3},{3,2},{4,5},{5,4},{6,7},{7,6},{8,9},{9,8},{10,11... | collective-permute-start | bytes 1572872 | tf_op jit(solution)/shard_map/ppermute | solution.py:30
  16.6 41.8 %collective-permute-start.5 = (f32[5,512,128]{2,1,0:T(8,128)}, f32[5,512,128]{2,1,0:T(8,128)}, u32[]{:S(2)}, u32[]{:S(2)}) collective-permute-start(f32[5,512,128]{2,1,0:T(8,128)} %get-tuple-element.44), channel_id=1, source_target_pairs={{0,1},{1,0},{2,3},{3,2},{4,5},{5,4},{6,7},{7,6},{8,9},{9,8},{10,11... | collective-permute-start | bytes 3932168 | tf_op jit(solution)/shard_map/ppermute | solution.py:30
  20.1 3.2 %copy-start.5 = (f32[1024,128]{1,0:T(8,128)S(1)}, f32[1024,128]{1,0:T(8,128)}, u32[]{:S(2)}) copy-start(f32[1024,128]{1,0:T(8,128)} %refs_0_.1) | copy-start | bytes 1572868
  21.9 36.6 %collective-permute-start.4 = (f32[5,512,128]{2,1,0:T(8,128)}, f32[5,512,128]{2,1,0:T(8,128)}, u32[]{:S(2)}, u32[]{:S(2)}) collective-permute-start(f32[5,512,128]{2,1,0:T(8,128)} %get-tuple-element.43), channel_id=1, source_target_pairs={{0,6},{1,7},{2,0},{3,1},{4,2},{5,3},{6,4},{7,5},{8,14},{9,15},{10,... | collective-permute-start | bytes 3932168 | tf_op jit(solution)/shard_map/ppermute | solution.py:26
  23.1 35.4 %collective-permute-start.3 = (f32[5,512,128]{2,1,0:T(8,128)}, f32[5,512,128]{2,1,0:T(8,128)}, u32[]{:S(2)}, u32[]{:S(2)}) collective-permute-start(f32[5,512,128]{2,1,0:T(8,128)} %get-tuple-element.42.refs_0_.refs_1_), channel_id=1, source_target_pairs={{0,2},{1,3},{2,4},{3,5},{4,6},{5,7},{6,0},{7,1},{8,10},{9,11},{10,... | collective-permute-start | bytes 3932168 | tf_op jit(solution)/shard_map/ppermute | solution.py:26
  24.6 33.9 %all-to-all-start = ((f32[16,8,8,128]{3,2,1,0:T(8,128)}), f32[16,8,8,128]{3,2,1,0:T(8,128)}, u32[]{:S(2)}, u32[]{:S(2)}) async-start(f32[16,8,8,128]{3,2,1,0:T(8,128)} %bitcast.15), calls=%async_computation | async-start | bytes 1048576 | tf_op jit(solution)/shard_map/all_to_all | solution.py:523
  44.3 1.0 copy-start.3
  45.3 13.2 %copy-start.4 = (f32[4,256,128]{2,1,0:T(8,128)S(1)}, f32[4,256,128]{2,1,0:T(8,128)}, u32[]{:S(2)}) copy-start(f32[4,256,128]{2,1,0:T(8,128)} %get-tuple-element.45.refs_1_.refs_5_.refs_0_) | copy-start | bytes 1572868
  62.1 19.1 %collective-permute-start.8 = (f32[3,512,128]{2,1,0:T(8,128)}, f32[3,512,128]{2,1,0:T(8,128)}, u32[]{:S(2)}, u32[]{:S(2)}) collective-permute-start(f32[3,512,128]{2,1,0:T(8,128)} %get-tuple-element.48), channel_id=1, source_target_pairs={{0,1},{1,0},{2,3},{3,2},{4,5},{5,4},{6,7},{7,6},{8,9},{9,8},{10,11... | collective-permute-start | bytes 2359304 | tf_op jit(solution)/shard_map/ppermute | solution.py:30
  62.1 13.5 %collective-permute-start.7 = (f32[2,512,128]{2,1,0:T(8,128)}, f32[2,512,128]{2,1,0:T(8,128)}, u32[]{:S(2)}, u32[]{:S(2)}) collective-permute-start(f32[2,512,128]{2,1,0:T(8,128)} %get-tuple-element.47), channel_id=1, source_target_pairs={{0,6},{1,7},{2,0},{3,1},{4,2},{5,3},{6,4},{7,5},{8,14},{9,15},{10,... | collective-permute-start | bytes 1572872 | tf_op jit(solution)/shard_map/ppermute | solution.py:26
  63.4 14.4 %collective-permute-start.6 = (f32[2,512,128]{2,1,0:T(8,128)}, f32[2,512,128]{2,1,0:T(8,128)}, u32[]{:S(2)}, u32[]{:S(2)}) collective-permute-start(f32[2,512,128]{2,1,0:T(8,128)} %get-tuple-element.46.refs_4_), channel_id=1, source_target_pairs={{0,2},{1,3},{2,4},{3,5},{4,6},{5,7},{6,0},{7,1},{8,10},{9,11},{10,... | collective-permute-start | bytes 1572872 | tf_op jit(solution)/shard_map/ppermute | solution.py:26
  65.9 3.7 %copy-start.1 = (f32[4,512,128]{2,1,0:T(8,128)}, f32[4,512,128]{2,1,0:T(8,128)S(1)}, u32[]{:S(2)}) copy-start(f32[4,512,128]{2,1,0:T(8,128)S(1)} %kv_beside_kernel.1.refs_7_.refs_0_) | copy-start | bytes 3145732
  69.5 11.7 %copy-start = (f32[1024,256]{1,0:T(8,128)S(1)}, f32[1024,256]{1,0:T(8,128)}, u32[]{:S(2)}) copy-start(f32[1024,256]{1,0:T(8,128)} %taps_kernel.1.refs_4_.refs_1_) | copy-start | bytes 3145732
  69.5 11.7 %copy-start.2 = (f32[4,512,128]{2,1,0:T(8,128)S(1)}, f32[4,512,128]{2,1,0:T(8,128)}, u32[]{:S(2)}) copy-start(f32[4,512,128]{2,1,0:T(8,128)} %copy-done.1) | copy-start | bytes 3145732
  69.6 21.7 %collective-permute-start.9 = (f32[4,256,128]{2,1,0:T(8,128)}, f32[4,256,128]{2,1,0:T(8,128)S(1)}, u32[]{:S(2)}, u32[]{:S(2)}) collective-permute-start(f32[4,256,128]{2,1,0:T(8,128)} %get-tuple-element.52), channel_id=1, source_target_pairs={{0,2},{1,3},{2,4},{3,5},{4,6},{5,7},{6,0},{7,1},{8,10},{9,11},{10,... | collective-permute-start | bytes 1572872 | tf_op jit(solution)/shard_map/ppermute | solution.py:26
  69.6 21.7 %collective-permute-start.10 = (f32[4,256,128]{2,1,0:T(8,128)}, f32[4,256,128]{2,1,0:T(8,128)S(1)}, u32[]{:S(2)}, u32[]{:S(2)}) collective-permute-start(f32[4,256,128]{2,1,0:T(8,128)} %get-tuple-element.53), channel_id=1, source_target_pairs={{0,6},{1,7},{2,0},{3,1},{4,2},{5,3},{6,4},{7,5},{8,14},{9,15},{10,... | collective-permute-start | bytes 1572872 | tf_op jit(solution)/shard_map/ppermute | solution.py:26
  75.6 15.7 %collective-permute-start.11 = (f32[3,256,128]{2,1,0:T(8,128)}, f32[3,256,128]{2,1,0:T(8,128)S(1)}, u32[]{:S(2)}, u32[]{:S(2)}) collective-permute-start(f32[3,256,128]{2,1,0:T(8,128)} %get-tuple-element.54), channel_id=1, source_target_pairs={{0,1},{1,0},{2,3},{3,2},{4,5},{5,4},{6,7},{7,6},{8,9},{9,8},{10,11... | collective-permute-start | bytes 1179656 | tf_op jit(solution)/shard_map/ppermute | solution.py:30
  83.9 17.8 %all-to-all-start.1 = ((f32[16,8,8,128]{3,2,1,0:T(8,128)}), f32[16,8,8,128]{3,2,1,0:T(8,128)S(1)}, u32[]{:S(2)}, u32[]{:S(2)}) async-start(f32[16,8,8,128]{3,2,1,0:T(8,128)} %bitcast.14), calls=%async_computation.1 | async-start | bytes 1048576 | tf_op jit(solution)/shard_map/all_to_all | solution.py:523
  90.6 21.4 %collective-permute-start.15 = (f32[3,256,128]{2,1,0:T(8,128)}, f32[3,256,128]{2,1,0:T(8,128)}, u32[]{:S(2)}, u32[]{:S(2)}) collective-permute-start(f32[3,256,128]{2,1,0:T(8,128)} %get-tuple-element.62), channel_id=1, source_target_pairs={{0,1},{1,0},{2,3},{3,2},{4,5},{5,4},{6,7},{7,6},{8,9},{9,8},{10,11... | collective-permute-start | bytes 1179656 | tf_op jit(solution)/shard_map/ppermute | solution.py:30
  93.7 18.2 %collective-permute-start.13 = (f32[3,256,128]{2,1,0:T(8,128)}, f32[3,256,128]{2,1,0:T(8,128)S(1)}, u32[]{:S(2)}, u32[]{:S(2)}) collective-permute-start(f32[3,256,128]{2,1,0:T(8,128)} %get-tuple-element.59), channel_id=1, source_target_pairs={{0,6},{1,7},{2,0},{3,1},{4,2},{5,3},{6,4},{7,5},{8,14},{9,15},{10,... | collective-permute-start | bytes 1179656 | tf_op jit(solution)/shard_map/ppermute | solution.py:26
  94.3 17.7 %collective-permute-start.12 = (f32[3,256,128]{2,1,0:T(8,128)}, f32[3,256,128]{2,1,0:T(8,128)S(1)}, u32[]{:S(2)}, u32[]{:S(2)}) collective-permute-start(f32[3,256,128]{2,1,0:T(8,128)} %get-tuple-element.58.refs_1_), channel_id=1, source_target_pairs={{0,2},{1,3},{2,4},{3,5},{4,6},{5,7},{6,0},{7,1},{8,10},{9,11},{10,... | collective-permute-start | bytes 1179656 | tf_op jit(solution)/shard_map/ppermute | solution.py:26
  106.5 23.4 %all-to-all-start.2 = ((f32[16,8,8,128]{3,2,1,0:T(8,128)}), f32[16,8,8,128]{3,2,1,0:T(8,128)S(1)}, u32[]{:S(2)}, u32[]{:S(2)}) async-start(f32[16,8,8,128]{3,2,1,0:T(8,128)} %conv_kernel.1), calls=%async_computation.2 | async-start | bytes 1048576 | tf_op jit(solution)/shard_map/all_to_all | solution.py:523
  111.1 13.1 %collective-permute-start.14 = (f32[2,256,128]{2,1,0:T(8,128)}, f32[2,256,128]{2,1,0:T(8,128)S(1)}, u32[]{:S(2)}, u32[]{:S(2)}) collective-permute-start(f32[2,256,128]{2,1,0:T(8,128)} %release.3), channel_id=1, source_target_pairs={{0,1},{1,0},{2,3},{3,2},{4,5},{5,4},{6,7},{7,6},{8,9},{9,8},{10,11... | collective-permute-start | bytes 786440 | tf_op jit(solution)/shard_map/ppermute | solution.py:30
  113.5 12.1 %collective-permute-start.17 = (f32[2,256,128]{2,1,0:T(8,128)S(1)}, f32[2,256,128]{2,1,0:T(8,128)S(1)}, u32[]{:S(2)}, u32[]{:S(2)}) collective-permute-start(f32[2,256,128]{2,1,0:T(8,128)S(1)} %get-tuple-element.65), channel_id=1, source_target_pairs={{0,6},{1,7},{2,0},{3,1},{4,2},{5,3},{6,4},{7,5},{8,14},{9,15},{10,... | collective-permute-start | bytes 786440 | tf_op jit(solution)/shard_map/ppermute | solution.py:26
  114.1 15.7 %collective-permute-start.18 = (f32[2,256,128]{2,1,0:T(8,128)S(1)}, f32[2,256,128]{2,1,0:T(8,128)S(1)}, u32[]{:S(2)}, u32[]{:S(2)}) collective-permute-start(f32[2,256,128]{2,1,0:T(8,128)S(1)} %get-tuple-element.66), channel_id=1, source_target_pairs={{0,1},{1,0},{2,3},{3,2},{4,5},{5,4},{6,7},{7,6},{8,9},{9,8},{10,11... | collective-permute-start | bytes 786440 | tf_op jit(solution)/shard_map/ppermute | solution.py:30
  115.3 14.6 %collective-permute-start.16 = (f32[2,256,128]{2,1,0:T(8,128)S(1)}, f32[2,256,128]{2,1,0:T(8,128)S(1)}, u32[]{:S(2)}, u32[]{:S(2)}) collective-permute-start(f32[2,256,128]{2,1,0:T(8,128)S(1)} %get-tuple-element.64.refs_7_), channel_id=1, source_target_pairs={{0,2},{1,3},{2,4},{3,5},{4,6},{5,7},{6,0},{7,1},{8,10},{9,11},{10,... | collective-permute-start | bytes 786440 | tf_op jit(solution)/shard_map/ppermute | solution.py:26

commit v8 on v7

--- a/solution.py
+++ b/solution.py
@@ -11,7 +11,7 @@
 
 BLOCK = 128
 X_SIZE = 4
-CHUNK = 256
+CHUNK = 512
 
 
 def params(mebibytes):
@@ -221,9 +221,7 @@
 
 
 def query_project_kernel(place, act, weight, *refs):
-    send_r, send_l, keep_r, keep_l, z_send, z_next, z_late, z_mine, x_other, x_mine, product = refs[
-        -11:
-    ]
+    send_r, send_l, keep_r, keep_l, z_send, z_next, z_mine, x_other, x_mine, product = refs[-10:]
     product[...] = jnp.dot(act[...], weight[0], preferred_element_type=jnp.float32)
 
     def put(owner, other, mine):
@@ -236,7 +234,8 @@
     def z_step(half):
         for owner in range(4):
             piece = 2 * owner + half
-            put(owner, ((z_send, z_next, z_late)[piece // 3], piece % 3), (z_mine, piece))
+            other = (z_send, piece) if piece < 3 else (z_next, piece - 3)
+            put(owner, other, (z_mine, piece))
 
     def x_step(half):
         far, right, left = (
@@ -264,9 +263,9 @@
     out_x[1] = x_other[1] + (got_r[2] + dep_l[0])
 
 
-def query_beside_kernel(dep_r, dep_l, got_r, got_l, z_got, z_mine, x_mine, out):
-    out[0] = z_mine[6] + z_got[0]
-    out[1] = z_mine[7] + z_got[1]
+def query_beside_kernel(dep_r, dep_l, got_r, got_l, z_next, z_mine, x_mine, out):
+    out[0] = z_mine[6] + z_next[3]
+    out[1] = z_mine[7] + z_next[4]
     out[2] = x_mine[0] + (dep_r[1] + got_l[3])
     out[3] = x_mine[1] + (got_r[3] + dep_l[1])
 
@@ -317,7 +316,7 @@
 
 def project_query(halves, place, activations, weight, after):
     features, columns = weight.shape[1:]
-    shapes = [halves.shape(count) for count in (4, 4, 2, 2, 3, 3, 2, 8, 2, 2)]
+    shapes = [halves.shape(count) for count in (4, 4, 2, 2, 3, 5, 8, 2, 2)]
     return pl.pallas_call(
         query_project_kernel,
         grid_spec=pltpu.PrefetchScalarGridSpec(
@@ -338,7 +337,7 @@
 
 
 def reduce_query(halves, projected, after):
-    send_r, send_l, keep_r, keep_l, z_send, z_next, z_late, z_mine, x_other, x_mine = projected
+    send_r, send_l, keep_r, keep_l, z_send, z_next, z_mine, x_other, x_mine = projected
     send_r, send_l, z_send, z_next = release((send_r, send_l, z_send, z_next), after)
     got_r, got_l, z_got = shift_x(send_r, 1), shift_x(send_l, -1), swap_z(z_send)
     z_next = swap_z(z_next)
@@ -349,8 +348,7 @@
         [got_r, got_l, z_got],
         [keep_r, keep_l, z_mine],
     )
-    (z_late,) = release((z_late,), dep_r)
-    dep_r, dep_l, late_got = shift_x(dep_r, 1), shift_x(dep_l, -1), swap_z(z_late)
+    dep_r, dep_l = shift_x(dep_r, 1), shift_x(dep_l, -1)
     last_r, last_l, x_sum = sum_call(
         query_second_sum_kernel,
         halves,
@@ -362,7 +360,7 @@
         query_beside_kernel,
         halves,
         [4],
-        [dep_r, dep_l, got_r, got_l, late_got],
+        [dep_r, dep_l, got_r, got_l, z_next],
         [z_mine, x_mine],
         after=(last_r,),
     )

time: 132 us -> 127 us (0.962)
  waiting for transfers between devices: 36.8 us -> 32.1 us
    ppermute x7 -> x6, waiting for transfers between devices: 17.8 us -> 10.6 us  [swap_z(): return lax.ppermute(value, 'chan', [(i, i ^ 1) for i in range(8)])]
    ppermute x12, waiting for transfers between devices: 6.23 us -> 9.86 us  [shift_x(): lax.ppermute(value, 'chan', [(i, (i + 2 * step) % 8) for i in range(8)])]
    ppermute x7 -> x6, starting transfers between devices: 5.6 us -> 5.03 us  [swap_z(): return lax.ppermute(value, 'chan', [(i, i ^ 1) for i in range(8)])]
  transfers between devices with their start and end apart: 22 -> 21, of which waited for: 9 -> 10; matrix products, arithmetic and copies ran while one was open for 0% -> 0% of each run, Pallas kernels for 33% -> 34%
where the time goes in v8:
time: 127 us
  Pallas kernels  52.3 us (41%)
  starting transfers between devices  41 us (32%)
  waiting for transfers between devices  32.1 us (25%)
    all_to_all x3, starting transfers between devices, exchange(): return lax.all_to_all(value, 'seq', split_axis=0, concat_axis=0, tiled=True)  23.2 us
    pallas_call x3, Pallas kernels, project(): pl.pallas_call(body, grid_spec=pltpu.PrefetchScalarGridSpec(num_scalar_pr...  18.3 us
    pallas_call x6, Pallas kernels, call(): pl.pallas_call(body, grid=(1,), in_specs=[pl.BlockSpec(memory_space=pltpu...  13.4 us
    pallas_call x6, Pallas kernels, sum_call(): pl.pallas_call(body, grid=(halves.rows // tile,), in_specs=[pl.BlockSpec(...  12.7 us
    ppermute x12, starting transfers between devices, shift_x(): lax.ppermute(value, 'chan', [(i, (i + 2 * step) % 8) for i in range(8)])  12.7 us
    all_to_all x3, waiting for transfers between devices, exchange(): return lax.all_to_all(value, 'seq', split_axis=0, concat_axis=0, tiled=True)  11.6 us
    ppermute x6, waiting for transfers between devices, swap_z(): return lax.ppermute(value, 'chan', [(i, i ^ 1) for i in range(8)])  10.6 us
    ppermute x12, waiting for transfers between devices, shift_x(): lax.ppermute(value, 'chan', [(i, (i + 2 * step) % 8) for i in range(8)])  9.86 us
  transfers between devices with their start and end apart: 21, of which 10 were waited for; matrix products, arithmetic and copies ran while one was open for 0% of the time, Pallas kernels for 34%

profile of v8, /device:TPU:1, one launch (start us, length us, event | category | flops | bytes accessed | tf_op | source)
XLA Modules:
  0.0 126.6 jit_solution(4638160014704348059)
XLA Ops:
  0.0 0.1 stack.23.at.place
  0.1 3.8 %first_kernel.1 = (f32[2,512,128]{2,1,0:T(8,128)S(1)}, f32[2,512,128]{2,1,0:T(8,128)S(1)}, f32[2,512,128]{2,1,0:T(8,128)S(1)}, f32[2,512,128]{2,1,0:T(8,128)S(1)}) custom-call(s32[5]{0:T(128)S(1)} %stack.23.at.place, bf16[1024,1024]{1,0:T(8,128)(2,1)} %act.7, bf16[3,1024,1024]{2,1,0:T(8,128)(2,1)} %bitcast.10), custom_call_target="tpu_custom_call" | custom-call | tf_op jit(solution)/shard_map/first_kernel/pallas_call | solution.py:135
  3.9 2.1 %collective-permute-start = (f32[2,512,128]{2,1,0:T(8,128)S(1)}, f32[2,512,128]{2,1,0:T(8,128)S(1)}, u32[]{:S(2)}, u32[]{:S(2)}) collective-permute-start(f32[2,512,128]{2,1,0:T(8,128)S(1)} %get-tuple-element.35), channel_id=1, source_target_pairs={{0,2},{1,3},{2,4},{3,5},{4,6},{5,7},{6,0},{7,1},{8,10},{9,11},{10,... | collective-permute-start | bytes 1572872 | tf_op jit(solution)/shard_map/ppermute | solution.py:26
  6.0 1.4 %collective-permute-start.1 = (f32[2,512,128]{2,1,0:T(8,128)S(1)}, f32[2,512,128]{2,1,0:T(8,128)S(1)}, u32[]{:S(2)}, u32[]{:S(2)}) collective-permute-start(f32[2,512,128]{2,1,0:T(8,128)S(1)} %get-tuple-element.36), channel_id=1, source_target_pairs={{0,6},{1,7},{2,0},{3,1},{4,2},{5,3},{6,4},{7,5},{8,14},{9,15},{10,... | collective-permute-start | bytes 1572872 | tf_op jit(solution)/shard_map/ppermute | solution.py:26
  7.4 1.8 %collective-permute-start.2 = (f32[2,512,128]{2,1,0:T(8,128)S(1)}, f32[2,512,128]{2,1,0:T(8,128)S(1)}, u32[]{:S(2)}, u32[]{:S(2)}) collective-permute-start(f32[2,512,128]{2,1,0:T(8,128)S(1)} %get-tuple-element.37), channel_id=1, source_target_pairs={{0,1},{1,0},{2,3},{3,2},{4,5},{5,4},{6,7},{7,6},{8,9},{9,8},{10,11... | collective-permute-start | bytes 1572872 | tf_op jit(solution)/shard_map/ppermute | solution.py:30
  9.2 7.5 %second_kernel.1 = (f32[5,512,128]{2,1,0:T(8,128)S(1)}, f32[5,512,128]{2,1,0:T(8,128)S(1)}, f32[5,512,128]{2,1,0:T(8,128)}) custom-call(s32[5]{0:T(128)S(1)} %stack.23.at.place, bf16[1024,1024]{1,0:T(8,128)(2,1)} %act.7, bf16[3,1024,1024]{2,1,0:T(8,128)(2,1)} %bitcast.11, f32[2,512,128]{2,1,0:T(8,128)S(1)} %get-tuple-element.38.refs_0_.refs_5_), custom_call_target="tpu_custom_call" | custom-call | tf_op jit(solution)/shard_map/second_kernel/pallas_call | solution.py:135
  16.6 0.0 collective-permute-start.5
  16.7 1.9 %collective-permute-done.refs_0_ = f32[2,512,128]{2,1,0:T(8,128)S(1)} collective-permute-done((f32[2,512,128]{2,1,0:T(8,128)S(1)}, f32[2,512,128]{2,1,0:T(8,128)S(1)}, u32[]{:S(2)}, u32[]{:S(2)}) %collective-permute-start) | collective-permute-done | bytes 524320 | tf_op jit(solution)/shard_map/ppermute | solution.py:26
  18.5 0.0 collective-permute-done.1.refs_1_
  18.5 1.6 %collective-permute-done.2.refs_2_ = f32[2,512,128]{2,1,0:T(8,128)S(1)} collective-permute-done((f32[2,512,128]{2,1,0:T(8,128)S(1)}, f32[2,512,128]{2,1,0:T(8,128)S(1)}, u32[]{:S(2)}, u32[]{:S(2)}) %collective-permute-start.2) | collective-permute-done | bytes 524320 | tf_op jit(solution)/shard_map/ppermute | solution.py:30
  20.1 1.8 %kv_first_sum_kernel.1 = (f32[5,512,128]{2,1,0:T(8,128)}, f32[5,512,128]{2,1,0:T(8,128)}) custom-call(f32[2,512,128]{2,1,0:T(8,128)S(1)} %collective-permute-done.refs_0_, f32[2,512,128]{2,1,0:T(8,128)S(1)} %collective-permute-done.1.refs_1_, f32[2,512,128]{2,1,0:T(8,128)S(1)} %collective-permute-done.2.refs_2_, ...), custom_call_target="tpu_custom_call" | custom-call | tf_op jit(solution)/shard_map/kv_first_sum_kernel/pallas_call | solution.py:162
  21.9 1.2 collective-permute-start.4
  23.1 0.3 collective-permute-start.3
  23.4 1.1 taps_turn_kernel.1
  24.5 11.8 %all-to-all-start = ((f32[16,8,8,128]{3,2,1,0:T(8,128)}), f32[16,8,8,128]{3,2,1,0:T(8,128)}, u32[]{:S(2)}, u32[]{:S(2)}) async-start(f32[16,8,8,128]{3,2,1,0:T(8,128)} %bitcast.15), calls=%async_computation | async-start | bytes 1048576 | tf_op jit(solution)/shard_map/all_to_all | solution.py:521
  36.4 7.9 %query_project_kernel.1 = (f32[4,256,128]{2,1,0:T(8,128)}, f32[4,256,128]{2,1,0:T(8,128)}, f32[2,256,128]{2,1,0:T(8,128)}, f32[2,256,128]{2,1,0:T(8,128)}, f32[3...) custom-call(s32[5]{0:T(128)S(1)} %stack.23.at.place, ...), custom_call_target="tpu_custom_call" | custom-call | tf_op jit(solution)/shard_map/query_project_kernel/pallas_call | solution.py:320
  44.2 1.0 copy-done.3
  45.3 6.9 %third_kernel.1.refs_3_ = f32[11,512,128]{2,1,0:T(8,128)S(1)} custom-call(s32[5]{0:T(128)S(1)} %stack.23.at.place, bf16[1024,1024]{1,0:T(8,128)(2,1)} %act.7, bf16[3,1024,1024]{2,1,0:T(8,128)(2,1)} %bitcast.13, f32[5,512,128]{2,1,0:T(8,128)} %get-tuple-element.41.refs_0_.refs_1_, f32[4,256,128]{2,1,0:T(8,128)S(1)} %copy-done.3), custom_call_target="tpu_custom_call" | custom-call | tf_op jit(solution)/shard_map/third_kernel/pallas_call | solution.py:135
  52.2 6.3 %all-to-all-done.refs_4_.refs_0_ = f32[16,8,8,128]{3,2,1,0:T(8,128)} async-done(((f32[16,8,8,128]{3,2,1,0:T(8,128)}), f32[16,8,8,128]{3,2,1,0:T(8,128)}, u32[]{:S(2)}, u32[]{:S(2)}) %all-to-all-start) | async-done | bytes 524320 | tf_op jit(solution)/shard_map/all_to_all | solution.py:521
  58.5 3.6 %kv_second_sum_kernel.1 = (f32[2,512,128]{2,1,0:T(8,128)}, f32[2,512,128]{2,1,0:T(8,128)}, f32[3,512,128]{2,1,0:T(8,128)}) custom-call(f32[5,512,128]{2,1,0:T(8,128)} %collective-permute-done.3.refs_0_, f32[5,512,128]{2,1,0:T(8,128)} %collective-permute-done.4.refs_1_, f32[5,512,128]{2,1,0:T(8,128)} %collective-permute-done.5.refs_2_, ...), custom_call_target="tpu_custom_call" | custom-call | tf_op jit(solution)/shard_map/kv_second_sum_kernel/pallas_call | solution.py:162
  62.1 1.3 %collective-permute-start.7 = (f32[2,512,128]{2,1,0:T(8,128)}, f32[2,512,128]{2,1,0:T(8,128)}, u32[]{:S(2)}, u32[]{:S(2)}) collective-permute-start(f32[2,512,128]{2,1,0:T(8,128)} %get-tuple-element.46), channel_id=1, source_target_pairs={{0,6},{1,7},{2,0},{3,1},{4,2},{5,3},{6,4},{7,5},{8,14},{9,15},{10,... | collective-permute-start | bytes 1572872 | tf_op jit(solution)/shard_map/ppermute | solution.py:26
  63.4 0.2 collective-permute-start.6
  63.6 2.3 %kv_beside_kernel.1.refs_7_.refs_0_ = f32[4,512,128]{2,1,0:T(8,128)S(1)} custom-call(f32[5,512,128]{2,1,0:T(8,128)} %collective-permute-done.3.refs_0_, f32[5,512,128]{2,1,0:T(8,128)} %collective-permute-done.4.refs_1_, f32[5,512,128]{2,1,0:T(8,128)} %collective-permute-done.5.refs_2_, f32[11,512,128]{2,1,0:T(8,128)S(1)} %third_kernel.1.refs_3_, ...), custom_call_target="tpu_custom_call" | custom-call | tf_op jit(solution)/shard_map/kv_beside_kernel/pallas_call | solution.py:162
  65.9 3.6 %taps_kernel.1.refs_4_.refs_1_ = f32[1024,256]{1,0:T(8,128)} custom-call(f32[16,8,8,128]{3,2,1,0:T(8,128)} %all-to-all-done.refs_4_.refs_0_, bf16[256,128]{1,0:T(8,128)(2,1)} %constant.72.clone.refs_1_.refs_2_, bf16[256,128]{1,0:T(8,128)(2,1)} %constant.73.clone.refs_2_.refs_3_, f32[128,128]{1,0:T(8,128)} %constant.74.clone.refs_3_.refs_4_, ...), custom_call_target="tpu_custom_call" | custom-call | tf_op jit(solution)/shard_map/taps_kernel/pallas_call | solution.py:504
  69.6 0.1 collective-permute-start.9
  69.6 2.7 %collective-permute-start.10 = (f32[4,256,128]{2,1,0:T(8,128)}, f32[4,256,128]{2,1,0:T(8,128)S(1)}, u32[]{:S(2)}, u32[]{:S(2)}) collective-permute-start(f32[4,256,128]{2,1,0:T(8,128)} %get-tuple-element.52), channel_id=1, source_target_pairs={{0,6},{1,7},{2,0},{3,1},{4,2},{5,3},{6,4},{7,5},{8,14},{9,15},{10,... | collective-permute-start | bytes 1572872 | tf_op jit(solution)/shard_map/ppermute | solution.py:26
  72.4 3.2 %collective-permute-done.7.refs_2_ = f32[2,512,128]{2,1,0:T(8,128)} collective-permute-done((f32[2,512,128]{2,1,0:T(8,128)}, f32[2,512,128]{2,1,0:T(8,128)}, u32[]{:S(2)}, u32[]{:S(2)}) %collective-permute-start.7) | collective-permute-done | bytes 524320 | tf_op jit(solution)/shard_map/ppermute | solution.py:26
  75.6 1.1 collective-permute-start.11
  76.8 1.0 collective-permute-done.6.refs_1_
  77.8 3.5 %collective-permute-done.8.refs_3_ = f32[3,512,128]{2,1,0:T(8,128)} collective-permute-done((f32[3,512,128]{2,1,0:T(8,128)}, f32[3,512,128]{2,1,0:T(8,128)}, u32[]{:S(2)}, u32[]{:S(2)}) %collective-permute-start.8) | collective-permute-done | bytes 786464 | tf_op jit(solution)/shard_map/ppermute | solution.py:30
  81.2 2.6 %kv_kernel.1 = f32[128,8,128]{2,1,0:T(8,128)} custom-call(f32[4,512,128]{2,1,0:T(8,128)S(1)} %copy-done.2, f32[2,512,128]{2,1,0:T(8,128)} %collective-permute-done.6.refs_1_, f32[2,512,128]{2,1,0:T(8,128)} %collective-permute-done.7.refs_2_, f32[3,512,128]{2,1,0:T(8,128)} %collective-permute-done.8.refs_3_, f32[1024,256]{1,0:T(8,128)S(1)} %copy-done), custom_call_target="tpu_custom_call" | custom-call | tf_op jit(solution)/shard_map/kv_kernel/pallas_call | solution.py:504
  83.9 6.7 %all-to-all-start.1 = ((f32[16,8,8,128]{3,2,1,0:T(8,128)}), f32[16,8,8,128]{3,2,1,0:T(8,128)S(1)}, u32[]{:S(2)}, u32[]{:S(2)}) async-start(f32[16,8,8,128]{3,2,1,0:T(8,128)} %bitcast.14), calls=%async_computation.1 | async-start | bytes 1048576 | tf_op jit(solution)/shard_map/all_to_all | solution.py:521
  90.6 0.7 collective-permute-start.14
  91.3 2.4 %first_sum_kernel.1 = (f32[3,256,128]{2,1,0:T(8,128)}, f32[3,256,128]{2,1,0:T(8,128)}) custom-call(f32[4,256,128]{2,1,0:T(8,128)S(1)} %collective-permute-done.9.refs_0_.refs_2_, f32[4,256,128]{2,1,0:T(8,128)S(1)} %collective-permute-done.10.refs_1_.refs_3_, f32[3,256,128]{2,1,0:T(8,128)S(1)} %collective-permute-done.11.refs_2_.refs_4_, ...), custom_call_target="tpu_custom_call" | custom-call | tf_op jit(solution)/shard_map/first_sum_kernel/pallas_call | solution.py:162
  93.7 2.7 %collective-permute-start.13 = (f32[3,256,128]{2,1,0:T(8,128)}, f32[3,256,128]{2,1,0:T(8,128)S(1)}, u32[]{:S(2)}, u32[]{:S(2)}) collective-permute-start(f32[3,256,128]{2,1,0:T(8,128)} %get-tuple-element.58), channel_id=1, source_target_pairs={{0,6},{1,7},{2,0},{3,1},{4,2},{5,3},{6,4},{7,5},{8,14},{9,15},{10,... | collective-permute-start | bytes 1179656 | tf_op jit(solution)/shard_map/ppermute | solution.py:26
  96.4 5.3 %all-to-all-done.1.refs_0_ = f32[16,8,8,128]{3,2,1,0:T(8,128)S(1)} async-done(((f32[16,8,8,128]{3,2,1,0:T(8,128)}), f32[16,8,8,128]{3,2,1,0:T(8,128)S(1)}, u32[]{:S(2)}, u32[]{:S(2)}) %all-to-all-start.1) | async-done | bytes 524320 | tf_op jit(solution)/shard_map/all_to_all | solution.py:521
  101.7 4.7 %conv_kernel.1 = f32[16,8,8,128]{3,2,1,0:T(8,128)} custom-call(f32[16,8,8,128]{3,2,1,0:T(8,128)S(1)} %all-to-all-done.1.refs_0_, f32[1024,256]{1,0:T(8,128)} %taps_kernel.1.refs_4_.refs_1_, bf16[256,128]{1,0:T(8,128)(2,1)} %constant.72.clone.refs_1_.refs_2_, bf16[256,128]{1,0:T(8,128)(2,1)} %constant.73.clone.refs_2_.refs_3_, ...), custom_call_target="tpu_custom_call" | custom-call | tf_op jit(solution)/shard_map/conv_kernel/pallas_call | solution.py:504
  106.5 4.7 %all-to-all-start.2 = ((f32[16,8,8,128]{3,2,1,0:T(8,128)}), f32[16,8,8,128]{3,2,1,0:T(8,128)S(1)}, u32[]{:S(2)}, u32[]{:S(2)}) async-start(f32[16,8,8,128]{3,2,1,0:T(8,128)} %conv_kernel.1), calls=%async_computation.2 | async-start | bytes 1048576 | tf_op jit(solution)/shard_map/all_to_all | solution.py:521
  111.1 1.1 collective-permute-done.14.refs_5_.refs_4_
  112.2 1.3 %query_second_sum_kernel.1 = (f32[2,256,128]{2,1,0:T(8,128)S(1)}, f32[2,256,128]{2,1,0:T(8,128)S(1)}, f32[2,256,128]{2,1,0:T(8,128)S(1)}) custom-call(f32[3,256,128]{2,1,0:T(8,128)S(1)} %collective-permute-done.12.refs_0_, f32[3,256,128]{2,1,0:T(8,128)S(1)} %collective-permute-done.13.refs_1_, f32[4,256,128]{2,1,0:T(8,128)S(1)} %collective-permute-done.9.refs_0_.refs_2_, ...), custom_call_target="tpu_custom_call" | custom-call | tf_op jit(solution)/shard_map/query_second_sum_kernel/pallas_call | solution.py:162
  113.6 0.4 collective-permute-start.16
  114.0 1.4 %collective-permute-start.17 = (f32[2,256,128]{2,1,0:T(8,128)S(1)}, f32[2,256,128]{2,1,0:T(8,128)S(1)}, u32[]{:S(2)}, u32[]{:S(2)}) collective-permute-start(f32[2,256,128]{2,1,0:T(8,128)S(1)} %get-tuple-element.64), channel_id=1, source_target_pairs={{0,1},{1,0},{2,3},{3,2},{4,5},{5,4},{6,7},{7,6},{8,9},{9,8},{10,11... | collective-permute-start | bytes 786440 | tf_op jit(solution)/shard_map/ppermute | solution.py:30
  115.3 0.5 collective-permute-start.15
  115.8 1.3 %query_beside_kernel.1.refs_0_ = f32[4,256,128]{2,1,0:T(8,128)S(1)} custom-call(f32[3,256,128]{2,1,0:T(8,128)S(1)} %collective-permute-done.12.refs_0_, f32[3,256,128]{2,1,0:T(8,128)S(1)} %collective-permute-done.13.refs_1_, f32[4,256,128]{2,1,0:T(8,128)S(1)} %collective-permute-done.9.refs_0_.refs_2_, ...), custom_call_target="tpu_custom_call" | custom-call | tf_op jit(solution)/shard_map/query_beside_kernel/pallas_call | solution.py:162
  117.1 3.7 %collective-permute-done.16.refs_2_ = f32[2,256,128]{2,1,0:T(8,128)S(1)} collective-permute-done((f32[2,256,128]{2,1,0:T(8,128)S(1)}, f32[2,256,128]{2,1,0:T(8,128)S(1)}, u32[]{:S(2)}, u32[]{:S(2)}) %collective-permute-start.16) | collective-permute-done | bytes 262176 | tf_op jit(solution)/shard_map/ppermute | solution.py:26
  120.9 4.5 %collective-permute-done.17.refs_3_ = f32[2,256,128]{2,1,0:T(8,128)S(1)} collective-permute-done((f32[2,256,128]{2,1,0:T(8,128)S(1)}, f32[2,256,128]{2,1,0:T(8,128)S(1)}, u32[]{:S(2)}, u32[]{:S(2)}) %collective-permute-start.17) | collective-permute-done | bytes 262176 | tf_op jit(solution)/shard_map/ppermute | solution.py:30
  125.3 0.1 query_kernel.1.refs_1_
  125.4 1.1 gate_kernel.1
  (24 shorter events, 0.1 us)
Async XLA Ops:
  3.9 14.6 %collective-permute-start = (f32[2,512,128]{2,1,0:T(8,128)S(1)}, f32[2,512,128]{2,1,0:T(8,128)S(1)}, u32[]{:S(2)}, u32[]{:S(2)}) collective-permute-start(f32[2,512,128]{2,1,0:T(8,128)S(1)} %get-tuple-element.35), channel_id=1, source_target_pairs={{0,2},{1,3},{2,4},{3,5},{4,6},{5,7},{6,0},{7,1},{8,10},{9,11},{10,... | collective-permute-start | bytes 1572872 | tf_op jit(solution)/shard_map/ppermute | solution.py:26
  6.0 12.5 %collective-permute-start.1 = (f32[2,512,128]{2,1,0:T(8,128)S(1)}, f32[2,512,128]{2,1,0:T(8,128)S(1)}, u32[]{:S(2)}, u32[]{:S(2)}) collective-permute-start(f32[2,512,128]{2,1,0:T(8,128)S(1)} %get-tuple-element.36), channel_id=1, source_target_pairs={{0,6},{1,7},{2,0},{3,1},{4,2},{5,3},{6,4},{7,5},{8,14},{9,15},{10,... | collective-permute-start | bytes 1572872 | tf_op jit(solution)/shard_map/ppermute | solution.py:26
  7.4 12.7 %collective-permute-start.2 = (f32[2,512,128]{2,1,0:T(8,128)S(1)}, f32[2,512,128]{2,1,0:T(8,128)S(1)}, u32[]{:S(2)}, u32[]{:S(2)}) collective-permute-start(f32[2,512,128]{2,1,0:T(8,128)S(1)} %get-tuple-element.37), channel_id=1, source_target_pairs={{0,1},{1,0},{2,3},{3,2},{4,5},{5,4},{6,7},{7,6},{8,9},{9,8},{10,11... | collective-permute-start | bytes 1572872 | tf_op jit(solution)/shard_map/ppermute | solution.py:30
  16.6 41.8 %collective-permute-start.5 = (f32[5,512,128]{2,1,0:T(8,128)}, f32[5,512,128]{2,1,0:T(8,128)}, u32[]{:S(2)}, u32[]{:S(2)}) collective-permute-start(f32[5,512,128]{2,1,0:T(8,128)} %get-tuple-element.43), channel_id=1, source_target_pairs={{0,1},{1,0},{2,3},{3,2},{4,5},{5,4},{6,7},{7,6},{8,9},{9,8},{10,11... | collective-permute-start | bytes 3932168 | tf_op jit(solution)/shard_map/ppermute | solution.py:30
  20.1 3.2 %copy-start.5 = (f32[1024,128]{1,0:T(8,128)S(1)}, f32[1024,128]{1,0:T(8,128)}, u32[]{:S(2)}) copy-start(f32[1024,128]{1,0:T(8,128)} %refs_0_.1) | copy-start | bytes 1572868
  21.9 36.5 %collective-permute-start.4 = (f32[5,512,128]{2,1,0:T(8,128)}, f32[5,512,128]{2,1,0:T(8,128)}, u32[]{:S(2)}, u32[]{:S(2)}) collective-permute-start(f32[5,512,128]{2,1,0:T(8,128)} %get-tuple-element.42), channel_id=1, source_target_pairs={{0,6},{1,7},{2,0},{3,1},{4,2},{5,3},{6,4},{7,5},{8,14},{9,15},{10,... | collective-permute-start | bytes 3932168 | tf_op jit(solution)/shard_map/ppermute | solution.py:26
  23.1 35.4 %collective-permute-start.3 = (f32[5,512,128]{2,1,0:T(8,128)}, f32[5,512,128]{2,1,0:T(8,128)}, u32[]{:S(2)}, u32[]{:S(2)}) collective-permute-start(f32[5,512,128]{2,1,0:T(8,128)} %get-tuple-element.41.refs_0_.refs_1_), channel_id=1, source_target_pairs={{0,2},{1,3},{2,4},{3,5},{4,6},{5,7},{6,0},{7,1},{8,10},{9,11},{10,... | collective-permute-start | bytes 3932168 | tf_op jit(solution)/shard_map/ppermute | solution.py:26
  24.5 33.9 %all-to-all-start = ((f32[16,8,8,128]{3,2,1,0:T(8,128)}), f32[16,8,8,128]{3,2,1,0:T(8,128)}, u32[]{:S(2)}, u32[]{:S(2)}) async-start(f32[16,8,8,128]{3,2,1,0:T(8,128)} %bitcast.15), calls=%async_computation | async-start | bytes 1048576 | tf_op jit(solution)/shard_map/all_to_all | solution.py:521
  44.2 1.0 copy-start.3
  45.3 13.2 %copy-start.4 = (f32[4,256,128]{2,1,0:T(8,128)S(1)}, f32[4,256,128]{2,1,0:T(8,128)}, u32[]{:S(2)}) copy-start(f32[4,256,128]{2,1,0:T(8,128)} %get-tuple-element.44.refs_1_.refs_5_.refs_0_) | copy-start | bytes 1572868
  62.1 19.1 %collective-permute-start.8 = (f32[3,512,128]{2,1,0:T(8,128)}, f32[3,512,128]{2,1,0:T(8,128)}, u32[]{:S(2)}, u32[]{:S(2)}) collective-permute-start(f32[3,512,128]{2,1,0:T(8,128)} %get-tuple-element.47), channel_id=1, source_target_pairs={{0,1},{1,0},{2,3},{3,2},{4,5},{5,4},{6,7},{7,6},{8,9},{9,8},{10,11... | collective-permute-start | bytes 2359304 | tf_op jit(solution)/shard_map/ppermute | solution.py:30
  62.1 13.5 %collective-permute-start.7 = (f32[2,512,128]{2,1,0:T(8,128)}, f32[2,512,128]{2,1,0:T(8,128)}, u32[]{:S(2)}, u32[]{:S(2)}) collective-permute-start(f32[2,512,128]{2,1,0:T(8,128)} %get-tuple-element.46), channel_id=1, source_target_pairs={{0,6},{1,7},{2,0},{3,1},{4,2},{5,3},{6,4},{7,5},{8,14},{9,15},{10,... | collective-permute-start | bytes 1572872 | tf_op jit(solution)/shard_map/ppermute | solution.py:26
  63.4 14.4 %collective-permute-start.6 = (f32[2,512,128]{2,1,0:T(8,128)}, f32[2,512,128]{2,1,0:T(8,128)}, u32[]{:S(2)}, u32[]{:S(2)}) collective-permute-start(f32[2,512,128]{2,1,0:T(8,128)} %get-tuple-element.45.refs_4_), channel_id=1, source_target_pairs={{0,2},{1,3},{2,4},{3,5},{4,6},{5,7},{6,0},{7,1},{8,10},{9,11},{10,... | collective-permute-start | bytes 1572872 | tf_op jit(solution)/shard_map/ppermute | solution.py:26
  65.9 3.7 %copy-start.1 = (f32[4,512,128]{2,1,0:T(8,128)}, f32[4,512,128]{2,1,0:T(8,128)S(1)}, u32[]{:S(2)}) copy-start(f32[4,512,128]{2,1,0:T(8,128)S(1)} %kv_beside_kernel.1.refs_7_.refs_0_) | copy-start | bytes 3145732
  69.5 11.7 %copy-start = (f32[1024,256]{1,0:T(8,128)S(1)}, f32[1024,256]{1,0:T(8,128)}, u32[]{:S(2)}) copy-start(f32[1024,256]{1,0:T(8,128)} %taps_kernel.1.refs_4_.refs_1_) | copy-start | bytes 3145732
  69.5 11.7 %copy-start.2 = (f32[4,512,128]{2,1,0:T(8,128)S(1)}, f32[4,512,128]{2,1,0:T(8,128)}, u32[]{:S(2)}) copy-start(f32[4,512,128]{2,1,0:T(8,128)} %copy-done.1) | copy-start | bytes 3145732
  69.6 21.7 %collective-permute-start.9 = (f32[4,256,128]{2,1,0:T(8,128)}, f32[4,256,128]{2,1,0:T(8,128)S(1)}, u32[]{:S(2)}, u32[]{:S(2)}) collective-permute-start(f32[4,256,128]{2,1,0:T(8,128)} %get-tuple-element.51), channel_id=1, source_target_pairs={{0,2},{1,3},{2,4},{3,5},{4,6},{5,7},{6,0},{7,1},{8,10},{9,11},{10,... | collective-permute-start | bytes 1572872 | tf_op jit(solution)/shard_map/ppermute | solution.py:26
  69.6 21.7 %collective-permute-start.10 = (f32[4,256,128]{2,1,0:T(8,128)}, f32[4,256,128]{2,1,0:T(8,128)S(1)}, u32[]{:S(2)}, u32[]{:S(2)}) collective-permute-start(f32[4,256,128]{2,1,0:T(8,128)} %get-tuple-element.52), channel_id=1, source_target_pairs={{0,6},{1,7},{2,0},{3,1},{4,2},{5,3},{6,4},{7,5},{8,14},{9,15},{10,... | collective-permute-start | bytes 1572872 | tf_op jit(solution)/shard_map/ppermute | solution.py:26
  75.6 15.7 %collective-permute-start.11 = (f32[3,256,128]{2,1,0:T(8,128)}, f32[3,256,128]{2,1,0:T(8,128)S(1)}, u32[]{:S(2)}, u32[]{:S(2)}) collective-permute-start(f32[3,256,128]{2,1,0:T(8,128)} %get-tuple-element.53), channel_id=1, source_target_pairs={{0,1},{1,0},{2,3},{3,2},{4,5},{5,4},{6,7},{7,6},{8,9},{9,8},{10,11... | collective-permute-start | bytes 1179656 | tf_op jit(solution)/shard_map/ppermute | solution.py:30
  83.9 17.8 %all-to-all-start.1 = ((f32[16,8,8,128]{3,2,1,0:T(8,128)}), f32[16,8,8,128]{3,2,1,0:T(8,128)S(1)}, u32[]{:S(2)}, u32[]{:S(2)}) async-start(f32[16,8,8,128]{3,2,1,0:T(8,128)} %bitcast.14), calls=%async_computation.1 | async-start | bytes 1048576 | tf_op jit(solution)/shard_map/all_to_all | solution.py:521
  90.6 21.6 %collective-permute-start.14 = (f32[5,256,128]{2,1,0:T(8,128)}, f32[5,256,128]{2,1,0:T(8,128)S(1)}, u32[]{:S(2)}, u32[]{:S(2)}) collective-permute-start(f32[5,256,128]{2,1,0:T(8,128)} %get-tuple-element.59), channel_id=1, source_target_pairs={{0,1},{1,0},{2,3},{3,2},{4,5},{5,4},{6,7},{7,6},{8,9},{9,8},{10,11... | collective-permute-start | bytes 1966088 | tf_op jit(solution)/shard_map/ppermute | solution.py:30
  93.7 18.5 %collective-permute-start.12 = (f32[3,256,128]{2,1,0:T(8,128)}, f32[3,256,128]{2,1,0:T(8,128)S(1)}, u32[]{:S(2)}, u32[]{:S(2)}) collective-permute-start(f32[3,256,128]{2,1,0:T(8,128)} %get-tuple-element.57), channel_id=1, source_target_pairs={{0,2},{1,3},{2,4},{3,5},{4,6},{5,7},{6,0},{7,1},{8,10},{9,11},{10,... | collective-permute-start | bytes 1179656 | tf_op jit(solution)/shard_map/ppermute | solution.py:26
  93.7 18.5 %collective-permute-start.13 = (f32[3,256,128]{2,1,0:T(8,128)}, f32[3,256,128]{2,1,0:T(8,128)S(1)}, u32[]{:S(2)}, u32[]{:S(2)}) collective-permute-start(f32[3,256,128]{2,1,0:T(8,128)} %get-tuple-element.58), channel_id=1, source_target_pairs={{0,6},{1,7},{2,0},{3,1},{4,2},{5,3},{6,4},{7,5},{8,14},{9,15},{10,... | collective-permute-start | bytes 1179656 | tf_op jit(solution)/shard_map/ppermute | solution.py:26
  106.5 18.9 %all-to-all-start.2 = ((f32[16,8,8,128]{3,2,1,0:T(8,128)}), f32[16,8,8,128]{3,2,1,0:T(8,128)S(1)}, u32[]{:S(2)}, u32[]{:S(2)}) async-start(f32[16,8,8,128]{3,2,1,0:T(8,128)} %conv_kernel.1), calls=%async_computation.2 | async-start | bytes 1048576 | tf_op jit(solution)/shard_map/all_to_all | solution.py:521
  113.6 7.3 %collective-permute-start.16 = (f32[2,256,128]{2,1,0:T(8,128)S(1)}, f32[2,256,128]{2,1,0:T(8,128)S(1)}, u32[]{:S(2)}, u32[]{:S(2)}) collective-permute-start(f32[2,256,128]{2,1,0:T(8,128)S(1)} %get-tuple-element.63), channel_id=1, source_target_pairs={{0,6},{1,7},{2,0},{3,1},{4,2},{5,3},{6,4},{7,5},{8,14},{9,15},{10,... | collective-permute-start | bytes 786440 | tf_op jit(solution)/shard_map/ppermute | solution.py:26
  114.0 11.4 %collective-permute-start.17 = (f32[2,256,128]{2,1,0:T(8,128)S(1)}, f32[2,256,128]{2,1,0:T(8,128)S(1)}, u32[]{:S(2)}, u32[]{:S(2)}) collective-permute-start(f32[2,256,128]{2,1,0:T(8,128)S(1)} %get-tuple-element.64), channel_id=1, source_target_pairs={{0,1},{1,0},{2,3},{3,2},{4,5},{5,4},{6,7},{7,6},{8,9},{9,8},{10,11... | collective-permute-start | bytes 786440 | tf_op jit(solution)/shard_map/ppermute | solution.py:30
  115.3 10.0 %collective-permute-start.15 = (f32[2,256,128]{2,1,0:T(8,128)S(1)}, f32[2,256,128]{2,1,0:T(8,128)S(1)}, u32[]{:S(2)}, u32[]{:S(2)}) collective-permute-start(f32[2,256,128]{2,1,0:T(8,128)S(1)} %get-tuple-element.62.refs_7_), channel_id=1, source_target_pairs={{0,2},{1,3},{2,4},{3,5},{4,6},{5,7},{6,0},{7,1},{8,10},{9,11},{10,... | collective-permute-start | bytes 786440 | tf_op jit(solution)/shard_map/ppermute | solution.py:26

commit v9 on v8

--- a/solution.py
+++ b/solution.py
@@ -188,21 +188,45 @@
         out[4] = z_mine[half] + z_got[half]
 
 
-def kv_second_sum_kernel(next_r, next_l, z_got, mine, out_r, out_l, out_xz):
-    out_r[0] = mine[0] + z_got[0] + next_r[4]
-    out_r[1] = mine[1] + z_got[1]
-    out_l[0] = mine[2] + z_got[2]
-    out_l[1] = mine[3] + z_got[3] + next_l[4]
-    out_xz[0] = mine[7] + (next_r[2] + next_l[0])
-    out_xz[1] = mine[8] + (next_r[0] + next_l[2])
-    out_xz[2] = mine[6]
-
-
-def kv_beside_kernel(next_r, next_l, z_got, mine, out):
-    out[0] = mine[4] + z_got[4]
-    out[1] = mine[5]
-    out[2] = mine[9] + (next_r[3] + next_l[1])
-    out[3] = mine[10] + (next_r[1] + next_l[3])
+def piece_call(kernel, halves, counts, pieces, after=()):
+    tile = min(2 * BLOCK, halves.rows)
+
+    def body(*refs):
+        kernel(*refs[: len(pieces)], *refs[len(pieces) + len(after) :])
+
+    def spec(index):
+        return pl.BlockSpec((1, tile, BLOCK), lambda i: (index, i, 0))
+
+    return pl.pallas_call(
+        body,
+        grid=(halves.rows // tile,),
+        in_specs=[spec(index) for _, index in pieces]
+        + [pl.BlockSpec(memory_space=pl.ANY)] * len(after),
+        out_specs=[pl.BlockSpec((n, tile, BLOCK), lambda i: (0, i, 0)) for n in counts],
+        out_shape=[jax.ShapeDtypeStruct(halves.shape(count), jnp.float32) for count in counts],
+        compiler_params=params(12),
+        name=kernel.__name__,
+    )(*[value for value, _ in pieces], *after)
+
+
+def kv_other_kernel(own_k, own_v, r_k, r_v, l_k, l_v, late, out):
+    out[0:1] = own_k[...] + (r_k[...] + l_k[...])
+    out[1:2] = own_v[...] + (r_v[...] + l_v[...])
+    out[2:3] = late[...]
+
+
+def kv_last_kernel(m0, m1, m2, m3, g0, g1, g2, g3, next_r, next_l, out_r, out_l):
+    out_r[0:1] = m0[...] + g0[...] + next_r[...]
+    out_r[1:2] = m1[...] + g1[...]
+    out_l[0:1] = m2[...] + g2[...]
+    out_l[1:2] = m3[...] + g3[...] + next_l[...]
+
+
+def kv_beside_kernel(m4, m5, g4, own_k, own_v, r_k, r_v, l_k, l_v, out):
+    out[0:1] = m4[...] + g4[...]
+    out[1:2] = m5[...]
+    out[2:3] = own_k[...] + (r_k[...] + l_k[...])
+    out[3:4] = own_v[...] + (r_v[...] + l_v[...])
 
 
 def release(values, after):
@@ -293,22 +317,28 @@
         after=(next_r,) + ready[1:],
     )
     next_r, next_l, z_five = shift_x(next_r, 1), shift_x(next_l, -1), swap_z(z_send)
-    last_r, last_l, last_xz = sum_call(
-        kv_second_sum_kernel,
+    (last_xz,) = piece_call(
+        kv_other_kernel,
         halves,
-        [2, 2, 3],
-        [next_r, next_l, z_five, mine],
-        [],
-        after=ready,
-    )
-    last = last_r
-    (part,) = sum_call(
+        [3],
+        [(mine, 7), (mine, 8), (next_r, 2), (next_r, 0), (next_l, 0), (next_l, 2), (mine, 6)],
+    )
+    last_r, last_l = piece_call(
+        kv_last_kernel,
+        halves,
+        [2, 2],
+        [(mine, i) for i in range(4)]
+        + [(z_five, i) for i in range(4)]
+        + [(next_r, 4), (next_l, 4)],
+        after=(last_xz,) + ready,
+    )
+    (part,) = piece_call(
         kv_beside_kernel,
         halves,
         [4],
-        [next_r, next_l, z_five, mine],
-        [],
-        after=(last,),
+        [(mine, 4), (mine, 5), (z_five, 4), (mine, 9), (mine, 10)]
+        + [(next_r, 3), (next_r, 1), (next_l, 1), (next_l, 3)],
+        after=(last_r,),
     )
     last_r, last_l, last_xz = shift_x(last_r, 1), shift_x(last_l, -1), swap_z(last_xz)
     return (part, last_r, last_l, last_xz), part

time: 127 us -> 131 us (1.031)
  starting transfers between devices: 41 us -> 43.8 us
    pallas_call x6 -> x4, Pallas kernels: 12.7 us -> 6.77 us  [sum_call(): pl.pallas_call(body, grid=(halves.rows // tile,), in_specs=[pl.BlockSpec(...]
    pallas_call x0 -> x3, Pallas kernels: none -> 5.9 us  [piece_call(): pl.pallas_call(body, grid=(halves.rows // tile,), in_specs=[spec(index) f...]
    ppermute x12, starting transfers between devices: 12.7 us -> 17 us  [shift_x(): lax.ppermute(value, 'chan', [(i, (i + 2 * step) % 8) for i in range(8)])]
    ppermute x6, waiting for transfers between devices: 10.6 us -> 7.06 us  [swap_z(): return lax.ppermute(value, 'chan', [(i, i ^ 1) for i in range(8)])]
    ppermute x12, waiting for transfers between devices: 9.86 us -> 13.4 us  [shift_x(): lax.ppermute(value, 'chan', [(i, (i + 2 * step) % 8) for i in range(8)])]
    all_to_all x3, starting transfers between devices: 23.2 us -> 21.6 us  [exchange(): return lax.all_to_all(value, 'seq', split_axis=0, concat_axis=0, tiled=True)]
  transfers between devices with their start and end apart: 21 -> 21, of which waited for: 10 -> 10; matrix products, arithmetic and copies ran while one was open for 0% -> 0% of each run, Pallas kernels for 34% -> 35%
where the time goes in v9:
time: 131 us; the launch traced here: 130 us
  Pallas kernels  52.2 us (40%)
  starting transfers between devices  43.8 us (33%)
  waiting for transfers between devices  33.1 us (25%)
    all_to_all x3, starting transfers between devices, exchange(): return lax.all_to_all(value, 'seq', split_axis=0, concat_axis=0, tiled=True)  21.6 us
    pallas_call x3, Pallas kernels, project(): pl.pallas_call(body, grid_spec=pltpu.PrefetchScalarGridSpec(num_scalar_pr...  18.3 us
    ppermute x12, starting transfers between devices, shift_x(): lax.ppermute(value, 'chan', [(i, (i + 2 * step) % 8) for i in range(8)])  17 us
    pallas_call x6, Pallas kernels, call(): pl.pallas_call(body, grid=(1,), in_specs=[pl.BlockSpec(memory_space=pltpu...  13.4 us
    ppermute x12, waiting for transfers between devices, shift_x(): lax.ppermute(value, 'chan', [(i, (i + 2 * step) % 8) for i in range(8)])  13.4 us
    all_to_all x3, waiting for transfers between devices, exchange(): return lax.all_to_all(value, 'seq', split_axis=0, concat_axis=0, tiled=True)  12.6 us
    pallas_call x1, Pallas kernels, project_query(): pl.pallas_call(query_project_kernel, grid_spec=pltpu.PrefetchScalarGridSp...  7.86 us
    ppermute x6, waiting for transfers between devices, swap_z(): return lax.ppermute(value, 'chan', [(i, i ^ 1) for i in range(8)])  7.06 us
  transfers between devices with their start and end apart: 21, of which 10 were waited for; matrix products, arithmetic and copies ran while one was open for 0% of the time, Pallas kernels for 35%

profile of v9, /device:TPU:1, one launch (start us, length us, event | category | flops | bytes accessed | tf_op | source)
XLA Modules:
  0.0 130.3 jit_solution(9232526172322741237)
XLA Ops:
  0.0 0.1 stack.23.at.place
  0.1 3.8 %first_kernel.1 = (f32[2,512,128]{2,1,0:T(8,128)S(1)}, f32[2,512,128]{2,1,0:T(8,128)S(1)}, f32[2,512,128]{2,1,0:T(8,128)S(1)}, f32[2,512,128]{2,1,0:T(8,128)S(1)}) custom-call(s32[5]{0:T(128)S(1)} %stack.23.at.place, bf16[1024,1024]{1,0:T(8,128)(2,1)} %act.7, bf16[3,1024,1024]{2,1,0:T(8,128)(2,1)} %bitcast.10), custom_call_target="tpu_custom_call" | custom-call | tf_op jit(solution)/shard_map/first_kernel/pallas_call | solution.py:135
  3.9 2.1 %collective-permute-start = (f32[2,512,128]{2,1,0:T(8,128)S(1)}, f32[2,512,128]{2,1,0:T(8,128)S(1)}, u32[]{:S(2)}, u32[]{:S(2)}) collective-permute-start(f32[2,512,128]{2,1,0:T(8,128)S(1)} %get-tuple-element.34), channel_id=1, source_target_pairs={{0,2},{1,3},{2,4},{3,5},{4,6},{5,7},{6,0},{7,1},{8,10},{9,11},{10,... | collective-permute-start | bytes 1572872 | tf_op jit(solution)/shard_map/ppermute | solution.py:26
  6.0 1.4 %collective-permute-start.1 = (f32[2,512,128]{2,1,0:T(8,128)S(1)}, f32[2,512,128]{2,1,0:T(8,128)S(1)}, u32[]{:S(2)}, u32[]{:S(2)}) collective-permute-start(f32[2,512,128]{2,1,0:T(8,128)S(1)} %get-tuple-element.35), channel_id=1, source_target_pairs={{0,6},{1,7},{2,0},{3,1},{4,2},{5,3},{6,4},{7,5},{8,14},{9,15},{10,... | collective-permute-start | bytes 1572872 | tf_op jit(solution)/shard_map/ppermute | solution.py:26
  7.4 1.8 %collective-permute-start.2 = (f32[2,512,128]{2,1,0:T(8,128)S(1)}, f32[2,512,128]{2,1,0:T(8,128)S(1)}, u32[]{:S(2)}, u32[]{:S(2)}) collective-permute-start(f32[2,512,128]{2,1,0:T(8,128)S(1)} %get-tuple-element.36), channel_id=1, source_target_pairs={{0,1},{1,0},{2,3},{3,2},{4,5},{5,4},{6,7},{7,6},{8,9},{9,8},{10,11... | collective-permute-start | bytes 1572872 | tf_op jit(solution)/shard_map/ppermute | solution.py:30
  9.2 7.5 %second_kernel.1 = (f32[5,512,128]{2,1,0:T(8,128)S(1)}, f32[5,512,128]{2,1,0:T(8,128)S(1)}, f32[5,512,128]{2,1,0:T(8,128)}) custom-call(s32[5]{0:T(128)S(1)} %stack.23.at.place, bf16[1024,1024]{1,0:T(8,128)(2,1)} %act.7, bf16[3,1024,1024]{2,1,0:T(8,128)(2,1)} %bitcast.11, f32[2,512,128]{2,1,0:T(8,128)S(1)} %get-tuple-element.37.refs_0_.refs_5_), custom_call_target="tpu_custom_call" | custom-call | tf_op jit(solution)/shard_map/second_kernel/pallas_call | solution.py:135
  16.6 1.9 %collective-permute-done.refs_0_ = f32[2,512,128]{2,1,0:T(8,128)S(1)} collective-permute-done((f32[2,512,128]{2,1,0:T(8,128)S(1)}, f32[2,512,128]{2,1,0:T(8,128)S(1)}, u32[]{:S(2)}, u32[]{:S(2)}) %collective-permute-start) | collective-permute-done | bytes 524320 | tf_op jit(solution)/shard_map/ppermute | solution.py:26
  18.5 1.6 %collective-permute-done.2.refs_2_ = f32[2,512,128]{2,1,0:T(8,128)S(1)} collective-permute-done((f32[2,512,128]{2,1,0:T(8,128)S(1)}, f32[2,512,128]{2,1,0:T(8,128)S(1)}, u32[]{:S(2)}, u32[]{:S(2)}) %collective-permute-start.2) | collective-permute-done | bytes 524320 | tf_op jit(solution)/shard_map/ppermute | solution.py:30
  20.1 1.8 %kv_first_sum_kernel.1 = (f32[5,512,128]{2,1,0:T(8,128)}, f32[5,512,128]{2,1,0:T(8,128)}) custom-call(f32[2,512,128]{2,1,0:T(8,128)S(1)} %collective-permute-done.refs_0_, f32[2,512,128]{2,1,0:T(8,128)S(1)} %collective-permute-done.1.refs_1_, f32[2,512,128]{2,1,0:T(8,128)S(1)} %collective-permute-done.2.refs_2_, ...), custom_call_target="tpu_custom_call" | custom-call | tf_op jit(solution)/shard_map/kv_first_sum_kernel/pallas_call | solution.py:162
  21.9 1.2 collective-permute-start.5
  23.1 0.3 collective-permute-start.4
  23.4 1.2 collective-permute-start.3
  24.6 1.1 taps_turn_kernel.1
  25.8 10.5 %all-to-all-start = ((f32[16,8,8,128]{3,2,1,0:T(8,128)}), f32[16,8,8,128]{3,2,1,0:T(8,128)}, u32[]{:S(2)}, u32[]{:S(2)}) async-start(f32[16,8,8,128]{3,2,1,0:T(8,128)} %bitcast.15), calls=%async_computation | async-start | bytes 1048576 | tf_op jit(solution)/shard_map/all_to_all | solution.py:551
  36.2 7.9 %query_project_kernel.1 = (f32[4,256,128]{2,1,0:T(8,128)}, f32[4,256,128]{2,1,0:T(8,128)}, f32[2,256,128]{2,1,0:T(8,128)}, f32[2,256,128]{2,1,0:T(8,128)}, f32[3...) custom-call(s32[5]{0:T(128)S(1)} %stack.23.at.place, ...), custom_call_target="tpu_custom_call" | custom-call | tf_op jit(solution)/shard_map/query_project_kernel/pallas_call | solution.py:350
  44.1 1.0 copy-done.3
  45.1 6.9 %third_kernel.1.refs_0_.refs_1_.refs_6_.refs_2_.refs_3_.refs_4_ = f32[11,512,128]{2,1,0:T(8,128)S(1)} custom-call(s32[5]{0:T(128)S(1)} %stack.23.at.place, bf16[1024,1024]{1,0:T(8,128)(2,1)} %act.7, bf16[3,1024,1024]{2,1,0:T(8,128)(2,1)} %bitcast.13, f32[5,512,128]{2,1,0:T(8,128)} %get-tuple-element.40.refs_0_.refs_1_, f32[4,256,128]{2,1,0:T(8,128)S(1)} %copy-done.3), custom_call_target="tpu_custom_call" | custom-call | tf_op jit(solution)/shard_map/third_kernel/pallas_call | solution.py:135
  52.0 0.0 copy-start.4
  52.1 0.5 collective-permute-done.4.refs_2_.refs_3_.refs_8_.refs_5_.refs_6_
  52.6 2.1 %kv_other_kernel.1.refs_10_ = f32[3,512,128]{2,1,0:T(8,128)} custom-call(f32[11,512,128]{2,1,0:T(8,128)S(1)} %third_kernel.1.refs_0_.refs_1_.refs_6_.refs_2_.refs_3_.refs_4_, f32[11,512,128]{2,1,0:T(8,128)S(1)} %third_kernel.1.refs_0_.refs_1_.refs_6_.refs_2_.refs_3_.refs_4_, f32[5,512,128]{2,1,0:T(8,128)} %collective-permute-done.4.refs_2_.refs_3_.refs_8_.refs_5_.refs_6_, ...), custom_call_target="tpu_custom_call" | custom-call | tf_op jit(solution)/shard_map/kv_other_kernel/pallas_call | solution.py:200
  54.7 1.6 %collective-permute-start.8 = (f32[3,512,128]{2,1,0:T(8,128)}, f32[3,512,128]{2,1,0:T(8,128)}, u32[]{:S(2)}, u32[]{:S(2)}) collective-permute-start(f32[3,512,128]{2,1,0:T(8,128)} %kv_other_kernel.1.refs_10_), channel_id=1, source_target_pairs={{0,1},{1,0},{2,3},{3,2},{4,5},{5,4},{6,7},{7,6},{8,9},{9,8},{10,11... | collective-permute-start | bytes 2359304 | tf_op jit(solution)/shard_map/ppermute | solution.py:30
  56.3 8.5 %all-to-all-done.refs_11_.refs_0_ = f32[16,8,8,128]{3,2,1,0:T(8,128)} async-done(((f32[16,8,8,128]{3,2,1,0:T(8,128)}), f32[16,8,8,128]{3,2,1,0:T(8,128)}, u32[]{:S(2)}, u32[]{:S(2)}) %all-to-all-start) | async-done | bytes 524320 | tf_op jit(solution)/shard_map/all_to_all | solution.py:551
  64.8 2.3 %kv_last_kernel.1 = (f32[2,512,128]{2,1,0:T(8,128)}, f32[2,512,128]{2,1,0:T(8,128)}) custom-call(f32[11,512,128]{2,1,0:T(8,128)S(1)} %third_kernel.1.refs_0_.refs_1_.refs_6_.refs_2_.refs_3_.refs_4_, f32[11,512,128]{2,1,0:T(8,128)S(1)} %third_kernel.1.refs_0_.refs_1_.refs_6_.refs_2_.refs_3_.refs_4_, ...), custom_call_target="tpu_custom_call" | custom-call | tf_op jit(solution)/shard_map/kv_last_kernel/pallas_call | solution.py:200
  67.2 3.7 %collective-permute-start.7 = (f32[2,512,128]{2,1,0:T(8,128)}, f32[2,512,128]{2,1,0:T(8,128)}, u32[]{:S(2)}, u32[]{:S(2)}) collective-permute-start(f32[2,512,128]{2,1,0:T(8,128)} %get-tuple-element.45), channel_id=1, source_target_pairs={{0,6},{1,7},{2,0},{3,1},{4,2},{5,3},{6,4},{7,5},{8,14},{9,15},{10,... | collective-permute-start | bytes 1572872 | tf_op jit(solution)/shard_map/ppermute | solution.py:26
  70.9 1.5 %kv_beside_kernel.1.refs_7_.refs_0_ = f32[4,512,128]{2,1,0:T(8,128)S(1)} custom-call(f32[11,512,128]{2,1,0:T(8,128)S(1)} %third_kernel.1.refs_0_.refs_1_.refs_6_.refs_2_.refs_3_.refs_4_, f32[11,512,128]{2,1,0:T(8,128)S(1)} %third_kernel.1.refs_0_.refs_1_.refs_6_.refs_2_.refs_3_.refs_4_, ...), custom_call_target="tpu_custom_call" | custom-call | tf_op jit(solution)/shard_map/kv_beside_kernel/pallas_call | solution.py:200
  72.4 3.6 %taps_kernel.1.refs_4_.refs_1_ = f32[1024,256]{1,0:T(8,128)} custom-call(f32[16,8,8,128]{3,2,1,0:T(8,128)} %all-to-all-done.refs_11_.refs_0_, bf16[256,128]{1,0:T(8,128)(2,1)} %constant.72.clone.refs_1_.refs_2_, bf16[256,128]{1,0:T(8,128)(2,1)} %constant.73.clone.refs_2_.refs_3_, f32[128,128]{1,0:T(8,128)} %constant.74.clone.refs_3_.refs_4_, ...), custom_call_target="tpu_custom_call" | custom-call | tf_op jit(solution)/shard_map/taps_kernel/pallas_call | solution.py:534
  76.1 0.1 collective-permute-start.9
  76.2 2.9 %collective-permute-start.10 = (f32[4,256,128]{2,1,0:T(8,128)}, f32[4,256,128]{2,1,0:T(8,128)S(1)}, u32[]{:S(2)}, u32[]{:S(2)}) collective-permute-start(f32[4,256,128]{2,1,0:T(8,128)} %get-tuple-element.50), channel_id=1, source_target_pairs={{0,6},{1,7},{2,0},{3,1},{4,2},{5,3},{6,4},{7,5},{8,14},{9,15},{10,... | collective-permute-start | bytes 1572872 | tf_op jit(solution)/shard_map/ppermute | solution.py:26
  79.1 3.5 %collective-permute-done.7.refs_2_ = f32[2,512,128]{2,1,0:T(8,128)} collective-permute-done((f32[2,512,128]{2,1,0:T(8,128)}, f32[2,512,128]{2,1,0:T(8,128)}, u32[]{:S(2)}, u32[]{:S(2)}) %collective-permute-start.7) | collective-permute-done | bytes 524320 | tf_op jit(solution)/shard_map/ppermute | solution.py:26
  82.6 3.1 %collective-permute-done.6.refs_1_ = f32[2,512,128]{2,1,0:T(8,128)} collective-permute-done((f32[2,512,128]{2,1,0:T(8,128)}, f32[2,512,128]{2,1,0:T(8,128)}, u32[]{:S(2)}, u32[]{:S(2)}) %collective-permute-start.6) | collective-permute-done | bytes 524320 | tf_op jit(solution)/shard_map/ppermute | solution.py:26
  85.7 2.6 %kv_kernel.1 = f32[128,8,128]{2,1,0:T(8,128)} custom-call(f32[4,512,128]{2,1,0:T(8,128)S(1)} %copy-done.2, f32[2,512,128]{2,1,0:T(8,128)} %collective-permute-done.6.refs_1_, f32[2,512,128]{2,1,0:T(8,128)} %collective-permute-done.7.refs_2_, f32[3,512,128]{2,1,0:T(8,128)} %collective-permute-done.8.refs_3_, f32[1024,256]{1,0:T(8,128)S(1)} %copy-done), custom_call_target="tpu_custom_call" | custom-call | tf_op jit(solution)/shard_map/kv_kernel/pallas_call | solution.py:534
  88.3 6.4 %all-to-all-start.1 = ((f32[16,8,8,128]{3,2,1,0:T(8,128)}), f32[16,8,8,128]{3,2,1,0:T(8,128)S(1)}, u32[]{:S(2)}, u32[]{:S(2)}) async-start(f32[16,8,8,128]{3,2,1,0:T(8,128)} %bitcast.14), calls=%async_computation.1 | async-start | bytes 1048576 | tf_op jit(solution)/shard_map/all_to_all | solution.py:551
  94.8 2.0 %collective-permute-done.9.refs_0_.refs_2_ = f32[4,256,128]{2,1,0:T(8,128)S(1)} collective-permute-done((f32[4,256,128]{2,1,0:T(8,128)}, f32[4,256,128]{2,1,0:T(8,128)S(1)}, u32[]{:S(2)}, u32[]{:S(2)}) %collective-permute-start.9) | collective-permute-done | bytes 524320 | tf_op jit(solution)/shard_map/ppermute | solution.py:26
  96.8 2.3 %first_sum_kernel.1 = (f32[3,256,128]{2,1,0:T(8,128)}, f32[3,256,128]{2,1,0:T(8,128)}) custom-call(f32[4,256,128]{2,1,0:T(8,128)S(1)} %collective-permute-done.9.refs_0_.refs_2_, f32[4,256,128]{2,1,0:T(8,128)S(1)} %collective-permute-done.10.refs_1_.refs_3_, f32[3,256,128]{2,1,0:T(8,128)S(1)} %collective-permute-done.11.refs_2_.refs_4_, ...), custom_call_target="tpu_custom_call" | custom-call | tf_op jit(solution)/shard_map/first_sum_kernel/pallas_call | solution.py:162
  99.1 2.7 %collective-permute-start.13 = (f32[3,256,128]{2,1,0:T(8,128)}, f32[3,256,128]{2,1,0:T(8,128)S(1)}, u32[]{:S(2)}, u32[]{:S(2)}) collective-permute-start(f32[3,256,128]{2,1,0:T(8,128)} %get-tuple-element.56), channel_id=1, source_target_pairs={{0,6},{1,7},{2,0},{3,1},{4,2},{5,3},{6,4},{7,5},{8,14},{9,15},{10,... | collective-permute-start | bytes 1179656 | tf_op jit(solution)/shard_map/ppermute | solution.py:26
  101.8 4.1 %all-to-all-done.1.refs_0_ = f32[16,8,8,128]{3,2,1,0:T(8,128)S(1)} async-done(((f32[16,8,8,128]{3,2,1,0:T(8,128)}), f32[16,8,8,128]{3,2,1,0:T(8,128)S(1)}, u32[]{:S(2)}, u32[]{:S(2)}) %all-to-all-start.1) | async-done | bytes 524320 | tf_op jit(solution)/shard_map/all_to_all | solution.py:551
  105.9 4.7 %conv_kernel.1 = f32[16,8,8,128]{3,2,1,0:T(8,128)} custom-call(f32[16,8,8,128]{3,2,1,0:T(8,128)S(1)} %all-to-all-done.1.refs_0_, f32[1024,256]{1,0:T(8,128)} %taps_kernel.1.refs_4_.refs_1_, bf16[256,128]{1,0:T(8,128)(2,1)} %constant.72.clone.refs_1_.refs_2_, bf16[256,128]{1,0:T(8,128)(2,1)} %constant.73.clone.refs_2_.refs_3_, ...), custom_call_target="tpu_custom_call" | custom-call | tf_op jit(solution)/shard_map/conv_kernel/pallas_call | solution.py:534
  110.7 4.7 %all-to-all-start.2 = ((f32[16,8,8,128]{3,2,1,0:T(8,128)}), f32[16,8,8,128]{3,2,1,0:T(8,128)S(1)}, u32[]{:S(2)}, u32[]{:S(2)}) async-start(f32[16,8,8,128]{3,2,1,0:T(8,128)} %conv_kernel.1), calls=%async_computation.2 | async-start | bytes 1048576 | tf_op jit(solution)/shard_map/all_to_all | solution.py:551
  115.3 0.0 collective-permute-done.14.refs_5_.refs_4_
  115.4 1.4 %query_second_sum_kernel.1 = (f32[2,256,128]{2,1,0:T(8,128)S(1)}, f32[2,256,128]{2,1,0:T(8,128)S(1)}, f32[2,256,128]{2,1,0:T(8,128)S(1)}) custom-call(f32[3,256,128]{2,1,0:T(8,128)S(1)} %collective-permute-done.12.refs_0_, f32[3,256,128]{2,1,0:T(8,128)S(1)} %collective-permute-done.13.refs_1_, f32[4,256,128]{2,1,0:T(8,128)S(1)} %collective-permute-done.9.refs_0_.refs_2_, ...), custom_call_target="tpu_custom_call" | custom-call | tf_op jit(solution)/shard_map/query_second_sum_kernel/pallas_call | solution.py:162
  116.7 1.6 %collective-permute-start.16 = (f32[2,256,128]{2,1,0:T(8,128)S(1)}, f32[2,256,128]{2,1,0:T(8,128)S(1)}, u32[]{:S(2)}, u32[]{:S(2)}) collective-permute-start(f32[2,256,128]{2,1,0:T(8,128)S(1)} %get-tuple-element.61), channel_id=1, source_target_pairs={{0,6},{1,7},{2,0},{3,1},{4,2},{5,3},{6,4},{7,5},{8,14},{9,15},{10,... | collective-permute-start | bytes 786440 | tf_op jit(solution)/shard_map/ppermute | solution.py:26
  118.3 0.6 collective-permute-start.17
  118.9 1.1 collective-permute-start.15
  120.0 1.3 %query_beside_kernel.1.refs_0_ = f32[4,256,128]{2,1,0:T(8,128)S(1)} custom-call(f32[3,256,128]{2,1,0:T(8,128)S(1)} %collective-permute-done.12.refs_0_, f32[3,256,128]{2,1,0:T(8,128)S(1)} %collective-permute-done.13.refs_1_, f32[4,256,128]{2,1,0:T(8,128)S(1)} %collective-permute-done.9.refs_0_.refs_2_, ...), custom_call_target="tpu_custom_call" | custom-call | tf_op jit(solution)/shard_map/query_beside_kernel/pallas_call | solution.py:162
  121.3 2.3 %collective-permute-done.16.refs_2_ = f32[2,256,128]{2,1,0:T(8,128)S(1)} collective-permute-done((f32[2,256,128]{2,1,0:T(8,128)S(1)}, f32[2,256,128]{2,1,0:T(8,128)S(1)}, u32[]{:S(2)}, u32[]{:S(2)}) %collective-permute-start.16) | collective-permute-done | bytes 262176 | tf_op jit(solution)/shard_map/ppermute | solution.py:26
  123.6 5.4 %collective-permute-done.17.refs_3_ = f32[2,256,128]{2,1,0:T(8,128)S(1)} collective-permute-done((f32[2,256,128]{2,1,0:T(8,128)S(1)}, f32[2,256,128]{2,1,0:T(8,128)S(1)}, u32[]{:S(2)}, u32[]{:S(2)}) %collective-permute-start.17) | collective-permute-done | bytes 262176 | tf_op jit(solution)/shard_map/ppermute | solution.py:30
  129.1 0.1 query_kernel.1.refs_1_
  129.2 1.1 gate_kernel.1
  (25 shorter events, 0.1 us)
Async XLA Ops:
  3.9 14.6 %collective-permute-start = (f32[2,512,128]{2,1,0:T(8,128)S(1)}, f32[2,512,128]{2,1,0:T(8,128)S(1)}, u32[]{:S(2)}, u32[]{:S(2)}) collective-permute-start(f32[2,512,128]{2,1,0:T(8,128)S(1)} %get-tuple-element.34), channel_id=1, source_target_pairs={{0,2},{1,3},{2,4},{3,5},{4,6},{5,7},{6,0},{7,1},{8,10},{9,11},{10,... | collective-permute-start | bytes 1572872 | tf_op jit(solution)/shard_map/ppermute | solution.py:26
  6.0 12.5 %collective-permute-start.1 = (f32[2,512,128]{2,1,0:T(8,128)S(1)}, f32[2,512,128]{2,1,0:T(8,128)S(1)}, u32[]{:S(2)}, u32[]{:S(2)}) collective-permute-start(f32[2,512,128]{2,1,0:T(8,128)S(1)} %get-tuple-element.35), channel_id=1, source_target_pairs={{0,6},{1,7},{2,0},{3,1},{4,2},{5,3},{6,4},{7,5},{8,14},{9,15},{10,... | collective-permute-start | bytes 1572872 | tf_op jit(solution)/shard_map/ppermute | solution.py:26
  7.4 12.7 %collective-permute-start.2 = (f32[2,512,128]{2,1,0:T(8,128)S(1)}, f32[2,512,128]{2,1,0:T(8,128)S(1)}, u32[]{:S(2)}, u32[]{:S(2)}) collective-permute-start(f32[2,512,128]{2,1,0:T(8,128)S(1)} %get-tuple-element.36), channel_id=1, source_target_pairs={{0,1},{1,0},{2,3},{3,2},{4,5},{5,4},{6,7},{7,6},{8,9},{9,8},{10,11... | collective-permute-start | bytes 1572872 | tf_op jit(solution)/shard_map/ppermute | solution.py:30
  20.1 4.5 %copy-start.5 = (f32[1024,128]{1,0:T(8,128)S(1)}, f32[1024,128]{1,0:T(8,128)}, u32[]{:S(2)}) copy-start(f32[1024,128]{1,0:T(8,128)} %refs_0_.1) | copy-start | bytes 1572868
  21.9 30.2 %collective-permute-start.5 = (f32[5,512,128]{2,1,0:T(8,128)}, f32[5,512,128]{2,1,0:T(8,128)}, u32[]{:S(2)}, u32[]{:S(2)}) collective-permute-start(f32[5,512,128]{2,1,0:T(8,128)} %get-tuple-element.43), channel_id=1, source_target_pairs={{0,6},{1,7},{2,0},{3,1},{4,2},{5,3},{6,4},{7,5},{8,14},{9,15},{10,... | collective-permute-start | bytes 3932168 | tf_op jit(solution)/shard_map/ppermute | solution.py:26
  23.1 29.5 %collective-permute-start.4 = (f32[5,512,128]{2,1,0:T(8,128)}, f32[5,512,128]{2,1,0:T(8,128)}, u32[]{:S(2)}, u32[]{:S(2)}) collective-permute-start(f32[5,512,128]{2,1,0:T(8,128)} %get-tuple-element.40.refs_0_.refs_1_), channel_id=1, source_target_pairs={{0,2},{1,3},{2,4},{3,5},{4,6},{5,7},{6,0},{7,1},{8,10},{9,11},{10,... | collective-permute-start | bytes 3932168 | tf_op jit(solution)/shard_map/ppermute | solution.py:26
  23.4 41.5 %collective-permute-start.3 = (f32[5,512,128]{2,1,0:T(8,128)}, f32[5,512,128]{2,1,0:T(8,128)}, u32[]{:S(2)}, u32[]{:S(2)}) collective-permute-start(f32[5,512,128]{2,1,0:T(8,128)} %get-tuple-element.42), channel_id=1, source_target_pairs={{0,1},{1,0},{2,3},{3,2},{4,5},{5,4},{6,7},{7,6},{8,9},{9,8},{10,11... | collective-permute-start | bytes 3932168 | tf_op jit(solution)/shard_map/ppermute | solution.py:30
  25.8 39.1 %all-to-all-start = ((f32[16,8,8,128]{3,2,1,0:T(8,128)}), f32[16,8,8,128]{3,2,1,0:T(8,128)}, u32[]{:S(2)}, u32[]{:S(2)}) async-start(f32[16,8,8,128]{3,2,1,0:T(8,128)} %bitcast.15), calls=%async_computation | async-start | bytes 1048576 | tf_op jit(solution)/shard_map/all_to_all | solution.py:551
  44.1 1.0 copy-start.3
  52.0 12.8 %copy-start.4 = (f32[4,256,128]{2,1,0:T(8,128)S(1)}, f32[4,256,128]{2,1,0:T(8,128)}, u32[]{:S(2)}) copy-start(f32[4,256,128]{2,1,0:T(8,128)} %get-tuple-element.41.refs_1_.refs_12_.refs_0_) | copy-start | bytes 1572868
  54.7 31.0 %collective-permute-start.8 = (f32[3,512,128]{2,1,0:T(8,128)}, f32[3,512,128]{2,1,0:T(8,128)}, u32[]{:S(2)}, u32[]{:S(2)}) collective-permute-start(f32[3,512,128]{2,1,0:T(8,128)} %kv_other_kernel.1.refs_10_), channel_id=1, source_target_pairs={{0,1},{1,0},{2,3},{3,2},{4,5},{5,4},{6,7},{7,6},{8,9},{9,8},{10,11... | collective-permute-start | bytes 2359304 | tf_op jit(solution)/shard_map/ppermute | solution.py:30
  67.2 15.4 %collective-permute-start.7 = (f32[2,512,128]{2,1,0:T(8,128)}, f32[2,512,128]{2,1,0:T(8,128)}, u32[]{:S(2)}, u32[]{:S(2)}) collective-permute-start(f32[2,512,128]{2,1,0:T(8,128)} %get-tuple-element.45), channel_id=1, source_target_pairs={{0,6},{1,7},{2,0},{3,1},{4,2},{5,3},{6,4},{7,5},{8,14},{9,15},{10,... | collective-permute-start | bytes 1572872 | tf_op jit(solution)/shard_map/ppermute | solution.py:26
  70.9 14.8 %collective-permute-start.6 = (f32[2,512,128]{2,1,0:T(8,128)}, f32[2,512,128]{2,1,0:T(8,128)}, u32[]{:S(2)}, u32[]{:S(2)}) collective-permute-start(f32[2,512,128]{2,1,0:T(8,128)} %get-tuple-element.44.refs_9_), channel_id=1, source_target_pairs={{0,2},{1,3},{2,4},{3,5},{4,6},{5,7},{6,0},{7,1},{8,10},{9,11},{10,... | collective-permute-start | bytes 1572872 | tf_op jit(solution)/shard_map/ppermute | solution.py:26
  72.4 3.7 %copy-start.1 = (f32[4,512,128]{2,1,0:T(8,128)}, f32[4,512,128]{2,1,0:T(8,128)S(1)}, u32[]{:S(2)}) copy-start(f32[4,512,128]{2,1,0:T(8,128)S(1)} %kv_beside_kernel.1.refs_7_.refs_0_) | copy-start | bytes 3145732
  76.0 9.6 %copy-start = (f32[1024,256]{1,0:T(8,128)S(1)}, f32[1024,256]{1,0:T(8,128)}, u32[]{:S(2)}) copy-start(f32[1024,256]{1,0:T(8,128)} %taps_kernel.1.refs_4_.refs_1_) | copy-start | bytes 3145732
  76.1 9.6 %copy-start.2 = (f32[4,512,128]{2,1,0:T(8,128)S(1)}, f32[4,512,128]{2,1,0:T(8,128)}, u32[]{:S(2)}) copy-start(f32[4,512,128]{2,1,0:T(8,128)} %copy-done.1) | copy-start | bytes 3145732
  76.1 20.7 %collective-permute-start.9 = (f32[4,256,128]{2,1,0:T(8,128)}, f32[4,256,128]{2,1,0:T(8,128)S(1)}, u32[]{:S(2)}, u32[]{:S(2)}) collective-permute-start(f32[4,256,128]{2,1,0:T(8,128)} %get-tuple-element.49), channel_id=1, source_target_pairs={{0,2},{1,3},{2,4},{3,5},{4,6},{5,7},{6,0},{7,1},{8,10},{9,11},{10,... | collective-permute-start | bytes 1572872 | tf_op jit(solution)/shard_map/ppermute | solution.py:26
  76.2 20.7 %collective-permute-start.10 = (f32[4,256,128]{2,1,0:T(8,128)}, f32[4,256,128]{2,1,0:T(8,128)S(1)}, u32[]{:S(2)}, u32[]{:S(2)}) collective-permute-start(f32[4,256,128]{2,1,0:T(8,128)} %get-tuple-element.50), channel_id=1, source_target_pairs={{0,6},{1,7},{2,0},{3,1},{4,2},{5,3},{6,4},{7,5},{8,14},{9,15},{10,... | collective-permute-start | bytes 1572872 | tf_op jit(solution)/shard_map/ppermute | solution.py:26
  82.6 12.2 %collective-permute-start.11 = (f32[3,256,128]{2,1,0:T(8,128)}, f32[3,256,128]{2,1,0:T(8,128)S(1)}, u32[]{:S(2)}, u32[]{:S(2)}) collective-permute-start(f32[3,256,128]{2,1,0:T(8,128)} %get-tuple-element.51), channel_id=1, source_target_pairs={{0,1},{1,0},{2,3},{3,2},{4,5},{5,4},{6,7},{7,6},{8,9},{9,8},{10,11... | collective-permute-start | bytes 1179656 | tf_op jit(solution)/shard_map/ppermute | solution.py:30
  88.3 17.6 %all-to-all-start.1 = ((f32[16,8,8,128]{3,2,1,0:T(8,128)}), f32[16,8,8,128]{3,2,1,0:T(8,128)S(1)}, u32[]{:S(2)}, u32[]{:S(2)}) async-start(f32[16,8,8,128]{3,2,1,0:T(8,128)} %bitcast.14), calls=%async_computation.1 | async-start | bytes 1048576 | tf_op jit(solution)/shard_map/all_to_all | solution.py:551
  94.8 20.6 %collective-permute-start.14 = (f32[5,256,128]{2,1,0:T(8,128)}, f32[5,256,128]{2,1,0:T(8,128)S(1)}, u32[]{:S(2)}, u32[]{:S(2)}) collective-permute-start(f32[5,256,128]{2,1,0:T(8,128)} %get-tuple-element.57), channel_id=1, source_target_pairs={{0,1},{1,0},{2,3},{3,2},{4,5},{5,4},{6,7},{7,6},{8,9},{9,8},{10,11... | collective-permute-start | bytes 1966088 | tf_op jit(solution)/shard_map/ppermute | solution.py:30
  99.1 16.2 %collective-permute-start.12 = (f32[3,256,128]{2,1,0:T(8,128)}, f32[3,256,128]{2,1,0:T(8,128)S(1)}, u32[]{:S(2)}, u32[]{:S(2)}) collective-permute-start(f32[3,256,128]{2,1,0:T(8,128)} %get-tuple-element.55), channel_id=1, source_target_pairs={{0,2},{1,3},{2,4},{3,5},{4,6},{5,7},{6,0},{7,1},{8,10},{9,11},{10,... | collective-permute-start | bytes 1179656 | tf_op jit(solution)/shard_map/ppermute | solution.py:26
  99.1 16.2 %collective-permute-start.13 = (f32[3,256,128]{2,1,0:T(8,128)}, f32[3,256,128]{2,1,0:T(8,128)S(1)}, u32[]{:S(2)}, u32[]{:S(2)}) collective-permute-start(f32[3,256,128]{2,1,0:T(8,128)} %get-tuple-element.56), channel_id=1, source_target_pairs={{0,6},{1,7},{2,0},{3,1},{4,2},{5,3},{6,4},{7,5},{8,14},{9,15},{10,... | collective-permute-start | bytes 1179656 | tf_op jit(solution)/shard_map/ppermute | solution.py:26
  110.7 18.5 %all-to-all-start.2 = ((f32[16,8,8,128]{3,2,1,0:T(8,128)}), f32[16,8,8,128]{3,2,1,0:T(8,128)S(1)}, u32[]{:S(2)}, u32[]{:S(2)}) async-start(f32[16,8,8,128]{3,2,1,0:T(8,128)} %conv_kernel.1), calls=%async_computation.2 | async-start | bytes 1048576 | tf_op jit(solution)/shard_map/all_to_all | solution.py:551
  116.7 6.9 %collective-permute-start.16 = (f32[2,256,128]{2,1,0:T(8,128)S(1)}, f32[2,256,128]{2,1,0:T(8,128)S(1)}, u32[]{:S(2)}, u32[]{:S(2)}) collective-permute-start(f32[2,256,128]{2,1,0:T(8,128)S(1)} %get-tuple-element.61), channel_id=1, source_target_pairs={{0,6},{1,7},{2,0},{3,1},{4,2},{5,3},{6,4},{7,5},{8,14},{9,15},{10,... | collective-permute-start | bytes 786440 | tf_op jit(solution)/shard_map/ppermute | solution.py:26
  118.3 10.8 %collective-permute-start.17 = (f32[2,256,128]{2,1,0:T(8,128)S(1)}, f32[2,256,128]{2,1,0:T(8,128)S(1)}, u32[]{:S(2)}, u32[]{:S(2)}) collective-permute-start(f32[2,256,128]{2,1,0:T(8,128)S(1)} %get-tuple-element.62), channel_id=1, source_target_pairs={{0,1},{1,0},{2,3},{3,2},{4,5},{5,4},{6,7},{7,6},{8,9},{9,8},{10,11... | collective-permute-start | bytes 786440 | tf_op jit(solution)/shard_map/ppermute | solution.py:30
  118.9 10.1 %collective-permute-start.15 = (f32[2,256,128]{2,1,0:T(8,128)S(1)}, f32[2,256,128]{2,1,0:T(8,128)S(1)}, u32[]{:S(2)}, u32[]{:S(2)}) collective-permute-start(f32[2,256,128]{2,1,0:T(8,128)S(1)} %get-tuple-element.60.refs_7_), channel_id=1, source_target_pairs={{0,2},{1,3},{2,4},{3,5},{4,6},{5,7},{6,0},{7,1},{8,10},{9,11},{10,... | collective-permute-start | bytes 786440 | tf_op jit(solution)/shard_map/ppermute | solution.py:26

commit v10 on v9

--- a/solution.py
+++ b/solution.py
@@ -82,6 +82,7 @@
         ((next_l, 0), (next_l, 1)),
         ((next_l, 2), (next_l, 3)),
         (None, None),
+        (None, None),
     )
     for i, outs in enumerate(x_outs):
         pl.when(pl.program_id(0) == i)(
@@ -94,12 +95,9 @@
 def third_kernel(halves, place, act, weight, outs):
     (mine,) = outs
     for i in range(6):
-        x_outs = (None, None) if i < 4 else ((mine, i + 3), (mine, i + 5))
-        z_other = (mine, 6) if i == 5 else None
+        x_outs = (None, None) if i < 4 else ((mine, i + 2), (mine, i + 4))
         pl.when(pl.program_id(0) == i)(
-            functools.partial(
-                halves.fill, place, act, weight, i % 2, x_outs, (z_other, (mine, i))
-            )
+            functools.partial(halves.fill, place, act, weight, i % 2, x_outs, (None, (mine, i)))
         )
 
 
@@ -209,22 +207,20 @@
     )(*[value for value, _ in pieces], *after)
 
 
-def kv_other_kernel(own_k, own_v, r_k, r_v, l_k, l_v, late, out):
-    out[0:1] = own_k[...] + (r_k[...] + l_k[...])
-    out[1:2] = own_v[...] + (r_v[...] + l_v[...])
-    out[2:3] = late[...]
-
-
-def kv_last_kernel(m0, m1, m2, m3, g0, g1, g2, g3, next_r, next_l, out_r, out_l):
-    out_r[0:1] = m0[...] + g0[...] + next_r[...]
+def kv_second_sum_kernel(*refs):
+    m0, m1, m2, m3, g0, g1, g2, g3, z_r, z_l = refs[:10]
+    own_k, own_v, r_k, r_v, l_k, l_v, out_r, out_l, out_x = refs[10:]
+    out_r[0:1] = m0[...] + g0[...] + z_r[...]
     out_r[1:2] = m1[...] + g1[...]
     out_l[0:1] = m2[...] + g2[...]
-    out_l[1:2] = m3[...] + g3[...] + next_l[...]
-
-
-def kv_beside_kernel(m4, m5, g4, own_k, own_v, r_k, r_v, l_k, l_v, out):
+    out_l[1:2] = m3[...] + g3[...] + z_l[...]
+    out_x[0:1] = own_k[...] + (r_k[...] + l_k[...])
+    out_x[1:2] = own_v[...] + (r_v[...] + l_v[...])
+
+
+def kv_beside_kernel(m4, m5, g4, g5, own_k, own_v, r_k, r_v, l_k, l_v, out):
     out[0:1] = m4[...] + g4[...]
-    out[1:2] = m5[...]
+    out[1:2] = m5[...] + g5[...]
     out[2:3] = own_k[...] + (r_k[...] + l_k[...])
     out[3:4] = own_v[...] + (r_v[...] + l_v[...])
 
@@ -303,7 +299,7 @@
     )
     got_r, got_l, z_got = shift_x(send_r, 1), shift_x(send_l, -1), swap_z(z_send)
     next_r, next_l, z_send = make(
-        second_kernel, owner=1, steps=5, outs=[(5, "vmem")] * 3, after=(z_mine,)
+        second_kernel, owner=1, steps=6, outs=[(5, "vmem")] * 2 + [(6, "vmem")], after=(z_mine,)
     )
     next_r, next_l = sum_call(
         kv_first_sum_kernel, halves, [5, 5], [got_r, got_l, z_got, next_r, next_l, z_mine], []
@@ -313,35 +309,30 @@
         third_kernel,
         owner=1,
         steps=6,
-        outs=[(11, "vmem")],
+        outs=[(10, "vmem")],
         after=(next_r,) + ready[1:],
     )
-    next_r, next_l, z_five = shift_x(next_r, 1), shift_x(next_l, -1), swap_z(z_send)
-    (last_xz,) = piece_call(
-        kv_other_kernel,
+    next_r, next_l, z_six = shift_x(next_r, 1), shift_x(next_l, -1), swap_z(z_send)
+    last_r, last_l, last_x = piece_call(
+        kv_second_sum_kernel,
         halves,
-        [3],
-        [(mine, 7), (mine, 8), (next_r, 2), (next_r, 0), (next_l, 0), (next_l, 2), (mine, 6)],
-    )
-    last_r, last_l = piece_call(
-        kv_last_kernel,
-        halves,
-        [2, 2],
+        [2, 2, 2],
         [(mine, i) for i in range(4)]
-        + [(z_five, i) for i in range(4)]
-        + [(next_r, 4), (next_l, 4)],
-        after=(last_xz,) + ready,
+        + [(z_six, i) for i in range(4)]
+        + [(next_r, 4), (next_l, 4), (mine, 6), (mine, 7)]
+        + [(next_r, 2), (next_r, 0), (next_l, 0), (next_l, 2)],
+        after=ready,
     )
     (part,) = piece_call(
         kv_beside_kernel,
         halves,
         [4],
-        [(mine, 4), (mine, 5), (z_five, 4), (mine, 9), (mine, 10)]
+        [(mine, 4), (mine, 5), (z_six, 4), (z_six, 5), (mine, 8), (mine, 9)]
         + [(next_r, 3), (next_r, 1), (next_l, 1), (next_l, 3)],
         after=(last_r,),
     )
-    last_r, last_l, last_xz = shift_x(last_r, 1), shift_x(last_l, -1), swap_z(last_xz)
-    return (part, last_r, last_l, last_xz), part
+    last_r, last_l, last_x = shift_x(last_r, 1), shift_x(last_l, -1), swap_z(last_x)
+    return (part, last_r, last_l, last_x), part
 
 
 def project_query(halves, place, activations, weight, after):
@@ -399,10 +390,9 @@
 
 
 def summed(part, last_r, last_l, last_x):
-    z_total = [part[h] + (last_r[h] + last_l[h]) for h in range(2)]
-    if last_x.shape[0] == 3:
-        z_total[1] = z_total[1] + last_x[2]
-    return z_total + [part[2 + h] + last_x[h] for h in range(2)]
+    return [part[h] + (last_r[h] + last_l[h]) for h in range(2)] + [
+        part[2 + h] + last_x[h] for h in range(2)
+    ]
 
 
 def split_bf16(table):

time: 131 us -> 130 us (level)
  starting transfers between devices: 43.8 us -> 41 us
  waiting for transfers between devices: 33.1 us -> 35.6 us
    all_to_all x3, waiting for transfers between devices: 12.6 us -> 17.8 us  [exchange(): return lax.all_to_all(value, 'seq', split_axis=0, concat_axis=0, tiled=True)]
    ppermute x12, waiting for transfers between devices: 13.4 us -> 9.65 us  [shift_x(): lax.ppermute(value, 'chan', [(i, (i + 2 * step) % 8) for i in range(8)])]
    ppermute x12, starting transfers between devices: 17 us -> 13.5 us  [shift_x(): lax.ppermute(value, 'chan', [(i, (i + 2 * step) % 8) for i in range(8)])]
    all_to_all x3, starting transfers between devices: 21.6 us -> 24.2 us  [exchange(): return lax.all_to_all(value, 'seq', split_axis=0, concat_axis=0, tiled=True)]
    ppermute x6, starting transfers between devices: 5.2 us -> 3.31 us  [swap_z(): return lax.ppermute(value, 'chan', [(i, i ^ 1) for i in range(8)])]
    pallas_call x3 -> x2, Pallas kernels: 5.9 us -> 4.38 us  [piece_call(): pl.pallas_call(body, grid=(halves.rows // tile,), in_specs=[spec(index) f...]
  transfers between devices with their start and end apart: 21 -> 21, of which waited for: 10 -> 10; matrix products, arithmetic and copies ran while one was open for 0% -> 0% of each run, Pallas kernels for 35% -> 34%
where the time goes in v10:
time: 130 us; the launch traced here: 129 us
  Pallas kernels  51.6 us (40%)
  starting transfers between devices  41 us (32%)
  waiting for transfers between devices  35.6 us (27%)
    all_to_all x3, starting transfers between devices, exchange(): return lax.all_to_all(value, 'seq', split_axis=0, concat_axis=0, tiled=True)  24.2 us
    pallas_call x3, Pallas kernels, project(): pl.pallas_call(body, grid_spec=pltpu.PrefetchScalarGridSpec(num_scalar_pr...  19.2 us
    all_to_all x3, waiting for transfers between devices, exchange(): return lax.all_to_all(value, 'seq', split_axis=0, concat_axis=0, tiled=True)  17.8 us
    ppermute x12, starting transfers between devices, shift_x(): lax.ppermute(value, 'chan', [(i, (i + 2 * step) % 8) for i in range(8)])  13.5 us
    pallas_call x6, Pallas kernels, call(): pl.pallas_call(body, grid=(1,), in_specs=[pl.BlockSpec(memory_space=pltpu...  13.3 us
    ppermute x12, waiting for transfers between devices, shift_x(): lax.ppermute(value, 'chan', [(i, (i + 2 * step) % 8) for i in range(8)])  9.65 us
    ppermute x6, waiting for transfers between devices, swap_z(): return lax.ppermute(value, 'chan', [(i, i ^ 1) for i in range(8)])  8.19 us
    pallas_call x1, Pallas kernels, project_query(): pl.pallas_call(query_project_kernel, grid_spec=pltpu.PrefetchScalarGridSp...  7.9 us
  transfers between devices with their start and end apart: 21, of which 10 were waited for; matrix products, arithmetic and copies ran while one was open for 0% of the time, Pallas kernels for 34%

profile of v10, /device:TPU:1, one launch (start us, length us, event | category | flops | bytes accessed | tf_op | source)
XLA Modules:
  0.0 129.5 jit_solution(10936237443303719055)
XLA Ops:
  0.0 0.1 stack.23.at.place
  0.1 3.8 %first_kernel.1 = (f32[2,512,128]{2,1,0:T(8,128)S(1)}, f32[2,512,128]{2,1,0:T(8,128)S(1)}, f32[2,512,128]{2,1,0:T(8,128)S(1)}, f32[2,512,128]{2,1,0:T(8,128)S(1)}) custom-call(s32[5]{0:T(128)S(1)} %stack.23.at.place, bf16[1024,1024]{1,0:T(8,128)(2,1)} %act.7, bf16[3,1024,1024]{2,1,0:T(8,128)(2,1)} %bitcast.10), custom_call_target="tpu_custom_call" | custom-call | tf_op jit(solution)/shard_map/first_kernel/pallas_call | solution.py:133
  3.9 2.1 %collective-permute-start = (f32[2,512,128]{2,1,0:T(8,128)S(1)}, f32[2,512,128]{2,1,0:T(8,128)S(1)}, u32[]{:S(2)}, u32[]{:S(2)}) collective-permute-start(f32[2,512,128]{2,1,0:T(8,128)S(1)} %get-tuple-element.35), channel_id=1, source_target_pairs={{0,2},{1,3},{2,4},{3,5},{4,6},{5,7},{6,0},{7,1},{8,10},{9,11},{10,... | collective-permute-start | bytes 1572872 | tf_op jit(solution)/shard_map/ppermute | solution.py:26
  6.0 1.4 %collective-permute-start.1 = (f32[2,512,128]{2,1,0:T(8,128)S(1)}, f32[2,512,128]{2,1,0:T(8,128)S(1)}, u32[]{:S(2)}, u32[]{:S(2)}) collective-permute-start(f32[2,512,128]{2,1,0:T(8,128)S(1)} %get-tuple-element.36), channel_id=1, source_target_pairs={{0,6},{1,7},{2,0},{3,1},{4,2},{5,3},{6,4},{7,5},{8,14},{9,15},{10,... | collective-permute-start | bytes 1572872 | tf_op jit(solution)/shard_map/ppermute | solution.py:26
  7.4 1.8 %collective-permute-start.2 = (f32[2,512,128]{2,1,0:T(8,128)S(1)}, f32[2,512,128]{2,1,0:T(8,128)S(1)}, u32[]{:S(2)}, u32[]{:S(2)}) collective-permute-start(f32[2,512,128]{2,1,0:T(8,128)S(1)} %get-tuple-element.37), channel_id=1, source_target_pairs={{0,1},{1,0},{2,3},{3,2},{4,5},{5,4},{6,7},{7,6},{8,9},{9,8},{10,11... | collective-permute-start | bytes 1572872 | tf_op jit(solution)/shard_map/ppermute | solution.py:30
  9.2 8.4 %second_kernel.1 = (f32[5,512,128]{2,1,0:T(8,128)S(1)}, f32[5,512,128]{2,1,0:T(8,128)S(1)}, f32[6,512,128]{2,1,0:T(8,128)}) custom-call(s32[5]{0:T(128)S(1)} %stack.23.at.place, bf16[1024,1024]{1,0:T(8,128)(2,1)} %act.7, bf16[3,1024,1024]{2,1,0:T(8,128)(2,1)} %bitcast.11, f32[2,512,128]{2,1,0:T(8,128)S(1)} %get-tuple-element.38.refs_0_.refs_5_), custom_call_target="tpu_custom_call" | custom-call | tf_op jit(solution)/shard_map/second_kernel/pallas_call | solution.py:133
  17.5 1.0 collective-permute-done.refs_0_
  18.5 1.6 %collective-permute-done.2.refs_2_ = f32[2,512,128]{2,1,0:T(8,128)S(1)} collective-permute-done((f32[2,512,128]{2,1,0:T(8,128)S(1)}, f32[2,512,128]{2,1,0:T(8,128)S(1)}, u32[]{:S(2)}, u32[]{:S(2)}) %collective-permute-start.2) | collective-permute-done | bytes 524320 | tf_op jit(solution)/shard_map/ppermute | solution.py:30
  20.1 1.8 %kv_first_sum_kernel.1 = (f32[5,512,128]{2,1,0:T(8,128)}, f32[5,512,128]{2,1,0:T(8,128)}) custom-call(f32[2,512,128]{2,1,0:T(8,128)S(1)} %collective-permute-done.refs_0_, f32[2,512,128]{2,1,0:T(8,128)S(1)} %collective-permute-done.1.refs_1_, f32[2,512,128]{2,1,0:T(8,128)S(1)} %collective-permute-done.2.refs_2_, ...), custom_call_target="tpu_custom_call" | custom-call | tf_op jit(solution)/shard_map/kv_first_sum_kernel/pallas_call | solution.py:160
  22.0 1.2 collective-permute-start.5
  23.1 0.3 collective-permute-start.4
  23.4 1.2 taps_turn_kernel.1
  24.6 11.3 %all-to-all-start = ((f32[16,8,8,128]{3,2,1,0:T(8,128)}), f32[16,8,8,128]{3,2,1,0:T(8,128)}, u32[]{:S(2)}, u32[]{:S(2)}) async-start(f32[16,8,8,128]{3,2,1,0:T(8,128)} %bitcast.14), calls=%async_computation | async-start | bytes 1048576 | tf_op jit(solution)/shard_map/all_to_all | solution.py:541
  35.9 7.9 %query_project_kernel.1 = (f32[4,256,128]{2,1,0:T(8,128)}, f32[4,256,128]{2,1,0:T(8,128)}, f32[2,256,128]{2,1,0:T(8,128)}, f32[2,256,128]{2,1,0:T(8,128)}, f32[3...) custom-call(s32[5]{0:T(128)S(1)} %stack.23.at.place, ...), custom_call_target="tpu_custom_call" | custom-call | tf_op jit(solution)/shard_map/query_project_kernel/pallas_call | solution.py:341
  43.8 1.0 copy-done.3
  44.8 6.9 %third_kernel.1.refs_0_.refs_1_.refs_2_.refs_3_.refs_10_.refs_11_.refs_4_.refs_5_ = f32[10,512,128]{2,1,0:T(8,128)S(1)} custom-call(s32[5]{0:T(128)S(1)} %stack.23.at.place, bf16[1024,1024]{1,0:T(8,128)(2,1)} %act.7, bf16[3,1024,1024]{2,1,0:T(8,128)(2,1)} %bitcast.13, f32[5,512,128]{2,1,0:T(8,128)} %get-tuple-element.41.refs_0_.refs_1_, ...), custom_call_target="tpu_custom_call" | custom-call | tf_op jit(solution)/shard_map/third_kernel/pallas_call | solution.py:133
  51.8 12.3 %all-to-all-done.refs_16_.refs_0_ = f32[16,8,8,128]{3,2,1,0:T(8,128)} async-done(((f32[16,8,8,128]{3,2,1,0:T(8,128)}), f32[16,8,8,128]{3,2,1,0:T(8,128)}, u32[]{:S(2)}, u32[]{:S(2)}) %all-to-all-start) | async-done | bytes 524320 | tf_op jit(solution)/shard_map/all_to_all | solution.py:541
  64.1 0.0 collective-permute-done.3.refs_4_.refs_5_.refs_6_.refs_7_.refs_2_.refs_3_
  64.1 0.0 collective-permute-done.5.refs_9_.refs_14_.refs_15_.refs_8_
  64.1 2.8 %kv_second_sum_kernel.1 = (f32[2,512,128]{2,1,0:T(8,128)}, f32[2,512,128]{2,1,0:T(8,128)}, f32[2,512,128]{2,1,0:T(8,128)}) custom-call(f32[10,512,128]{2,1,0:T(8,128)S(1)} %third_kernel.1.refs_0_.refs_1_.refs_2_.refs_3_.refs_10_.refs_11_.refs_4_.refs_5_, f32[10,512,128]{2,1,0:T(8,128)S(1)} %third_kernel.1.refs_0_.refs_1_.refs_2_.refs_3_.refs_10_.refs_11_.refs_4_.refs_5_, ...), custom_call_target="tpu_custom_call" | custom-call | tf_op jit(solution)/shard_map/kv_second_sum_kernel/pallas_call | solution.py:198
  66.9 1.3 %collective-permute-start.7 = (f32[2,512,128]{2,1,0:T(8,128)}, f32[2,512,128]{2,1,0:T(8,128)}, u32[]{:S(2)}, u32[]{:S(2)}) collective-permute-start(f32[2,512,128]{2,1,0:T(8,128)} %get-tuple-element.46), channel_id=1, source_target_pairs={{0,6},{1,7},{2,0},{3,1},{4,2},{5,3},{6,4},{7,5},{8,14},{9,15},{10,... | collective-permute-start | bytes 1572872 | tf_op jit(solution)/shard_map/ppermute | solution.py:26
  68.2 0.0 collective-permute-start.8
  68.2 0.2 collective-permute-start.6
  68.4 1.6 %kv_beside_kernel.1.refs_7_.refs_0_ = f32[4,512,128]{2,1,0:T(8,128)S(1)} custom-call(f32[10,512,128]{2,1,0:T(8,128)S(1)} %third_kernel.1.refs_0_.refs_1_.refs_2_.refs_3_.refs_10_.refs_11_.refs_4_.refs_5_, f32[10,512,128]{2,1,0:T(8,128)S(1)} %third_kernel.1.refs_0_.refs_1_.refs_2_.refs_3_.refs_10_.refs_11_.refs_4_.refs_5_, ...), custom_call_target="tpu_custom_call" | custom-call | tf_op jit(solution)/shard_map/kv_beside_kernel/pallas_call | solution.py:198
  70.0 3.6 %taps_kernel.1.refs_4_.refs_1_ = f32[1024,256]{1,0:T(8,128)} custom-call(f32[16,8,8,128]{3,2,1,0:T(8,128)} %all-to-all-done.refs_16_.refs_0_, bf16[256,128]{1,0:T(8,128)(2,1)} %constant.72.clone.refs_1_.refs_2_, bf16[256,128]{1,0:T(8,128)(2,1)} %constant.73.clone.refs_2_.refs_3_, f32[128,128]{1,0:T(8,128)} %constant.74.clone.refs_3_.refs_4_, ...), custom_call_target="tpu_custom_call" | custom-call | tf_op jit(solution)/shard_map/taps_kernel/pallas_call | solution.py:524
  73.7 0.3 collective-permute-start.9
  74.0 2.7 %collective-permute-start.10 = (f32[4,256,128]{2,1,0:T(8,128)}, f32[4,256,128]{2,1,0:T(8,128)S(1)}, u32[]{:S(2)}, u32[]{:S(2)}) collective-permute-start(f32[4,256,128]{2,1,0:T(8,128)} %get-tuple-element.52), channel_id=1, source_target_pairs={{0,6},{1,7},{2,0},{3,1},{4,2},{5,3},{6,4},{7,5},{8,14},{9,15},{10,... | collective-permute-start | bytes 1572872 | tf_op jit(solution)/shard_map/ppermute | solution.py:26
  76.6 3.8 %collective-permute-done.7.refs_2_ = f32[2,512,128]{2,1,0:T(8,128)} collective-permute-done((f32[2,512,128]{2,1,0:T(8,128)}, f32[2,512,128]{2,1,0:T(8,128)}, u32[]{:S(2)}, u32[]{:S(2)}) %collective-permute-start.7) | collective-permute-done | bytes 524320 | tf_op jit(solution)/shard_map/ppermute | solution.py:26
  80.5 0.9 collective-permute-done.8.refs_3_
  81.4 1.2 collective-permute-done.6.refs_1_
  82.6 2.5 %kv_kernel.1 = f32[128,8,128]{2,1,0:T(8,128)} custom-call(f32[4,512,128]{2,1,0:T(8,128)S(1)} %copy-done.2, f32[2,512,128]{2,1,0:T(8,128)} %collective-permute-done.6.refs_1_, f32[2,512,128]{2,1,0:T(8,128)} %collective-permute-done.7.refs_2_, f32[2,512,128]{2,1,0:T(8,128)} %collective-permute-done.8.refs_3_, f32[1024,256]{1,0:T(8,128)S(1)} %copy-done), custom_call_target="tpu_custom_call" | custom-call | tf_op jit(solution)/shard_map/kv_kernel/pallas_call | solution.py:524
  85.1 8.2 %all-to-all-start.1 = ((f32[16,8,8,128]{3,2,1,0:T(8,128)}), f32[16,8,8,128]{3,2,1,0:T(8,128)S(1)}, u32[]{:S(2)}, u32[]{:S(2)}) async-start(f32[16,8,8,128]{3,2,1,0:T(8,128)} %bitcast.15), calls=%async_computation.1 | async-start | bytes 1048576 | tf_op jit(solution)/shard_map/all_to_all | solution.py:541
  93.4 0.6 collective-permute-start.14
  94.0 2.4 %first_sum_kernel.1 = (f32[3,256,128]{2,1,0:T(8,128)}, f32[3,256,128]{2,1,0:T(8,128)}) custom-call(f32[4,256,128]{2,1,0:T(8,128)S(1)} %collective-permute-done.9.refs_0_.refs_2_, f32[4,256,128]{2,1,0:T(8,128)S(1)} %collective-permute-done.10.refs_1_.refs_3_, f32[3,256,128]{2,1,0:T(8,128)S(1)} %collective-permute-done.11.refs_2_.refs_4_, ...), custom_call_target="tpu_custom_call" | custom-call | tf_op jit(solution)/shard_map/first_sum_kernel/pallas_call | solution.py:160
  96.4 2.7 %collective-permute-start.13 = (f32[3,256,128]{2,1,0:T(8,128)}, f32[3,256,128]{2,1,0:T(8,128)S(1)}, u32[]{:S(2)}, u32[]{:S(2)}) collective-permute-start(f32[3,256,128]{2,1,0:T(8,128)} %get-tuple-element.58), channel_id=1, source_target_pairs={{0,6},{1,7},{2,0},{3,1},{4,2},{5,3},{6,4},{7,5},{8,14},{9,15},{10,... | collective-permute-start | bytes 1179656 | tf_op jit(solution)/shard_map/ppermute | solution.py:26
  99.0 5.5 %all-to-all-done.1.refs_0_ = f32[16,8,8,128]{3,2,1,0:T(8,128)S(1)} async-done(((f32[16,8,8,128]{3,2,1,0:T(8,128)}), f32[16,8,8,128]{3,2,1,0:T(8,128)S(1)}, u32[]{:S(2)}, u32[]{:S(2)}) %all-to-all-start.1) | async-done | bytes 524320 | tf_op jit(solution)/shard_map/all_to_all | solution.py:541
  104.5 4.7 %conv_kernel.1 = f32[16,8,8,128]{3,2,1,0:T(8,128)} custom-call(f32[16,8,8,128]{3,2,1,0:T(8,128)S(1)} %all-to-all-done.1.refs_0_, f32[1024,256]{1,0:T(8,128)} %taps_kernel.1.refs_4_.refs_1_, bf16[256,128]{1,0:T(8,128)(2,1)} %constant.72.clone.refs_1_.refs_2_, bf16[256,128]{1,0:T(8,128)(2,1)} %constant.73.clone.refs_2_.refs_3_, ...), custom_call_target="tpu_custom_call" | custom-call | tf_op jit(solution)/shard_map/conv_kernel/pallas_call | solution.py:524
  109.3 4.7 %all-to-all-start.2 = ((f32[16,8,8,128]{3,2,1,0:T(8,128)}), f32[16,8,8,128]{3,2,1,0:T(8,128)S(1)}, u32[]{:S(2)}, u32[]{:S(2)}) async-start(f32[16,8,8,128]{3,2,1,0:T(8,128)} %conv_kernel.1), calls=%async_computation.2 | async-start | bytes 1048576 | tf_op jit(solution)/shard_map/all_to_all | solution.py:541
  113.9 0.9 collective-permute-done.14.refs_5_.refs_4_
  114.9 1.3 %query_second_sum_kernel.1 = (f32[2,256,128]{2,1,0:T(8,128)S(1)}, f32[2,256,128]{2,1,0:T(8,128)S(1)}, f32[2,256,128]{2,1,0:T(8,128)S(1)}) custom-call(f32[3,256,128]{2,1,0:T(8,128)S(1)} %collective-permute-done.12.refs_0_, f32[3,256,128]{2,1,0:T(8,128)S(1)} %collective-permute-done.13.refs_1_, f32[4,256,128]{2,1,0:T(8,128)S(1)} %collective-permute-done.9.refs_0_.refs_2_, ...), custom_call_target="tpu_custom_call" | custom-call | tf_op jit(solution)/shard_map/query_second_sum_kernel/pallas_call | solution.py:160
  116.2 0.1 collective-permute-start.16
  116.3 0.9 collective-permute-start.17
  117.2 1.4 %collective-permute-start.15 = (f32[2,256,128]{2,1,0:T(8,128)S(1)}, f32[2,256,128]{2,1,0:T(8,128)S(1)}, u32[]{:S(2)}, u32[]{:S(2)}) collective-permute-start(f32[2,256,128]{2,1,0:T(8,128)S(1)} %get-tuple-element.62.refs_7_), channel_id=1, source_target_pairs={{0,2},{1,3},{2,4},{3,5},{4,6},{5,7},{6,0},{7,1},{8,10},{9,11},{10,... | collective-permute-start | bytes 786440 | tf_op jit(solution)/shard_map/ppermute | solution.py:26
  118.6 1.3 %query_beside_kernel.1.refs_0_ = f32[4,256,128]{2,1,0:T(8,128)S(1)} custom-call(f32[3,256,128]{2,1,0:T(8,128)S(1)} %collective-permute-done.12.refs_0_, f32[3,256,128]{2,1,0:T(8,128)S(1)} %collective-permute-done.13.refs_1_, f32[4,256,128]{2,1,0:T(8,128)S(1)} %collective-permute-done.9.refs_0_.refs_2_, ...), custom_call_target="tpu_custom_call" | custom-call | tf_op jit(solution)/shard_map/query_beside_kernel/pallas_call | solution.py:160
  119.9 3.6 %collective-permute-done.16.refs_2_ = f32[2,256,128]{2,1,0:T(8,128)S(1)} collective-permute-done((f32[2,256,128]{2,1,0:T(8,128)S(1)}, f32[2,256,128]{2,1,0:T(8,128)S(1)}, u32[]{:S(2)}, u32[]{:S(2)}) %collective-permute-start.16) | collective-permute-done | bytes 262176 | tf_op jit(solution)/shard_map/ppermute | solution.py:26
  123.5 4.7 %collective-permute-done.17.refs_3_ = f32[2,256,128]{2,1,0:T(8,128)S(1)} collective-permute-done((f32[2,256,128]{2,1,0:T(8,128)S(1)}, f32[2,256,128]{2,1,0:T(8,128)S(1)}, u32[]{:S(2)}, u32[]{:S(2)}) %collective-permute-start.17) | collective-permute-done | bytes 262176 | tf_op jit(solution)/shard_map/ppermute | solution.py:30
  128.2 0.1 query_kernel.1.refs_1_
  128.3 1.1 gate_kernel.1
  (24 shorter events, 0.1 us)
Async XLA Ops:
  3.9 14.6 %collective-permute-start = (f32[2,512,128]{2,1,0:T(8,128)S(1)}, f32[2,512,128]{2,1,0:T(8,128)S(1)}, u32[]{:S(2)}, u32[]{:S(2)}) collective-permute-start(f32[2,512,128]{2,1,0:T(8,128)S(1)} %get-tuple-element.35), channel_id=1, source_target_pairs={{0,2},{1,3},{2,4},{3,5},{4,6},{5,7},{6,0},{7,1},{8,10},{9,11},{10,... | collective-permute-start | bytes 1572872 | tf_op jit(solution)/shard_map/ppermute | solution.py:26
  6.0 12.5 %collective-permute-start.1 = (f32[2,512,128]{2,1,0:T(8,128)S(1)}, f32[2,512,128]{2,1,0:T(8,128)S(1)}, u32[]{:S(2)}, u32[]{:S(2)}) collective-permute-start(f32[2,512,128]{2,1,0:T(8,128)S(1)} %get-tuple-element.36), channel_id=1, source_target_pairs={{0,6},{1,7},{2,0},{3,1},{4,2},{5,3},{6,4},{7,5},{8,14},{9,15},{10,... | collective-permute-start | bytes 1572872 | tf_op jit(solution)/shard_map/ppermute | solution.py:26
  7.4 12.7 %collective-permute-start.2 = (f32[2,512,128]{2,1,0:T(8,128)S(1)}, f32[2,512,128]{2,1,0:T(8,128)S(1)}, u32[]{:S(2)}, u32[]{:S(2)}) collective-permute-start(f32[2,512,128]{2,1,0:T(8,128)S(1)} %get-tuple-element.37), channel_id=1, source_target_pairs={{0,1},{1,0},{2,3},{3,2},{4,5},{5,4},{6,7},{7,6},{8,9},{9,8},{10,11... | collective-permute-start | bytes 1572872 | tf_op jit(solution)/shard_map/ppermute | solution.py:30
  17.5 46.5 %collective-permute-start.3 = (f32[6,512,128]{2,1,0:T(8,128)}, f32[6,512,128]{2,1,0:T(8,128)}, u32[]{:S(2)}, u32[]{:S(2)}) collective-permute-start(f32[6,512,128]{2,1,0:T(8,128)} %get-tuple-element.43), channel_id=1, source_target_pairs={{0,1},{1,0},{2,3},{3,2},{4,5},{5,4},{6,7},{7,6},{8,9},{9,8},{10,11... | collective-permute-start | bytes 4718600 | tf_op jit(solution)/shard_map/ppermute | solution.py:30
  20.1 3.3 %copy-start.5 = (f32[1024,128]{1,0:T(8,128)S(1)}, f32[1024,128]{1,0:T(8,128)}, u32[]{:S(2)}) copy-start(f32[1024,128]{1,0:T(8,128)} %refs_0_.1) | copy-start | bytes 1572868
  22.0 42.1 %collective-permute-start.5 = (f32[5,512,128]{2,1,0:T(8,128)}, f32[5,512,128]{2,1,0:T(8,128)}, u32[]{:S(2)}, u32[]{:S(2)}) collective-permute-start(f32[5,512,128]{2,1,0:T(8,128)} %get-tuple-element.44), channel_id=1, source_target_pairs={{0,6},{1,7},{2,0},{3,1},{4,2},{5,3},{6,4},{7,5},{8,14},{9,15},{10,... | collective-permute-start | bytes 3932168 | tf_op jit(solution)/shard_map/ppermute | solution.py:26
  23.1 40.9 %collective-permute-start.4 = (f32[5,512,128]{2,1,0:T(8,128)}, f32[5,512,128]{2,1,0:T(8,128)}, u32[]{:S(2)}, u32[]{:S(2)}) collective-permute-start(f32[5,512,128]{2,1,0:T(8,128)} %get-tuple-element.41.refs_0_.refs_1_), channel_id=1, source_target_pairs={{0,2},{1,3},{2,4},{3,5},{4,6},{5,7},{6,0},{7,1},{8,10},{9,11},{10,... | collective-permute-start | bytes 3932168 | tf_op jit(solution)/shard_map/ppermute | solution.py:26
  24.6 39.5 %all-to-all-start = ((f32[16,8,8,128]{3,2,1,0:T(8,128)}), f32[16,8,8,128]{3,2,1,0:T(8,128)}, u32[]{:S(2)}, u32[]{:S(2)}) async-start(f32[16,8,8,128]{3,2,1,0:T(8,128)} %bitcast.14), calls=%async_computation | async-start | bytes 1048576 | tf_op jit(solution)/shard_map/all_to_all | solution.py:541
  43.8 1.0 copy-start.3
  44.8 19.3 %copy-start.4 = (f32[4,256,128]{2,1,0:T(8,128)S(1)}, f32[4,256,128]{2,1,0:T(8,128)}, u32[]{:S(2)}) copy-start(f32[4,256,128]{2,1,0:T(8,128)} %get-tuple-element.42.refs_1_.refs_17_.refs_0_) | copy-start | bytes 1572868
  66.9 13.6 %collective-permute-start.7 = (f32[2,512,128]{2,1,0:T(8,128)}, f32[2,512,128]{2,1,0:T(8,128)}, u32[]{:S(2)}, u32[]{:S(2)}) collective-permute-start(f32[2,512,128]{2,1,0:T(8,128)} %get-tuple-element.46), channel_id=1, source_target_pairs={{0,6},{1,7},{2,0},{3,1},{4,2},{5,3},{6,4},{7,5},{8,14},{9,15},{10,... | collective-permute-start | bytes 1572872 | tf_op jit(solution)/shard_map/ppermute | solution.py:26
  68.2 13.2 %collective-permute-start.8 = (f32[2,512,128]{2,1,0:T(8,128)}, f32[2,512,128]{2,1,0:T(8,128)}, u32[]{:S(2)}, u32[]{:S(2)}) collective-permute-start(f32[2,512,128]{2,1,0:T(8,128)} %get-tuple-element.47), channel_id=1, source_target_pairs={{0,1},{1,0},{2,3},{3,2},{4,5},{5,4},{6,7},{7,6},{8,9},{9,8},{10,11... | collective-permute-start | bytes 1572872 | tf_op jit(solution)/shard_map/ppermute | solution.py:30
  68.2 14.4 %collective-permute-start.6 = (f32[2,512,128]{2,1,0:T(8,128)}, f32[2,512,128]{2,1,0:T(8,128)}, u32[]{:S(2)}, u32[]{:S(2)}) collective-permute-start(f32[2,512,128]{2,1,0:T(8,128)} %get-tuple-element.45.refs_10_), channel_id=1, source_target_pairs={{0,2},{1,3},{2,4},{3,5},{4,6},{5,7},{6,0},{7,1},{8,10},{9,11},{10,... | collective-permute-start | bytes 1572872 | tf_op jit(solution)/shard_map/ppermute | solution.py:26
  70.0 3.7 %copy-start.1 = (f32[4,512,128]{2,1,0:T(8,128)}, f32[4,512,128]{2,1,0:T(8,128)S(1)}, u32[]{:S(2)}) copy-start(f32[4,512,128]{2,1,0:T(8,128)S(1)} %kv_beside_kernel.1.refs_7_.refs_0_) | copy-start | bytes 3145732
  73.7 8.9 %copy-start = (f32[1024,256]{1,0:T(8,128)S(1)}, f32[1024,256]{1,0:T(8,128)}, u32[]{:S(2)}) copy-start(f32[1024,256]{1,0:T(8,128)} %taps_kernel.1.refs_4_.refs_1_) | copy-start | bytes 3145732
  73.7 8.9 %copy-start.2 = (f32[4,512,128]{2,1,0:T(8,128)S(1)}, f32[4,512,128]{2,1,0:T(8,128)}, u32[]{:S(2)}) copy-start(f32[4,512,128]{2,1,0:T(8,128)} %copy-done.1) | copy-start | bytes 3145732
  73.7 20.3 %collective-permute-start.9 = (f32[4,256,128]{2,1,0:T(8,128)}, f32[4,256,128]{2,1,0:T(8,128)S(1)}, u32[]{:S(2)}, u32[]{:S(2)}) collective-permute-start(f32[4,256,128]{2,1,0:T(8,128)} %get-tuple-element.51), channel_id=1, source_target_pairs={{0,2},{1,3},{2,4},{3,5},{4,6},{5,7},{6,0},{7,1},{8,10},{9,11},{10,... | collective-permute-start | bytes 1572872 | tf_op jit(solution)/shard_map/ppermute | solution.py:26
  74.0 20.0 %collective-permute-start.10 = (f32[4,256,128]{2,1,0:T(8,128)}, f32[4,256,128]{2,1,0:T(8,128)S(1)}, u32[]{:S(2)}, u32[]{:S(2)}) collective-permute-start(f32[4,256,128]{2,1,0:T(8,128)} %get-tuple-element.52), channel_id=1, source_target_pairs={{0,6},{1,7},{2,0},{3,1},{4,2},{5,3},{6,4},{7,5},{8,14},{9,15},{10,... | collective-permute-start | bytes 1572872 | tf_op jit(solution)/shard_map/ppermute | solution.py:26
  80.5 13.5 %collective-permute-start.11 = (f32[3,256,128]{2,1,0:T(8,128)}, f32[3,256,128]{2,1,0:T(8,128)S(1)}, u32[]{:S(2)}, u32[]{:S(2)}) collective-permute-start(f32[3,256,128]{2,1,0:T(8,128)} %get-tuple-element.53), channel_id=1, source_target_pairs={{0,1},{1,0},{2,3},{3,2},{4,5},{5,4},{6,7},{7,6},{8,9},{9,8},{10,11... | collective-permute-start | bytes 1179656 | tf_op jit(solution)/shard_map/ppermute | solution.py:30
  85.1 19.4 %all-to-all-start.1 = ((f32[16,8,8,128]{3,2,1,0:T(8,128)}), f32[16,8,8,128]{3,2,1,0:T(8,128)S(1)}, u32[]{:S(2)}, u32[]{:S(2)}) async-start(f32[16,8,8,128]{3,2,1,0:T(8,128)} %bitcast.15), calls=%async_computation.1 | async-start | bytes 1048576 | tf_op jit(solution)/shard_map/all_to_all | solution.py:541
  93.4 21.5 %collective-permute-start.14 = (f32[5,256,128]{2,1,0:T(8,128)}, f32[5,256,128]{2,1,0:T(8,128)S(1)}, u32[]{:S(2)}, u32[]{:S(2)}) collective-permute-start(f32[5,256,128]{2,1,0:T(8,128)} %get-tuple-element.59), channel_id=1, source_target_pairs={{0,1},{1,0},{2,3},{3,2},{4,5},{5,4},{6,7},{7,6},{8,9},{9,8},{10,11... | collective-permute-start | bytes 1966088 | tf_op jit(solution)/shard_map/ppermute | solution.py:30
  96.4 18.5 %collective-permute-start.12 = (f32[3,256,128]{2,1,0:T(8,128)}, f32[3,256,128]{2,1,0:T(8,128)S(1)}, u32[]{:S(2)}, u32[]{:S(2)}) collective-permute-start(f32[3,256,128]{2,1,0:T(8,128)} %get-tuple-element.57), channel_id=1, source_target_pairs={{0,2},{1,3},{2,4},{3,5},{4,6},{5,7},{6,0},{7,1},{8,10},{9,11},{10,... | collective-permute-start | bytes 1179656 | tf_op jit(solution)/shard_map/ppermute | solution.py:26
  96.4 18.5 %collective-permute-start.13 = (f32[3,256,128]{2,1,0:T(8,128)}, f32[3,256,128]{2,1,0:T(8,128)S(1)}, u32[]{:S(2)}, u32[]{:S(2)}) collective-permute-start(f32[3,256,128]{2,1,0:T(8,128)} %get-tuple-element.58), channel_id=1, source_target_pairs={{0,6},{1,7},{2,0},{3,1},{4,2},{5,3},{6,4},{7,5},{8,14},{9,15},{10,... | collective-permute-start | bytes 1179656 | tf_op jit(solution)/shard_map/ppermute | solution.py:26
  109.3 19.1 %all-to-all-start.2 = ((f32[16,8,8,128]{3,2,1,0:T(8,128)}), f32[16,8,8,128]{3,2,1,0:T(8,128)S(1)}, u32[]{:S(2)}, u32[]{:S(2)}) async-start(f32[16,8,8,128]{3,2,1,0:T(8,128)} %conv_kernel.1), calls=%async_computation.2 | async-start | bytes 1048576 | tf_op jit(solution)/shard_map/all_to_all | solution.py:541
  116.2 7.3 %collective-permute-start.16 = (f32[2,256,128]{2,1,0:T(8,128)S(1)}, f32[2,256,128]{2,1,0:T(8,128)S(1)}, u32[]{:S(2)}, u32[]{:S(2)}) collective-permute-start(f32[2,256,128]{2,1,0:T(8,128)S(1)} %get-tuple-element.63), channel_id=1, source_target_pairs={{0,6},{1,7},{2,0},{3,1},{4,2},{5,3},{6,4},{7,5},{8,14},{9,15},{10,... | collective-permute-start | bytes 786440 | tf_op jit(solution)/shard_map/ppermute | solution.py:26
  116.3 11.9 %collective-permute-start.17 = (f32[2,256,128]{2,1,0:T(8,128)S(1)}, f32[2,256,128]{2,1,0:T(8,128)S(1)}, u32[]{:S(2)}, u32[]{:S(2)}) collective-permute-start(f32[2,256,128]{2,1,0:T(8,128)S(1)} %get-tuple-element.64), channel_id=1, source_target_pairs={{0,1},{1,0},{2,3},{3,2},{4,5},{5,4},{6,7},{7,6},{8,9},{9,8},{10,11... | collective-permute-start | bytes 786440 | tf_op jit(solution)/shard_map/ppermute | solution.py:30
  117.2 11.0 %collective-permute-start.15 = (f32[2,256,128]{2,1,0:T(8,128)S(1)}, f32[2,256,128]{2,1,0:T(8,128)S(1)}, u32[]{:S(2)}, u32[]{:S(2)}) collective-permute-start(f32[2,256,128]{2,1,0:T(8,128)S(1)} %get-tuple-element.62.refs_7_), channel_id=1, source_target_pairs={{0,2},{1,3},{2,4},{3,5},{4,6},{5,7},{6,0},{7,1},{8,10},{9,11},{10,... | collective-permute-start | bytes 786440 | tf_op jit(solution)/shard_map/ppermute | solution.py:26

commit v11 on v10

--- a/solution.py
+++ b/solution.py
@@ -310,7 +310,7 @@
         owner=1,
         steps=6,
         outs=[(10, "vmem")],
-        after=(next_r,) + ready[1:],
+        after=(next_r,) + ready,
     )
     next_r, next_l, z_six = shift_x(next_r, 1), shift_x(next_l, -1), swap_z(z_send)
     last_r, last_l, last_x = piece_call(
@@ -430,15 +430,11 @@
     return dot(left[0], right[0]) + (dot(left[0], right[1]) + dot(left[1], right[0]))
 
 
-def forward(signal_ref, first, turn, second):
-    seqs, channels = signal_ref.shape[:2]
-    rows = seqs * signal_ref.shape[2]
-    signal = jnp.concatenate(
-        [signal_ref[:, c].reshape(rows, BLOCK) for c in range(channels)], axis=1
-    )
-    part = dot3(first, split_value(signal))
+def forward(signals, first, turn, second):
+    rows = signals[0].shape[0]
+    part = dot3(first, split_value(jnp.concatenate(signals, axis=1)))
     turned = []
-    for c in range(channels):
+    for c in range(len(signals)):
         real = part[:rows, c * BLOCK : (c + 1) * BLOCK]
         imag = part[rows:, c * BLOCK : (c + 1) * BLOCK]
         turned.append(
@@ -449,21 +445,23 @@
     return dot3(split_value(jnp.concatenate(turned, axis=0)), second)
 
 
-def taps_kernel(taps_ref, f_hi, f_lo, t_re, t_im, s_hi, s_lo, out_ref):
-    out_ref[...] = forward(
-        taps_ref, (f_hi[...], f_lo[...]), (t_re[...], t_im[...]), (s_hi[...], s_lo[...])
-    )
-
-
 def conv_kernel(
-    kv_ref, spec_ref, f_hi, f_lo, t_re, t_im, s_hi, s_lo, b_hi, b_lo, i_hi, i_lo, out_ref
+    both_ref, f_hi, f_lo, t_re, t_im, s_hi, s_lo, b_hi, b_lo, i_hi, i_lo, out_ref
 ):
-    seqs, channels, blocks, _ = kv_ref.shape
+    seqs, _, channels, blocks, _ = both_ref.shape
     rows = seqs * blocks
     turn = (t_re[...], t_im[...])
-    spectrum = forward(kv_ref, (f_hi[...], f_lo[...]), turn, (s_hi[...], s_lo[...]))
-    real, imag = spectrum[:, :BLOCK], spectrum[:, BLOCK:]
-    taps_real, taps_imag = spec_ref[:, :BLOCK], spec_ref[:, BLOCK:]
+    kv_spectrum, taps_spectrum = (
+        forward(
+            [both_ref[:, part, c].reshape(rows, BLOCK) for c in range(channels)],
+            (f_hi[...], f_lo[...]),
+            turn,
+            (s_hi[...], s_lo[...]),
+        )
+        for part in range(2)
+    )
+    real, imag = kv_spectrum[:, :BLOCK], kv_spectrum[:, BLOCK:]
+    taps_real, taps_imag = taps_spectrum[:, :BLOCK], taps_spectrum[:, BLOCK:]
     product = jnp.concatenate(
         [real * taps_real - imag * taps_imag, real * taps_imag + imag * taps_real], axis=1
     )
@@ -491,13 +489,15 @@
     turn_blocks(taps_ref, out_ref)
 
 
-def kv_kernel(*refs):
-    parts, out_ref, kv_ref = refs[:-2], refs[-2], refs[-1]
-    z_key, z_value, x_key, x_value = summed(*parts)
-    rows = z_key.shape[0]
-    kv_ref[:rows] = z_key * z_value
+def kv_kernel(part, last_r, last_l, last_x, taps, out_ref, kv_ref, turned_ref):
+    key, value, x_key, x_value = summed(part, last_r, last_l, last_x)
+    rows = key.shape[0]
+    kv_ref[:rows] = key * value
     kv_ref[rows:] = x_key * x_value
-    turn_blocks(kv_ref, out_ref)
+    turn_blocks(kv_ref, turned_ref)
+    shape = out_ref.shape[:1] + out_ref.shape[2:]
+    out_ref[:, 0] = turned_ref[...].reshape(shape)
+    out_ref[:, 1] = taps[...].reshape(shape)
 
 
 def query_kernel(*refs):
@@ -562,35 +562,28 @@
     kv_halves, q_halves = Halves(tokens, (1, 2)), Halves(tokens, (0,))
 
     def prepare(ready):
-        taps = call(taps_turn_kernel, turned_shape, filter_taps, after=(ready,), to_hbm=True)
-        hold["taps"] = exchange(taps.reshape(moved_shape))
+        hold["taps"] = call(taps_turn_kernel, turned_shape, filter_taps, after=(ready,))
         hold["query"] = project_query(q_halves, place, activations, weight, ready)
-        return hold["taps"], hold["query"][0]
+        return hold["query"][0], hold["taps"]
 
     kv_parts, kv_part = reduce_kv(kv_halves, place, activations, weight, prepare)
-    spectrum = call(
-        taps_kernel,
-        (owned * length // BLOCK, 2 * BLOCK),
+    both = call(
+        kv_kernel,
+        (seqs, 2, owned, blocks, BLOCK),
+        *kv_parts,
         hold["taps"],
-        tables=first + turn + second,
-        after=(kv_part,),
+        scratch=[
+            pltpu.VMEM((tokens, channels), jnp.float32),
+            pltpu.VMEM(turned_shape, jnp.float32),
+        ],
         to_hbm=True,
     )
-    kv = call(
-        kv_kernel,
-        turned_shape,
-        *kv_parts,
-        after=(spectrum,),
-        scratch=[pltpu.VMEM((tokens, channels), jnp.float32)],
-        to_hbm=True,
-    )
-    q_parts = reduce_query(q_halves, hold["query"], spectrum)
-    moved = exchange(kv.reshape(moved_shape))
+    q_parts = reduce_query(q_halves, hold["query"], kv_part)
     convolved = call(
         conv_kernel,
         moved_shape,
-        moved,
-        tables=(spectrum,) + first + turn + second + back + inverse,
+        exchange(both),
+        tables=first + turn + second + back + inverse,
         to_hbm=True,
     )
     query = call(query_kernel, (tokens, channels), *q_parts)

time: 130 us -> 137 us (1.054)
  waiting for transfers between devices: 35.6 us -> 56.8 us
  Pallas kernels: 51.6 us -> 40.2 us
  starting transfers between devices: 41 us -> 38.3 us
    ppermute x6, waiting for transfers between devices: 8.19 us -> 39.8 us  [swap_z(): return lax.ppermute(value, 'chan', [(i, i ^ 1) for i in range(8)])]
    all_to_all x3 -> x2, waiting for transfers between devices: 17.8 us -> 0.01 us  [exchange(): return lax.all_to_all(value, 'seq', split_axis=0, concat_axis=0, tiled=True)]
    ppermute x12, waiting for transfers between devices: 9.65 us -> 17 us  [shift_x(): lax.ppermute(value, 'chan', [(i, (i + 2 * step) % 8) for i in range(8)])]
    pallas_call x6 -> x5, Pallas kernels: 13.3 us -> 8.31 us  [call(): pl.pallas_call(body, grid=(1,), in_specs=[pl.BlockSpec(memory_space=pltpu...]
    all_to_all x3 -> x2, starting transfers between devices: 24.2 us -> 19.5 us  [exchange(): return lax.all_to_all(value, 'seq', split_axis=0, concat_axis=0, tiled=True)]
    pallas_call x2, Pallas kernels: 4.38 us -> 0.56 us  [piece_call(): pl.pallas_call(body, grid=(halves.rows // tile,), in_specs=[spec(index) f...]
    ppermute x6, starting transfers between devices: 3.31 us -> 5.44 us  [swap_z(): return lax.ppermute(value, 'chan', [(i, i ^ 1) for i in range(8)])]
    pallas_call x4, Pallas kernels: 6.85 us -> 5.42 us  [sum_call(): pl.pallas_call(body, grid=(halves.rows // tile,), in_specs=[pl.BlockSpec(...]
  transfers between devices with their start and end apart: 21 -> 20, of which waited for: 10 -> 9; matrix products, arithmetic and copies ran while one was open for 0% -> 0% of each run, Pallas kernels for 34% -> 25%
where the time goes in v11:
time: 137 us; the launch traced here: 136 us
  waiting for transfers between devices  56.8 us (41%)
  Pallas kernels  40.2 us (29%)
  starting transfers between devices  38.3 us (28%)
    ppermute x6, waiting for transfers between devices, swap_z(): return lax.ppermute(value, 'chan', [(i, i ^ 1) for i in range(8)])  39.8 us
    all_to_all x2, starting transfers between devices, exchange(): return lax.all_to_all(value, 'seq', split_axis=0, concat_axis=0, tiled=True)  19.5 us
    pallas_call x3, Pallas kernels, project(): pl.pallas_call(body, grid_spec=pltpu.PrefetchScalarGridSpec(num_scalar_pr...  18 us
    ppermute x12, waiting for transfers between devices, shift_x(): lax.ppermute(value, 'chan', [(i, (i + 2 * step) % 8) for i in range(8)])  17 us
    ppermute x12, starting transfers between devices, shift_x(): lax.ppermute(value, 'chan', [(i, (i + 2 * step) % 8) for i in range(8)])  13.3 us
    pallas_call x5, Pallas kernels, call(): pl.pallas_call(body, grid=(1,), in_specs=[pl.BlockSpec(memory_space=pltpu...  8.31 us
    pallas_call x1, Pallas kernels, project_query(): pl.pallas_call(query_project_kernel, grid_spec=pltpu.PrefetchScalarGridSp...  7.91 us
    ppermute x6, starting transfers between devices, swap_z(): return lax.ppermute(value, 'chan', [(i, i ^ 1) for i in range(8)])  5.44 us
  transfers between devices with their start and end apart: 20, of which 9 were waited for; matrix products, arithmetic and copies ran while one was open for 0% of the time, Pallas kernels for 25%

profile of v11, /device:TPU:1, one launch (start us, length us, event | category | flops | bytes accessed | tf_op | source)
XLA Modules:
  0.0 136.2 jit_solution(9727072708893317342)
XLA Ops:
  0.0 0.1 stack.23.at.place
  0.1 3.8 %first_kernel.1 = (f32[2,512,128]{2,1,0:T(8,128)S(1)}, f32[2,512,128]{2,1,0:T(8,128)S(1)}, f32[2,512,128]{2,1,0:T(8,128)S(1)}, f32[2,512,128]{2,1,0:T(8,128)S(1)}) custom-call(s32[5]{0:T(128)S(1)} %stack.23.at.place, bf16[1024,1024]{1,0:T(8,128)(2,1)} %act.7, bf16[3,1024,1024]{2,1,0:T(8,128)(2,1)} %bitcast.8), custom_call_target="tpu_custom_call" | custom-call | tf_op jit(solution)/shard_map/first_kernel/pallas_call | solution.py:133
  3.9 2.1 %collective-permute-start = (f32[2,512,128]{2,1,0:T(8,128)S(1)}, f32[2,512,128]{2,1,0:T(8,128)S(1)}, u32[]{:S(2)}, u32[]{:S(2)}) collective-permute-start(f32[2,512,128]{2,1,0:T(8,128)S(1)} %get-tuple-element.35), channel_id=1, source_target_pairs={{0,2},{1,3},{2,4},{3,5},{4,6},{5,7},{6,0},{7,1},{8,10},{9,11},{10,... | collective-permute-start | bytes 1572872 | tf_op jit(solution)/shard_map/ppermute | solution.py:26
  6.0 1.4 collective-permute-start.1
  7.4 1.8 %collective-permute-start.2 = (f32[2,512,128]{2,1,0:T(8,128)S(1)}, f32[2,512,128]{2,1,0:T(8,128)S(1)}, u32[]{:S(2)}, u32[]{:S(2)}) collective-permute-start(f32[2,512,128]{2,1,0:T(8,128)S(1)} %get-tuple-element.37), channel_id=1, source_target_pairs={{0,1},{1,0},{2,3},{3,2},{4,5},{5,4},{6,7},{7,6},{8,9},{9,8},{10,11... | collective-permute-start | bytes 1572872 | tf_op jit(solution)/shard_map/ppermute | solution.py:30
  9.2 7.3 %second_kernel.1 = (f32[5,512,128]{2,1,0:T(8,128)S(1)}, f32[5,512,128]{2,1,0:T(8,128)S(1)}, f32[6,512,128]{2,1,0:T(8,128)S(1)}) custom-call(s32[5]{0:T(128)S(1)} %stack.23.at.place, bf16[1024,1024]{1,0:T(8,128)(2,1)} %act.7, bf16[3,1024,1024]{2,1,0:T(8,128)(2,1)} %bitcast.9, f32[2,512,128]{2,1,0:T(8,128)S(1)} %get-tuple-element.38.refs_0_.refs_5_), custom_call_target="tpu_custom_call" | custom-call | tf_op jit(solution)/shard_map/second_kernel/pallas_call | solution.py:133
  16.4 0.1 collective-permute-start.3
  16.5 2.0 %collective-permute-done.refs_0_ = f32[2,512,128]{2,1,0:T(8,128)S(1)} collective-permute-done((f32[2,512,128]{2,1,0:T(8,128)S(1)}, f32[2,512,128]{2,1,0:T(8,128)S(1)}, u32[]{:S(2)}, u32[]{:S(2)}) %collective-permute-start) | collective-permute-done | bytes 524320 | tf_op jit(solution)/shard_map/ppermute | solution.py:26
  18.5 1.6 %collective-permute-done.2.refs_2_ = f32[2,512,128]{2,1,0:T(8,128)S(1)} collective-permute-done((f32[2,512,128]{2,1,0:T(8,128)S(1)}, f32[2,512,128]{2,1,0:T(8,128)S(1)}, u32[]{:S(2)}, u32[]{:S(2)}) %collective-permute-start.2) | collective-permute-done | bytes 524320 | tf_op jit(solution)/shard_map/ppermute | solution.py:30
  20.1 0.3 kv_first_sum_kernel.1
  20.4 1.2 collective-permute-start.5
  21.7 0.3 collective-permute-start.4
  22.0 7.9 %query_project_kernel.1 = (f32[4,256,128]{2,1,0:T(8,128)}, f32[4,256,128]{2,1,0:T(8,128)}, f32[2,256,128]{2,1,0:T(8,128)}, f32[2,256,128]{2,1,0:T(8,128)}, f32[3...) custom-call(s32[5]{0:T(128)S(1)} %stack.23.at.place, ...), custom_call_target="tpu_custom_call" | custom-call | tf_op jit(solution)/shard_map/query_project_kernel/pallas_call | solution.py:341
  29.9 0.4 taps_turn_kernel.1.refs_2_.refs_17_.refs_4_
  30.2 0.7 copy-done.1
  30.9 6.9 %third_kernel.1.refs_0_.refs_1_.refs_2_.refs_3_.refs_10_.refs_11_.refs_4_.refs_5_ = f32[10,512,128]{2,1,0:T(8,128)S(1)} custom-call(s32[5]{0:T(128)S(1)} %stack.23.at.place, bf16[1024,1024]{1,0:T(8,128)(2,1)} %act.7, bf16[3,1024,1024]{2,1,0:T(8,128)(2,1)} %bitcast.11, f32[5,512,128]{2,1,0:T(8,128)S(1)} %get-tuple-element.41.refs_0_.refs_1_, ...), custom_call_target="tpu_custom_call" | custom-call | tf_op jit(solution)/shard_map/third_kernel/pallas_call | solution.py:133
  37.8 16.0 %collective-permute-done.3.refs_4_.refs_5_.refs_6_.refs_7_.refs_2_.refs_3_ = f32[6,512,128]{2,1,0:T(8,128)S(1)} collective-permute-done((f32[6,512,128]{2,1,0:T(8,128)S(1)}, f32[6,512,128]{2,1,0:T(8,128)S(1)}, u32[]{:S(2)}, u32[]{:S(2)}) %collective-permute-start.3) | collective-permute-done | bytes 1572896 | tf_op jit(solution)/shard_map/ppermute | solution.py:30
  53.8 0.0 collective-permute-done.4.refs_8_.refs_12_.refs_13_.refs_6_.refs_7_
  53.8 0.3 kv_second_sum_kernel.1
  54.2 1.2 collective-permute-start.7
  55.4 1.3 collective-permute-start.8
  56.7 0.2 collective-permute-start.6
  56.9 0.2 kv_beside_kernel.1.refs_0_.refs_4_
  57.2 8.6 %collective-permute-done.7.refs_2_ = f32[2,512,128]{2,1,0:T(8,128)S(1)} collective-permute-done((f32[2,512,128]{2,1,0:T(8,128)S(1)}, f32[2,512,128]{2,1,0:T(8,128)S(1)}, u32[]{:S(2)}, u32[]{:S(2)}) %collective-permute-start.7) | collective-permute-done | bytes 524320 | tf_op jit(solution)/shard_map/ppermute | solution.py:26
  65.8 0.8 collective-permute-done.8.refs_3_
  66.6 2.0 %collective-permute-done.6.refs_1_ = f32[2,512,128]{2,1,0:T(8,128)S(1)} collective-permute-done((f32[2,512,128]{2,1,0:T(8,128)S(1)}, f32[2,512,128]{2,1,0:T(8,128)S(1)}, u32[]{:S(2)}, u32[]{:S(2)}) %collective-permute-start.6) | collective-permute-done | bytes 524320 | tf_op jit(solution)/shard_map/ppermute | solution.py:26
  68.6 1.5 %kv_kernel.1 = f32[16,2,8,8,128]{4,3,2,1,0:T(8,128)} custom-call(f32[4,512,128]{2,1,0:T(8,128)S(1)} %kv_beside_kernel.1.refs_0_.refs_4_, f32[2,512,128]{2,1,0:T(8,128)S(1)} %collective-permute-done.6.refs_1_, f32[2,512,128]{2,1,0:T(8,128)S(1)} %collective-permute-done.7.refs_2_, f32[2,512,128]{2,1,0:T(8,128)S(1)} %collective-permute-done.8.refs_3_, ...), custom_call_target="tpu_custom_call" | custom-call | tf_op jit(solution)/shard_map/kv_kernel/pallas_call | solution.py:524
  70.1 11.2 %all-to-all-start = ((f32[16,2,8,8,128]{4,3,2,1,0:T(8,128)}), f32[16,2,8,8,128]{4,3,2,1,0:T(8,128)S(1)}, u32[]{:S(2)}, u32[]{:S(2)}) async-start(f32[16,2,8,8,128]{4,3,2,1,0:T(8,128)} %kv_kernel.1), calls=%async_computation | async-start | bytes 2097152 | tf_op jit(solution)/shard_map/all_to_all | solution.py:541
  81.3 0.1 collective-permute-start.9
  81.3 2.7 %collective-permute-start.10 = (f32[4,256,128]{2,1,0:T(8,128)}, f32[4,256,128]{2,1,0:T(8,128)S(1)}, u32[]{:S(2)}, u32[]{:S(2)}) collective-permute-start(f32[4,256,128]{2,1,0:T(8,128)} %get-tuple-element.52), channel_id=1, source_target_pairs={{0,6},{1,7},{2,0},{3,1},{4,2},{5,3},{6,4},{7,5},{8,14},{9,15},{10,... | collective-permute-start | bytes 1572872 | tf_op jit(solution)/shard_map/ppermute | solution.py:26
  84.0 0.0 collective-permute-start.11
  84.0 1.5 %collective-permute-start.14 = (f32[5,256,128]{2,1,0:T(8,128)}, f32[5,256,128]{2,1,0:T(8,128)S(1)}, u32[]{:S(2)}, u32[]{:S(2)}) collective-permute-start(f32[5,256,128]{2,1,0:T(8,128)} %get-tuple-element.59), channel_id=1, source_target_pairs={{0,1},{1,0},{2,3},{3,2},{4,5},{5,4},{6,7},{7,6},{8,9},{9,8},{10,11... | collective-permute-start | bytes 1966088 | tf_op jit(solution)/shard_map/ppermute | solution.py:30
  85.5 17.0 %collective-permute-done.11.refs_2_.refs_4_ = f32[3,256,128]{2,1,0:T(8,128)S(1)} collective-permute-done((f32[3,256,128]{2,1,0:T(8,128)}, f32[3,256,128]{2,1,0:T(8,128)S(1)}, u32[]{:S(2)}, u32[]{:S(2)}) %collective-permute-start.11) | collective-permute-done | bytes 393248 | tf_op jit(solution)/shard_map/ppermute | solution.py:30
  102.5 0.0 collective-permute-done.9.refs_0_.refs_2_
  102.5 0.0 collective-permute-done.10.refs_1_.refs_3_
  102.5 2.5 %first_sum_kernel.1 = (f32[3,256,128]{2,1,0:T(8,128)}, f32[3,256,128]{2,1,0:T(8,128)}) custom-call(f32[4,256,128]{2,1,0:T(8,128)S(1)} %collective-permute-done.9.refs_0_.refs_2_, f32[4,256,128]{2,1,0:T(8,128)S(1)} %collective-permute-done.10.refs_1_.refs_3_, f32[3,256,128]{2,1,0:T(8,128)S(1)} %collective-permute-done.11.refs_2_.refs_4_, ...), custom_call_target="tpu_custom_call" | custom-call | tf_op jit(solution)/shard_map/first_sum_kernel/pallas_call | solution.py:160
  105.0 2.7 %collective-permute-start.13 = (f32[3,256,128]{2,1,0:T(8,128)}, f32[3,256,128]{2,1,0:T(8,128)S(1)}, u32[]{:S(2)}, u32[]{:S(2)}) collective-permute-start(f32[3,256,128]{2,1,0:T(8,128)} %get-tuple-element.58), channel_id=1, source_target_pairs={{0,6},{1,7},{2,0},{3,1},{4,2},{5,3},{6,4},{7,5},{8,14},{9,15},{10,... | collective-permute-start | bytes 1179656 | tf_op jit(solution)/shard_map/ppermute | solution.py:26
  107.7 5.3 %conv_kernel.1 = f32[16,8,8,128]{3,2,1,0:T(8,128)} custom-call(f32[16,2,8,8,128]{4,3,2,1,0:T(8,128)S(1)} %all-to-all-done.refs_0_, bf16[256,128]{1,0:T(8,128)(2,1)} %constant.72.clone.refs_1_, bf16[256,128]{1,0:T(8,128)(2,1)} %constant.73.clone.refs_2_, f32[128,128]{1,0:T(8,128)} %constant.74.clone.refs_3_, f32[128,128]{1,0:T(8,128)} %constant.75.clone.refs_4_, ...), custom_call_target="tpu_custom_call" | custom-call | tf_op jit(solution)/shard_map/conv_kernel/pallas_call | solution.py:524
  113.0 8.4 %all-to-all-start.1 = ((f32[16,8,8,128]{3,2,1,0:T(8,128)}), f32[16,8,8,128]{3,2,1,0:T(8,128)S(1)}, u32[]{:S(2)}, u32[]{:S(2)}) async-start(f32[16,8,8,128]{3,2,1,0:T(8,128)} %conv_kernel.1), calls=%async_computation.1 | async-start | bytes 1048576 | tf_op jit(solution)/shard_map/all_to_all | solution.py:541
  121.4 1.4 query_second_sum_kernel.1
  122.8 0.1 collective-permute-start.16
  122.8 0.8 collective-permute-start.17
  123.7 1.4 %collective-permute-start.15 = (f32[2,256,128]{2,1,0:T(8,128)S(1)}, f32[2,256,128]{2,1,0:T(8,128)S(1)}, u32[]{:S(2)}, u32[]{:S(2)}) collective-permute-start(f32[2,256,128]{2,1,0:T(8,128)S(1)} %get-tuple-element.62.refs_7_), channel_id=1, source_target_pairs={{0,2},{1,3},{2,4},{3,5},{4,6},{5,7},{6,0},{7,1},{8,10},{9,11},{10,... | collective-permute-start | bytes 786440 | tf_op jit(solution)/shard_map/ppermute | solution.py:26
  125.1 1.3 query_beside_kernel.1.refs_0_
  126.4 4.3 %collective-permute-done.16.refs_2_ = f32[2,256,128]{2,1,0:T(8,128)S(1)} collective-permute-done((f32[2,256,128]{2,1,0:T(8,128)S(1)}, f32[2,256,128]{2,1,0:T(8,128)S(1)}, u32[]{:S(2)}, u32[]{:S(2)}) %collective-permute-start.16) | collective-permute-done | bytes 262176 | tf_op jit(solution)/shard_map/ppermute | solution.py:26
  130.7 4.3 %collective-permute-done.17.refs_3_ = f32[2,256,128]{2,1,0:T(8,128)S(1)} collective-permute-done((f32[2,256,128]{2,1,0:T(8,128)S(1)}, f32[2,256,128]{2,1,0:T(8,128)S(1)}, u32[]{:S(2)}, u32[]{:S(2)}) %collective-permute-start.17) | collective-permute-done | bytes 262176 | tf_op jit(solution)/shard_map/ppermute | solution.py:30
  135.0 0.1 query_kernel.1.refs_1_
  135.1 1.1 gate_kernel.1
  (19 shorter events, 0.0 us)
Async XLA Ops:
  3.9 14.6 %collective-permute-start = (f32[2,512,128]{2,1,0:T(8,128)S(1)}, f32[2,512,128]{2,1,0:T(8,128)S(1)}, u32[]{:S(2)}, u32[]{:S(2)}) collective-permute-start(f32[2,512,128]{2,1,0:T(8,128)S(1)} %get-tuple-element.35), channel_id=1, source_target_pairs={{0,2},{1,3},{2,4},{3,5},{4,6},{5,7},{6,0},{7,1},{8,10},{9,11},{10,... | collective-permute-start | bytes 1572872 | tf_op jit(solution)/shard_map/ppermute | solution.py:26
  6.0 12.5 %collective-permute-start.1 = (f32[2,512,128]{2,1,0:T(8,128)S(1)}, f32[2,512,128]{2,1,0:T(8,128)S(1)}, u32[]{:S(2)}, u32[]{:S(2)}) collective-permute-start(f32[2,512,128]{2,1,0:T(8,128)S(1)} %get-tuple-element.36), channel_id=1, source_target_pairs={{0,6},{1,7},{2,0},{3,1},{4,2},{5,3},{6,4},{7,5},{8,14},{9,15},{10,... | collective-permute-start | bytes 1572872 | tf_op jit(solution)/shard_map/ppermute | solution.py:26
  7.4 12.7 %collective-permute-start.2 = (f32[2,512,128]{2,1,0:T(8,128)S(1)}, f32[2,512,128]{2,1,0:T(8,128)S(1)}, u32[]{:S(2)}, u32[]{:S(2)}) collective-permute-start(f32[2,512,128]{2,1,0:T(8,128)S(1)} %get-tuple-element.37), channel_id=1, source_target_pairs={{0,1},{1,0},{2,3},{3,2},{4,5},{5,4},{6,7},{7,6},{8,9},{9,8},{10,11... | collective-permute-start | bytes 1572872 | tf_op jit(solution)/shard_map/ppermute | solution.py:30
  16.4 37.4 %collective-permute-start.3 = (f32[6,512,128]{2,1,0:T(8,128)S(1)}, f32[6,512,128]{2,1,0:T(8,128)S(1)}, u32[]{:S(2)}, u32[]{:S(2)}) collective-permute-start(f32[6,512,128]{2,1,0:T(8,128)S(1)} %get-tuple-element.43), channel_id=1, source_target_pairs={{0,1},{1,0},{2,3},{3,2},{4,5},{5,4},{6,7},{7,6},{8,9},{9,8},{10,11... | collective-permute-start | bytes 4718600 | tf_op jit(solution)/shard_map/ppermute | solution.py:30
  20.4 33.4 %collective-permute-start.5 = (f32[5,512,128]{2,1,0:T(8,128)S(1)}, f32[5,512,128]{2,1,0:T(8,128)S(1)}, u32[]{:S(2)}, u32[]{:S(2)}) collective-permute-start(f32[5,512,128]{2,1,0:T(8,128)S(1)} %get-tuple-element.44), channel_id=1, source_target_pairs={{0,6},{1,7},{2,0},{3,1},{4,2},{5,3},{6,4},{7,5},{8,14},{9,15},{10,... | collective-permute-start | bytes 3932168 | tf_op jit(solution)/shard_map/ppermute | solution.py:26
  21.7 8.2 %copy-start.4 = (f32[1024,128]{1,0:T(8,128)S(1)}, f32[1024,128]{1,0:T(8,128)}, u32[]{:S(2)}) copy-start(f32[1024,128]{1,0:T(8,128)} %refs_0_.1) | copy-start | bytes 1572868
  21.7 32.2 %collective-permute-start.4 = (f32[5,512,128]{2,1,0:T(8,128)S(1)}, f32[5,512,128]{2,1,0:T(8,128)S(1)}, u32[]{:S(2)}, u32[]{:S(2)}) collective-permute-start(f32[5,512,128]{2,1,0:T(8,128)S(1)} %get-tuple-element.41.refs_0_.refs_1_), channel_id=1, source_target_pairs={{0,2},{1,3},{2,4},{3,5},{4,6},{5,7},{6,0},{7,1},{8,10},{9,11},{10,... | collective-permute-start | bytes 3932168 | tf_op jit(solution)/shard_map/ppermute | solution.py:26
  29.9 1.0 copy-start.1
  54.2 11.6 %collective-permute-start.7 = (f32[2,512,128]{2,1,0:T(8,128)S(1)}, f32[2,512,128]{2,1,0:T(8,128)S(1)}, u32[]{:S(2)}, u32[]{:S(2)}) collective-permute-start(f32[2,512,128]{2,1,0:T(8,128)S(1)} %get-tuple-element.46), channel_id=1, source_target_pairs={{0,6},{1,7},{2,0},{3,1},{4,2},{5,3},{6,4},{7,5},{8,14},{9,15},{10,... | collective-permute-start | bytes 1572872 | tf_op jit(solution)/shard_map/ppermute | solution.py:26
  55.4 11.2 %collective-permute-start.8 = (f32[2,512,128]{2,1,0:T(8,128)S(1)}, f32[2,512,128]{2,1,0:T(8,128)S(1)}, u32[]{:S(2)}, u32[]{:S(2)}) collective-permute-start(f32[2,512,128]{2,1,0:T(8,128)S(1)} %get-tuple-element.47), channel_id=1, source_target_pairs={{0,1},{1,0},{2,3},{3,2},{4,5},{5,4},{6,7},{7,6},{8,9},{9,8},{10,11... | collective-permute-start | bytes 1572872 | tf_op jit(solution)/shard_map/ppermute | solution.py:30
  56.7 11.9 %collective-permute-start.6 = (f32[2,512,128]{2,1,0:T(8,128)S(1)}, f32[2,512,128]{2,1,0:T(8,128)S(1)}, u32[]{:S(2)}, u32[]{:S(2)}) collective-permute-start(f32[2,512,128]{2,1,0:T(8,128)S(1)} %get-tuple-element.45.refs_10_), channel_id=1, source_target_pairs={{0,2},{1,3},{2,4},{3,5},{4,6},{5,7},{6,0},{7,1},{8,10},{9,11},{10,... | collective-permute-start | bytes 1572872 | tf_op jit(solution)/shard_map/ppermute | solution.py:26
  57.2 12.9 %copy-start = (f32[4,512,128]{2,1,0:T(8,128)}, f32[4,512,128]{2,1,0:T(8,128)S(1)}, u32[]{:S(2)}) copy-start(f32[4,512,128]{2,1,0:T(8,128)S(1)} %kv_beside_kernel.1.refs_0_.refs_4_) | copy-start | bytes 3145732
  70.1 37.6 %all-to-all-start = ((f32[16,2,8,8,128]{4,3,2,1,0:T(8,128)}), f32[16,2,8,8,128]{4,3,2,1,0:T(8,128)S(1)}, u32[]{:S(2)}, u32[]{:S(2)}) async-start(f32[16,2,8,8,128]{4,3,2,1,0:T(8,128)} %kv_kernel.1), calls=%async_computation | async-start | bytes 2097152 | tf_op jit(solution)/shard_map/all_to_all | solution.py:541
  81.3 21.3 %collective-permute-start.9 = (f32[4,256,128]{2,1,0:T(8,128)}, f32[4,256,128]{2,1,0:T(8,128)S(1)}, u32[]{:S(2)}, u32[]{:S(2)}) collective-permute-start(f32[4,256,128]{2,1,0:T(8,128)} %get-tuple-element.51), channel_id=1, source_target_pairs={{0,2},{1,3},{2,4},{3,5},{4,6},{5,7},{6,0},{7,1},{8,10},{9,11},{10,... | collective-permute-start | bytes 1572872 | tf_op jit(solution)/shard_map/ppermute | solution.py:26
  81.3 21.2 %collective-permute-start.10 = (f32[4,256,128]{2,1,0:T(8,128)}, f32[4,256,128]{2,1,0:T(8,128)S(1)}, u32[]{:S(2)}, u32[]{:S(2)}) collective-permute-start(f32[4,256,128]{2,1,0:T(8,128)} %get-tuple-element.52), channel_id=1, source_target_pairs={{0,6},{1,7},{2,0},{3,1},{4,2},{5,3},{6,4},{7,5},{8,14},{9,15},{10,... | collective-permute-start | bytes 1572872 | tf_op jit(solution)/shard_map/ppermute | solution.py:26
  84.0 18.5 %collective-permute-start.11 = (f32[3,256,128]{2,1,0:T(8,128)}, f32[3,256,128]{2,1,0:T(8,128)S(1)}, u32[]{:S(2)}, u32[]{:S(2)}) collective-permute-start(f32[3,256,128]{2,1,0:T(8,128)} %get-tuple-element.53), channel_id=1, source_target_pairs={{0,1},{1,0},{2,3},{3,2},{4,5},{5,4},{6,7},{7,6},{8,9},{9,8},{10,11... | collective-permute-start | bytes 1179656 | tf_op jit(solution)/shard_map/ppermute | solution.py:30
  84.0 37.3 %collective-permute-start.14 = (f32[5,256,128]{2,1,0:T(8,128)}, f32[5,256,128]{2,1,0:T(8,128)S(1)}, u32[]{:S(2)}, u32[]{:S(2)}) collective-permute-start(f32[5,256,128]{2,1,0:T(8,128)} %get-tuple-element.59), channel_id=1, source_target_pairs={{0,1},{1,0},{2,3},{3,2},{4,5},{5,4},{6,7},{7,6},{8,9},{9,8},{10,11... | collective-permute-start | bytes 1966088 | tf_op jit(solution)/shard_map/ppermute | solution.py:30
  102.5 2.5 %copy-start.2 = (f32[3,256,128]{2,1,0:T(8,128)}, f32[3,256,128]{2,1,0:T(8,128)S(1)}, u32[]{:S(2)}) copy-start(f32[3,256,128]{2,1,0:T(8,128)S(1)} %collective-permute-done.11.refs_2_.refs_4_) | copy-start | bytes 1179652
  105.0 16.3 %collective-permute-start.12 = (f32[3,256,128]{2,1,0:T(8,128)}, f32[3,256,128]{2,1,0:T(8,128)S(1)}, u32[]{:S(2)}, u32[]{:S(2)}) collective-permute-start(f32[3,256,128]{2,1,0:T(8,128)} %get-tuple-element.57), channel_id=1, source_target_pairs={{0,2},{1,3},{2,4},{3,5},{4,6},{5,7},{6,0},{7,1},{8,10},{9,11},{10,... | collective-permute-start | bytes 1179656 | tf_op jit(solution)/shard_map/ppermute | solution.py:26
  105.0 16.3 %collective-permute-start.13 = (f32[3,256,128]{2,1,0:T(8,128)}, f32[3,256,128]{2,1,0:T(8,128)S(1)}, u32[]{:S(2)}, u32[]{:S(2)}) collective-permute-start(f32[3,256,128]{2,1,0:T(8,128)} %get-tuple-element.58), channel_id=1, source_target_pairs={{0,6},{1,7},{2,0},{3,1},{4,2},{5,3},{6,4},{7,5},{8,14},{9,15},{10,... | collective-permute-start | bytes 1179656 | tf_op jit(solution)/shard_map/ppermute | solution.py:26
  113.0 8.4 %copy-start.3 = (f32[3,256,128]{2,1,0:T(8,128)S(1)}, f32[3,256,128]{2,1,0:T(8,128)}, u32[]{:S(2)}) copy-start(f32[3,256,128]{2,1,0:T(8,128)} %copy-done.2) | copy-start | bytes 1179652
  113.0 22.1 %all-to-all-start.1 = ((f32[16,8,8,128]{3,2,1,0:T(8,128)}), f32[16,8,8,128]{3,2,1,0:T(8,128)S(1)}, u32[]{:S(2)}, u32[]{:S(2)}) async-start(f32[16,8,8,128]{3,2,1,0:T(8,128)} %conv_kernel.1), calls=%async_computation.1 | async-start | bytes 1048576 | tf_op jit(solution)/shard_map/all_to_all | solution.py:541
  122.8 7.9 %collective-permute-start.16 = (f32[2,256,128]{2,1,0:T(8,128)S(1)}, f32[2,256,128]{2,1,0:T(8,128)S(1)}, u32[]{:S(2)}, u32[]{:S(2)}) collective-permute-start(f32[2,256,128]{2,1,0:T(8,128)S(1)} %get-tuple-element.63), channel_id=1, source_target_pairs={{0,6},{1,7},{2,0},{3,1},{4,2},{5,3},{6,4},{7,5},{8,14},{9,15},{10,... | collective-permute-start | bytes 786440 | tf_op jit(solution)/shard_map/ppermute | solution.py:26
  122.8 12.2 %collective-permute-start.17 = (f32[2,256,128]{2,1,0:T(8,128)S(1)}, f32[2,256,128]{2,1,0:T(8,128)S(1)}, u32[]{:S(2)}, u32[]{:S(2)}) collective-permute-start(f32[2,256,128]{2,1,0:T(8,128)S(1)} %get-tuple-element.64), channel_id=1, source_target_pairs={{0,1},{1,0},{2,3},{3,2},{4,5},{5,4},{6,7},{7,6},{8,9},{9,8},{10,11... | collective-permute-start | bytes 786440 | tf_op jit(solution)/shard_map/ppermute | solution.py:30
  123.7 11.3 %collective-permute-start.15 = (f32[2,256,128]{2,1,0:T(8,128)S(1)}, f32[2,256,128]{2,1,0:T(8,128)S(1)}, u32[]{:S(2)}, u32[]{:S(2)}) collective-permute-start(f32[2,256,128]{2,1,0:T(8,128)S(1)} %get-tuple-element.62.refs_7_), channel_id=1, source_target_pairs={{0,2},{1,3},{2,4},{3,5},{4,6},{5,7},{6,0},{7,1},{8,10},{9,11},{10,... | collective-permute-start | bytes 786440 | tf_op jit(solution)/shard_map/ppermute | solution.py:26

commit v12 on v9

--- a/solution.py
+++ b/solution.py
@@ -322,6 +322,7 @@
         halves,
         [3],
         [(mine, 7), (mine, 8), (next_r, 2), (next_r, 0), (next_l, 0), (next_l, 2), (mine, 6)],
+        after=(z_five,) + ready,
     )
     last_r, last_l = piece_call(
         kv_last_kernel,
@@ -330,7 +331,7 @@
         [(mine, i) for i in range(4)]
         + [(z_five, i) for i in range(4)]
         + [(next_r, 4), (next_l, 4)],
-        after=(last_xz,) + ready,
+        after=(last_xz,),
     )
     (part,) = piece_call(
         kv_beside_kernel,

time: 131 us -> 126 us (0.962)
  starting transfers between devices: 43.8 us -> 41.3 us
  waiting for transfers between devices: 33.1 us -> 30.6 us
    ppermute x12, starting transfers between devices: 17 us -> 12.9 us  [shift_x(): lax.ppermute(value, 'chan', [(i, (i + 2 * step) % 8) for i in range(8)])]
    ppermute x12, waiting for transfers between devices: 13.4 us -> 10.6 us  [shift_x(): lax.ppermute(value, 'chan', [(i, (i + 2 * step) % 8) for i in range(8)])]
    all_to_all x3, starting transfers between devices: 21.6 us -> 23.6 us  [exchange(): return lax.all_to_all(value, 'seq', split_axis=0, concat_axis=0, tiled=True)]
  transfers between devices with their start and end apart: 21 -> 21, of which waited for: 10 -> 10; matrix products, arithmetic and copies ran while one was open for 0% -> 0% of each run, Pallas kernels for 35% -> 36%
where the time goes in v12:
time: 126 us; the launch traced here: 125 us
  Pallas kernels  52.2 us (41%)
  starting transfers between devices  41.3 us (33%)
  waiting for transfers between devices  30.6 us (24%)
    all_to_all x3, starting transfers between devices, exchange(): return lax.all_to_all(value, 'seq', split_axis=0, concat_axis=0, tiled=True)  23.6 us
    pallas_call x3, Pallas kernels, project(): pl.pallas_call(body, grid_spec=pltpu.PrefetchScalarGridSpec(num_scalar_pr...  18.3 us
    pallas_call x6, Pallas kernels, call(): pl.pallas_call(body, grid=(1,), in_specs=[pl.BlockSpec(memory_space=pltpu...  13.4 us
    ppermute x12, starting transfers between devices, shift_x(): lax.ppermute(value, 'chan', [(i, (i + 2 * step) % 8) for i in range(8)])  12.9 us
    all_to_all x3, waiting for transfers between devices, exchange(): return lax.all_to_all(value, 'seq', split_axis=0, concat_axis=0, tiled=True)  11.7 us
    ppermute x12, waiting for transfers between devices, shift_x(): lax.ppermute(value, 'chan', [(i, (i + 2 * step) % 8) for i in range(8)])  10.6 us
    ppermute x6, waiting for transfers between devices, swap_z(): return lax.ppermute(value, 'chan', [(i, i ^ 1) for i in range(8)])  8.27 us
    pallas_call x1, Pallas kernels, project_query(): pl.pallas_call(query_project_kernel, grid_spec=pltpu.PrefetchScalarGridSp...  7.87 us
  transfers between devices with their start and end apart: 21, of which 10 were waited for; matrix products, arithmetic and copies ran while one was open for 0% of the time, Pallas kernels for 36%

profile of v12, /device:TPU:1, one launch (start us, length us, event | category | flops | bytes accessed | tf_op | source)
XLA Modules:
  0.0 125.4 jit_solution(3088532240538493115)
XLA Ops:
  0.0 0.1 stack.23.at.place
  0.1 3.8 %first_kernel.1 = (f32[2,512,128]{2,1,0:T(8,128)S(1)}, f32[2,512,128]{2,1,0:T(8,128)S(1)}, f32[2,512,128]{2,1,0:T(8,128)S(1)}, f32[2,512,128]{2,1,0:T(8,128)S(1)}) custom-call(s32[5]{0:T(128)S(1)} %stack.23.at.place, bf16[1024,1024]{1,0:T(8,128)(2,1)} %act.7, bf16[3,1024,1024]{2,1,0:T(8,128)(2,1)} %bitcast.10), custom_call_target="tpu_custom_call" | custom-call | tf_op jit(solution)/shard_map/first_kernel/pallas_call | solution.py:135
  3.9 2.1 %collective-permute-start = (f32[2,512,128]{2,1,0:T(8,128)S(1)}, f32[2,512,128]{2,1,0:T(8,128)S(1)}, u32[]{:S(2)}, u32[]{:S(2)}) collective-permute-start(f32[2,512,128]{2,1,0:T(8,128)S(1)} %get-tuple-element.34), channel_id=1, source_target_pairs={{0,2},{1,3},{2,4},{3,5},{4,6},{5,7},{6,0},{7,1},{8,10},{9,11},{10,... | collective-permute-start | bytes 1572872 | tf_op jit(solution)/shard_map/ppermute | solution.py:26
  6.0 1.4 %collective-permute-start.1 = (f32[2,512,128]{2,1,0:T(8,128)S(1)}, f32[2,512,128]{2,1,0:T(8,128)S(1)}, u32[]{:S(2)}, u32[]{:S(2)}) collective-permute-start(f32[2,512,128]{2,1,0:T(8,128)S(1)} %get-tuple-element.35), channel_id=1, source_target_pairs={{0,6},{1,7},{2,0},{3,1},{4,2},{5,3},{6,4},{7,5},{8,14},{9,15},{10,... | collective-permute-start | bytes 1572872 | tf_op jit(solution)/shard_map/ppermute | solution.py:26
  7.4 1.8 %collective-permute-start.2 = (f32[2,512,128]{2,1,0:T(8,128)S(1)}, f32[2,512,128]{2,1,0:T(8,128)S(1)}, u32[]{:S(2)}, u32[]{:S(2)}) collective-permute-start(f32[2,512,128]{2,1,0:T(8,128)S(1)} %get-tuple-element.36), channel_id=1, source_target_pairs={{0,1},{1,0},{2,3},{3,2},{4,5},{5,4},{6,7},{7,6},{8,9},{9,8},{10,11... | collective-permute-start | bytes 1572872 | tf_op jit(solution)/shard_map/ppermute | solution.py:30
  9.2 7.5 %second_kernel.1 = (f32[5,512,128]{2,1,0:T(8,128)S(1)}, f32[5,512,128]{2,1,0:T(8,128)S(1)}, f32[5,512,128]{2,1,0:T(8,128)}) custom-call(s32[5]{0:T(128)S(1)} %stack.23.at.place, bf16[1024,1024]{1,0:T(8,128)(2,1)} %act.7, bf16[3,1024,1024]{2,1,0:T(8,128)(2,1)} %bitcast.11, f32[2,512,128]{2,1,0:T(8,128)S(1)} %get-tuple-element.37.refs_0_.refs_5_), custom_call_target="tpu_custom_call" | custom-call | tf_op jit(solution)/shard_map/second_kernel/pallas_call | solution.py:135
  16.6 0.0 collective-permute-start.3
  16.7 1.9 %collective-permute-done.refs_0_ = f32[2,512,128]{2,1,0:T(8,128)S(1)} collective-permute-done((f32[2,512,128]{2,1,0:T(8,128)S(1)}, f32[2,512,128]{2,1,0:T(8,128)S(1)}, u32[]{:S(2)}, u32[]{:S(2)}) %collective-permute-start) | collective-permute-done | bytes 524320 | tf_op jit(solution)/shard_map/ppermute | solution.py:26
  18.5 1.6 %collective-permute-done.2.refs_2_ = f32[2,512,128]{2,1,0:T(8,128)S(1)} collective-permute-done((f32[2,512,128]{2,1,0:T(8,128)S(1)}, f32[2,512,128]{2,1,0:T(8,128)S(1)}, u32[]{:S(2)}, u32[]{:S(2)}) %collective-permute-start.2) | collective-permute-done | bytes 524320 | tf_op jit(solution)/shard_map/ppermute | solution.py:30
  20.1 1.8 %kv_first_sum_kernel.1 = (f32[5,512,128]{2,1,0:T(8,128)}, f32[5,512,128]{2,1,0:T(8,128)}) custom-call(f32[2,512,128]{2,1,0:T(8,128)S(1)} %collective-permute-done.refs_0_, f32[2,512,128]{2,1,0:T(8,128)S(1)} %collective-permute-done.1.refs_1_, f32[2,512,128]{2,1,0:T(8,128)S(1)} %collective-permute-done.2.refs_2_, ...), custom_call_target="tpu_custom_call" | custom-call | tf_op jit(solution)/shard_map/kv_first_sum_kernel/pallas_call | solution.py:162
  21.9 1.2 collective-permute-start.5
  23.1 0.3 collective-permute-start.4
  23.4 1.1 taps_turn_kernel.1
  24.5 11.8 %all-to-all-start = ((f32[16,8,8,128]{3,2,1,0:T(8,128)}), f32[16,8,8,128]{3,2,1,0:T(8,128)}, u32[]{:S(2)}, u32[]{:S(2)}) async-start(f32[16,8,8,128]{3,2,1,0:T(8,128)} %bitcast.15), calls=%async_computation | async-start | bytes 1048576 | tf_op jit(solution)/shard_map/all_to_all | solution.py:552
  36.4 7.9 %query_project_kernel.1 = (f32[4,256,128]{2,1,0:T(8,128)}, f32[4,256,128]{2,1,0:T(8,128)}, f32[2,256,128]{2,1,0:T(8,128)}, f32[2,256,128]{2,1,0:T(8,128)}, f32[3...) custom-call(s32[5]{0:T(128)S(1)} %stack.23.at.place, ...), custom_call_target="tpu_custom_call" | custom-call | tf_op jit(solution)/shard_map/query_project_kernel/pallas_call | solution.py:351
  44.2 1.0 copy-done.3
  45.3 6.9 %third_kernel.1.refs_0_.refs_1_.refs_6_.refs_2_.refs_3_.refs_4_ = f32[11,512,128]{2,1,0:T(8,128)S(1)} custom-call(s32[5]{0:T(128)S(1)} %stack.23.at.place, bf16[1024,1024]{1,0:T(8,128)(2,1)} %act.7, bf16[3,1024,1024]{2,1,0:T(8,128)(2,1)} %bitcast.13, f32[5,512,128]{2,1,0:T(8,128)} %get-tuple-element.40.refs_0_.refs_1_, f32[4,256,128]{2,1,0:T(8,128)S(1)} %copy-done.3), custom_call_target="tpu_custom_call" | custom-call | tf_op jit(solution)/shard_map/third_kernel/pallas_call | solution.py:135
  52.2 6.3 %all-to-all-done.refs_8_.refs_0_ = f32[16,8,8,128]{3,2,1,0:T(8,128)} async-done(((f32[16,8,8,128]{3,2,1,0:T(8,128)}), f32[16,8,8,128]{3,2,1,0:T(8,128)}, u32[]{:S(2)}, u32[]{:S(2)}) %all-to-all-start) | async-done | bytes 524320 | tf_op jit(solution)/shard_map/all_to_all | solution.py:552
  58.5 2.1 %kv_other_kernel.1.refs_10_ = f32[3,512,128]{2,1,0:T(8,128)} custom-call(f32[11,512,128]{2,1,0:T(8,128)S(1)} %third_kernel.1.refs_0_.refs_1_.refs_6_.refs_2_.refs_3_.refs_4_, f32[11,512,128]{2,1,0:T(8,128)S(1)} %third_kernel.1.refs_0_.refs_1_.refs_6_.refs_2_.refs_3_.refs_4_, f32[5,512,128]{2,1,0:T(8,128)} %collective-permute-done.4.refs_2_.refs_3_.refs_8_.refs_5_.refs_6_, ...), custom_call_target="tpu_custom_call" | custom-call | tf_op jit(solution)/shard_map/kv_other_kernel/pallas_call | solution.py:200
  60.6 2.3 %kv_last_kernel.1 = (f32[2,512,128]{2,1,0:T(8,128)}, f32[2,512,128]{2,1,0:T(8,128)}) custom-call(f32[11,512,128]{2,1,0:T(8,128)S(1)} %third_kernel.1.refs_0_.refs_1_.refs_6_.refs_2_.refs_3_.refs_4_, f32[11,512,128]{2,1,0:T(8,128)S(1)} %third_kernel.1.refs_0_.refs_1_.refs_6_.refs_2_.refs_3_.refs_4_, ...), custom_call_target="tpu_custom_call" | custom-call | tf_op jit(solution)/shard_map/kv_last_kernel/pallas_call | solution.py:200
  62.9 1.3 %collective-permute-start.7 = (f32[2,512,128]{2,1,0:T(8,128)}, f32[2,512,128]{2,1,0:T(8,128)}, u32[]{:S(2)}, u32[]{:S(2)}) collective-permute-start(f32[2,512,128]{2,1,0:T(8,128)} %get-tuple-element.45), channel_id=1, source_target_pairs={{0,6},{1,7},{2,0},{3,1},{4,2},{5,3},{6,4},{7,5},{8,14},{9,15},{10,... | collective-permute-start | bytes 1572872 | tf_op jit(solution)/shard_map/ppermute | solution.py:26
  64.2 0.2 collective-permute-start.6
  64.4 1.5 %kv_beside_kernel.1.refs_7_.refs_0_ = f32[4,512,128]{2,1,0:T(8,128)S(1)} custom-call(f32[11,512,128]{2,1,0:T(8,128)S(1)} %third_kernel.1.refs_0_.refs_1_.refs_6_.refs_2_.refs_3_.refs_4_, f32[11,512,128]{2,1,0:T(8,128)S(1)} %third_kernel.1.refs_0_.refs_1_.refs_6_.refs_2_.refs_3_.refs_4_, ...), custom_call_target="tpu_custom_call" | custom-call | tf_op jit(solution)/shard_map/kv_beside_kernel/pallas_call | solution.py:200
  65.9 3.6 %taps_kernel.1.refs_4_.refs_1_ = f32[1024,256]{1,0:T(8,128)} custom-call(f32[16,8,8,128]{3,2,1,0:T(8,128)} %all-to-all-done.refs_8_.refs_0_, bf16[256,128]{1,0:T(8,128)(2,1)} %constant.72.clone.refs_1_.refs_2_, bf16[256,128]{1,0:T(8,128)(2,1)} %constant.73.clone.refs_2_.refs_3_, f32[128,128]{1,0:T(8,128)} %constant.74.clone.refs_3_.refs_4_, ...), custom_call_target="tpu_custom_call" | custom-call | tf_op jit(solution)/shard_map/taps_kernel/pallas_call | solution.py:535
  69.5 0.1 collective-permute-start.9
  69.6 2.7 %collective-permute-start.10 = (f32[4,256,128]{2,1,0:T(8,128)}, f32[4,256,128]{2,1,0:T(8,128)S(1)}, u32[]{:S(2)}, u32[]{:S(2)}) collective-permute-start(f32[4,256,128]{2,1,0:T(8,128)} %get-tuple-element.50), channel_id=1, source_target_pairs={{0,6},{1,7},{2,0},{3,1},{4,2},{5,3},{6,4},{7,5},{8,14},{9,15},{10,... | collective-permute-start | bytes 1572872 | tf_op jit(solution)/shard_map/ppermute | solution.py:26
  72.3 4.0 %collective-permute-done.7.refs_2_ = f32[2,512,128]{2,1,0:T(8,128)} collective-permute-done((f32[2,512,128]{2,1,0:T(8,128)}, f32[2,512,128]{2,1,0:T(8,128)}, u32[]{:S(2)}, u32[]{:S(2)}) %collective-permute-start.7) | collective-permute-done | bytes 524320 | tf_op jit(solution)/shard_map/ppermute | solution.py:26
  76.4 1.1 collective-permute-start.11
  77.5 1.0 collective-permute-done.6.refs_1_
  78.5 1.1 collective-permute-done.8.refs_3_
  79.7 2.6 %kv_kernel.1 = f32[128,8,128]{2,1,0:T(8,128)} custom-call(f32[4,512,128]{2,1,0:T(8,128)S(1)} %copy-done.2, f32[2,512,128]{2,1,0:T(8,128)} %collective-permute-done.6.refs_1_, f32[2,512,128]{2,1,0:T(8,128)} %collective-permute-done.7.refs_2_, f32[3,512,128]{2,1,0:T(8,128)} %collective-permute-done.8.refs_3_, f32[1024,256]{1,0:T(8,128)S(1)} %copy-done), custom_call_target="tpu_custom_call" | custom-call | tf_op jit(solution)/shard_map/kv_kernel/pallas_call | solution.py:535
  82.3 7.1 %all-to-all-start.1 = ((f32[16,8,8,128]{3,2,1,0:T(8,128)}), f32[16,8,8,128]{3,2,1,0:T(8,128)S(1)}, u32[]{:S(2)}, u32[]{:S(2)}) async-start(f32[16,8,8,128]{3,2,1,0:T(8,128)} %bitcast.14), calls=%async_computation.1 | async-start | bytes 1048576 | tf_op jit(solution)/shard_map/all_to_all | solution.py:552
  89.4 0.6 collective-permute-start.14
  90.0 2.4 %first_sum_kernel.1 = (f32[3,256,128]{2,1,0:T(8,128)}, f32[3,256,128]{2,1,0:T(8,128)}) custom-call(f32[4,256,128]{2,1,0:T(8,128)S(1)} %collective-permute-done.9.refs_0_.refs_2_, f32[4,256,128]{2,1,0:T(8,128)S(1)} %collective-permute-done.10.refs_1_.refs_3_, f32[3,256,128]{2,1,0:T(8,128)S(1)} %collective-permute-done.11.refs_2_.refs_4_, ...), custom_call_target="tpu_custom_call" | custom-call | tf_op jit(solution)/shard_map/first_sum_kernel/pallas_call | solution.py:162
  92.4 2.7 %collective-permute-start.13 = (f32[3,256,128]{2,1,0:T(8,128)}, f32[3,256,128]{2,1,0:T(8,128)S(1)}, u32[]{:S(2)}, u32[]{:S(2)}) collective-permute-start(f32[3,256,128]{2,1,0:T(8,128)} %get-tuple-element.56), channel_id=1, source_target_pairs={{0,6},{1,7},{2,0},{3,1},{4,2},{5,3},{6,4},{7,5},{8,14},{9,15},{10,... | collective-permute-start | bytes 1179656 | tf_op jit(solution)/shard_map/ppermute | solution.py:26
  95.1 5.5 %all-to-all-done.1.refs_0_ = f32[16,8,8,128]{3,2,1,0:T(8,128)S(1)} async-done(((f32[16,8,8,128]{3,2,1,0:T(8,128)}), f32[16,8,8,128]{3,2,1,0:T(8,128)S(1)}, u32[]{:S(2)}, u32[]{:S(2)}) %all-to-all-start.1) | async-done | bytes 524320 | tf_op jit(solution)/shard_map/all_to_all | solution.py:552
  100.6 4.7 %conv_kernel.1 = f32[16,8,8,128]{3,2,1,0:T(8,128)} custom-call(f32[16,8,8,128]{3,2,1,0:T(8,128)S(1)} %all-to-all-done.1.refs_0_, f32[1024,256]{1,0:T(8,128)} %taps_kernel.1.refs_4_.refs_1_, bf16[256,128]{1,0:T(8,128)(2,1)} %constant.72.clone.refs_1_.refs_2_, bf16[256,128]{1,0:T(8,128)(2,1)} %constant.73.clone.refs_2_.refs_3_, ...), custom_call_target="tpu_custom_call" | custom-call | tf_op jit(solution)/shard_map/conv_kernel/pallas_call | solution.py:535
  105.3 4.7 %all-to-all-start.2 = ((f32[16,8,8,128]{3,2,1,0:T(8,128)}), f32[16,8,8,128]{3,2,1,0:T(8,128)S(1)}, u32[]{:S(2)}, u32[]{:S(2)}) async-start(f32[16,8,8,128]{3,2,1,0:T(8,128)} %conv_kernel.1), calls=%async_computation.2 | async-start | bytes 1048576 | tf_op jit(solution)/shard_map/all_to_all | solution.py:552
  110.0 0.9 collective-permute-done.14.refs_5_.refs_4_
  110.9 1.3 %query_second_sum_kernel.1 = (f32[2,256,128]{2,1,0:T(8,128)S(1)}, f32[2,256,128]{2,1,0:T(8,128)S(1)}, f32[2,256,128]{2,1,0:T(8,128)S(1)}) custom-call(f32[3,256,128]{2,1,0:T(8,128)S(1)} %collective-permute-done.12.refs_0_, f32[3,256,128]{2,1,0:T(8,128)S(1)} %collective-permute-done.13.refs_1_, f32[4,256,128]{2,1,0:T(8,128)S(1)} %collective-permute-done.9.refs_0_.refs_2_, ...), custom_call_target="tpu_custom_call" | custom-call | tf_op jit(solution)/shard_map/query_second_sum_kernel/pallas_call | solution.py:162
  112.3 0.2 collective-permute-start.16
  112.4 1.4 %collective-permute-start.17 = (f32[2,256,128]{2,1,0:T(8,128)S(1)}, f32[2,256,128]{2,1,0:T(8,128)S(1)}, u32[]{:S(2)}, u32[]{:S(2)}) collective-permute-start(f32[2,256,128]{2,1,0:T(8,128)S(1)} %get-tuple-element.62), channel_id=1, source_target_pairs={{0,1},{1,0},{2,3},{3,2},{4,5},{5,4},{6,7},{7,6},{8,9},{9,8},{10,11... | collective-permute-start | bytes 786440 | tf_op jit(solution)/shard_map/ppermute | solution.py:30
  113.8 0.9 collective-permute-start.15
  114.7 1.3 %query_beside_kernel.1.refs_0_ = f32[4,256,128]{2,1,0:T(8,128)S(1)} custom-call(f32[3,256,128]{2,1,0:T(8,128)S(1)} %collective-permute-done.12.refs_0_, f32[3,256,128]{2,1,0:T(8,128)S(1)} %collective-permute-done.13.refs_1_, f32[4,256,128]{2,1,0:T(8,128)S(1)} %collective-permute-done.9.refs_0_.refs_2_, ...), custom_call_target="tpu_custom_call" | custom-call | tf_op jit(solution)/shard_map/query_beside_kernel/pallas_call | solution.py:162
  116.0 3.6 %collective-permute-done.16.refs_2_ = f32[2,256,128]{2,1,0:T(8,128)S(1)} collective-permute-done((f32[2,256,128]{2,1,0:T(8,128)S(1)}, f32[2,256,128]{2,1,0:T(8,128)S(1)}, u32[]{:S(2)}, u32[]{:S(2)}) %collective-permute-start.16) | collective-permute-done | bytes 262176 | tf_op jit(solution)/shard_map/ppermute | solution.py:26
  119.6 4.6 %collective-permute-done.17.refs_3_ = f32[2,256,128]{2,1,0:T(8,128)S(1)} collective-permute-done((f32[2,256,128]{2,1,0:T(8,128)S(1)}, f32[2,256,128]{2,1,0:T(8,128)S(1)}, u32[]{:S(2)}, u32[]{:S(2)}) %collective-permute-start.17) | collective-permute-done | bytes 262176 | tf_op jit(solution)/shard_map/ppermute | solution.py:30
  124.2 0.1 query_kernel.1.refs_1_
  124.2 1.1 gate_kernel.1
  (25 shorter events, 0.1 us)
Async XLA Ops:
  3.9 14.6 %collective-permute-start = (f32[2,512,128]{2,1,0:T(8,128)S(1)}, f32[2,512,128]{2,1,0:T(8,128)S(1)}, u32[]{:S(2)}, u32[]{:S(2)}) collective-permute-start(f32[2,512,128]{2,1,0:T(8,128)S(1)} %get-tuple-element.34), channel_id=1, source_target_pairs={{0,2},{1,3},{2,4},{3,5},{4,6},{5,7},{6,0},{7,1},{8,10},{9,11},{10,... | collective-permute-start | bytes 1572872 | tf_op jit(solution)/shard_map/ppermute | solution.py:26
  6.0 12.5 %collective-permute-start.1 = (f32[2,512,128]{2,1,0:T(8,128)S(1)}, f32[2,512,128]{2,1,0:T(8,128)S(1)}, u32[]{:S(2)}, u32[]{:S(2)}) collective-permute-start(f32[2,512,128]{2,1,0:T(8,128)S(1)} %get-tuple-element.35), channel_id=1, source_target_pairs={{0,6},{1,7},{2,0},{3,1},{4,2},{5,3},{6,4},{7,5},{8,14},{9,15},{10,... | collective-permute-start | bytes 1572872 | tf_op jit(solution)/shard_map/ppermute | solution.py:26
  7.4 12.7 %collective-permute-start.2 = (f32[2,512,128]{2,1,0:T(8,128)S(1)}, f32[2,512,128]{2,1,0:T(8,128)S(1)}, u32[]{:S(2)}, u32[]{:S(2)}) collective-permute-start(f32[2,512,128]{2,1,0:T(8,128)S(1)} %get-tuple-element.36), channel_id=1, source_target_pairs={{0,1},{1,0},{2,3},{3,2},{4,5},{5,4},{6,7},{7,6},{8,9},{9,8},{10,11... | collective-permute-start | bytes 1572872 | tf_op jit(solution)/shard_map/ppermute | solution.py:30
  16.6 41.8 %collective-permute-start.3 = (f32[5,512,128]{2,1,0:T(8,128)}, f32[5,512,128]{2,1,0:T(8,128)}, u32[]{:S(2)}, u32[]{:S(2)}) collective-permute-start(f32[5,512,128]{2,1,0:T(8,128)} %get-tuple-element.42), channel_id=1, source_target_pairs={{0,1},{1,0},{2,3},{3,2},{4,5},{5,4},{6,7},{7,6},{8,9},{9,8},{10,11... | collective-permute-start | bytes 3932168 | tf_op jit(solution)/shard_map/ppermute | solution.py:30
  20.1 3.2 %copy-start.5 = (f32[1024,128]{1,0:T(8,128)S(1)}, f32[1024,128]{1,0:T(8,128)}, u32[]{:S(2)}) copy-start(f32[1024,128]{1,0:T(8,128)} %refs_0_.1) | copy-start | bytes 1572868
  21.9 36.5 %collective-permute-start.5 = (f32[5,512,128]{2,1,0:T(8,128)}, f32[5,512,128]{2,1,0:T(8,128)}, u32[]{:S(2)}, u32[]{:S(2)}) collective-permute-start(f32[5,512,128]{2,1,0:T(8,128)} %get-tuple-element.43), channel_id=1, source_target_pairs={{0,6},{1,7},{2,0},{3,1},{4,2},{5,3},{6,4},{7,5},{8,14},{9,15},{10,... | collective-permute-start | bytes 3932168 | tf_op jit(solution)/shard_map/ppermute | solution.py:26
  23.1 35.4 %collective-permute-start.4 = (f32[5,512,128]{2,1,0:T(8,128)}, f32[5,512,128]{2,1,0:T(8,128)}, u32[]{:S(2)}, u32[]{:S(2)}) collective-permute-start(f32[5,512,128]{2,1,0:T(8,128)} %get-tuple-element.40.refs_0_.refs_1_), channel_id=1, source_target_pairs={{0,2},{1,3},{2,4},{3,5},{4,6},{5,7},{6,0},{7,1},{8,10},{9,11},{10,... | collective-permute-start | bytes 3932168 | tf_op jit(solution)/shard_map/ppermute | solution.py:26
  24.5 33.9 %all-to-all-start = ((f32[16,8,8,128]{3,2,1,0:T(8,128)}), f32[16,8,8,128]{3,2,1,0:T(8,128)}, u32[]{:S(2)}, u32[]{:S(2)}) async-start(f32[16,8,8,128]{3,2,1,0:T(8,128)} %bitcast.15), calls=%async_computation | async-start | bytes 1048576 | tf_op jit(solution)/shard_map/all_to_all | solution.py:552
  44.2 1.0 copy-start.3
  45.3 13.2 %copy-start.4 = (f32[4,256,128]{2,1,0:T(8,128)S(1)}, f32[4,256,128]{2,1,0:T(8,128)}, u32[]{:S(2)}) copy-start(f32[4,256,128]{2,1,0:T(8,128)} %get-tuple-element.41.refs_1_.refs_9_.refs_0_) | copy-start | bytes 1572868
  60.6 19.1 %collective-permute-start.8 = (f32[3,512,128]{2,1,0:T(8,128)}, f32[3,512,128]{2,1,0:T(8,128)}, u32[]{:S(2)}, u32[]{:S(2)}) collective-permute-start(f32[3,512,128]{2,1,0:T(8,128)} %kv_other_kernel.1.refs_10_), channel_id=1, source_target_pairs={{0,1},{1,0},{2,3},{3,2},{4,5},{5,4},{6,7},{7,6},{8,9},{9,8},{10,11... | collective-permute-start | bytes 2359304 | tf_op jit(solution)/shard_map/ppermute | solution.py:30
  62.9 13.5 %collective-permute-start.7 = (f32[2,512,128]{2,1,0:T(8,128)}, f32[2,512,128]{2,1,0:T(8,128)}, u32[]{:S(2)}, u32[]{:S(2)}) collective-permute-start(f32[2,512,128]{2,1,0:T(8,128)} %get-tuple-element.45), channel_id=1, source_target_pairs={{0,6},{1,7},{2,0},{3,1},{4,2},{5,3},{6,4},{7,5},{8,14},{9,15},{10,... | collective-permute-start | bytes 1572872 | tf_op jit(solution)/shard_map/ppermute | solution.py:26
  64.2 14.4 %collective-permute-start.6 = (f32[2,512,128]{2,1,0:T(8,128)}, f32[2,512,128]{2,1,0:T(8,128)}, u32[]{:S(2)}, u32[]{:S(2)}) collective-permute-start(f32[2,512,128]{2,1,0:T(8,128)} %get-tuple-element.44.refs_9_), channel_id=1, source_target_pairs={{0,2},{1,3},{2,4},{3,5},{4,6},{5,7},{6,0},{7,1},{8,10},{9,11},{10,... | collective-permute-start | bytes 1572872 | tf_op jit(solution)/shard_map/ppermute | solution.py:26
  65.9 3.7 %copy-start.1 = (f32[4,512,128]{2,1,0:T(8,128)}, f32[4,512,128]{2,1,0:T(8,128)S(1)}, u32[]{:S(2)}) copy-start(f32[4,512,128]{2,1,0:T(8,128)S(1)} %kv_beside_kernel.1.refs_7_.refs_0_) | copy-start | bytes 3145732
  69.5 10.2 %copy-start = (f32[1024,256]{1,0:T(8,128)S(1)}, f32[1024,256]{1,0:T(8,128)}, u32[]{:S(2)}) copy-start(f32[1024,256]{1,0:T(8,128)} %taps_kernel.1.refs_4_.refs_1_) | copy-start | bytes 3145732
  69.5 10.2 %copy-start.2 = (f32[4,512,128]{2,1,0:T(8,128)S(1)}, f32[4,512,128]{2,1,0:T(8,128)}, u32[]{:S(2)}) copy-start(f32[4,512,128]{2,1,0:T(8,128)} %copy-done.1) | copy-start | bytes 3145732
  69.5 20.5 %collective-permute-start.9 = (f32[4,256,128]{2,1,0:T(8,128)}, f32[4,256,128]{2,1,0:T(8,128)S(1)}, u32[]{:S(2)}, u32[]{:S(2)}) collective-permute-start(f32[4,256,128]{2,1,0:T(8,128)} %get-tuple-element.49), channel_id=1, source_target_pairs={{0,2},{1,3},{2,4},{3,5},{4,6},{5,7},{6,0},{7,1},{8,10},{9,11},{10,... | collective-permute-start | bytes 1572872 | tf_op jit(solution)/shard_map/ppermute | solution.py:26
  69.6 20.4 %collective-permute-start.10 = (f32[4,256,128]{2,1,0:T(8,128)}, f32[4,256,128]{2,1,0:T(8,128)S(1)}, u32[]{:S(2)}, u32[]{:S(2)}) collective-permute-start(f32[4,256,128]{2,1,0:T(8,128)} %get-tuple-element.50), channel_id=1, source_target_pairs={{0,6},{1,7},{2,0},{3,1},{4,2},{5,3},{6,4},{7,5},{8,14},{9,15},{10,... | collective-permute-start | bytes 1572872 | tf_op jit(solution)/shard_map/ppermute | solution.py:26
  76.4 13.6 %collective-permute-start.11 = (f32[3,256,128]{2,1,0:T(8,128)}, f32[3,256,128]{2,1,0:T(8,128)S(1)}, u32[]{:S(2)}, u32[]{:S(2)}) collective-permute-start(f32[3,256,128]{2,1,0:T(8,128)} %get-tuple-element.51), channel_id=1, source_target_pairs={{0,1},{1,0},{2,3},{3,2},{4,5},{5,4},{6,7},{7,6},{8,9},{9,8},{10,11... | collective-permute-start | bytes 1179656 | tf_op jit(solution)/shard_map/ppermute | solution.py:30
  82.3 18.2 %all-to-all-start.1 = ((f32[16,8,8,128]{3,2,1,0:T(8,128)}), f32[16,8,8,128]{3,2,1,0:T(8,128)S(1)}, u32[]{:S(2)}, u32[]{:S(2)}) async-start(f32[16,8,8,128]{3,2,1,0:T(8,128)} %bitcast.14), calls=%async_computation.1 | async-start | bytes 1048576 | tf_op jit(solution)/shard_map/all_to_all | solution.py:552
  89.4 21.5 %collective-permute-start.14 = (f32[5,256,128]{2,1,0:T(8,128)}, f32[5,256,128]{2,1,0:T(8,128)S(1)}, u32[]{:S(2)}, u32[]{:S(2)}) collective-permute-start(f32[5,256,128]{2,1,0:T(8,128)} %get-tuple-element.57), channel_id=1, source_target_pairs={{0,1},{1,0},{2,3},{3,2},{4,5},{5,4},{6,7},{7,6},{8,9},{9,8},{10,11... | collective-permute-start | bytes 1966088 | tf_op jit(solution)/shard_map/ppermute | solution.py:30
  92.4 18.5 %collective-permute-start.12 = (f32[3,256,128]{2,1,0:T(8,128)}, f32[3,256,128]{2,1,0:T(8,128)S(1)}, u32[]{:S(2)}, u32[]{:S(2)}) collective-permute-start(f32[3,256,128]{2,1,0:T(8,128)} %get-tuple-element.55), channel_id=1, source_target_pairs={{0,2},{1,3},{2,4},{3,5},{4,6},{5,7},{6,0},{7,1},{8,10},{9,11},{10,... | collective-permute-start | bytes 1179656 | tf_op jit(solution)/shard_map/ppermute | solution.py:26
  92.4 18.5 %collective-permute-start.13 = (f32[3,256,128]{2,1,0:T(8,128)}, f32[3,256,128]{2,1,0:T(8,128)S(1)}, u32[]{:S(2)}, u32[]{:S(2)}) collective-permute-start(f32[3,256,128]{2,1,0:T(8,128)} %get-tuple-element.56), channel_id=1, source_target_pairs={{0,6},{1,7},{2,0},{3,1},{4,2},{5,3},{6,4},{7,5},{8,14},{9,15},{10,... | collective-permute-start | bytes 1179656 | tf_op jit(solution)/shard_map/ppermute | solution.py:26
  105.3 18.9 %all-to-all-start.2 = ((f32[16,8,8,128]{3,2,1,0:T(8,128)}), f32[16,8,8,128]{3,2,1,0:T(8,128)S(1)}, u32[]{:S(2)}, u32[]{:S(2)}) async-start(f32[16,8,8,128]{3,2,1,0:T(8,128)} %conv_kernel.1), calls=%async_computation.2 | async-start | bytes 1048576 | tf_op jit(solution)/shard_map/all_to_all | solution.py:552
  112.3 7.3 %collective-permute-start.16 = (f32[2,256,128]{2,1,0:T(8,128)S(1)}, f32[2,256,128]{2,1,0:T(8,128)S(1)}, u32[]{:S(2)}, u32[]{:S(2)}) collective-permute-start(f32[2,256,128]{2,1,0:T(8,128)S(1)} %get-tuple-element.61), channel_id=1, source_target_pairs={{0,6},{1,7},{2,0},{3,1},{4,2},{5,3},{6,4},{7,5},{8,14},{9,15},{10,... | collective-permute-start | bytes 786440 | tf_op jit(solution)/shard_map/ppermute | solution.py:26
  112.4 11.7 %collective-permute-start.17 = (f32[2,256,128]{2,1,0:T(8,128)S(1)}, f32[2,256,128]{2,1,0:T(8,128)S(1)}, u32[]{:S(2)}, u32[]{:S(2)}) collective-permute-start(f32[2,256,128]{2,1,0:T(8,128)S(1)} %get-tuple-element.62), channel_id=1, source_target_pairs={{0,1},{1,0},{2,3},{3,2},{4,5},{5,4},{6,7},{7,6},{8,9},{9,8},{10,11... | collective-permute-start | bytes 786440 | tf_op jit(solution)/shard_map/ppermute | solution.py:30
  113.8 10.4 %collective-permute-start.15 = (f32[2,256,128]{2,1,0:T(8,128)S(1)}, f32[2,256,128]{2,1,0:T(8,128)S(1)}, u32[]{:S(2)}, u32[]{:S(2)}) collective-permute-start(f32[2,256,128]{2,1,0:T(8,128)S(1)} %get-tuple-element.60.refs_7_), channel_id=1, source_target_pairs={{0,2},{1,3},{2,4},{3,5},{4,6},{5,7},{6,0},{7,1},{8,10},{9,11},{10,... | collective-permute-start | bytes 786440 | tf_op jit(solution)/shard_map/ppermute | solution.py:26

commit v13 on v12

--- a/solution.py
+++ b/solution.py
@@ -60,18 +60,14 @@
 
 def first_kernel(halves, place, act, weight, outs):
     send_r, send_l, z_other, z_mine = outs
+
+    def put(other, mine):
+        other[0][other[1]], mine[0][mine[1]] = parts_of(act[...], weight[0], place[4])
+
     for half, send in enumerate((send_r, send_l)):
-        pl.when(pl.program_id(0) == half)(
-            functools.partial(
-                halves.fill,
-                place,
-                act,
-                weight,
-                half,
-                ((send, 0), (send, 1)),
-                ((z_other, half), (z_mine, half)),
-            )
-        )
+        step = pl.program_id(0) - 2 * half
+        pl.when(step == 0)(functools.partial(put, (send, 0), (send, 1)))
+        pl.when(step == 1)(functools.partial(put, (z_other, half), (z_mine, half)))
 
 
 def second_kernel(halves, place, act, weight, outs):
@@ -103,10 +99,11 @@
         )
 
 
-def project(kernel, halves, place, activations, weight, owner, steps, outs, after=()):
+def project(kernel, halves, place, activations, weight, owner, steps, outs, after=(), split=1):
     first, last = halves.columns[0], halves.columns[-1]
 
     def weight_block(i, at):
+        i = i // split
         return (first + (last - first) * (i % 2), 0, at[owner + i // 2])
 
     def body(at, act, weight_ref, *refs):
@@ -138,7 +135,10 @@
             num_scalar_prefetch=1,
             grid=(steps,),
             in_specs=[
-                pl.BlockSpec(activations.shape, lambda i, at: (0, 0)),
+                pl.BlockSpec(
+                    (activations.shape[0] // split, activations.shape[1]),
+                    lambda i, at: (split - 1 - i % split, 0),
+                ),
                 pl.BlockSpec((1, weight.shape[1], 2 * BLOCK), weight_block),
             ]
             + [pl.BlockSpec(memory_space=pl.ANY)] * len(after),
@@ -299,7 +299,7 @@
         project, halves=halves, place=place, activations=activations, weight=weight
     )
     send_r, send_l, z_send, z_mine = make(
-        first_kernel, owner=0, steps=2, outs=[(2, "vmem")] * 4
+        first_kernel, owner=0, steps=4, outs=[(2, "vmem")] * 4, split=2
     )
     got_r, got_l, z_got = shift_x(send_r, 1), shift_x(send_l, -1), swap_z(z_send)
     next_r, next_l, z_send = make(
@@ -502,13 +502,32 @@
     turn_blocks(taps_ref, out_ref)
 
 
-def kv_kernel(*refs):
-    parts, out_ref, kv_ref = refs[:-2], refs[-2], refs[-1]
-    z_key, z_value, x_key, x_value = summed(*parts)
-    rows = z_key.shape[0]
-    kv_ref[:rows] = z_key * z_value
-    kv_ref[rows:] = x_key * x_value
-    turn_blocks(kv_ref, out_ref)
+def kv_kernel(part, last_r, last_l, last_x, out_ref):
+    key, value, x_key, x_value = summed(part, last_r, last_l, last_x)
+    first, second = (key * value).T, (x_key * x_value).T
+    steps = out_ref.shape[1] // 2
+
+    def put(step):
+        out_ref[:, step, :] = first
+        out_ref[:, steps + step, :] = second
+
+    for step in range(steps):
+        pl.when(pl.program_id(0) == step)(functools.partial(put, step))
+
+
+def multiply_kv(parts, out_shape):
+    def spec(value):
+        return pl.BlockSpec((value.shape[0], BLOCK, BLOCK), lambda i: (0, i, 0))
+
+    return pl.pallas_call(
+        kv_kernel,
+        grid=(parts[0].shape[1] // BLOCK,),
+        in_specs=[spec(value) for value in parts],
+        out_specs=pl.BlockSpec(out_shape, lambda i: (0, 0, 0)),
+        out_shape=pltpu.HBM(out_shape, jnp.float32),
+        compiler_params=params(8),
+        name="kv_kernel",
+    )(*parts)
 
 
 def query_kernel(*refs):
@@ -587,14 +606,7 @@
         after=(kv_part,),
         to_hbm=True,
     )
-    kv = call(
-        kv_kernel,
-        turned_shape,
-        *kv_parts,
-        after=(spectrum,),
-        scratch=[pltpu.VMEM((tokens, channels), jnp.float32)],
-        to_hbm=True,
-    )
+    kv = multiply_kv(kv_parts, turned_shape)
     q_parts = reduce_query(q_halves, hold["query"], spectrum)
     moved = exchange(kv.reshape(moved_shape))
     convolved = call(

time: 126 us -> 129 us (1.024)
  local copies, waits for them, and re-layouts: 1.14 us -> 2.98 us
  Pallas kernels: 52.2 us -> 54 us
    pallas_call x0 -> x1, Pallas kernels: none -> 3.48 us  [multiply_kv(): pl.pallas_call(kv_kernel, grid=(parts[0].shape[1] // BLOCK,), in_specs=[s...]
    pallas_call x6 -> x5, Pallas kernels: 13.4 us -> 10.7 us  [call(): pl.pallas_call(body, grid=(1,), in_specs=[pl.BlockSpec(memory_space=pltpu...]
    unnamed x12 -> x14, local copies, waits for them, and re-layouts: 1.06 us -> 2.89 us
where the time goes in v13:
time: 129 us; the launch traced here: 128 us
  Pallas kernels  54 us (42%)
  starting transfers between devices  41.5 us (32%)
  waiting for transfers between devices  29.8 us (23%)
  local copies, waits for them, and re-layouts  2.98 us (2%)
    all_to_all x3, starting transfers between devices, exchange(): return lax.all_to_all(value, 'seq', split_axis=0, concat_axis=0, tiled=True)  23.6 us
    pallas_call x3, Pallas kernels, project(): pl.pallas_call(body, grid_spec=pltpu.PrefetchScalarGridSpec(num_scalar_pr...  19.2 us
    ppermute x12, starting transfers between devices, shift_x(): lax.ppermute(value, 'chan', [(i, (i + 2 * step) % 8) for i in range(8)])  13 us
    all_to_all x3, waiting for transfers between devices, exchange(): return lax.all_to_all(value, 'seq', split_axis=0, concat_axis=0, tiled=True)  11.7 us
    pallas_call x5, Pallas kernels, call(): pl.pallas_call(body, grid=(1,), in_specs=[pl.BlockSpec(memory_space=pltpu...  10.7 us
    ppermute x12, waiting for transfers between devices, shift_x(): lax.ppermute(value, 'chan', [(i, (i + 2 * step) % 8) for i in range(8)])  9.68 us
    ppermute x6, waiting for transfers between devices, swap_z(): return lax.ppermute(value, 'chan', [(i, i ^ 1) for i in range(8)])  8.43 us
    pallas_call x1, Pallas kernels, project_query(): pl.pallas_call(query_project_kernel, grid_spec=pltpu.PrefetchScalarGridSp...  7.88 us
  transfers between devices with their start and end apart: 21, of which 10 were waited for; matrix products, arithmetic and copies ran while one was open for 0% of the time, Pallas kernels for 36%

profile of v13, /device:TPU:1, one launch (start us, length us, event | category | flops | bytes accessed | tf_op | source)
XLA Modules:
  0.0 128.4 jit_solution(16788147151413512798)
XLA Ops:
  0.0 0.1 stack.23.at.place
  0.1 4.7 %first_kernel.1 = (f32[2,512,128]{2,1,0:T(8,128)S(1)}, f32[2,512,128]{2,1,0:T(8,128)S(1)}, f32[2,512,128]{2,1,0:T(8,128)S(1)}, f32[2,512,128]{2,1,0:T(8,128)S(1)}) custom-call(s32[5]{0:T(128)S(1)} %stack.23.at.place, bf16[1024,1024]{1,0:T(8,128)(2,1)} %act.7, bf16[3,1024,1024]{2,1,0:T(8,128)(2,1)} %bitcast.10), custom_call_target="tpu_custom_call" | custom-call | tf_op jit(solution)/shard_map/first_kernel/pallas_call | solution.py:132
  4.8 2.1 %collective-permute-start = (f32[2,512,128]{2,1,0:T(8,128)S(1)}, f32[2,512,128]{2,1,0:T(8,128)S(1)}, u32[]{:S(2)}, u32[]{:S(2)}) collective-permute-start(f32[2,512,128]{2,1,0:T(8,128)S(1)} %get-tuple-element.34), channel_id=1, source_target_pairs={{0,2},{1,3},{2,4},{3,5},{4,6},{5,7},{6,0},{7,1},{8,10},{9,11},{10,... | collective-permute-start | bytes 1572872 | tf_op jit(solution)/shard_map/ppermute | solution.py:26
  7.0 1.3 %collective-permute-start.1 = (f32[2,512,128]{2,1,0:T(8,128)S(1)}, f32[2,512,128]{2,1,0:T(8,128)S(1)}, u32[]{:S(2)}, u32[]{:S(2)}) collective-permute-start(f32[2,512,128]{2,1,0:T(8,128)S(1)} %get-tuple-element.35), channel_id=1, source_target_pairs={{0,6},{1,7},{2,0},{3,1},{4,2},{5,3},{6,4},{7,5},{8,14},{9,15},{10,... | collective-permute-start | bytes 1572872 | tf_op jit(solution)/shard_map/ppermute | solution.py:26
  8.3 1.8 %collective-permute-start.2 = (f32[2,512,128]{2,1,0:T(8,128)S(1)}, f32[2,512,128]{2,1,0:T(8,128)S(1)}, u32[]{:S(2)}, u32[]{:S(2)}) collective-permute-start(f32[2,512,128]{2,1,0:T(8,128)S(1)} %get-tuple-element.36), channel_id=1, source_target_pairs={{0,1},{1,0},{2,3},{3,2},{4,5},{5,4},{6,7},{7,6},{8,9},{9,8},{10,11... | collective-permute-start | bytes 1572872 | tf_op jit(solution)/shard_map/ppermute | solution.py:30
  10.1 7.5 %second_kernel.1 = (f32[5,512,128]{2,1,0:T(8,128)S(1)}, f32[5,512,128]{2,1,0:T(8,128)S(1)}, f32[5,512,128]{2,1,0:T(8,128)}) custom-call(s32[5]{0:T(128)S(1)} %stack.23.at.place, bf16[1024,1024]{1,0:T(8,128)(2,1)} %act.7, bf16[3,1024,1024]{2,1,0:T(8,128)(2,1)} %bitcast.11, f32[2,512,128]{2,1,0:T(8,128)S(1)} %get-tuple-element.37.refs_0_.refs_5_), custom_call_target="tpu_custom_call" | custom-call | tf_op jit(solution)/shard_map/second_kernel/pallas_call | solution.py:132
  17.6 1.9 %collective-permute-done.refs_0_ = f32[2,512,128]{2,1,0:T(8,128)S(1)} collective-permute-done((f32[2,512,128]{2,1,0:T(8,128)S(1)}, f32[2,512,128]{2,1,0:T(8,128)S(1)}, u32[]{:S(2)}, u32[]{:S(2)}) %collective-permute-start) | collective-permute-done | bytes 524320 | tf_op jit(solution)/shard_map/ppermute | solution.py:26
  19.4 1.6 %collective-permute-done.2.refs_2_ = f32[2,512,128]{2,1,0:T(8,128)S(1)} collective-permute-done((f32[2,512,128]{2,1,0:T(8,128)S(1)}, f32[2,512,128]{2,1,0:T(8,128)S(1)}, u32[]{:S(2)}, u32[]{:S(2)}) %collective-permute-start.2) | collective-permute-done | bytes 524320 | tf_op jit(solution)/shard_map/ppermute | solution.py:30
  21.0 1.8 %kv_first_sum_kernel.1 = (f32[5,512,128]{2,1,0:T(8,128)}, f32[5,512,128]{2,1,0:T(8,128)}) custom-call(f32[2,512,128]{2,1,0:T(8,128)S(1)} %collective-permute-done.refs_0_, f32[2,512,128]{2,1,0:T(8,128)S(1)} %collective-permute-done.1.refs_1_, f32[2,512,128]{2,1,0:T(8,128)S(1)} %collective-permute-done.2.refs_2_, ...), custom_call_target="tpu_custom_call" | custom-call | tf_op jit(solution)/shard_map/kv_first_sum_kernel/pallas_call | solution.py:162
  22.8 1.2 collective-permute-start.5
  24.0 0.3 collective-permute-start.4
  24.3 1.1 taps_turn_kernel.1
  25.4 11.8 %all-to-all-start = ((f32[16,8,8,128]{3,2,1,0:T(8,128)}), f32[16,8,8,128]{3,2,1,0:T(8,128)}, u32[]{:S(2)}, u32[]{:S(2)}) async-start(f32[16,8,8,128]{3,2,1,0:T(8,128)} %bitcast.15), calls=%async_computation | async-start | bytes 1048576 | tf_op jit(solution)/shard_map/all_to_all | solution.py:571
  37.2 7.9 %query_project_kernel.1 = (f32[4,256,128]{2,1,0:T(8,128)}, f32[4,256,128]{2,1,0:T(8,128)}, f32[2,256,128]{2,1,0:T(8,128)}, f32[2,256,128]{2,1,0:T(8,128)}, f32[3...) custom-call(s32[5]{0:T(128)S(1)} %stack.23.at.place, ...), custom_call_target="tpu_custom_call" | custom-call | tf_op jit(solution)/shard_map/query_project_kernel/pallas_call | solution.py:351
  45.1 1.0 copy-done.2
  46.2 6.9 %third_kernel.1.refs_0_.refs_1_.refs_6_.refs_2_.refs_3_.refs_4_ = f32[11,512,128]{2,1,0:T(8,128)S(1)} custom-call(s32[5]{0:T(128)S(1)} %stack.23.at.place, bf16[1024,1024]{1,0:T(8,128)(2,1)} %act.7, bf16[3,1024,1024]{2,1,0:T(8,128)(2,1)} %bitcast.13, f32[5,512,128]{2,1,0:T(8,128)} %get-tuple-element.40.refs_0_.refs_1_, f32[4,256,128]{2,1,0:T(8,128)S(1)} %copy-done.2), custom_call_target="tpu_custom_call" | custom-call | tf_op jit(solution)/shard_map/third_kernel/pallas_call | solution.py:132
  53.1 6.3 %all-to-all-done.refs_8_.refs_0_ = f32[16,8,8,128]{3,2,1,0:T(8,128)} async-done(((f32[16,8,8,128]{3,2,1,0:T(8,128)}), f32[16,8,8,128]{3,2,1,0:T(8,128)}, u32[]{:S(2)}, u32[]{:S(2)}) %all-to-all-start) | async-done | bytes 524320 | tf_op jit(solution)/shard_map/all_to_all | solution.py:571
  59.4 2.1 %kv_other_kernel.1.refs_10_ = f32[3,512,128]{2,1,0:T(8,128)} custom-call(f32[11,512,128]{2,1,0:T(8,128)S(1)} %third_kernel.1.refs_0_.refs_1_.refs_6_.refs_2_.refs_3_.refs_4_, f32[11,512,128]{2,1,0:T(8,128)S(1)} %third_kernel.1.refs_0_.refs_1_.refs_6_.refs_2_.refs_3_.refs_4_, f32[5,512,128]{2,1,0:T(8,128)} %collective-permute-done.4.refs_2_.refs_3_.refs_8_.refs_5_.refs_6_, ...), custom_call_target="tpu_custom_call" | custom-call | tf_op jit(solution)/shard_map/kv_other_kernel/pallas_call | solution.py:200
  61.5 2.3 %kv_last_kernel.1 = (f32[2,512,128]{2,1,0:T(8,128)}, f32[2,512,128]{2,1,0:T(8,128)}) custom-call(f32[11,512,128]{2,1,0:T(8,128)S(1)} %third_kernel.1.refs_0_.refs_1_.refs_6_.refs_2_.refs_3_.refs_4_, f32[11,512,128]{2,1,0:T(8,128)S(1)} %third_kernel.1.refs_0_.refs_1_.refs_6_.refs_2_.refs_3_.refs_4_, ...), custom_call_target="tpu_custom_call" | custom-call | tf_op jit(solution)/shard_map/kv_last_kernel/pallas_call | solution.py:200
  63.8 1.3 collective-permute-start.7
  65.1 0.2 collective-permute-start.6
  65.3 1.5 %kv_beside_kernel.1.part.refs_7_ = f32[4,512,128]{2,1,0:T(8,128)S(1)} custom-call(f32[11,512,128]{2,1,0:T(8,128)S(1)} %third_kernel.1.refs_0_.refs_1_.refs_6_.refs_2_.refs_3_.refs_4_, f32[11,512,128]{2,1,0:T(8,128)S(1)} %third_kernel.1.refs_0_.refs_1_.refs_6_.refs_2_.refs_3_.refs_4_, ...), custom_call_target="tpu_custom_call" | custom-call | tf_op jit(solution)/shard_map/kv_beside_kernel/pallas_call | solution.py:200
  66.8 3.6 %taps_kernel.1.refs_1_.refs_4_ = f32[1024,256]{1,0:T(8,128)} custom-call(f32[16,8,8,128]{3,2,1,0:T(8,128)} %all-to-all-done.refs_8_.refs_0_, bf16[256,128]{1,0:T(8,128)(2,1)} %constant.72.clone.refs_1_.refs_2_, bf16[256,128]{1,0:T(8,128)(2,1)} %constant.73.clone.refs_2_.refs_3_, f32[128,128]{1,0:T(8,128)} %constant.74.clone.refs_3_.refs_4_, ...), custom_call_target="tpu_custom_call" | custom-call | tf_op jit(solution)/shard_map/taps_kernel/pallas_call | solution.py:554
  70.4 0.3 collective-permute-start.9
  70.7 2.7 %collective-permute-start.10 = (f32[4,256,128]{2,1,0:T(8,128)}, f32[4,256,128]{2,1,0:T(8,128)S(1)}, u32[]{:S(2)}, u32[]{:S(2)}) collective-permute-start(f32[4,256,128]{2,1,0:T(8,128)} %get-tuple-element.50), channel_id=1, source_target_pairs={{0,6},{1,7},{2,0},{3,1},{4,2},{5,3},{6,4},{7,5},{8,14},{9,15},{10,... | collective-permute-start | bytes 1572872 | tf_op jit(solution)/shard_map/ppermute | solution.py:26
  73.4 4.0 %collective-permute-done.7.last_l = f32[2,512,128]{2,1,0:T(8,128)S(1)} collective-permute-done((f32[2,512,128]{2,1,0:T(8,128)}, f32[2,512,128]{2,1,0:T(8,128)S(1)}, u32[]{:S(2)}, u32[]{:S(2)}) %collective-permute-start.7) | collective-permute-done | bytes 524320 | tf_op jit(solution)/shard_map/ppermute | solution.py:26
  77.3 0.8 copy-done.5
  78.1 1.1 collective-permute-start.11
  79.3 0.2 collective-permute-done.6.last_r
  79.5 1.1 collective-permute-done.8.last_x
  80.6 1.0 copy-done.6
  81.7 3.5 %kv_kernel.1 = f32[128,8,128]{2,1,0:T(8,128)} custom-call(f32[4,512,128]{2,1,0:T(8,128)S(1)} %copy-done.1, f32[2,512,128]{2,1,0:T(8,128)} %collective-permute-done.6.last_r, f32[2,512,128]{2,1,0:T(8,128)S(1)} %copy-done.6, f32[3,512,128]{2,1,0:T(8,128)} %collective-permute-done.8.last_x), custom_call_target="tpu_custom_call" | custom-call | tf_op jit(solution)/shard_map/kv_kernel/pallas_call | solution.py:522
  85.1 7.1 %all-to-all-start.1 = ((f32[16,8,8,128]{3,2,1,0:T(8,128)}), f32[16,8,8,128]{3,2,1,0:T(8,128)S(1)}, u32[]{:S(2)}, u32[]{:S(2)}) async-start(f32[16,8,8,128]{3,2,1,0:T(8,128)} %bitcast.14), calls=%async_computation.1 | async-start | bytes 1048576 | tf_op jit(solution)/shard_map/all_to_all | solution.py:571
  92.2 0.6 collective-permute-start.14
  92.8 2.4 %first_sum_kernel.1 = (f32[3,256,128]{2,1,0:T(8,128)}, f32[3,256,128]{2,1,0:T(8,128)}) custom-call(f32[4,256,128]{2,1,0:T(8,128)S(1)} %collective-permute-done.9.refs_0_.refs_2_, f32[4,256,128]{2,1,0:T(8,128)S(1)} %collective-permute-done.10.refs_1_.refs_3_, f32[3,256,128]{2,1,0:T(8,128)S(1)} %collective-permute-done.11.refs_2_.refs_4_, ...), custom_call_target="tpu_custom_call" | custom-call | tf_op jit(solution)/shard_map/first_sum_kernel/pallas_call | solution.py:162
  95.2 2.7 %collective-permute-start.13 = (f32[3,256,128]{2,1,0:T(8,128)}, f32[3,256,128]{2,1,0:T(8,128)S(1)}, u32[]{:S(2)}, u32[]{:S(2)}) collective-permute-start(f32[3,256,128]{2,1,0:T(8,128)} %get-tuple-element.56), channel_id=1, source_target_pairs={{0,6},{1,7},{2,0},{3,1},{4,2},{5,3},{6,4},{7,5},{8,14},{9,15},{10,... | collective-permute-start | bytes 1179656 | tf_op jit(solution)/shard_map/ppermute | solution.py:26
  97.9 5.5 %all-to-all-done.1.refs_0_ = f32[16,8,8,128]{3,2,1,0:T(8,128)S(1)} async-done(((f32[16,8,8,128]{3,2,1,0:T(8,128)}), f32[16,8,8,128]{3,2,1,0:T(8,128)S(1)}, u32[]{:S(2)}, u32[]{:S(2)}) %all-to-all-start.1) | async-done | bytes 524320 | tf_op jit(solution)/shard_map/all_to_all | solution.py:571
  103.4 4.7 %conv_kernel.1 = f32[16,8,8,128]{3,2,1,0:T(8,128)} custom-call(f32[16,8,8,128]{3,2,1,0:T(8,128)S(1)} %all-to-all-done.1.refs_0_, f32[1024,256]{1,0:T(8,128)} %taps_kernel.1.refs_1_.refs_4_, bf16[256,128]{1,0:T(8,128)(2,1)} %constant.72.clone.refs_1_.refs_2_, bf16[256,128]{1,0:T(8,128)(2,1)} %constant.73.clone.refs_2_.refs_3_, ...), custom_call_target="tpu_custom_call" | custom-call | tf_op jit(solution)/shard_map/conv_kernel/pallas_call | solution.py:554
  108.1 4.7 %all-to-all-start.2 = ((f32[16,8,8,128]{3,2,1,0:T(8,128)}), f32[16,8,8,128]{3,2,1,0:T(8,128)S(1)}, u32[]{:S(2)}, u32[]{:S(2)}) async-start(f32[16,8,8,128]{3,2,1,0:T(8,128)} %conv_kernel.1), calls=%async_computation.2 | async-start | bytes 1048576 | tf_op jit(solution)/shard_map/all_to_all | solution.py:571
  112.8 0.9 collective-permute-done.14.refs_5_.refs_4_
  113.7 1.3 %query_second_sum_kernel.1 = (f32[2,256,128]{2,1,0:T(8,128)S(1)}, f32[2,256,128]{2,1,0:T(8,128)S(1)}, f32[2,256,128]{2,1,0:T(8,128)S(1)}) custom-call(f32[3,256,128]{2,1,0:T(8,128)S(1)} %collective-permute-done.12.refs_0_, f32[3,256,128]{2,1,0:T(8,128)S(1)} %collective-permute-done.13.refs_1_, f32[4,256,128]{2,1,0:T(8,128)S(1)} %collective-permute-done.9.refs_0_.refs_2_, ...), custom_call_target="tpu_custom_call" | custom-call | tf_op jit(solution)/shard_map/query_second_sum_kernel/pallas_call | solution.py:162
  115.1 0.8 collective-permute-start.16
  115.9 1.4 %collective-permute-start.17 = (f32[2,256,128]{2,1,0:T(8,128)S(1)}, f32[2,256,128]{2,1,0:T(8,128)S(1)}, u32[]{:S(2)}, u32[]{:S(2)}) collective-permute-start(f32[2,256,128]{2,1,0:T(8,128)S(1)} %get-tuple-element.62), channel_id=1, source_target_pairs={{0,1},{1,0},{2,3},{3,2},{4,5},{5,4},{6,7},{7,6},{8,9},{9,8},{10,11... | collective-permute-start | bytes 786440 | tf_op jit(solution)/shard_map/ppermute | solution.py:30
  117.3 0.2 collective-permute-start.15
  117.5 1.3 %query_beside_kernel.1.refs_0_ = f32[4,256,128]{2,1,0:T(8,128)S(1)} custom-call(f32[3,256,128]{2,1,0:T(8,128)S(1)} %collective-permute-done.12.refs_0_, f32[3,256,128]{2,1,0:T(8,128)S(1)} %collective-permute-done.13.refs_1_, f32[4,256,128]{2,1,0:T(8,128)S(1)} %collective-permute-done.9.refs_0_.refs_2_, ...), custom_call_target="tpu_custom_call" | custom-call | tf_op jit(solution)/shard_map/query_beside_kernel/pallas_call | solution.py:162
  118.8 3.6 %collective-permute-done.16.refs_2_ = f32[2,256,128]{2,1,0:T(8,128)S(1)} collective-permute-done((f32[2,256,128]{2,1,0:T(8,128)S(1)}, f32[2,256,128]{2,1,0:T(8,128)S(1)}, u32[]{:S(2)}, u32[]{:S(2)}) %collective-permute-start.16) | collective-permute-done | bytes 262176 | tf_op jit(solution)/shard_map/ppermute | solution.py:26
  122.4 4.8 %collective-permute-done.17.refs_3_ = f32[2,256,128]{2,1,0:T(8,128)S(1)} collective-permute-done((f32[2,256,128]{2,1,0:T(8,128)S(1)}, f32[2,256,128]{2,1,0:T(8,128)S(1)}, u32[]{:S(2)}, u32[]{:S(2)}) %collective-permute-start.17) | collective-permute-done | bytes 262176 | tf_op jit(solution)/shard_map/ppermute | solution.py:30
  127.2 1.1 gate_kernel.1
  (27 shorter events, 0.1 us)
Async XLA Ops:
  4.8 14.6 %collective-permute-start = (f32[2,512,128]{2,1,0:T(8,128)S(1)}, f32[2,512,128]{2,1,0:T(8,128)S(1)}, u32[]{:S(2)}, u32[]{:S(2)}) collective-permute-start(f32[2,512,128]{2,1,0:T(8,128)S(1)} %get-tuple-element.34), channel_id=1, source_target_pairs={{0,2},{1,3},{2,4},{3,5},{4,6},{5,7},{6,0},{7,1},{8,10},{9,11},{10,... | collective-permute-start | bytes 1572872 | tf_op jit(solution)/shard_map/ppermute | solution.py:26
  7.0 12.5 %collective-permute-start.1 = (f32[2,512,128]{2,1,0:T(8,128)S(1)}, f32[2,512,128]{2,1,0:T(8,128)S(1)}, u32[]{:S(2)}, u32[]{:S(2)}) collective-permute-start(f32[2,512,128]{2,1,0:T(8,128)S(1)} %get-tuple-element.35), channel_id=1, source_target_pairs={{0,6},{1,7},{2,0},{3,1},{4,2},{5,3},{6,4},{7,5},{8,14},{9,15},{10,... | collective-permute-start | bytes 1572872 | tf_op jit(solution)/shard_map/ppermute | solution.py:26
  8.3 12.7 %collective-permute-start.2 = (f32[2,512,128]{2,1,0:T(8,128)S(1)}, f32[2,512,128]{2,1,0:T(8,128)S(1)}, u32[]{:S(2)}, u32[]{:S(2)}) collective-permute-start(f32[2,512,128]{2,1,0:T(8,128)S(1)} %get-tuple-element.36), channel_id=1, source_target_pairs={{0,1},{1,0},{2,3},{3,2},{4,5},{5,4},{6,7},{7,6},{8,9},{9,8},{10,11... | collective-permute-start | bytes 1572872 | tf_op jit(solution)/shard_map/ppermute | solution.py:30
  17.5 41.8 %collective-permute-start.3 = (f32[5,512,128]{2,1,0:T(8,128)}, f32[5,512,128]{2,1,0:T(8,128)}, u32[]{:S(2)}, u32[]{:S(2)}) collective-permute-start(f32[5,512,128]{2,1,0:T(8,128)} %get-tuple-element.42), channel_id=1, source_target_pairs={{0,1},{1,0},{2,3},{3,2},{4,5},{5,4},{6,7},{7,6},{8,9},{9,8},{10,11... | collective-permute-start | bytes 3932168 | tf_op jit(solution)/shard_map/ppermute | solution.py:30
  21.0 3.2 %copy-start.4 = (f32[1024,128]{1,0:T(8,128)S(1)}, f32[1024,128]{1,0:T(8,128)}, u32[]{:S(2)}) copy-start(f32[1024,128]{1,0:T(8,128)} %refs_0_.1) | copy-start | bytes 1572868
  22.8 36.6 %collective-permute-start.5 = (f32[5,512,128]{2,1,0:T(8,128)}, f32[5,512,128]{2,1,0:T(8,128)}, u32[]{:S(2)}, u32[]{:S(2)}) collective-permute-start(f32[5,512,128]{2,1,0:T(8,128)} %get-tuple-element.43), channel_id=1, source_target_pairs={{0,6},{1,7},{2,0},{3,1},{4,2},{5,3},{6,4},{7,5},{8,14},{9,15},{10,... | collective-permute-start | bytes 3932168 | tf_op jit(solution)/shard_map/ppermute | solution.py:26
  24.0 35.4 %collective-permute-start.4 = (f32[5,512,128]{2,1,0:T(8,128)}, f32[5,512,128]{2,1,0:T(8,128)}, u32[]{:S(2)}, u32[]{:S(2)}) collective-permute-start(f32[5,512,128]{2,1,0:T(8,128)} %get-tuple-element.40.refs_0_.refs_1_), channel_id=1, source_target_pairs={{0,2},{1,3},{2,4},{3,5},{4,6},{5,7},{6,0},{7,1},{8,10},{9,11},{10,... | collective-permute-start | bytes 3932168 | tf_op jit(solution)/shard_map/ppermute | solution.py:26
  25.4 33.9 %all-to-all-start = ((f32[16,8,8,128]{3,2,1,0:T(8,128)}), f32[16,8,8,128]{3,2,1,0:T(8,128)}, u32[]{:S(2)}, u32[]{:S(2)}) async-start(f32[16,8,8,128]{3,2,1,0:T(8,128)} %bitcast.15), calls=%async_computation | async-start | bytes 1048576 | tf_op jit(solution)/shard_map/all_to_all | solution.py:571
  45.1 1.0 copy-start.2
  46.2 13.2 %copy-start.3 = (f32[4,256,128]{2,1,0:T(8,128)S(1)}, f32[4,256,128]{2,1,0:T(8,128)}, u32[]{:S(2)}) copy-start(f32[4,256,128]{2,1,0:T(8,128)} %get-tuple-element.41.refs_1_.refs_9_.refs_0_) | copy-start | bytes 1572868
  61.5 19.1 %collective-permute-start.8 = (f32[3,512,128]{2,1,0:T(8,128)}, f32[3,512,128]{2,1,0:T(8,128)}, u32[]{:S(2)}, u32[]{:S(2)}) collective-permute-start(f32[3,512,128]{2,1,0:T(8,128)} %kv_other_kernel.1.refs_10_), channel_id=1, source_target_pairs={{0,1},{1,0},{2,3},{3,2},{4,5},{5,4},{6,7},{7,6},{8,9},{9,8},{10,11... | collective-permute-start | bytes 2359304 | tf_op jit(solution)/shard_map/ppermute | solution.py:30
  63.8 13.5 %collective-permute-start.7 = (f32[2,512,128]{2,1,0:T(8,128)}, f32[2,512,128]{2,1,0:T(8,128)S(1)}, u32[]{:S(2)}, u32[]{:S(2)}) collective-permute-start(f32[2,512,128]{2,1,0:T(8,128)} %get-tuple-element.45), channel_id=1, source_target_pairs={{0,6},{1,7},{2,0},{3,1},{4,2},{5,3},{6,4},{7,5},{8,14},{9,15},{10,... | collective-permute-start | bytes 1572872 | tf_op jit(solution)/shard_map/ppermute | solution.py:26
  65.1 14.4 %collective-permute-start.6 = (f32[2,512,128]{2,1,0:T(8,128)}, f32[2,512,128]{2,1,0:T(8,128)}, u32[]{:S(2)}, u32[]{:S(2)}) collective-permute-start(f32[2,512,128]{2,1,0:T(8,128)} %get-tuple-element.44.refs_9_), channel_id=1, source_target_pairs={{0,2},{1,3},{2,4},{3,5},{4,6},{5,7},{6,0},{7,1},{8,10},{9,11},{10,... | collective-permute-start | bytes 1572872 | tf_op jit(solution)/shard_map/ppermute | solution.py:26
  66.8 3.7 %copy-start = (f32[4,512,128]{2,1,0:T(8,128)}, f32[4,512,128]{2,1,0:T(8,128)S(1)}, u32[]{:S(2)}) copy-start(f32[4,512,128]{2,1,0:T(8,128)S(1)} %kv_beside_kernel.1.part.refs_7_) | copy-start | bytes 3145732
  70.4 10.2 %copy-start.1 = (f32[4,512,128]{2,1,0:T(8,128)S(1)}, f32[4,512,128]{2,1,0:T(8,128)}, u32[]{:S(2)}) copy-start(f32[4,512,128]{2,1,0:T(8,128)} %copy-done) | copy-start | bytes 3145732
  70.4 22.4 %collective-permute-start.9 = (f32[4,256,128]{2,1,0:T(8,128)}, f32[4,256,128]{2,1,0:T(8,128)S(1)}, u32[]{:S(2)}, u32[]{:S(2)}) collective-permute-start(f32[4,256,128]{2,1,0:T(8,128)} %get-tuple-element.49), channel_id=1, source_target_pairs={{0,2},{1,3},{2,4},{3,5},{4,6},{5,7},{6,0},{7,1},{8,10},{9,11},{10,... | collective-permute-start | bytes 1572872 | tf_op jit(solution)/shard_map/ppermute | solution.py:26
  70.7 22.1 %collective-permute-start.10 = (f32[4,256,128]{2,1,0:T(8,128)}, f32[4,256,128]{2,1,0:T(8,128)S(1)}, u32[]{:S(2)}, u32[]{:S(2)}) collective-permute-start(f32[4,256,128]{2,1,0:T(8,128)} %get-tuple-element.50), channel_id=1, source_target_pairs={{0,6},{1,7},{2,0},{3,1},{4,2},{5,3},{6,4},{7,5},{8,14},{9,15},{10,... | collective-permute-start | bytes 1572872 | tf_op jit(solution)/shard_map/ppermute | solution.py:26
  77.3 0.8 copy-start.5
  78.1 14.7 %collective-permute-start.11 = (f32[3,256,128]{2,1,0:T(8,128)}, f32[3,256,128]{2,1,0:T(8,128)S(1)}, u32[]{:S(2)}, u32[]{:S(2)}) collective-permute-start(f32[3,256,128]{2,1,0:T(8,128)} %get-tuple-element.51), channel_id=1, source_target_pairs={{0,1},{1,0},{2,3},{3,2},{4,5},{5,4},{6,7},{7,6},{8,9},{9,8},{10,11... | collective-permute-start | bytes 1179656 | tf_op jit(solution)/shard_map/ppermute | solution.py:30
  80.6 1.0 copy-start.6
  85.1 18.2 %all-to-all-start.1 = ((f32[16,8,8,128]{3,2,1,0:T(8,128)}), f32[16,8,8,128]{3,2,1,0:T(8,128)S(1)}, u32[]{:S(2)}, u32[]{:S(2)}) async-start(f32[16,8,8,128]{3,2,1,0:T(8,128)} %bitcast.14), calls=%async_computation.1 | async-start | bytes 1048576 | tf_op jit(solution)/shard_map/all_to_all | solution.py:571
  92.2 21.5 %collective-permute-start.14 = (f32[5,256,128]{2,1,0:T(8,128)}, f32[5,256,128]{2,1,0:T(8,128)S(1)}, u32[]{:S(2)}, u32[]{:S(2)}) collective-permute-start(f32[5,256,128]{2,1,0:T(8,128)} %get-tuple-element.57), channel_id=1, source_target_pairs={{0,1},{1,0},{2,3},{3,2},{4,5},{5,4},{6,7},{7,6},{8,9},{9,8},{10,11... | collective-permute-start | bytes 1966088 | tf_op jit(solution)/shard_map/ppermute | solution.py:30
  95.2 18.5 %collective-permute-start.12 = (f32[3,256,128]{2,1,0:T(8,128)}, f32[3,256,128]{2,1,0:T(8,128)S(1)}, u32[]{:S(2)}, u32[]{:S(2)}) collective-permute-start(f32[3,256,128]{2,1,0:T(8,128)} %get-tuple-element.55), channel_id=1, source_target_pairs={{0,2},{1,3},{2,4},{3,5},{4,6},{5,7},{6,0},{7,1},{8,10},{9,11},{10,... | collective-permute-start | bytes 1179656 | tf_op jit(solution)/shard_map/ppermute | solution.py:26
  95.2 18.5 %collective-permute-start.13 = (f32[3,256,128]{2,1,0:T(8,128)}, f32[3,256,128]{2,1,0:T(8,128)S(1)}, u32[]{:S(2)}, u32[]{:S(2)}) collective-permute-start(f32[3,256,128]{2,1,0:T(8,128)} %get-tuple-element.56), channel_id=1, source_target_pairs={{0,6},{1,7},{2,0},{3,1},{4,2},{5,3},{6,4},{7,5},{8,14},{9,15},{10,... | collective-permute-start | bytes 1179656 | tf_op jit(solution)/shard_map/ppermute | solution.py:26
  108.1 19.1 %all-to-all-start.2 = ((f32[16,8,8,128]{3,2,1,0:T(8,128)}), f32[16,8,8,128]{3,2,1,0:T(8,128)S(1)}, u32[]{:S(2)}, u32[]{:S(2)}) async-start(f32[16,8,8,128]{3,2,1,0:T(8,128)} %conv_kernel.1), calls=%async_computation.2 | async-start | bytes 1048576 | tf_op jit(solution)/shard_map/all_to_all | solution.py:571
  115.1 7.3 %collective-permute-start.16 = (f32[2,256,128]{2,1,0:T(8,128)S(1)}, f32[2,256,128]{2,1,0:T(8,128)S(1)}, u32[]{:S(2)}, u32[]{:S(2)}) collective-permute-start(f32[2,256,128]{2,1,0:T(8,128)S(1)} %get-tuple-element.61), channel_id=1, source_target_pairs={{0,6},{1,7},{2,0},{3,1},{4,2},{5,3},{6,4},{7,5},{8,14},{9,15},{10,... | collective-permute-start | bytes 786440 | tf_op jit(solution)/shard_map/ppermute | solution.py:26
  115.9 11.2 %collective-permute-start.17 = (f32[2,256,128]{2,1,0:T(8,128)S(1)}, f32[2,256,128]{2,1,0:T(8,128)S(1)}, u32[]{:S(2)}, u32[]{:S(2)}) collective-permute-start(f32[2,256,128]{2,1,0:T(8,128)S(1)} %get-tuple-element.62), channel_id=1, source_target_pairs={{0,1},{1,0},{2,3},{3,2},{4,5},{5,4},{6,7},{7,6},{8,9},{9,8},{10,11... | collective-permute-start | bytes 786440 | tf_op jit(solution)/shard_map/ppermute | solution.py:30
  117.3 9.9 %collective-permute-start.15 = (f32[2,256,128]{2,1,0:T(8,128)S(1)}, f32[2,256,128]{2,1,0:T(8,128)S(1)}, u32[]{:S(2)}, u32[]{:S(2)}) collective-permute-start(f32[2,256,128]{2,1,0:T(8,128)S(1)} %get-tuple-element.60.refs_7_), channel_id=1, source_target_pairs={{0,2},{1,3},{2,4},{3,5},{4,6},{5,7},{6,0},{7,1},{8,10},{9,11},{10,... | collective-permute-start | bytes 786440 | tf_op jit(solution)/shard_map/ppermute | solution.py:26

commit v14 on v12

--- a/solution.py
+++ b/solution.py
@@ -151,7 +151,7 @@
 
 
 def sum_call(kernel, halves, counts, near, far, after=()):
-    tile = min(BLOCK, halves.rows)
+    tile = halves.rows
 
     def body(*refs):
         rows = pl.ds(pl.multiple_of(pl.program_id(0) * tile, tile), tile)
@@ -189,7 +189,7 @@
 
 
 def piece_call(kernel, halves, counts, pieces, after=()):
-    tile = min(2 * BLOCK, halves.rows)
+    tile = halves.rows
 
     def body(*refs):
         kernel(*refs[: len(pieces)], *refs[len(pieces) + len(after) :])

time: 126 us -> 126 us (level)
  no operation moved by 1% of the time
where the time goes in v14:
time: 126 us
  Pallas kernels  52.2 us (41%)
  starting transfers between devices  41.5 us (33%)
  waiting for transfers between devices  30.5 us (24%)
    all_to_all x3, starting transfers between devices, exchange(): return lax.all_to_all(value, 'seq', split_axis=0, concat_axis=0, tiled=True)  23.7 us
    pallas_call x3, Pallas kernels, project(): pl.pallas_call(body, grid_spec=pltpu.PrefetchScalarGridSpec(num_scalar_pr...  18.3 us
    pallas_call x6, Pallas kernels, call(): pl.pallas_call(body, grid=(1,), in_specs=[pl.BlockSpec(memory_space=pltpu...  13.4 us
    ppermute x12, starting transfers between devices, shift_x(): lax.ppermute(value, 'chan', [(i, (i + 2 * step) % 8) for i in range(8)])  13 us
    all_to_all x3, waiting for transfers between devices, exchange(): return lax.all_to_all(value, 'seq', split_axis=0, concat_axis=0, tiled=True)  11.8 us
    ppermute x12, waiting for transfers between devices, shift_x(): lax.ppermute(value, 'chan', [(i, (i + 2 * step) % 8) for i in range(8)])  10.5 us
    ppermute x6, waiting for transfers between devices, swap_z(): return lax.ppermute(value, 'chan', [(i, i ^ 1) for i in range(8)])  8.17 us
    pallas_call x1, Pallas kernels, project_query(): pl.pallas_call(query_project_kernel, grid_spec=pltpu.PrefetchScalarGridSp...  7.87 us
  transfers between devices with their start and end apart: 21, of which 10 were waited for; matrix products, arithmetic and copies ran while one was open for 0% of the time, Pallas kernels for 36%

profile of v14, /device:TPU:1, one launch (start us, length us, event | category | flops | bytes accessed | tf_op | source)
XLA Modules:
  0.0 125.6 jit_solution(2316832741462777092)
XLA Ops:
  0.0 0.1 stack.23.at.place
  0.1 3.8 %first_kernel.1 = (f32[2,512,128]{2,1,0:T(8,128)S(1)}, f32[2,512,128]{2,1,0:T(8,128)S(1)}, f32[2,512,128]{2,1,0:T(8,128)S(1)}, f32[2,512,128]{2,1,0:T(8,128)S(1)}) custom-call(s32[5]{0:T(128)S(1)} %stack.23.at.place, bf16[1024,1024]{1,0:T(8,128)(2,1)} %act.7, bf16[3,1024,1024]{2,1,0:T(8,128)(2,1)} %bitcast.10), custom_call_target="tpu_custom_call" | custom-call | tf_op jit(solution)/shard_map/first_kernel/pallas_call | solution.py:135
  3.9 2.1 %collective-permute-start = (f32[2,512,128]{2,1,0:T(8,128)S(1)}, f32[2,512,128]{2,1,0:T(8,128)S(1)}, u32[]{:S(2)}, u32[]{:S(2)}) collective-permute-start(f32[2,512,128]{2,1,0:T(8,128)S(1)} %get-tuple-element.34), channel_id=1, source_target_pairs={{0,2},{1,3},{2,4},{3,5},{4,6},{5,7},{6,0},{7,1},{8,10},{9,11},{10,... | collective-permute-start | bytes 1572872 | tf_op jit(solution)/shard_map/ppermute | solution.py:26
  6.0 1.4 %collective-permute-start.1 = (f32[2,512,128]{2,1,0:T(8,128)S(1)}, f32[2,512,128]{2,1,0:T(8,128)S(1)}, u32[]{:S(2)}, u32[]{:S(2)}) collective-permute-start(f32[2,512,128]{2,1,0:T(8,128)S(1)} %get-tuple-element.35), channel_id=1, source_target_pairs={{0,6},{1,7},{2,0},{3,1},{4,2},{5,3},{6,4},{7,5},{8,14},{9,15},{10,... | collective-permute-start | bytes 1572872 | tf_op jit(solution)/shard_map/ppermute | solution.py:26
  7.4 1.8 %collective-permute-start.2 = (f32[2,512,128]{2,1,0:T(8,128)S(1)}, f32[2,512,128]{2,1,0:T(8,128)S(1)}, u32[]{:S(2)}, u32[]{:S(2)}) collective-permute-start(f32[2,512,128]{2,1,0:T(8,128)S(1)} %get-tuple-element.36), channel_id=1, source_target_pairs={{0,1},{1,0},{2,3},{3,2},{4,5},{5,4},{6,7},{7,6},{8,9},{9,8},{10,11... | collective-permute-start | bytes 1572872 | tf_op jit(solution)/shard_map/ppermute | solution.py:30
  9.2 7.5 %second_kernel.1 = (f32[5,512,128]{2,1,0:T(8,128)S(1)}, f32[5,512,128]{2,1,0:T(8,128)S(1)}, f32[5,512,128]{2,1,0:T(8,128)}) custom-call(s32[5]{0:T(128)S(1)} %stack.23.at.place, bf16[1024,1024]{1,0:T(8,128)(2,1)} %act.7, bf16[3,1024,1024]{2,1,0:T(8,128)(2,1)} %bitcast.11, f32[2,512,128]{2,1,0:T(8,128)S(1)} %get-tuple-element.37.refs_0_.refs_5_), custom_call_target="tpu_custom_call" | custom-call | tf_op jit(solution)/shard_map/second_kernel/pallas_call | solution.py:135
  16.6 0.0 collective-permute-start.3
  16.7 1.9 %collective-permute-done.refs_0_ = f32[2,512,128]{2,1,0:T(8,128)S(1)} collective-permute-done((f32[2,512,128]{2,1,0:T(8,128)S(1)}, f32[2,512,128]{2,1,0:T(8,128)S(1)}, u32[]{:S(2)}, u32[]{:S(2)}) %collective-permute-start) | collective-permute-done | bytes 524320 | tf_op jit(solution)/shard_map/ppermute | solution.py:26
  18.5 1.6 %collective-permute-done.2.refs_2_ = f32[2,512,128]{2,1,0:T(8,128)S(1)} collective-permute-done((f32[2,512,128]{2,1,0:T(8,128)S(1)}, f32[2,512,128]{2,1,0:T(8,128)S(1)}, u32[]{:S(2)}, u32[]{:S(2)}) %collective-permute-start.2) | collective-permute-done | bytes 524320 | tf_op jit(solution)/shard_map/ppermute | solution.py:30
  20.1 1.7 %kv_first_sum_kernel.1 = (f32[5,512,128]{2,1,0:T(8,128)}, f32[5,512,128]{2,1,0:T(8,128)}) custom-call(f32[2,512,128]{2,1,0:T(8,128)S(1)} %collective-permute-done.refs_0_, f32[2,512,128]{2,1,0:T(8,128)S(1)} %collective-permute-done.1.refs_1_, f32[2,512,128]{2,1,0:T(8,128)S(1)} %collective-permute-done.2.refs_2_, ...), custom_call_target="tpu_custom_call" | custom-call | tf_op jit(solution)/shard_map/kv_first_sum_kernel/pallas_call | solution.py:162
  21.9 1.2 collective-permute-start.5
  23.0 0.3 collective-permute-start.4
  23.3 1.1 taps_turn_kernel.1
  24.5 11.8 %all-to-all-start = ((f32[16,8,8,128]{3,2,1,0:T(8,128)}), f32[16,8,8,128]{3,2,1,0:T(8,128)}, u32[]{:S(2)}, u32[]{:S(2)}) async-start(f32[16,8,8,128]{3,2,1,0:T(8,128)} %bitcast.15), calls=%async_computation | async-start | bytes 1048576 | tf_op jit(solution)/shard_map/all_to_all | solution.py:552
  36.3 7.9 %query_project_kernel.1 = (f32[4,256,128]{2,1,0:T(8,128)}, f32[4,256,128]{2,1,0:T(8,128)}, f32[2,256,128]{2,1,0:T(8,128)}, f32[2,256,128]{2,1,0:T(8,128)}, f32[3...) custom-call(s32[5]{0:T(128)S(1)} %stack.23.at.place, ...), custom_call_target="tpu_custom_call" | custom-call | tf_op jit(solution)/shard_map/query_project_kernel/pallas_call | solution.py:351
  44.2 1.0 copy-done.3
  45.2 6.9 %third_kernel.1.refs_0_.refs_1_.refs_6_.refs_2_.refs_3_.refs_4_ = f32[11,512,128]{2,1,0:T(8,128)S(1)} custom-call(s32[5]{0:T(128)S(1)} %stack.23.at.place, bf16[1024,1024]{1,0:T(8,128)(2,1)} %act.7, bf16[3,1024,1024]{2,1,0:T(8,128)(2,1)} %bitcast.13, f32[5,512,128]{2,1,0:T(8,128)} %get-tuple-element.40.refs_0_.refs_1_, f32[4,256,128]{2,1,0:T(8,128)S(1)} %copy-done.3), custom_call_target="tpu_custom_call" | custom-call | tf_op jit(solution)/shard_map/third_kernel/pallas_call | solution.py:135
  52.2 6.3 %all-to-all-done.refs_8_.refs_0_ = f32[16,8,8,128]{3,2,1,0:T(8,128)} async-done(((f32[16,8,8,128]{3,2,1,0:T(8,128)}), f32[16,8,8,128]{3,2,1,0:T(8,128)}, u32[]{:S(2)}, u32[]{:S(2)}) %all-to-all-start) | async-done | bytes 524320 | tf_op jit(solution)/shard_map/all_to_all | solution.py:552
  58.5 2.2 %kv_other_kernel.1.refs_10_ = f32[3,512,128]{2,1,0:T(8,128)} custom-call(f32[11,512,128]{2,1,0:T(8,128)S(1)} %third_kernel.1.refs_0_.refs_1_.refs_6_.refs_2_.refs_3_.refs_4_, f32[11,512,128]{2,1,0:T(8,128)S(1)} %third_kernel.1.refs_0_.refs_1_.refs_6_.refs_2_.refs_3_.refs_4_, f32[5,512,128]{2,1,0:T(8,128)} %collective-permute-done.4.refs_2_.refs_3_.refs_8_.refs_5_.refs_6_, ...), custom_call_target="tpu_custom_call" | custom-call | tf_op jit(solution)/shard_map/kv_other_kernel/pallas_call | solution.py:200
  60.7 2.4 %kv_last_kernel.1 = (f32[2,512,128]{2,1,0:T(8,128)}, f32[2,512,128]{2,1,0:T(8,128)}) custom-call(f32[11,512,128]{2,1,0:T(8,128)S(1)} %third_kernel.1.refs_0_.refs_1_.refs_6_.refs_2_.refs_3_.refs_4_, f32[11,512,128]{2,1,0:T(8,128)S(1)} %third_kernel.1.refs_0_.refs_1_.refs_6_.refs_2_.refs_3_.refs_4_, ...), custom_call_target="tpu_custom_call" | custom-call | tf_op jit(solution)/shard_map/kv_last_kernel/pallas_call | solution.py:200
  63.1 1.3 %collective-permute-start.7 = (f32[2,512,128]{2,1,0:T(8,128)}, f32[2,512,128]{2,1,0:T(8,128)}, u32[]{:S(2)}, u32[]{:S(2)}) collective-permute-start(f32[2,512,128]{2,1,0:T(8,128)} %get-tuple-element.45), channel_id=1, source_target_pairs={{0,6},{1,7},{2,0},{3,1},{4,2},{5,3},{6,4},{7,5},{8,14},{9,15},{10,... | collective-permute-start | bytes 1572872 | tf_op jit(solution)/shard_map/ppermute | solution.py:26
  64.3 0.2 collective-permute-start.6
  64.5 1.4 %kv_beside_kernel.1.refs_7_.refs_0_ = f32[4,512,128]{2,1,0:T(8,128)S(1)} custom-call(f32[11,512,128]{2,1,0:T(8,128)S(1)} %third_kernel.1.refs_0_.refs_1_.refs_6_.refs_2_.refs_3_.refs_4_, f32[11,512,128]{2,1,0:T(8,128)S(1)} %third_kernel.1.refs_0_.refs_1_.refs_6_.refs_2_.refs_3_.refs_4_, ...), custom_call_target="tpu_custom_call" | custom-call | tf_op jit(solution)/shard_map/kv_beside_kernel/pallas_call | solution.py:200
  65.9 3.6 %taps_kernel.1.refs_4_.refs_1_ = f32[1024,256]{1,0:T(8,128)} custom-call(f32[16,8,8,128]{3,2,1,0:T(8,128)} %all-to-all-done.refs_8_.refs_0_, bf16[256,128]{1,0:T(8,128)(2,1)} %constant.72.clone.refs_1_.refs_2_, bf16[256,128]{1,0:T(8,128)(2,1)} %constant.73.clone.refs_2_.refs_3_, f32[128,128]{1,0:T(8,128)} %constant.74.clone.refs_3_.refs_4_, ...), custom_call_target="tpu_custom_call" | custom-call | tf_op jit(solution)/shard_map/taps_kernel/pallas_call | solution.py:535
  69.6 0.3 collective-permute-start.9
  69.9 2.7 %collective-permute-start.10 = (f32[4,256,128]{2,1,0:T(8,128)}, f32[4,256,128]{2,1,0:T(8,128)S(1)}, u32[]{:S(2)}, u32[]{:S(2)}) collective-permute-start(f32[4,256,128]{2,1,0:T(8,128)} %get-tuple-element.50), channel_id=1, source_target_pairs={{0,6},{1,7},{2,0},{3,1},{4,2},{5,3},{6,4},{7,5},{8,14},{9,15},{10,... | collective-permute-start | bytes 1572872 | tf_op jit(solution)/shard_map/ppermute | solution.py:26
  72.5 4.0 %collective-permute-done.7.refs_2_ = f32[2,512,128]{2,1,0:T(8,128)} collective-permute-done((f32[2,512,128]{2,1,0:T(8,128)}, f32[2,512,128]{2,1,0:T(8,128)}, u32[]{:S(2)}, u32[]{:S(2)}) %collective-permute-start.7) | collective-permute-done | bytes 524320 | tf_op jit(solution)/shard_map/ppermute | solution.py:26
  76.6 1.1 collective-permute-start.11
  77.7 1.0 collective-permute-done.6.refs_1_
  78.7 1.1 collective-permute-done.8.refs_3_
  79.8 2.6 %kv_kernel.1 = f32[128,8,128]{2,1,0:T(8,128)} custom-call(f32[4,512,128]{2,1,0:T(8,128)S(1)} %copy-done.2, f32[2,512,128]{2,1,0:T(8,128)} %collective-permute-done.6.refs_1_, f32[2,512,128]{2,1,0:T(8,128)} %collective-permute-done.7.refs_2_, f32[3,512,128]{2,1,0:T(8,128)} %collective-permute-done.8.refs_3_, f32[1024,256]{1,0:T(8,128)S(1)} %copy-done), custom_call_target="tpu_custom_call" | custom-call | tf_op jit(solution)/shard_map/kv_kernel/pallas_call | solution.py:535
  82.4 7.1 %all-to-all-start.1 = ((f32[16,8,8,128]{3,2,1,0:T(8,128)}), f32[16,8,8,128]{3,2,1,0:T(8,128)S(1)}, u32[]{:S(2)}, u32[]{:S(2)}) async-start(f32[16,8,8,128]{3,2,1,0:T(8,128)} %bitcast.14), calls=%async_computation.1 | async-start | bytes 1048576 | tf_op jit(solution)/shard_map/all_to_all | solution.py:552
  89.6 0.6 collective-permute-start.14
  90.2 2.3 %first_sum_kernel.1 = (f32[3,256,128]{2,1,0:T(8,128)}, f32[3,256,128]{2,1,0:T(8,128)}) custom-call(f32[4,256,128]{2,1,0:T(8,128)S(1)} %collective-permute-done.9.refs_0_.refs_2_, f32[4,256,128]{2,1,0:T(8,128)S(1)} %collective-permute-done.10.refs_1_.refs_3_, f32[3,256,128]{2,1,0:T(8,128)S(1)} %collective-permute-done.11.refs_2_.refs_4_, ...), custom_call_target="tpu_custom_call" | custom-call | tf_op jit(solution)/shard_map/first_sum_kernel/pallas_call | solution.py:162
  92.6 2.7 %collective-permute-start.13 = (f32[3,256,128]{2,1,0:T(8,128)}, f32[3,256,128]{2,1,0:T(8,128)S(1)}, u32[]{:S(2)}, u32[]{:S(2)}) collective-permute-start(f32[3,256,128]{2,1,0:T(8,128)} %get-tuple-element.56), channel_id=1, source_target_pairs={{0,6},{1,7},{2,0},{3,1},{4,2},{5,3},{6,4},{7,5},{8,14},{9,15},{10,... | collective-permute-start | bytes 1179656 | tf_op jit(solution)/shard_map/ppermute | solution.py:26
  95.2 5.5 %all-to-all-done.1.refs_0_ = f32[16,8,8,128]{3,2,1,0:T(8,128)S(1)} async-done(((f32[16,8,8,128]{3,2,1,0:T(8,128)}), f32[16,8,8,128]{3,2,1,0:T(8,128)S(1)}, u32[]{:S(2)}, u32[]{:S(2)}) %all-to-all-start.1) | async-done | bytes 524320 | tf_op jit(solution)/shard_map/all_to_all | solution.py:552
  100.7 4.7 %conv_kernel.1 = f32[16,8,8,128]{3,2,1,0:T(8,128)} custom-call(f32[16,8,8,128]{3,2,1,0:T(8,128)S(1)} %all-to-all-done.1.refs_0_, f32[1024,256]{1,0:T(8,128)} %taps_kernel.1.refs_4_.refs_1_, bf16[256,128]{1,0:T(8,128)(2,1)} %constant.72.clone.refs_1_.refs_2_, bf16[256,128]{1,0:T(8,128)(2,1)} %constant.73.clone.refs_2_.refs_3_, ...), custom_call_target="tpu_custom_call" | custom-call | tf_op jit(solution)/shard_map/conv_kernel/pallas_call | solution.py:535
  105.5 4.7 %all-to-all-start.2 = ((f32[16,8,8,128]{3,2,1,0:T(8,128)}), f32[16,8,8,128]{3,2,1,0:T(8,128)S(1)}, u32[]{:S(2)}, u32[]{:S(2)}) async-start(f32[16,8,8,128]{3,2,1,0:T(8,128)} %conv_kernel.1), calls=%async_computation.2 | async-start | bytes 1048576 | tf_op jit(solution)/shard_map/all_to_all | solution.py:552
  110.2 0.9 collective-permute-done.14.refs_5_.refs_4_
  111.1 1.4 %query_second_sum_kernel.1 = (f32[2,256,128]{2,1,0:T(8,128)S(1)}, f32[2,256,128]{2,1,0:T(8,128)S(1)}, f32[2,256,128]{2,1,0:T(8,128)S(1)}) custom-call(f32[3,256,128]{2,1,0:T(8,128)S(1)} %collective-permute-done.12.refs_0_, f32[3,256,128]{2,1,0:T(8,128)S(1)} %collective-permute-done.13.refs_1_, f32[4,256,128]{2,1,0:T(8,128)S(1)} %collective-permute-done.9.refs_0_.refs_2_, ...), custom_call_target="tpu_custom_call" | custom-call | tf_op jit(solution)/shard_map/query_second_sum_kernel/pallas_call | solution.py:162
  112.5 0.2 collective-permute-start.16
  112.6 1.4 %collective-permute-start.17 = (f32[2,256,128]{2,1,0:T(8,128)S(1)}, f32[2,256,128]{2,1,0:T(8,128)S(1)}, u32[]{:S(2)}, u32[]{:S(2)}) collective-permute-start(f32[2,256,128]{2,1,0:T(8,128)S(1)} %get-tuple-element.62), channel_id=1, source_target_pairs={{0,1},{1,0},{2,3},{3,2},{4,5},{5,4},{6,7},{7,6},{8,9},{9,8},{10,11... | collective-permute-start | bytes 786440 | tf_op jit(solution)/shard_map/ppermute | solution.py:30
  114.0 0.9 collective-permute-start.15
  114.8 1.3 %query_beside_kernel.1.refs_0_ = f32[4,256,128]{2,1,0:T(8,128)S(1)} custom-call(f32[3,256,128]{2,1,0:T(8,128)S(1)} %collective-permute-done.12.refs_0_, f32[3,256,128]{2,1,0:T(8,128)S(1)} %collective-permute-done.13.refs_1_, f32[4,256,128]{2,1,0:T(8,128)S(1)} %collective-permute-done.9.refs_0_.refs_2_, ...), custom_call_target="tpu_custom_call" | custom-call | tf_op jit(solution)/shard_map/query_beside_kernel/pallas_call | solution.py:162
  116.2 3.6 %collective-permute-done.16.refs_2_ = f32[2,256,128]{2,1,0:T(8,128)S(1)} collective-permute-done((f32[2,256,128]{2,1,0:T(8,128)S(1)}, f32[2,256,128]{2,1,0:T(8,128)S(1)}, u32[]{:S(2)}, u32[]{:S(2)}) %collective-permute-start.16) | collective-permute-done | bytes 262176 | tf_op jit(solution)/shard_map/ppermute | solution.py:26
  119.8 4.5 %collective-permute-done.17.refs_3_ = f32[2,256,128]{2,1,0:T(8,128)S(1)} collective-permute-done((f32[2,256,128]{2,1,0:T(8,128)S(1)}, f32[2,256,128]{2,1,0:T(8,128)S(1)}, u32[]{:S(2)}, u32[]{:S(2)}) %collective-permute-start.17) | collective-permute-done | bytes 262176 | tf_op jit(solution)/shard_map/ppermute | solution.py:30
  124.3 0.1 query_kernel.1.refs_1_
  124.4 1.1 gate_kernel.1
  (25 shorter events, 0.1 us)
Async XLA Ops:
  3.9 14.6 %collective-permute-start = (f32[2,512,128]{2,1,0:T(8,128)S(1)}, f32[2,512,128]{2,1,0:T(8,128)S(1)}, u32[]{:S(2)}, u32[]{:S(2)}) collective-permute-start(f32[2,512,128]{2,1,0:T(8,128)S(1)} %get-tuple-element.34), channel_id=1, source_target_pairs={{0,2},{1,3},{2,4},{3,5},{4,6},{5,7},{6,0},{7,1},{8,10},{9,11},{10,... | collective-permute-start | bytes 1572872 | tf_op jit(solution)/shard_map/ppermute | solution.py:26
  6.0 12.5 %collective-permute-start.1 = (f32[2,512,128]{2,1,0:T(8,128)S(1)}, f32[2,512,128]{2,1,0:T(8,128)S(1)}, u32[]{:S(2)}, u32[]{:S(2)}) collective-permute-start(f32[2,512,128]{2,1,0:T(8,128)S(1)} %get-tuple-element.35), channel_id=1, source_target_pairs={{0,6},{1,7},{2,0},{3,1},{4,2},{5,3},{6,4},{7,5},{8,14},{9,15},{10,... | collective-permute-start | bytes 1572872 | tf_op jit(solution)/shard_map/ppermute | solution.py:26
  7.4 12.7 %collective-permute-start.2 = (f32[2,512,128]{2,1,0:T(8,128)S(1)}, f32[2,512,128]{2,1,0:T(8,128)S(1)}, u32[]{:S(2)}, u32[]{:S(2)}) collective-permute-start(f32[2,512,128]{2,1,0:T(8,128)S(1)} %get-tuple-element.36), channel_id=1, source_target_pairs={{0,1},{1,0},{2,3},{3,2},{4,5},{5,4},{6,7},{7,6},{8,9},{9,8},{10,11... | collective-permute-start | bytes 1572872 | tf_op jit(solution)/shard_map/ppermute | solution.py:30
  16.6 41.8 %collective-permute-start.3 = (f32[5,512,128]{2,1,0:T(8,128)}, f32[5,512,128]{2,1,0:T(8,128)}, u32[]{:S(2)}, u32[]{:S(2)}) collective-permute-start(f32[5,512,128]{2,1,0:T(8,128)} %get-tuple-element.42), channel_id=1, source_target_pairs={{0,1},{1,0},{2,3},{3,2},{4,5},{5,4},{6,7},{7,6},{8,9},{9,8},{10,11... | collective-permute-start | bytes 3932168 | tf_op jit(solution)/shard_map/ppermute | solution.py:30
  20.1 3.2 %copy-start.5 = (f32[1024,128]{1,0:T(8,128)S(1)}, f32[1024,128]{1,0:T(8,128)}, u32[]{:S(2)}) copy-start(f32[1024,128]{1,0:T(8,128)} %refs_0_.1) | copy-start | bytes 1572868
  21.9 36.6 %collective-permute-start.5 = (f32[5,512,128]{2,1,0:T(8,128)}, f32[5,512,128]{2,1,0:T(8,128)}, u32[]{:S(2)}, u32[]{:S(2)}) collective-permute-start(f32[5,512,128]{2,1,0:T(8,128)} %get-tuple-element.43), channel_id=1, source_target_pairs={{0,6},{1,7},{2,0},{3,1},{4,2},{5,3},{6,4},{7,5},{8,14},{9,15},{10,... | collective-permute-start | bytes 3932168 | tf_op jit(solution)/shard_map/ppermute | solution.py:26
  23.0 35.4 %collective-permute-start.4 = (f32[5,512,128]{2,1,0:T(8,128)}, f32[5,512,128]{2,1,0:T(8,128)}, u32[]{:S(2)}, u32[]{:S(2)}) collective-permute-start(f32[5,512,128]{2,1,0:T(8,128)} %get-tuple-element.40.refs_0_.refs_1_), channel_id=1, source_target_pairs={{0,2},{1,3},{2,4},{3,5},{4,6},{5,7},{6,0},{7,1},{8,10},{9,11},{10,... | collective-permute-start | bytes 3932168 | tf_op jit(solution)/shard_map/ppermute | solution.py:26
  24.5 34.0 %all-to-all-start = ((f32[16,8,8,128]{3,2,1,0:T(8,128)}), f32[16,8,8,128]{3,2,1,0:T(8,128)}, u32[]{:S(2)}, u32[]{:S(2)}) async-start(f32[16,8,8,128]{3,2,1,0:T(8,128)} %bitcast.15), calls=%async_computation | async-start | bytes 1048576 | tf_op jit(solution)/shard_map/all_to_all | solution.py:552
  44.2 1.0 copy-start.3
  45.2 13.2 %copy-start.4 = (f32[4,256,128]{2,1,0:T(8,128)S(1)}, f32[4,256,128]{2,1,0:T(8,128)}, u32[]{:S(2)}) copy-start(f32[4,256,128]{2,1,0:T(8,128)} %get-tuple-element.41.refs_1_.refs_9_.refs_0_) | copy-start | bytes 1572868
  60.7 19.1 %collective-permute-start.8 = (f32[3,512,128]{2,1,0:T(8,128)}, f32[3,512,128]{2,1,0:T(8,128)}, u32[]{:S(2)}, u32[]{:S(2)}) collective-permute-start(f32[3,512,128]{2,1,0:T(8,128)} %kv_other_kernel.1.refs_10_), channel_id=1, source_target_pairs={{0,1},{1,0},{2,3},{3,2},{4,5},{5,4},{6,7},{7,6},{8,9},{9,8},{10,11... | collective-permute-start | bytes 2359304 | tf_op jit(solution)/shard_map/ppermute | solution.py:30
  63.1 13.5 %collective-permute-start.7 = (f32[2,512,128]{2,1,0:T(8,128)}, f32[2,512,128]{2,1,0:T(8,128)}, u32[]{:S(2)}, u32[]{:S(2)}) collective-permute-start(f32[2,512,128]{2,1,0:T(8,128)} %get-tuple-element.45), channel_id=1, source_target_pairs={{0,6},{1,7},{2,0},{3,1},{4,2},{5,3},{6,4},{7,5},{8,14},{9,15},{10,... | collective-permute-start | bytes 1572872 | tf_op jit(solution)/shard_map/ppermute | solution.py:26
  64.3 14.4 %collective-permute-start.6 = (f32[2,512,128]{2,1,0:T(8,128)}, f32[2,512,128]{2,1,0:T(8,128)}, u32[]{:S(2)}, u32[]{:S(2)}) collective-permute-start(f32[2,512,128]{2,1,0:T(8,128)} %get-tuple-element.44.refs_9_), channel_id=1, source_target_pairs={{0,2},{1,3},{2,4},{3,5},{4,6},{5,7},{6,0},{7,1},{8,10},{9,11},{10,... | collective-permute-start | bytes 1572872 | tf_op jit(solution)/shard_map/ppermute | solution.py:26
  65.9 3.7 %copy-start.1 = (f32[4,512,128]{2,1,0:T(8,128)}, f32[4,512,128]{2,1,0:T(8,128)S(1)}, u32[]{:S(2)}) copy-start(f32[4,512,128]{2,1,0:T(8,128)S(1)} %kv_beside_kernel.1.refs_7_.refs_0_) | copy-start | bytes 3145732
  69.6 10.2 %copy-start = (f32[1024,256]{1,0:T(8,128)S(1)}, f32[1024,256]{1,0:T(8,128)}, u32[]{:S(2)}) copy-start(f32[1024,256]{1,0:T(8,128)} %taps_kernel.1.refs_4_.refs_1_) | copy-start | bytes 3145732
  69.6 10.2 %copy-start.2 = (f32[4,512,128]{2,1,0:T(8,128)S(1)}, f32[4,512,128]{2,1,0:T(8,128)}, u32[]{:S(2)}) copy-start(f32[4,512,128]{2,1,0:T(8,128)} %copy-done.1) | copy-start | bytes 3145732
  69.6 20.6 %collective-permute-start.9 = (f32[4,256,128]{2,1,0:T(8,128)}, f32[4,256,128]{2,1,0:T(8,128)S(1)}, u32[]{:S(2)}, u32[]{:S(2)}) collective-permute-start(f32[4,256,128]{2,1,0:T(8,128)} %get-tuple-element.49), channel_id=1, source_target_pairs={{0,2},{1,3},{2,4},{3,5},{4,6},{5,7},{6,0},{7,1},{8,10},{9,11},{10,... | collective-permute-start | bytes 1572872 | tf_op jit(solution)/shard_map/ppermute | solution.py:26
  69.9 20.4 %collective-permute-start.10 = (f32[4,256,128]{2,1,0:T(8,128)}, f32[4,256,128]{2,1,0:T(8,128)S(1)}, u32[]{:S(2)}, u32[]{:S(2)}) collective-permute-start(f32[4,256,128]{2,1,0:T(8,128)} %get-tuple-element.50), channel_id=1, source_target_pairs={{0,6},{1,7},{2,0},{3,1},{4,2},{5,3},{6,4},{7,5},{8,14},{9,15},{10,... | collective-permute-start | bytes 1572872 | tf_op jit(solution)/shard_map/ppermute | solution.py:26
  76.6 13.7 %collective-permute-start.11 = (f32[3,256,128]{2,1,0:T(8,128)}, f32[3,256,128]{2,1,0:T(8,128)S(1)}, u32[]{:S(2)}, u32[]{:S(2)}) collective-permute-start(f32[3,256,128]{2,1,0:T(8,128)} %get-tuple-element.51), channel_id=1, source_target_pairs={{0,1},{1,0},{2,3},{3,2},{4,5},{5,4},{6,7},{7,6},{8,9},{9,8},{10,11... | collective-permute-start | bytes 1179656 | tf_op jit(solution)/shard_map/ppermute | solution.py:30
  82.4 18.3 %all-to-all-start.1 = ((f32[16,8,8,128]{3,2,1,0:T(8,128)}), f32[16,8,8,128]{3,2,1,0:T(8,128)S(1)}, u32[]{:S(2)}, u32[]{:S(2)}) async-start(f32[16,8,8,128]{3,2,1,0:T(8,128)} %bitcast.14), calls=%async_computation.1 | async-start | bytes 1048576 | tf_op jit(solution)/shard_map/all_to_all | solution.py:552
  89.6 21.5 %collective-permute-start.14 = (f32[5,256,128]{2,1,0:T(8,128)}, f32[5,256,128]{2,1,0:T(8,128)S(1)}, u32[]{:S(2)}, u32[]{:S(2)}) collective-permute-start(f32[5,256,128]{2,1,0:T(8,128)} %get-tuple-element.57), channel_id=1, source_target_pairs={{0,1},{1,0},{2,3},{3,2},{4,5},{5,4},{6,7},{7,6},{8,9},{9,8},{10,11... | collective-permute-start | bytes 1966088 | tf_op jit(solution)/shard_map/ppermute | solution.py:30
  92.6 18.5 %collective-permute-start.12 = (f32[3,256,128]{2,1,0:T(8,128)}, f32[3,256,128]{2,1,0:T(8,128)S(1)}, u32[]{:S(2)}, u32[]{:S(2)}) collective-permute-start(f32[3,256,128]{2,1,0:T(8,128)} %get-tuple-element.55), channel_id=1, source_target_pairs={{0,2},{1,3},{2,4},{3,5},{4,6},{5,7},{6,0},{7,1},{8,10},{9,11},{10,... | collective-permute-start | bytes 1179656 | tf_op jit(solution)/shard_map/ppermute | solution.py:26
  92.6 18.5 %collective-permute-start.13 = (f32[3,256,128]{2,1,0:T(8,128)}, f32[3,256,128]{2,1,0:T(8,128)S(1)}, u32[]{:S(2)}, u32[]{:S(2)}) collective-permute-start(f32[3,256,128]{2,1,0:T(8,128)} %get-tuple-element.56), channel_id=1, source_target_pairs={{0,6},{1,7},{2,0},{3,1},{4,2},{5,3},{6,4},{7,5},{8,14},{9,15},{10,... | collective-permute-start | bytes 1179656 | tf_op jit(solution)/shard_map/ppermute | solution.py:26
  105.5 18.9 %all-to-all-start.2 = ((f32[16,8,8,128]{3,2,1,0:T(8,128)}), f32[16,8,8,128]{3,2,1,0:T(8,128)S(1)}, u32[]{:S(2)}, u32[]{:S(2)}) async-start(f32[16,8,8,128]{3,2,1,0:T(8,128)} %conv_kernel.1), calls=%async_computation.2 | async-start | bytes 1048576 | tf_op jit(solution)/shard_map/all_to_all | solution.py:552
  112.5 7.3 %collective-permute-start.16 = (f32[2,256,128]{2,1,0:T(8,128)S(1)}, f32[2,256,128]{2,1,0:T(8,128)S(1)}, u32[]{:S(2)}, u32[]{:S(2)}) collective-permute-start(f32[2,256,128]{2,1,0:T(8,128)S(1)} %get-tuple-element.61), channel_id=1, source_target_pairs={{0,6},{1,7},{2,0},{3,1},{4,2},{5,3},{6,4},{7,5},{8,14},{9,15},{10,... | collective-permute-start | bytes 786440 | tf_op jit(solution)/shard_map/ppermute | solution.py:26
  112.6 11.7 %collective-permute-start.17 = (f32[2,256,128]{2,1,0:T(8,128)S(1)}, f32[2,256,128]{2,1,0:T(8,128)S(1)}, u32[]{:S(2)}, u32[]{:S(2)}) collective-permute-start(f32[2,256,128]{2,1,0:T(8,128)S(1)} %get-tuple-element.62), channel_id=1, source_target_pairs={{0,1},{1,0},{2,3},{3,2},{4,5},{5,4},{6,7},{7,6},{8,9},{9,8},{10,11... | collective-permute-start | bytes 786440 | tf_op jit(solution)/shard_map/ppermute | solution.py:30
  114.0 10.3 %collective-permute-start.15 = (f32[2,256,128]{2,1,0:T(8,128)S(1)}, f32[2,256,128]{2,1,0:T(8,128)S(1)}, u32[]{:S(2)}, u32[]{:S(2)}) collective-permute-start(f32[2,256,128]{2,1,0:T(8,128)S(1)} %get-tuple-element.60.refs_7_), channel_id=1, source_target_pairs={{0,2},{1,3},{2,4},{3,5},{4,6},{5,7},{6,0},{7,1},{8,10},{9,11},{10,... | collective-permute-start | bytes 786440 | tf_op jit(solution)/shard_map/ppermute | solution.py:26

commit v15 on v14

--- a/solution.py
+++ b/solution.py
@@ -579,23 +579,22 @@
         return hold["taps"], hold["query"][0]
 
     kv_parts, kv_part = reduce_kv(kv_halves, place, activations, weight, prepare)
+    kv = call(
+        kv_kernel,
+        turned_shape,
+        *kv_parts,
+        scratch=[pltpu.VMEM((tokens, channels), jnp.float32)],
+        to_hbm=True,
+    )
     spectrum = call(
         taps_kernel,
         (owned * length // BLOCK, 2 * BLOCK),
         hold["taps"],
         tables=first + turn + second,
-        after=(kv_part,),
+        after=(kv,),
         to_hbm=True,
     )
-    kv = call(
-        kv_kernel,
-        turned_shape,
-        *kv_parts,
-        after=(spectrum,),
-        scratch=[pltpu.VMEM((tokens, channels), jnp.float32)],
-        to_hbm=True,
-    )
-    q_parts = reduce_query(q_halves, hold["query"], spectrum)
+    q_parts = reduce_query(q_halves, hold["query"], kv_part)
     moved = exchange(kv.reshape(moved_shape))
     convolved = call(
         conv_kernel,

time: 126 us -> 129 us (1.024)
  local copies, waits for them, and re-layouts: 1.14 us -> 3.14 us
    ppermute x12, waiting for transfers between devices: 10.5 us -> 14.7 us  [shift_x(): lax.ppermute(value, 'chan', [(i, (i + 2 * step) % 8) for i in range(8)])]
    all_to_all x3, waiting for transfers between devices: 11.8 us -> 8.38 us  [exchange(): return lax.all_to_all(value, 'seq', split_axis=0, concat_axis=0, tiled=True)]
    unnamed x12 -> x14, local copies, waits for them, and re-layouts: 1.06 us -> 3.05 us
    all_to_all x3, starting transfers between devices: 23.7 us -> 25.5 us  [exchange(): return lax.all_to_all(value, 'seq', split_axis=0, concat_axis=0, tiled=True)]
    ppermute x6, waiting for transfers between devices: 8.17 us -> 6.45 us  [swap_z(): return lax.ppermute(value, 'chan', [(i, i ^ 1) for i in range(8)])]
  transfers between devices with their start and end apart: 21 -> 21, of which waited for: 10 -> 9; matrix products, arithmetic and copies ran while one was open for 0% -> 0% of each run, Pallas kernels for 36% -> 35%
where the time goes in v15:
time: 129 us; the launch traced here: 128 us
  Pallas kernels  52.5 us (41%)
  starting transfers between devices  42.3 us (33%)
  waiting for transfers between devices  29.5 us (23%)
  local copies, waits for them, and re-layouts  3.14 us (2%)
    all_to_all x3, starting transfers between devices, exchange(): return lax.all_to_all(value, 'seq', split_axis=0, concat_axis=0, tiled=True)  25.5 us
    pallas_call x3, Pallas kernels, project(): pl.pallas_call(body, grid_spec=pltpu.PrefetchScalarGridSpec(num_scalar_pr...  18.3 us
    ppermute x12, waiting for transfers between devices, shift_x(): lax.ppermute(value, 'chan', [(i, (i + 2 * step) % 8) for i in range(8)])  14.7 us
    pallas_call x6, Pallas kernels, call(): pl.pallas_call(body, grid=(1,), in_specs=[pl.BlockSpec(memory_space=pltpu...  12.9 us
    ppermute x12, starting transfers between devices, shift_x(): lax.ppermute(value, 'chan', [(i, (i + 2 * step) % 8) for i in range(8)])  12.8 us
    all_to_all x3, waiting for transfers between devices, exchange(): return lax.all_to_all(value, 'seq', split_axis=0, concat_axis=0, tiled=True)  8.38 us
    pallas_call x1, Pallas kernels, project_query(): pl.pallas_call(query_project_kernel, grid_spec=pltpu.PrefetchScalarGridSp...  7.88 us
    pallas_call x4, Pallas kernels, sum_call(): pl.pallas_call(body, grid=(halves.rows // tile,), in_specs=[pl.BlockSpec(...  7.51 us
  transfers between devices with their start and end apart: 21, of which 9 were waited for; matrix products, arithmetic and copies ran while one was open for 0% of the time, Pallas kernels for 35%

profile of v15, /device:TPU:1, one launch (start us, length us, event | category | flops | bytes accessed | tf_op | source)
XLA Modules:
  0.0 127.6 jit_solution(12981651092287141348)
XLA Ops:
  0.0 0.1 stack.23.at.place
  0.1 3.8 %first_kernel.1 = (f32[2,512,128]{2,1,0:T(8,128)S(1)}, f32[2,512,128]{2,1,0:T(8,128)S(1)}, f32[2,512,128]{2,1,0:T(8,128)S(1)}, f32[2,512,128]{2,1,0:T(8,128)S(1)}) custom-call(s32[5]{0:T(128)S(1)} %stack.23.at.place, bf16[1024,1024]{1,0:T(8,128)(2,1)} %act.7, bf16[3,1024,1024]{2,1,0:T(8,128)(2,1)} %bitcast.11), custom_call_target="tpu_custom_call" | custom-call | tf_op jit(solution)/shard_map/first_kernel/pallas_call | solution.py:135
  3.9 2.1 %collective-permute-start = (f32[2,512,128]{2,1,0:T(8,128)S(1)}, f32[2,512,128]{2,1,0:T(8,128)S(1)}, u32[]{:S(2)}, u32[]{:S(2)}) collective-permute-start(f32[2,512,128]{2,1,0:T(8,128)S(1)} %get-tuple-element.34), channel_id=1, source_target_pairs={{0,2},{1,3},{2,4},{3,5},{4,6},{5,7},{6,0},{7,1},{8,10},{9,11},{10,... | collective-permute-start | bytes 1572872 | tf_op jit(solution)/shard_map/ppermute | solution.py:26
  6.0 1.4 %collective-permute-start.1 = (f32[2,512,128]{2,1,0:T(8,128)S(1)}, f32[2,512,128]{2,1,0:T(8,128)S(1)}, u32[]{:S(2)}, u32[]{:S(2)}) collective-permute-start(f32[2,512,128]{2,1,0:T(8,128)S(1)} %get-tuple-element.35), channel_id=1, source_target_pairs={{0,6},{1,7},{2,0},{3,1},{4,2},{5,3},{6,4},{7,5},{8,14},{9,15},{10,... | collective-permute-start | bytes 1572872 | tf_op jit(solution)/shard_map/ppermute | solution.py:26
  7.4 1.8 %collective-permute-start.2 = (f32[2,512,128]{2,1,0:T(8,128)S(1)}, f32[2,512,128]{2,1,0:T(8,128)S(1)}, u32[]{:S(2)}, u32[]{:S(2)}) collective-permute-start(f32[2,512,128]{2,1,0:T(8,128)S(1)} %get-tuple-element.36), channel_id=1, source_target_pairs={{0,1},{1,0},{2,3},{3,2},{4,5},{5,4},{6,7},{7,6},{8,9},{9,8},{10,11... | collective-permute-start | bytes 1572872 | tf_op jit(solution)/shard_map/ppermute | solution.py:30
  9.2 7.5 %second_kernel.1 = (f32[5,512,128]{2,1,0:T(8,128)S(1)}, f32[5,512,128]{2,1,0:T(8,128)S(1)}, f32[5,512,128]{2,1,0:T(8,128)}) custom-call(s32[5]{0:T(128)S(1)} %stack.23.at.place, bf16[1024,1024]{1,0:T(8,128)(2,1)} %act.7, bf16[3,1024,1024]{2,1,0:T(8,128)(2,1)} %bitcast.12, f32[2,512,128]{2,1,0:T(8,128)S(1)} %get-tuple-element.37.refs_0_.refs_5_), custom_call_target="tpu_custom_call" | custom-call | tf_op jit(solution)/shard_map/second_kernel/pallas_call | solution.py:135
  16.6 1.9 %collective-permute-done.refs_0_ = f32[2,512,128]{2,1,0:T(8,128)S(1)} collective-permute-done((f32[2,512,128]{2,1,0:T(8,128)S(1)}, f32[2,512,128]{2,1,0:T(8,128)S(1)}, u32[]{:S(2)}, u32[]{:S(2)}) %collective-permute-start) | collective-permute-done | bytes 524320 | tf_op jit(solution)/shard_map/ppermute | solution.py:26
  18.5 1.6 %collective-permute-done.2.refs_2_ = f32[2,512,128]{2,1,0:T(8,128)S(1)} collective-permute-done((f32[2,512,128]{2,1,0:T(8,128)S(1)}, f32[2,512,128]{2,1,0:T(8,128)S(1)}, u32[]{:S(2)}, u32[]{:S(2)}) %collective-permute-start.2) | collective-permute-done | bytes 524320 | tf_op jit(solution)/shard_map/ppermute | solution.py:30
  20.1 1.7 %kv_first_sum_kernel.1 = (f32[5,512,128]{2,1,0:T(8,128)}, f32[5,512,128]{2,1,0:T(8,128)}) custom-call(f32[2,512,128]{2,1,0:T(8,128)S(1)} %collective-permute-done.refs_0_, f32[2,512,128]{2,1,0:T(8,128)S(1)} %collective-permute-done.1.refs_1_, f32[2,512,128]{2,1,0:T(8,128)S(1)} %collective-permute-done.2.refs_2_, ...), custom_call_target="tpu_custom_call" | custom-call | tf_op jit(solution)/shard_map/kv_first_sum_kernel/pallas_call | solution.py:162
  21.9 1.2 collective-permute-start.5
  23.0 0.3 collective-permute-start.4
  23.3 1.1 taps_turn_kernel.1
  24.5 11.8 %all-to-all-start = ((f32[16,8,8,128]{3,2,1,0:T(8,128)}), f32[16,8,8,128]{3,2,1,0:T(8,128)S(1)}, u32[]{:S(2)}, u32[]{:S(2)}) async-start(f32[16,8,8,128]{3,2,1,0:T(8,128)} %bitcast.15), calls=%async_computation | async-start | bytes 1048576 | tf_op jit(solution)/shard_map/all_to_all | solution.py:552
  36.3 7.9 %query_project_kernel.1 = (f32[4,256,128]{2,1,0:T(8,128)}, f32[4,256,128]{2,1,0:T(8,128)}, f32[2,256,128]{2,1,0:T(8,128)}, f32[2,256,128]{2,1,0:T(8,128)}, f32[3...) custom-call(s32[5]{0:T(128)S(1)} %stack.23.at.place, ...), custom_call_target="tpu_custom_call" | custom-call | tf_op jit(solution)/shard_map/query_project_kernel/pallas_call | solution.py:351
  44.2 1.0 copy-done.2
  45.2 6.9 %third_kernel.1.refs_0_.refs_1_.refs_6_.refs_2_.refs_3_.refs_4_ = f32[11,512,128]{2,1,0:T(8,128)S(1)} custom-call(s32[5]{0:T(128)S(1)} %stack.23.at.place, bf16[1024,1024]{1,0:T(8,128)(2,1)} %act.7, bf16[3,1024,1024]{2,1,0:T(8,128)(2,1)} %bitcast.14, f32[5,512,128]{2,1,0:T(8,128)} %get-tuple-element.40.refs_0_.refs_1_, f32[4,256,128]{2,1,0:T(8,128)S(1)} %copy-done.2), custom_call_target="tpu_custom_call" | custom-call | tf_op jit(solution)/shard_map/third_kernel/pallas_call | solution.py:135
  52.2 6.2 %all-to-all-done.refs_8_.refs_0_ = f32[16,8,8,128]{3,2,1,0:T(8,128)S(1)} async-done(((f32[16,8,8,128]{3,2,1,0:T(8,128)}), f32[16,8,8,128]{3,2,1,0:T(8,128)S(1)}, u32[]{:S(2)}, u32[]{:S(2)}) %all-to-all-start) | async-done | bytes 524320 | tf_op jit(solution)/shard_map/all_to_all | solution.py:552
  58.4 0.0 copy-start.3
  58.4 1.0 copy-done.3
  59.4 2.2 %kv_other_kernel.1.refs_10_ = f32[3,512,128]{2,1,0:T(8,128)} custom-call(f32[11,512,128]{2,1,0:T(8,128)S(1)} %third_kernel.1.refs_0_.refs_1_.refs_6_.refs_2_.refs_3_.refs_4_, f32[11,512,128]{2,1,0:T(8,128)S(1)} %third_kernel.1.refs_0_.refs_1_.refs_6_.refs_2_.refs_3_.refs_4_, f32[5,512,128]{2,1,0:T(8,128)} %collective-permute-done.4.refs_2_.refs_3_.refs_8_.refs_5_.refs_6_, ...), custom_call_target="tpu_custom_call" | custom-call | tf_op jit(solution)/shard_map/kv_other_kernel/pallas_call | solution.py:200
  61.6 2.4 %kv_last_kernel.1 = (f32[2,512,128]{2,1,0:T(8,128)}, f32[2,512,128]{2,1,0:T(8,128)}) custom-call(f32[11,512,128]{2,1,0:T(8,128)S(1)} %third_kernel.1.refs_0_.refs_1_.refs_6_.refs_2_.refs_3_.refs_4_, f32[11,512,128]{2,1,0:T(8,128)S(1)} %third_kernel.1.refs_0_.refs_1_.refs_6_.refs_2_.refs_3_.refs_4_, ...), custom_call_target="tpu_custom_call" | custom-call | tf_op jit(solution)/shard_map/kv_last_kernel/pallas_call | solution.py:200
  64.0 1.3 collective-permute-start.7
  65.2 0.2 collective-permute-start.6
  65.4 1.4 %kv_beside_kernel.1.refs_0_.refs_4_ = f32[4,512,128]{2,1,0:T(8,128)S(1)} custom-call(f32[11,512,128]{2,1,0:T(8,128)S(1)} %third_kernel.1.refs_0_.refs_1_.refs_6_.refs_2_.refs_3_.refs_4_, f32[11,512,128]{2,1,0:T(8,128)S(1)} %third_kernel.1.refs_0_.refs_1_.refs_6_.refs_2_.refs_3_.refs_4_, ...), custom_call_target="tpu_custom_call" | custom-call | tf_op jit(solution)/shard_map/kv_beside_kernel/pallas_call | solution.py:200
  66.8 1.0 copy-done
  67.8 2.7 %collective-permute-start.10 = (f32[4,256,128]{2,1,0:T(8,128)}, f32[4,256,128]{2,1,0:T(8,128)S(1)}, u32[]{:S(2)}, u32[]{:S(2)}) collective-permute-start(f32[4,256,128]{2,1,0:T(8,128)} %get-tuple-element.50), channel_id=1, source_target_pairs={{0,6},{1,7},{2,0},{3,1},{4,2},{5,3},{6,4},{7,5},{8,14},{9,15},{10,... | collective-permute-start | bytes 1572872 | tf_op jit(solution)/shard_map/ppermute | solution.py:26
  70.5 7.0 %collective-permute-done.7.refs_2_ = f32[2,512,128]{2,1,0:T(8,128)} collective-permute-done((f32[2,512,128]{2,1,0:T(8,128)}, f32[2,512,128]{2,1,0:T(8,128)}, u32[]{:S(2)}, u32[]{:S(2)}) %collective-permute-start.7) | collective-permute-done | bytes 524320 | tf_op jit(solution)/shard_map/ppermute | solution.py:26
  77.5 1.1 collective-permute-start.11
  78.6 1.0 collective-permute-done.6.refs_1_
  79.6 1.1 collective-permute-done.8.refs_3_
  80.7 2.6 %kv_kernel.1.refs_7_ = f32[128,8,128]{2,1,0:T(8,128)} custom-call(f32[4,512,128]{2,1,0:T(8,128)S(1)} %copy-done.1, f32[2,512,128]{2,1,0:T(8,128)} %collective-permute-done.6.refs_1_, f32[2,512,128]{2,1,0:T(8,128)} %collective-permute-done.7.refs_2_, f32[3,512,128]{2,1,0:T(8,128)} %collective-permute-done.8.refs_3_), custom_call_target="tpu_custom_call" | custom-call | tf_op jit(solution)/shard_map/kv_kernel/pallas_call | solution.py:535
  83.3 7.2 %all-to-all-start.1 = ((f32[16,8,8,128]{3,2,1,0:T(8,128)}), f32[16,8,8,128]{3,2,1,0:T(8,128)S(1)}, u32[]{:S(2)}, u32[]{:S(2)}) async-start(f32[16,8,8,128]{3,2,1,0:T(8,128)} %bitcast.9), calls=%async_computation.1 | async-start | bytes 1048576 | tf_op jit(solution)/shard_map/all_to_all | solution.py:552
  90.6 0.6 collective-permute-start.14
  91.2 2.5 %first_sum_kernel.1 = (f32[3,256,128]{2,1,0:T(8,128)}, f32[3,256,128]{2,1,0:T(8,128)}) custom-call(f32[4,256,128]{2,1,0:T(8,128)S(1)} %collective-permute-done.9.refs_0_.refs_2_, f32[4,256,128]{2,1,0:T(8,128)S(1)} %collective-permute-done.10.refs_1_.refs_3_, f32[3,256,128]{2,1,0:T(8,128)} %collective-permute-done.11.refs_2_.refs_4_, ...), custom_call_target="tpu_custom_call" | custom-call | tf_op jit(solution)/shard_map/first_sum_kernel/pallas_call | solution.py:162
  93.7 2.7 %collective-permute-start.13 = (f32[3,256,128]{2,1,0:T(8,128)}, f32[3,256,128]{2,1,0:T(8,128)}, u32[]{:S(2)}, u32[]{:S(2)}) collective-permute-start(f32[3,256,128]{2,1,0:T(8,128)} %get-tuple-element.56), channel_id=1, source_target_pairs={{0,6},{1,7},{2,0},{3,1},{4,2},{5,3},{6,4},{7,5},{8,14},{9,15},{10,... | collective-permute-start | bytes 1179656 | tf_op jit(solution)/shard_map/ppermute | solution.py:26
  96.4 3.1 %taps_kernel.1.refs_1_ = f32[1024,256]{1,0:T(8,128)} custom-call(f32[16,8,8,128]{3,2,1,0:T(8,128)S(1)} %all-to-all-done.refs_8_.refs_0_, bf16[256,128]{1,0:T(8,128)(2,1)} %constant.72.clone.refs_1_.refs_2_, bf16[256,128]{1,0:T(8,128)(2,1)} %constant.73.clone.refs_2_.refs_3_, f32[128,128]{1,0:T(8,128)} %constant.74.clone.refs_3_.refs_4_, ...), custom_call_target="tpu_custom_call" | custom-call | tf_op jit(solution)/shard_map/taps_kernel/pallas_call | solution.py:535
  99.5 2.2 %all-to-all-done.1.refs_0_ = f32[16,8,8,128]{3,2,1,0:T(8,128)S(1)} async-done(((f32[16,8,8,128]{3,2,1,0:T(8,128)}), f32[16,8,8,128]{3,2,1,0:T(8,128)S(1)}, u32[]{:S(2)}, u32[]{:S(2)}) %all-to-all-start.1) | async-done | bytes 524320 | tf_op jit(solution)/shard_map/all_to_all | solution.py:552
  101.7 4.7 %conv_kernel.1 = f32[16,8,8,128]{3,2,1,0:T(8,128)} custom-call(f32[16,8,8,128]{3,2,1,0:T(8,128)S(1)} %all-to-all-done.1.refs_0_, f32[1024,256]{1,0:T(8,128)} %taps_kernel.1.refs_1_, bf16[256,128]{1,0:T(8,128)(2,1)} %constant.72.clone.refs_1_.refs_2_, bf16[256,128]{1,0:T(8,128)(2,1)} %constant.73.clone.refs_2_.refs_3_, ...), custom_call_target="tpu_custom_call" | custom-call | tf_op jit(solution)/shard_map/conv_kernel/pallas_call | solution.py:535
  106.5 6.4 %all-to-all-start.2 = ((f32[16,8,8,128]{3,2,1,0:T(8,128)}), f32[16,8,8,128]{3,2,1,0:T(8,128)S(1)}, u32[]{:S(2)}, u32[]{:S(2)}) async-start(f32[16,8,8,128]{3,2,1,0:T(8,128)} %conv_kernel.1), calls=%async_computation.2 | async-start | bytes 1048576 | tf_op jit(solution)/shard_map/all_to_all | solution.py:552
  113.0 1.7 %query_second_sum_kernel.1 = (f32[2,256,128]{2,1,0:T(8,128)S(1)}, f32[2,256,128]{2,1,0:T(8,128)S(1)}, f32[2,256,128]{2,1,0:T(8,128)S(1)}) custom-call(f32[3,256,128]{2,1,0:T(8,128)} %collective-permute-done.12.refs_0_, f32[3,256,128]{2,1,0:T(8,128)} %collective-permute-done.13.refs_1_, f32[4,256,128]{2,1,0:T(8,128)S(1)} %collective-permute-done.9.refs_0_.refs_2_, ...), custom_call_target="tpu_custom_call" | custom-call | tf_op jit(solution)/shard_map/query_second_sum_kernel/pallas_call | solution.py:162
  114.7 0.1 collective-permute-start.16
  114.8 0.5 collective-permute-start.17
  115.2 1.0 collective-permute-start.15
  116.3 1.6 %query_beside_kernel.1.refs_0_ = f32[4,256,128]{2,1,0:T(8,128)S(1)} custom-call(f32[3,256,128]{2,1,0:T(8,128)} %collective-permute-done.12.refs_0_, f32[3,256,128]{2,1,0:T(8,128)} %collective-permute-done.13.refs_1_, f32[4,256,128]{2,1,0:T(8,128)S(1)} %collective-permute-done.9.refs_0_.refs_2_, f32[4,256,128]{2,1,0:T(8,128)S(1)} %collective-permute-done.10.refs_1_.refs_3_, ...), custom_call_target="tpu_custom_call" | custom-call | tf_op jit(solution)/shard_map/query_beside_kernel/pallas_call | solution.py:162
  117.8 4.8 %collective-permute-done.16.refs_2_ = f32[2,256,128]{2,1,0:T(8,128)S(1)} collective-permute-done((f32[2,256,128]{2,1,0:T(8,128)S(1)}, f32[2,256,128]{2,1,0:T(8,128)S(1)}, u32[]{:S(2)}, u32[]{:S(2)}) %collective-permute-start.16) | collective-permute-done | bytes 262176 | tf_op jit(solution)/shard_map/ppermute | solution.py:26
  122.6 3.8 %collective-permute-done.17.refs_3_ = f32[2,256,128]{2,1,0:T(8,128)S(1)} collective-permute-done((f32[2,256,128]{2,1,0:T(8,128)S(1)}, f32[2,256,128]{2,1,0:T(8,128)S(1)}, u32[]{:S(2)}, u32[]{:S(2)}) %collective-permute-start.17) | collective-permute-done | bytes 262176 | tf_op jit(solution)/shard_map/ppermute | solution.py:30
  126.4 0.1 query_kernel.1.refs_1_
  126.5 1.1 gate_kernel.1
  (27 shorter events, 0.1 us)
Async XLA Ops:
  3.9 14.6 %collective-permute-start = (f32[2,512,128]{2,1,0:T(8,128)S(1)}, f32[2,512,128]{2,1,0:T(8,128)S(1)}, u32[]{:S(2)}, u32[]{:S(2)}) collective-permute-start(f32[2,512,128]{2,1,0:T(8,128)S(1)} %get-tuple-element.34), channel_id=1, source_target_pairs={{0,2},{1,3},{2,4},{3,5},{4,6},{5,7},{6,0},{7,1},{8,10},{9,11},{10,... | collective-permute-start | bytes 1572872 | tf_op jit(solution)/shard_map/ppermute | solution.py:26
  6.0 12.5 %collective-permute-start.1 = (f32[2,512,128]{2,1,0:T(8,128)S(1)}, f32[2,512,128]{2,1,0:T(8,128)S(1)}, u32[]{:S(2)}, u32[]{:S(2)}) collective-permute-start(f32[2,512,128]{2,1,0:T(8,128)S(1)} %get-tuple-element.35), channel_id=1, source_target_pairs={{0,6},{1,7},{2,0},{3,1},{4,2},{5,3},{6,4},{7,5},{8,14},{9,15},{10,... | collective-permute-start | bytes 1572872 | tf_op jit(solution)/shard_map/ppermute | solution.py:26
  7.4 12.7 %collective-permute-start.2 = (f32[2,512,128]{2,1,0:T(8,128)S(1)}, f32[2,512,128]{2,1,0:T(8,128)S(1)}, u32[]{:S(2)}, u32[]{:S(2)}) collective-permute-start(f32[2,512,128]{2,1,0:T(8,128)S(1)} %get-tuple-element.36), channel_id=1, source_target_pairs={{0,1},{1,0},{2,3},{3,2},{4,5},{5,4},{6,7},{7,6},{8,9},{9,8},{10,11... | collective-permute-start | bytes 1572872 | tf_op jit(solution)/shard_map/ppermute | solution.py:30
  16.6 41.7 %collective-permute-start.3 = (f32[5,512,128]{2,1,0:T(8,128)}, f32[5,512,128]{2,1,0:T(8,128)}, u32[]{:S(2)}, u32[]{:S(2)}) collective-permute-start(f32[5,512,128]{2,1,0:T(8,128)} %get-tuple-element.42), channel_id=1, source_target_pairs={{0,1},{1,0},{2,3},{3,2},{4,5},{5,4},{6,7},{7,6},{8,9},{9,8},{10,11... | collective-permute-start | bytes 3932168 | tf_op jit(solution)/shard_map/ppermute | solution.py:30
  20.1 3.2 %copy-start.5 = (f32[1024,128]{1,0:T(8,128)S(1)}, f32[1024,128]{1,0:T(8,128)}, u32[]{:S(2)}) copy-start(f32[1024,128]{1,0:T(8,128)} %refs_0_.1) | copy-start | bytes 1572868
  21.9 36.5 %collective-permute-start.5 = (f32[5,512,128]{2,1,0:T(8,128)}, f32[5,512,128]{2,1,0:T(8,128)}, u32[]{:S(2)}, u32[]{:S(2)}) collective-permute-start(f32[5,512,128]{2,1,0:T(8,128)} %get-tuple-element.43), channel_id=1, source_target_pairs={{0,6},{1,7},{2,0},{3,1},{4,2},{5,3},{6,4},{7,5},{8,14},{9,15},{10,... | collective-permute-start | bytes 3932168 | tf_op jit(solution)/shard_map/ppermute | solution.py:26
  23.0 35.3 %collective-permute-start.4 = (f32[5,512,128]{2,1,0:T(8,128)}, f32[5,512,128]{2,1,0:T(8,128)}, u32[]{:S(2)}, u32[]{:S(2)}) collective-permute-start(f32[5,512,128]{2,1,0:T(8,128)} %get-tuple-element.40.refs_0_.refs_1_), channel_id=1, source_target_pairs={{0,2},{1,3},{2,4},{3,5},{4,6},{5,7},{6,0},{7,1},{8,10},{9,11},{10,... | collective-permute-start | bytes 3932168 | tf_op jit(solution)/shard_map/ppermute | solution.py:26
  24.5 33.9 %all-to-all-start = ((f32[16,8,8,128]{3,2,1,0:T(8,128)}), f32[16,8,8,128]{3,2,1,0:T(8,128)S(1)}, u32[]{:S(2)}, u32[]{:S(2)}) async-start(f32[16,8,8,128]{3,2,1,0:T(8,128)} %bitcast.15), calls=%async_computation | async-start | bytes 1048576 | tf_op jit(solution)/shard_map/all_to_all | solution.py:552
  44.2 1.0 copy-start.2
  58.4 1.0 copy-start.3
  61.6 19.1 %collective-permute-start.8 = (f32[3,512,128]{2,1,0:T(8,128)}, f32[3,512,128]{2,1,0:T(8,128)}, u32[]{:S(2)}, u32[]{:S(2)}) collective-permute-start(f32[3,512,128]{2,1,0:T(8,128)} %kv_other_kernel.1.refs_10_), channel_id=1, source_target_pairs={{0,1},{1,0},{2,3},{3,2},{4,5},{5,4},{6,7},{7,6},{8,9},{9,8},{10,11... | collective-permute-start | bytes 2359304 | tf_op jit(solution)/shard_map/ppermute | solution.py:30
  64.0 13.5 %collective-permute-start.7 = (f32[2,512,128]{2,1,0:T(8,128)}, f32[2,512,128]{2,1,0:T(8,128)}, u32[]{:S(2)}, u32[]{:S(2)}) collective-permute-start(f32[2,512,128]{2,1,0:T(8,128)} %get-tuple-element.45), channel_id=1, source_target_pairs={{0,6},{1,7},{2,0},{3,1},{4,2},{5,3},{6,4},{7,5},{8,14},{9,15},{10,... | collective-permute-start | bytes 1572872 | tf_op jit(solution)/shard_map/ppermute | solution.py:26
  65.2 14.4 %collective-permute-start.6 = (f32[2,512,128]{2,1,0:T(8,128)}, f32[2,512,128]{2,1,0:T(8,128)}, u32[]{:S(2)}, u32[]{:S(2)}) collective-permute-start(f32[2,512,128]{2,1,0:T(8,128)} %get-tuple-element.44.refs_9_), channel_id=1, source_target_pairs={{0,2},{1,3},{2,4},{3,5},{4,6},{5,7},{6,0},{7,1},{8,10},{9,11},{10,... | collective-permute-start | bytes 1572872 | tf_op jit(solution)/shard_map/ppermute | solution.py:26
  66.8 1.0 copy-start
  67.8 12.9 %copy-start.1 = (f32[4,512,128]{2,1,0:T(8,128)S(1)}, f32[4,512,128]{2,1,0:T(8,128)}, u32[]{:S(2)}) copy-start(f32[4,512,128]{2,1,0:T(8,128)} %copy-done) | copy-start | bytes 3145732
  67.8 23.4 %collective-permute-start.9 = (f32[4,256,128]{2,1,0:T(8,128)}, f32[4,256,128]{2,1,0:T(8,128)S(1)}, u32[]{:S(2)}, u32[]{:S(2)}) collective-permute-start(f32[4,256,128]{2,1,0:T(8,128)} %get-tuple-element.49), channel_id=1, source_target_pairs={{0,2},{1,3},{2,4},{3,5},{4,6},{5,7},{6,0},{7,1},{8,10},{9,11},{10,... | collective-permute-start | bytes 1572872 | tf_op jit(solution)/shard_map/ppermute | solution.py:26
  67.8 23.4 %collective-permute-start.10 = (f32[4,256,128]{2,1,0:T(8,128)}, f32[4,256,128]{2,1,0:T(8,128)S(1)}, u32[]{:S(2)}, u32[]{:S(2)}) collective-permute-start(f32[4,256,128]{2,1,0:T(8,128)} %get-tuple-element.50), channel_id=1, source_target_pairs={{0,6},{1,7},{2,0},{3,1},{4,2},{5,3},{6,4},{7,5},{8,14},{9,15},{10,... | collective-permute-start | bytes 1572872 | tf_op jit(solution)/shard_map/ppermute | solution.py:26
  77.5 13.1 %copy-start.6 = (f32[5,256,128]{2,1,0:T(8,128)S(1)}, f32[5,256,128]{2,1,0:T(8,128)}, u32[]{:S(2)}) copy-start(f32[5,256,128]{2,1,0:T(8,128)} %get-tuple-element.57) | copy-start | bytes 1966084
  77.5 13.8 %collective-permute-start.11 = (f32[3,256,128]{2,1,0:T(8,128)}, f32[3,256,128]{2,1,0:T(8,128)}, u32[]{:S(2)}, u32[]{:S(2)}) collective-permute-start(f32[3,256,128]{2,1,0:T(8,128)} %get-tuple-element.51), channel_id=1, source_target_pairs={{0,1},{1,0},{2,3},{3,2},{4,5},{5,4},{6,7},{7,6},{8,9},{9,8},{10,11... | collective-permute-start | bytes 1179656 | tf_op jit(solution)/shard_map/ppermute | solution.py:30
  83.3 18.4 %all-to-all-start.1 = ((f32[16,8,8,128]{3,2,1,0:T(8,128)}), f32[16,8,8,128]{3,2,1,0:T(8,128)S(1)}, u32[]{:S(2)}, u32[]{:S(2)}) async-start(f32[16,8,8,128]{3,2,1,0:T(8,128)} %bitcast.9), calls=%async_computation.1 | async-start | bytes 1048576 | tf_op jit(solution)/shard_map/all_to_all | solution.py:552
  90.6 22.3 %collective-permute-start.14 = (f32[5,256,128]{2,1,0:T(8,128)S(1)}, f32[5,256,128]{2,1,0:T(8,128)S(1)}, u32[]{:S(2)}, u32[]{:S(2)}) collective-permute-start(f32[5,256,128]{2,1,0:T(8,128)S(1)} %copy-done.6), channel_id=1, source_target_pairs={{0,1},{1,0},{2,3},{3,2},{4,5},{5,4},{6,7},{7,6},{8,9},{9,8},{10,11... | collective-permute-start | bytes 1966088 | tf_op jit(solution)/shard_map/ppermute | solution.py:30
  91.2 5.2 %copy-start.4 = (f32[128,8,128]{2,1,0:T(8,128)S(1)}, f32[128,8,128]{2,1,0:T(8,128)}, u32[]{:S(2)}) copy-start(f32[128,8,128]{2,1,0:T(8,128)} %kv_kernel.1.refs_7_) | copy-start | bytes 1572868
  93.7 19.2 %collective-permute-start.12 = (f32[3,256,128]{2,1,0:T(8,128)}, f32[3,256,128]{2,1,0:T(8,128)}, u32[]{:S(2)}, u32[]{:S(2)}) collective-permute-start(f32[3,256,128]{2,1,0:T(8,128)} %get-tuple-element.55), channel_id=1, source_target_pairs={{0,2},{1,3},{2,4},{3,5},{4,6},{5,7},{6,0},{7,1},{8,10},{9,11},{10,... | collective-permute-start | bytes 1179656 | tf_op jit(solution)/shard_map/ppermute | solution.py:26
  93.7 19.2 %collective-permute-start.13 = (f32[3,256,128]{2,1,0:T(8,128)}, f32[3,256,128]{2,1,0:T(8,128)}, u32[]{:S(2)}, u32[]{:S(2)}) collective-permute-start(f32[3,256,128]{2,1,0:T(8,128)} %get-tuple-element.56), channel_id=1, source_target_pairs={{0,6},{1,7},{2,0},{3,1},{4,2},{5,3},{6,4},{7,5},{8,14},{9,15},{10,... | collective-permute-start | bytes 1179656 | tf_op jit(solution)/shard_map/ppermute | solution.py:26
  106.5 20.0 %all-to-all-start.2 = ((f32[16,8,8,128]{3,2,1,0:T(8,128)}), f32[16,8,8,128]{3,2,1,0:T(8,128)S(1)}, u32[]{:S(2)}, u32[]{:S(2)}) async-start(f32[16,8,8,128]{3,2,1,0:T(8,128)} %conv_kernel.1), calls=%async_computation.2 | async-start | bytes 1048576 | tf_op jit(solution)/shard_map/all_to_all | solution.py:552
  114.7 7.9 %collective-permute-start.16 = (f32[2,256,128]{2,1,0:T(8,128)S(1)}, f32[2,256,128]{2,1,0:T(8,128)S(1)}, u32[]{:S(2)}, u32[]{:S(2)}) collective-permute-start(f32[2,256,128]{2,1,0:T(8,128)S(1)} %get-tuple-element.61), channel_id=1, source_target_pairs={{0,6},{1,7},{2,0},{3,1},{4,2},{5,3},{6,4},{7,5},{8,14},{9,15},{10,... | collective-permute-start | bytes 786440 | tf_op jit(solution)/shard_map/ppermute | solution.py:26
  114.8 11.6 %collective-permute-start.17 = (f32[2,256,128]{2,1,0:T(8,128)S(1)}, f32[2,256,128]{2,1,0:T(8,128)S(1)}, u32[]{:S(2)}, u32[]{:S(2)}) collective-permute-start(f32[2,256,128]{2,1,0:T(8,128)S(1)} %get-tuple-element.62), channel_id=1, source_target_pairs={{0,1},{1,0},{2,3},{3,2},{4,5},{5,4},{6,7},{7,6},{8,9},{9,8},{10,11... | collective-permute-start | bytes 786440 | tf_op jit(solution)/shard_map/ppermute | solution.py:30
  115.2 11.2 %collective-permute-start.15 = (f32[2,256,128]{2,1,0:T(8,128)S(1)}, f32[2,256,128]{2,1,0:T(8,128)S(1)}, u32[]{:S(2)}, u32[]{:S(2)}) collective-permute-start(f32[2,256,128]{2,1,0:T(8,128)S(1)} %get-tuple-element.60.refs_7_), channel_id=1, source_target_pairs={{0,2},{1,3},{2,4},{3,5},{4,6},{5,7},{6,0},{7,1},{8,10},{9,11},{10,... | collective-permute-start | bytes 786440 | tf_op jit(solution)/shard_map/ppermute | solution.py:26

commit v16 on v14

--- a/solution.py
+++ b/solution.py
@@ -258,7 +258,7 @@
     def z_step(half):
         for owner in range(4):
             piece = 2 * owner + half
-            other = (z_send, piece) if piece < 3 else (z_next, piece - 3)
+            other = (z_send, piece) if piece < 2 else (z_next, piece - 2)
             put(owner, other, (z_mine, piece))
 
     def x_step(half):
@@ -279,17 +279,17 @@
 def query_second_sum_kernel(
     dep_r, dep_l, got_r, got_l, z_got, z_next, z_mine, x_other, out_r, out_l, out_x
 ):
-    out_r[0] = z_mine[2] + z_got[2] + dep_r[2]
-    out_r[1] = z_mine[3] + z_next[0]
-    out_l[0] = z_mine[4] + z_next[1]
-    out_l[1] = z_mine[5] + z_next[2] + dep_l[2]
+    out_r[0] = z_mine[2] + z_next[0] + dep_r[2]
+    out_r[1] = z_mine[3] + z_next[1]
+    out_l[0] = z_mine[4] + z_next[2]
+    out_l[1] = z_mine[5] + z_next[3] + dep_l[2]
     out_x[0] = x_other[0] + (dep_r[0] + got_l[2])
     out_x[1] = x_other[1] + (got_r[2] + dep_l[0])
 
 
 def query_beside_kernel(dep_r, dep_l, got_r, got_l, z_next, z_mine, x_mine, out):
-    out[0] = z_mine[6] + z_next[3]
-    out[1] = z_mine[7] + z_next[4]
+    out[0] = z_mine[6] + z_next[4]
+    out[1] = z_mine[7] + z_next[5]
     out[2] = x_mine[0] + (dep_r[1] + got_l[3])
     out[3] = x_mine[1] + (got_r[3] + dep_l[1])
 
@@ -347,7 +347,7 @@
 
 def project_query(halves, place, activations, weight, after):
     features, columns = weight.shape[1:]
-    shapes = [halves.shape(count) for count in (4, 4, 2, 2, 3, 5, 8, 2, 2)]
+    shapes = [halves.shape(count) for count in (4, 4, 2, 2, 2, 6, 8, 2, 2)]
     return pl.pallas_call(
         query_project_kernel,
         grid_spec=pltpu.PrefetchScalarGridSpec(

time: 126 us -> 139 us (1.10)
  waiting for transfers between devices: 30.5 us -> 41.3 us
  starting transfers between devices: 41.5 us -> 43.3 us
    ppermute x6, waiting for transfers between devices: 8.17 us -> 23.5 us  [swap_z(): return lax.ppermute(value, 'chan', [(i, i ^ 1) for i in range(8)])]
    all_to_all x3, waiting for transfers between devices: 11.8 us -> 6.28 us  [exchange(): return lax.all_to_all(value, 'seq', split_axis=0, concat_axis=0, tiled=True)]
    all_to_all x3, starting transfers between devices: 23.7 us -> 25.9 us  [exchange(): return lax.all_to_all(value, 'seq', split_axis=0, concat_axis=0, tiled=True)]
  transfers between devices with their start and end apart: 21 -> 21, of which waited for: 10 -> 9; matrix products, arithmetic and copies ran while one was open for 0% -> 0% of each run, Pallas kernels for 36% -> 33%
where the time goes in v16:
time: 139 us
  Pallas kernels  52.6 us (38%)
  starting transfers between devices  43.3 us (31%)
  waiting for transfers between devices  41.3 us (30%)
    all_to_all x3, starting transfers between devices, exchange(): return lax.all_to_all(value, 'seq', split_axis=0, concat_axis=0, tiled=True)  25.9 us
    ppermute x6, waiting for transfers between devices, swap_z(): return lax.ppermute(value, 'chan', [(i, i ^ 1) for i in range(8)])  23.5 us
    pallas_call x3, Pallas kernels, project(): pl.pallas_call(body, grid_spec=pltpu.PrefetchScalarGridSpec(num_scalar_pr...  18.3 us
    pallas_call x6, Pallas kernels, call(): pl.pallas_call(body, grid=(1,), in_specs=[pl.BlockSpec(memory_space=pltpu...  13.4 us
    ppermute x12, starting transfers between devices, shift_x(): lax.ppermute(value, 'chan', [(i, (i + 2 * step) % 8) for i in range(8)])  12.6 us
    ppermute x12, waiting for transfers between devices, shift_x(): lax.ppermute(value, 'chan', [(i, (i + 2 * step) % 8) for i in range(8)])  11.6 us
    pallas_call x1, Pallas kernels, project_query(): pl.pallas_call(query_project_kernel, grid_spec=pltpu.PrefetchScalarGridSp...  7.88 us
    pallas_call x4, Pallas kernels, sum_call(): pl.pallas_call(body, grid=(halves.rows // tile,), in_specs=[pl.BlockSpec(...  7.14 us
  transfers between devices with their start and end apart: 21, of which 9 were waited for; matrix products, arithmetic and copies ran while one was open for 0% of the time, Pallas kernels for 33%

profile of v16, /device:TPU:1, one launch (start us, length us, event | category | flops | bytes accessed | tf_op | source)
XLA Modules:
  0.0 138.5 jit_solution(390940560258271630)
XLA Ops:
  0.0 0.1 stack.23.at.place
  0.1 3.8 %first_kernel.1 = (f32[2,512,128]{2,1,0:T(8,128)S(1)}, f32[2,512,128]{2,1,0:T(8,128)S(1)}, f32[2,512,128]{2,1,0:T(8,128)S(1)}, f32[2,512,128]{2,1,0:T(8,128)S(1)}) custom-call(s32[5]{0:T(128)S(1)} %stack.23.at.place, bf16[1024,1024]{1,0:T(8,128)(2,1)} %act.7, bf16[3,1024,1024]{2,1,0:T(8,128)(2,1)} %bitcast.10), custom_call_target="tpu_custom_call" | custom-call | tf_op jit(solution)/shard_map/first_kernel/pallas_call | solution.py:135
  3.9 2.1 %collective-permute-start = (f32[2,512,128]{2,1,0:T(8,128)S(1)}, f32[2,512,128]{2,1,0:T(8,128)S(1)}, u32[]{:S(2)}, u32[]{:S(2)}) collective-permute-start(f32[2,512,128]{2,1,0:T(8,128)S(1)} %get-tuple-element.34), channel_id=1, source_target_pairs={{0,2},{1,3},{2,4},{3,5},{4,6},{5,7},{6,0},{7,1},{8,10},{9,11},{10,... | collective-permute-start | bytes 1572872 | tf_op jit(solution)/shard_map/ppermute | solution.py:26
  6.0 1.4 collective-permute-start.1
  7.4 1.8 %collective-permute-start.2 = (f32[2,512,128]{2,1,0:T(8,128)S(1)}, f32[2,512,128]{2,1,0:T(8,128)S(1)}, u32[]{:S(2)}, u32[]{:S(2)}) collective-permute-start(f32[2,512,128]{2,1,0:T(8,128)S(1)} %get-tuple-element.36), channel_id=1, source_target_pairs={{0,1},{1,0},{2,3},{3,2},{4,5},{5,4},{6,7},{7,6},{8,9},{9,8},{10,11... | collective-permute-start | bytes 1572872 | tf_op jit(solution)/shard_map/ppermute | solution.py:30
  9.2 7.5 %second_kernel.1 = (f32[5,512,128]{2,1,0:T(8,128)S(1)}, f32[5,512,128]{2,1,0:T(8,128)S(1)}, f32[5,512,128]{2,1,0:T(8,128)}) custom-call(s32[5]{0:T(128)S(1)} %stack.23.at.place, bf16[1024,1024]{1,0:T(8,128)(2,1)} %act.7, bf16[3,1024,1024]{2,1,0:T(8,128)(2,1)} %bitcast.11, f32[2,512,128]{2,1,0:T(8,128)S(1)} %get-tuple-element.37.refs_0_.refs_5_), custom_call_target="tpu_custom_call" | custom-call | tf_op jit(solution)/shard_map/second_kernel/pallas_call | solution.py:135
  16.6 0.0 collective-permute-start.3
  16.6 1.9 %collective-permute-done.refs_0_ = f32[2,512,128]{2,1,0:T(8,128)S(1)} collective-permute-done((f32[2,512,128]{2,1,0:T(8,128)S(1)}, f32[2,512,128]{2,1,0:T(8,128)S(1)}, u32[]{:S(2)}, u32[]{:S(2)}) %collective-permute-start) | collective-permute-done | bytes 524320 | tf_op jit(solution)/shard_map/ppermute | solution.py:26
  18.5 0.0 collective-permute-done.1.refs_1_
  18.5 1.6 %collective-permute-done.2.refs_2_ = f32[2,512,128]{2,1,0:T(8,128)S(1)} collective-permute-done((f32[2,512,128]{2,1,0:T(8,128)S(1)}, f32[2,512,128]{2,1,0:T(8,128)S(1)}, u32[]{:S(2)}, u32[]{:S(2)}) %collective-permute-start.2) | collective-permute-done | bytes 524320 | tf_op jit(solution)/shard_map/ppermute | solution.py:30
  20.1 1.7 %kv_first_sum_kernel.1 = (f32[5,512,128]{2,1,0:T(8,128)}, f32[5,512,128]{2,1,0:T(8,128)}) custom-call(f32[2,512,128]{2,1,0:T(8,128)S(1)} %collective-permute-done.refs_0_, f32[2,512,128]{2,1,0:T(8,128)S(1)} %collective-permute-done.1.refs_1_, f32[2,512,128]{2,1,0:T(8,128)S(1)} %collective-permute-done.2.refs_2_, ...), custom_call_target="tpu_custom_call" | custom-call | tf_op jit(solution)/shard_map/kv_first_sum_kernel/pallas_call | solution.py:162
  21.9 1.2 collective-permute-start.5
  23.0 0.3 collective-permute-start.4
  23.3 1.2 taps_turn_kernel.1
  24.5 11.8 %all-to-all-start = ((f32[16,8,8,128]{3,2,1,0:T(8,128)}), f32[16,8,8,128]{3,2,1,0:T(8,128)}, u32[]{:S(2)}, u32[]{:S(2)}) async-start(f32[16,8,8,128]{3,2,1,0:T(8,128)} %bitcast.15), calls=%async_computation | async-start | bytes 1048576 | tf_op jit(solution)/shard_map/all_to_all | solution.py:552
  36.3 7.9 %query_project_kernel.1 = (f32[4,256,128]{2,1,0:T(8,128)}, f32[4,256,128]{2,1,0:T(8,128)}, f32[2,256,128]{2,1,0:T(8,128)}, f32[2,256,128]{2,1,0:T(8,128)}, f32[2...) custom-call(s32[5]{0:T(128)S(1)} %stack.23.at.place, ...), custom_call_target="tpu_custom_call" | custom-call | tf_op jit(solution)/shard_map/query_project_kernel/pallas_call | solution.py:351
  44.2 1.0 copy-done.3
  45.2 6.9 %third_kernel.1.refs_0_.refs_1_.refs_6_.refs_2_.refs_3_.refs_4_ = f32[11,512,128]{2,1,0:T(8,128)S(1)} custom-call(s32[5]{0:T(128)S(1)} %stack.23.at.place, bf16[1024,1024]{1,0:T(8,128)(2,1)} %act.7, bf16[3,1024,1024]{2,1,0:T(8,128)(2,1)} %bitcast.13, f32[5,512,128]{2,1,0:T(8,128)} %get-tuple-element.40.refs_0_.refs_1_, f32[4,256,128]{2,1,0:T(8,128)S(1)} %copy-done.3), custom_call_target="tpu_custom_call" | custom-call | tf_op jit(solution)/shard_map/third_kernel/pallas_call | solution.py:135
  52.2 6.3 %all-to-all-done.refs_8_.refs_0_ = f32[16,8,8,128]{3,2,1,0:T(8,128)} async-done(((f32[16,8,8,128]{3,2,1,0:T(8,128)}), f32[16,8,8,128]{3,2,1,0:T(8,128)}, u32[]{:S(2)}, u32[]{:S(2)}) %all-to-all-start) | async-done | bytes 524320 | tf_op jit(solution)/shard_map/all_to_all | solution.py:552
  58.5 2.2 %kv_other_kernel.1.refs_10_ = f32[3,512,128]{2,1,0:T(8,128)} custom-call(f32[11,512,128]{2,1,0:T(8,128)S(1)} %third_kernel.1.refs_0_.refs_1_.refs_6_.refs_2_.refs_3_.refs_4_, f32[11,512,128]{2,1,0:T(8,128)S(1)} %third_kernel.1.refs_0_.refs_1_.refs_6_.refs_2_.refs_3_.refs_4_, f32[5,512,128]{2,1,0:T(8,128)} %collective-permute-done.4.refs_2_.refs_3_.refs_8_.refs_5_.refs_6_, ...), custom_call_target="tpu_custom_call" | custom-call | tf_op jit(solution)/shard_map/kv_other_kernel/pallas_call | solution.py:200
  60.7 2.4 %kv_last_kernel.1 = (f32[2,512,128]{2,1,0:T(8,128)}, f32[2,512,128]{2,1,0:T(8,128)}) custom-call(f32[11,512,128]{2,1,0:T(8,128)S(1)} %third_kernel.1.refs_0_.refs_1_.refs_6_.refs_2_.refs_3_.refs_4_, f32[11,512,128]{2,1,0:T(8,128)S(1)} %third_kernel.1.refs_0_.refs_1_.refs_6_.refs_2_.refs_3_.refs_4_, ...), custom_call_target="tpu_custom_call" | custom-call | tf_op jit(solution)/shard_map/kv_last_kernel/pallas_call | solution.py:200
  63.1 1.3 collective-permute-start.7
  64.3 0.2 collective-permute-start.6
  64.5 1.4 %kv_beside_kernel.1.refs_7_.refs_0_ = f32[4,512,128]{2,1,0:T(8,128)S(1)} custom-call(f32[11,512,128]{2,1,0:T(8,128)S(1)} %third_kernel.1.refs_0_.refs_1_.refs_6_.refs_2_.refs_3_.refs_4_, f32[11,512,128]{2,1,0:T(8,128)S(1)} %third_kernel.1.refs_0_.refs_1_.refs_6_.refs_2_.refs_3_.refs_4_, ...), custom_call_target="tpu_custom_call" | custom-call | tf_op jit(solution)/shard_map/kv_beside_kernel/pallas_call | solution.py:200
  65.9 3.6 %taps_kernel.1.refs_4_.refs_1_ = f32[1024,256]{1,0:T(8,128)} custom-call(f32[16,8,8,128]{3,2,1,0:T(8,128)} %all-to-all-done.refs_8_.refs_0_, bf16[256,128]{1,0:T(8,128)(2,1)} %constant.72.clone.refs_1_.refs_2_, bf16[256,128]{1,0:T(8,128)(2,1)} %constant.73.clone.refs_2_.refs_3_, f32[128,128]{1,0:T(8,128)} %constant.74.clone.refs_3_.refs_4_, ...), custom_call_target="tpu_custom_call" | custom-call | tf_op jit(solution)/shard_map/taps_kernel/pallas_call | solution.py:535
  69.6 0.3 collective-permute-start.9
  69.8 2.7 %collective-permute-start.10 = (f32[4,256,128]{2,1,0:T(8,128)}, f32[4,256,128]{2,1,0:T(8,128)S(1)}, u32[]{:S(2)}, u32[]{:S(2)}) collective-permute-start(f32[4,256,128]{2,1,0:T(8,128)} %get-tuple-element.50), channel_id=1, source_target_pairs={{0,6},{1,7},{2,0},{3,1},{4,2},{5,3},{6,4},{7,5},{8,14},{9,15},{10,... | collective-permute-start | bytes 1572872 | tf_op jit(solution)/shard_map/ppermute | solution.py:26
  72.5 4.0 %collective-permute-done.7.refs_2_ = f32[2,512,128]{2,1,0:T(8,128)} collective-permute-done((f32[2,512,128]{2,1,0:T(8,128)}, f32[2,512,128]{2,1,0:T(8,128)}, u32[]{:S(2)}, u32[]{:S(2)}) %collective-permute-start.7) | collective-permute-done | bytes 524320 | tf_op jit(solution)/shard_map/ppermute | solution.py:26
  76.5 1.1 collective-permute-start.14
  77.7 1.0 collective-permute-done.6.refs_1_
  78.7 1.1 collective-permute-done.8.refs_3_
  79.8 2.6 %kv_kernel.1 = f32[128,8,128]{2,1,0:T(8,128)} custom-call(f32[4,512,128]{2,1,0:T(8,128)S(1)} %copy-done.2, f32[2,512,128]{2,1,0:T(8,128)} %collective-permute-done.6.refs_1_, f32[2,512,128]{2,1,0:T(8,128)} %collective-permute-done.7.refs_2_, f32[3,512,128]{2,1,0:T(8,128)} %collective-permute-done.8.refs_3_, f32[1024,256]{1,0:T(8,128)S(1)} %copy-done), custom_call_target="tpu_custom_call" | custom-call | tf_op jit(solution)/shard_map/kv_kernel/pallas_call | solution.py:535
  82.4 7.1 %all-to-all-start.1 = ((f32[16,8,8,128]{3,2,1,0:T(8,128)}), f32[16,8,8,128]{3,2,1,0:T(8,128)S(1)}, u32[]{:S(2)}, u32[]{:S(2)}) async-start(f32[16,8,8,128]{3,2,1,0:T(8,128)} %bitcast.14), calls=%async_computation.1 | async-start | bytes 1048576 | tf_op jit(solution)/shard_map/all_to_all | solution.py:552
  89.6 0.7 collective-permute-start.11
  90.3 16.7 %collective-permute-done.11.refs_2_.refs_4_ = f32[2,256,128]{2,1,0:T(8,128)S(1)} collective-permute-done((f32[2,256,128]{2,1,0:T(8,128)S(1)}, f32[2,256,128]{2,1,0:T(8,128)S(1)}, u32[]{:S(2)}, u32[]{:S(2)}) %collective-permute-start.11) | collective-permute-done | bytes 262176 | tf_op jit(solution)/shard_map/ppermute | solution.py:30
  107.0 2.2 %first_sum_kernel.1 = (f32[3,256,128]{2,1,0:T(8,128)}, f32[3,256,128]{2,1,0:T(8,128)S(1)}) custom-call(f32[4,256,128]{2,1,0:T(8,128)S(1)} %collective-permute-done.9.refs_0_.refs_2_, f32[4,256,128]{2,1,0:T(8,128)S(1)} %collective-permute-done.10.refs_1_.refs_3_, f32[2,256,128]{2,1,0:T(8,128)S(1)} %collective-permute-done.11.refs_2_.refs_4_, ...), custom_call_target="tpu_custom_call" | custom-call | tf_op jit(solution)/shard_map/first_sum_kernel/pallas_call | solution.py:162
  109.3 2.7 %collective-permute-start.13 = (f32[3,256,128]{2,1,0:T(8,128)S(1)}, f32[3,256,128]{2,1,0:T(8,128)S(1)}, u32[]{:S(2)}, u32[]{:S(2)}) collective-permute-start(f32[3,256,128]{2,1,0:T(8,128)S(1)} %get-tuple-element.56), channel_id=1, source_target_pairs={{0,6},{1,7},{2,0},{3,1},{4,2},{5,3},{6,4},{7,5},{8,14},{9,15},{10,... | collective-permute-start | bytes 1179656 | tf_op jit(solution)/shard_map/ppermute | solution.py:26
  111.9 4.7 %conv_kernel.1 = f32[16,8,8,128]{3,2,1,0:T(8,128)} custom-call(f32[16,8,8,128]{3,2,1,0:T(8,128)S(1)} %all-to-all-done.1.refs_0_, f32[1024,256]{1,0:T(8,128)} %taps_kernel.1.refs_4_.refs_1_, bf16[256,128]{1,0:T(8,128)(2,1)} %constant.72.clone.refs_1_.refs_2_, bf16[256,128]{1,0:T(8,128)(2,1)} %constant.73.clone.refs_2_.refs_3_, ...), custom_call_target="tpu_custom_call" | custom-call | tf_op jit(solution)/shard_map/conv_kernel/pallas_call | solution.py:535
  116.7 7.0 %all-to-all-start.2 = ((f32[16,8,8,128]{3,2,1,0:T(8,128)}), f32[16,8,8,128]{3,2,1,0:T(8,128)S(1)}, u32[]{:S(2)}, u32[]{:S(2)}) async-start(f32[16,8,8,128]{3,2,1,0:T(8,128)} %conv_kernel.1), calls=%async_computation.2 | async-start | bytes 1048576 | tf_op jit(solution)/shard_map/all_to_all | solution.py:552
  123.7 1.6 %query_second_sum_kernel.1 = (f32[2,256,128]{2,1,0:T(8,128)S(1)}, f32[2,256,128]{2,1,0:T(8,128)S(1)}, f32[2,256,128]{2,1,0:T(8,128)S(1)}) custom-call(f32[3,256,128]{2,1,0:T(8,128)S(1)} %collective-permute-done.12.refs_0_, f32[3,256,128]{2,1,0:T(8,128)S(1)} %collective-permute-done.13.refs_1_, f32[4,256,128]{2,1,0:T(8,128)S(1)} %collective-permute-done.9.refs_0_.refs_2_, ...), custom_call_target="tpu_custom_call" | custom-call | tf_op jit(solution)/shard_map/query_second_sum_kernel/pallas_call | solution.py:162
  125.3 0.4 collective-permute-start.16
  125.6 1.2 collective-permute-start.17
  126.8 0.2 collective-permute-start.15
  127.0 1.6 %query_beside_kernel.1.refs_0_ = f32[4,256,128]{2,1,0:T(8,128)S(1)} custom-call(f32[3,256,128]{2,1,0:T(8,128)S(1)} %collective-permute-done.12.refs_0_, f32[3,256,128]{2,1,0:T(8,128)S(1)} %collective-permute-done.13.refs_1_, f32[4,256,128]{2,1,0:T(8,128)S(1)} %collective-permute-done.9.refs_0_.refs_2_, ...), custom_call_target="tpu_custom_call" | custom-call | tf_op jit(solution)/shard_map/query_beside_kernel/pallas_call | solution.py:162
  128.6 4.6 %collective-permute-done.16.refs_2_ = f32[2,256,128]{2,1,0:T(8,128)S(1)} collective-permute-done((f32[2,256,128]{2,1,0:T(8,128)S(1)}, f32[2,256,128]{2,1,0:T(8,128)S(1)}, u32[]{:S(2)}, u32[]{:S(2)}) %collective-permute-start.16) | collective-permute-done | bytes 262176 | tf_op jit(solution)/shard_map/ppermute | solution.py:26
  133.2 4.1 %collective-permute-done.17.refs_3_ = f32[2,256,128]{2,1,0:T(8,128)S(1)} collective-permute-done((f32[2,256,128]{2,1,0:T(8,128)S(1)}, f32[2,256,128]{2,1,0:T(8,128)S(1)}, u32[]{:S(2)}, u32[]{:S(2)}) %collective-permute-start.17) | collective-permute-done | bytes 262176 | tf_op jit(solution)/shard_map/ppermute | solution.py:30
  137.3 0.1 query_kernel.1.refs_1_
  137.4 1.1 gate_kernel.1
  (27 shorter events, 0.1 us)
Async XLA Ops:
  3.9 14.6 %collective-permute-start = (f32[2,512,128]{2,1,0:T(8,128)S(1)}, f32[2,512,128]{2,1,0:T(8,128)S(1)}, u32[]{:S(2)}, u32[]{:S(2)}) collective-permute-start(f32[2,512,128]{2,1,0:T(8,128)S(1)} %get-tuple-element.34), channel_id=1, source_target_pairs={{0,2},{1,3},{2,4},{3,5},{4,6},{5,7},{6,0},{7,1},{8,10},{9,11},{10,... | collective-permute-start | bytes 1572872 | tf_op jit(solution)/shard_map/ppermute | solution.py:26
  6.0 12.5 %collective-permute-start.1 = (f32[2,512,128]{2,1,0:T(8,128)S(1)}, f32[2,512,128]{2,1,0:T(8,128)S(1)}, u32[]{:S(2)}, u32[]{:S(2)}) collective-permute-start(f32[2,512,128]{2,1,0:T(8,128)S(1)} %get-tuple-element.35), channel_id=1, source_target_pairs={{0,6},{1,7},{2,0},{3,1},{4,2},{5,3},{6,4},{7,5},{8,14},{9,15},{10,... | collective-permute-start | bytes 1572872 | tf_op jit(solution)/shard_map/ppermute | solution.py:26
  7.4 12.7 %collective-permute-start.2 = (f32[2,512,128]{2,1,0:T(8,128)S(1)}, f32[2,512,128]{2,1,0:T(8,128)S(1)}, u32[]{:S(2)}, u32[]{:S(2)}) collective-permute-start(f32[2,512,128]{2,1,0:T(8,128)S(1)} %get-tuple-element.36), channel_id=1, source_target_pairs={{0,1},{1,0},{2,3},{3,2},{4,5},{5,4},{6,7},{7,6},{8,9},{9,8},{10,11... | collective-permute-start | bytes 1572872 | tf_op jit(solution)/shard_map/ppermute | solution.py:30
  16.6 41.8 %collective-permute-start.3 = (f32[5,512,128]{2,1,0:T(8,128)}, f32[5,512,128]{2,1,0:T(8,128)}, u32[]{:S(2)}, u32[]{:S(2)}) collective-permute-start(f32[5,512,128]{2,1,0:T(8,128)} %get-tuple-element.42), channel_id=1, source_target_pairs={{0,1},{1,0},{2,3},{3,2},{4,5},{5,4},{6,7},{7,6},{8,9},{9,8},{10,11... | collective-permute-start | bytes 3932168 | tf_op jit(solution)/shard_map/ppermute | solution.py:30
  20.1 3.2 %copy-start.5 = (f32[1024,128]{1,0:T(8,128)S(1)}, f32[1024,128]{1,0:T(8,128)}, u32[]{:S(2)}) copy-start(f32[1024,128]{1,0:T(8,128)} %refs_0_.1) | copy-start | bytes 1572868
  21.9 36.6 %collective-permute-start.5 = (f32[5,512,128]{2,1,0:T(8,128)}, f32[5,512,128]{2,1,0:T(8,128)}, u32[]{:S(2)}, u32[]{:S(2)}) collective-permute-start(f32[5,512,128]{2,1,0:T(8,128)} %get-tuple-element.43), channel_id=1, source_target_pairs={{0,6},{1,7},{2,0},{3,1},{4,2},{5,3},{6,4},{7,5},{8,14},{9,15},{10,... | collective-permute-start | bytes 3932168 | tf_op jit(solution)/shard_map/ppermute | solution.py:26
  23.0 35.4 %collective-permute-start.4 = (f32[5,512,128]{2,1,0:T(8,128)}, f32[5,512,128]{2,1,0:T(8,128)}, u32[]{:S(2)}, u32[]{:S(2)}) collective-permute-start(f32[5,512,128]{2,1,0:T(8,128)} %get-tuple-element.40.refs_0_.refs_1_), channel_id=1, source_target_pairs={{0,2},{1,3},{2,4},{3,5},{4,6},{5,7},{6,0},{7,1},{8,10},{9,11},{10,... | collective-permute-start | bytes 3932168 | tf_op jit(solution)/shard_map/ppermute | solution.py:26
  24.5 34.0 %all-to-all-start = ((f32[16,8,8,128]{3,2,1,0:T(8,128)}), f32[16,8,8,128]{3,2,1,0:T(8,128)}, u32[]{:S(2)}, u32[]{:S(2)}) async-start(f32[16,8,8,128]{3,2,1,0:T(8,128)} %bitcast.15), calls=%async_computation | async-start | bytes 1048576 | tf_op jit(solution)/shard_map/all_to_all | solution.py:552
  44.2 1.0 copy-start.3
  45.2 13.2 %copy-start.4 = (f32[4,256,128]{2,1,0:T(8,128)S(1)}, f32[4,256,128]{2,1,0:T(8,128)}, u32[]{:S(2)}) copy-start(f32[4,256,128]{2,1,0:T(8,128)} %get-tuple-element.41.refs_1_.refs_9_.refs_0_) | copy-start | bytes 1572868
  60.7 19.1 %collective-permute-start.8 = (f32[3,512,128]{2,1,0:T(8,128)}, f32[3,512,128]{2,1,0:T(8,128)}, u32[]{:S(2)}, u32[]{:S(2)}) collective-permute-start(f32[3,512,128]{2,1,0:T(8,128)} %kv_other_kernel.1.refs_10_), channel_id=1, source_target_pairs={{0,1},{1,0},{2,3},{3,2},{4,5},{5,4},{6,7},{7,6},{8,9},{9,8},{10,11... | collective-permute-start | bytes 2359304 | tf_op jit(solution)/shard_map/ppermute | solution.py:30
  63.1 13.5 %collective-permute-start.7 = (f32[2,512,128]{2,1,0:T(8,128)}, f32[2,512,128]{2,1,0:T(8,128)}, u32[]{:S(2)}, u32[]{:S(2)}) collective-permute-start(f32[2,512,128]{2,1,0:T(8,128)} %get-tuple-element.45), channel_id=1, source_target_pairs={{0,6},{1,7},{2,0},{3,1},{4,2},{5,3},{6,4},{7,5},{8,14},{9,15},{10,... | collective-permute-start | bytes 1572872 | tf_op jit(solution)/shard_map/ppermute | solution.py:26
  64.3 14.4 %collective-permute-start.6 = (f32[2,512,128]{2,1,0:T(8,128)}, f32[2,512,128]{2,1,0:T(8,128)}, u32[]{:S(2)}, u32[]{:S(2)}) collective-permute-start(f32[2,512,128]{2,1,0:T(8,128)} %get-tuple-element.44.refs_9_), channel_id=1, source_target_pairs={{0,2},{1,3},{2,4},{3,5},{4,6},{5,7},{6,0},{7,1},{8,10},{9,11},{10,... | collective-permute-start | bytes 1572872 | tf_op jit(solution)/shard_map/ppermute | solution.py:26
  65.9 3.7 %copy-start.1 = (f32[4,512,128]{2,1,0:T(8,128)}, f32[4,512,128]{2,1,0:T(8,128)S(1)}, u32[]{:S(2)}) copy-start(f32[4,512,128]{2,1,0:T(8,128)S(1)} %kv_beside_kernel.1.refs_7_.refs_0_) | copy-start | bytes 3145732
  69.6 10.2 %copy-start = (f32[1024,256]{1,0:T(8,128)S(1)}, f32[1024,256]{1,0:T(8,128)}, u32[]{:S(2)}) copy-start(f32[1024,256]{1,0:T(8,128)} %taps_kernel.1.refs_4_.refs_1_) | copy-start | bytes 3145732
  69.6 10.2 %copy-start.2 = (f32[4,512,128]{2,1,0:T(8,128)S(1)}, f32[4,512,128]{2,1,0:T(8,128)}, u32[]{:S(2)}) copy-start(f32[4,512,128]{2,1,0:T(8,128)} %copy-done.1) | copy-start | bytes 3145732
  69.6 37.4 %collective-permute-start.9 = (f32[4,256,128]{2,1,0:T(8,128)}, f32[4,256,128]{2,1,0:T(8,128)S(1)}, u32[]{:S(2)}, u32[]{:S(2)}) collective-permute-start(f32[4,256,128]{2,1,0:T(8,128)} %get-tuple-element.49), channel_id=1, source_target_pairs={{0,2},{1,3},{2,4},{3,5},{4,6},{5,7},{6,0},{7,1},{8,10},{9,11},{10,... | collective-permute-start | bytes 1572872 | tf_op jit(solution)/shard_map/ppermute | solution.py:26
  69.8 37.2 %collective-permute-start.10 = (f32[4,256,128]{2,1,0:T(8,128)}, f32[4,256,128]{2,1,0:T(8,128)S(1)}, u32[]{:S(2)}, u32[]{:S(2)}) collective-permute-start(f32[4,256,128]{2,1,0:T(8,128)} %get-tuple-element.50), channel_id=1, source_target_pairs={{0,6},{1,7},{2,0},{3,1},{4,2},{5,3},{6,4},{7,5},{8,14},{9,15},{10,... | collective-permute-start | bytes 1572872 | tf_op jit(solution)/shard_map/ppermute | solution.py:26
  76.5 13.0 %copy-start.6 = (f32[2,256,128]{2,1,0:T(8,128)S(1)}, f32[2,256,128]{2,1,0:T(8,128)}, u32[]{:S(2)}) copy-start(f32[2,256,128]{2,1,0:T(8,128)} %get-tuple-element.51) | copy-start | bytes 786436
  76.5 47.1 %collective-permute-start.14 = (f32[6,256,128]{2,1,0:T(8,128)}, f32[6,256,128]{2,1,0:T(8,128)}, u32[]{:S(2)}, u32[]{:S(2)}) collective-permute-start(f32[6,256,128]{2,1,0:T(8,128)} %get-tuple-element.57), channel_id=1, source_target_pairs={{0,1},{1,0},{2,3},{3,2},{4,5},{5,4},{6,7},{7,6},{8,9},{9,8},{10,11... | collective-permute-start | bytes 2359304 | tf_op jit(solution)/shard_map/ppermute | solution.py:30
  82.4 29.5 %all-to-all-start.1 = ((f32[16,8,8,128]{3,2,1,0:T(8,128)}), f32[16,8,8,128]{3,2,1,0:T(8,128)S(1)}, u32[]{:S(2)}, u32[]{:S(2)}) async-start(f32[16,8,8,128]{3,2,1,0:T(8,128)} %bitcast.14), calls=%async_computation.1 | async-start | bytes 1048576 | tf_op jit(solution)/shard_map/all_to_all | solution.py:552
  89.6 17.4 %collective-permute-start.11 = (f32[2,256,128]{2,1,0:T(8,128)S(1)}, f32[2,256,128]{2,1,0:T(8,128)S(1)}, u32[]{:S(2)}, u32[]{:S(2)}) collective-permute-start(f32[2,256,128]{2,1,0:T(8,128)S(1)} %copy-done.6), channel_id=1, source_target_pairs={{0,1},{1,0},{2,3},{3,2},{4,5},{5,4},{6,7},{7,6},{8,9},{9,8},{10,11... | collective-permute-start | bytes 786440 | tf_op jit(solution)/shard_map/ppermute | solution.py:30
  109.3 14.4 %collective-permute-start.12 = (f32[3,256,128]{2,1,0:T(8,128)}, f32[3,256,128]{2,1,0:T(8,128)S(1)}, u32[]{:S(2)}, u32[]{:S(2)}) collective-permute-start(f32[3,256,128]{2,1,0:T(8,128)} %get-tuple-element.55), channel_id=1, source_target_pairs={{0,2},{1,3},{2,4},{3,5},{4,6},{5,7},{6,0},{7,1},{8,10},{9,11},{10,... | collective-permute-start | bytes 1179656 | tf_op jit(solution)/shard_map/ppermute | solution.py:26
  109.3 14.4 %collective-permute-start.13 = (f32[3,256,128]{2,1,0:T(8,128)S(1)}, f32[3,256,128]{2,1,0:T(8,128)S(1)}, u32[]{:S(2)}, u32[]{:S(2)}) collective-permute-start(f32[3,256,128]{2,1,0:T(8,128)S(1)} %get-tuple-element.56), channel_id=1, source_target_pairs={{0,6},{1,7},{2,0},{3,1},{4,2},{5,3},{6,4},{7,5},{8,14},{9,15},{10,... | collective-permute-start | bytes 1179656 | tf_op jit(solution)/shard_map/ppermute | solution.py:26
  116.7 20.7 %all-to-all-start.2 = ((f32[16,8,8,128]{3,2,1,0:T(8,128)}), f32[16,8,8,128]{3,2,1,0:T(8,128)S(1)}, u32[]{:S(2)}, u32[]{:S(2)}) async-start(f32[16,8,8,128]{3,2,1,0:T(8,128)} %conv_kernel.1), calls=%async_computation.2 | async-start | bytes 1048576 | tf_op jit(solution)/shard_map/all_to_all | solution.py:552
  125.3 7.9 %collective-permute-start.16 = (f32[2,256,128]{2,1,0:T(8,128)S(1)}, f32[2,256,128]{2,1,0:T(8,128)S(1)}, u32[]{:S(2)}, u32[]{:S(2)}) collective-permute-start(f32[2,256,128]{2,1,0:T(8,128)S(1)} %get-tuple-element.61), channel_id=1, source_target_pairs={{0,6},{1,7},{2,0},{3,1},{4,2},{5,3},{6,4},{7,5},{8,14},{9,15},{10,... | collective-permute-start | bytes 786440 | tf_op jit(solution)/shard_map/ppermute | solution.py:26
  125.6 11.6 %collective-permute-start.17 = (f32[2,256,128]{2,1,0:T(8,128)S(1)}, f32[2,256,128]{2,1,0:T(8,128)S(1)}, u32[]{:S(2)}, u32[]{:S(2)}) collective-permute-start(f32[2,256,128]{2,1,0:T(8,128)S(1)} %get-tuple-element.62), channel_id=1, source_target_pairs={{0,1},{1,0},{2,3},{3,2},{4,5},{5,4},{6,7},{7,6},{8,9},{9,8},{10,11... | collective-permute-start | bytes 786440 | tf_op jit(solution)/shard_map/ppermute | solution.py:30
  126.8 10.5 %collective-permute-start.15 = (f32[2,256,128]{2,1,0:T(8,128)S(1)}, f32[2,256,128]{2,1,0:T(8,128)S(1)}, u32[]{:S(2)}, u32[]{:S(2)}) collective-permute-start(f32[2,256,128]{2,1,0:T(8,128)S(1)} %get-tuple-element.60.refs_7_), channel_id=1, source_target_pairs={{0,2},{1,3},{2,4},{3,5},{4,6},{5,7},{6,0},{7,1},{8,10},{9,11},{10,... | collective-permute-start | bytes 786440 | tf_op jit(solution)/shard_map/ppermute | solution.py:26

commit v17 on v14

--- a/solution.py
+++ b/solution.py
@@ -258,7 +258,7 @@
     def z_step(half):
         for owner in range(4):
             piece = 2 * owner + half
-            other = (z_send, piece) if piece < 3 else (z_next, piece - 3)
+            other = (z_send, piece) if piece < 4 else (z_next, piece - 4)
             put(owner, other, (z_mine, piece))
 
     def x_step(half):
@@ -280,16 +280,16 @@
     dep_r, dep_l, got_r, got_l, z_got, z_next, z_mine, x_other, out_r, out_l, out_x
 ):
     out_r[0] = z_mine[2] + z_got[2] + dep_r[2]
-    out_r[1] = z_mine[3] + z_next[0]
-    out_l[0] = z_mine[4] + z_next[1]
-    out_l[1] = z_mine[5] + z_next[2] + dep_l[2]
+    out_r[1] = z_mine[3] + z_got[3]
+    out_l[0] = z_mine[4] + z_next[0]
+    out_l[1] = z_mine[5] + z_next[1] + dep_l[2]
     out_x[0] = x_other[0] + (dep_r[0] + got_l[2])
     out_x[1] = x_other[1] + (got_r[2] + dep_l[0])
 
 
 def query_beside_kernel(dep_r, dep_l, got_r, got_l, z_next, z_mine, x_mine, out):
-    out[0] = z_mine[6] + z_next[3]
-    out[1] = z_mine[7] + z_next[4]
+    out[0] = z_mine[6] + z_next[2]
+    out[1] = z_mine[7] + z_next[3]
     out[2] = x_mine[0] + (dep_r[1] + got_l[3])
     out[3] = x_mine[1] + (got_r[3] + dep_l[1])
 
@@ -347,7 +347,7 @@
 
 def project_query(halves, place, activations, weight, after):
     features, columns = weight.shape[1:]
-    shapes = [halves.shape(count) for count in (4, 4, 2, 2, 3, 5, 8, 2, 2)]
+    shapes = [halves.shape(count) for count in (4, 4, 2, 2, 4, 4, 8, 2, 2)]
     return pl.pallas_call(
         query_project_kernel,
         grid_spec=pltpu.PrefetchScalarGridSpec(

time: 126 us -> 128 us (1.016)
  starting transfers between devices: 41.5 us -> 43.1 us
where the time goes in v17:
time: 128 us; the launch traced here: 127 us
  Pallas kernels  52.6 us (41%)
  starting transfers between devices  43.1 us (34%)
  waiting for transfers between devices  30.4 us (24%)
    all_to_all x3, starting transfers between devices, exchange(): return lax.all_to_all(value, 'seq', split_axis=0, concat_axis=0, tiled=True)  24.7 us
    pallas_call x3, Pallas kernels, project(): pl.pallas_call(body, grid_spec=pltpu.PrefetchScalarGridSpec(num_scalar_pr...  18.3 us
    ppermute x12, starting transfers between devices, shift_x(): lax.ppermute(value, 'chan', [(i, (i + 2 * step) % 8) for i in range(8)])  13.8 us
    pallas_call x6, Pallas kernels, call(): pl.pallas_call(body, grid=(1,), in_specs=[pl.BlockSpec(memory_space=pltpu...  13.4 us
    all_to_all x3, waiting for transfers between devices, exchange(): return lax.all_to_all(value, 'seq', split_axis=0, concat_axis=0, tiled=True)  11.6 us
    ppermute x12, waiting for transfers between devices, shift_x(): lax.ppermute(value, 'chan', [(i, (i + 2 * step) % 8) for i in range(8)])  10.6 us
    ppermute x6, waiting for transfers between devices, swap_z(): return lax.ppermute(value, 'chan', [(i, i ^ 1) for i in range(8)])  8.22 us
    pallas_call x1, Pallas kernels, project_query(): pl.pallas_call(query_project_kernel, grid_spec=pltpu.PrefetchScalarGridSp...  7.86 us
  transfers between devices with their start and end apart: 21, of which 10 were waited for; matrix products, arithmetic and copies ran while one was open for 0% of the time, Pallas kernels for 36%

profile of v17, /device:TPU:1, one launch (start us, length us, event | category | flops | bytes accessed | tf_op | source)
XLA Modules:
  0.0 127.4 jit_solution(18045363518167954755)
XLA Ops:
  0.0 0.1 stack.23.at.place
  0.1 3.8 %first_kernel.1 = (f32[2,512,128]{2,1,0:T(8,128)S(1)}, f32[2,512,128]{2,1,0:T(8,128)S(1)}, f32[2,512,128]{2,1,0:T(8,128)S(1)}, f32[2,512,128]{2,1,0:T(8,128)S(1)}) custom-call(s32[5]{0:T(128)S(1)} %stack.23.at.place, bf16[1024,1024]{1,0:T(8,128)(2,1)} %act.7, bf16[3,1024,1024]{2,1,0:T(8,128)(2,1)} %bitcast.10), custom_call_target="tpu_custom_call" | custom-call | tf_op jit(solution)/shard_map/first_kernel/pallas_call | solution.py:135
  3.9 2.1 %collective-permute-start = (f32[2,512,128]{2,1,0:T(8,128)S(1)}, f32[2,512,128]{2,1,0:T(8,128)S(1)}, u32[]{:S(2)}, u32[]{:S(2)}) collective-permute-start(f32[2,512,128]{2,1,0:T(8,128)S(1)} %get-tuple-element.34), channel_id=1, source_target_pairs={{0,2},{1,3},{2,4},{3,5},{4,6},{5,7},{6,0},{7,1},{8,10},{9,11},{10,... | collective-permute-start | bytes 1572872 | tf_op jit(solution)/shard_map/ppermute | solution.py:26
  6.0 1.4 %collective-permute-start.1 = (f32[2,512,128]{2,1,0:T(8,128)S(1)}, f32[2,512,128]{2,1,0:T(8,128)S(1)}, u32[]{:S(2)}, u32[]{:S(2)}) collective-permute-start(f32[2,512,128]{2,1,0:T(8,128)S(1)} %get-tuple-element.35), channel_id=1, source_target_pairs={{0,6},{1,7},{2,0},{3,1},{4,2},{5,3},{6,4},{7,5},{8,14},{9,15},{10,... | collective-permute-start | bytes 1572872 | tf_op jit(solution)/shard_map/ppermute | solution.py:26
  7.4 1.8 %collective-permute-start.2 = (f32[2,512,128]{2,1,0:T(8,128)S(1)}, f32[2,512,128]{2,1,0:T(8,128)S(1)}, u32[]{:S(2)}, u32[]{:S(2)}) collective-permute-start(f32[2,512,128]{2,1,0:T(8,128)S(1)} %get-tuple-element.36), channel_id=1, source_target_pairs={{0,1},{1,0},{2,3},{3,2},{4,5},{5,4},{6,7},{7,6},{8,9},{9,8},{10,11... | collective-permute-start | bytes 1572872 | tf_op jit(solution)/shard_map/ppermute | solution.py:30
  9.2 7.5 %second_kernel.1 = (f32[5,512,128]{2,1,0:T(8,128)S(1)}, f32[5,512,128]{2,1,0:T(8,128)S(1)}, f32[5,512,128]{2,1,0:T(8,128)}) custom-call(s32[5]{0:T(128)S(1)} %stack.23.at.place, bf16[1024,1024]{1,0:T(8,128)(2,1)} %act.7, bf16[3,1024,1024]{2,1,0:T(8,128)(2,1)} %bitcast.11, f32[2,512,128]{2,1,0:T(8,128)S(1)} %get-tuple-element.37.refs_0_.refs_5_), custom_call_target="tpu_custom_call" | custom-call | tf_op jit(solution)/shard_map/second_kernel/pallas_call | solution.py:135
  16.6 0.0 collective-permute-start.3
  16.7 1.9 %collective-permute-done.refs_0_ = f32[2,512,128]{2,1,0:T(8,128)S(1)} collective-permute-done((f32[2,512,128]{2,1,0:T(8,128)S(1)}, f32[2,512,128]{2,1,0:T(8,128)S(1)}, u32[]{:S(2)}, u32[]{:S(2)}) %collective-permute-start) | collective-permute-done | bytes 524320 | tf_op jit(solution)/shard_map/ppermute | solution.py:26
  18.5 0.0 collective-permute-done.1.refs_1_
  18.5 1.6 %collective-permute-done.2.refs_2_ = f32[2,512,128]{2,1,0:T(8,128)S(1)} collective-permute-done((f32[2,512,128]{2,1,0:T(8,128)S(1)}, f32[2,512,128]{2,1,0:T(8,128)S(1)}, u32[]{:S(2)}, u32[]{:S(2)}) %collective-permute-start.2) | collective-permute-done | bytes 524320 | tf_op jit(solution)/shard_map/ppermute | solution.py:30
  20.1 1.7 %kv_first_sum_kernel.1 = (f32[5,512,128]{2,1,0:T(8,128)}, f32[5,512,128]{2,1,0:T(8,128)}) custom-call(f32[2,512,128]{2,1,0:T(8,128)S(1)} %collective-permute-done.refs_0_, f32[2,512,128]{2,1,0:T(8,128)S(1)} %collective-permute-done.1.refs_1_, f32[2,512,128]{2,1,0:T(8,128)S(1)} %collective-permute-done.2.refs_2_, ...), custom_call_target="tpu_custom_call" | custom-call | tf_op jit(solution)/shard_map/kv_first_sum_kernel/pallas_call | solution.py:162
  21.9 1.2 collective-permute-start.5
  23.0 0.3 collective-permute-start.4
  23.3 1.1 taps_turn_kernel.1
  24.5 11.8 %all-to-all-start = ((f32[16,8,8,128]{3,2,1,0:T(8,128)}), f32[16,8,8,128]{3,2,1,0:T(8,128)}, u32[]{:S(2)}, u32[]{:S(2)}) async-start(f32[16,8,8,128]{3,2,1,0:T(8,128)} %bitcast.15), calls=%async_computation | async-start | bytes 1048576 | tf_op jit(solution)/shard_map/all_to_all | solution.py:552
  36.3 7.9 %query_project_kernel.1 = (f32[4,256,128]{2,1,0:T(8,128)}, f32[4,256,128]{2,1,0:T(8,128)}, f32[2,256,128]{2,1,0:T(8,128)}, f32[2,256,128]{2,1,0:T(8,128)}, f32[4...) custom-call(s32[5]{0:T(128)S(1)} %stack.23.at.place, ...), custom_call_target="tpu_custom_call" | custom-call | tf_op jit(solution)/shard_map/query_project_kernel/pallas_call | solution.py:351
  44.2 1.0 copy-done.3
  45.2 6.9 %third_kernel.1.refs_0_.refs_1_.refs_6_.refs_2_.refs_3_.refs_4_ = f32[11,512,128]{2,1,0:T(8,128)S(1)} custom-call(s32[5]{0:T(128)S(1)} %stack.23.at.place, bf16[1024,1024]{1,0:T(8,128)(2,1)} %act.7, bf16[3,1024,1024]{2,1,0:T(8,128)(2,1)} %bitcast.13, f32[5,512,128]{2,1,0:T(8,128)} %get-tuple-element.40.refs_0_.refs_1_, f32[4,256,128]{2,1,0:T(8,128)S(1)} %copy-done.3), custom_call_target="tpu_custom_call" | custom-call | tf_op jit(solution)/shard_map/third_kernel/pallas_call | solution.py:135
  52.1 6.3 %all-to-all-done.refs_8_.refs_0_ = f32[16,8,8,128]{3,2,1,0:T(8,128)} async-done(((f32[16,8,8,128]{3,2,1,0:T(8,128)}), f32[16,8,8,128]{3,2,1,0:T(8,128)}, u32[]{:S(2)}, u32[]{:S(2)}) %all-to-all-start) | async-done | bytes 524320 | tf_op jit(solution)/shard_map/all_to_all | solution.py:552
  58.5 2.2 %kv_other_kernel.1.refs_10_ = f32[3,512,128]{2,1,0:T(8,128)} custom-call(f32[11,512,128]{2,1,0:T(8,128)S(1)} %third_kernel.1.refs_0_.refs_1_.refs_6_.refs_2_.refs_3_.refs_4_, f32[11,512,128]{2,1,0:T(8,128)S(1)} %third_kernel.1.refs_0_.refs_1_.refs_6_.refs_2_.refs_3_.refs_4_, f32[5,512,128]{2,1,0:T(8,128)} %collective-permute-done.4.refs_2_.refs_3_.refs_8_.refs_5_.refs_6_, ...), custom_call_target="tpu_custom_call" | custom-call | tf_op jit(solution)/shard_map/kv_other_kernel/pallas_call | solution.py:200
  60.7 2.4 %kv_last_kernel.1 = (f32[2,512,128]{2,1,0:T(8,128)}, f32[2,512,128]{2,1,0:T(8,128)}) custom-call(f32[11,512,128]{2,1,0:T(8,128)S(1)} %third_kernel.1.refs_0_.refs_1_.refs_6_.refs_2_.refs_3_.refs_4_, f32[11,512,128]{2,1,0:T(8,128)S(1)} %third_kernel.1.refs_0_.refs_1_.refs_6_.refs_2_.refs_3_.refs_4_, ...), custom_call_target="tpu_custom_call" | custom-call | tf_op jit(solution)/shard_map/kv_last_kernel/pallas_call | solution.py:200
  63.1 1.3 collective-permute-start.7
  64.3 0.2 collective-permute-start.6
  64.5 1.4 %kv_beside_kernel.1.refs_7_.refs_0_ = f32[4,512,128]{2,1,0:T(8,128)S(1)} custom-call(f32[11,512,128]{2,1,0:T(8,128)S(1)} %third_kernel.1.refs_0_.refs_1_.refs_6_.refs_2_.refs_3_.refs_4_, f32[11,512,128]{2,1,0:T(8,128)S(1)} %third_kernel.1.refs_0_.refs_1_.refs_6_.refs_2_.refs_3_.refs_4_, ...), custom_call_target="tpu_custom_call" | custom-call | tf_op jit(solution)/shard_map/kv_beside_kernel/pallas_call | solution.py:200
  65.9 3.6 %taps_kernel.1.refs_4_.refs_1_ = f32[1024,256]{1,0:T(8,128)} custom-call(f32[16,8,8,128]{3,2,1,0:T(8,128)} %all-to-all-done.refs_8_.refs_0_, bf16[256,128]{1,0:T(8,128)(2,1)} %constant.72.clone.refs_1_.refs_2_, bf16[256,128]{1,0:T(8,128)(2,1)} %constant.73.clone.refs_2_.refs_3_, f32[128,128]{1,0:T(8,128)} %constant.74.clone.refs_3_.refs_4_, ...), custom_call_target="tpu_custom_call" | custom-call | tf_op jit(solution)/shard_map/taps_kernel/pallas_call | solution.py:535
  69.6 0.3 collective-permute-start.9
  69.8 2.7 %collective-permute-start.10 = (f32[4,256,128]{2,1,0:T(8,128)}, f32[4,256,128]{2,1,0:T(8,128)S(1)}, u32[]{:S(2)}, u32[]{:S(2)}) collective-permute-start(f32[4,256,128]{2,1,0:T(8,128)} %get-tuple-element.50), channel_id=1, source_target_pairs={{0,6},{1,7},{2,0},{3,1},{4,2},{5,3},{6,4},{7,5},{8,14},{9,15},{10,... | collective-permute-start | bytes 1572872 | tf_op jit(solution)/shard_map/ppermute | solution.py:26
  72.5 4.0 %collective-permute-done.7.refs_2_ = f32[2,512,128]{2,1,0:T(8,128)} collective-permute-done((f32[2,512,128]{2,1,0:T(8,128)}, f32[2,512,128]{2,1,0:T(8,128)}, u32[]{:S(2)}, u32[]{:S(2)}) %collective-permute-start.7) | collective-permute-done | bytes 524320 | tf_op jit(solution)/shard_map/ppermute | solution.py:26
  76.5 1.1 collective-permute-start.11
  77.7 1.0 collective-permute-done.6.refs_1_
  78.7 1.1 collective-permute-done.8.refs_3_
  79.8 2.6 %kv_kernel.1 = f32[128,8,128]{2,1,0:T(8,128)} custom-call(f32[4,512,128]{2,1,0:T(8,128)S(1)} %copy-done.2, f32[2,512,128]{2,1,0:T(8,128)} %collective-permute-done.6.refs_1_, f32[2,512,128]{2,1,0:T(8,128)} %collective-permute-done.7.refs_2_, f32[3,512,128]{2,1,0:T(8,128)} %collective-permute-done.8.refs_3_, f32[1024,256]{1,0:T(8,128)S(1)} %copy-done), custom_call_target="tpu_custom_call" | custom-call | tf_op jit(solution)/shard_map/kv_kernel/pallas_call | solution.py:535
  82.4 7.1 %all-to-all-start.1 = ((f32[16,8,8,128]{3,2,1,0:T(8,128)}), f32[16,8,8,128]{3,2,1,0:T(8,128)S(1)}, u32[]{:S(2)}, u32[]{:S(2)}) async-start(f32[16,8,8,128]{3,2,1,0:T(8,128)} %bitcast.14), calls=%async_computation.1 | async-start | bytes 1048576 | tf_op jit(solution)/shard_map/all_to_all | solution.py:552
  89.6 0.6 collective-permute-start.14
  90.2 0.1 collective-permute-done.11.refs_2_.refs_4_
  90.3 2.5 %first_sum_kernel.1 = (f32[3,256,128]{2,1,0:T(8,128)}, f32[3,256,128]{2,1,0:T(8,128)}) custom-call(f32[4,256,128]{2,1,0:T(8,128)S(1)} %collective-permute-done.9.refs_0_.refs_2_, f32[4,256,128]{2,1,0:T(8,128)S(1)} %collective-permute-done.10.refs_1_.refs_3_, f32[4,256,128]{2,1,0:T(8,128)} %collective-permute-done.11.refs_2_.refs_4_, ...), custom_call_target="tpu_custom_call" | custom-call | tf_op jit(solution)/shard_map/first_sum_kernel/pallas_call | solution.py:162
  92.8 2.7 %collective-permute-start.13 = (f32[3,256,128]{2,1,0:T(8,128)}, f32[3,256,128]{2,1,0:T(8,128)S(1)}, u32[]{:S(2)}, u32[]{:S(2)}) collective-permute-start(f32[3,256,128]{2,1,0:T(8,128)} %get-tuple-element.56), channel_id=1, source_target_pairs={{0,6},{1,7},{2,0},{3,1},{4,2},{5,3},{6,4},{7,5},{8,14},{9,15},{10,... | collective-permute-start | bytes 1179656 | tf_op jit(solution)/shard_map/ppermute | solution.py:26
  95.5 5.3 %all-to-all-done.1.refs_0_ = f32[16,8,8,128]{3,2,1,0:T(8,128)S(1)} async-done(((f32[16,8,8,128]{3,2,1,0:T(8,128)}), f32[16,8,8,128]{3,2,1,0:T(8,128)S(1)}, u32[]{:S(2)}, u32[]{:S(2)}) %all-to-all-start.1) | async-done | bytes 524320 | tf_op jit(solution)/shard_map/all_to_all | solution.py:552
  100.7 4.7 %conv_kernel.1 = f32[16,8,8,128]{3,2,1,0:T(8,128)} custom-call(f32[16,8,8,128]{3,2,1,0:T(8,128)S(1)} %all-to-all-done.1.refs_0_, f32[1024,256]{1,0:T(8,128)} %taps_kernel.1.refs_4_.refs_1_, bf16[256,128]{1,0:T(8,128)(2,1)} %constant.72.clone.refs_1_.refs_2_, bf16[256,128]{1,0:T(8,128)(2,1)} %constant.73.clone.refs_2_.refs_3_, ...), custom_call_target="tpu_custom_call" | custom-call | tf_op jit(solution)/shard_map/conv_kernel/pallas_call | solution.py:535
  105.5 5.7 %all-to-all-start.2 = ((f32[16,8,8,128]{3,2,1,0:T(8,128)}), f32[16,8,8,128]{3,2,1,0:T(8,128)S(1)}, u32[]{:S(2)}, u32[]{:S(2)}) async-start(f32[16,8,8,128]{3,2,1,0:T(8,128)} %conv_kernel.1), calls=%async_computation.2 | async-start | bytes 1048576 | tf_op jit(solution)/shard_map/all_to_all | solution.py:552
  111.2 1.5 %query_second_sum_kernel.1 = (f32[2,256,128]{2,1,0:T(8,128)S(1)}, f32[2,256,128]{2,1,0:T(8,128)S(1)}, f32[2,256,128]{2,1,0:T(8,128)S(1)}) custom-call(f32[3,256,128]{2,1,0:T(8,128)S(1)} %collective-permute-done.12.refs_0_, f32[3,256,128]{2,1,0:T(8,128)S(1)} %collective-permute-done.13.refs_1_, f32[4,256,128]{2,1,0:T(8,128)S(1)} %collective-permute-done.9.refs_0_.refs_2_, ...), custom_call_target="tpu_custom_call" | custom-call | tf_op jit(solution)/shard_map/query_second_sum_kernel/pallas_call | solution.py:162
  112.7 1.8 %collective-permute-start.16 = (f32[2,256,128]{2,1,0:T(8,128)S(1)}, f32[2,256,128]{2,1,0:T(8,128)S(1)}, u32[]{:S(2)}, u32[]{:S(2)}) collective-permute-start(f32[2,256,128]{2,1,0:T(8,128)S(1)} %get-tuple-element.61), channel_id=1, source_target_pairs={{0,6},{1,7},{2,0},{3,1},{4,2},{5,3},{6,4},{7,5},{8,14},{9,15},{10,... | collective-permute-start | bytes 786440 | tf_op jit(solution)/shard_map/ppermute | solution.py:26
  114.6 1.1 collective-permute-start.17
  115.6 1.3 %query_beside_kernel.1.refs_0_ = f32[4,256,128]{2,1,0:T(8,128)S(1)} custom-call(f32[3,256,128]{2,1,0:T(8,128)S(1)} %collective-permute-done.12.refs_0_, f32[3,256,128]{2,1,0:T(8,128)S(1)} %collective-permute-done.13.refs_1_, f32[4,256,128]{2,1,0:T(8,128)S(1)} %collective-permute-done.9.refs_0_.refs_2_, ...), custom_call_target="tpu_custom_call" | custom-call | tf_op jit(solution)/shard_map/query_beside_kernel/pallas_call | solution.py:162
  117.0 3.7 %collective-permute-done.16.refs_2_ = f32[2,256,128]{2,1,0:T(8,128)S(1)} collective-permute-done((f32[2,256,128]{2,1,0:T(8,128)S(1)}, f32[2,256,128]{2,1,0:T(8,128)S(1)}, u32[]{:S(2)}, u32[]{:S(2)}) %collective-permute-start.16) | collective-permute-done | bytes 262176 | tf_op jit(solution)/shard_map/ppermute | solution.py:26
  120.7 5.5 %collective-permute-done.17.refs_3_ = f32[2,256,128]{2,1,0:T(8,128)S(1)} collective-permute-done((f32[2,256,128]{2,1,0:T(8,128)S(1)}, f32[2,256,128]{2,1,0:T(8,128)S(1)}, u32[]{:S(2)}, u32[]{:S(2)}) %collective-permute-start.17) | collective-permute-done | bytes 262176 | tf_op jit(solution)/shard_map/ppermute | solution.py:30
  126.1 0.1 query_kernel.1.refs_1_
  126.2 1.1 gate_kernel.1
  (25 shorter events, 0.1 us)
Async XLA Ops:
  3.9 14.6 %collective-permute-start = (f32[2,512,128]{2,1,0:T(8,128)S(1)}, f32[2,512,128]{2,1,0:T(8,128)S(1)}, u32[]{:S(2)}, u32[]{:S(2)}) collective-permute-start(f32[2,512,128]{2,1,0:T(8,128)S(1)} %get-tuple-element.34), channel_id=1, source_target_pairs={{0,2},{1,3},{2,4},{3,5},{4,6},{5,7},{6,0},{7,1},{8,10},{9,11},{10,... | collective-permute-start | bytes 1572872 | tf_op jit(solution)/shard_map/ppermute | solution.py:26
  6.0 12.5 %collective-permute-start.1 = (f32[2,512,128]{2,1,0:T(8,128)S(1)}, f32[2,512,128]{2,1,0:T(8,128)S(1)}, u32[]{:S(2)}, u32[]{:S(2)}) collective-permute-start(f32[2,512,128]{2,1,0:T(8,128)S(1)} %get-tuple-element.35), channel_id=1, source_target_pairs={{0,6},{1,7},{2,0},{3,1},{4,2},{5,3},{6,4},{7,5},{8,14},{9,15},{10,... | collective-permute-start | bytes 1572872 | tf_op jit(solution)/shard_map/ppermute | solution.py:26
  7.4 12.7 %collective-permute-start.2 = (f32[2,512,128]{2,1,0:T(8,128)S(1)}, f32[2,512,128]{2,1,0:T(8,128)S(1)}, u32[]{:S(2)}, u32[]{:S(2)}) collective-permute-start(f32[2,512,128]{2,1,0:T(8,128)S(1)} %get-tuple-element.36), channel_id=1, source_target_pairs={{0,1},{1,0},{2,3},{3,2},{4,5},{5,4},{6,7},{7,6},{8,9},{9,8},{10,11... | collective-permute-start | bytes 1572872 | tf_op jit(solution)/shard_map/ppermute | solution.py:30
  16.6 41.8 %collective-permute-start.3 = (f32[5,512,128]{2,1,0:T(8,128)}, f32[5,512,128]{2,1,0:T(8,128)}, u32[]{:S(2)}, u32[]{:S(2)}) collective-permute-start(f32[5,512,128]{2,1,0:T(8,128)} %get-tuple-element.42), channel_id=1, source_target_pairs={{0,1},{1,0},{2,3},{3,2},{4,5},{5,4},{6,7},{7,6},{8,9},{9,8},{10,11... | collective-permute-start | bytes 3932168 | tf_op jit(solution)/shard_map/ppermute | solution.py:30
  20.1 3.2 %copy-start.5 = (f32[1024,128]{1,0:T(8,128)S(1)}, f32[1024,128]{1,0:T(8,128)}, u32[]{:S(2)}) copy-start(f32[1024,128]{1,0:T(8,128)} %refs_0_.1) | copy-start | bytes 1572868
  21.9 36.6 %collective-permute-start.5 = (f32[5,512,128]{2,1,0:T(8,128)}, f32[5,512,128]{2,1,0:T(8,128)}, u32[]{:S(2)}, u32[]{:S(2)}) collective-permute-start(f32[5,512,128]{2,1,0:T(8,128)} %get-tuple-element.43), channel_id=1, source_target_pairs={{0,6},{1,7},{2,0},{3,1},{4,2},{5,3},{6,4},{7,5},{8,14},{9,15},{10,... | collective-permute-start | bytes 3932168 | tf_op jit(solution)/shard_map/ppermute | solution.py:26
  23.0 35.4 %collective-permute-start.4 = (f32[5,512,128]{2,1,0:T(8,128)}, f32[5,512,128]{2,1,0:T(8,128)}, u32[]{:S(2)}, u32[]{:S(2)}) collective-permute-start(f32[5,512,128]{2,1,0:T(8,128)} %get-tuple-element.40.refs_0_.refs_1_), channel_id=1, source_target_pairs={{0,2},{1,3},{2,4},{3,5},{4,6},{5,7},{6,0},{7,1},{8,10},{9,11},{10,... | collective-permute-start | bytes 3932168 | tf_op jit(solution)/shard_map/ppermute | solution.py:26
  24.5 34.0 %all-to-all-start = ((f32[16,8,8,128]{3,2,1,0:T(8,128)}), f32[16,8,8,128]{3,2,1,0:T(8,128)}, u32[]{:S(2)}, u32[]{:S(2)}) async-start(f32[16,8,8,128]{3,2,1,0:T(8,128)} %bitcast.15), calls=%async_computation | async-start | bytes 1048576 | tf_op jit(solution)/shard_map/all_to_all | solution.py:552
  44.2 1.0 copy-start.3
  45.2 13.3 %copy-start.4 = (f32[4,256,128]{2,1,0:T(8,128)S(1)}, f32[4,256,128]{2,1,0:T(8,128)}, u32[]{:S(2)}) copy-start(f32[4,256,128]{2,1,0:T(8,128)} %get-tuple-element.41.refs_1_.refs_9_.refs_0_) | copy-start | bytes 1572868
  60.7 19.1 %collective-permute-start.8 = (f32[3,512,128]{2,1,0:T(8,128)}, f32[3,512,128]{2,1,0:T(8,128)}, u32[]{:S(2)}, u32[]{:S(2)}) collective-permute-start(f32[3,512,128]{2,1,0:T(8,128)} %kv_other_kernel.1.refs_10_), channel_id=1, source_target_pairs={{0,1},{1,0},{2,3},{3,2},{4,5},{5,4},{6,7},{7,6},{8,9},{9,8},{10,11... | collective-permute-start | bytes 2359304 | tf_op jit(solution)/shard_map/ppermute | solution.py:30
  63.1 13.5 %collective-permute-start.7 = (f32[2,512,128]{2,1,0:T(8,128)}, f32[2,512,128]{2,1,0:T(8,128)}, u32[]{:S(2)}, u32[]{:S(2)}) collective-permute-start(f32[2,512,128]{2,1,0:T(8,128)} %get-tuple-element.45), channel_id=1, source_target_pairs={{0,6},{1,7},{2,0},{3,1},{4,2},{5,3},{6,4},{7,5},{8,14},{9,15},{10,... | collective-permute-start | bytes 1572872 | tf_op jit(solution)/shard_map/ppermute | solution.py:26
  64.3 14.4 %collective-permute-start.6 = (f32[2,512,128]{2,1,0:T(8,128)}, f32[2,512,128]{2,1,0:T(8,128)}, u32[]{:S(2)}, u32[]{:S(2)}) collective-permute-start(f32[2,512,128]{2,1,0:T(8,128)} %get-tuple-element.44.refs_9_), channel_id=1, source_target_pairs={{0,2},{1,3},{2,4},{3,5},{4,6},{5,7},{6,0},{7,1},{8,10},{9,11},{10,... | collective-permute-start | bytes 1572872 | tf_op jit(solution)/shard_map/ppermute | solution.py:26
  65.9 3.7 %copy-start.1 = (f32[4,512,128]{2,1,0:T(8,128)}, f32[4,512,128]{2,1,0:T(8,128)S(1)}, u32[]{:S(2)}) copy-start(f32[4,512,128]{2,1,0:T(8,128)S(1)} %kv_beside_kernel.1.refs_7_.refs_0_) | copy-start | bytes 3145732
  69.6 10.2 %copy-start = (f32[1024,256]{1,0:T(8,128)S(1)}, f32[1024,256]{1,0:T(8,128)}, u32[]{:S(2)}) copy-start(f32[1024,256]{1,0:T(8,128)} %taps_kernel.1.refs_4_.refs_1_) | copy-start | bytes 3145732
  69.6 10.2 %copy-start.2 = (f32[4,512,128]{2,1,0:T(8,128)S(1)}, f32[4,512,128]{2,1,0:T(8,128)}, u32[]{:S(2)}) copy-start(f32[4,512,128]{2,1,0:T(8,128)} %copy-done.1) | copy-start | bytes 3145732
  69.6 20.6 %collective-permute-start.9 = (f32[4,256,128]{2,1,0:T(8,128)}, f32[4,256,128]{2,1,0:T(8,128)S(1)}, u32[]{:S(2)}, u32[]{:S(2)}) collective-permute-start(f32[4,256,128]{2,1,0:T(8,128)} %get-tuple-element.49), channel_id=1, source_target_pairs={{0,2},{1,3},{2,4},{3,5},{4,6},{5,7},{6,0},{7,1},{8,10},{9,11},{10,... | collective-permute-start | bytes 1572872 | tf_op jit(solution)/shard_map/ppermute | solution.py:26
  69.8 20.4 %collective-permute-start.10 = (f32[4,256,128]{2,1,0:T(8,128)}, f32[4,256,128]{2,1,0:T(8,128)S(1)}, u32[]{:S(2)}, u32[]{:S(2)}) collective-permute-start(f32[4,256,128]{2,1,0:T(8,128)} %get-tuple-element.50), channel_id=1, source_target_pairs={{0,6},{1,7},{2,0},{3,1},{4,2},{5,3},{6,4},{7,5},{8,14},{9,15},{10,... | collective-permute-start | bytes 1572872 | tf_op jit(solution)/shard_map/ppermute | solution.py:26
  76.5 13.7 %collective-permute-start.11 = (f32[4,256,128]{2,1,0:T(8,128)}, f32[4,256,128]{2,1,0:T(8,128)}, u32[]{:S(2)}, u32[]{:S(2)}) collective-permute-start(f32[4,256,128]{2,1,0:T(8,128)} %get-tuple-element.51), channel_id=1, source_target_pairs={{0,1},{1,0},{2,3},{3,2},{4,5},{5,4},{6,7},{7,6},{8,9},{9,8},{10,11... | collective-permute-start | bytes 1572872 | tf_op jit(solution)/shard_map/ppermute | solution.py:30
  82.4 18.3 %all-to-all-start.1 = ((f32[16,8,8,128]{3,2,1,0:T(8,128)}), f32[16,8,8,128]{3,2,1,0:T(8,128)S(1)}, u32[]{:S(2)}, u32[]{:S(2)}) async-start(f32[16,8,8,128]{3,2,1,0:T(8,128)} %bitcast.14), calls=%async_computation.1 | async-start | bytes 1048576 | tf_op jit(solution)/shard_map/all_to_all | solution.py:552
  89.6 21.6 %collective-permute-start.14 = (f32[4,256,128]{2,1,0:T(8,128)}, f32[4,256,128]{2,1,0:T(8,128)S(1)}, u32[]{:S(2)}, u32[]{:S(2)}) collective-permute-start(f32[4,256,128]{2,1,0:T(8,128)} %get-tuple-element.57), channel_id=1, source_target_pairs={{0,1},{1,0},{2,3},{3,2},{4,5},{5,4},{6,7},{7,6},{8,9},{9,8},{10,11... | collective-permute-start | bytes 1572872 | tf_op jit(solution)/shard_map/ppermute | solution.py:30
  92.8 18.4 %collective-permute-start.12 = (f32[3,256,128]{2,1,0:T(8,128)}, f32[3,256,128]{2,1,0:T(8,128)S(1)}, u32[]{:S(2)}, u32[]{:S(2)}) collective-permute-start(f32[3,256,128]{2,1,0:T(8,128)} %get-tuple-element.55), channel_id=1, source_target_pairs={{0,2},{1,3},{2,4},{3,5},{4,6},{5,7},{6,0},{7,1},{8,10},{9,11},{10,... | collective-permute-start | bytes 1179656 | tf_op jit(solution)/shard_map/ppermute | solution.py:26
  92.8 18.4 %collective-permute-start.13 = (f32[3,256,128]{2,1,0:T(8,128)}, f32[3,256,128]{2,1,0:T(8,128)S(1)}, u32[]{:S(2)}, u32[]{:S(2)}) collective-permute-start(f32[3,256,128]{2,1,0:T(8,128)} %get-tuple-element.56), channel_id=1, source_target_pairs={{0,6},{1,7},{2,0},{3,1},{4,2},{5,3},{6,4},{7,5},{8,14},{9,15},{10,... | collective-permute-start | bytes 1179656 | tf_op jit(solution)/shard_map/ppermute | solution.py:26
  105.5 20.7 %all-to-all-start.2 = ((f32[16,8,8,128]{3,2,1,0:T(8,128)}), f32[16,8,8,128]{3,2,1,0:T(8,128)S(1)}, u32[]{:S(2)}, u32[]{:S(2)}) async-start(f32[16,8,8,128]{3,2,1,0:T(8,128)} %conv_kernel.1), calls=%async_computation.2 | async-start | bytes 1048576 | tf_op jit(solution)/shard_map/all_to_all | solution.py:552
  112.7 7.9 %collective-permute-start.16 = (f32[2,256,128]{2,1,0:T(8,128)S(1)}, f32[2,256,128]{2,1,0:T(8,128)S(1)}, u32[]{:S(2)}, u32[]{:S(2)}) collective-permute-start(f32[2,256,128]{2,1,0:T(8,128)S(1)} %get-tuple-element.61), channel_id=1, source_target_pairs={{0,6},{1,7},{2,0},{3,1},{4,2},{5,3},{6,4},{7,5},{8,14},{9,15},{10,... | collective-permute-start | bytes 786440 | tf_op jit(solution)/shard_map/ppermute | solution.py:26
  114.6 11.6 %collective-permute-start.17 = (f32[2,256,128]{2,1,0:T(8,128)S(1)}, f32[2,256,128]{2,1,0:T(8,128)S(1)}, u32[]{:S(2)}, u32[]{:S(2)}) collective-permute-start(f32[2,256,128]{2,1,0:T(8,128)S(1)} %get-tuple-element.62), channel_id=1, source_target_pairs={{0,1},{1,0},{2,3},{3,2},{4,5},{5,4},{6,7},{7,6},{8,9},{9,8},{10,11... | collective-permute-start | bytes 786440 | tf_op jit(solution)/shard_map/ppermute | solution.py:30
  115.6 10.5 %collective-permute-start.15 = (f32[2,256,128]{2,1,0:T(8,128)S(1)}, f32[2,256,128]{2,1,0:T(8,128)S(1)}, u32[]{:S(2)}, u32[]{:S(2)}) collective-permute-start(f32[2,256,128]{2,1,0:T(8,128)S(1)} %get-tuple-element.60.refs_7_), channel_id=1, source_target_pairs={{0,2},{1,3},{2,4},{3,5},{4,6},{5,7},{6,0},{7,1},{8,10},{9,11},{10,... | collective-permute-start | bytes 786440 | tf_op jit(solution)/shard_map/ppermute | solution.py:26
